TPU v7x, 32 devices: a whole 2x2x4 slice. The times are simulated.
32 devices in a mesh: tm: 8 (over y, x, core), zone: 4 (over z).
Axes of the slice: x: 2, y: 2, z: 4, core: 2. Of those that a mesh axis runs over, the one named last changes fastest.
Arguments:
- states: bfloat16 [32, 512, 512], P('tm', 'zone'), may hold values from -6 to 6
- gain_attn: float32 [512], replicated, may hold values from 0.1 to 1.9
- w_qkv: bfloat16 [512, 1536], P('zone')
- w_out_attn: bfloat16 [512, 512], P('zone'), may hold values from -0.25 to 0.25
- pattern: int32 [8, 2], P('tm'), may hold values from 0 to 1, as said below
- gain_mix: float32 [512], replicated, may hold values from 0.1 to 1.9
- neighbours: int32 [4, 3], replicated, may hold values from 0 to 3, as said below
- degree: int32 [4], replicated, may hold values from 1 to 3
- mix: bfloat16 [4, 3, 128, 128], replicated, may hold values from -0.3125 to 0.3125
- gain_ffn: float32 [512], replicated, may hold values from 0.1 to 1.9
- w_in: bfloat16 [512, 2048], P('zone'), may hold values from -0.25 to 0.25
- w_out: bfloat16 [2048, 512], P('zone'), may hold values from -0.125 to 0.125
Outputs:
- evolved: bfloat16 [32, 512, 512], P('tm', 'zone')
Inputs may be any that keep to these rules, and one draw needn't show every extreme that they name: `pattern`: time blocks 1 to 2 each attend to time block 0. `neighbours`: each row names 3 different zone blocks.
All inputs are finite; a program needn't handle non-finite values.
Results may differ from a plain program's by a relative error of at most 0.008.
Values may be sent and summed in bfloat16 or wider, within the bound.
No kernel may reach another device: no remote copies, remote signals or barrier semaphores. Data moves between devices by JAX's collectives and lax.ppermute only.
A program may use at most 64 MiB of HBM per device.

v0:
```python
import jax
import jax.numpy as jnp
from jax import lax
from jax.sharding import PartitionSpec as P

HEADS = 4


def shifted(value, axis, steps):
    count = lax.axis_size(axis)
    first, last = (max(0, -steps), min(count, count - steps))
    return lax.ppermute(value, axis, [(source, source + steps) for source in range(first, last)])


def rms_scale(values, gain):
    mean_sq = jnp.mean(values * values, axis=-1, keepdims=True)
    return values * lax.rsqrt(mean_sq + 1e-06) * gain


def on_device(
    states,
    gain_attn,
    w_qkv,
    w_out_attn,
    pattern,
    gain_mix,
    neighbours,
    degree,
    mix,
    gain_ffn,
    w_in,
    w_out,
):
    steps, zone_rows, width = states.shape
    head_size = width // HEADS
    reach = pattern.shape[1]
    full_qkv, full_attn, full_in, full_out = (
        lax.all_gather(w_qkv, "zone", axis=0, tiled=True),
        lax.all_gather(w_out_attn, "zone", axis=0, tiled=True),
        lax.all_gather(w_in, "zone", axis=0, tiled=True),
        lax.all_gather(w_out, "zone", axis=0, tiled=True),
    )
    input_wide = states.astype(jnp.float32)
    normed = rms_scale(input_wide, gain_attn).astype(jnp.bfloat16)
    projected = jnp.dot(
        normed.reshape(-1, width), full_qkv, preferred_element_type=jnp.float32
    ).astype(jnp.bfloat16)
    projected = projected.reshape(steps, zone_rows, 3 * width)
    queries = projected[..., :width].reshape(steps, zone_rows, HEADS, head_size)
    own_pairs = projected[..., width:]
    earlier = []
    for offset in range(reach, 0, -1):
        earlier.append(shifted(own_pairs, "tm", offset))
    all_pairs = jnp.concatenate(earlier + [own_pairs], axis=0)
    key_count = all_pairs.shape[0]
    keys_all = all_pairs[..., :width].reshape(key_count, zone_rows, HEADS, head_size)
    values_all = all_pairs[..., width:].reshape(key_count, zone_rows, HEADS, head_size)
    scores = jnp.einsum(
        "tzhd,szhd->zhts", queries, keys_all, preferred_element_type=jnp.float32
    ) * head_size ** (-0.5)
    my_block = lax.axis_index("tm")
    key_index = jnp.arange(key_count, dtype=jnp.int32)
    back = reach - key_index // steps
    pattern_row = jnp.concatenate([jnp.ones((1,), jnp.int32), pattern[0]])
    live_back = jnp.sum(
        jnp.where(
            back[:, None] == jnp.arange(reach + 1, dtype=jnp.int32)[None, :],
            pattern_row[None, :],
            0,
        ),
        axis=1,
    )
    query_pos = jnp.arange(steps, dtype=jnp.int32)
    local_key = key_index - reach * steps
    earlier_ok = (back > 0) & (live_back == 1) & (my_block - back >= 0)
    allowed = earlier_ok[None, :] | (back[None, :] == 0) & (
        local_key[None, :] <= query_pos[:, None]
    )
    masked = jnp.where(allowed, scores, -1e30)
    top = jnp.max(masked, axis=-1, keepdims=True)
    expw = jnp.where(allowed, jnp.exp(masked - top), 0.0)
    total = jnp.sum(expw, axis=-1)
    probs = expw.astype(jnp.bfloat16)
    context = jnp.einsum("zhts,szhd->tzhd", probs, values_all, preferred_element_type=jnp.float32)
    context = (
        (context / jnp.transpose(total, (2, 0, 1))[..., None])
        .astype(jnp.bfloat16)
        .reshape(-1, width)
    )
    after_attn = input_wide + jnp.dot(
        context, full_attn, preferred_element_type=jnp.float32
    ).reshape(steps, zone_rows, width)
    mixin = jnp.transpose(rms_scale(after_attn, gain_mix).astype(jnp.bfloat16), (0, 2, 1))
    slot_live = jnp.arange(mix.shape[1], dtype=jnp.int32)[None, :] < degree[:, None]
    live_mix = jnp.where(slot_live[:, :, None, None], mix, jnp.zeros_like(mix))
    items = lax.all_to_all(mixin, "zone", split_axis=1, concat_axis=2, tiled=True)
    count, channels, zones_all = items.shape
    block_count = neighbours.shape[0]
    grid = items.reshape(count, channels, block_count, zones_all // block_count)
    nearby = grid[:, :, neighbours, :]
    spatial = jnp.einsum("ncbky,bkzy->ncbz", nearby, live_mix, preferred_element_type=jnp.float32)
    spatial = spatial.astype(jnp.bfloat16).reshape(count, channels, zones_all)
    returned = lax.all_to_all(spatial, "zone", split_axis=2, concat_axis=1, tiled=True)
    after_mix = after_attn + jnp.transpose(returned, (0, 2, 1)).astype(jnp.float32)
    ffn_in = rms_scale(after_mix, gain_ffn).astype(jnp.bfloat16).reshape(-1, width)
    hidden = jax.nn.gelu(
        jnp.dot(ffn_in, full_in, preferred_element_type=jnp.float32), approximate=True
    ).astype(jnp.bfloat16)
    evolved = after_mix + jnp.dot(hidden, full_out, preferred_element_type=jnp.float32).reshape(
        steps, zone_rows, width
    )
    return evolved.astype(jnp.bfloat16)


def solution(mesh):
    return jax.shard_map(
        on_device,
        mesh=mesh,
        in_specs=(
            P("tm", "zone", None),
            P(),
            P("zone", None),
            P("zone", None),
            P("tm", None),
            P(),
            P(),
            P(),
            P(),
            P(),
            P("zone", None),
            P("zone", None),
        ),
        out_specs=P("tm", "zone", None),
        check_vma=False,
    )
```

profile of v0, /device:TPU:3, one launch (start us, length us, event | category | flops | bytes accessed | tf_op | source)
XLA Modules:
  0.0 180.6 jit_solution(7076595060963715557)
XLA Ops:
  8.7 1.2 fusion.19
  10.0 0.9 fusion.21
  10.9 36.3 %all-gather.4.cloned.1.call-done = bf16[512,1536]{1,0:T(8,128)(2,1)} async-done(((bf16[128,1536]{1,0:T(8,128)(2,1)}), bf16[512,1536]{1,0:T(8,128)(2,1)}) %all-gather.4.cloned.1.call-update) | async-done | bytes 1572880 | tf_op jit(solution)/shard_map/all_gather | solution.py:38
  47.2 2.4 %convolution_convert_fusion = bf16[512,1536]{1,0:T(8,128)(2,1)S(1)} fusion(bf16[512,512]{1,0:T(8,128)(2,1)S(1)} %bitcast.100, bf16[512,1536]{1,0:T(8,128)(2,1)} %all-gather.4.cloned.1.call-done), kind=kOutput, calls=%fused_computation.12 | convolution fusion | flops 806092800 | bytes 3670016 | tf_op jit(solution)/shard_map/dot_general | solution.py:45
  49.6 1.2 copy-done.3
  51.5 3.1 %collective-permute-start = (bf16[4,128,1024]{1,2,0:T(8,128)(2,1)S(1)}, bf16[4,128,1024]{1,2,0:T(8,128)(2,1)S(1)}, u32[]{:S(2)}, u32[]{:S(2)}) collective-permute-start(bf16[4,128,1024]{1,2,0:T(8,128)(2,1)S(1)} %copy.55), channel_id=1, source_target_pairs={{0,8},{4,12},{8,16},{12,20},{16,24},{20,28},{1,9},{5,13},{9,17},{1... | collective-permute-start | bytes 3145736 | tf_op jit(solution)/shard_map/ppermute | solution.py:12
  54.6 4.1 %collective-permute-start.1 = (bf16[4,128,1024]{1,2,0:T(8,128)(2,1)S(1)}, bf16[4,128,1024]{1,2,0:T(8,128)(2,1)}, u32[]{:S(2)}, u32[]{:S(2)}) collective-permute-start(bf16[4,128,1024]{1,2,0:T(8,128)(2,1)S(1)} %copy.55), channel_id=1, source_target_pairs={{0,4},{4,8},{8,12},{12,16},{16,20},{20,24},{24,28},{1,5},{5,9},{9,... | collective-permute-start | bytes 3145736 | tf_op jit(solution)/shard_map/ppermute | solution.py:12
  58.9 21.1 %all_gather.13 = bf16[512,512]{1,0:T(8,128)(2,1)} all-gather(bf16[128,512]{1,0:T(8,128)(2,1)S(1)} %copy-done.6), channel_id=1, replica_groups=mesh['tm'=8,'zone'=4] {'zone'}, dimensions={0}, use_global_device_ids=true | all-gather | bytes 655360 | tf_op jit(solution)/shard_map/all_gather | solution.py:39
  80.0 1.1 slice.20
  81.3 1.2 copy.40
  82.5 6.3 %collective-permute-done.1 = bf16[4,128,1024]{1,2,0:T(8,128)(2,1)} collective-permute-done((bf16[4,128,1024]{1,2,0:T(8,128)(2,1)S(1)}, bf16[4,128,1024]{1,2,0:T(8,128)(2,1)}, u32[]{:S(2)}, u32[]{:S(2)}) %collective-permute-start.1) | collective-permute-done | bytes 1048608 | tf_op jit(solution)/shard_map/ppermute | solution.py:12
  88.8 1.4 pad_maximum_fusion
  90.5 3.0 %copy.41 = bf16[12,128,4,128]{3,0,2,1:T(8,128)(2,1)} copy(bf16[12,128,4,128]{1,3,2,0:T(8,128)(2,1)S(1)} %bitcast.93) | data formatting | bytes 3145728 | tf_op jit(solution)/shard_map/reshape | solution.py:56
  93.4 3.0 %copy.42 = bf16[12,128,4,128]{3,0,2,1:T(8,128)(2,1)} copy(bf16[12,128,4,128]{1,3,2,0:T(8,128)(2,1)S(1)} %bitcast.92) | data formatting | bytes 3145728 | tf_op jit(solution)/shard_map/reshape | solution.py:57
  96.4 3.0 %fusion.39 = (f32[128,4,4]{2,1,0:T(4,128)S(1)}, bf16[128,4,4,12]{3,2,1,0:T(4,128)(2,1)S(1)}) fusion(pred[4,12]{1,0:T(4,128)(4,1)S(1)} %fusion.31, bf16[4,128,4,128]{3,0,2,1:T(4,128)(2,1)S(1)} %copy-done.4, bf16[12,128,4,128]{3,0,2,1:T(8,128)(2,1)} %copy.41), kind=kOutput, calls=%fused_computation.72 | convolution fusion | flops 6438923 | bytes 2154544 | tf_op jit(solution)/shard_map/sub | solution.py:81
  99.5 2.5 %fusion.17 = bf16[4,128,4,128]{3,0,2,1:T(4,128)(2,1)S(1)} fusion(bf16[12,128,4,128]{3,0,2,1:T(8,128)(2,1)} %copy.42, f32[4,128,4]{0,2,1:T(4,128)S(1)} %bitcast.103, bf16[128,4,4,12]{3,2,1,0:T(4,128)(2,1)S(1)} %get-tuple-element.8), kind=kOutput, calls=%fused_computation.26 | convolution fusion | flops 6815744 | bytes 2154496 | tf_op jit(solution)/shard_map/zhts,szhd->tzhd/dot_general | solution.py:84
  103.2 1.1 copy.45
  104.3 3.5 %all-to-all-start = ((bf16[4,512,128]{2,0,1:T(4,128)(2,1)}), bf16[4,512,128]{2,0,1:T(4,128)(2,1)S(1)}, u32[]{:S(2)}, u32[]{:S(2)}) async-start(bf16[4,512,128]{2,0,1:T(4,128)(2,1)} %copy.45), calls=%async_computation | async-start | bytes 1048576 | tf_op jit(solution)/shard_map/all_to_all | solution.py:96
  108.0 21.4 %all-to-all-done = bf16[4,512,128]{2,0,1:T(4,128)(2,1)S(1)} async-done(((bf16[4,512,128]{2,0,1:T(4,128)(2,1)}), bf16[4,512,128]{2,0,1:T(4,128)(2,1)S(1)}, u32[]{:S(2)}, u32[]{:S(2)}) %all-to-all-start) | async-done | bytes 524320 | tf_op jit(solution)/shard_map/all_to_all | solution.py:96
  129.4 0.8 gather_fusion
  131.6 28.5 %all_to_all.24 = bf16[4,128,512]{1,0,2:T(4,128)(2,1)S(1)} all-to-all(bf16[4,128,512]{1,0,2:T(4,128)(2,1)S(1)} %copy.49), channel_id=1, replica_groups=mesh['tm'=8,'zone'=4] {'zone'}, dimensions={2} | all-to-all | bytes 1048576 | tf_op jit(solution)/shard_map/all_to_all | solution.py:103
  160.6 7.5 %all-gather.8.cloned.1.call-done = bf16[2048,512]{1,0:T(8,128)(2,1)} async-done(((bf16[512,512]{1,0:T(8,128)(2,1)}), bf16[2048,512]{1,0:T(8,128)(2,1)}) %all-gather.8.cloned.1.call-update) | async-done | bytes 2097168 | tf_op jit(solution)/shard_map/all_gather | solution.py:41
  168.2 4.8 %fusion.9 = f32[512,512]{1,0:T(8,128)S(1)} fusion(bf16[2048,512]{1,0:T(8,128)(2,1)} %all-gather.8.cloned.1.call-done, bf16[512,512]{1,0:T(8,128)(2,1)S(1)} %bitcast.101, bf16[512,2048]{1,0:T(8,128)(2,1)} %all-gather.6.cloned.1.call-done), kind=kOutput, calls=%fused_computation.13 | convolution fusion | flops 2156920832 | bytes 5767168 | tf_op jit(solution)/shard_map/dot_general | solution.py:109
  173.0 1.1 add_convert_fusion
  (58 shorter events, 6.8 us)
Async XLA Ops:
  6.5 3.4 %copy-start = (bf16[4,128,512]{2,1,0:T(8,128)(2,1)S(1)}, bf16[4,128,512]{2,1,0:T(8,128)(2,1)}, u32[]{:S(2)}) copy-start(bf16[4,128,512]{2,1,0:T(8,128)(2,1)} %param.12) | copy-start | bytes 1572868
  6.5 40.6 %all-gather.4.cloned.1.call-start = ((), (), s32[]{:S(2)}) async-start(), calls=%async_computation.2 | async-start | bytes 1966080 | tf_op jit(solution)/shard_map/all_gather | solution.py:38
  7.3 153.4 %all-gather.6.cloned.1.call-start = ((), (), s32[]{:S(2)}) async-start(), calls=%async_computation.3 | async-start | bytes 2621440 | tf_op jit(solution)/shard_map/all_gather | solution.py:40
  8.0 160.1 %all-gather.8.cloned.1.call-start = ((), (), s32[]{:S(2)}) async-start(), calls=%async_computation.4 | async-start | bytes 2621440 | tf_op jit(solution)/shard_map/all_gather | solution.py:41
  49.6 1.2 copy-start.3
  50.7 8.0 %copy-start.10 = (s32[1,2]{1,0:T(1,128)S(1)}, s32[1,2]{1,0:T(1,128)}, u32[]{:S(2)}) copy-start(s32[1,2]{1,0:T(1,128)} %param.16) | copy-start | bytes 28
  50.7 8.2 %copy-start.6 = (bf16[128,512]{1,0:T(8,128)(2,1)S(1)}, bf16[128,512]{1,0:T(8,128)(2,1)}, u32[]{:S(2)}) copy-start(bf16[128,512]{1,0:T(8,128)(2,1)} %param.15) | copy-start | bytes 393220
  51.5 31.0 %collective-permute-start = (bf16[4,128,1024]{1,2,0:T(8,128)(2,1)S(1)}, bf16[4,128,1024]{1,2,0:T(8,128)(2,1)S(1)}, u32[]{:S(2)}, u32[]{:S(2)}) collective-permute-start(bf16[4,128,1024]{1,2,0:T(8,128)(2,1)S(1)} %copy.55), channel_id=1, source_target_pairs={{0,8},{4,12},{8,16},{12,20},{16,24},{20,28},{1,9},{5,13},{9,17},{1... | collective-permute-start | bytes 3145736 | tf_op jit(solution)/shard_map/ppermute | solution.py:12
  54.6 34.2 %collective-permute-start.1 = (bf16[4,128,1024]{1,2,0:T(8,128)(2,1)S(1)}, bf16[4,128,1024]{1,2,0:T(8,128)(2,1)}, u32[]{:S(2)}, u32[]{:S(2)}) collective-permute-start(bf16[4,128,1024]{1,2,0:T(8,128)(2,1)S(1)} %copy.55), channel_id=1, source_target_pairs={{0,4},{4,8},{8,12},{12,16},{16,20},{20,24},{24,28},{1,5},{5,9},{9,... | collective-permute-start | bytes 3145736 | tf_op jit(solution)/shard_map/ppermute | solution.py:12
  93.4 3.0 %copy-start.4 = (bf16[4,128,4,128]{3,0,2,1:T(4,128)(2,1)S(1)}, bf16[4,128,4,128]{3,0,2,1:T(4,128)(2,1)}, u32[]{:S(2)}) copy-start(bf16[4,128,4,128]{3,0,2,1:T(4,128)(2,1)} %copy.40) | copy-start | bytes 1572868
  99.5 3.0 %copy-start.1 = (bf16[4,128,512]{2,1,0:T(8,128)(2,1)S(1)}, bf16[4,128,512]{2,1,0:T(8,128)(2,1)}, u32[]{:S(2)}) copy-start(bf16[4,128,512]{2,1,0:T(8,128)(2,1)} %param.12) | copy-start | bytes 1572868
  99.5 3.0 %copy-start.2 = (bf16[512,512]{1,0:T(8,128)(2,1)S(1)}, bf16[512,512]{1,0:T(8,128)(2,1)}, u32[]{:S(2)}) copy-start(bf16[512,512]{1,0:T(8,128)(2,1)} %all_gather.13) | copy-start | bytes 1572868
  102.0 1.1 copy-start.7
  103.0 4.7 %copy-start.8 = (s32[4,3]{1,0:T(4,128)S(1)}, s32[4,3]{1,0:T(4,128)}, u32[]{:S(2)}) copy-start(s32[4,3]{1,0:T(4,128)} %param.18) | copy-start | bytes 148
  103.0 4.9 %copy-start.11 = (s32[4]{0:T(128)S(1)}, s32[4]{0:T(128)}, u32[]{:S(2)}) copy-start(s32[4]{0:T(128)} %param.19) | copy-start | bytes 52
  104.3 25.1 %all-to-all-start = ((bf16[4,512,128]{2,0,1:T(4,128)(2,1)}), bf16[4,512,128]{2,0,1:T(4,128)(2,1)S(1)}, u32[]{:S(2)}, u32[]{:S(2)}) async-start(bf16[4,512,128]{2,0,1:T(4,128)(2,1)} %copy.45), calls=%async_computation | async-start | bytes 1048576 | tf_op jit(solution)/shard_map/all_to_all | solution.py:96
  129.4 1.0 copy-start.5
  131.5 28.9 %copy-start.9 = (f32[512]{0:T(512)S(1)}, f32[512]{0:T(512)}, u32[]{:S(2)}) copy-start(f32[512]{0:T(512)} %param.21) | copy-start | bytes 6148
Sparse Core Ops, SparseCore 0:
  8.9 38.1 all-gather.3
  48.7 53.2 all-gather.5
  103.6 64.5 all-gather.7
where the time goes:
time: 181 us
  waiting for transfers between devices  73.6 us (41%)
  blocking collectives  49.6 us (27%)
  local copies, waits for them, and re-layouts  13.9 us (8%)
  matrix products  13.9 us (8%)
  between operations  13.4 us (7%)
  starting transfers between devices  10.7 us (6%)
  other arithmetic  5.44 us (3%)
    all_gather x1, waiting for transfers between devices, on_device(): lax.all_gather(w_qkv, 'zone', axis=0, tiled=True)  36.3 us
    all_to_all x1, blocking collectives, on_device(): lax.all_to_all(spatial, 'zone', split_axis=2, concat_axis=1, tiled=True)  28.5 us
    all_to_all x1, waiting for transfers between devices, on_device(): lax.all_to_all(mixin, 'zone', split_axis=1, concat_axis=2, tiled=True)  21.4 us
    all_gather x1, blocking collectives, on_device(): lax.all_gather(w_out_attn, 'zone', axis=0, tiled=True)  21.1 us
    all_gather x1, waiting for transfers between devices, on_device(): lax.all_gather(w_out, 'zone', axis=0, tiled=True)  7.52 us
    ppermute x2, starting transfers between devices, shifted(): lax.ppermute(value, axis, [(source, source + steps) for source in range(f...  7.15 us
    ppermute x2, waiting for transfers between devices, shifted(): lax.ppermute(value, axis, [(source, source + steps) for source in range(f...  6.3 us
    dot_general x1, matrix products, on_device(): jnp.dot(hidden, full_out, preferred_element_type=jnp.float32)  4.84 us
  transfers between devices with their start and end apart: 6, of which 4 were waited for; matrix products, arithmetic and copies ran while one was open for 14% of the time, Pallas kernels for 0%

commit v1 on v0

--- a/solution.py
+++ b/solution.py
@@ -10,6 +10,11 @@
     count = lax.axis_size(axis)
     first, last = (max(0, -steps), min(count, count - steps))
     return lax.ppermute(value, axis, [(source, source + steps) for source in range(first, last)])
+
+
+def tm_slice(weight, spread):
+    rows = weight.shape[0] // spread
+    return lax.dynamic_slice_in_dim(weight, lax.axis_index("tm") * rows, rows, axis=0)
 
 
 def rms_scale(values, gain):
@@ -34,27 +39,26 @@
     steps, zone_rows, width = states.shape
     head_size = width // HEADS
     reach = pattern.shape[1]
-    full_qkv, full_attn, full_in, full_out = (
-        lax.all_gather(w_qkv, "zone", axis=0, tiled=True),
-        lax.all_gather(w_out_attn, "zone", axis=0, tiled=True),
-        lax.all_gather(w_in, "zone", axis=0, tiled=True),
-        lax.all_gather(w_out, "zone", axis=0, tiled=True),
-    )
+    spread = lax.axis_size("tm")
+    first = jnp.concatenate([tm_slice(w_qkv, spread), tm_slice(w_out_attn, spread)], axis=1)
+    full_first = lax.all_gather(first, ("zone", "tm"), axis=0, tiled=True)
+    full_qkv, full_attn = full_first[:, : 3 * width], full_first[:, 3 * width :]
+    full_in = lax.all_gather(tm_slice(w_in, spread), ("zone", "tm"), axis=0, tiled=True)
+    full_out = lax.all_gather(tm_slice(w_out, spread), ("zone", "tm"), axis=0, tiled=True)
+    earlier = []
+    for offset in range(reach, 0, -1):
+        earlier.append(shifted(states, "tm", offset))
+    all_states = jnp.concatenate(earlier + [states], axis=0).astype(jnp.float32)
     input_wide = states.astype(jnp.float32)
-    normed = rms_scale(input_wide, gain_attn).astype(jnp.bfloat16)
+    normed = rms_scale(all_states, gain_attn).astype(jnp.bfloat16)
+    key_count = normed.shape[0]
     projected = jnp.dot(
         normed.reshape(-1, width), full_qkv, preferred_element_type=jnp.float32
     ).astype(jnp.bfloat16)
-    projected = projected.reshape(steps, zone_rows, 3 * width)
-    queries = projected[..., :width].reshape(steps, zone_rows, HEADS, head_size)
-    own_pairs = projected[..., width:]
-    earlier = []
-    for offset in range(reach, 0, -1):
-        earlier.append(shifted(own_pairs, "tm", offset))
-    all_pairs = jnp.concatenate(earlier + [own_pairs], axis=0)
-    key_count = all_pairs.shape[0]
-    keys_all = all_pairs[..., :width].reshape(key_count, zone_rows, HEADS, head_size)
-    values_all = all_pairs[..., width:].reshape(key_count, zone_rows, HEADS, head_size)
+    projected = projected.reshape(key_count, zone_rows, 3 * width)
+    queries = projected[-steps:, :, :width].reshape(steps, zone_rows, HEADS, head_size)
+    keys_all = projected[..., width : 2 * width].reshape(key_count, zone_rows, HEADS, head_size)
+    values_all = projected[..., 2 * width :].reshape(key_count, zone_rows, HEADS, head_size)
     scores = jnp.einsum(
         "tzhd,szhd->zhts", queries, keys_all, preferred_element_type=jnp.float32
     ) * head_size ** (-0.5)

time: 181 us -> 199 us (1.099)
  the two profiles are of different devices: /device:TPU:3 before, /device:TPU:0 now
where the time goes in v1:
time: 199 us
  waiting for transfers between devices  111 us (56%)
  local copies, waits for them, and re-layouts  22.6 us (11%)
  matrix products  19.6 us (10%)
  blocking collectives  16.6 us (8%)
  between operations  13.4 us (7%)
  starting transfers between devices  9.93 us (5%)
  other arithmetic  5.99 us (3%)
    all_gather x1, waiting for transfers between devices, on_device(): lax.all_gather(tm_slice(w_out, spread), ('zone', 'tm'), axis=0, tiled=True)  44.1 us
    all_gather x1, waiting for transfers between devices, on_device(): full_first = lax.all_gather(first, ('zone', 'tm'), axis=0, tiled=True)  39.4 us
    all_to_all x1, waiting for transfers between devices, on_device(): lax.all_to_all(mixin, 'zone', split_axis=1, concat_axis=2, tiled=True)  17.9 us
    all_to_all x1, blocking collectives, on_device(): lax.all_to_all(spatial, 'zone', split_axis=2, concat_axis=1, tiled=True)  16.6 us
    ppermute x2, waiting for transfers between devices, shifted(): lax.ppermute(value, axis, [(source, source + steps) for source in range(f...  9.22 us
    ppermute x2, starting transfers between devices, shifted(): lax.ppermute(value, axis, [(source, source + steps) for source in range(f...  6.37 us
    dot_general x1, matrix products, on_device(): jnp.dot(hidden, full_out, preferred_element_type=jnp.float32)  4.98 us
    unnamed x21, local copies, waits for them, and re-layouts  4.56 us
  transfers between devices with their start and end apart: 6, of which 4 were waited for; matrix products, arithmetic and copies ran while one was open for 20% of the time, Pallas kernels for 0%

profile of v1, /device:TPU:0, one launch (start us, length us, event | category | flops | bytes accessed | tf_op | source)
XLA Modules:
  0.0 198.8 jit_solution(11521089290191185315)
XLA Ops:
  9.6 4.9 %collective-permute-start = (bf16[4,128,512]{2,1,0:T(8,128)(2,1)}, bf16[4,128,512]{2,1,0:T(8,128)(2,1)S(1)}, u32[]{:S(2)}, u32[]{:S(2)}) collective-permute-start(bf16[4,128,512]{2,1,0:T(8,128)(2,1)} %param.12), channel_id=1, source_target_pairs={{0,8},{4,12},{8,16},{12,20},{16,24},{20,28},{1,9},{5,13},{9,17},{1... | collective-permute-start | bytes 1572872 | tf_op jit(solution)/shard_map/ppermute | solution.py:12
  14.5 1.5 collective-permute-start.1
  16.0 1.5 constant_dynamic-slice_fusion
  18.4 9.2 %collective-permute-done = bf16[4,128,512]{2,1,0:T(8,128)(2,1)S(1)} collective-permute-done((bf16[4,128,512]{2,1,0:T(8,128)(2,1)}, bf16[4,128,512]{2,1,0:T(8,128)(2,1)S(1)}, u32[]{:S(2)}, u32[]{:S(2)}) %collective-permute-start) | collective-permute-done | bytes 524320 | tf_op jit(solution)/shard_map/ppermute | solution.py:12
  27.6 1.4 multiply_reduce_fusion
  30.1 39.4 %all-gather.4.cloned.1.call-done = bf16[512,2048]{1,0:T(8,128)(2,1)} async-done(((bf16[16,2048]{1,0:T(8,128)(2,1)}), bf16[512,2048]{1,0:T(8,128)(2,1)}) %all-gather.4.cloned.1.call-update) | async-done | bytes 2097168 | tf_op jit(solution)/shard_map/all_gather | solution.py:44
  69.4 4.2 %convolution_convert_fusion = bf16[1536,1536]{1,0:T(8,128)(2,1)S(1)} fusion(bf16[1536,512]{1,0:T(8,128)(2,1)S(1)} %fusion.10, bf16[512,2048]{1,0:T(8,128)(2,1)} %all-gather.4.cloned.1.call-done), kind=kOutput, calls=%fused_computation.2 | convolution fusion | flops 2418278400 | bytes 7864320 | tf_op jit(solution)/shard_map/dot_general | solution.py:55
  73.6 2.0 %fusion.37 = (bf16[12,128,512]{2,1,0:T(8,128)(2,1)}, bf16[12,128,512]{2,1,0:T(8,128)(2,1)}) fusion(bf16[12,128,1536]{2,1,0:T(8,128)(2,1)S(1)} %bitcast.100), kind=kLoop, calls=%fused_computation.76 | loop fusion | bytes 6291456 | tf_op jit(solution)/shard_map/slice | solution.py:60
  75.7 1.9 copy.60
  77.6 3.0 %copy.44 = bf16[12,128,4,128]{3,0,2,1:T(8,128)(2,1)} copy(bf16[12,128,4,128]{1,3,2,0:T(8,128)(2,1)S(1)} %bitcast.98) | data formatting | bytes 3145728 | tf_op jit(solution)/shard_map/reshape | solution.py:60
  80.8 1.2 copy.43
  82.0 1.9 copy.58
  83.9 3.0 %copy.45 = bf16[12,128,4,128]{3,0,2,1:T(8,128)(2,1)} copy(bf16[12,128,4,128]{1,3,2,0:T(8,128)(2,1)S(1)} %bitcast.99) | data formatting | bytes 3145728 | tf_op jit(solution)/shard_map/reshape | solution.py:61
  86.9 4.1 %fusion.38 = (f32[128,4,4]{2,1,0:T(4,128)S(1)}, bf16[128,4,4,12]{3,2,1,0:T(4,128)(2,1)}) fusion(pred[4,12]{1,0:T(4,128)(4,1)S(1)} %fusion.30, bf16[4,128,4,128]{3,0,2,1:T(4,128)(2,1)} %copy.43, bf16[12,128,4,128]{3,0,2,1:T(8,128)(2,1)} %copy.44), kind=kOutput, calls=%fused_computation.77 | convolution fusion | flops 6438923 | bytes 2154544 | tf_op jit(solution)/shard_map/sub | solution.py:85
  91.0 2.7 %fusion.20 = bf16[4,128,4,128]{3,0,2,1:T(4,128)(2,1)} fusion(bf16[12,128,4,128]{3,0,2,1:T(8,128)(2,1)S(1)} %copy-done.2, f32[4,128,4]{0,2,1:T(4,128)S(1)} %bitcast.108, bf16[128,4,4,12]{3,2,1,0:T(4,128)(2,1)} %get-tuple-element.8), kind=kOutput, calls=%fused_computation.29 | convolution fusion | flops 6815744 | bytes 2154496 | tf_op jit(solution)/shard_map/zhts,szhd->tzhd/dot_general | solution.py:88
  93.7 1.5 copy.46
  95.2 1.6 multiply_reduce_fusion.2
  98.1 3.5 %all-to-all-start = ((bf16[4,512,128]{2,0,1:T(4,128)(2,1)}), bf16[4,512,128]{2,0,1:T(4,128)(2,1)S(1)}, u32[]{:S(2)}, u32[]{:S(2)}) async-start(bf16[4,512,128]{2,0,1:T(4,128)(2,1)} %copy.48), calls=%async_computation | async-start | bytes 1048576 | tf_op jit(solution)/shard_map/all_to_all | solution.py:100
  101.8 17.9 %all-to-all-done = bf16[4,512,128]{2,0,1:T(4,128)(2,1)S(1)} async-done(((bf16[4,512,128]{2,0,1:T(4,128)(2,1)}), bf16[4,512,128]{2,0,1:T(4,128)(2,1)S(1)}, u32[]{:S(2)}, u32[]{:S(2)}) %all-to-all-start) | async-done | bytes 524320 | tf_op jit(solution)/shard_map/all_to_all | solution.py:100
  119.7 2.0 gather_fusion
  121.7 2.0 %fusion.21 = bf16[4,128,4,128]{1,3,0,2:T(8,128)(2,1)S(1)} fusion(bf16[4,128,4,3,128]{4,1,0,3,2:T(8,128)(2,1)} %bitcast.94, bf16[4,3,128,128]{3,2,1,0:T(8,128)(2,1)S(1)} %copy-done.3, pred[4,3]{1,0:T(4,128)(4,1)S(1)} %iota_compare_fusion), kind=kOutput, calls=%fused_computation.30 | convolution fusion | flops 201785344 | bytes 2490380 | tf_op jit(solution)/shard_map/ncbky,bkzy->ncbz/dot_general | solution.py:105
  124.2 16.6 %all_to_all.24 = bf16[4,128,512]{1,0,2:T(4,128)(2,1)S(1)} all-to-all(bf16[4,128,512]{1,0,2:T(4,128)(2,1)S(1)} %copy.52), channel_id=1, replica_groups=mesh['tm'=8,'zone'=4] {'zone'}, dimensions={2} | all-to-all | bytes 1048576 | tf_op jit(solution)/shard_map/all_to_all | solution.py:107
  142.1 44.1 %all-gather.8.cloned.1.call-done = bf16[2048,512]{1,0:T(8,128)(2,1)} async-done(((bf16[64,512]{1,0:T(8,128)(2,1)}), bf16[2048,512]{1,0:T(8,128)(2,1)}) %all-gather.8.cloned.1.call-update) | async-done | bytes 2097168 | tf_op jit(solution)/shard_map/all_gather | solution.py:47
  186.2 5.0 %fusion.11 = f32[512,512]{1,0:T(8,128)S(1)} fusion(bf16[2048,512]{1,0:T(8,128)(2,1)} %all-gather.8.cloned.1.call-done, bf16[512,512]{1,0:T(8,128)(2,1)} %bitcast.106, bf16[512,2048]{1,0:T(8,128)(2,1)} %all-gather.6.cloned.1.call-done), kind=kOutput, calls=%fused_computation.16 | convolution fusion | flops 2156920832 | bytes 5767168 | tf_op jit(solution)/shard_map/dot_general | solution.py:113
  (56 shorter events, 9.5 us)
Async XLA Ops:
  6.5 2.3 %copy-start = (bf16[128,2048]{1,0:T(8,128)(2,1)S(1)}, bf16[128,2048]{1,0:T(8,128)(2,1)}, u32[]{:S(2)}) copy-start(bf16[128,2048]{1,0:T(8,128)(2,1)} %param.22) | copy-start | bytes 1572868
  6.5 22.5 %copy-start.1 = (bf16[4,128,512]{2,1,0:T(8,128)(2,1)S(1)}, bf16[4,128,512]{2,1,0:T(8,128)(2,1)}, u32[]{:S(2)}) copy-start(bf16[4,128,512]{2,1,0:T(8,128)(2,1)} %param.12) | copy-start | bytes 1572868
  6.5 62.9 %all-gather.4.cloned.1.call-start = ((), (), s32[]{:S(2)}) async-start(), calls=%async_computation.2 | async-start | bytes 2162688 | tf_op jit(solution)/shard_map/all_gather | solution.py:44
  8.8 133.3 %all-gather.6.cloned.1.call-start = ((), (), s32[]{:S(2)}) async-start(), calls=%async_computation.3 | async-start | bytes 2162688 | tf_op jit(solution)/shard_map/all_gather | solution.py:46
  9.6 176.6 %all-gather.8.cloned.1.call-start = ((), (), s32[]{:S(2)}) async-start(), calls=%async_computation.4 | async-start | bytes 2162688 | tf_op jit(solution)/shard_map/all_gather | solution.py:47
  9.6 18.0 %collective-permute-start = (bf16[4,128,512]{2,1,0:T(8,128)(2,1)}, bf16[4,128,512]{2,1,0:T(8,128)(2,1)S(1)}, u32[]{:S(2)}, u32[]{:S(2)}) collective-permute-start(bf16[4,128,512]{2,1,0:T(8,128)(2,1)} %param.12), channel_id=1, source_target_pairs={{0,8},{4,12},{8,16},{12,20},{16,24},{20,28},{1,9},{5,13},{9,17},{1... | collective-permute-start | bytes 1572872 | tf_op jit(solution)/shard_map/ppermute | solution.py:12
  14.5 13.1 %collective-permute-start.1 = (bf16[4,128,512]{2,1,0:T(8,128)(2,1)}, bf16[4,128,512]{2,1,0:T(8,128)(2,1)S(1)}, u32[]{:S(2)}, u32[]{:S(2)}) collective-permute-start(bf16[4,128,512]{2,1,0:T(8,128)(2,1)} %param.12), channel_id=1, source_target_pairs={{0,4},{4,8},{8,12},{12,16},{16,20},{20,24},{24,28},{1,5},{5,9},{9,... | collective-permute-start | bytes 1572872 | tf_op jit(solution)/shard_map/ppermute | solution.py:12
  29.0 0.7 copy-start.4
  86.9 4.1 %copy-start.2 = (bf16[12,128,4,128]{3,0,2,1:T(8,128)(2,1)S(1)}, bf16[12,128,4,128]{3,0,2,1:T(8,128)(2,1)}, u32[]{:S(2)}) copy-start(bf16[12,128,4,128]{3,0,2,1:T(8,128)(2,1)} %copy.45) | copy-start | bytes 4718596
  93.7 3.2 %copy-start.5 = (f32[512]{0:T(512)S(1)}, f32[512]{0:T(512)}, u32[]{:S(2)}) copy-start(f32[512]{0:T(512)} %param.17) | copy-start | bytes 6148
  96.8 4.7 %copy-start.6 = (s32[4,3]{1,0:T(4,128)S(1)}, s32[4,3]{1,0:T(4,128)}, u32[]{:S(2)}) copy-start(s32[4,3]{1,0:T(4,128)} %param.18) | copy-start | bytes 148
  96.8 4.9 %copy-start.8 = (s32[4]{0:T(128)S(1)}, s32[4]{0:T(128)}, u32[]{:S(2)}) copy-start(s32[4]{0:T(128)} %param.19) | copy-start | bytes 52
  98.1 21.5 %all-to-all-start = ((bf16[4,512,128]{2,0,1:T(4,128)(2,1)}), bf16[4,512,128]{2,0,1:T(4,128)(2,1)S(1)}, u32[]{:S(2)}, u32[]{:S(2)}) async-start(bf16[4,512,128]{2,0,1:T(4,128)(2,1)} %copy.48), calls=%async_computation | async-start | bytes 1048576 | tf_op jit(solution)/shard_map/all_to_all | solution.py:100
  119.7 2.0 copy-start.3
  124.2 16.9 %copy-start.7 = (f32[512]{0:T(512)S(1)}, f32[512]{0:T(512)}, u32[]{:S(2)}) copy-start(f32[512]{0:T(512)} %param.21) | copy-start | bytes 6148
Sparse Core Ops, SparseCore 0:
  10.2 59.1 all-gather.3
  72.3 55.8 all-gather.5
  131.0 55.0 all-gather.7

commit v2 on v0

v2 whole, which is shorter than its diff:
```python
import functools

import jax
import jax.numpy as jnp
from jax import lax
from jax.experimental import pallas as pl
from jax.experimental.pallas import tpu as pltpu
from jax.sharding import PartitionSpec as P

HEADS = 4
SPREAD = 8
LANES = 128
F32 = jnp.float32
BF16 = jnp.bfloat16
VMEM_LIMIT = 48 * 1024 * 1024


def shifted(value, axis, steps):
    count = lax.axis_size(axis)
    return lax.ppermute(value, axis, [(source, source + steps) for source in range(count - steps)])


def rotated(value, axis, steps):
    count = lax.axis_size(axis)
    return lax.ppermute(value, axis, [(source, (source + steps) % count) for source in range(count)])


def swapped(value, axis, bits):
    count = lax.axis_size(axis)
    return lax.ppermute(value, axis, [(source, source ^ bits) for source in range(count)])


def rms_scale(values, gain):
    mean_sq = jnp.mean(values * values, axis=-1, keepdims=True)
    return values * lax.rsqrt(mean_sq + 1e-06) * gain


def row_sum(value):
    return jnp.sum(value, axis=0, keepdims=True)


def attention_kernel(zones, reach, place, pattern, states, *refs):
    earlier, refs = refs[:reach], refs[reach:]
    (gain_attn, gain_mix, own_qkv, own_attn), refs = refs[:4], refs[4:]
    direct, refs = refs[: zones - 1], refs[zones - 1 :]
    partner, refs = refs[: zones - 1], refs[zones - 1 :]
    after_out, mixin_out, w_qkv, w_attn, w_turned, normed, projected, context = refs
    steps, zone_rows, width = states.shape
    head_size = width // HEADS
    key_count = (reach + 1) * steps
    my_block, my_zone = place[0], place[1]
    my_half = lax.rem(my_block, 2)
    shard = own_qkv.shape[0]
    half = shard // 2

    def put(rows, qkv, attn):
        w_qkv[rows, :] = qkv
        w_attn[rows, :] = attn

    put(pl.ds(pl.multiple_of(my_zone * shard, shard), shard), own_qkv[...], own_attn[...])
    for step in range(1, zones):
        source = lax.rem(my_zone - step + zones, zones)
        for pieces, which in ((direct, my_half), (partner, 1 - my_half)):
            start = pl.multiple_of(source * shard + which * half, half)
            piece = pieces[step - 1]
            put(pl.ds(start, half), piece[:, : 3 * width], piece[:, 3 * width :])
    for block in range(3 * width // LANES):
        cols = slice(block * LANES, (block + 1) * LANES)
        w_turned[cols, :] = w_qkv[:, cols].T

    blocks = list(earlier) + [states]
    gain = gain_attn[...]
    for index, block in enumerate(blocks):
        for step in range(steps):
            row = (index * steps + step) * zone_rows
            normed[row : row + zone_rows, :] = rms_scale(block[step].astype(F32), gain).astype(BF16)

    def project(first, last, weight_rows):
        return lax.dot_general(
            w_turned[weight_rows, :],
            normed[first:last, :],
            (((1,), (1,)), ((), ())),
            preferred_element_type=F32,
        ).astype(BF16).astype(F32)

    span = 2 * zone_rows
    for first in range(0, key_count * zone_rows, span):
        own = first >= reach * steps * zone_rows
        rows = slice(0 if own else width, 3 * width)
        projected[rows, first : first + span] = project(first, first + span, rows)

    allowed_back = [
        (pattern[0, back - 1] == 1) & (my_block >= back) for back in range(reach, 0, -1)
    ]
    chunks = head_size // 8

    def usable(query):
        return range(reach * steps + query + 1)

    def head_body(head, carry):
        base = head * head_size

        def tile(kind, chunk, key):
            row = pl.multiple_of(kind * width + base + chunk * 8, 8)
            return projected[pl.ds(row, 8), key * zone_rows : (key + 1) * zone_rows]

        for pair in range(0, steps, 2):
            queries = range(pair, min(pair + 2, steps))
            sums = {}
            for chunk in range(chunks):
                q_tiles = {q: tile(0, chunk, reach * steps + q) for q in queries}
                for key in usable(queries[-1]):
                    k_tile = tile(1, chunk, key)
                    for q in queries:
                        if key in usable(q):
                            term = q_tiles[q] * k_tile
                            sums[q, key] = term if chunk == 0 else sums[q, key] + term
            weights, scales = {}, {}
            for q in queries:
                scores = jnp.concatenate([row_sum(sums[q, key]) for key in usable(q)], axis=0)
                scores = scores * head_size ** (-0.5)
                row_id = lax.broadcasted_iota(jnp.int32, scores.shape, 0)
                allowed = row_id >= reach * steps
                for index, live in enumerate(allowed_back):
                    inside = (row_id >= index * steps) & (row_id < (index + 1) * steps)
                    allowed = allowed | (inside & live)
                masked = jnp.where(allowed, scores, -1e30)
                top = jnp.max(masked, axis=0, keepdims=True)
                expw = jnp.where(allowed, jnp.exp(masked - top), 0.0)
                scales[q] = jnp.broadcast_to(1.0 / row_sum(expw), (8, zone_rows))
                probs = expw.astype(BF16).astype(F32)
                for key in usable(q):
                    weights[q, key] = jnp.broadcast_to(probs[key : key + 1, :], (8, zone_rows))
            for chunk in range(chunks):
                sums = {}
                for key in usable(queries[-1]):
                    v_tile = tile(2, chunk, key)
                    for q in queries:
                        if key in usable(q):
                            term = weights[q, key] * v_tile
                            sums[q] = term if key == 0 else sums[q] + term
                for q in queries:
                    row = pl.multiple_of(base + chunk * 8, 8)
                    context[pl.ds(row, 8), q * zone_rows : (q + 1) * zone_rows] = sums[q] * scales[q]
        return carry

    lax.fori_loop(0, HEADS, head_body, 0)

    mix_gain = gain_mix[...]
    for step in range(steps):
        rows = slice(step * zone_rows, (step + 1) * zone_rows)
        turned = context[:, rows].T.astype(BF16)
        after = states[step].astype(F32) + jnp.dot(turned, w_attn[...], preferred_element_type=F32)
        after_out[rows, :] = after
        mixin = rms_scale(after, mix_gain).astype(BF16)
        if len(mixin_out.shape) == 2:
            mixin_out[rows, :] = mixin
        else:
            part = mixin_out.shape[-1]
            for index in range(mixin_out.shape[0]):
                mixin_out[index, rows, :] = mixin[:, index * part : (index + 1) * part]


def mixing_kernel(steps, neighbours, degree, mix, items, out):
    block_count, slots, zone_rows, _ = mix.shape
    part = items.shape[-1]
    group = 2 if part % LANES == 0 and steps % 2 == 0 else 1

    def block_body(block, carry):
        left = []
        for slot in range(slots):
            tile = mix[block, slot]
            left.append(jnp.where(degree[block] > slot, tile, jnp.zeros_like(tile)))
        left = jnp.concatenate(left, axis=1)
        for step in range(0, steps, group):
            right = []
            for slot in range(slots):
                source = neighbours[block, slot]
                right.append(
                    jnp.concatenate(
                        [
                            items[source, (step + index) * zone_rows : (step + index + 1) * zone_rows, :]
                            for index in range(group)
                        ],
                        axis=1,
                    )
                )
            result = jnp.dot(left, jnp.concatenate(right, axis=0), preferred_element_type=F32)
            for index in range(group):
                rows = slice((step + index) * zone_rows, (step + index + 1) * zone_rows)
                out[block, rows, :] = result[:, index * part : (index + 1) * part].astype(BF16)
        return carry

    lax.fori_loop(0, block_count, block_body, 0)


def ffn_kernel(zones, place, spatial, after_attn, gain_ffn, own_in, own_out, *refs):
    pieces, (out, w_in, w_out, after_mix, ffn_in) = refs[:SPREAD], refs[SPREAD:]
    rows_all, width = after_attn.shape
    my_block, my_zone = place[0], place[1]
    in_shard, hidden = own_in.shape
    out_shard = own_out.shape[0]
    in_cols, out_rows = hidden // SPREAD, out_shard // SPREAD
    folds = width // in_cols

    start = pl.multiple_of(my_zone * in_shard, in_shard)
    for index in range(SPREAD):
        w_in[index, pl.ds(start, in_shard), :] = own_in[:, index * in_cols : (index + 1) * in_cols]
    w_out[pl.ds(pl.multiple_of(my_zone * out_shard, out_shard), out_shard), :] = own_out[...]
    for bits in range(SPREAD):
        slot = lax.rem(my_block, SPREAD) ^ bits
        for step in range(1, zones):
            source = lax.rem(my_zone - step + zones, zones)
            piece = pieces[bits]
            w_in[slot, pl.ds(pl.multiple_of(source * in_shard, in_shard), in_shard), :] = piece[
                step - 1, :in_shard, :
            ]
            start = pl.multiple_of(source * out_shard + slot * out_rows, out_rows)
            for fold in range(folds):
                first = in_shard + fold * out_rows
                w_out[pl.ds(start, out_rows), fold * in_cols : (fold + 1) * in_cols] = piece[
                    step - 1, first : first + out_rows, :
                ]

    gain = gain_ffn[...]
    span = 128
    for first in range(0, rows_all, span):
        rows = slice(first, first + span)
        if len(spatial.shape) == 2:
            moved = spatial[rows, :]
        else:
            moved = jnp.concatenate([spatial[index, rows, :] for index in range(spatial.shape[0])], axis=1)
        total = after_attn[rows, :] + moved.astype(F32)
        after_mix[rows, :] = total
        ffn_in[rows, :] = rms_scale(total, gain).astype(BF16)
    span = 256
    for first in range(0, rows_all, span):
        rows = slice(first, first + span)
        total = after_mix[rows, :]
        for index in range(SPREAD):
            hidden_part = jnp.dot(ffn_in[rows, :], w_in[index], preferred_element_type=F32)
            hidden_part = jax.nn.gelu(hidden_part, approximate=True).astype(BF16)
            total = total + jnp.dot(
                hidden_part,
                w_out[index * in_cols : (index + 1) * in_cols, :],
                preferred_element_type=F32,
            )
        out[rows, :] = total.astype(BF16)


def call(kernel, out_shape, scratch, flops, smem, args):
    in_specs = [
        pl.BlockSpec(memory_space=pltpu.SMEM if index in smem else pltpu.VMEM)
        for index in range(len(args))
    ]
    moved = sum(arg.size * arg.dtype.itemsize for arg in args)
    return pl.pallas_call(
        kernel,
        out_shape=out_shape,
        in_specs=in_specs,
        out_specs=jax.tree.map(lambda _: pl.BlockSpec(memory_space=pltpu.VMEM), out_shape),
        scratch_shapes=scratch,
        cost_estimate=pl.CostEstimate(flops=flops, bytes_accessed=moved, transcendentals=0),
        compiler_params=pltpu.CompilerParams(vmem_limit_bytes=VMEM_LIMIT),
    )(*args)


def on_device(
    states,
    gain_attn,
    w_qkv,
    w_out_attn,
    pattern,
    gain_mix,
    neighbours,
    degree,
    mix,
    gain_ffn,
    w_in,
    w_out,
):
    steps, zone_rows, width = states.shape
    rows = steps * zone_rows
    reach = pattern.shape[1]
    zones = lax.axis_size("zone")
    my_block, my_zone = lax.axis_index("tm"), lax.axis_index("zone")
    place = jnp.stack([my_block, my_zone]).astype(jnp.int32)
    key_count = (reach + 1) * steps

    half = w_qkv.shape[0] // 2
    first = lax.dynamic_slice_in_dim(
        jnp.concatenate([w_qkv, w_out_attn], axis=1), (my_block % 2) * half, half, axis=0
    )
    direct = [rotated(first, "zone", step) for step in range(1, zones)]
    earlier = [shifted(states, "tm", offset) for offset in range(reach, 0, -1)]
    partner = [swapped(piece, "tm", 1) for piece in direct]

    in_cols = w_in.shape[1] // SPREAD
    out_rows = w_out.shape[0] // SPREAD
    slot = my_block % SPREAD
    out_slice = lax.dynamic_slice_in_dim(w_out, slot * out_rows, out_rows, axis=0)
    second = jnp.concatenate(
        [lax.dynamic_slice_in_dim(w_in, slot * in_cols, in_cols, axis=1)]
        + [out_slice[:, at : at + in_cols] for at in range(0, width, in_cols)],
        axis=0,
    )
    across = jnp.stack([rotated(second, "zone", step) for step in range(1, zones)])
    pieces = {0: across}
    for bits in range(2, SPREAD, 2):
        pieces[bits] = swapped(across, "tm", bits)
    for bits in range(0, SPREAD, 2):
        pieces[bits + 1] = swapped(pieces[bits], "tm", 1)

    part = width // zones
    wide = part % LANES == 0
    mixin_shape = (zones, rows, part) if wide else (rows, width)
    after_attn, mixin = call(
        functools.partial(attention_kernel, zones, reach),
        (jax.ShapeDtypeStruct((rows, width), F32), jax.ShapeDtypeStruct(mixin_shape, BF16)),
        [
            pltpu.VMEM((width, 3 * width), BF16),
            pltpu.VMEM((width, width), BF16),
            pltpu.VMEM((3 * width, width), BF16),
            pltpu.VMEM((key_count * zone_rows, width), BF16),
            pltpu.VMEM((3 * width, key_count * zone_rows), F32),
            pltpu.VMEM((width, rows), F32),
        ],
        2 * rows * width * width * 10,
        (0, 1),
        [place, pattern, states]
        + earlier
        + [gain_attn.reshape(1, -1), gain_mix.reshape(1, -1), w_qkv, w_out_attn]
        + direct
        + partner,
    )
    if not wide:
        mixin = jnp.transpose(mixin.reshape(rows, zones, part), (1, 0, 2))
    items = lax.all_to_all(mixin, "zone", split_axis=0, concat_axis=0, tiled=True)
    spatial = call(
        functools.partial(mixing_kernel, steps),
        jax.ShapeDtypeStruct((zones, rows, part), BF16),
        [],
        2 * rows * width * zone_rows * 3,
        (0, 1),
        [neighbours, degree, mix, items],
    )
    spatial = lax.all_to_all(spatial, "zone", split_axis=0, concat_axis=0, tiled=True)
    if not wide:
        spatial = jnp.transpose(spatial, (1, 0, 2)).reshape(rows, width)
    hidden = w_in.shape[1]
    evolved = call(
        functools.partial(ffn_kernel, zones),
        jax.ShapeDtypeStruct((rows, width), BF16),
        [
            pltpu.VMEM((SPREAD, width, in_cols), BF16),
            pltpu.VMEM((hidden, width), BF16),
            pltpu.VMEM((rows, width), F32),
            pltpu.VMEM((rows, width), BF16),
        ],
        4 * rows * width * hidden,
        (0,),
        [place, spatial, after_attn, gain_ffn.reshape(1, -1), w_in, w_out]
        + [pieces[bits] for bits in range(SPREAD)],
    )
    return evolved.reshape(steps, zone_rows, width)


def solution(mesh):
    return jax.shard_map(
        on_device,
        mesh=mesh,
        in_specs=(
            P("tm", "zone", None),
            P(),
            P("zone", None),
            P("zone", None),
            P("tm", None),
            P(),
            P(),
            P(),
            P(),
            P(),
            P("zone", None),
            P("zone", None),
        ),
        out_specs=P("tm", "zone", None),
        check_vma=False,
    )
```

time: 181 us -> 99.3 us (0.55)
  the two profiles are of different devices: /device:TPU:3 before, /device:TPU:0 now
where the time goes in v2:
time: 99.3 us; the launch traced here: 98.8 us
  waiting for transfers between devices  39 us (39%)
  starting transfers between devices  36.9 us (37%)
  Pallas kernels  12.5 us (13%)
  local copies, waits for them, and re-layouts  9.14 us (9%)
  other arithmetic  1.15 us (1%)
    ppermute x6, waiting for transfers between devices, rotated(): lax.ppermute(value, axis, [(source, (source + steps) % count) for source...  27.6 us
    ppermute x6, starting transfers between devices, rotated(): lax.ppermute(value, axis, [(source, (source + steps) % count) for source...  12.9 us
    pallas_call x3, Pallas kernels, call(): pl.pallas_call(kernel, out_shape=out_shape, in_specs=in_specs, out_specs=...  12.5 us
    ppermute x10, waiting for transfers between devices, swapped(): lax.ppermute(value, axis, [(source, source ^ bits) for source in range(co...  10.2 us
    unnamed x40, local copies, waits for them, and re-layouts  9.12 us
    all_to_all x1, starting transfers between devices, on_device(): lax.all_to_all(mixin, 'zone', split_axis=0, concat_axis=0, tiled=True)  8.51 us
    ppermute x10, starting transfers between devices, swapped(): lax.ppermute(value, axis, [(source, source ^ bits) for source in range(co...  6.21 us
    ppermute x2, starting transfers between devices, shifted(): lax.ppermute(value, axis, [(source, source + steps) for source in range(c...  4.74 us
  transfers between devices with their start and end apart: 20, of which 10 were waited for; matrix products, arithmetic and copies ran while one was open for 0% of the time, Pallas kernels for 2%

profile of v2, /device:TPU:0, one launch (start us, length us, event | category | flops | bytes accessed | tf_op | source)
XLA Modules:
  0.0 98.8 jit_solution(14783369864398924477)
XLA Ops:
  1.0 3.1 %collective-permute-start.2 = (bf16[64,2048]{1,0:T(8,128)(2,1)S(1)}, bf16[64,2048]{1,0:T(8,128)(2,1)S(1)}, u32[]{:S(2)}, u32[]{:S(2)}) collective-permute-start(bf16[64,2048]{1,0:T(8,128)(2,1)S(1)} %fusion), channel_id=1, source_target_pairs={{0,1},{1,2},{2,3},{3,0},{4,5},{5,6},{6,7},{7,4},{8,9},{9,10},{10,1... | collective-permute-start | bytes 786440 | tf_op jit(solution)/shard_map/ppermute | solution.py:25
  4.1 2.6 %collective-permute-start.3 = (bf16[64,2048]{1,0:T(8,128)(2,1)S(1)}, bf16[64,2048]{1,0:T(8,128)(2,1)S(1)}, u32[]{:S(2)}, u32[]{:S(2)}) collective-permute-start(bf16[64,2048]{1,0:T(8,128)(2,1)S(1)} %fusion), channel_id=1, source_target_pairs={{0,2},{1,3},{2,0},{3,1},{4,6},{5,7},{6,4},{7,5},{8,10},{9,11},{10,... | collective-permute-start | bytes 786440 | tf_op jit(solution)/shard_map/ppermute | solution.py:25
  6.7 1.3 %collective-permute-start.4 = (bf16[64,2048]{1,0:T(8,128)(2,1)S(1)}, bf16[64,2048]{1,0:T(8,128)(2,1)S(1)}, u32[]{:S(2)}, u32[]{:S(2)}) collective-permute-start(bf16[64,2048]{1,0:T(8,128)(2,1)S(1)} %fusion), channel_id=1, source_target_pairs={{0,3},{1,0},{2,1},{3,2},{4,7},{5,4},{6,5},{7,6},{8,11},{9,8},{10,9... | collective-permute-start | bytes 786440 | tf_op jit(solution)/shard_map/ppermute | solution.py:25
  8.0 3.4 %collective-permute-start = (bf16[4,128,512]{2,1,0:T(8,128)(2,1)}, bf16[4,128,512]{2,1,0:T(8,128)(2,1)S(1)}, u32[]{:S(2)}, u32[]{:S(2)}) collective-permute-start(bf16[4,128,512]{2,1,0:T(8,128)(2,1)} %states.1), channel_id=1, source_target_pairs={{0,8},{4,12},{8,16},{12,20},{16,24},{20,28},{1,9},{5,13},{9,17},{1... | collective-permute-start | bytes 1572872 | tf_op jit(solution)/shard_map/ppermute | solution.py:20
  11.5 1.3 %collective-permute-start.1 = (bf16[4,128,512]{2,1,0:T(8,128)(2,1)}, bf16[4,128,512]{2,1,0:T(8,128)(2,1)S(1)}, u32[]{:S(2)}, u32[]{:S(2)}) collective-permute-start(bf16[4,128,512]{2,1,0:T(8,128)(2,1)} %states.1), channel_id=1, source_target_pairs={{0,4},{4,8},{8,12},{12,16},{16,20},{20,24},{24,28},{1,5},{5,9},{9,... | collective-permute-start | bytes 1572872 | tf_op jit(solution)/shard_map/ppermute | solution.py:20
  13.4 1.6 %collective-permute-start.5 = (bf16[64,2048]{1,0:T(8,128)(2,1)S(1)}, bf16[64,2048]{1,0:T(8,128)(2,1)S(1)}, u32[]{:S(2)}, u32[]{:S(2)}) collective-permute-start(bf16[64,2048]{1,0:T(8,128)(2,1)S(1)} %collective-permute-done.2.refs_6_), channel_id=1, source_target_pairs={{0,4},{4,0},{8,12},{12,8},{16,20},{20,16},{24,28},{28,24},{1,5},{5... | collective-permute-start | bytes 786440 | tf_op jit(solution)/shard_map/ppermute | solution.py:30
  15.0 8.8 %collective-permute-done.3.refs_7_ = bf16[64,2048]{1,0:T(8,128)(2,1)S(1)} collective-permute-done((bf16[64,2048]{1,0:T(8,128)(2,1)S(1)}, bf16[64,2048]{1,0:T(8,128)(2,1)S(1)}, u32[]{:S(2)}, u32[]{:S(2)}) %collective-permute-start.3) | collective-permute-done | bytes 262176 | tf_op jit(solution)/shard_map/ppermute | solution.py:25
  26.4 1.0 %copy-done.7 = bf16[4,128,512]{2,1,0:T(8,128)(2,1)S(1)} copy-done((bf16[4,128,512]{2,1,0:T(8,128)(2,1)S(1)}, bf16[4,128,512]{2,1,0:T(8,128)(2,1)}, u32[]{:S(2)}) %copy-start.7) | copy-done | bytes 524312
  27.4 6.0 %shard_map.118 = (f32[512,512]{1,0:T(8,128)S(1)}, bf16[4,512,128]{2,1,0:T(8,128)(2,1)}) custom-call(s32[2]{0:T(128)S(1)} %pad_add_fusion.place, s32[1,2]{1,0:T(1,128)S(1)} %copy-done.17, bf16[4,128,512]{2,1,0:T(8,128)(2,1)S(1)} %copy-done.7, bf16[4,128,512]{2,1,0:T(8,128)(2,1)S(1)} %collective-permute-done.refs_0_, ...), custom_call_target="tpu_custom_call" | custom-call | flops 2684354560 | bytes 3674128 | tf_op jit(solution)/shard_map/pallas_call | solution.py:257
  34.4 8.5 %all-to-all-start = ((bf16[4,512,128]{2,1,0:T(8,128)(2,1)}), bf16[4,512,128]{2,1,0:T(8,128)(2,1)S(1)}, u32[]{:S(2)}, u32[]{:S(2)}) async-start(bf16[4,512,128]{2,1,0:T(8,128)(2,1)} %get-tuple-element.7), calls=%async_computation | async-start | bytes 1048576 | tf_op jit(solution)/shard_map/all_to_all | solution.py:338
  43.0 2.1 %collective-permute-start.8 = (bf16[256,256]{1,0:T(8,128)(2,1)S(1)}, bf16[256,256]{1,0:T(8,128)(2,1)S(1)}, u32[]{:S(2)}, u32[]{:S(2)}) collective-permute-start(bf16[256,256]{1,0:T(8,128)(2,1)S(1)} %pad_maximum_fusion.1), channel_id=1, source_target_pairs={{0,1},{1,2},{2,3},{3,0},{4,5},{5,6},{6,7},{7,4},{8,9},{9,10},{10,1... | collective-permute-start | bytes 393224 | tf_op jit(solution)/shard_map/ppermute | solution.py:25
  45.1 2.4 %collective-permute-start.9 = (bf16[256,256]{1,0:T(8,128)(2,1)S(1)}, bf16[256,256]{1,0:T(8,128)(2,1)S(1)}, u32[]{:S(2)}, u32[]{:S(2)}) collective-permute-start(bf16[256,256]{1,0:T(8,128)(2,1)S(1)} %pad_maximum_fusion.1), channel_id=1, source_target_pairs={{0,2},{1,3},{2,0},{3,1},{4,6},{5,7},{6,4},{7,5},{8,10},{9,11},{10,... | collective-permute-start | bytes 393224 | tf_op jit(solution)/shard_map/ppermute | solution.py:25
  47.5 1.5 %collective-permute-start.10 = (bf16[256,256]{1,0:T(8,128)(2,1)S(1)}, bf16[256,256]{1,0:T(8,128)(2,1)S(1)}, u32[]{:S(2)}, u32[]{:S(2)}) collective-permute-start(bf16[256,256]{1,0:T(8,128)(2,1)S(1)} %pad_maximum_fusion.1), channel_id=1, source_target_pairs={{0,3},{1,0},{2,1},{3,2},{4,7},{5,4},{6,5},{7,6},{8,11},{9,8},{10,9... | collective-permute-start | bytes 393224 | tf_op jit(solution)/shard_map/ppermute | solution.py:25
  48.9 10.9 %collective-permute-done.8 = bf16[256,256]{1,0:T(8,128)(2,1)S(1)} collective-permute-done((bf16[256,256]{1,0:T(8,128)(2,1)S(1)}, bf16[256,256]{1,0:T(8,128)(2,1)S(1)}, u32[]{:S(2)}, u32[]{:S(2)}) %collective-permute-start.8) | collective-permute-done | bytes 131104 | tf_op jit(solution)/shard_map/ppermute | solution.py:25
  59.9 7.3 %collective-permute-done.9 = bf16[256,256]{1,0:T(8,128)(2,1)S(1)} collective-permute-done((bf16[256,256]{1,0:T(8,128)(2,1)S(1)}, bf16[256,256]{1,0:T(8,128)(2,1)S(1)}, u32[]{:S(2)}, u32[]{:S(2)}) %collective-permute-start.9) | collective-permute-done | bytes 131104 | tf_op jit(solution)/shard_map/ppermute | solution.py:25
  67.2 1.6 %collective-permute-start.12 = (bf16[3,256,256]{2,1,0:T(8,128)(2,1)S(1)}, bf16[3,256,256]{2,1,0:T(8,128)(2,1)S(1)}, u32[]{:S(2)}, u32[]{:S(2)}) collective-permute-start(bf16[3,256,256]{2,1,0:T(8,128)(2,1)S(1)} %pad_maximum_fusion.refs_0_), channel_id=1, source_target_pairs={{0,8},{4,12},{8,0},{12,4},{16,24},{20,28},{24,16},{28,20},{1,9},{5... | collective-permute-start | bytes 1179656 | tf_op jit(solution)/shard_map/ppermute | solution.py:30
  68.8 1.5 %collective-permute-start.14 = (bf16[3,256,256]{2,1,0:T(8,128)(2,1)S(1)}, bf16[3,256,256]{2,1,0:T(8,128)(2,1)S(1)}, u32[]{:S(2)}, u32[]{:S(2)}) collective-permute-start(bf16[3,256,256]{2,1,0:T(8,128)(2,1)S(1)} %pad_maximum_fusion.refs_0_), channel_id=1, source_target_pairs={{0,16},{4,20},{8,24},{12,28},{16,0},{20,4},{24,8},{28,12},{1,17},{... | collective-permute-start | bytes 1179656 | tf_op jit(solution)/shard_map/ppermute | solution.py:30
  70.8 2.3 %shard_map.119 = bf16[4,512,128]{2,1,0:T(8,128)(2,1)} custom-call(s32[4,3]{1,0:T(4,128)S(1)} %copy-done.5, s32[4]{0:T(128)S(1)} %copy-done.6, bf16[4,3,128,128]{3,2,1,0:T(8,128)(2,1)S(1)} %copy-done.1, bf16[4,512,128]{2,1,0:T(8,128)(2,1)S(1)} %all-to-all-done.items), custom_call_target="tpu_custom_call" | custom-call | flops 201326592 | bytes 917568 | tf_op jit(solution)/shard_map/pallas_call | solution.py:257
  73.1 4.5 %all-to-all-start.1 = ((bf16[4,512,128]{2,1,0:T(8,128)(2,1)}), bf16[4,512,128]{2,1,0:T(8,128)(2,1)S(1)}, u32[]{:S(2)}, u32[]{:S(2)}) async-start(bf16[4,512,128]{2,1,0:T(8,128)(2,1)} %shard_map.119), calls=%async_computation.1 | async-start | bytes 1048576 | tf_op jit(solution)/shard_map/all_to_all | solution.py:347
  77.7 1.7 %collective-permute-done.12.refs_2_ = bf16[3,256,256]{2,1,0:T(8,128)(2,1)S(1)} collective-permute-done((bf16[3,256,256]{2,1,0:T(8,128)(2,1)S(1)}, bf16[3,256,256]{2,1,0:T(8,128)(2,1)S(1)}, u32[]{:S(2)}, u32[]{:S(2)}) %collective-permute-start.12) | collective-permute-done | bytes 393248 | tf_op jit(solution)/shard_map/ppermute | solution.py:30
  79.4 6.7 %collective-permute-done.14.refs_4_ = bf16[3,256,256]{2,1,0:T(8,128)(2,1)S(1)} collective-permute-done((bf16[3,256,256]{2,1,0:T(8,128)(2,1)S(1)}, bf16[3,256,256]{2,1,0:T(8,128)(2,1)S(1)}, u32[]{:S(2)}, u32[]{:S(2)}) %collective-permute-start.14) | collective-permute-done | bytes 393248 | tf_op jit(solution)/shard_map/ppermute | solution.py:30
  89.3 1.2 %all-to-all-done.1.spatial = bf16[4,512,128]{2,1,0:T(8,128)(2,1)S(1)} async-done(((bf16[4,512,128]{2,1,0:T(8,128)(2,1)}), bf16[4,512,128]{2,1,0:T(8,128)(2,1)S(1)}, u32[]{:S(2)}, u32[]{:S(2)}) %all-to-all-start.1) | async-done | bytes 524320 | tf_op jit(solution)/shard_map/all_to_all | solution.py:347
  93.5 1.2 %copy-done.19 = f32[512,512]{1,0:T(8,128)S(1)} copy-done((f32[512,512]{1,0:T(8,128)S(1)}, f32[512,512]{1,0:T(8,128)}, u32[]{:S(2)}) %copy-start.19) | copy-done | bytes 1048600
  94.7 4.2 %shard_map.120 = bf16[512,512]{1,0:T(8,128)(2,1)} custom-call(s32[2]{0:T(128)S(1)} %pad_add_fusion.place, bf16[4,512,128]{2,1,0:T(8,128)(2,1)S(1)} %all-to-all-done.1.spatial, f32[512,512]{1,0:T(8,128)S(1)} %copy-done.19, f32[1,512]{1,0:T(1,128)S(1)} %bitcast.11, bf16[128,2048]{1,0:T(8,128)(2,1)S(1)} %copy-done.3, bf16[512,512]{1,0:T(8,128)(2,1)S(1)} %copy-done.4, ...), custom_call_target="tpu_custom_call" | custom-call | flops 2147483648 | bytes 5769224 | tf_op jit(solution)/shard_map/pallas_call | solution.py:257
  (65 shorter events, 11.9 us)
Async XLA Ops:
  0.0 25.7 %copy-start = (bf16[128,1536]{1,0:T(8,128)(2,1)S(1)}, bf16[128,1536]{1,0:T(8,128)(2,1)}, u32[]{:S(2)}) copy-start(bf16[128,1536]{1,0:T(8,128)(2,1)} %refs_4_.1) | copy-start | bytes 1179652
  0.0 25.7 %copy-start.2 = (bf16[128,512]{1,0:T(8,128)(2,1)S(1)}, bf16[128,512]{1,0:T(8,128)(2,1)}, u32[]{:S(2)}) copy-start(bf16[128,512]{1,0:T(8,128)(2,1)} %refs_5_.1) | copy-start | bytes 393220
  1.0 12.4 %collective-permute-start.2 = (bf16[64,2048]{1,0:T(8,128)(2,1)S(1)}, bf16[64,2048]{1,0:T(8,128)(2,1)S(1)}, u32[]{:S(2)}, u32[]{:S(2)}) collective-permute-start(bf16[64,2048]{1,0:T(8,128)(2,1)S(1)} %fusion), channel_id=1, source_target_pairs={{0,1},{1,2},{2,3},{3,0},{4,5},{5,6},{6,7},{7,4},{8,9},{9,10},{10,1... | collective-permute-start | bytes 786440 | tf_op jit(solution)/shard_map/ppermute | solution.py:25
  4.1 19.7 %collective-permute-start.3 = (bf16[64,2048]{1,0:T(8,128)(2,1)S(1)}, bf16[64,2048]{1,0:T(8,128)(2,1)S(1)}, u32[]{:S(2)}, u32[]{:S(2)}) collective-permute-start(bf16[64,2048]{1,0:T(8,128)(2,1)S(1)} %fusion), channel_id=1, source_target_pairs={{0,2},{1,3},{2,0},{3,1},{4,6},{5,7},{6,4},{7,5},{8,10},{9,11},{10,... | collective-permute-start | bytes 786440 | tf_op jit(solution)/shard_map/ppermute | solution.py:25
  6.7 17.1 %collective-permute-start.4 = (bf16[64,2048]{1,0:T(8,128)(2,1)S(1)}, bf16[64,2048]{1,0:T(8,128)(2,1)S(1)}, u32[]{:S(2)}, u32[]{:S(2)}) collective-permute-start(bf16[64,2048]{1,0:T(8,128)(2,1)S(1)} %fusion), channel_id=1, source_target_pairs={{0,3},{1,0},{2,1},{3,2},{4,7},{5,4},{6,5},{7,6},{8,11},{9,8},{10,9... | collective-permute-start | bytes 786440 | tf_op jit(solution)/shard_map/ppermute | solution.py:25
  8.0 17.7 %collective-permute-start = (bf16[4,128,512]{2,1,0:T(8,128)(2,1)}, bf16[4,128,512]{2,1,0:T(8,128)(2,1)S(1)}, u32[]{:S(2)}, u32[]{:S(2)}) collective-permute-start(bf16[4,128,512]{2,1,0:T(8,128)(2,1)} %states.1), channel_id=1, source_target_pairs={{0,8},{4,12},{8,16},{12,20},{16,24},{20,28},{1,9},{5,13},{9,17},{1... | collective-permute-start | bytes 1572872 | tf_op jit(solution)/shard_map/ppermute | solution.py:20
  11.5 14.3 %collective-permute-start.1 = (bf16[4,128,512]{2,1,0:T(8,128)(2,1)}, bf16[4,128,512]{2,1,0:T(8,128)(2,1)S(1)}, u32[]{:S(2)}, u32[]{:S(2)}) collective-permute-start(bf16[4,128,512]{2,1,0:T(8,128)(2,1)} %states.1), channel_id=1, source_target_pairs={{0,4},{4,8},{8,12},{12,16},{16,20},{20,24},{24,28},{1,5},{5,9},{9,... | collective-permute-start | bytes 1572872 | tf_op jit(solution)/shard_map/ppermute | solution.py:20
  13.4 11.0 %collective-permute-start.5 = (bf16[64,2048]{1,0:T(8,128)(2,1)S(1)}, bf16[64,2048]{1,0:T(8,128)(2,1)S(1)}, u32[]{:S(2)}, u32[]{:S(2)}) collective-permute-start(bf16[64,2048]{1,0:T(8,128)(2,1)S(1)} %collective-permute-done.2.refs_6_), channel_id=1, source_target_pairs={{0,4},{4,0},{8,12},{12,8},{16,20},{20,16},{24,28},{28,24},{1,5},{5... | collective-permute-start | bytes 786440 | tf_op jit(solution)/shard_map/ppermute | solution.py:30
  23.8 1.5 %collective-permute-start.6 = (bf16[64,2048]{1,0:T(8,128)(2,1)S(1)}, bf16[64,2048]{1,0:T(8,128)(2,1)S(1)}, u32[]{:S(2)}, u32[]{:S(2)}) collective-permute-start(bf16[64,2048]{1,0:T(8,128)(2,1)S(1)} %collective-permute-done.3.refs_7_), channel_id=1, source_target_pairs={{0,4},{4,0},{8,12},{12,8},{16,20},{20,16},{24,28},{28,24},{1,5},{5... | collective-permute-start | bytes 786440 | tf_op jit(solution)/shard_map/ppermute | solution.py:30
  23.8 1.9 %collective-permute-start.7 = (bf16[64,2048]{1,0:T(8,128)(2,1)S(1)}, bf16[64,2048]{1,0:T(8,128)(2,1)S(1)}, u32[]{:S(2)}, u32[]{:S(2)}) collective-permute-start(bf16[64,2048]{1,0:T(8,128)(2,1)S(1)} %collective-permute-done.4.refs_8_), channel_id=1, source_target_pairs={{0,4},{4,0},{8,12},{12,8},{16,20},{20,16},{24,28},{28,24},{1,5},{5... | collective-permute-start | bytes 786440 | tf_op jit(solution)/shard_map/ppermute | solution.py:30
  34.4 8.5 %copy-start.4 = (bf16[512,512]{1,0:T(8,128)(2,1)S(1)}, bf16[512,512]{1,0:T(8,128)(2,1)}, u32[]{:S(2)}) copy-start(bf16[512,512]{1,0:T(8,128)(2,1)} %own_out.1) | copy-start | bytes 1572868
  34.4 36.4 %all-to-all-start = ((bf16[4,512,128]{2,1,0:T(8,128)(2,1)}), bf16[4,512,128]{2,1,0:T(8,128)(2,1)S(1)}, u32[]{:S(2)}, u32[]{:S(2)}) async-start(bf16[4,512,128]{2,1,0:T(8,128)(2,1)} %get-tuple-element.7), calls=%async_computation | async-start | bytes 1048576 | tf_op jit(solution)/shard_map/all_to_all | solution.py:338
  43.0 16.8 %collective-permute-start.8 = (bf16[256,256]{1,0:T(8,128)(2,1)S(1)}, bf16[256,256]{1,0:T(8,128)(2,1)S(1)}, u32[]{:S(2)}, u32[]{:S(2)}) collective-permute-start(bf16[256,256]{1,0:T(8,128)(2,1)S(1)} %pad_maximum_fusion.1), channel_id=1, source_target_pairs={{0,1},{1,2},{2,3},{3,0},{4,5},{5,6},{6,7},{7,4},{8,9},{9,10},{10,1... | collective-permute-start | bytes 393224 | tf_op jit(solution)/shard_map/ppermute | solution.py:25
  45.1 22.1 %collective-permute-start.9 = (bf16[256,256]{1,0:T(8,128)(2,1)S(1)}, bf16[256,256]{1,0:T(8,128)(2,1)S(1)}, u32[]{:S(2)}, u32[]{:S(2)}) collective-permute-start(bf16[256,256]{1,0:T(8,128)(2,1)S(1)} %pad_maximum_fusion.1), channel_id=1, source_target_pairs={{0,2},{1,3},{2,0},{3,1},{4,6},{5,7},{6,4},{7,5},{8,10},{9,11},{10,... | collective-permute-start | bytes 393224 | tf_op jit(solution)/shard_map/ppermute | solution.py:25
  47.5 19.7 %collective-permute-start.10 = (bf16[256,256]{1,0:T(8,128)(2,1)S(1)}, bf16[256,256]{1,0:T(8,128)(2,1)S(1)}, u32[]{:S(2)}, u32[]{:S(2)}) collective-permute-start(bf16[256,256]{1,0:T(8,128)(2,1)S(1)} %pad_maximum_fusion.1), channel_id=1, source_target_pairs={{0,3},{1,0},{2,1},{3,2},{4,7},{5,4},{6,5},{7,6},{8,11},{9,8},{10,9... | collective-permute-start | bytes 393224 | tf_op jit(solution)/shard_map/ppermute | solution.py:25
  67.2 12.1 %collective-permute-start.12 = (bf16[3,256,256]{2,1,0:T(8,128)(2,1)S(1)}, bf16[3,256,256]{2,1,0:T(8,128)(2,1)S(1)}, u32[]{:S(2)}, u32[]{:S(2)}) collective-permute-start(bf16[3,256,256]{2,1,0:T(8,128)(2,1)S(1)} %pad_maximum_fusion.refs_0_), channel_id=1, source_target_pairs={{0,8},{4,12},{8,0},{12,4},{16,24},{20,28},{24,16},{28,20},{1,9},{5... | collective-permute-start | bytes 1179656 | tf_op jit(solution)/shard_map/ppermute | solution.py:30
  68.8 17.3 %collective-permute-start.14 = (bf16[3,256,256]{2,1,0:T(8,128)(2,1)S(1)}, bf16[3,256,256]{2,1,0:T(8,128)(2,1)S(1)}, u32[]{:S(2)}, u32[]{:S(2)}) collective-permute-start(bf16[3,256,256]{2,1,0:T(8,128)(2,1)S(1)} %pad_maximum_fusion.refs_0_), channel_id=1, source_target_pairs={{0,16},{4,20},{8,24},{12,28},{16,0},{20,4},{24,8},{28,12},{1,17},{... | collective-permute-start | bytes 1179656 | tf_op jit(solution)/shard_map/ppermute | solution.py:30
  70.3 15.8 %collective-permute-start.16 = (bf16[3,256,256]{2,1,0:T(8,128)(2,1)S(1)}, bf16[3,256,256]{2,1,0:T(8,128)(2,1)S(1)}, u32[]{:S(2)}, u32[]{:S(2)}) collective-permute-start(bf16[3,256,256]{2,1,0:T(8,128)(2,1)S(1)} %pad_maximum_fusion.refs_0_), channel_id=1, source_target_pairs={{0,24},{4,28},{8,16},{12,20},{16,8},{20,12},{24,0},{28,4},{1,25},{... | collective-permute-start | bytes 1179656 | tf_op jit(solution)/shard_map/ppermute | solution.py:30
  73.1 17.3 %all-to-all-start.1 = ((bf16[4,512,128]{2,1,0:T(8,128)(2,1)}), bf16[4,512,128]{2,1,0:T(8,128)(2,1)S(1)}, u32[]{:S(2)}, u32[]{:S(2)}) async-start(bf16[4,512,128]{2,1,0:T(8,128)(2,1)} %shard_map.119), calls=%async_computation.1 | async-start | bytes 1048576 | tf_op jit(solution)/shard_map/all_to_all | solution.py:347
  77.7 12.8 %copy-start.16 = (f32[512]{0:T(512)S(1)}, f32[512]{0:T(512)}, u32[]{:S(2)}) copy-start(f32[512]{0:T(512)} %param.21) | copy-start | bytes 6148
  77.7 8.9 %collective-permute-start.11 = (bf16[3,256,256]{2,1,0:T(8,128)(2,1)S(1)}, bf16[3,256,256]{2,1,0:T(8,128)(2,1)S(1)}, u32[]{:S(2)}, u32[]{:S(2)}) collective-permute-start(bf16[3,256,256]{2,1,0:T(8,128)(2,1)S(1)} %pad_maximum_fusion.refs_0_), channel_id=1, source_target_pairs={{0,4},{4,0},{8,12},{12,8},{16,20},{20,16},{24,28},{28,24},{1,5},{5... | collective-permute-start | bytes 1179656 | tf_op jit(solution)/shard_map/ppermute | solution.py:30
  79.4 7.2 %collective-permute-start.13 = (bf16[3,256,256]{2,1,0:T(8,128)(2,1)S(1)}, bf16[3,256,256]{2,1,0:T(8,128)(2,1)S(1)}, u32[]{:S(2)}, u32[]{:S(2)}) collective-permute-start(bf16[3,256,256]{2,1,0:T(8,128)(2,1)S(1)} %collective-permute-done.12.refs_2_), channel_id=1, source_target_pairs={{0,4},{4,0},{8,12},{12,8},{16,20},{20,16},{24,28},{28,24},{1,5},{5... | collective-permute-start | bytes 1179656 | tf_op jit(solution)/shard_map/ppermute | solution.py:30
  86.1 1.7 %collective-permute-start.15 = (bf16[3,256,256]{2,1,0:T(8,128)(2,1)S(1)}, bf16[3,256,256]{2,1,0:T(8,128)(2,1)S(1)}, u32[]{:S(2)}, u32[]{:S(2)}) collective-permute-start(bf16[3,256,256]{2,1,0:T(8,128)(2,1)S(1)} %collective-permute-done.14.refs_4_), channel_id=1, source_target_pairs={{0,4},{4,0},{8,12},{12,8},{16,20},{20,16},{24,28},{28,24},{1,5},{5... | collective-permute-start | bytes 1179656 | tf_op jit(solution)/shard_map/ppermute | solution.py:30
  86.1 2.5 %collective-permute-start.17 = (bf16[3,256,256]{2,1,0:T(8,128)(2,1)S(1)}, bf16[3,256,256]{2,1,0:T(8,128)(2,1)S(1)}, u32[]{:S(2)}, u32[]{:S(2)}) collective-permute-start(bf16[3,256,256]{2,1,0:T(8,128)(2,1)S(1)} %collective-permute-done.16.refs_6_), channel_id=1, source_target_pairs={{0,4},{4,0},{8,12},{12,8},{16,20},{20,16},{24,28},{28,24},{1,5},{5... | collective-permute-start | bytes 1179656 | tf_op jit(solution)/shard_map/ppermute | solution.py:30
  (16 other events, 31.3 us)

commit v3 on v2

--- a/solution.py
+++ b/solution.py
@@ -12,7 +12,7 @@
 LANES = 128
 F32 = jnp.float32
 BF16 = jnp.bfloat16
-VMEM_LIMIT = 48 * 1024 * 1024
+MIB = 1024 * 1024
 
 
 def shifted(value, axis, steps):
@@ -35,6 +35,10 @@
     return values * lax.rsqrt(mean_sq + 1e-06) * gain
 
 
+def quarter_of(block):
+    return lax.rem(block, 2) + 2 * lax.rem(lax.div(block, 4), 2)
+
+
 def row_sum(value):
     return jnp.sum(value, axis=0, keepdims=True)
 
@@ -42,31 +46,29 @@
 def attention_kernel(zones, reach, place, pattern, states, *refs):
     earlier, refs = refs[:reach], refs[reach:]
     (gain_attn, gain_mix, own_qkv, own_attn), refs = refs[:4], refs[4:]
-    direct, refs = refs[: zones - 1], refs[zones - 1 :]
-    partner, refs = refs[: zones - 1], refs[zones - 1 :]
-    after_out, mixin_out, w_qkv, w_attn, w_turned, normed, projected, context = refs
+    pieces, refs = refs[:4], refs[4:]
+    after_out, mixin_out, weights, w_turned, normed, projected, context = refs
     steps, zone_rows, width = states.shape
     head_size = width // HEADS
     key_count = (reach + 1) * steps
     my_block, my_zone = place[0], place[1]
-    my_half = lax.rem(my_block, 2)
     shard = own_qkv.shape[0]
-    half = shard // 2
-
-    def put(rows, qkv, attn):
-        w_qkv[rows, :] = qkv
-        w_attn[rows, :] = attn
-
-    put(pl.ds(pl.multiple_of(my_zone * shard, shard), shard), own_qkv[...], own_attn[...])
-    for step in range(1, zones):
-        source = lax.rem(my_zone - step + zones, zones)
-        for pieces, which in ((direct, my_half), (partner, 1 - my_half)):
-            start = pl.multiple_of(source * shard + which * half, half)
-            piece = pieces[step - 1]
-            put(pl.ds(start, half), piece[:, : 3 * width], piece[:, 3 * width :])
-    for block in range(3 * width // LANES):
-        cols = slice(block * LANES, (block + 1) * LANES)
-        w_turned[cols, :] = w_qkv[:, cols].T
+
+    own_rows = pl.ds(pl.multiple_of(my_zone * shard, shard), shard)
+    for index in range(3):
+        weights[index, own_rows, :] = own_qkv[:, index * width : (index + 1) * width]
+    weights[3, own_rows, :] = own_attn[...]
+    my_quarter = quarter_of(my_block)
+    for bits in range(4):
+        for step in range(1, zones):
+            source = lax.rem(my_zone - step + zones, zones)
+            rows = pl.ds(pl.multiple_of(source * shard, shard), shard)
+            weights[my_quarter ^ bits, rows, :] = pieces[bits][step - 1]
+    for index in range(3):
+        for block in range(width // LANES):
+            first = block * LANES
+            rows = slice(index * width + first, index * width + first + LANES)
+            w_turned[rows, :] = weights[index, :, first : first + LANES].T
 
     blocks = list(earlier) + [states]
     gain = gain_attn[...]
@@ -150,7 +152,7 @@
     for step in range(steps):
         rows = slice(step * zone_rows, (step + 1) * zone_rows)
         turned = context[:, rows].T.astype(BF16)
-        after = states[step].astype(F32) + jnp.dot(turned, w_attn[...], preferred_element_type=F32)
+        after = states[step].astype(F32) + jnp.dot(turned, weights[3], preferred_element_type=F32)
         after_out[rows, :] = after
         mixin = rms_scale(after, mix_gain).astype(BF16)
         if len(mixin_out.shape) == 2:
@@ -248,7 +250,7 @@
         out[rows, :] = total.astype(BF16)
 
 
-def call(kernel, out_shape, scratch, flops, smem, args):
+def call(kernel, out_shape, scratch, flops, smem, limit, args):
     in_specs = [
         pl.BlockSpec(memory_space=pltpu.SMEM if index in smem else pltpu.VMEM)
         for index in range(len(args))
@@ -261,7 +263,7 @@
         out_specs=jax.tree.map(lambda _: pl.BlockSpec(memory_space=pltpu.VMEM), out_shape),
         scratch_shapes=scratch,
         cost_estimate=pl.CostEstimate(flops=flops, bytes_accessed=moved, transcendentals=0),
-        compiler_params=pltpu.CompilerParams(vmem_limit_bytes=VMEM_LIMIT),
+        compiler_params=pltpu.CompilerParams(vmem_limit_bytes=limit * MIB),
     )(*args)
 
 
@@ -287,13 +289,14 @@
     place = jnp.stack([my_block, my_zone]).astype(jnp.int32)
     key_count = (reach + 1) * steps
 
-    half = w_qkv.shape[0] // 2
     first = lax.dynamic_slice_in_dim(
-        jnp.concatenate([w_qkv, w_out_attn], axis=1), (my_block % 2) * half, half, axis=0
+        jnp.concatenate([w_qkv, w_out_attn], axis=1), quarter_of(my_block) * width, width, axis=1
     )
     direct = [rotated(first, "zone", step) for step in range(1, zones)]
     earlier = [shifted(states, "tm", offset) for offset in range(reach, 0, -1)]
-    partner = [swapped(piece, "tm", 1) for piece in direct]
+    direct = jnp.stack(direct)
+    over = swapped(direct, "tm", 4)
+    quarters = [direct, swapped(direct, "tm", 1), over, swapped(over, "tm", 1)]
 
     in_cols = w_in.shape[1] // SPREAD
     out_rows = w_out.shape[0] // SPREAD
@@ -304,7 +307,9 @@
         + [out_slice[:, at : at + in_cols] for at in range(0, width, in_cols)],
         axis=0,
     )
+    second, _ = lax.optimization_barrier((second, direct))
     across = jnp.stack([rotated(second, "zone", step) for step in range(1, zones)])
+    across, quarters = lax.optimization_barrier((across, quarters))
     pieces = {0: across}
     for bits in range(2, SPREAD, 2):
         pieces[bits] = swapped(across, "tm", bits)
@@ -318,8 +323,7 @@
         functools.partial(attention_kernel, zones, reach),
         (jax.ShapeDtypeStruct((rows, width), F32), jax.ShapeDtypeStruct(mixin_shape, BF16)),
         [
-            pltpu.VMEM((width, 3 * width), BF16),
-            pltpu.VMEM((width, width), BF16),
+            pltpu.VMEM((4, width, width), BF16),
             pltpu.VMEM((3 * width, width), BF16),
             pltpu.VMEM((key_count * zone_rows, width), BF16),
             pltpu.VMEM((3 * width, key_count * zone_rows), F32),
@@ -327,11 +331,11 @@
         ],
         2 * rows * width * width * 10,
         (0, 1),
+        24,
         [place, pattern, states]
         + earlier
         + [gain_attn.reshape(1, -1), gain_mix.reshape(1, -1), w_qkv, w_out_attn]
-        + direct
-        + partner,
+        + quarters,
     )
     if not wide:
         mixin = jnp.transpose(mixin.reshape(rows, zones, part), (1, 0, 2))
@@ -342,6 +346,7 @@
         [],
         2 * rows * width * zone_rows * 3,
         (0, 1),
+        8,
         [neighbours, degree, mix, items],
     )
     spatial = lax.all_to_all(spatial, "zone", split_axis=0, concat_axis=0, tiled=True)
@@ -359,6 +364,7 @@
         ],
         4 * rows * width * hidden,
         (0,),
+        16,
         [place, spatial, after_attn, gain_ffn.reshape(1, -1), w_in, w_out]
         + [pieces[bits] for bits in range(SPREAD)],
     )

time: 99.3 us -> 108 us (1.088)
  waiting for transfers between devices: 39 us -> 53.1 us
  starting transfers between devices: 36.9 us -> 30.5 us
  other arithmetic: 1.15 us -> 2.28 us
    ppermute x6, waiting for transfers between devices: 27.6 us -> 15.9 us  [rotated(): lax.ppermute(value, axis, [(source, (source + steps) % count) for source...]
    all_to_all x1, waiting for transfers between devices: 0.01 us -> 9.92 us  [on_device(): lax.all_to_all(mixin, 'zone', split_axis=0, concat_axis=0, tiled=True)]
    all_to_all x1, waiting for transfers between devices: 1.19 us -> 9.35 us  [on_device(): lax.all_to_all(spatial, 'zone', split_axis=0, concat_axis=0, tiled=True)]
    ppermute x10, waiting for transfers between devices: 10.2 us -> 17.9 us  [swapped(): lax.ppermute(value, axis, [(source, source ^ bits) for source in range(co...]
    all_to_all x1, starting transfers between devices: 8.51 us -> 3.6 us  [on_device(): lax.all_to_all(mixin, 'zone', split_axis=0, concat_axis=0, tiled=True)]
    ppermute x6, starting transfers between devices: 12.9 us -> 11.3 us  [rotated(): lax.ppermute(value, axis, [(source, (source + steps) % count) for source...]
    another operation x1, other arithmetic: 0.05 us -> 1.13 us  [on_device(): jnp.stack([rotated(second, 'zone', step) for step in range(1, zones)])]
  transfers between devices with their start and end apart: 20 -> 20, of which waited for: 10 -> 9; matrix products, arithmetic and copies ran while one was open for 0% -> 1% of each run, Pallas kernels for 2% -> 2%
where the time goes in v3:
time: 108 us; the launch traced here: 107 us
  waiting for transfers between devices  53.1 us (49%)
  starting transfers between devices  30.5 us (28%)
  Pallas kernels  13.2 us (12%)
  local copies, waits for them, and re-layouts  8.11 us (8%)
  other arithmetic  2.28 us (2%)
    ppermute x10, waiting for transfers between devices, swapped(): lax.ppermute(value, axis, [(source, source ^ bits) for source in range(co...  17.9 us
    ppermute x6, waiting for transfers between devices, rotated(): lax.ppermute(value, axis, [(source, (source + steps) % count) for source...  15.9 us
    pallas_call x3, Pallas kernels, call(): pl.pallas_call(kernel, out_shape=out_shape, in_specs=in_specs, out_specs=...  13.2 us
    ppermute x6, starting transfers between devices, rotated(): lax.ppermute(value, axis, [(source, (source + steps) % count) for source...  11.3 us
    all_to_all x1, waiting for transfers between devices, on_device(): lax.all_to_all(mixin, 'zone', split_axis=0, concat_axis=0, tiled=True)  9.92 us
    all_to_all x1, waiting for transfers between devices, on_device(): lax.all_to_all(spatial, 'zone', split_axis=0, concat_axis=0, tiled=True)  9.35 us
    unnamed x40, local copies, waits for them, and re-layouts  8.09 us
    ppermute x10, starting transfers between devices, swapped(): lax.ppermute(value, axis, [(source, source ^ bits) for source in range(co...  6.63 us
  transfers between devices with their start and end apart: 20, of which 9 were waited for; matrix products, arithmetic and copies ran while one was open for 1% of the time, Pallas kernels for 2%

profile of v3, /device:TPU:0, one launch (start us, length us, event | category | flops | bytes accessed | tf_op | source)
XLA Modules:
  0.0 107.3 jit_solution(6976954017242659126)
XLA Ops:
  0.0 1.0 fusion
  1.0 3.1 %collective-permute-start.2 = (bf16[128,512]{1,0:T(8,128)(2,1)S(1)}, bf16[128,512]{1,0:T(8,128)(2,1)S(1)}, u32[]{:S(2)}, u32[]{:S(2)}) collective-permute-start(bf16[128,512]{1,0:T(8,128)(2,1)S(1)} %fusion), channel_id=1, source_target_pairs={{0,1},{1,2},{2,3},{3,0},{4,5},{5,6},{6,7},{7,4},{8,9},{9,10},{10,1... | collective-permute-start | bytes 393224 | tf_op jit(solution)/shard_map/ppermute | solution.py:25
  4.1 2.6 %collective-permute-start.3 = (bf16[128,512]{1,0:T(8,128)(2,1)S(1)}, bf16[128,512]{1,0:T(8,128)(2,1)S(1)}, u32[]{:S(2)}, u32[]{:S(2)}) collective-permute-start(bf16[128,512]{1,0:T(8,128)(2,1)S(1)} %fusion), channel_id=1, source_target_pairs={{0,2},{1,3},{2,0},{3,1},{4,6},{5,7},{6,4},{7,5},{8,10},{9,11},{10,... | collective-permute-start | bytes 393224 | tf_op jit(solution)/shard_map/ppermute | solution.py:25
  6.7 1.3 %collective-permute-start.4 = (bf16[128,512]{1,0:T(8,128)(2,1)S(1)}, bf16[128,512]{1,0:T(8,128)(2,1)S(1)}, u32[]{:S(2)}, u32[]{:S(2)}) collective-permute-start(bf16[128,512]{1,0:T(8,128)(2,1)S(1)} %fusion), channel_id=1, source_target_pairs={{0,3},{1,0},{2,1},{3,2},{4,7},{5,4},{6,5},{7,6},{8,11},{9,8},{10,9... | collective-permute-start | bytes 393224 | tf_op jit(solution)/shard_map/ppermute | solution.py:25
  8.0 3.4 %collective-permute-start = (bf16[4,128,512]{2,1,0:T(8,128)(2,1)}, bf16[4,128,512]{2,1,0:T(8,128)(2,1)S(1)}, u32[]{:S(2)}, u32[]{:S(2)}) collective-permute-start(bf16[4,128,512]{2,1,0:T(8,128)(2,1)} %states.1), channel_id=1, source_target_pairs={{0,8},{4,12},{8,16},{12,20},{16,24},{20,28},{1,9},{5,13},{9,17},{1... | collective-permute-start | bytes 1572872 | tf_op jit(solution)/shard_map/ppermute | solution.py:20
  11.5 2.1 %collective-permute-start.1 = (bf16[4,128,512]{2,1,0:T(8,128)(2,1)}, bf16[4,128,512]{2,1,0:T(8,128)(2,1)}, u32[]{:S(2)}, u32[]{:S(2)}) collective-permute-start(bf16[4,128,512]{2,1,0:T(8,128)(2,1)} %states.1), channel_id=1, source_target_pairs={{0,4},{4,8},{8,12},{12,16},{16,20},{20,24},{24,28},{1,5},{5,9},{9,... | collective-permute-start | bytes 1572872 | tf_op jit(solution)/shard_map/ppermute | solution.py:20
  13.6 1.8 %collective-permute-done.3 = bf16[128,512]{1,0:T(8,128)(2,1)S(1)} collective-permute-done((bf16[128,512]{1,0:T(8,128)(2,1)S(1)}, bf16[128,512]{1,0:T(8,128)(2,1)S(1)}, u32[]{:S(2)}, u32[]{:S(2)}) %collective-permute-start.3) | collective-permute-done | bytes 131104 | tf_op jit(solution)/shard_map/ppermute | solution.py:25
  15.4 1.6 %collective-permute-start.9 = (bf16[3,128,512]{2,1,0:T(8,128)(2,1)S(1)}, bf16[3,128,512]{2,1,0:T(8,128)(2,1)S(1)}, u32[]{:S(2)}, u32[]{:S(2)}) collective-permute-start(bf16[3,128,512]{2,1,0:T(8,128)(2,1)S(1)} %pad_maximum_fusion.refs_6_), channel_id=1, source_target_pairs={{0,16},{4,20},{8,24},{12,28},{16,0},{20,4},{24,8},{28,12},{1,17},{... | collective-permute-start | bytes 1179656 | tf_op jit(solution)/shard_map/ppermute | solution.py:30
  17.1 3.3 %collective-permute-start.5 = (bf16[256,256]{1,0:T(8,128)(2,1)S(1)}, bf16[256,256]{1,0:T(8,128)(2,1)}, u32[]{:S(2)}, u32[]{:S(2)}) collective-permute-start(bf16[256,256]{1,0:T(8,128)(2,1)S(1)} %pad_maximum_fusion.2), channel_id=1, source_target_pairs={{0,1},{1,2},{2,3},{3,0},{4,5},{5,6},{6,7},{7,4},{8,9},{9,10},{10,1... | collective-permute-start | bytes 393224 | tf_op jit(solution)/shard_map/ppermute | solution.py:25
  20.4 16.5 %collective-permute-done.9.refs_8_ = bf16[3,128,512]{2,1,0:T(8,128)(2,1)S(1)} collective-permute-done((bf16[3,128,512]{2,1,0:T(8,128)(2,1)S(1)}, bf16[3,128,512]{2,1,0:T(8,128)(2,1)S(1)}, u32[]{:S(2)}, u32[]{:S(2)}) %collective-permute-start.9) | collective-permute-done | bytes 393248 | tf_op jit(solution)/shard_map/ppermute | solution.py:30
  37.4 9.2 %collective-permute-done.6 = bf16[256,256]{1,0:T(8,128)(2,1)} collective-permute-done((bf16[256,256]{1,0:T(8,128)(2,1)S(1)}, bf16[256,256]{1,0:T(8,128)(2,1)}, u32[]{:S(2)}, u32[]{:S(2)}) %collective-permute-start.6) | collective-permute-done | bytes 131104 | tf_op jit(solution)/shard_map/ppermute | solution.py:25
  47.2 4.9 %collective-permute-done.7 = bf16[256,256]{1,0:T(8,128)(2,1)} collective-permute-done((bf16[256,256]{1,0:T(8,128)(2,1)S(1)}, bf16[256,256]{1,0:T(8,128)(2,1)}, u32[]{:S(2)}, u32[]{:S(2)}) %collective-permute-start.7) | collective-permute-done | bytes 131104 | tf_op jit(solution)/shard_map/ppermute | solution.py:25
  52.1 1.1 %pad_maximum_fusion.1.refs_0_ = bf16[3,256,256]{2,1,0:T(8,128)(2,1)S(1)} fusion(bf16[1,256,256]{2,1,0:T(8,128)(2,1)} %bitcast.9, bf16[1,256,256]{2,1,0:T(8,128)(2,1)} %bitcast.8, bf16[1,256,256]{2,1,0:T(8,128)(2,1)} %bitcast.7), kind=kLoop, calls=%fused_computation.3 | loop fusion | flops 393216 | bytes 786432 | tf_op jit(solution)/shard_map/stack | solution.py:311
  53.9 6.7 %shard_map.118 = (f32[512,512]{1,0:T(8,128)S(1)}, bf16[4,512,128]{2,1,0:T(8,128)(2,1)}) custom-call(s32[2]{0:T(128)S(1)} %pad_add_fusion.place, s32[1,2]{1,0:T(1,128)S(1)} %copy-done.17, bf16[4,128,512]{2,1,0:T(8,128)(2,1)S(1)} %copy-done.7, bf16[4,128,512]{2,1,0:T(8,128)(2,1)S(1)} %collective-permute-done.refs_0_, ...), custom_call_target="tpu_custom_call" | custom-call | flops 2684354560 | bytes 3674128 | tf_op jit(solution)/shard_map/pallas_call | solution.py:259
  61.7 3.6 %all-to-all-start = ((bf16[4,512,128]{2,1,0:T(8,128)(2,1)}), bf16[4,512,128]{2,1,0:T(8,128)(2,1)S(1)}, u32[]{:S(2)}, u32[]{:S(2)}) async-start(bf16[4,512,128]{2,1,0:T(8,128)(2,1)} %get-tuple-element.18), calls=%async_computation | async-start | bytes 1048576 | tf_op jit(solution)/shard_map/all_to_all | solution.py:342
  65.4 2.5 %collective-permute-start.14 = (bf16[3,256,256]{2,1,0:T(8,128)(2,1)S(1)}, bf16[3,256,256]{2,1,0:T(8,128)(2,1)S(1)}, u32[]{:S(2)}, u32[]{:S(2)}) collective-permute-start(bf16[3,256,256]{2,1,0:T(8,128)(2,1)S(1)} %pad_maximum_fusion.1.refs_0_), channel_id=1, source_target_pairs={{0,16},{4,20},{8,24},{12,28},{16,0},{20,4},{24,8},{28,12},{1,17},{... | collective-permute-start | bytes 1179656 | tf_op jit(solution)/shard_map/ppermute | solution.py:30
  67.9 1.4 %collective-permute-start.16 = (bf16[3,256,256]{2,1,0:T(8,128)(2,1)S(1)}, bf16[3,256,256]{2,1,0:T(8,128)(2,1)S(1)}, u32[]{:S(2)}, u32[]{:S(2)}) collective-permute-start(bf16[3,256,256]{2,1,0:T(8,128)(2,1)S(1)} %pad_maximum_fusion.1.refs_0_), channel_id=1, source_target_pairs={{0,24},{4,28},{8,16},{12,20},{16,8},{20,12},{24,0},{28,4},{1,25},{... | collective-permute-start | bytes 1179656 | tf_op jit(solution)/shard_map/ppermute | solution.py:30
  69.3 9.9 %all-to-all-done.items = bf16[4,512,128]{2,1,0:T(8,128)(2,1)S(1)} async-done(((bf16[4,512,128]{2,1,0:T(8,128)(2,1)}), bf16[4,512,128]{2,1,0:T(8,128)(2,1)S(1)}, u32[]{:S(2)}, u32[]{:S(2)}) %all-to-all-start) | async-done | bytes 524320 | tf_op jit(solution)/shard_map/all_to_all | solution.py:342
  79.2 2.3 %shard_map.119 = bf16[4,512,128]{2,1,0:T(8,128)(2,1)} custom-call(s32[4,3]{1,0:T(4,128)S(1)} %copy-done.5, s32[4]{0:T(128)S(1)} %copy-done.6, bf16[4,3,128,128]{3,2,1,0:T(8,128)(2,1)S(1)} %copy-done.1, bf16[4,512,128]{2,1,0:T(8,128)(2,1)S(1)} %all-to-all-done.items), custom_call_target="tpu_custom_call" | custom-call | flops 201326592 | bytes 917568 | tf_op jit(solution)/shard_map/pallas_call | solution.py:259
  81.5 3.5 %all-to-all-start.1 = ((bf16[4,512,128]{2,1,0:T(8,128)(2,1)}), bf16[4,512,128]{2,1,0:T(8,128)(2,1)S(1)}, u32[]{:S(2)}, u32[]{:S(2)}) async-start(bf16[4,512,128]{2,1,0:T(8,128)(2,1)} %shard_map.119), calls=%async_computation.1 | async-start | bytes 1048576 | tf_op jit(solution)/shard_map/all_to_all | solution.py:352
  89.6 9.4 %all-to-all-done.1.spatial = bf16[4,512,128]{2,1,0:T(8,128)(2,1)S(1)} async-done(((bf16[4,512,128]{2,1,0:T(8,128)(2,1)}), bf16[4,512,128]{2,1,0:T(8,128)(2,1)S(1)}, u32[]{:S(2)}, u32[]{:S(2)}) %all-to-all-start.1) | async-done | bytes 524320 | tf_op jit(solution)/shard_map/all_to_all | solution.py:352
  99.0 1.0 copy-done.9
  102.0 1.2 %copy-done.19 = f32[512,512]{1,0:T(8,128)S(1)} copy-done((f32[512,512]{1,0:T(8,128)S(1)}, f32[512,512]{1,0:T(8,128)}, u32[]{:S(2)}) %copy-start.19) | copy-done | bytes 1048600
  103.2 4.2 %shard_map.120 = bf16[512,512]{1,0:T(8,128)(2,1)} custom-call(s32[2]{0:T(128)S(1)} %pad_add_fusion.place, bf16[4,512,128]{2,1,0:T(8,128)(2,1)S(1)} %all-to-all-done.1.spatial, f32[512,512]{1,0:T(8,128)S(1)} %copy-done.19, f32[1,512]{1,0:T(1,128)S(1)} %bitcast.14, bf16[128,2048]{1,0:T(8,128)(2,1)S(1)} %copy-done.3, bf16[512,512]{1,0:T(8,128)(2,1)S(1)} %copy-done.4, ...), custom_call_target="tpu_custom_call" | custom-call | flops 2147483648 | bytes 5769224 | tf_op jit(solution)/shard_map/pallas_call | solution.py:259
  (66 shorter events, 9.4 us)
Async XLA Ops:
  1.0 12.5 %collective-permute-start.2 = (bf16[128,512]{1,0:T(8,128)(2,1)S(1)}, bf16[128,512]{1,0:T(8,128)(2,1)S(1)}, u32[]{:S(2)}, u32[]{:S(2)}) collective-permute-start(bf16[128,512]{1,0:T(8,128)(2,1)S(1)} %fusion), channel_id=1, source_target_pairs={{0,1},{1,2},{2,3},{3,0},{4,5},{5,6},{6,7},{7,4},{8,9},{9,10},{10,1... | collective-permute-start | bytes 393224 | tf_op jit(solution)/shard_map/ppermute | solution.py:25
  4.1 11.2 %collective-permute-start.3 = (bf16[128,512]{1,0:T(8,128)(2,1)S(1)}, bf16[128,512]{1,0:T(8,128)(2,1)S(1)}, u32[]{:S(2)}, u32[]{:S(2)}) collective-permute-start(bf16[128,512]{1,0:T(8,128)(2,1)S(1)} %fusion), channel_id=1, source_target_pairs={{0,2},{1,3},{2,0},{3,1},{4,6},{5,7},{6,4},{7,5},{8,10},{9,11},{10,... | collective-permute-start | bytes 393224 | tf_op jit(solution)/shard_map/ppermute | solution.py:25
  6.7 8.6 %collective-permute-start.4 = (bf16[128,512]{1,0:T(8,128)(2,1)S(1)}, bf16[128,512]{1,0:T(8,128)(2,1)S(1)}, u32[]{:S(2)}, u32[]{:S(2)}) collective-permute-start(bf16[128,512]{1,0:T(8,128)(2,1)S(1)} %fusion), channel_id=1, source_target_pairs={{0,3},{1,0},{2,1},{3,2},{4,7},{5,4},{6,5},{7,6},{8,11},{9,8},{10,9... | collective-permute-start | bytes 393224 | tf_op jit(solution)/shard_map/ppermute | solution.py:25
  8.0 45.2 %collective-permute-start = (bf16[4,128,512]{2,1,0:T(8,128)(2,1)}, bf16[4,128,512]{2,1,0:T(8,128)(2,1)S(1)}, u32[]{:S(2)}, u32[]{:S(2)}) collective-permute-start(bf16[4,128,512]{2,1,0:T(8,128)(2,1)} %states.1), channel_id=1, source_target_pairs={{0,8},{4,12},{8,16},{12,20},{16,24},{20,28},{1,9},{5,13},{9,17},{1... | collective-permute-start | bytes 1572872 | tf_op jit(solution)/shard_map/ppermute | solution.py:20
  11.5 41.8 %collective-permute-start.1 = (bf16[4,128,512]{2,1,0:T(8,128)(2,1)}, bf16[4,128,512]{2,1,0:T(8,128)(2,1)}, u32[]{:S(2)}, u32[]{:S(2)}) collective-permute-start(bf16[4,128,512]{2,1,0:T(8,128)(2,1)} %states.1), channel_id=1, source_target_pairs={{0,4},{4,8},{8,12},{12,16},{16,20},{20,24},{24,28},{1,5},{5,9},{9,... | collective-permute-start | bytes 1572872 | tf_op jit(solution)/shard_map/ppermute | solution.py:20
  15.4 21.6 %collective-permute-start.9 = (bf16[3,128,512]{2,1,0:T(8,128)(2,1)S(1)}, bf16[3,128,512]{2,1,0:T(8,128)(2,1)S(1)}, u32[]{:S(2)}, u32[]{:S(2)}) collective-permute-start(bf16[3,128,512]{2,1,0:T(8,128)(2,1)S(1)} %pad_maximum_fusion.refs_6_), channel_id=1, source_target_pairs={{0,16},{4,20},{8,24},{12,28},{16,0},{20,4},{24,8},{28,12},{1,17},{... | collective-permute-start | bytes 1179656 | tf_op jit(solution)/shard_map/ppermute | solution.py:30
  17.0 36.3 %copy-start.7 = (bf16[4,128,512]{2,1,0:T(8,128)(2,1)S(1)}, bf16[4,128,512]{2,1,0:T(8,128)(2,1)}, u32[]{:S(2)}) copy-start(bf16[4,128,512]{2,1,0:T(8,128)(2,1)} %states.1) | copy-start | bytes 1572868
  17.1 19.9 %collective-permute-start.5 = (bf16[256,256]{1,0:T(8,128)(2,1)S(1)}, bf16[256,256]{1,0:T(8,128)(2,1)}, u32[]{:S(2)}, u32[]{:S(2)}) collective-permute-start(bf16[256,256]{1,0:T(8,128)(2,1)S(1)} %pad_maximum_fusion.2), channel_id=1, source_target_pairs={{0,1},{1,2},{2,3},{3,0},{4,5},{5,6},{6,7},{7,4},{8,9},{9,10},{10,1... | collective-permute-start | bytes 393224 | tf_op jit(solution)/shard_map/ppermute | solution.py:25
  20.4 32.8 %collective-permute-start.8 = (bf16[3,128,512]{2,1,0:T(8,128)(2,1)S(1)}, bf16[3,128,512]{2,1,0:T(8,128)(2,1)}, u32[]{:S(2)}, u32[]{:S(2)}) collective-permute-start(bf16[3,128,512]{2,1,0:T(8,128)(2,1)S(1)} %pad_maximum_fusion.refs_6_), channel_id=1, source_target_pairs={{0,4},{4,0},{8,12},{12,8},{16,20},{20,16},{24,28},{28,24},{1,5},{5... | collective-permute-start | bytes 1179656 | tf_op jit(solution)/shard_map/ppermute | solution.py:30
  36.9 16.3 %collective-permute-start.10 = (bf16[3,128,512]{2,1,0:T(8,128)(2,1)S(1)}, bf16[3,128,512]{2,1,0:T(8,128)(2,1)}, u32[]{:S(2)}, u32[]{:S(2)}) collective-permute-start(bf16[3,128,512]{2,1,0:T(8,128)(2,1)S(1)} %collective-permute-done.9.refs_8_), channel_id=1, source_target_pairs={{0,4},{4,0},{8,12},{12,8},{16,20},{20,16},{24,28},{28,24},{1,5},{5... | collective-permute-start | bytes 1179656 | tf_op jit(solution)/shard_map/ppermute | solution.py:30
  37.0 9.7 %collective-permute-start.6 = (bf16[256,256]{1,0:T(8,128)(2,1)S(1)}, bf16[256,256]{1,0:T(8,128)(2,1)}, u32[]{:S(2)}, u32[]{:S(2)}) collective-permute-start(bf16[256,256]{1,0:T(8,128)(2,1)S(1)} %pad_maximum_fusion.2), channel_id=1, source_target_pairs={{0,2},{1,3},{2,0},{3,1},{4,6},{5,7},{6,4},{7,5},{8,10},{9,11},{10,... | collective-permute-start | bytes 393224 | tf_op jit(solution)/shard_map/ppermute | solution.py:25
  46.7 5.4 %collective-permute-start.7 = (bf16[256,256]{1,0:T(8,128)(2,1)S(1)}, bf16[256,256]{1,0:T(8,128)(2,1)}, u32[]{:S(2)}, u32[]{:S(2)}) collective-permute-start(bf16[256,256]{1,0:T(8,128)(2,1)S(1)} %pad_maximum_fusion.2), channel_id=1, source_target_pairs={{0,3},{1,0},{2,1},{3,2},{4,7},{5,4},{6,5},{7,6},{8,11},{9,8},{10,9... | collective-permute-start | bytes 393224 | tf_op jit(solution)/shard_map/ppermute | solution.py:25
  61.7 17.6 %copy-start.1 = (bf16[4,3,128,128]{3,2,1,0:T(8,128)(2,1)S(1)}, bf16[4,3,128,128]{3,2,1,0:T(8,128)(2,1)}, u32[]{:S(2)}) copy-start(bf16[4,3,128,128]{3,2,1,0:T(8,128)(2,1)} %mix.1) | copy-start | bytes 1179652
  61.7 17.6 %copy-start.5 = (s32[4,3]{1,0:T(4,128)S(1)}, s32[4,3]{1,0:T(4,128)}, u32[]{:S(2)}) copy-start(s32[4,3]{1,0:T(4,128)} %neighbours.1) | copy-start | bytes 148
  61.7 17.6 %copy-start.6 = (s32[4]{0:T(128)S(1)}, s32[4]{0:T(128)}, u32[]{:S(2)}) copy-start(s32[4]{0:T(128)} %degree.1) | copy-start | bytes 52
  61.7 17.5 %all-to-all-start = ((bf16[4,512,128]{2,1,0:T(8,128)(2,1)}), bf16[4,512,128]{2,1,0:T(8,128)(2,1)S(1)}, u32[]{:S(2)}, u32[]{:S(2)}) async-start(bf16[4,512,128]{2,1,0:T(8,128)(2,1)} %get-tuple-element.18), calls=%async_computation | async-start | bytes 1048576 | tf_op jit(solution)/shard_map/all_to_all | solution.py:342
  65.3 19.8 %collective-permute-start.12 = (bf16[3,256,256]{2,1,0:T(8,128)(2,1)S(1)}, bf16[3,256,256]{2,1,0:T(8,128)(2,1)S(1)}, u32[]{:S(2)}, u32[]{:S(2)}) collective-permute-start(bf16[3,256,256]{2,1,0:T(8,128)(2,1)S(1)} %pad_maximum_fusion.1.refs_0_), channel_id=1, source_target_pairs={{0,8},{4,12},{8,0},{12,4},{16,24},{20,28},{24,16},{28,20},{1,9},{5... | collective-permute-start | bytes 1179656 | tf_op jit(solution)/shard_map/ppermute | solution.py:30
  65.4 20.2 %collective-permute-start.14 = (bf16[3,256,256]{2,1,0:T(8,128)(2,1)S(1)}, bf16[3,256,256]{2,1,0:T(8,128)(2,1)S(1)}, u32[]{:S(2)}, u32[]{:S(2)}) collective-permute-start(bf16[3,256,256]{2,1,0:T(8,128)(2,1)S(1)} %pad_maximum_fusion.1.refs_0_), channel_id=1, source_target_pairs={{0,16},{4,20},{8,24},{12,28},{16,0},{20,4},{24,8},{28,12},{1,17},{... | collective-permute-start | bytes 1179656 | tf_op jit(solution)/shard_map/ppermute | solution.py:30
  67.9 17.8 %collective-permute-start.16 = (bf16[3,256,256]{2,1,0:T(8,128)(2,1)S(1)}, bf16[3,256,256]{2,1,0:T(8,128)(2,1)S(1)}, u32[]{:S(2)}, u32[]{:S(2)}) collective-permute-start(bf16[3,256,256]{2,1,0:T(8,128)(2,1)S(1)} %pad_maximum_fusion.1.refs_0_), channel_id=1, source_target_pairs={{0,24},{4,28},{8,16},{12,20},{16,8},{20,12},{24,0},{28,4},{1,25},{... | collective-permute-start | bytes 1179656 | tf_op jit(solution)/shard_map/ppermute | solution.py:30
  81.5 17.4 %all-to-all-start.1 = ((bf16[4,512,128]{2,1,0:T(8,128)(2,1)}), bf16[4,512,128]{2,1,0:T(8,128)(2,1)S(1)}, u32[]{:S(2)}, u32[]{:S(2)}) async-start(bf16[4,512,128]{2,1,0:T(8,128)(2,1)} %shard_map.119), calls=%async_computation.1 | async-start | bytes 1048576 | tf_op jit(solution)/shard_map/all_to_all | solution.py:352
  85.0 1.8 %collective-permute-start.11 = (bf16[3,256,256]{2,1,0:T(8,128)(2,1)S(1)}, bf16[3,256,256]{2,1,0:T(8,128)(2,1)S(1)}, u32[]{:S(2)}, u32[]{:S(2)}) collective-permute-start(bf16[3,256,256]{2,1,0:T(8,128)(2,1)S(1)} %pad_maximum_fusion.1.refs_0_), channel_id=1, source_target_pairs={{0,4},{4,0},{8,12},{12,8},{16,20},{20,16},{24,28},{28,24},{1,5},{5... | collective-permute-start | bytes 1179656 | tf_op jit(solution)/shard_map/ppermute | solution.py:30
  85.1 2.3 %collective-permute-start.13 = (bf16[3,256,256]{2,1,0:T(8,128)(2,1)S(1)}, bf16[3,256,256]{2,1,0:T(8,128)(2,1)S(1)}, u32[]{:S(2)}, u32[]{:S(2)}) collective-permute-start(bf16[3,256,256]{2,1,0:T(8,128)(2,1)S(1)} %collective-permute-done.12.refs_2_), channel_id=1, source_target_pairs={{0,4},{4,0},{8,12},{12,8},{16,20},{20,16},{24,28},{28,24},{1,5},{5... | collective-permute-start | bytes 1179656 | tf_op jit(solution)/shard_map/ppermute | solution.py:30
  85.6 2.5 %collective-permute-start.15 = (bf16[3,256,256]{2,1,0:T(8,128)(2,1)S(1)}, bf16[3,256,256]{2,1,0:T(8,128)(2,1)S(1)}, u32[]{:S(2)}, u32[]{:S(2)}) collective-permute-start(bf16[3,256,256]{2,1,0:T(8,128)(2,1)S(1)} %collective-permute-done.14.refs_4_), channel_id=1, source_target_pairs={{0,4},{4,0},{8,12},{12,8},{16,20},{20,16},{24,28},{28,24},{1,5},{5... | collective-permute-start | bytes 1179656 | tf_op jit(solution)/shard_map/ppermute | solution.py:30
  85.8 3.1 %collective-permute-start.17 = (bf16[3,256,256]{2,1,0:T(8,128)(2,1)S(1)}, bf16[3,256,256]{2,1,0:T(8,128)(2,1)S(1)}, u32[]{:S(2)}, u32[]{:S(2)}) collective-permute-start(bf16[3,256,256]{2,1,0:T(8,128)(2,1)S(1)} %collective-permute-done.16.refs_6_), channel_id=1, source_target_pairs={{0,4},{4,0},{8,12},{12,8},{16,20},{20,16},{24,28},{28,24},{1,5},{5... | collective-permute-start | bytes 1179656 | tf_op jit(solution)/shard_map/ppermute | solution.py:30
  (16 other events, 59.4 us)

commit v4 on v3

--- a/solution.py
+++ b/solution.py
@@ -9,6 +9,8 @@
 
 HEADS = 4
 SPREAD = 8
+FIRST_BITS = (0, 2, 4, 6, 1, 3, 5, 7)
+SECOND_BITS = (0, 4, 2, 6, 1, 5, 3, 7)
 LANES = 128
 F32 = jnp.float32
 BF16 = jnp.bfloat16
@@ -36,21 +38,30 @@
 
 
 def quarter_of(block):
-    return lax.rem(block, 2) + 2 * lax.rem(lax.div(block, 4), 2)
+    parity = lax.rem(lax.div(block, 2) + lax.div(block, 4), 2)
+    return lax.rem(block, 2) + 2 * parity
 
 
 def row_sum(value):
     return jnp.sum(value, axis=0, keepdims=True)
 
 
-def attention_kernel(zones, reach, place, pattern, states, *refs):
-    earlier, refs = refs[:reach], refs[reach:]
-    (gain_attn, gain_mix, own_qkv, own_attn), refs = refs[:4], refs[4:]
-    pieces, refs = refs[:4], refs[4:]
-    after_out, mixin_out, weights, w_turned, normed, projected, context = refs
-    steps, zone_rows, width = states.shape
+def norm_kernel(*refs):
+    blocks, (gain_attn, normed) = refs[:-2], refs[-2:]
+    steps, zone_rows, _ = blocks[0].shape
+    gain = gain_attn[...]
+    for index, block in enumerate(blocks):
+        for step in range(steps):
+            row = (index * steps + step) * zone_rows
+            normed[row : row + zone_rows, :] = rms_scale(block[step].astype(F32), gain).astype(BF16)
+
+
+def attention_kernel(zones, reach, steps, place, pattern, normed, own_qkv, own_attn, *refs):
+    pieces, (context_out, attn_out, weights, w_turned, projected, context) = refs[:-6], refs[-6:]
+    key_count = (reach + 1) * steps
+    zone_rows = normed.shape[0] // key_count
+    width = normed.shape[1]
     head_size = width // HEADS
-    key_count = (reach + 1) * steps
     my_block, my_zone = place[0], place[1]
     shard = own_qkv.shape[0]
 
@@ -59,23 +70,18 @@
         weights[index, own_rows, :] = own_qkv[:, index * width : (index + 1) * width]
     weights[3, own_rows, :] = own_attn[...]
     my_quarter = quarter_of(my_block)
-    for bits in range(4):
-        for step in range(1, zones):
-            source = lax.rem(my_zone - step + zones, zones)
-            rows = pl.ds(pl.multiple_of(source * shard, shard), shard)
-            weights[my_quarter ^ bits, rows, :] = pieces[bits][step - 1]
+    half = shard // 2
+    for step in range(1, zones):
+        source = lax.rem(my_zone - step + zones, zones)
+        for piece, bits, part in zip(pieces, (0, 1, 2, 2, 3, 3), (0, 0, 0, 1, 0, 1)):
+            rows = pl.ds(pl.multiple_of(source * shard + part * half, half), piece.shape[1])
+            weights[my_quarter ^ bits, rows, :] = piece[step - 1]
+    attn_out[...] = weights[3]
     for index in range(3):
         for block in range(width // LANES):
             first = block * LANES
             rows = slice(index * width + first, index * width + first + LANES)
             w_turned[rows, :] = weights[index, :, first : first + LANES].T
-
-    blocks = list(earlier) + [states]
-    gain = gain_attn[...]
-    for index, block in enumerate(blocks):
-        for step in range(steps):
-            row = (index * steps + step) * zone_rows
-            normed[row : row + zone_rows, :] = rms_scale(block[step].astype(F32), gain).astype(BF16)
 
     def project(first, last, weight_rows):
         return lax.dot_general(
@@ -148,27 +154,41 @@
 
     lax.fori_loop(0, HEADS, head_body, 0)
 
-    mix_gain = gain_mix[...]
     for step in range(steps):
         rows = slice(step * zone_rows, (step + 1) * zone_rows)
-        turned = context[:, rows].T.astype(BF16)
-        after = states[step].astype(F32) + jnp.dot(turned, weights[3], preferred_element_type=F32)
+        context_out[rows, :] = context[:, rows].T.astype(BF16)
+
+
+def project_kernel(place, states, context, w_attn, gain_mix, *refs):
+    (after_out, *outs), parts = refs[:-1], refs[-1]
+    steps, zone_rows, _ = states.shape
+    zones, _, part = parts.shape
+    my_zone = place[1]
+    gain = gain_mix[...]
+    for step in range(steps):
+        rows = slice(step * zone_rows, (step + 1) * zone_rows)
+        after = states[step].astype(F32) + jnp.dot(
+            context[rows, :], w_attn[...], preferred_element_type=F32
+        )
         after_out[rows, :] = after
-        mixin = rms_scale(after, mix_gain).astype(BF16)
-        if len(mixin_out.shape) == 2:
-            mixin_out[rows, :] = mixin
-        else:
-            part = mixin_out.shape[-1]
-            for index in range(mixin_out.shape[0]):
-                mixin_out[index, rows, :] = mixin[:, index * part : (index + 1) * part]
-
-
-def mixing_kernel(steps, neighbours, degree, mix, items, out):
-    block_count, slots, zone_rows, _ = mix.shape
+        mixin = rms_scale(after, gain).astype(BF16)
+        for index in range(zones):
+            parts[index, rows, :] = mixin[:, index * part : (index + 1) * part]
+    for step in range(zones):
+        outs[step][...] = parts[lax.rem(my_zone + step, zones)]
+
+
+def mixing_kernel(steps, zones, place, neighbours, degree, mix, *refs):
+    arrived, outs, items = refs[:zones], refs[zones : 2 * zones], refs[-1]
+    _, slots, zone_rows, _ = mix.shape
     part = items.shape[-1]
+    my_zone = place[1]
     group = 2 if part % LANES == 0 and steps % 2 == 0 else 1
-
-    def block_body(block, carry):
+    for step in range(zones):
+        items[lax.rem(my_zone - step + zones, zones)] = arrived[step][...]
+
+    for target in range(zones):
+        block = lax.rem(my_zone + target, zones)
         left = []
         for slot in range(slots):
             tile = mix[block, slot]
@@ -190,51 +210,45 @@
             result = jnp.dot(left, jnp.concatenate(right, axis=0), preferred_element_type=F32)
             for index in range(group):
                 rows = slice((step + index) * zone_rows, (step + index + 1) * zone_rows)
-                out[block, rows, :] = result[:, index * part : (index + 1) * part].astype(BF16)
-        return carry
-
-    lax.fori_loop(0, block_count, block_body, 0)
-
-
-def ffn_kernel(zones, place, spatial, after_attn, gain_ffn, own_in, own_out, *refs):
-    pieces, (out, w_in, w_out, after_mix, ffn_in) = refs[:SPREAD], refs[SPREAD:]
+                outs[target][rows, :] = result[:, index * part : (index + 1) * part].astype(BF16)
+
+
+def ffn_kernel(zones, place, after_attn, gain_ffn, own_in, own_out, *refs):
+    arrived, refs = refs[:zones], refs[zones:]
+    pieces, (out, w_in, w_out, after_mix, ffn_in, parts) = refs[:-6], refs[-6:]
     rows_all, width = after_attn.shape
     my_block, my_zone = place[0], place[1]
     in_shard, hidden = own_in.shape
     out_shard = own_out.shape[0]
     in_cols, out_rows = hidden // SPREAD, out_shard // SPREAD
-    folds = width // in_cols
-
+
+    for step in range(zones):
+        parts[lax.rem(my_zone - step + zones, zones)] = arrived[step][...]
     start = pl.multiple_of(my_zone * in_shard, in_shard)
     for index in range(SPREAD):
         w_in[index, pl.ds(start, in_shard), :] = own_in[:, index * in_cols : (index + 1) * in_cols]
     w_out[pl.ds(pl.multiple_of(my_zone * out_shard, out_shard), out_shard), :] = own_out[...]
-    for bits in range(SPREAD):
+    for index, bits in enumerate(FIRST_BITS + SECOND_BITS):
         slot = lax.rem(my_block, SPREAD) ^ bits
+        piece = pieces[index]
         for step in range(1, zones):
             source = lax.rem(my_zone - step + zones, zones)
-            piece = pieces[bits]
-            w_in[slot, pl.ds(pl.multiple_of(source * in_shard, in_shard), in_shard), :] = piece[
-                step - 1, :in_shard, :
-            ]
-            start = pl.multiple_of(source * out_shard + slot * out_rows, out_rows)
-            for fold in range(folds):
-                first = in_shard + fold * out_rows
-                w_out[pl.ds(start, out_rows), fold * in_cols : (fold + 1) * in_cols] = piece[
-                    step - 1, first : first + out_rows, :
-                ]
+            if index < SPREAD:
+                rows = pl.ds(pl.multiple_of(source * in_shard, in_shard), in_shard)
+                w_in[slot, rows, :] = piece[step - 1]
+            else:
+                rows = pl.ds(pl.multiple_of(source * out_shard + slot * out_rows, out_rows), out_rows)
+                w_out[rows, :] = piece[step - 1]
 
     gain = gain_ffn[...]
     span = 128
+    part = parts.shape[-1]
     for first in range(0, rows_all, span):
         rows = slice(first, first + span)
-        if len(spatial.shape) == 2:
-            moved = spatial[rows, :]
-        else:
-            moved = jnp.concatenate([spatial[index, rows, :] for index in range(spatial.shape[0])], axis=1)
-        total = after_attn[rows, :] + moved.astype(F32)
-        after_mix[rows, :] = total
-        ffn_in[rows, :] = rms_scale(total, gain).astype(BF16)
+        for index in range(zones):
+            cols = slice(index * part, (index + 1) * part)
+            after_mix[rows, cols] = after_attn[rows, cols] + parts[index, rows, :].astype(F32)
+        ffn_in[rows, :] = rms_scale(after_mix[rows, :], gain).astype(BF16)
     span = 256
     for first in range(0, rows_all, span):
         rows = slice(first, first + span)
@@ -288,71 +302,103 @@
     my_block, my_zone = lax.axis_index("tm"), lax.axis_index("zone")
     place = jnp.stack([my_block, my_zone]).astype(jnp.int32)
     key_count = (reach + 1) * steps
-
+    hidden = w_in.shape[1]
+    in_cols = hidden // SPREAD
+    out_rows = w_out.shape[0] // SPREAD
+    part = width // zones
+    rotations = range(1, zones)
+
+    before = shifted(states, "tm", 2)
     first = lax.dynamic_slice_in_dim(
         jnp.concatenate([w_qkv, w_out_attn], axis=1), quarter_of(my_block) * width, width, axis=1
     )
-    direct = [rotated(first, "zone", step) for step in range(1, zones)]
-    earlier = [shifted(states, "tm", offset) for offset in range(reach, 0, -1)]
-    direct = jnp.stack(direct)
-    over = swapped(direct, "tm", 4)
-    quarters = [direct, swapped(direct, "tm", 1), over, swapped(over, "tm", 1)]
-
-    in_cols = w_in.shape[1] // SPREAD
-    out_rows = w_out.shape[0] // SPREAD
+    direct = [rotated(first, "zone", step) for step in rotations]
     slot = my_block % SPREAD
-    out_slice = lax.dynamic_slice_in_dim(w_out, slot * out_rows, out_rows, axis=0)
-    second = jnp.concatenate(
-        [lax.dynamic_slice_in_dim(w_in, slot * in_cols, in_cols, axis=1)]
-        + [out_slice[:, at : at + in_cols] for at in range(0, width, in_cols)],
-        axis=0,
-    )
-    second, _ = lax.optimization_barrier((second, direct))
-    across = jnp.stack([rotated(second, "zone", step) for step in range(1, zones)])
-    across, quarters = lax.optimization_barrier((across, quarters))
-    pieces = {0: across}
-    for bits in range(2, SPREAD, 2):
-        pieces[bits] = swapped(across, "tm", bits)
-    for bits in range(0, SPREAD, 2):
-        pieces[bits + 1] = swapped(pieces[bits], "tm", 1)
-
-    part = width // zones
-    wide = part % LANES == 0
-    mixin_shape = (zones, rows, part) if wide else (rows, width)
-    after_attn, mixin = call(
-        functools.partial(attention_kernel, zones, reach),
-        (jax.ShapeDtypeStruct((rows, width), F32), jax.ShapeDtypeStruct(mixin_shape, BF16)),
+    slice_in = lax.dynamic_slice_in_dim(w_in, slot * in_cols, in_cols, axis=1)
+    slice_out = lax.dynamic_slice_in_dim(w_out, slot * out_rows, out_rows, axis=0)
+
+    half = first.shape[0] // 2
+    upper = jnp.stack([piece[:half] for piece in direct])
+    lower = jnp.stack([piece[half:] for piece in direct])
+    direct = jnp.concatenate([upper, lower], axis=1)
+    over_x, over_y = swapped(upper, "tm", 2), swapped(lower, "tm", 4)
+    quarters = [direct, swapped(direct, "tm", 1), over_x, over_y]
+    quarters += [swapped(over_x, "tm", 1), swapped(over_y, "tm", 1)]
+
+    last = swapped(jnp.where(my_block % 2 == 1, before, states), "tm", 1)
+    normed = call(
+        norm_kernel,
+        jax.ShapeDtypeStruct((key_count * zone_rows, width), BF16),
+        [],
+        8 * key_count * zone_rows * width,
+        (),
+        8,
+        [before, last, states, gain_attn.reshape(1, -1)],
+    )
+
+    packed = jnp.concatenate(
+        [slice_in] + [slice_out[:, at : at + in_cols] for at in range(0, width, in_cols)], axis=0
+    )
+    packed, _ = lax.optimization_barrier((packed, direct))
+    across = jnp.stack([rotated(packed, "zone", step) for step in rotations])
+
+    context, w_attn = call(
+        functools.partial(attention_kernel, zones, reach, steps),
+        (
+            jax.ShapeDtypeStruct((rows, width), BF16),
+            jax.ShapeDtypeStruct((width, width), BF16),
+        ),
         [
             pltpu.VMEM((4, width, width), BF16),
             pltpu.VMEM((3 * width, width), BF16),
-            pltpu.VMEM((key_count * zone_rows, width), BF16),
             pltpu.VMEM((3 * width, key_count * zone_rows), F32),
             pltpu.VMEM((width, rows), F32),
         ],
-        2 * rows * width * width * 10,
+        2 * rows * width * width * 20,
         (0, 1),
-        24,
-        [place, pattern, states]
-        + earlier
-        + [gain_attn.reshape(1, -1), gain_mix.reshape(1, -1), w_qkv, w_out_attn]
-        + quarters,
-    )
-    if not wide:
-        mixin = jnp.transpose(mixin.reshape(rows, zones, part), (1, 0, 2))
-    items = lax.all_to_all(mixin, "zone", split_axis=0, concat_axis=0, tiled=True)
+        22,
+        [place, pattern, normed, w_qkv, w_out_attn] + quarters,
+    )
+    context, across = lax.optimization_barrier((context, across))
+
+    chunk = jax.ShapeDtypeStruct((rows, part), BF16)
+    after_attn, *chunks = call(
+        project_kernel,
+        (jax.ShapeDtypeStruct((rows, width), F32),) + (chunk,) * zones,
+        [pltpu.VMEM((zones, rows, part), BF16)],
+        2 * rows * width * width,
+        (0,),
+        8,
+        [place, states, context, w_attn, gain_mix.reshape(1, -1)],
+    )
+    arrived = [chunks[0]] + [rotated(chunks[step], "zone", step) for step in rotations]
+
+    in_shard = w_in.shape[0]
+    from_in = across[:, :in_shard]
+    from_out = jnp.concatenate(
+        [
+            across[:, in_shard + fold * out_rows : in_shard + (fold + 1) * out_rows]
+            for fold in range(width // in_cols)
+        ],
+        axis=2,
+    )
+    ins, outs = [from_in], [from_out]
+    for bits_in, bits_out in ((2, 4), (4, 2)):
+        ins += [swapped(value, "tm", bits_in) for value in ins]
+        outs += [swapped(value, "tm", bits_out) for value in outs]
+    pieces = ins + [swapped(value, "tm", 1) for value in ins]
+    pieces += outs + [swapped(value, "tm", 1) for value in outs]
+
     spatial = call(
-        functools.partial(mixing_kernel, steps),
-        jax.ShapeDtypeStruct((zones, rows, part), BF16),
-        [],
+        functools.partial(mixing_kernel, steps, zones),
+        (chunk,) * zones,
+        [pltpu.VMEM((zones, rows, part), BF16)],
         2 * rows * width * zone_rows * 3,
-        (0, 1),
+        (0, 1, 2),
         8,
-        [neighbours, degree, mix, items],
-    )
-    spatial = lax.all_to_all(spatial, "zone", split_axis=0, concat_axis=0, tiled=True)
-    if not wide:
-        spatial = jnp.transpose(spatial, (1, 0, 2)).reshape(rows, width)
-    hidden = w_in.shape[1]
+        [place, neighbours, degree, mix] + arrived,
+    )
+    arrived = [spatial[0]] + [rotated(spatial[step], "zone", step) for step in rotations]
     evolved = call(
         functools.partial(ffn_kernel, zones),
         jax.ShapeDtypeStruct((rows, width), BF16),
@@ -361,12 +407,12 @@
             pltpu.VMEM((hidden, width), BF16),
             pltpu.VMEM((rows, width), F32),
             pltpu.VMEM((rows, width), BF16),
+            pltpu.VMEM((zones, rows, part), BF16),
         ],
         4 * rows * width * hidden,
         (0,),
         16,
-        [place, spatial, after_attn, gain_ffn.reshape(1, -1), w_in, w_out]
-        + [pieces[bits] for bits in range(SPREAD)],
+        [place, after_attn, gain_ffn.reshape(1, -1), w_in, w_out] + arrived + pieces,
     )
     return evolved.reshape(steps, zone_rows, width)
 

time: 108 us -> 86.3 us (0.80)
  waiting for transfers between devices: 53.1 us -> 34.7 us
  local copies, waits for them, and re-layouts: 8.11 us -> 2.07 us
  starting transfers between devices: 30.5 us -> 33.4 us
  other arithmetic: 2.28 us -> 3.65 us
  Pallas kernels: 13.2 us -> 11.9 us
    all_to_all x2 -> x0, waiting for transfers between devices: 19.3 us -> none  [the longest x1 9.92 us: on_device(): lax.all_to_all(mixin, 'zone', split_axis=0, concat_axis=0, tiled=True)]
    ppermute x10 -> x20, waiting for transfers between devices: 17.9 us -> 1.86 us  [swapped(): lax.ppermute(value, axis, [(source, source ^ bits) for source in range(co...]
    ppermute x6 -> x12, waiting for transfers between devices: 15.9 us -> 28 us  [rotated(): lax.ppermute(value, axis, [(source, (source + steps) % count) for source...]
    unnamed x40 -> x24, local copies, waits for them, and re-layouts: 8.09 us -> 0.38 us
    all_to_all x2 -> x0, starting transfers between devices: 7.07 us -> none  [the longest x1 3.6 us: on_device(): lax.all_to_all(mixin, 'zone', split_axis=0, concat_axis=0, tiled=True)]
    ppermute x6 -> x12, starting transfers between devices: 11.3 us -> 17.7 us  [rotated(): lax.ppermute(value, axis, [(source, (source + steps) % count) for source...]
    ppermute x10 -> x20, starting transfers between devices: 6.63 us -> 12.2 us  [swapped(): lax.ppermute(value, axis, [(source, source ^ bits) for source in range(co...]
    ppermute x2 -> x1, waiting for transfers between devices: 0.01 us -> 4.81 us  [shifted(): lax.ppermute(value, axis, [(source, source + steps) for source in range(c...]
  transfers between devices with their start and end apart: 20 -> 33, of which waited for: 9 -> 14; matrix products, arithmetic and copies ran while one was open for 1% -> 5% of each run, Pallas kernels for 2% -> 3%
where the time goes in v4:
time: 86.3 us; the launch traced here: 86 us
  waiting for transfers between devices  34.7 us (40%)
  starting transfers between devices  33.4 us (39%)
  Pallas kernels  11.9 us (14%)
  other arithmetic  3.65 us (4%)
  local copies, waits for them, and re-layouts  2.07 us (2%)
    ppermute x12, waiting for transfers between devices, rotated(): lax.ppermute(value, axis, [(source, (source + steps) % count) for source...  28 us
    ppermute x12, starting transfers between devices, rotated(): lax.ppermute(value, axis, [(source, (source + steps) % count) for source...  17.7 us
    ppermute x20, starting transfers between devices, swapped(): lax.ppermute(value, axis, [(source, source ^ bits) for source in range(co...  12.2 us
    pallas_call x5, Pallas kernels, call(): pl.pallas_call(kernel, out_shape=out_shape, in_specs=in_specs, out_specs=...  11.9 us
    ppermute x1, waiting for transfers between devices, shifted(): lax.ppermute(value, axis, [(source, source + steps) for source in range(c...  4.81 us
    ppermute x1, starting transfers between devices, shifted(): lax.ppermute(value, axis, [(source, source + steps) for source in range(c...  3.42 us
    ppermute x20, waiting for transfers between devices, swapped(): lax.ppermute(value, axis, [(source, source ^ bits) for source in range(co...  1.86 us
  transfers between devices with their start and end apart: 33, of which 14 were waited for; matrix products, arithmetic and copies ran while one was open for 5% of the time, Pallas kernels for 3%

profile of v4, /device:TPU:0, one launch (start us, length us, event | category | flops | bytes accessed | tf_op | source)
XLA Modules:
  0.0 86.0 jit_solution(13217612476371371274)
XLA Ops:
  1.0 3.1 %collective-permute-start.2 = (bf16[128,512]{1,0:T(8,128)(2,1)S(1)}, bf16[128,512]{1,0:T(8,128)(2,1)S(1)}, u32[]{:S(2)}, u32[]{:S(2)}) collective-permute-start(bf16[128,512]{1,0:T(8,128)(2,1)S(1)} %fusion), channel_id=1, source_target_pairs={{0,1},{1,2},{2,3},{3,0},{4,5},{5,6},{6,7},{7,4},{8,9},{9,10},{10,1... | collective-permute-start | bytes 393224 | tf_op jit(solution)/shard_map/ppermute | solution.py:27
  4.1 2.6 %collective-permute-start.3 = (bf16[128,512]{1,0:T(8,128)(2,1)S(1)}, bf16[128,512]{1,0:T(8,128)(2,1)S(1)}, u32[]{:S(2)}, u32[]{:S(2)}) collective-permute-start(bf16[128,512]{1,0:T(8,128)(2,1)S(1)} %fusion), channel_id=1, source_target_pairs={{0,2},{1,3},{2,0},{3,1},{4,6},{5,7},{6,4},{7,5},{8,10},{9,11},{10,... | collective-permute-start | bytes 393224 | tf_op jit(solution)/shard_map/ppermute | solution.py:27
  6.7 1.3 %collective-permute-start.4 = (bf16[128,512]{1,0:T(8,128)(2,1)S(1)}, bf16[128,512]{1,0:T(8,128)(2,1)S(1)}, u32[]{:S(2)}, u32[]{:S(2)}) collective-permute-start(bf16[128,512]{1,0:T(8,128)(2,1)S(1)} %fusion), channel_id=1, source_target_pairs={{0,3},{1,0},{2,1},{3,2},{4,7},{5,4},{6,5},{7,6},{8,11},{9,8},{10,9... | collective-permute-start | bytes 393224 | tf_op jit(solution)/shard_map/ppermute | solution.py:27
  8.0 3.4 %collective-permute-start = (bf16[4,128,512]{2,1,0:T(8,128)(2,1)}, bf16[4,128,512]{2,1,0:T(8,128)(2,1)S(1)}, u32[]{:S(2)}, u32[]{:S(2)}) collective-permute-start(bf16[4,128,512]{2,1,0:T(8,128)(2,1)} %states.1), channel_id=1, source_target_pairs={{0,8},{4,12},{8,16},{12,20},{16,24},{20,28},{1,9},{5,13},{9,17},{1... | collective-permute-start | bytes 1572872 | tf_op jit(solution)/shard_map/ppermute | solution.py:22
  13.8 1.5 %collective-permute-done.3 = bf16[128,512]{1,0:T(8,128)(2,1)S(1)} collective-permute-done((bf16[128,512]{1,0:T(8,128)(2,1)S(1)}, bf16[128,512]{1,0:T(8,128)(2,1)S(1)}, u32[]{:S(2)}, u32[]{:S(2)}) %collective-permute-start.3) | collective-permute-done | bytes 131104 | tf_op jit(solution)/shard_map/ppermute | solution.py:27
  15.4 2.3 %collective-permute-start.11 = (bf16[256,256]{1,0:T(8,128)(2,1)}, bf16[256,256]{1,0:T(8,128)(2,1)}, u32[]{:S(2)}, u32[]{:S(2)}) collective-permute-start(bf16[256,256]{1,0:T(8,128)(2,1)} %pad_maximum_fusion.4), channel_id=1, source_target_pairs={{0,2},{1,3},{2,0},{3,1},{4,6},{5,7},{6,4},{7,5},{8,10},{9,11},{10,... | collective-permute-start | bytes 393224 | tf_op jit(solution)/shard_map/ppermute | solution.py:27
  17.7 1.6 %collective-permute-start.6 = (bf16[3,64,512]{2,1,0:T(8,128)(2,1)S(1)}, bf16[3,64,512]{2,1,0:T(8,128)(2,1)S(1)}, u32[]{:S(2)}, u32[]{:S(2)}) collective-permute-start(bf16[3,64,512]{2,1,0:T(8,128)(2,1)S(1)} %pad_maximum_fusion.1), channel_id=1, source_target_pairs={{0,8},{4,12},{8,0},{12,4},{16,24},{20,28},{24,16},{28,20},{1,9},{5... | collective-permute-start | bytes 589832 | tf_op jit(solution)/shard_map/ppermute | solution.py:32
  19.3 4.8 %collective-permute-done.refs_0_ = bf16[4,128,512]{2,1,0:T(8,128)(2,1)S(1)} collective-permute-done((bf16[4,128,512]{2,1,0:T(8,128)(2,1)}, bf16[4,128,512]{2,1,0:T(8,128)(2,1)S(1)}, u32[]{:S(2)}, u32[]{:S(2)}) %collective-permute-start) | collective-permute-done | bytes 524320 | tf_op jit(solution)/shard_map/ppermute | solution.py:22
  25.0 3.3 %collective-permute-start.7 = (bf16[3,64,512]{2,1,0:T(8,128)(2,1)}, bf16[3,64,512]{2,1,0:T(8,128)(2,1)S(1)}, u32[]{:S(2)}, u32[]{:S(2)}) collective-permute-start(bf16[3,64,512]{2,1,0:T(8,128)(2,1)} %pad_maximum_fusion.2), channel_id=1, source_target_pairs={{0,16},{4,20},{8,24},{12,28},{16,0},{20,4},{24,8},{28,12},{1,17},{... | collective-permute-start | bytes 589832 | tf_op jit(solution)/shard_map/ppermute | solution.py:32
  28.5 6.0 %collective-permute-done.12 = bf16[256,256]{1,0:T(8,128)(2,1)} collective-permute-done((bf16[256,256]{1,0:T(8,128)(2,1)}, bf16[256,256]{1,0:T(8,128)(2,1)}, u32[]{:S(2)}, u32[]{:S(2)}) %collective-permute-start.12) | collective-permute-done | bytes 131104 | tf_op jit(solution)/shard_map/ppermute | solution.py:27
  35.8 5.8 %collective-permute-done.10 = bf16[256,256]{1,0:T(8,128)(2,1)} collective-permute-done((bf16[256,256]{1,0:T(8,128)(2,1)}, bf16[256,256]{1,0:T(8,128)(2,1)}, u32[]{:S(2)}, u32[]{:S(2)}) %collective-permute-start.10) | collective-permute-done | bytes 131104 | tf_op jit(solution)/shard_map/ppermute | solution.py:27
  43.7 4.7 %shard_map.119 = (bf16[512,512]{1,0:T(8,128)(2,1)S(1)}, bf16[512,512]{1,0:T(8,128)(2,1)S(1)}) custom-call(s32[2]{0:T(128)S(1)} %pad_add_fusion.place, s32[1,2]{1,0:T(1,128)S(1)} %copy-done.11, bf16[1536,512]{1,0:T(8,128)(2,1)S(1)} %shard_map.118.normed, bf16[128,1536]{1,0:T(8,128)(2,1)S(1)} %copy-done.1, bf16[128,512]{1,0:T(8,128)(2,1)S(1)} %copy-done.3, ...), custom_call_target="tpu_custom_call" | custom-call | flops 5368709120 | bytes 3670032 | tf_op jit(solution)/shard_map/pallas_call | solution.py:273
  48.7 1.1 %shard_map.120 = (f32[512,512]{1,0:T(8,128)S(1)}, bf16[512,128]{1,0:T(8,128)(2,1)S(1)}, bf16[512,128]{1,0:T(8,128)(2,1)S(1)}, bf16[512,128]{1,0:T(8,128)(2,1)S(1)}, bf16[512,128]{1,0:T(8,128)(2,1)S(1)}) custom-call(s32[2]{0:T(128)S(1)} %pad_add_fusion.place, bf16[4,128,512]{2,1,0:T(8,128)(2,1)S(1)} %copy-done, ...), custom_call_target="tpu_custom_call" | custom-call | flops 268435456 | bytes 1574920 | tf_op jit(solution)/shard_map/pallas_call | solution.py:273
  49.9 1.3 %collective-permute-start.14 = (bf16[512,128]{1,0:T(8,128)(2,1)S(1)}, bf16[512,128]{1,0:T(8,128)(2,1)S(1)}, u32[]{:S(2)}, u32[]{:S(2)}) collective-permute-start(bf16[512,128]{1,0:T(8,128)(2,1)S(1)} %get-tuple-element.26), channel_id=1, source_target_pairs={{0,2},{1,3},{2,0},{3,1},{4,6},{5,7},{6,4},{7,5},{8,10},{9,11},{10,... | collective-permute-start | bytes 393224 | tf_op jit(solution)/shard_map/ppermute | solution.py:27
  51.2 2.5 %collective-permute-start.15 = (bf16[512,128]{1,0:T(8,128)(2,1)S(1)}, bf16[512,128]{1,0:T(8,128)(2,1)S(1)}, u32[]{:S(2)}, u32[]{:S(2)}) collective-permute-start(bf16[512,128]{1,0:T(8,128)(2,1)S(1)} %get-tuple-element.27), channel_id=1, source_target_pairs={{0,3},{1,0},{2,1},{3,2},{4,7},{5,4},{6,5},{7,6},{8,11},{9,8},{10,9... | collective-permute-start | bytes 393224 | tf_op jit(solution)/shard_map/ppermute | solution.py:27
  54.8 3.3 %collective-permute-done.13.refs_1_ = bf16[512,128]{1,0:T(8,128)(2,1)S(1)} collective-permute-done((bf16[512,128]{1,0:T(8,128)(2,1)S(1)}, bf16[512,128]{1,0:T(8,128)(2,1)S(1)}, u32[]{:S(2)}, u32[]{:S(2)}) %collective-permute-start.13) | collective-permute-done | bytes 131104 | tf_op jit(solution)/shard_map/ppermute | solution.py:27
  58.1 3.1 %collective-permute-done.14.refs_2_ = bf16[512,128]{1,0:T(8,128)(2,1)S(1)} collective-permute-done((bf16[512,128]{1,0:T(8,128)(2,1)S(1)}, bf16[512,128]{1,0:T(8,128)(2,1)S(1)}, u32[]{:S(2)}, u32[]{:S(2)}) %collective-permute-start.14) | collective-permute-done | bytes 131104 | tf_op jit(solution)/shard_map/ppermute | solution.py:27
  62.0 1.5 %collective-permute-start.20 = (bf16[3,128,256]{2,1,0:T(8,128)(2,1)S(1)}, bf16[3,128,256]{2,1,0:T(8,128)(2,1)S(1)}, u32[]{:S(2)}, u32[]{:S(2)}) collective-permute-start(bf16[3,128,256]{2,1,0:T(8,128)(2,1)S(1)} %slice.41.refs_4_), channel_id=1, source_target_pairs={{0,16},{4,20},{8,24},{12,28},{16,0},{20,4},{24,8},{28,12},{1,17},{... | collective-permute-start | bytes 589832 | tf_op jit(solution)/shard_map/ppermute | solution.py:32
  64.6 1.8 %collective-permute-start.16 = (bf16[512,128]{1,0:T(8,128)(2,1)S(1)}, bf16[512,128]{1,0:T(8,128)(2,1)S(1)}, u32[]{:S(2)}, u32[]{:S(2)}) collective-permute-start(bf16[512,128]{1,0:T(8,128)(2,1)S(1)} %get-tuple-element.29), channel_id=1, source_target_pairs={{0,1},{1,2},{2,3},{3,0},{4,5},{5,6},{6,7},{7,4},{8,9},{9,10},{10,1... | collective-permute-start | bytes 393224 | tf_op jit(solution)/shard_map/ppermute | solution.py:27
  67.6 1.5 %collective-permute-start.21 = (bf16[3,128,256]{2,1,0:T(8,128)(2,1)S(1)}, bf16[3,128,256]{2,1,0:T(8,128)(2,1)S(1)}, u32[]{:S(2)}, u32[]{:S(2)}) collective-permute-start(bf16[3,128,256]{2,1,0:T(8,128)(2,1)S(1)} %collective-permute-done.19.refs_5_), channel_id=1, source_target_pairs={{0,16},{4,20},{8,24},{12,28},{16,0},{20,4},{24,8},{28,12},{1,17},{... | collective-permute-start | bytes 589832 | tf_op jit(solution)/shard_map/ppermute | solution.py:32
  70.2 2.4 %collective-permute-done.16.refs_1_ = bf16[512,128]{1,0:T(8,128)(2,1)S(1)} collective-permute-done((bf16[512,128]{1,0:T(8,128)(2,1)S(1)}, bf16[512,128]{1,0:T(8,128)(2,1)S(1)}, u32[]{:S(2)}, u32[]{:S(2)}) %collective-permute-start.16) | collective-permute-done | bytes 131104 | tf_op jit(solution)/shard_map/ppermute | solution.py:27
  73.6 4.5 %collective-permute-done.17.refs_2_ = bf16[512,128]{1,0:T(8,128)(2,1)S(1)} collective-permute-done((bf16[512,128]{1,0:T(8,128)(2,1)S(1)}, bf16[512,128]{1,0:T(8,128)(2,1)S(1)}, u32[]{:S(2)}, u32[]{:S(2)}) %collective-permute-start.17) | collective-permute-done | bytes 131104 | tf_op jit(solution)/shard_map/ppermute | solution.py:27
  78.1 1.3 %collective-permute-done.18.refs_3_ = bf16[512,128]{1,0:T(8,128)(2,1)S(1)} collective-permute-done((bf16[512,128]{1,0:T(8,128)(2,1)S(1)}, bf16[512,128]{1,0:T(8,128)(2,1)S(1)}, u32[]{:S(2)}, u32[]{:S(2)}) %collective-permute-start.18) | collective-permute-done | bytes 131104 | tf_op jit(solution)/shard_map/ppermute | solution.py:27
  81.7 4.3 %shard_map.122 = bf16[512,512]{1,0:T(8,128)(2,1)} custom-call(s32[2]{0:T(128)S(1)} %pad_add_fusion.place, f32[512,512]{1,0:T(8,128)S(1)} %get-tuple-element.23.after_attn, f32[1,512]{1,0:T(1,128)S(1)} %bitcast.23, bf16[128,2048]{1,0:T(8,128)(2,1)S(1)} %copy-done.4, bf16[512,512]{1,0:T(8,128)(2,1)S(1)} %copy-done.5, ...), custom_call_target="tpu_custom_call" | custom-call | flops 2147483648 | bytes 5769224 | tf_op jit(solution)/shard_map/pallas_call | solution.py:273
  (87 shorter events, 16.4 us)
Async XLA Ops:
  1.0 12.8 %collective-permute-start.2 = (bf16[128,512]{1,0:T(8,128)(2,1)S(1)}, bf16[128,512]{1,0:T(8,128)(2,1)S(1)}, u32[]{:S(2)}, u32[]{:S(2)}) collective-permute-start(bf16[128,512]{1,0:T(8,128)(2,1)S(1)} %fusion), channel_id=1, source_target_pairs={{0,1},{1,2},{2,3},{3,0},{4,5},{5,6},{6,7},{7,4},{8,9},{9,10},{10,1... | collective-permute-start | bytes 393224 | tf_op jit(solution)/shard_map/ppermute | solution.py:27
  4.1 11.2 %collective-permute-start.3 = (bf16[128,512]{1,0:T(8,128)(2,1)S(1)}, bf16[128,512]{1,0:T(8,128)(2,1)S(1)}, u32[]{:S(2)}, u32[]{:S(2)}) collective-permute-start(bf16[128,512]{1,0:T(8,128)(2,1)S(1)} %fusion), channel_id=1, source_target_pairs={{0,2},{1,3},{2,0},{3,1},{4,6},{5,7},{6,4},{7,5},{8,10},{9,11},{10,... | collective-permute-start | bytes 393224 | tf_op jit(solution)/shard_map/ppermute | solution.py:27
  6.7 8.7 %collective-permute-start.4 = (bf16[128,512]{1,0:T(8,128)(2,1)S(1)}, bf16[128,512]{1,0:T(8,128)(2,1)S(1)}, u32[]{:S(2)}, u32[]{:S(2)}) collective-permute-start(bf16[128,512]{1,0:T(8,128)(2,1)S(1)} %fusion), channel_id=1, source_target_pairs={{0,3},{1,0},{2,1},{3,2},{4,7},{5,4},{6,5},{7,6},{8,11},{9,8},{10,9... | collective-permute-start | bytes 393224 | tf_op jit(solution)/shard_map/ppermute | solution.py:27
  8.0 16.1 %collective-permute-start = (bf16[4,128,512]{2,1,0:T(8,128)(2,1)}, bf16[4,128,512]{2,1,0:T(8,128)(2,1)S(1)}, u32[]{:S(2)}, u32[]{:S(2)}) collective-permute-start(bf16[4,128,512]{2,1,0:T(8,128)(2,1)} %states.1), channel_id=1, source_target_pairs={{0,8},{4,12},{8,16},{12,20},{16,24},{20,28},{1,9},{5,13},{9,17},{1... | collective-permute-start | bytes 1572872 | tf_op jit(solution)/shard_map/ppermute | solution.py:22
  15.4 13.1 %collective-permute-start.11 = (bf16[256,256]{1,0:T(8,128)(2,1)}, bf16[256,256]{1,0:T(8,128)(2,1)}, u32[]{:S(2)}, u32[]{:S(2)}) collective-permute-start(bf16[256,256]{1,0:T(8,128)(2,1)} %pad_maximum_fusion.4), channel_id=1, source_target_pairs={{0,2},{1,3},{2,0},{3,1},{4,6},{5,7},{6,4},{7,5},{8,10},{9,11},{10,... | collective-permute-start | bytes 393224 | tf_op jit(solution)/shard_map/ppermute | solution.py:27
  17.7 17.4 %collective-permute-start.6 = (bf16[3,64,512]{2,1,0:T(8,128)(2,1)S(1)}, bf16[3,64,512]{2,1,0:T(8,128)(2,1)S(1)}, u32[]{:S(2)}, u32[]{:S(2)}) collective-permute-start(bf16[3,64,512]{2,1,0:T(8,128)(2,1)S(1)} %pad_maximum_fusion.1), channel_id=1, source_target_pairs={{0,8},{4,12},{8,0},{12,4},{16,24},{20,28},{24,16},{28,20},{1,9},{5... | collective-permute-start | bytes 589832 | tf_op jit(solution)/shard_map/ppermute | solution.py:32
  24.2 18.5 %collective-permute-start.1 = (bf16[4,128,512]{2,1,0:T(8,128)(2,1)S(1)}, bf16[4,128,512]{2,1,0:T(8,128)(2,1)S(1)}, u32[]{:S(2)}, u32[]{:S(2)}) collective-permute-start(bf16[4,128,512]{2,1,0:T(8,128)(2,1)S(1)} %broadcast_select_fusion), channel_id=1, source_target_pairs={{0,4},{4,0},{8,12},{12,8},{16,20},{20,16},{24,28},{28,24},{1,5},{5... | collective-permute-start | bytes 1572872 | tf_op jit(solution)/shard_map/ppermute | solution.py:32
  25.0 10.2 %collective-permute-start.7 = (bf16[3,64,512]{2,1,0:T(8,128)(2,1)}, bf16[3,64,512]{2,1,0:T(8,128)(2,1)S(1)}, u32[]{:S(2)}, u32[]{:S(2)}) collective-permute-start(bf16[3,64,512]{2,1,0:T(8,128)(2,1)} %pad_maximum_fusion.2), channel_id=1, source_target_pairs={{0,16},{4,20},{8,24},{12,28},{16,0},{20,4},{24,8},{28,12},{1,17},{... | collective-permute-start | bytes 589832 | tf_op jit(solution)/shard_map/ppermute | solution.py:32
  28.3 15.1 %collective-permute-start.5 = (bf16[3,128,512]{2,1,0:T(8,128)(2,1)S(1)}, bf16[3,128,512]{2,1,0:T(8,128)(2,1)S(1)}, u32[]{:S(2)}, u32[]{:S(2)}) collective-permute-start(bf16[3,128,512]{2,1,0:T(8,128)(2,1)S(1)} %maximum_maximum_fusion.refs_0_), channel_id=1, source_target_pairs={{0,4},{4,0},{8,12},{12,8},{16,20},{20,16},{24,28},{28,24},{1,5},{5... | collective-permute-start | bytes 1179656 | tf_op jit(solution)/shard_map/ppermute | solution.py:32
  34.5 7.1 %collective-permute-start.10 = (bf16[256,256]{1,0:T(8,128)(2,1)}, bf16[256,256]{1,0:T(8,128)(2,1)}, u32[]{:S(2)}, u32[]{:S(2)}) collective-permute-start(bf16[256,256]{1,0:T(8,128)(2,1)} %pad_maximum_fusion.4), channel_id=1, source_target_pairs={{0,1},{1,2},{2,3},{3,0},{4,5},{5,6},{6,7},{7,4},{8,9},{9,10},{10,1... | collective-permute-start | bytes 393224 | tf_op jit(solution)/shard_map/ppermute | solution.py:27
  35.2 8.2 %collective-permute-start.8 = (bf16[3,64,512]{2,1,0:T(8,128)(2,1)S(1)}, bf16[3,64,512]{2,1,0:T(8,128)(2,1)S(1)}, u32[]{:S(2)}, u32[]{:S(2)}) collective-permute-start(bf16[3,64,512]{2,1,0:T(8,128)(2,1)S(1)} %collective-permute-done.6.refs_2_), channel_id=1, source_target_pairs={{0,4},{4,0},{8,12},{12,8},{16,20},{20,16},{24,28},{28,24},{1,5},{5... | collective-permute-start | bytes 589832 | tf_op jit(solution)/shard_map/ppermute | solution.py:32
  35.2 8.2 %collective-permute-start.9 = (bf16[3,64,512]{2,1,0:T(8,128)(2,1)S(1)}, bf16[3,64,512]{2,1,0:T(8,128)(2,1)S(1)}, u32[]{:S(2)}, u32[]{:S(2)}) collective-permute-start(bf16[3,64,512]{2,1,0:T(8,128)(2,1)S(1)} %collective-permute-done.7.refs_3_), channel_id=1, source_target_pairs={{0,4},{4,0},{8,12},{12,8},{16,20},{20,16},{24,28},{28,24},{1,5},{5... | collective-permute-start | bytes 589832 | tf_op jit(solution)/shard_map/ppermute | solution.py:32
  48.6 14.9 %collective-permute-start.26 = (bf16[3,64,512]{2,1,0:T(8,128)(2,1)S(1)}, bf16[3,64,512]{2,1,0:T(8,128)(2,1)S(1)}, u32[]{:S(2)}, u32[]{:S(2)}) collective-permute-start(bf16[3,64,512]{2,1,0:T(8,128)(2,1)S(1)} %pad_maximum_fusion.3.refs_12_), channel_id=1, source_target_pairs={{0,16},{4,20},{8,24},{12,28},{16,0},{20,4},{24,8},{28,12},{1,17},{... | collective-permute-start | bytes 589832 | tf_op jit(solution)/shard_map/ppermute | solution.py:32
  49.8 8.3 %collective-permute-start.13 = (bf16[512,128]{1,0:T(8,128)(2,1)S(1)}, bf16[512,128]{1,0:T(8,128)(2,1)S(1)}, u32[]{:S(2)}, u32[]{:S(2)}) collective-permute-start(bf16[512,128]{1,0:T(8,128)(2,1)S(1)} %get-tuple-element.25), channel_id=1, source_target_pairs={{0,1},{1,2},{2,3},{3,0},{4,5},{5,6},{6,7},{7,4},{8,9},{9,10},{10,1... | collective-permute-start | bytes 393224 | tf_op jit(solution)/shard_map/ppermute | solution.py:27
  49.9 11.3 %collective-permute-start.14 = (bf16[512,128]{1,0:T(8,128)(2,1)S(1)}, bf16[512,128]{1,0:T(8,128)(2,1)S(1)}, u32[]{:S(2)}, u32[]{:S(2)}) collective-permute-start(bf16[512,128]{1,0:T(8,128)(2,1)S(1)} %get-tuple-element.26), channel_id=1, source_target_pairs={{0,2},{1,3},{2,0},{3,1},{4,6},{5,7},{6,4},{7,5},{8,10},{9,11},{10,... | collective-permute-start | bytes 393224 | tf_op jit(solution)/shard_map/ppermute | solution.py:27
  51.2 10.7 %collective-permute-start.15 = (bf16[512,128]{1,0:T(8,128)(2,1)S(1)}, bf16[512,128]{1,0:T(8,128)(2,1)S(1)}, u32[]{:S(2)}, u32[]{:S(2)}) collective-permute-start(bf16[512,128]{1,0:T(8,128)(2,1)S(1)} %get-tuple-element.27), channel_id=1, source_target_pairs={{0,3},{1,0},{2,1},{3,2},{4,7},{5,4},{6,5},{7,6},{8,11},{9,8},{10,9... | collective-permute-start | bytes 393224 | tf_op jit(solution)/shard_map/ppermute | solution.py:27
  53.7 10.9 %collective-permute-start.27 = (bf16[3,64,512]{2,1,0:T(8,128)(2,1)S(1)}, bf16[3,64,512]{2,1,0:T(8,128)(2,1)S(1)}, u32[]{:S(2)}, u32[]{:S(2)}) collective-permute-start(bf16[3,64,512]{2,1,0:T(8,128)(2,1)S(1)} %pad_maximum_fusion.3.refs_12_), channel_id=1, source_target_pairs={{0,8},{4,12},{8,0},{12,4},{16,24},{20,28},{24,16},{28,20},{1,9},{5... | collective-permute-start | bytes 589832 | tf_op jit(solution)/shard_map/ppermute | solution.py:32
  58.1 8.4 %collective-permute-start.29 = (bf16[3,64,512]{2,1,0:T(8,128)(2,1)S(1)}, bf16[3,64,512]{2,1,0:T(8,128)(2,1)S(1)}, u32[]{:S(2)}, u32[]{:S(2)}) collective-permute-start(bf16[3,64,512]{2,1,0:T(8,128)(2,1)S(1)} %pad_maximum_fusion.3.refs_12_), channel_id=1, source_target_pairs={{0,4},{4,0},{8,12},{12,8},{16,20},{20,16},{24,28},{28,24},{1,5},{5... | collective-permute-start | bytes 589832 | tf_op jit(solution)/shard_map/ppermute | solution.py:32
  64.6 8.0 %collective-permute-start.16 = (bf16[512,128]{1,0:T(8,128)(2,1)S(1)}, bf16[512,128]{1,0:T(8,128)(2,1)S(1)}, u32[]{:S(2)}, u32[]{:S(2)}) collective-permute-start(bf16[512,128]{1,0:T(8,128)(2,1)S(1)} %get-tuple-element.29), channel_id=1, source_target_pairs={{0,1},{1,2},{2,3},{3,0},{4,5},{5,6},{6,7},{7,4},{8,9},{9,10},{10,1... | collective-permute-start | bytes 393224 | tf_op jit(solution)/shard_map/ppermute | solution.py:27
  66.5 12.9 %collective-permute-start.28 = (bf16[3,64,512]{2,1,0:T(8,128)(2,1)S(1)}, bf16[3,64,512]{2,1,0:T(8,128)(2,1)S(1)}, u32[]{:S(2)}, u32[]{:S(2)}) collective-permute-start(bf16[3,64,512]{2,1,0:T(8,128)(2,1)S(1)} %collective-permute-done.26.refs_13_), channel_id=1, source_target_pairs={{0,8},{4,12},{8,0},{12,4},{16,24},{20,28},{24,16},{28,20},{1,9},{5... | collective-permute-start | bytes 589832 | tf_op jit(solution)/shard_map/ppermute | solution.py:32
  67.1 12.8 %collective-permute-start.30 = (bf16[3,64,512]{2,1,0:T(8,128)(2,1)S(1)}, bf16[3,64,512]{2,1,0:T(8,128)(2,1)S(1)}, u32[]{:S(2)}, u32[]{:S(2)}) collective-permute-start(bf16[3,64,512]{2,1,0:T(8,128)(2,1)S(1)} %collective-permute-done.26.refs_13_), channel_id=1, source_target_pairs={{0,4},{4,0},{8,12},{12,8},{16,20},{20,16},{24,28},{28,24},{1,5},{5... | collective-permute-start | bytes 589832 | tf_op jit(solution)/shard_map/ppermute | solution.py:32
  67.6 12.3 %collective-permute-start.21 = (bf16[3,128,256]{2,1,0:T(8,128)(2,1)S(1)}, bf16[3,128,256]{2,1,0:T(8,128)(2,1)S(1)}, u32[]{:S(2)}, u32[]{:S(2)}) collective-permute-start(bf16[3,128,256]{2,1,0:T(8,128)(2,1)S(1)} %collective-permute-done.19.refs_5_), channel_id=1, source_target_pairs={{0,16},{4,20},{8,24},{12,28},{16,0},{20,4},{24,8},{28,12},{1,17},{... | collective-permute-start | bytes 589832 | tf_op jit(solution)/shard_map/ppermute | solution.py:32
  69.2 8.9 %collective-permute-start.17 = (bf16[512,128]{1,0:T(8,128)(2,1)S(1)}, bf16[512,128]{1,0:T(8,128)(2,1)S(1)}, u32[]{:S(2)}, u32[]{:S(2)}) collective-permute-start(bf16[512,128]{1,0:T(8,128)(2,1)S(1)} %get-tuple-element.30), channel_id=1, source_target_pairs={{0,2},{1,3},{2,0},{3,1},{4,6},{5,7},{6,4},{7,5},{8,10},{9,11},{10,... | collective-permute-start | bytes 393224 | tf_op jit(solution)/shard_map/ppermute | solution.py:27
  72.6 6.8 %collective-permute-start.18 = (bf16[512,128]{1,0:T(8,128)(2,1)S(1)}, bf16[512,128]{1,0:T(8,128)(2,1)S(1)}, u32[]{:S(2)}, u32[]{:S(2)}) collective-permute-start(bf16[512,128]{1,0:T(8,128)(2,1)S(1)} %get-tuple-element.31), channel_id=1, source_target_pairs={{0,3},{1,0},{2,1},{3,2},{4,7},{5,4},{6,5},{7,6},{8,11},{9,8},{10,9... | collective-permute-start | bytes 393224 | tf_op jit(solution)/shard_map/ppermute | solution.py:27
  (21 other events, 236.6 us)

commit v5 on v4

--- a/solution.py
+++ b/solution.py
@@ -9,8 +9,6 @@
 
 HEADS = 4
 SPREAD = 8
-FIRST_BITS = (0, 2, 4, 6, 1, 3, 5, 7)
-SECOND_BITS = (0, 4, 2, 6, 1, 5, 3, 7)
 LANES = 128
 F32 = jnp.float32
 BF16 = jnp.bfloat16
@@ -38,8 +36,7 @@
 
 
 def quarter_of(block):
-    parity = lax.rem(lax.div(block, 2) + lax.div(block, 4), 2)
-    return lax.rem(block, 2) + 2 * parity
+    return lax.rem(block, 2) + 2 * lax.rem(lax.div(block, 4), 2)
 
 
 def row_sum(value):
@@ -56,6 +53,21 @@
             normed[row : row + zone_rows, :] = rms_scale(block[step].astype(F32), gain).astype(BF16)
 
 
+def pack_kernel(place, own_in, own_out, *refs):
+    arrived, (stacked, packed) = refs[:-2], refs[-2:]
+    in_shard, hidden = own_in.shape
+    out_shard, width = own_out.shape
+    in_cols, out_rows = hidden // SPREAD, out_shard // SPREAD
+    slot = lax.rem(place[0], SPREAD)
+    for index, piece in enumerate(arrived):
+        stacked[index] = piece[...]
+    packed[:in_shard, :] = own_in[:, pl.ds(pl.multiple_of(slot * in_cols, in_cols), in_cols)]
+    rows = pl.ds(pl.multiple_of(slot * out_rows, out_rows), out_rows)
+    for fold in range(width // in_cols):
+        first = in_shard + fold * out_rows
+        packed[first : first + out_rows, :] = own_out[rows, fold * in_cols : (fold + 1) * in_cols]
+
+
 def attention_kernel(zones, reach, steps, place, pattern, normed, own_qkv, own_attn, *refs):
     pieces, (context_out, attn_out, weights, w_turned, projected, context) = refs[:-6], refs[-6:]
     key_count = (reach + 1) * steps
@@ -70,11 +82,10 @@
         weights[index, own_rows, :] = own_qkv[:, index * width : (index + 1) * width]
     weights[3, own_rows, :] = own_attn[...]
     my_quarter = quarter_of(my_block)
-    half = shard // 2
     for step in range(1, zones):
         source = lax.rem(my_zone - step + zones, zones)
-        for piece, bits, part in zip(pieces, (0, 1, 2, 2, 3, 3), (0, 0, 0, 1, 0, 1)):
-            rows = pl.ds(pl.multiple_of(source * shard + part * half, half), piece.shape[1])
+        rows = pl.ds(pl.multiple_of(source * shard, shard), shard)
+        for bits, piece in enumerate(pieces):
             weights[my_quarter ^ bits, rows, :] = piece[step - 1]
     attn_out[...] = weights[3]
     for index in range(3):
@@ -160,9 +171,12 @@
 
 
 def project_kernel(place, states, context, w_attn, gain_mix, *refs):
-    (after_out, *outs), parts = refs[:-1], refs[-1]
+    parts = refs[-1]
     steps, zone_rows, _ = states.shape
     zones, _, part = parts.shape
+    across, (after_out, *outs, across_out) = refs[: zones - 1], refs[zones - 1 : -1]
+    for index, piece in enumerate(across):
+        across_out[index] = piece[...]
     my_zone = place[1]
     gain = gain_mix[...]
     for step in range(steps):
@@ -228,17 +242,17 @@
     for index in range(SPREAD):
         w_in[index, pl.ds(start, in_shard), :] = own_in[:, index * in_cols : (index + 1) * in_cols]
     w_out[pl.ds(pl.multiple_of(my_zone * out_shard, out_shard), out_shard), :] = own_out[...]
-    for index, bits in enumerate(FIRST_BITS + SECOND_BITS):
+    for bits, piece in enumerate(pieces):
         slot = lax.rem(my_block, SPREAD) ^ bits
-        piece = pieces[index]
         for step in range(1, zones):
             source = lax.rem(my_zone - step + zones, zones)
-            if index < SPREAD:
-                rows = pl.ds(pl.multiple_of(source * in_shard, in_shard), in_shard)
-                w_in[slot, rows, :] = piece[step - 1]
-            else:
-                rows = pl.ds(pl.multiple_of(source * out_shard + slot * out_rows, out_rows), out_rows)
-                w_out[rows, :] = piece[step - 1]
+            rows = pl.ds(pl.multiple_of(source * in_shard, in_shard), in_shard)
+            w_in[slot, rows, :] = piece[step - 1, :in_shard, :]
+            rows = pl.ds(pl.multiple_of(source * out_shard + slot * out_rows, out_rows), out_rows)
+            for fold in range(width // in_cols):
+                first = in_shard + fold * out_rows
+                cols = slice(fold * in_cols, (fold + 1) * in_cols)
+                w_out[rows, cols] = piece[step - 1, first : first + out_rows, :]
 
     gain = gain_ffn[...]
     span = 128
@@ -313,17 +327,23 @@
         jnp.concatenate([w_qkv, w_out_attn], axis=1), quarter_of(my_block) * width, width, axis=1
     )
     direct = [rotated(first, "zone", step) for step in rotations]
-    slot = my_block % SPREAD
-    slice_in = lax.dynamic_slice_in_dim(w_in, slot * in_cols, in_cols, axis=1)
-    slice_out = lax.dynamic_slice_in_dim(w_out, slot * out_rows, out_rows, axis=0)
-
-    half = first.shape[0] // 2
-    upper = jnp.stack([piece[:half] for piece in direct])
-    lower = jnp.stack([piece[half:] for piece in direct])
-    direct = jnp.concatenate([upper, lower], axis=1)
-    over_x, over_y = swapped(upper, "tm", 2), swapped(lower, "tm", 4)
-    quarters = [direct, swapped(direct, "tm", 1), over_x, over_y]
-    quarters += [swapped(over_x, "tm", 1), swapped(over_y, "tm", 1)]
+    in_shard = w_in.shape[0]
+    packed_shape = (in_shard + out_rows * (width // in_cols), in_cols)
+    direct, packed = call(
+        pack_kernel,
+        (
+            jax.ShapeDtypeStruct((zones - 1,) + first.shape, BF16),
+            jax.ShapeDtypeStruct(packed_shape, BF16),
+        ),
+        [],
+        0,
+        (0,),
+        8,
+        [place, w_in, w_out] + direct,
+    )
+    over = swapped(direct, "tm", 4)
+    quarters = [direct, swapped(direct, "tm", 1), over, swapped(over, "tm", 1)]
+    across = [rotated(packed, "zone", step) for step in rotations]
 
     last = swapped(jnp.where(my_block % 2 == 1, before, states), "tm", 1)
     normed = call(
@@ -335,12 +355,6 @@
         8,
         [before, last, states, gain_attn.reshape(1, -1)],
     )
-
-    packed = jnp.concatenate(
-        [slice_in] + [slice_out[:, at : at + in_cols] for at in range(0, width, in_cols)], axis=0
-    )
-    packed, _ = lax.optimization_barrier((packed, direct))
-    across = jnp.stack([rotated(packed, "zone", step) for step in rotations])
 
     context, w_attn = call(
         functools.partial(attention_kernel, zones, reach, steps),
@@ -359,35 +373,25 @@
         22,
         [place, pattern, normed, w_qkv, w_out_attn] + quarters,
     )
-    context, across = lax.optimization_barrier((context, across))
 
     chunk = jax.ShapeDtypeStruct((rows, part), BF16)
-    after_attn, *chunks = call(
+    after_attn, *chunks, across = call(
         project_kernel,
-        (jax.ShapeDtypeStruct((rows, width), F32),) + (chunk,) * zones,
+        (jax.ShapeDtypeStruct((rows, width), F32),)
+        + (chunk,) * zones
+        + (jax.ShapeDtypeStruct((zones - 1,) + packed_shape, BF16),),
         [pltpu.VMEM((zones, rows, part), BF16)],
         2 * rows * width * width,
         (0,),
         8,
-        [place, states, context, w_attn, gain_mix.reshape(1, -1)],
+        [place, states, context, w_attn, gain_mix.reshape(1, -1)] + across,
     )
     arrived = [chunks[0]] + [rotated(chunks[step], "zone", step) for step in rotations]
 
-    in_shard = w_in.shape[0]
-    from_in = across[:, :in_shard]
-    from_out = jnp.concatenate(
-        [
-            across[:, in_shard + fold * out_rows : in_shard + (fold + 1) * out_rows]
-            for fold in range(width // in_cols)
-        ],
-        axis=2,
-    )
-    ins, outs = [from_in], [from_out]
-    for bits_in, bits_out in ((2, 4), (4, 2)):
-        ins += [swapped(value, "tm", bits_in) for value in ins]
-        outs += [swapped(value, "tm", bits_out) for value in outs]
-    pieces = ins + [swapped(value, "tm", 1) for value in ins]
-    pieces += outs + [swapped(value, "tm", 1) for value in outs]
+    pieces = {bits: swapped(across, "tm", bits) for bits in range(2, SPREAD, 2)}
+    pieces[0] = across
+    for bits in range(0, SPREAD, 2):
+        pieces[bits + 1] = swapped(pieces[bits], "tm", 1)
 
     spatial = call(
         functools.partial(mixing_kernel, steps, zones),
@@ -412,7 +416,9 @@
         4 * rows * width * hidden,
         (0,),
         16,
-        [place, after_attn, gain_ffn.reshape(1, -1), w_in, w_out] + arrived + pieces,
+        [place, after_attn, gain_ffn.reshape(1, -1), w_in, w_out]
+        + arrived
+        + [pieces[bits] for bits in range(SPREAD)],
     )
     return evolved.reshape(steps, zone_rows, width)
 

time: 86.3 us -> 92.4 us (1.071)
  waiting for transfers between devices: 34.7 us -> 48.7 us
  starting transfers between devices: 33.4 us -> 27.1 us
  other arithmetic: 3.65 us -> 1.1 us
    ppermute x12, waiting for transfers between devices: 28 us -> 41 us  [rotated(): lax.ppermute(value, axis, [(source, (source + steps) % count) for source...]
    ppermute x20 -> x11, waiting for transfers between devices: 1.86 us -> 7.66 us  [swapped(): lax.ppermute(value, axis, [(source, source ^ bits) for source in range(co...]
    ppermute x20 -> x11, starting transfers between devices: 12.2 us -> 6.65 us  [swapped(): lax.ppermute(value, axis, [(source, source ^ bits) for source in range(co...]
    ppermute x1, waiting for transfers between devices: 4.81 us -> 0.01 us  [shifted(): lax.ppermute(value, axis, [(source, source + steps) for source in range(c...]
    ppermute x12, starting transfers between devices: 17.7 us -> 15.4 us  [rotated(): lax.ppermute(value, axis, [(source, (source + steps) % count) for source...]
    unnamed x24 -> x28, local copies, waits for them, and re-layouts: 0.38 us -> 2.49 us
    another operation x3 -> x0, other arithmetic: 1.8 us -> none  [the longest x1 1.07 us: on_device(): across = jnp.stack([rotated(packed, 'zone', step) for step in rotations])]
    ppermute x1, starting transfers between devices: 3.42 us -> 4.99 us  [shifted(): lax.ppermute(value, axis, [(source, source + steps) for source in range(c...]
  transfers between devices with their start and end apart: 33 -> 24, of which waited for: 14 -> 12; matrix products, arithmetic and copies ran while one was open for 5% -> 1% of each run, Pallas kernels for 3% -> 8%
where the time goes in v5:
time: 92.4 us; the launch traced here: 92.1 us
  waiting for transfers between devices  48.7 us (53%)
  starting transfers between devices  27.1 us (29%)
  Pallas kernels  12.5 us (14%)
  local copies, waits for them, and re-layouts  2.49 us (3%)
  other arithmetic  1.1 us (1%)
    ppermute x12, waiting for transfers between devices, rotated(): lax.ppermute(value, axis, [(source, (source + steps) % count) for source...  41 us
    ppermute x12, starting transfers between devices, rotated(): lax.ppermute(value, axis, [(source, (source + steps) % count) for source...  15.4 us
    pallas_call x6, Pallas kernels, call(): pl.pallas_call(kernel, out_shape=out_shape, in_specs=in_specs, out_specs=...  12.5 us
    ppermute x11, waiting for transfers between devices, swapped(): lax.ppermute(value, axis, [(source, source ^ bits) for source in range(co...  7.66 us
    ppermute x11, starting transfers between devices, swapped(): lax.ppermute(value, axis, [(source, source ^ bits) for source in range(co...  6.65 us
    ppermute x1, starting transfers between devices, shifted(): lax.ppermute(value, axis, [(source, source + steps) for source in range(c...  4.99 us
    unnamed x28, local copies, waits for them, and re-layouts  2.49 us
  transfers between devices with their start and end apart: 24, of which 12 were waited for; matrix products, arithmetic and copies ran while one was open for 1% of the time, Pallas kernels for 8%

profile of v5, /device:TPU:0, one launch (start us, length us, event | category | flops | bytes accessed | tf_op | source)
XLA Modules:
  0.0 92.1 jit_solution(9512416795982660769)
XLA Ops:
  0.0 5.0 %collective-permute-start = (bf16[4,128,512]{2,1,0:T(8,128)(2,1)}, bf16[4,128,512]{2,1,0:T(8,128)(2,1)S(1)}, u32[]{:S(2)}, u32[]{:S(2)}) collective-permute-start(bf16[4,128,512]{2,1,0:T(8,128)(2,1)} %states.1), channel_id=1, source_target_pairs={{0,8},{4,12},{8,16},{12,20},{16,24},{20,28},{1,9},{5,13},{9,17},{1... | collective-permute-start | bytes 1572872 | tf_op jit(solution)/shard_map/ppermute | solution.py:20
  6.0 2.7 %collective-permute-start.3 = (bf16[128,512]{1,0:T(8,128)(2,1)S(1)}, bf16[128,512]{1,0:T(8,128)(2,1)S(1)}, u32[]{:S(2)}, u32[]{:S(2)}) collective-permute-start(bf16[128,512]{1,0:T(8,128)(2,1)S(1)} %fusion), channel_id=1, source_target_pairs={{0,2},{1,3},{2,0},{3,1},{4,6},{5,7},{6,4},{7,5},{8,10},{9,11},{10,... | collective-permute-start | bytes 393224 | tf_op jit(solution)/shard_map/ppermute | solution.py:25
  8.7 1.6 %collective-permute-start.2 = (bf16[128,512]{1,0:T(8,128)(2,1)S(1)}, bf16[128,512]{1,0:T(8,128)(2,1)S(1)}, u32[]{:S(2)}, u32[]{:S(2)}) collective-permute-start(bf16[128,512]{1,0:T(8,128)(2,1)S(1)} %fusion), channel_id=1, source_target_pairs={{0,1},{1,2},{2,3},{3,0},{4,5},{5,6},{6,7},{7,4},{8,9},{9,10},{10,1... | collective-permute-start | bytes 393224 | tf_op jit(solution)/shard_map/ppermute | solution.py:25
  10.2 2.2 %collective-permute-start.4 = (bf16[128,512]{1,0:T(8,128)(2,1)S(1)}, bf16[128,512]{1,0:T(8,128)(2,1)S(1)}, u32[]{:S(2)}, u32[]{:S(2)}) collective-permute-start(bf16[128,512]{1,0:T(8,128)(2,1)S(1)} %fusion), channel_id=1, source_target_pairs={{0,3},{1,0},{2,1},{3,2},{4,7},{5,4},{6,5},{7,6},{8,11},{9,8},{10,9... | collective-permute-start | bytes 393224 | tf_op jit(solution)/shard_map/ppermute | solution.py:25
  12.6 6.2 %collective-permute-done.3.refs_1_ = bf16[128,512]{1,0:T(8,128)(2,1)S(1)} collective-permute-done((bf16[128,512]{1,0:T(8,128)(2,1)S(1)}, bf16[128,512]{1,0:T(8,128)(2,1)S(1)}, u32[]{:S(2)}, u32[]{:S(2)}) %collective-permute-start.3) | collective-permute-done | bytes 131104 | tf_op jit(solution)/shard_map/ppermute | solution.py:25
  21.8 1.6 %collective-permute-start.6 = (bf16[3,128,512]{2,1,0:T(8,128)(2,1)S(1)}, bf16[3,128,512]{2,1,0:T(8,128)(2,1)S(1)}, u32[]{:S(2)}, u32[]{:S(2)}) collective-permute-start(bf16[3,128,512]{2,1,0:T(8,128)(2,1)S(1)} %get-tuple-element.19.refs_0_), channel_id=1, source_target_pairs={{0,16},{4,20},{8,24},{12,28},{16,0},{20,4},{24,8},{28,12},{1,17},{... | collective-permute-start | bytes 1179656 | tf_op jit(solution)/shard_map/ppermute | solution.py:30
  24.0 6.8 %collective-permute-done.6.refs_2_ = bf16[3,128,512]{2,1,0:T(8,128)(2,1)S(1)} collective-permute-done((bf16[3,128,512]{2,1,0:T(8,128)(2,1)S(1)}, bf16[3,128,512]{2,1,0:T(8,128)(2,1)S(1)}, u32[]{:S(2)}, u32[]{:S(2)}) %collective-permute-start.6) | collective-permute-done | bytes 393248 | tf_op jit(solution)/shard_map/ppermute | solution.py:30
  30.9 2.5 %collective-permute-start.10 = (bf16[256,256]{1,0:T(8,128)(2,1)S(1)}, bf16[256,256]{1,0:T(8,128)(2,1)S(1)}, u32[]{:S(2)}, u32[]{:S(2)}) collective-permute-start(bf16[256,256]{1,0:T(8,128)(2,1)S(1)} %get-tuple-element.22), channel_id=1, source_target_pairs={{0,3},{1,0},{2,1},{3,2},{4,7},{5,4},{6,5},{7,6},{8,11},{9,8},{10,9... | collective-permute-start | bytes 393224 | tf_op jit(solution)/shard_map/ppermute | solution.py:25
  33.4 3.4 %collective-permute-start.9 = (bf16[256,256]{1,0:T(8,128)(2,1)S(1)}, bf16[256,256]{1,0:T(8,128)(2,1)S(1)}, u32[]{:S(2)}, u32[]{:S(2)}) collective-permute-start(bf16[256,256]{1,0:T(8,128)(2,1)S(1)} %get-tuple-element.22), channel_id=1, source_target_pairs={{0,2},{1,3},{2,0},{3,1},{4,6},{5,7},{6,4},{7,5},{8,10},{9,11},{10,... | collective-permute-start | bytes 393224 | tf_op jit(solution)/shard_map/ppermute | solution.py:25
  36.7 2.0 %collective-permute-start.8 = (bf16[256,256]{1,0:T(8,128)(2,1)S(1)}, bf16[256,256]{1,0:T(8,128)(2,1)S(1)}, u32[]{:S(2)}, u32[]{:S(2)}) collective-permute-start(bf16[256,256]{1,0:T(8,128)(2,1)S(1)} %get-tuple-element.22), channel_id=1, source_target_pairs={{0,1},{1,2},{2,3},{3,0},{4,5},{5,6},{6,7},{7,4},{8,9},{9,10},{10,1... | collective-permute-start | bytes 393224 | tf_op jit(solution)/shard_map/ppermute | solution.py:25
  39.8 4.7 %shard_map.120 = (bf16[512,512]{1,0:T(8,128)(2,1)S(1)}, bf16[512,512]{1,0:T(8,128)(2,1)S(1)}) custom-call(s32[2]{0:T(128)S(1)} %pad_add_fusion.place, s32[1,2]{1,0:T(1,128)S(1)} %copy-done.13, bf16[1536,512]{1,0:T(8,128)(2,1)S(1)} %shard_map.118.normed, bf16[128,1536]{1,0:T(8,128)(2,1)S(1)} %copy-done.5, bf16[128,512]{1,0:T(8,128)(2,1)S(1)} %copy-done.7, ...), custom_call_target="tpu_custom_call" | custom-call | flops 5368709120 | bytes 3670032 | tf_op jit(solution)/shard_map/pallas_call | solution.py:287
  44.6 4.7 %collective-permute-done.9.refs_1_ = bf16[256,256]{1,0:T(8,128)(2,1)S(1)} collective-permute-done((bf16[256,256]{1,0:T(8,128)(2,1)S(1)}, bf16[256,256]{1,0:T(8,128)(2,1)S(1)}, u32[]{:S(2)}, u32[]{:S(2)}) %collective-permute-start.9) | collective-permute-done | bytes 131104 | tf_op jit(solution)/shard_map/ppermute | solution.py:25
  49.3 1.2 %shard_map.121 = (f32[512,512]{1,0:T(8,128)S(1)}, bf16[512,128]{1,0:T(8,128)(2,1)S(1)}, bf16[512,128]{1,0:T(8,128)(2,1)S(1)}, bf16[512,128]{1,0:T(8,128)(2,1)S(1...) custom-call(s32[2]{0:T(128)S(1)} %pad_add_fusion.place, bf16[4,128,512]{2,1,0:T(8,128)(2,1)S(1)} %copy-done, ...), custom_call_target="tpu_custom_call" | custom-call | flops 268435456 | bytes 1968136 | tf_op jit(solution)/shard_map/pallas_call | solution.py:287
  50.5 1.2 %collective-permute-start.22 = (bf16[3,256,256]{2,1,0:T(8,128)(2,1)S(1)}, bf16[3,256,256]{2,1,0:T(8,128)(2,1)S(1)}, u32[]{:S(2)}, u32[]{:S(2)}) collective-permute-start(bf16[3,256,256]{2,1,0:T(8,128)(2,1)S(1)} %get-tuple-element.32.refs_4_), channel_id=1, source_target_pairs={{0,24},{4,28},{8,16},{12,20},{16,8},{20,12},{24,0},{28,4},{1,25},{... | collective-permute-start | bytes 1179656 | tf_op jit(solution)/shard_map/ppermute | solution.py:30
  51.7 1.7 %collective-permute-start.20 = (bf16[3,256,256]{2,1,0:T(8,128)(2,1)S(1)}, bf16[3,256,256]{2,1,0:T(8,128)(2,1)S(1)}, u32[]{:S(2)}, u32[]{:S(2)}) collective-permute-start(bf16[3,256,256]{2,1,0:T(8,128)(2,1)S(1)} %get-tuple-element.32.refs_4_), channel_id=1, source_target_pairs={{0,16},{4,20},{8,24},{12,28},{16,0},{20,4},{24,8},{28,12},{1,17},{... | collective-permute-start | bytes 1179656 | tf_op jit(solution)/shard_map/ppermute | solution.py:30
  54.1 8.3 %collective-permute-done.11.refs_1_ = bf16[512,128]{1,0:T(8,128)(2,1)S(1)} collective-permute-done((bf16[512,128]{1,0:T(8,128)(2,1)S(1)}, bf16[512,128]{1,0:T(8,128)(2,1)S(1)}, u32[]{:S(2)}, u32[]{:S(2)}) %collective-permute-start.11) | collective-permute-done | bytes 131104 | tf_op jit(solution)/shard_map/ppermute | solution.py:25
  62.4 3.7 %collective-permute-done.12.refs_2_ = bf16[512,128]{1,0:T(8,128)(2,1)S(1)} collective-permute-done((bf16[512,128]{1,0:T(8,128)(2,1)S(1)}, bf16[512,128]{1,0:T(8,128)(2,1)S(1)}, u32[]{:S(2)}, u32[]{:S(2)}) %collective-permute-start.12) | collective-permute-done | bytes 131104 | tf_op jit(solution)/shard_map/ppermute | solution.py:25
  66.1 1.3 %collective-permute-done.13.refs_3_ = bf16[512,128]{1,0:T(8,128)(2,1)S(1)} collective-permute-done((bf16[512,128]{1,0:T(8,128)(2,1)S(1)}, bf16[512,128]{1,0:T(8,128)(2,1)S(1)}, u32[]{:S(2)}, u32[]{:S(2)}) %collective-permute-start.13) | collective-permute-done | bytes 131104 | tf_op jit(solution)/shard_map/ppermute | solution.py:25
  67.4 1.1 %shard_map.122 = (bf16[512,128]{1,0:T(8,128)(2,1)S(1)}, bf16[512,128]{1,0:T(8,128)(2,1)S(1)}, bf16[512,128]{1,0:T(8,128)(2,1)S(1)}, bf16[512,128]{1,0:T(8,128)(2,1)S(1)}) custom-call(s32[2]{0:T(128)S(1)} %pad_add_fusion.place, s32[4,3]{1,0:T(4,128)S(1)} %copy-done.9, s32[4]{0:T(128)S(1)} %copy-done.11, bf16[4,3,128,128]{3,2,1,0:T(8,128)(2,1)S(1)} %copy-done.6, ...), custom_call_target="tpu_custom_call" | custom-call | flops 201326592 | bytes 917576 | tf_op jit(solution)/shard_map/pallas_call | solution.py:287
  68.5 1.1 %collective-permute-start.14 = (bf16[512,128]{1,0:T(8,128)(2,1)S(1)}, bf16[512,128]{1,0:T(8,128)(2,1)S(1)}, u32[]{:S(2)}, u32[]{:S(2)}) collective-permute-start(bf16[512,128]{1,0:T(8,128)(2,1)S(1)} %get-tuple-element.29), channel_id=1, source_target_pairs={{0,1},{1,2},{2,3},{3,0},{4,5},{5,6},{6,7},{7,4},{8,9},{9,10},{10,1... | collective-permute-start | bytes 393224 | tf_op jit(solution)/shard_map/ppermute | solution.py:25
  71.4 4.0 %collective-permute-done.14.refs_1_ = bf16[512,128]{1,0:T(8,128)(2,1)S(1)} collective-permute-done((bf16[512,128]{1,0:T(8,128)(2,1)S(1)}, bf16[512,128]{1,0:T(8,128)(2,1)S(1)}, u32[]{:S(2)}, u32[]{:S(2)}) %collective-permute-start.14) | collective-permute-done | bytes 131104 | tf_op jit(solution)/shard_map/ppermute | solution.py:25
  75.4 7.4 %collective-permute-done.15.refs_2_ = bf16[512,128]{1,0:T(8,128)(2,1)S(1)} collective-permute-done((bf16[512,128]{1,0:T(8,128)(2,1)S(1)}, bf16[512,128]{1,0:T(8,128)(2,1)S(1)}, u32[]{:S(2)}, u32[]{:S(2)}) %collective-permute-start.15) | collective-permute-done | bytes 131104 | tf_op jit(solution)/shard_map/ppermute | solution.py:25
  82.8 5.0 %collective-permute-done.16.refs_3_ = bf16[512,128]{1,0:T(8,128)(2,1)S(1)} collective-permute-done((bf16[512,128]{1,0:T(8,128)(2,1)S(1)}, bf16[512,128]{1,0:T(8,128)(2,1)S(1)}, u32[]{:S(2)}, u32[]{:S(2)}) %collective-permute-start.16) | collective-permute-done | bytes 131104 | tf_op jit(solution)/shard_map/ppermute | solution.py:25
  87.8 4.3 %shard_map.123 = bf16[512,512]{1,0:T(8,128)(2,1)} custom-call(s32[2]{0:T(128)S(1)} %pad_add_fusion.place, f32[512,512]{1,0:T(8,128)S(1)} %get-tuple-element.23.after_attn, f32[1,512]{1,0:T(1,128)S(1)} %bitcast.8, bf16[128,2048]{1,0:T(8,128)(2,1)S(1)} %copy-done.2, bf16[512,512]{1,0:T(8,128)(2,1)S(1)} %copy-done.4, ...), custom_call_target="tpu_custom_call" | custom-call | flops 2147483648 | bytes 5769224 | tf_op jit(solution)/shard_map/pallas_call | solution.py:287
  (61 shorter events, 8.2 us)
Async XLA Ops:
  0.0 23.4 %collective-permute-start = (bf16[4,128,512]{2,1,0:T(8,128)(2,1)}, bf16[4,128,512]{2,1,0:T(8,128)(2,1)S(1)}, u32[]{:S(2)}, u32[]{:S(2)}) collective-permute-start(bf16[4,128,512]{2,1,0:T(8,128)(2,1)} %states.1), channel_id=1, source_target_pairs={{0,8},{4,12},{8,16},{12,20},{16,24},{20,28},{1,9},{5,13},{9,17},{1... | collective-permute-start | bytes 1572872 | tf_op jit(solution)/shard_map/ppermute | solution.py:20
  6.0 12.7 %collective-permute-start.3 = (bf16[128,512]{1,0:T(8,128)(2,1)S(1)}, bf16[128,512]{1,0:T(8,128)(2,1)S(1)}, u32[]{:S(2)}, u32[]{:S(2)}) collective-permute-start(bf16[128,512]{1,0:T(8,128)(2,1)S(1)} %fusion), channel_id=1, source_target_pairs={{0,2},{1,3},{2,0},{3,1},{4,6},{5,7},{6,4},{7,5},{8,10},{9,11},{10,... | collective-permute-start | bytes 393224 | tf_op jit(solution)/shard_map/ppermute | solution.py:25
  8.7 10.1 %collective-permute-start.2 = (bf16[128,512]{1,0:T(8,128)(2,1)S(1)}, bf16[128,512]{1,0:T(8,128)(2,1)S(1)}, u32[]{:S(2)}, u32[]{:S(2)}) collective-permute-start(bf16[128,512]{1,0:T(8,128)(2,1)S(1)} %fusion), channel_id=1, source_target_pairs={{0,1},{1,2},{2,3},{3,0},{4,5},{5,6},{6,7},{7,4},{8,9},{9,10},{10,1... | collective-permute-start | bytes 393224 | tf_op jit(solution)/shard_map/ppermute | solution.py:25
  10.2 8.9 %collective-permute-start.4 = (bf16[128,512]{1,0:T(8,128)(2,1)S(1)}, bf16[128,512]{1,0:T(8,128)(2,1)S(1)}, u32[]{:S(2)}, u32[]{:S(2)}) collective-permute-start(bf16[128,512]{1,0:T(8,128)(2,1)S(1)} %fusion), channel_id=1, source_target_pairs={{0,3},{1,0},{2,1},{3,2},{4,7},{5,4},{6,5},{7,6},{8,11},{9,8},{10,9... | collective-permute-start | bytes 393224 | tf_op jit(solution)/shard_map/ppermute | solution.py:25
  21.8 9.0 %collective-permute-start.6 = (bf16[3,128,512]{2,1,0:T(8,128)(2,1)S(1)}, bf16[3,128,512]{2,1,0:T(8,128)(2,1)S(1)}, u32[]{:S(2)}, u32[]{:S(2)}) collective-permute-start(bf16[3,128,512]{2,1,0:T(8,128)(2,1)S(1)} %get-tuple-element.19.refs_0_), channel_id=1, source_target_pairs={{0,16},{4,20},{8,24},{12,28},{16,0},{20,4},{24,8},{28,12},{1,17},{... | collective-permute-start | bytes 1179656 | tf_op jit(solution)/shard_map/ppermute | solution.py:30
  23.4 13.3 %collective-permute-start.1 = (bf16[4,128,512]{2,1,0:T(8,128)(2,1)S(1)}, bf16[4,128,512]{2,1,0:T(8,128)(2,1)S(1)}, u32[]{:S(2)}, u32[]{:S(2)}) collective-permute-start(bf16[4,128,512]{2,1,0:T(8,128)(2,1)S(1)} %broadcast_select_fusion), channel_id=1, source_target_pairs={{0,4},{4,0},{8,12},{12,8},{16,20},{20,16},{24,28},{28,24},{1,5},{5... | collective-permute-start | bytes 1572872 | tf_op jit(solution)/shard_map/ppermute | solution.py:30
  23.5 15.9 %collective-permute-start.5 = (bf16[3,128,512]{2,1,0:T(8,128)(2,1)S(1)}, bf16[3,128,512]{2,1,0:T(8,128)(2,1)S(1)}, u32[]{:S(2)}, u32[]{:S(2)}) collective-permute-start(bf16[3,128,512]{2,1,0:T(8,128)(2,1)S(1)} %get-tuple-element.19.refs_0_), channel_id=1, source_target_pairs={{0,4},{4,0},{8,12},{12,8},{16,20},{20,16},{24,28},{28,24},{1,5},{5... | collective-permute-start | bytes 1179656 | tf_op jit(solution)/shard_map/ppermute | solution.py:30
  30.9 8.6 %collective-permute-start.7 = (bf16[3,128,512]{2,1,0:T(8,128)(2,1)S(1)}, bf16[3,128,512]{2,1,0:T(8,128)(2,1)S(1)}, u32[]{:S(2)}, u32[]{:S(2)}) collective-permute-start(bf16[3,128,512]{2,1,0:T(8,128)(2,1)S(1)} %collective-permute-done.6.refs_2_), channel_id=1, source_target_pairs={{0,4},{4,0},{8,12},{12,8},{16,20},{20,16},{24,28},{28,24},{1,5},{5... | collective-permute-start | bytes 1179656 | tf_op jit(solution)/shard_map/ppermute | solution.py:30
  30.9 13.7 %collective-permute-start.10 = (bf16[256,256]{1,0:T(8,128)(2,1)S(1)}, bf16[256,256]{1,0:T(8,128)(2,1)S(1)}, u32[]{:S(2)}, u32[]{:S(2)}) collective-permute-start(bf16[256,256]{1,0:T(8,128)(2,1)S(1)} %get-tuple-element.22), channel_id=1, source_target_pairs={{0,3},{1,0},{2,1},{3,2},{4,7},{5,4},{6,5},{7,6},{8,11},{9,8},{10,9... | collective-permute-start | bytes 393224 | tf_op jit(solution)/shard_map/ppermute | solution.py:25
  33.4 15.9 %collective-permute-start.9 = (bf16[256,256]{1,0:T(8,128)(2,1)S(1)}, bf16[256,256]{1,0:T(8,128)(2,1)S(1)}, u32[]{:S(2)}, u32[]{:S(2)}) collective-permute-start(bf16[256,256]{1,0:T(8,128)(2,1)S(1)} %get-tuple-element.22), channel_id=1, source_target_pairs={{0,2},{1,3},{2,0},{3,1},{4,6},{5,7},{6,4},{7,5},{8,10},{9,11},{10,... | collective-permute-start | bytes 393224 | tf_op jit(solution)/shard_map/ppermute | solution.py:25
  36.7 12.6 %collective-permute-start.8 = (bf16[256,256]{1,0:T(8,128)(2,1)S(1)}, bf16[256,256]{1,0:T(8,128)(2,1)S(1)}, u32[]{:S(2)}, u32[]{:S(2)}) collective-permute-start(bf16[256,256]{1,0:T(8,128)(2,1)S(1)} %get-tuple-element.22), channel_id=1, source_target_pairs={{0,1},{1,2},{2,3},{3,0},{4,5},{5,6},{6,7},{7,4},{8,9},{9,10},{10,1... | collective-permute-start | bytes 393224 | tf_op jit(solution)/shard_map/ppermute | solution.py:25
  50.5 19.1 %collective-permute-start.22 = (bf16[3,256,256]{2,1,0:T(8,128)(2,1)S(1)}, bf16[3,256,256]{2,1,0:T(8,128)(2,1)S(1)}, u32[]{:S(2)}, u32[]{:S(2)}) collective-permute-start(bf16[3,256,256]{2,1,0:T(8,128)(2,1)S(1)} %get-tuple-element.32.refs_4_), channel_id=1, source_target_pairs={{0,24},{4,28},{8,16},{12,20},{16,8},{20,12},{24,0},{28,4},{1,25},{... | collective-permute-start | bytes 1179656 | tf_op jit(solution)/shard_map/ppermute | solution.py:30
  51.7 19.1 %collective-permute-start.20 = (bf16[3,256,256]{2,1,0:T(8,128)(2,1)S(1)}, bf16[3,256,256]{2,1,0:T(8,128)(2,1)S(1)}, u32[]{:S(2)}, u32[]{:S(2)}) collective-permute-start(bf16[3,256,256]{2,1,0:T(8,128)(2,1)S(1)} %get-tuple-element.32.refs_4_), channel_id=1, source_target_pairs={{0,16},{4,20},{8,24},{12,28},{16,0},{20,4},{24,8},{28,12},{1,17},{... | collective-permute-start | bytes 1179656 | tf_op jit(solution)/shard_map/ppermute | solution.py:30
  53.5 17.4 %collective-permute-start.18 = (bf16[3,256,256]{2,1,0:T(8,128)(2,1)S(1)}, bf16[3,256,256]{2,1,0:T(8,128)(2,1)S(1)}, u32[]{:S(2)}, u32[]{:S(2)}) collective-permute-start(bf16[3,256,256]{2,1,0:T(8,128)(2,1)S(1)} %get-tuple-element.32.refs_4_), channel_id=1, source_target_pairs={{0,8},{4,12},{8,0},{12,4},{16,24},{20,28},{24,16},{28,20},{1,9},{5... | collective-permute-start | bytes 1179656 | tf_op jit(solution)/shard_map/ppermute | solution.py:30
  54.1 8.3 %collective-permute-start.11 = (bf16[512,128]{1,0:T(8,128)(2,1)S(1)}, bf16[512,128]{1,0:T(8,128)(2,1)S(1)}, u32[]{:S(2)}, u32[]{:S(2)}) collective-permute-start(bf16[512,128]{1,0:T(8,128)(2,1)S(1)} %get-tuple-element.25), channel_id=1, source_target_pairs={{0,1},{1,2},{2,3},{3,0},{4,5},{5,6},{6,7},{7,4},{8,9},{9,10},{10,1... | collective-permute-start | bytes 393224 | tf_op jit(solution)/shard_map/ppermute | solution.py:25
  54.1 12.1 %collective-permute-start.12 = (bf16[512,128]{1,0:T(8,128)(2,1)S(1)}, bf16[512,128]{1,0:T(8,128)(2,1)S(1)}, u32[]{:S(2)}, u32[]{:S(2)}) collective-permute-start(bf16[512,128]{1,0:T(8,128)(2,1)S(1)} %get-tuple-element.26), channel_id=1, source_target_pairs={{0,2},{1,3},{2,0},{3,1},{4,6},{5,7},{6,4},{7,5},{8,10},{9,11},{10,... | collective-permute-start | bytes 393224 | tf_op jit(solution)/shard_map/ppermute | solution.py:25
  62.4 5.1 %collective-permute-start.13 = (bf16[512,128]{1,0:T(8,128)(2,1)S(1)}, bf16[512,128]{1,0:T(8,128)(2,1)S(1)}, u32[]{:S(2)}, u32[]{:S(2)}) collective-permute-start(bf16[512,128]{1,0:T(8,128)(2,1)S(1)} %get-tuple-element.27), channel_id=1, source_target_pairs={{0,3},{1,0},{2,1},{3,2},{4,7},{5,4},{6,5},{7,6},{8,11},{9,8},{10,9... | collective-permute-start | bytes 393224 | tf_op jit(solution)/shard_map/ppermute | solution.py:25
  68.5 6.9 %collective-permute-start.14 = (bf16[512,128]{1,0:T(8,128)(2,1)S(1)}, bf16[512,128]{1,0:T(8,128)(2,1)S(1)}, u32[]{:S(2)}, u32[]{:S(2)}) collective-permute-start(bf16[512,128]{1,0:T(8,128)(2,1)S(1)} %get-tuple-element.29), channel_id=1, source_target_pairs={{0,1},{1,2},{2,3},{3,0},{4,5},{5,6},{6,7},{7,4},{8,9},{9,10},{10,1... | collective-permute-start | bytes 393224 | tf_op jit(solution)/shard_map/ppermute | solution.py:25
  69.6 18.1 %collective-permute-start.17 = (bf16[3,256,256]{2,1,0:T(8,128)(2,1)S(1)}, bf16[3,256,256]{2,1,0:T(8,128)(2,1)S(1)}, u32[]{:S(2)}, u32[]{:S(2)}) collective-permute-start(bf16[3,256,256]{2,1,0:T(8,128)(2,1)S(1)} %get-tuple-element.32.refs_4_), channel_id=1, source_target_pairs={{0,4},{4,0},{8,12},{12,8},{16,20},{20,16},{24,28},{28,24},{1,5},{5... | collective-permute-start | bytes 1179656 | tf_op jit(solution)/shard_map/ppermute | solution.py:30
  69.6 18.1 %collective-permute-start.23 = (bf16[3,256,256]{2,1,0:T(8,128)(2,1)S(1)}, bf16[3,256,256]{2,1,0:T(8,128)(2,1)S(1)}, u32[]{:S(2)}, u32[]{:S(2)}) collective-permute-start(bf16[3,256,256]{2,1,0:T(8,128)(2,1)S(1)} %collective-permute-done.22.refs_10_), channel_id=1, source_target_pairs={{0,4},{4,0},{8,12},{12,8},{16,20},{20,16},{24,28},{28,24},{1,5},{5... | collective-permute-start | bytes 1179656 | tf_op jit(solution)/shard_map/ppermute | solution.py:30
  70.8 16.9 %collective-permute-start.21 = (bf16[3,256,256]{2,1,0:T(8,128)(2,1)S(1)}, bf16[3,256,256]{2,1,0:T(8,128)(2,1)S(1)}, u32[]{:S(2)}, u32[]{:S(2)}) collective-permute-start(bf16[3,256,256]{2,1,0:T(8,128)(2,1)S(1)} %collective-permute-done.20.refs_8_), channel_id=1, source_target_pairs={{0,4},{4,0},{8,12},{12,8},{16,20},{20,16},{24,28},{28,24},{1,5},{5... | collective-permute-start | bytes 1179656 | tf_op jit(solution)/shard_map/ppermute | solution.py:30
  70.9 16.8 %collective-permute-start.19 = (bf16[3,256,256]{2,1,0:T(8,128)(2,1)S(1)}, bf16[3,256,256]{2,1,0:T(8,128)(2,1)S(1)}, u32[]{:S(2)}, u32[]{:S(2)}) collective-permute-start(bf16[3,256,256]{2,1,0:T(8,128)(2,1)S(1)} %collective-permute-done.18.refs_6_), channel_id=1, source_target_pairs={{0,4},{4,0},{8,12},{12,8},{16,20},{20,16},{24,28},{28,24},{1,5},{5... | collective-permute-start | bytes 1179656 | tf_op jit(solution)/shard_map/ppermute | solution.py:30
  75.4 7.4 %collective-permute-start.15 = (bf16[512,128]{1,0:T(8,128)(2,1)S(1)}, bf16[512,128]{1,0:T(8,128)(2,1)S(1)}, u32[]{:S(2)}, u32[]{:S(2)}) collective-permute-start(bf16[512,128]{1,0:T(8,128)(2,1)S(1)} %get-tuple-element.30), channel_id=1, source_target_pairs={{0,2},{1,3},{2,0},{3,1},{4,6},{5,7},{6,4},{7,5},{8,10},{9,11},{10,... | collective-permute-start | bytes 393224 | tf_op jit(solution)/shard_map/ppermute | solution.py:25
  82.8 5.0 %collective-permute-start.16 = (bf16[512,128]{1,0:T(8,128)(2,1)S(1)}, bf16[512,128]{1,0:T(8,128)(2,1)S(1)}, u32[]{:S(2)}, u32[]{:S(2)}) collective-permute-start(bf16[512,128]{1,0:T(8,128)(2,1)S(1)} %get-tuple-element.31), channel_id=1, source_target_pairs={{0,3},{1,0},{2,1},{3,2},{4,7},{5,4},{6,5},{7,6},{8,11},{9,8},{10,9... | collective-permute-start | bytes 393224 | tf_op jit(solution)/shard_map/ppermute | solution.py:25
  (14 other events, 269.5 us)

commit v6 on v5

--- a/solution.py
+++ b/solution.py
@@ -9,6 +9,8 @@
 
 HEADS = 4
 SPREAD = 8
+IN_BITS = ((0, 2), (4, 6), (1, 3), (5, 7))
+OUT_BITS = ((0, 4), (2, 6), (1, 5), (3, 7))
 LANES = 128
 F32 = jnp.float32
 BF16 = jnp.bfloat16
@@ -54,22 +56,39 @@
 
 
 def pack_kernel(place, own_in, own_out, *refs):
-    arrived, (stacked, packed) = refs[:-2], refs[-2:]
+    arrived, (stacked, packed, sems) = refs[:-3], refs[-3:]
     in_shard, hidden = own_in.shape
     out_shard, width = own_out.shape
     in_cols, out_rows = hidden // SPREAD, out_shard // SPREAD
     slot = lax.rem(place[0], SPREAD)
+    cols = pl.ds(pl.multiple_of(slot * in_cols, in_cols), in_cols)
+    rows = pl.ds(pl.multiple_of(slot * out_rows, out_rows), out_rows)
+    copies = [pltpu.make_async_copy(own_in.at[:, cols], packed.at[:in_shard, :], sems.at[0])]
+    for fold in range(width // in_cols):
+        first = in_shard + fold * out_rows
+        copies.append(
+            pltpu.make_async_copy(
+                own_out.at[rows, fold * in_cols : (fold + 1) * in_cols],
+                packed.at[first : first + out_rows, :],
+                sems.at[1 + fold],
+            )
+        )
+    for copy in copies:
+        copy.start()
     for index, piece in enumerate(arrived):
         stacked[index] = piece[...]
-    packed[:in_shard, :] = own_in[:, pl.ds(pl.multiple_of(slot * in_cols, in_cols), in_cols)]
-    rows = pl.ds(pl.multiple_of(slot * out_rows, out_rows), out_rows)
-    for fold in range(width // in_cols):
-        first = in_shard + fold * out_rows
-        packed[first : first + out_rows, :] = own_out[rows, fold * in_cols : (fold + 1) * in_cols]
+    for copy in copies:
+        copy.wait()
+
+
+def pair_kernel(*refs):
+    ins, outs = refs[:4], refs[4:]
+    for index, value in enumerate(ins):
+        outs[index // 2][index % 2] = value[...]
 
 
 def attention_kernel(zones, reach, steps, place, pattern, normed, own_qkv, own_attn, *refs):
-    pieces, (context_out, attn_out, weights, w_turned, projected, context) = refs[:-6], refs[-6:]
+    pieces, (context_out, attn_out, weights, w_turned, projected, context, sems) = refs[:-7], refs[-7:]
     key_count = (reach + 1) * steps
     zone_rows = normed.shape[0] // key_count
     width = normed.shape[1]
@@ -78,15 +97,25 @@
     shard = own_qkv.shape[0]
 
     own_rows = pl.ds(pl.multiple_of(my_zone * shard, shard), shard)
-    for index in range(3):
-        weights[index, own_rows, :] = own_qkv[:, index * width : (index + 1) * width]
-    weights[3, own_rows, :] = own_attn[...]
+    copies = [
+        pltpu.make_async_copy(
+            own_qkv.at[:, index * width : (index + 1) * width],
+            weights.at[index, own_rows, :],
+            sems.at[index],
+        )
+        for index in range(3)
+    ]
+    copies.append(pltpu.make_async_copy(own_attn, weights.at[3, own_rows, :], sems.at[3]))
+    for copy in copies:
+        copy.start()
     my_quarter = quarter_of(my_block)
     for step in range(1, zones):
         source = lax.rem(my_zone - step + zones, zones)
         rows = pl.ds(pl.multiple_of(source * shard, shard), shard)
         for bits, piece in enumerate(pieces):
             weights[my_quarter ^ bits, rows, :] = piece[step - 1]
+    for copy in copies:
+        copy.wait()
     attn_out[...] = weights[3]
     for index in range(3):
         for block in range(width // LANES):
@@ -174,9 +203,11 @@
     parts = refs[-1]
     steps, zone_rows, _ = states.shape
     zones, _, part = parts.shape
-    across, (after_out, *outs, across_out) = refs[: zones - 1], refs[zones - 1 : -1]
+    across, (after_out, *outs, first_out, second_out) = refs[: zones - 1], refs[zones - 1 : -1]
+    split = first_out.shape[1]
     for index, piece in enumerate(across):
-        across_out[index] = piece[...]
+        first_out[index] = piece[:split, :]
+        second_out[index] = piece[split:, :]
     my_zone = place[1]
     gain = gain_mix[...]
     for step in range(steps):
@@ -193,7 +224,7 @@
 
 
 def mixing_kernel(steps, zones, place, neighbours, degree, mix, *refs):
-    arrived, outs, items = refs[:zones], refs[zones : 2 * zones], refs[-1]
+    arrived, outs, items = refs[:zones], refs[-1 - zones : -1], refs[-1]
     _, slots, zone_rows, _ = mix.shape
     part = items.shape[-1]
     my_zone = place[1]
@@ -229,30 +260,47 @@
 
 def ffn_kernel(zones, place, after_attn, gain_ffn, own_in, own_out, *refs):
     arrived, refs = refs[:zones], refs[zones:]
-    pieces, (out, w_in, w_out, after_mix, ffn_in, parts) = refs[:-6], refs[-6:]
+    pieces, (out, w_in, w_out, after_mix, ffn_in, parts, sems) = refs[:-7], refs[-7:]
     rows_all, width = after_attn.shape
     my_block, my_zone = place[0], place[1]
     in_shard, hidden = own_in.shape
     out_shard = own_out.shape[0]
     in_cols, out_rows = hidden // SPREAD, out_shard // SPREAD
 
+    own_rows = pl.ds(pl.multiple_of(my_zone * in_shard, in_shard), in_shard)
+    copies = [
+        pltpu.make_async_copy(
+            own_in.at[:, index * in_cols : (index + 1) * in_cols],
+            w_in.at[index, own_rows, :],
+            sems.at[index],
+        )
+        for index in range(SPREAD)
+    ]
+    own_rows = pl.ds(pl.multiple_of(my_zone * out_shard, out_shard), out_shard)
+    copies.append(pltpu.make_async_copy(own_out, w_out.at[own_rows, :], sems.at[SPREAD]))
+    for copy in copies:
+        copy.start()
     for step in range(zones):
         parts[lax.rem(my_zone - step + zones, zones)] = arrived[step][...]
-    start = pl.multiple_of(my_zone * in_shard, in_shard)
-    for index in range(SPREAD):
-        w_in[index, pl.ds(start, in_shard), :] = own_in[:, index * in_cols : (index + 1) * in_cols]
-    w_out[pl.ds(pl.multiple_of(my_zone * out_shard, out_shard), out_shard), :] = own_out[...]
-    for bits, piece in enumerate(pieces):
-        slot = lax.rem(my_block, SPREAD) ^ bits
-        for step in range(1, zones):
-            source = lax.rem(my_zone - step + zones, zones)
-            rows = pl.ds(pl.multiple_of(source * in_shard, in_shard), in_shard)
-            w_in[slot, rows, :] = piece[step - 1, :in_shard, :]
-            rows = pl.ds(pl.multiple_of(source * out_shard + slot * out_rows, out_rows), out_rows)
-            for fold in range(width // in_cols):
-                first = in_shard + fold * out_rows
-                cols = slice(fold * in_cols, (fold + 1) * in_cols)
-                w_out[rows, cols] = piece[step - 1, first : first + out_rows, :]
+    for piece, bits_pair in zip(pieces[:4], IN_BITS):
+        for index, bits in enumerate(bits_pair):
+            slot = lax.rem(my_block, SPREAD) ^ bits
+            for step in range(1, zones):
+                source = lax.rem(my_zone - step + zones, zones)
+                rows = pl.ds(pl.multiple_of(source * in_shard, in_shard), in_shard)
+                w_in[slot, rows, :] = piece[index, step - 1]
+    for piece, bits_pair in zip(pieces[4:], OUT_BITS):
+        for index, bits in enumerate(bits_pair):
+            slot = lax.rem(my_block, SPREAD) ^ bits
+            for step in range(1, zones):
+                source = lax.rem(my_zone - step + zones, zones)
+                first = pl.multiple_of(source * out_shard + slot * out_rows, out_rows)
+                for fold in range(width // in_cols):
+                    cols = slice(fold * in_cols, (fold + 1) * in_cols)
+                    rows = slice(fold * out_rows, (fold + 1) * out_rows)
+                    w_out[pl.ds(first, out_rows), cols] = piece[index, step - 1, rows, :]
+    for copy in copies:
+        copy.wait()
 
     gain = gain_ffn[...]
     span = 128
@@ -278,19 +326,17 @@
         out[rows, :] = total.astype(BF16)
 
 
-def call(kernel, out_shape, scratch, flops, smem, limit, args):
-    in_specs = [
-        pl.BlockSpec(memory_space=pltpu.SMEM if index in smem else pltpu.VMEM)
-        for index in range(len(args))
-    ]
-    moved = sum(arg.size * arg.dtype.itemsize for arg in args)
+def call(kernel, out_shape, scratch, smem, hbm, limit, args):
+    spaces = {index: pltpu.SMEM for index in smem} | {index: pltpu.HBM for index in hbm}
     return pl.pallas_call(
         kernel,
         out_shape=out_shape,
-        in_specs=in_specs,
+        in_specs=[
+            pl.BlockSpec(memory_space=spaces.get(index, pltpu.VMEM)) for index in range(len(args))
+        ],
         out_specs=jax.tree.map(lambda _: pl.BlockSpec(memory_space=pltpu.VMEM), out_shape),
         scratch_shapes=scratch,
-        cost_estimate=pl.CostEstimate(flops=flops, bytes_accessed=moved, transcendentals=0),
+        cost_estimate=pl.CostEstimate(flops=0, bytes_accessed=0, transcendentals=0),
         compiler_params=pltpu.CompilerParams(vmem_limit_bytes=limit * MIB),
     )(*args)
 
@@ -328,16 +374,17 @@
     )
     direct = [rotated(first, "zone", step) for step in rotations]
     in_shard = w_in.shape[0]
-    packed_shape = (in_shard + out_rows * (width // in_cols), in_cols)
+    sizes = (in_shard, out_rows * (width // in_cols))
+    packed_shape = (sum(sizes), in_cols)
     direct, packed = call(
         pack_kernel,
         (
             jax.ShapeDtypeStruct((zones - 1,) + first.shape, BF16),
             jax.ShapeDtypeStruct(packed_shape, BF16),
         ),
-        [],
-        0,
+        [pltpu.SemaphoreType.DMA((1 + width // in_cols,))],
         (0,),
+        (1, 2),
         8,
         [place, w_in, w_out] + direct,
     )
@@ -350,7 +397,7 @@
         norm_kernel,
         jax.ShapeDtypeStruct((key_count * zone_rows, width), BF16),
         [],
-        8 * key_count * zone_rows * width,
+        (),
         (),
         8,
         [before, last, states, gain_attn.reshape(1, -1)],
@@ -367,40 +414,51 @@
             pltpu.VMEM((3 * width, width), BF16),
             pltpu.VMEM((3 * width, key_count * zone_rows), F32),
             pltpu.VMEM((width, rows), F32),
+            pltpu.SemaphoreType.DMA((4,)),
         ],
-        2 * rows * width * width * 20,
         (0, 1),
+        (3, 4),
         22,
         [place, pattern, normed, w_qkv, w_out_attn] + quarters,
     )
 
     chunk = jax.ShapeDtypeStruct((rows, part), BF16)
-    after_attn, *chunks, across = call(
+    after_attn, *chunks, part_in, part_out = call(
         project_kernel,
         (jax.ShapeDtypeStruct((rows, width), F32),)
         + (chunk,) * zones
-        + (jax.ShapeDtypeStruct((zones - 1,) + packed_shape, BF16),),
+        + tuple(jax.ShapeDtypeStruct((zones - 1, size, in_cols), BF16) for size in sizes),
         [pltpu.VMEM((zones, rows, part), BF16)],
-        2 * rows * width * width,
         (0,),
+        (),
         8,
         [place, states, context, w_attn, gain_mix.reshape(1, -1)] + across,
     )
     arrived = [chunks[0]] + [rotated(chunks[step], "zone", step) for step in rotations]
 
-    pieces = {bits: swapped(across, "tm", bits) for bits in range(2, SPREAD, 2)}
-    pieces[0] = across
-    for bits in range(0, SPREAD, 2):
-        pieces[bits + 1] = swapped(pieces[bits], "tm", 1)
+    over_in, over_out = swapped(part_in, "tm", 2), swapped(part_out, "tm", 4)
+    pair_in, pair_out = call(
+        pair_kernel,
+        tuple(jax.ShapeDtypeStruct((2,) + value.shape, BF16) for value in (part_in, part_out)),
+        [],
+        (),
+        (),
+        8,
+        [part_in, over_in, part_out, over_out],
+    )
+    pieces_in = [pair_in, swapped(pair_in, "tm", 4)]
+    pieces_out = [pair_out, swapped(pair_out, "tm", 2)]
+    pieces = pieces_in + [swapped(value, "tm", 1) for value in pieces_in]
+    pieces += pieces_out + [swapped(value, "tm", 1) for value in pieces_out]
 
     spatial = call(
         functools.partial(mixing_kernel, steps, zones),
         (chunk,) * zones,
         [pltpu.VMEM((zones, rows, part), BF16)],
-        2 * rows * width * zone_rows * 3,
         (0, 1, 2),
+        (),
         8,
-        [place, neighbours, degree, mix] + arrived,
+        [place, neighbours, degree, mix] + arrived + [pair_in],
     )
     arrived = [spatial[0]] + [rotated(spatial[step], "zone", step) for step in rotations]
     evolved = call(
@@ -412,13 +470,14 @@
             pltpu.VMEM((rows, width), F32),
             pltpu.VMEM((rows, width), BF16),
             pltpu.VMEM((zones, rows, part), BF16),
+            pltpu.SemaphoreType.DMA((SPREAD + 1,)),
         ],
-        4 * rows * width * hidden,
         (0,),
+        (3, 4),
         16,
         [place, after_attn, gain_ffn.reshape(1, -1), w_in, w_out]
         + arrived
-        + [pieces[bits] for bits in range(SPREAD)],
+        + pieces,
     )
     return evolved.reshape(steps, zone_rows, width)
 

time: 92.4 us -> 98.2 us (1.063)
  starting transfers between devices: 27.1 us -> 32.6 us
    ppermute x12, waiting for transfers between devices: 41 us -> 35.4 us  [rotated(): lax.ppermute(value, axis, [(source, (source + steps) % count) for source...]
    ppermute x11 -> x12, waiting for transfers between devices: 7.66 us -> 13 us  [swapped(): lax.ppermute(value, axis, [(source, source ^ bits) for source in range(co...]
    ppermute x12, starting transfers between devices: 15.4 us -> 20.6 us  [rotated(): lax.ppermute(value, axis, [(source, (source + steps) % count) for source...]
    pallas_call x6 -> x7, Pallas kernels: 12.5 us -> 13 us  [call(): pl.pallas_call(kernel, out_shape=out_shape, in_specs=[pl.BlockSpec(memory...]
    ppermute x11 -> x12, starting transfers between devices: 6.65 us -> 7.07 us  [swapped(): lax.ppermute(value, axis, [(source, source ^ bits) for source in range(co...]
  transfers between devices with their start and end apart: 24 -> 25, of which waited for: 12 -> 11; matrix products, arithmetic and copies ran while one was open for 1% -> 1% of each run, Pallas kernels for 8% -> 7%
where the time goes in v6:
time: 98.2 us; the launch traced here: 97.9 us
  waiting for transfers between devices  48.4 us (49%)
  starting transfers between devices  32.6 us (33%)
  Pallas kernels  13 us (13%)
  local copies, waits for them, and re-layouts  2.49 us (3%)
  other arithmetic  1.1 us (1%)
    ppermute x12, waiting for transfers between devices, rotated(): lax.ppermute(value, axis, [(source, (source + steps) % count) for source...  35.4 us
    ppermute x12, starting transfers between devices, rotated(): lax.ppermute(value, axis, [(source, (source + steps) % count) for source...  20.6 us
    ppermute x12, waiting for transfers between devices, swapped(): lax.ppermute(value, axis, [(source, source ^ bits) for source in range(co...  13 us
    pallas_call x7, Pallas kernels, call(): pl.pallas_call(kernel, out_shape=out_shape, in_specs=[pl.BlockSpec(memory...  13 us
    ppermute x12, starting transfers between devices, swapped(): lax.ppermute(value, axis, [(source, source ^ bits) for source in range(co...  7.07 us
    ppermute x1, starting transfers between devices, shifted(): lax.ppermute(value, axis, [(source, source + steps) for source in range(c...  4.99 us
    unnamed x28, local copies, waits for them, and re-layouts  2.49 us
  transfers between devices with their start and end apart: 25, of which 11 were waited for; matrix products, arithmetic and copies ran while one was open for 1% of the time, Pallas kernels for 7%

profile of v6, /device:TPU:0, one launch (start us, length us, event | category | flops | bytes accessed | tf_op | source)
XLA Modules:
  0.0 97.9 jit_solution(11950945567115194573)
XLA Ops:
  0.0 5.0 %collective-permute-start = (bf16[4,128,512]{2,1,0:T(8,128)(2,1)}, bf16[4,128,512]{2,1,0:T(8,128)(2,1)S(1)}, u32[]{:S(2)}, u32[]{:S(2)}) collective-permute-start(bf16[4,128,512]{2,1,0:T(8,128)(2,1)} %states.1), channel_id=1, source_target_pairs={{0,8},{4,12},{8,16},{12,20},{16,24},{20,28},{1,9},{5,13},{9,17},{1... | collective-permute-start | bytes 1572872 | tf_op jit(solution)/shard_map/ppermute | solution.py:22
  6.0 2.7 %collective-permute-start.3 = (bf16[128,512]{1,0:T(8,128)(2,1)S(1)}, bf16[128,512]{1,0:T(8,128)(2,1)S(1)}, u32[]{:S(2)}, u32[]{:S(2)}) collective-permute-start(bf16[128,512]{1,0:T(8,128)(2,1)S(1)} %fusion), channel_id=1, source_target_pairs={{0,2},{1,3},{2,0},{3,1},{4,6},{5,7},{6,4},{7,5},{8,10},{9,11},{10,... | collective-permute-start | bytes 393224 | tf_op jit(solution)/shard_map/ppermute | solution.py:27
  8.7 1.6 %collective-permute-start.2 = (bf16[128,512]{1,0:T(8,128)(2,1)S(1)}, bf16[128,512]{1,0:T(8,128)(2,1)S(1)}, u32[]{:S(2)}, u32[]{:S(2)}) collective-permute-start(bf16[128,512]{1,0:T(8,128)(2,1)S(1)} %fusion), channel_id=1, source_target_pairs={{0,1},{1,2},{2,3},{3,0},{4,5},{5,6},{6,7},{7,4},{8,9},{9,10},{10,1... | collective-permute-start | bytes 393224 | tf_op jit(solution)/shard_map/ppermute | solution.py:27
  10.2 2.2 %collective-permute-start.4 = (bf16[128,512]{1,0:T(8,128)(2,1)S(1)}, bf16[128,512]{1,0:T(8,128)(2,1)S(1)}, u32[]{:S(2)}, u32[]{:S(2)}) collective-permute-start(bf16[128,512]{1,0:T(8,128)(2,1)S(1)} %fusion), channel_id=1, source_target_pairs={{0,3},{1,0},{2,1},{3,2},{4,7},{5,4},{6,5},{7,6},{8,11},{9,8},{10,9... | collective-permute-start | bytes 393224 | tf_op jit(solution)/shard_map/ppermute | solution.py:27
  12.6 6.2 %collective-permute-done.3.refs_1_ = bf16[128,512]{1,0:T(8,128)(2,1)S(1)} collective-permute-done((bf16[128,512]{1,0:T(8,128)(2,1)S(1)}, bf16[128,512]{1,0:T(8,128)(2,1)S(1)}, u32[]{:S(2)}, u32[]{:S(2)}) %collective-permute-start.3) | collective-permute-done | bytes 131104 | tf_op jit(solution)/shard_map/ppermute | solution.py:27
  21.9 1.6 %collective-permute-start.6 = (bf16[3,128,512]{2,1,0:T(8,128)(2,1)S(1)}, bf16[3,128,512]{2,1,0:T(8,128)(2,1)S(1)}, u32[]{:S(2)}, u32[]{:S(2)}) collective-permute-start(bf16[3,128,512]{2,1,0:T(8,128)(2,1)S(1)} %get-tuple-element.22.refs_0_), channel_id=1, source_target_pairs={{0,16},{4,20},{8,24},{12,28},{16,0},{20,4},{24,8},{28,12},{1,17},{... | collective-permute-start | bytes 1179656 | tf_op jit(solution)/shard_map/ppermute | solution.py:32
  24.1 6.8 %collective-permute-done.6.refs_2_ = bf16[3,128,512]{2,1,0:T(8,128)(2,1)S(1)} collective-permute-done((bf16[3,128,512]{2,1,0:T(8,128)(2,1)S(1)}, bf16[3,128,512]{2,1,0:T(8,128)(2,1)S(1)}, u32[]{:S(2)}, u32[]{:S(2)}) %collective-permute-start.6) | collective-permute-done | bytes 393248 | tf_op jit(solution)/shard_map/ppermute | solution.py:32
  30.9 2.5 %collective-permute-start.10 = (bf16[256,256]{1,0:T(8,128)(2,1)S(1)}, bf16[256,256]{1,0:T(8,128)(2,1)S(1)}, u32[]{:S(2)}, u32[]{:S(2)}) collective-permute-start(bf16[256,256]{1,0:T(8,128)(2,1)S(1)} %get-tuple-element.25), channel_id=1, source_target_pairs={{0,3},{1,0},{2,1},{3,2},{4,7},{5,4},{6,5},{7,6},{8,11},{9,8},{10,9... | collective-permute-start | bytes 393224 | tf_op jit(solution)/shard_map/ppermute | solution.py:27
  33.4 3.4 %collective-permute-start.9 = (bf16[256,256]{1,0:T(8,128)(2,1)S(1)}, bf16[256,256]{1,0:T(8,128)(2,1)S(1)}, u32[]{:S(2)}, u32[]{:S(2)}) collective-permute-start(bf16[256,256]{1,0:T(8,128)(2,1)S(1)} %get-tuple-element.25), channel_id=1, source_target_pairs={{0,2},{1,3},{2,0},{3,1},{4,6},{5,7},{6,4},{7,5},{8,10},{9,11},{10,... | collective-permute-start | bytes 393224 | tf_op jit(solution)/shard_map/ppermute | solution.py:27
  36.8 2.0 %collective-permute-start.8 = (bf16[256,256]{1,0:T(8,128)(2,1)S(1)}, bf16[256,256]{1,0:T(8,128)(2,1)S(1)}, u32[]{:S(2)}, u32[]{:S(2)}) collective-permute-start(bf16[256,256]{1,0:T(8,128)(2,1)S(1)} %get-tuple-element.25), channel_id=1, source_target_pairs={{0,1},{1,2},{2,3},{3,0},{4,5},{5,6},{6,7},{7,4},{8,9},{9,10},{10,1... | collective-permute-start | bytes 393224 | tf_op jit(solution)/shard_map/ppermute | solution.py:27
  39.8 5.0 %shard_map.120 = (bf16[512,512]{1,0:T(8,128)(2,1)S(1)}, bf16[512,512]{1,0:T(8,128)(2,1)S(1)}) custom-call(s32[2]{0:T(128)S(1)} %pad_add_fusion.place, s32[1,2]{1,0:T(1,128)S(1)} %copy-done.12, bf16[1536,512]{1,0:T(8,128)(2,1)S(1)} %shard_map.118.normed, bf16[128,1536]{1,0:T(8,128)(2,1)S(1)} %copy-done.5, bf16[128,512]{1,0:T(8,128)(2,1)S(1)} %copy-done.6, ...), custom_call_target="tpu_custom_call" | custom-call | tf_op jit(solution)/shard_map/pallas_call | solution.py:331
  44.9 4.5 %collective-permute-done.9.refs_1_ = bf16[256,256]{1,0:T(8,128)(2,1)S(1)} collective-permute-done((bf16[256,256]{1,0:T(8,128)(2,1)S(1)}, bf16[256,256]{1,0:T(8,128)(2,1)S(1)}, u32[]{:S(2)}, u32[]{:S(2)}) %collective-permute-start.9) | collective-permute-done | bytes 131104 | tf_op jit(solution)/shard_map/ppermute | solution.py:27
  50.6 1.5 %collective-permute-start.14 = (bf16[3,128,256]{2,1,0:T(8,128)(2,1)S(1)}, bf16[3,128,256]{2,1,0:T(8,128)(2,1)S(1)}, u32[]{:S(2)}, u32[]{:S(2)}) collective-permute-start(bf16[3,128,256]{2,1,0:T(8,128)(2,1)S(1)} %get-tuple-element.31.refs_0_), channel_id=1, source_target_pairs={{0,8},{4,12},{8,0},{12,4},{16,24},{20,28},{24,16},{28,20},{1,9},{5... | collective-permute-start | bytes 589832 | tf_op jit(solution)/shard_map/ppermute | solution.py:32
  52.4 5.0 %collective-permute-done.14.refs_1_ = bf16[3,128,256]{2,1,0:T(8,128)(2,1)S(1)} collective-permute-done((bf16[3,128,256]{2,1,0:T(8,128)(2,1)S(1)}, bf16[3,128,256]{2,1,0:T(8,128)(2,1)S(1)}, u32[]{:S(2)}, u32[]{:S(2)}) %collective-permute-start.14) | collective-permute-done | bytes 196640 | tf_op jit(solution)/shard_map/ppermute | solution.py:32
  57.4 1.2 %collective-permute-done.15.refs_3_ = bf16[3,128,256]{2,1,0:T(8,128)(2,1)S(1)} collective-permute-done((bf16[3,128,256]{2,1,0:T(8,128)(2,1)S(1)}, bf16[3,128,256]{2,1,0:T(8,128)(2,1)S(1)}, u32[]{:S(2)}, u32[]{:S(2)}) %collective-permute-start.15) | collective-permute-done | bytes 196640 | tf_op jit(solution)/shard_map/ppermute | solution.py:32
  59.2 1.5 %collective-permute-start.19 = (bf16[2,3,128,256]{3,2,1,0:T(8,128)(2,1)S(1)}, bf16[2,3,128,256]{3,2,1,0:T(8,128)(2,1)S(1)}, u32[]{:S(2)}, u32[]{:S(2)}) collective-permute-start(bf16[2,3,128,256]{3,2,1,0:T(8,128)(2,1)S(1)} %get-tuple-element.33.refs_4_), channel_id=1, source_target_pairs={{0,16},{4,20},{8,24},{12,28},{16,0},{20,4},{24,8},{28,12},{1,17},{... | collective-permute-start | bytes 1179656 | tf_op jit(solution)/shard_map/ppermute | solution.py:32
  60.7 3.8 %collective-permute-start.13 = (bf16[512,128]{1,0:T(8,128)(2,1)S(1)}, bf16[512,128]{1,0:T(8,128)(2,1)S(1)}, u32[]{:S(2)}, u32[]{:S(2)}) collective-permute-start(bf16[512,128]{1,0:T(8,128)(2,1)S(1)} %get-tuple-element.30), channel_id=1, source_target_pairs={{0,3},{1,0},{2,1},{3,2},{4,7},{5,4},{6,5},{7,6},{8,11},{9,8},{10,9... | collective-permute-start | bytes 393224 | tf_op jit(solution)/shard_map/ppermute | solution.py:27
  64.6 4.4 %collective-permute-done.11.refs_1_ = bf16[512,128]{1,0:T(8,128)(2,1)S(1)} collective-permute-done((bf16[512,128]{1,0:T(8,128)(2,1)S(1)}, bf16[512,128]{1,0:T(8,128)(2,1)S(1)}, u32[]{:S(2)}, u32[]{:S(2)}) %collective-permute-start.11) | collective-permute-done | bytes 131104 | tf_op jit(solution)/shard_map/ppermute | solution.py:27
  69.0 2.9 %collective-permute-done.12.refs_2_ = bf16[512,128]{1,0:T(8,128)(2,1)S(1)} collective-permute-done((bf16[512,128]{1,0:T(8,128)(2,1)S(1)}, bf16[512,128]{1,0:T(8,128)(2,1)S(1)}, u32[]{:S(2)}, u32[]{:S(2)}) %collective-permute-start.12) | collective-permute-done | bytes 131104 | tf_op jit(solution)/shard_map/ppermute | solution.py:27
  73.0 2.4 %collective-permute-start.16 = (bf16[512,128]{1,0:T(8,128)(2,1)S(1)}, bf16[512,128]{1,0:T(8,128)(2,1)S(1)}, u32[]{:S(2)}, u32[]{:S(2)}) collective-permute-start(bf16[512,128]{1,0:T(8,128)(2,1)S(1)} %get-tuple-element.35), channel_id=1, source_target_pairs={{0,1},{1,2},{2,3},{3,0},{4,5},{5,6},{6,7},{7,4},{8,9},{9,10},{10,1... | collective-permute-start | bytes 393224 | tf_op jit(solution)/shard_map/ppermute | solution.py:27
  76.4 3.4 %collective-permute-done.16.refs_1_ = bf16[512,128]{1,0:T(8,128)(2,1)S(1)} collective-permute-done((bf16[512,128]{1,0:T(8,128)(2,1)S(1)}, bf16[512,128]{1,0:T(8,128)(2,1)S(1)}, u32[]{:S(2)}, u32[]{:S(2)}) %collective-permute-start.16) | collective-permute-done | bytes 131104 | tf_op jit(solution)/shard_map/ppermute | solution.py:27
  79.8 8.5 %collective-permute-done.17.refs_2_ = bf16[512,128]{1,0:T(8,128)(2,1)S(1)} collective-permute-done((bf16[512,128]{1,0:T(8,128)(2,1)S(1)}, bf16[512,128]{1,0:T(8,128)(2,1)S(1)}, u32[]{:S(2)}, u32[]{:S(2)}) %collective-permute-start.17) | collective-permute-done | bytes 131104 | tf_op jit(solution)/shard_map/ppermute | solution.py:27
  88.4 5.0 %collective-permute-done.18.refs_3_ = bf16[512,128]{1,0:T(8,128)(2,1)S(1)} collective-permute-done((bf16[512,128]{1,0:T(8,128)(2,1)S(1)}, bf16[512,128]{1,0:T(8,128)(2,1)S(1)}, u32[]{:S(2)}, u32[]{:S(2)}) %collective-permute-start.18) | collective-permute-done | bytes 131104 | tf_op jit(solution)/shard_map/ppermute | solution.py:27
  93.4 4.5 %shard_map.124 = bf16[512,512]{1,0:T(8,128)(2,1)} custom-call(s32[2]{0:T(128)S(1)} %pad_add_fusion.place, f32[512,512]{1,0:T(8,128)S(1)} %get-tuple-element.26.after_attn, f32[1,512]{1,0:T(1,128)S(1)} %bitcast.7, bf16[128,2048]{1,0:T(8,128)(2,1)S(1)} %copy-done.2, bf16[512,512]{1,0:T(8,128)(2,1)S(1)} %copy-done.4, ...), custom_call_target="tpu_custom_call" | custom-call | tf_op jit(solution)/shard_map/pallas_call | solution.py:331
  (64 shorter events, 10.1 us)
Async XLA Ops:
  0.0 23.4 %collective-permute-start = (bf16[4,128,512]{2,1,0:T(8,128)(2,1)}, bf16[4,128,512]{2,1,0:T(8,128)(2,1)S(1)}, u32[]{:S(2)}, u32[]{:S(2)}) collective-permute-start(bf16[4,128,512]{2,1,0:T(8,128)(2,1)} %states.1), channel_id=1, source_target_pairs={{0,8},{4,12},{8,16},{12,20},{16,24},{20,28},{1,9},{5,13},{9,17},{1... | collective-permute-start | bytes 1572872 | tf_op jit(solution)/shard_map/ppermute | solution.py:22
  6.0 12.7 %collective-permute-start.3 = (bf16[128,512]{1,0:T(8,128)(2,1)S(1)}, bf16[128,512]{1,0:T(8,128)(2,1)S(1)}, u32[]{:S(2)}, u32[]{:S(2)}) collective-permute-start(bf16[128,512]{1,0:T(8,128)(2,1)S(1)} %fusion), channel_id=1, source_target_pairs={{0,2},{1,3},{2,0},{3,1},{4,6},{5,7},{6,4},{7,5},{8,10},{9,11},{10,... | collective-permute-start | bytes 393224 | tf_op jit(solution)/shard_map/ppermute | solution.py:27
  8.7 10.1 %collective-permute-start.2 = (bf16[128,512]{1,0:T(8,128)(2,1)S(1)}, bf16[128,512]{1,0:T(8,128)(2,1)S(1)}, u32[]{:S(2)}, u32[]{:S(2)}) collective-permute-start(bf16[128,512]{1,0:T(8,128)(2,1)S(1)} %fusion), channel_id=1, source_target_pairs={{0,1},{1,2},{2,3},{3,0},{4,5},{5,6},{6,7},{7,4},{8,9},{9,10},{10,1... | collective-permute-start | bytes 393224 | tf_op jit(solution)/shard_map/ppermute | solution.py:27
  10.2 8.9 %collective-permute-start.4 = (bf16[128,512]{1,0:T(8,128)(2,1)S(1)}, bf16[128,512]{1,0:T(8,128)(2,1)S(1)}, u32[]{:S(2)}, u32[]{:S(2)}) collective-permute-start(bf16[128,512]{1,0:T(8,128)(2,1)S(1)} %fusion), channel_id=1, source_target_pairs={{0,3},{1,0},{2,1},{3,2},{4,7},{5,4},{6,5},{7,6},{8,11},{9,8},{10,9... | collective-permute-start | bytes 393224 | tf_op jit(solution)/shard_map/ppermute | solution.py:27
  21.9 9.0 %collective-permute-start.6 = (bf16[3,128,512]{2,1,0:T(8,128)(2,1)S(1)}, bf16[3,128,512]{2,1,0:T(8,128)(2,1)S(1)}, u32[]{:S(2)}, u32[]{:S(2)}) collective-permute-start(bf16[3,128,512]{2,1,0:T(8,128)(2,1)S(1)} %get-tuple-element.22.refs_0_), channel_id=1, source_target_pairs={{0,16},{4,20},{8,24},{12,28},{16,0},{20,4},{24,8},{28,12},{1,17},{... | collective-permute-start | bytes 1179656 | tf_op jit(solution)/shard_map/ppermute | solution.py:32
  23.5 13.3 %collective-permute-start.1 = (bf16[4,128,512]{2,1,0:T(8,128)(2,1)S(1)}, bf16[4,128,512]{2,1,0:T(8,128)(2,1)S(1)}, u32[]{:S(2)}, u32[]{:S(2)}) collective-permute-start(bf16[4,128,512]{2,1,0:T(8,128)(2,1)S(1)} %broadcast_select_fusion), channel_id=1, source_target_pairs={{0,4},{4,0},{8,12},{12,8},{16,20},{20,16},{24,28},{28,24},{1,5},{5... | collective-permute-start | bytes 1572872 | tf_op jit(solution)/shard_map/ppermute | solution.py:32
  23.6 15.9 %collective-permute-start.5 = (bf16[3,128,512]{2,1,0:T(8,128)(2,1)S(1)}, bf16[3,128,512]{2,1,0:T(8,128)(2,1)S(1)}, u32[]{:S(2)}, u32[]{:S(2)}) collective-permute-start(bf16[3,128,512]{2,1,0:T(8,128)(2,1)S(1)} %get-tuple-element.22.refs_0_), channel_id=1, source_target_pairs={{0,4},{4,0},{8,12},{12,8},{16,20},{20,16},{24,28},{28,24},{1,5},{5... | collective-permute-start | bytes 1179656 | tf_op jit(solution)/shard_map/ppermute | solution.py:32
  30.9 8.6 %collective-permute-start.7 = (bf16[3,128,512]{2,1,0:T(8,128)(2,1)S(1)}, bf16[3,128,512]{2,1,0:T(8,128)(2,1)S(1)}, u32[]{:S(2)}, u32[]{:S(2)}) collective-permute-start(bf16[3,128,512]{2,1,0:T(8,128)(2,1)S(1)} %collective-permute-done.6.refs_2_), channel_id=1, source_target_pairs={{0,4},{4,0},{8,12},{12,8},{16,20},{20,16},{24,28},{28,24},{1,5},{5... | collective-permute-start | bytes 1179656 | tf_op jit(solution)/shard_map/ppermute | solution.py:32
  30.9 13.9 %collective-permute-start.10 = (bf16[256,256]{1,0:T(8,128)(2,1)S(1)}, bf16[256,256]{1,0:T(8,128)(2,1)S(1)}, u32[]{:S(2)}, u32[]{:S(2)}) collective-permute-start(bf16[256,256]{1,0:T(8,128)(2,1)S(1)} %get-tuple-element.25), channel_id=1, source_target_pairs={{0,3},{1,0},{2,1},{3,2},{4,7},{5,4},{6,5},{7,6},{8,11},{9,8},{10,9... | collective-permute-start | bytes 393224 | tf_op jit(solution)/shard_map/ppermute | solution.py:27
  33.4 15.9 %collective-permute-start.9 = (bf16[256,256]{1,0:T(8,128)(2,1)S(1)}, bf16[256,256]{1,0:T(8,128)(2,1)S(1)}, u32[]{:S(2)}, u32[]{:S(2)}) collective-permute-start(bf16[256,256]{1,0:T(8,128)(2,1)S(1)} %get-tuple-element.25), channel_id=1, source_target_pairs={{0,2},{1,3},{2,0},{3,1},{4,6},{5,7},{6,4},{7,5},{8,10},{9,11},{10,... | collective-permute-start | bytes 393224 | tf_op jit(solution)/shard_map/ppermute | solution.py:27
  36.8 12.6 %collective-permute-start.8 = (bf16[256,256]{1,0:T(8,128)(2,1)S(1)}, bf16[256,256]{1,0:T(8,128)(2,1)S(1)}, u32[]{:S(2)}, u32[]{:S(2)}) collective-permute-start(bf16[256,256]{1,0:T(8,128)(2,1)S(1)} %get-tuple-element.25), channel_id=1, source_target_pairs={{0,1},{1,2},{2,3},{3,0},{4,5},{5,6},{6,7},{7,4},{8,9},{9,10},{10,1... | collective-permute-start | bytes 393224 | tf_op jit(solution)/shard_map/ppermute | solution.py:27
  50.6 6.8 %collective-permute-start.14 = (bf16[3,128,256]{2,1,0:T(8,128)(2,1)S(1)}, bf16[3,128,256]{2,1,0:T(8,128)(2,1)S(1)}, u32[]{:S(2)}, u32[]{:S(2)}) collective-permute-start(bf16[3,128,256]{2,1,0:T(8,128)(2,1)S(1)} %get-tuple-element.31.refs_0_), channel_id=1, source_target_pairs={{0,8},{4,12},{8,0},{12,4},{16,24},{20,28},{24,16},{28,20},{1,9},{5... | collective-permute-start | bytes 589832 | tf_op jit(solution)/shard_map/ppermute | solution.py:32
  52.1 6.5 %collective-permute-start.15 = (bf16[3,128,256]{2,1,0:T(8,128)(2,1)S(1)}, bf16[3,128,256]{2,1,0:T(8,128)(2,1)S(1)}, u32[]{:S(2)}, u32[]{:S(2)}) collective-permute-start(bf16[3,128,256]{2,1,0:T(8,128)(2,1)S(1)} %get-tuple-element.32.refs_2_), channel_id=1, source_target_pairs={{0,16},{4,20},{8,24},{12,28},{16,0},{20,4},{24,8},{28,12},{1,17},{... | collective-permute-start | bytes 589832 | tf_op jit(solution)/shard_map/ppermute | solution.py:32
  58.6 17.3 %collective-permute-start.22 = (bf16[2,3,128,256]{3,2,1,0:T(8,128)(2,1)S(1)}, bf16[2,3,128,256]{3,2,1,0:T(8,128)(2,1)S(1)}, u32[]{:S(2)}, u32[]{:S(2)}) collective-permute-start(bf16[2,3,128,256]{3,2,1,0:T(8,128)(2,1)S(1)} %get-tuple-element.38.refs_8_), channel_id=1, source_target_pairs={{0,8},{4,12},{8,0},{12,4},{16,24},{20,28},{24,16},{28,20},{1,9},{5... | collective-permute-start | bytes 1179656 | tf_op jit(solution)/shard_map/ppermute | solution.py:32
  59.2 16.6 %collective-permute-start.19 = (bf16[2,3,128,256]{3,2,1,0:T(8,128)(2,1)S(1)}, bf16[2,3,128,256]{3,2,1,0:T(8,128)(2,1)S(1)}, u32[]{:S(2)}, u32[]{:S(2)}) collective-permute-start(bf16[2,3,128,256]{3,2,1,0:T(8,128)(2,1)S(1)} %get-tuple-element.33.refs_4_), channel_id=1, source_target_pairs={{0,16},{4,20},{8,24},{12,28},{16,0},{20,4},{24,8},{28,12},{1,17},{... | collective-permute-start | bytes 1179656 | tf_op jit(solution)/shard_map/ppermute | solution.py:32
  60.7 8.2 %collective-permute-start.11 = (bf16[512,128]{1,0:T(8,128)(2,1)S(1)}, bf16[512,128]{1,0:T(8,128)(2,1)S(1)}, u32[]{:S(2)}, u32[]{:S(2)}) collective-permute-start(bf16[512,128]{1,0:T(8,128)(2,1)S(1)} %get-tuple-element.28), channel_id=1, source_target_pairs={{0,1},{1,2},{2,3},{3,0},{4,5},{5,6},{6,7},{7,4},{8,9},{9,10},{10,1... | collective-permute-start | bytes 393224 | tf_op jit(solution)/shard_map/ppermute | solution.py:27
  60.7 11.2 %collective-permute-start.12 = (bf16[512,128]{1,0:T(8,128)(2,1)S(1)}, bf16[512,128]{1,0:T(8,128)(2,1)S(1)}, u32[]{:S(2)}, u32[]{:S(2)}) collective-permute-start(bf16[512,128]{1,0:T(8,128)(2,1)S(1)} %get-tuple-element.29), channel_id=1, source_target_pairs={{0,2},{1,3},{2,0},{3,1},{4,6},{5,7},{6,4},{7,5},{8,10},{9,11},{10,... | collective-permute-start | bytes 393224 | tf_op jit(solution)/shard_map/ppermute | solution.py:27
  60.7 11.2 %collective-permute-start.13 = (bf16[512,128]{1,0:T(8,128)(2,1)S(1)}, bf16[512,128]{1,0:T(8,128)(2,1)S(1)}, u32[]{:S(2)}, u32[]{:S(2)}) collective-permute-start(bf16[512,128]{1,0:T(8,128)(2,1)S(1)} %get-tuple-element.30), channel_id=1, source_target_pairs={{0,3},{1,0},{2,1},{3,2},{4,7},{5,4},{6,5},{7,6},{8,11},{9,8},{10,9... | collective-permute-start | bytes 393224 | tf_op jit(solution)/shard_map/ppermute | solution.py:27
  73.0 6.8 %collective-permute-start.16 = (bf16[512,128]{1,0:T(8,128)(2,1)S(1)}, bf16[512,128]{1,0:T(8,128)(2,1)S(1)}, u32[]{:S(2)}, u32[]{:S(2)}) collective-permute-start(bf16[512,128]{1,0:T(8,128)(2,1)S(1)} %get-tuple-element.35), channel_id=1, source_target_pairs={{0,1},{1,2},{2,3},{3,0},{4,5},{5,6},{6,7},{7,4},{8,9},{9,10},{10,1... | collective-permute-start | bytes 393224 | tf_op jit(solution)/shard_map/ppermute | solution.py:27
  75.4 18.0 %collective-permute-start.23 = (bf16[2,3,128,256]{3,2,1,0:T(8,128)(2,1)S(1)}, bf16[2,3,128,256]{3,2,1,0:T(8,128)(2,1)S(1)}, u32[]{:S(2)}, u32[]{:S(2)}) collective-permute-start(bf16[2,3,128,256]{3,2,1,0:T(8,128)(2,1)S(1)} %get-tuple-element.38.refs_8_), channel_id=1, source_target_pairs={{0,4},{4,0},{8,12},{12,8},{16,20},{20,16},{24,28},{28,24},{1,5},{5... | collective-permute-start | bytes 1179656 | tf_op jit(solution)/shard_map/ppermute | solution.py:32
  75.4 18.0 %collective-permute-start.20 = (bf16[2,3,128,256]{3,2,1,0:T(8,128)(2,1)S(1)}, bf16[2,3,128,256]{3,2,1,0:T(8,128)(2,1)S(1)}, u32[]{:S(2)}, u32[]{:S(2)}) collective-permute-start(bf16[2,3,128,256]{3,2,1,0:T(8,128)(2,1)S(1)} %get-tuple-element.33.refs_4_), channel_id=1, source_target_pairs={{0,4},{4,0},{8,12},{12,8},{16,20},{20,16},{24,28},{28,24},{1,5},{5... | collective-permute-start | bytes 1179656 | tf_op jit(solution)/shard_map/ppermute | solution.py:32
  75.9 17.5 %collective-permute-start.24 = (bf16[2,3,128,256]{3,2,1,0:T(8,128)(2,1)S(1)}, bf16[2,3,128,256]{3,2,1,0:T(8,128)(2,1)S(1)}, u32[]{:S(2)}, u32[]{:S(2)}) collective-permute-start(bf16[2,3,128,256]{3,2,1,0:T(8,128)(2,1)S(1)} %collective-permute-done.22.refs_9_), channel_id=1, source_target_pairs={{0,4},{4,0},{8,12},{12,8},{16,20},{20,16},{24,28},{28,24},{1,5},{5... | collective-permute-start | bytes 1179656 | tf_op jit(solution)/shard_map/ppermute | solution.py:32
  75.9 17.5 %collective-permute-start.21 = (bf16[2,3,128,256]{3,2,1,0:T(8,128)(2,1)S(1)}, bf16[2,3,128,256]{3,2,1,0:T(8,128)(2,1)S(1)}, u32[]{:S(2)}, u32[]{:S(2)}) collective-permute-start(bf16[2,3,128,256]{3,2,1,0:T(8,128)(2,1)S(1)} %collective-permute-done.19.refs_5_), channel_id=1, source_target_pairs={{0,4},{4,0},{8,12},{12,8},{16,20},{20,16},{24,28},{28,24},{1,5},{5... | collective-permute-start | bytes 1179656 | tf_op jit(solution)/shard_map/ppermute | solution.py:32
  79.8 8.5 %collective-permute-start.17 = (bf16[512,128]{1,0:T(8,128)(2,1)S(1)}, bf16[512,128]{1,0:T(8,128)(2,1)S(1)}, u32[]{:S(2)}, u32[]{:S(2)}) collective-permute-start(bf16[512,128]{1,0:T(8,128)(2,1)S(1)} %get-tuple-element.36), channel_id=1, source_target_pairs={{0,2},{1,3},{2,0},{3,1},{4,6},{5,7},{6,4},{7,5},{8,10},{9,11},{10,... | collective-permute-start | bytes 393224 | tf_op jit(solution)/shard_map/ppermute | solution.py:27
  (15 other events, 289.6 us)

commit v7 on v6

--- a/solution.py
+++ b/solution.py
@@ -9,8 +9,8 @@
 
 HEADS = 4
 SPREAD = 8
-IN_BITS = ((0, 2), (4, 6), (1, 3), (5, 7))
-OUT_BITS = ((0, 4), (2, 6), (1, 5), (3, 7))
+IN_BITS = (0, 2, 4, 6)
+OUT_BITS = (0, 4, 2, 6)
 LANES = 128
 F32 = jnp.float32
 BF16 = jnp.bfloat16
@@ -38,7 +38,8 @@
 
 
 def quarter_of(block):
-    return lax.rem(block, 2) + 2 * lax.rem(lax.div(block, 4), 2)
+    parity = lax.rem(lax.div(block, 2) + lax.div(block, 4), 2)
+    return lax.rem(block, 2) + 2 * parity
 
 
 def row_sum(value):
@@ -55,40 +56,30 @@
             normed[row : row + zone_rows, :] = rms_scale(block[step].astype(F32), gain).astype(BF16)
 
 
-def pack_kernel(place, own_in, own_out, *refs):
-    arrived, (stacked, packed, sems) = refs[:-3], refs[-3:]
-    in_shard, hidden = own_in.shape
-    out_shard, width = own_out.shape
-    in_cols, out_rows = hidden // SPREAD, out_shard // SPREAD
-    slot = lax.rem(place[0], SPREAD)
-    cols = pl.ds(pl.multiple_of(slot * in_cols, in_cols), in_cols)
-    rows = pl.ds(pl.multiple_of(slot * out_rows, out_rows), out_rows)
-    copies = [pltpu.make_async_copy(own_in.at[:, cols], packed.at[:in_shard, :], sems.at[0])]
-    for fold in range(width // in_cols):
-        first = in_shard + fold * out_rows
-        copies.append(
-            pltpu.make_async_copy(
-                own_out.at[rows, fold * in_cols : (fold + 1) * in_cols],
-                packed.at[first : first + out_rows, :],
-                sems.at[1 + fold],
-            )
-        )
-    for copy in copies:
-        copy.start()
+def split_kernel(packed, before, *refs):
+    arrived, (upper, lower, packed_out) = refs[:-3], refs[-3:]
+    half = upper.shape[1]
     for index, piece in enumerate(arrived):
-        stacked[index] = piece[...]
-    for copy in copies:
-        copy.wait()
-
-
-def pair_kernel(*refs):
-    ins, outs = refs[:4], refs[4:]
-    for index, value in enumerate(ins):
-        outs[index // 2][index % 2] = value[...]
+        upper[index] = piece[:half, :]
+        lower[index] = piece[half:, :]
+    packed_out[...] = packed[...]
+
+
+def gather_kernel(place, states, before, upper, lower, over_x, over_y, *refs):
+    across, (quarters, last, first_out, second_out) = refs[:-4], refs[-4:]
+    half = upper.shape[1]
+    for index, (top, bottom) in enumerate(((upper, lower), (over_x, over_y))):
+        quarters[index, :, :half, :] = top[...]
+        quarters[index, :, half:, :] = bottom[...]
+    last[...] = jnp.where(lax.rem(place[0], 2) == 1, before[...], states[...])
+    split = first_out.shape[1]
+    for index, piece in enumerate(across):
+        first_out[index] = piece[:split, :]
+        second_out[index] = piece[split:, :]
 
 
 def attention_kernel(zones, reach, steps, place, pattern, normed, own_qkv, own_attn, *refs):
-    pieces, (context_out, attn_out, weights, w_turned, projected, context, sems) = refs[:-7], refs[-7:]
+    quarters, (context_out, attn_out, weights, w_turned, projected, context, sems) = refs[:-7], refs[-7:]
     key_count = (reach + 1) * steps
     zone_rows = normed.shape[0] // key_count
     width = normed.shape[1]
@@ -112,8 +103,9 @@
     for step in range(1, zones):
         source = lax.rem(my_zone - step + zones, zones)
         rows = pl.ds(pl.multiple_of(source * shard, shard), shard)
-        for bits, piece in enumerate(pieces):
-            weights[my_quarter ^ bits, rows, :] = piece[step - 1]
+        for core, pair in enumerate(quarters):
+            for index in range(2):
+                weights[my_quarter ^ (core + 2 * index), rows, :] = pair[index, step - 1]
     for copy in copies:
         copy.wait()
     attn_out[...] = weights[3]
@@ -200,14 +192,11 @@
 
 
 def project_kernel(place, states, context, w_attn, gain_mix, *refs):
-    parts = refs[-1]
+    halves, (after_out, *outs, pair_in, pair_out, parts) = refs[:4], refs[4:]
     steps, zone_rows, _ = states.shape
     zones, _, part = parts.shape
-    across, (after_out, *outs, first_out, second_out) = refs[: zones - 1], refs[zones - 1 : -1]
-    split = first_out.shape[1]
-    for index, piece in enumerate(across):
-        first_out[index] = piece[:split, :]
-        second_out[index] = piece[split:, :]
+    for index, value in enumerate(halves):
+        (pair_in, pair_out)[index // 2][index % 2] = value[...]
     my_zone = place[1]
     gain = gain_mix[...]
     for step in range(steps):
@@ -224,7 +213,9 @@
 
 
 def mixing_kernel(steps, zones, place, neighbours, degree, mix, *refs):
-    arrived, outs, items = refs[:zones], refs[-1 - zones : -1], refs[-1]
+    arrived, pairs, (*outs, gathered, items) = refs[:zones], refs[zones : zones + 4], refs[zones + 4 :]
+    for index, pair in enumerate(pairs):
+        gathered[2 * index : 2 * index + 2] = pair[...]
     _, slots, zone_rows, _ = mix.shape
     part = items.shape[-1]
     my_zone = place[1]
@@ -258,10 +249,9 @@
                 outs[target][rows, :] = result[:, index * part : (index + 1) * part].astype(BF16)
 
 
-def ffn_kernel(zones, place, after_attn, gain_ffn, own_in, own_out, *refs):
-    arrived, refs = refs[:zones], refs[zones:]
-    pieces, (out, w_in, w_out, after_mix, ffn_in, parts, sems) = refs[:-7], refs[-7:]
-    rows_all, width = after_attn.shape
+def order_kernel(zones, place, own_in, own_out, *refs):
+    gathered, (w_in, w_out, sems) = refs[:2], refs[2:]
+    width = own_out.shape[1]
     my_block, my_zone = place[0], place[1]
     in_shard, hidden = own_in.shape
     out_shard = own_out.shape[0]
@@ -280,27 +270,30 @@
     copies.append(pltpu.make_async_copy(own_out, w_out.at[own_rows, :], sems.at[SPREAD]))
     for copy in copies:
         copy.start()
-    for step in range(zones):
-        parts[lax.rem(my_zone - step + zones, zones)] = arrived[step][...]
-    for piece, bits_pair in zip(pieces[:4], IN_BITS):
-        for index, bits in enumerate(bits_pair):
-            slot = lax.rem(my_block, SPREAD) ^ bits
+    for core, pieces in enumerate(gathered):
+        for index in range(4):
+            slot_in = lax.rem(my_block, SPREAD) ^ (IN_BITS[index] + core)
+            slot_out = lax.rem(my_block, SPREAD) ^ (OUT_BITS[index] + core)
             for step in range(1, zones):
                 source = lax.rem(my_zone - step + zones, zones)
                 rows = pl.ds(pl.multiple_of(source * in_shard, in_shard), in_shard)
-                w_in[slot, rows, :] = piece[index, step - 1]
-    for piece, bits_pair in zip(pieces[4:], OUT_BITS):
-        for index, bits in enumerate(bits_pair):
-            slot = lax.rem(my_block, SPREAD) ^ bits
-            for step in range(1, zones):
-                source = lax.rem(my_zone - step + zones, zones)
-                first = pl.multiple_of(source * out_shard + slot * out_rows, out_rows)
+                w_in[slot_in, rows, :] = pieces[index, step - 1]
+                first = pl.multiple_of(source * out_shard + slot_out * out_rows, out_rows)
                 for fold in range(width // in_cols):
                     cols = slice(fold * in_cols, (fold + 1) * in_cols)
                     rows = slice(fold * out_rows, (fold + 1) * out_rows)
-                    w_out[pl.ds(first, out_rows), cols] = piece[index, step - 1, rows, :]
+                    w_out[pl.ds(first, out_rows), cols] = pieces[4 + index, step - 1, rows, :]
     for copy in copies:
         copy.wait()
+
+
+def ffn_kernel(zones, place, after_attn, gain_ffn, w_in, w_out, *refs):
+    arrived, (out, after_mix, ffn_in, parts) = refs[:zones], refs[zones:]
+    rows_all, width = after_attn.shape
+    my_zone = place[1]
+    in_cols = w_in.shape[2]
+    for step in range(zones):
+        parts[lax.rem(my_zone - step + zones, zones)] = arrived[step][...]
 
     gain = gain_ffn[...]
     span = 128
@@ -373,33 +366,50 @@
         jnp.concatenate([w_qkv, w_out_attn], axis=1), quarter_of(my_block) * width, width, axis=1
     )
     direct = [rotated(first, "zone", step) for step in rotations]
+    slot = my_block % SPREAD
+    slice_in = lax.dynamic_slice_in_dim(w_in, slot * in_cols, in_cols, axis=1)
+    slice_out = lax.dynamic_slice_in_dim(w_out, slot * out_rows, out_rows, axis=0)
     in_shard = w_in.shape[0]
     sizes = (in_shard, out_rows * (width // in_cols))
-    packed_shape = (sum(sizes), in_cols)
-    direct, packed = call(
-        pack_kernel,
+    packed = jnp.concatenate(
+        [slice_in] + [slice_out[:, at : at + in_cols] for at in range(0, width, in_cols)], axis=0
+    )
+    half = first.shape[0] // 2
+    half_shape = jax.ShapeDtypeStruct((zones - 1, half, width), BF16)
+    upper, lower, packed = call(
+        split_kernel,
+        (half_shape, half_shape, jax.ShapeDtypeStruct(packed.shape, BF16)),
+        [],
+        (),
+        (),
+        4,
+        [packed, before] + direct,
+    )
+    over_x, over_y = swapped(upper, "tm", 2), swapped(lower, "tm", 4)
+    across = [rotated(packed, "zone", step) for step in rotations]
+    quarters, last, part_in, part_out = call(
+        gather_kernel,
         (
-            jax.ShapeDtypeStruct((zones - 1,) + first.shape, BF16),
-            jax.ShapeDtypeStruct(packed_shape, BF16),
-        ),
-        [pltpu.SemaphoreType.DMA((1 + width // in_cols,))],
+            jax.ShapeDtypeStruct((2, zones - 1) + first.shape, BF16),
+            jax.ShapeDtypeStruct(states.shape, BF16),
+        )
+        + tuple(jax.ShapeDtypeStruct((zones - 1, size, in_cols), BF16) for size in sizes),
+        [],
         (0,),
-        (1, 2),
-        8,
-        [place, w_in, w_out] + direct,
-    )
-    over = swapped(direct, "tm", 4)
-    quarters = [direct, swapped(direct, "tm", 1), over, swapped(over, "tm", 1)]
-    across = [rotated(packed, "zone", step) for step in rotations]
-
-    last = swapped(jnp.where(my_block % 2 == 1, before, states), "tm", 1)
+        (),
+        4,
+        [place, states, before, upper, lower, over_x, over_y] + across,
+    )
+    quarters = [quarters, swapped(quarters, "tm", 1)]
+    last = swapped(last, "tm", 1)
+    over_in, over_out = swapped(part_in, "tm", 2), swapped(part_out, "tm", 4)
     normed = call(
         norm_kernel,
         jax.ShapeDtypeStruct((key_count * zone_rows, width), BF16),
         [],
         (),
         (),
-        8,
+        4,
         [before, last, states, gain_attn.reshape(1, -1)],
     )
 
@@ -423,61 +433,57 @@
     )
 
     chunk = jax.ShapeDtypeStruct((rows, part), BF16)
-    after_attn, *chunks, part_in, part_out = call(
+    after_attn, *chunks, pair_in, pair_out = call(
         project_kernel,
         (jax.ShapeDtypeStruct((rows, width), F32),)
         + (chunk,) * zones
-        + tuple(jax.ShapeDtypeStruct((zones - 1, size, in_cols), BF16) for size in sizes),
+        + tuple(jax.ShapeDtypeStruct((2, zones - 1, size, in_cols), BF16) for size in sizes),
         [pltpu.VMEM((zones, rows, part), BF16)],
         (0,),
         (),
         8,
-        [place, states, context, w_attn, gain_mix.reshape(1, -1)] + across,
+        [place, states, context, w_attn, gain_mix.reshape(1, -1)]
+        + [part_in, over_in, part_out, over_out],
     )
     arrived = [chunks[0]] + [rotated(chunks[step], "zone", step) for step in rotations]
 
-    over_in, over_out = swapped(part_in, "tm", 2), swapped(part_out, "tm", 4)
-    pair_in, pair_out = call(
-        pair_kernel,
-        tuple(jax.ShapeDtypeStruct((2,) + value.shape, BF16) for value in (part_in, part_out)),
-        [],
-        (),
-        (),
-        8,
-        [part_in, over_in, part_out, over_out],
-    )
-    pieces_in = [pair_in, swapped(pair_in, "tm", 4)]
-    pieces_out = [pair_out, swapped(pair_out, "tm", 2)]
-    pieces = pieces_in + [swapped(value, "tm", 1) for value in pieces_in]
-    pieces += pieces_out + [swapped(value, "tm", 1) for value in pieces_out]
-
-    spatial = call(
+    pairs = [pair_in, swapped(pair_in, "tm", 4), pair_out, swapped(pair_out, "tm", 2)]
+
+    *spatial, gathered = call(
         functools.partial(mixing_kernel, steps, zones),
-        (chunk,) * zones,
+        (chunk,) * zones
+        + (jax.ShapeDtypeStruct((SPREAD, zones - 1, in_shard, in_cols), BF16),),
         [pltpu.VMEM((zones, rows, part), BF16)],
         (0, 1, 2),
         (),
         8,
-        [place, neighbours, degree, mix] + arrived + [pair_in],
+        [place, neighbours, degree, mix] + arrived + pairs,
+    )
+    full_in, full_out = call(
+        functools.partial(order_kernel, zones),
+        (
+            jax.ShapeDtypeStruct((SPREAD, width, in_cols), BF16),
+            jax.ShapeDtypeStruct((hidden, width), BF16),
+        ),
+        [pltpu.SemaphoreType.DMA((SPREAD + 1,))],
+        (0,),
+        (1, 2),
+        8,
+        [place, w_in, w_out, gathered, swapped(gathered, "tm", 1)],
     )
     arrived = [spatial[0]] + [rotated(spatial[step], "zone", step) for step in rotations]
     evolved = call(
         functools.partial(ffn_kernel, zones),
         jax.ShapeDtypeStruct((rows, width), BF16),
         [
-            pltpu.VMEM((SPREAD, width, in_cols), BF16),
-            pltpu.VMEM((hidden, width), BF16),
             pltpu.VMEM((rows, width), F32),
             pltpu.VMEM((rows, width), BF16),
             pltpu.VMEM((zones, rows, part), BF16),
-            pltpu.SemaphoreType.DMA((SPREAD + 1,)),
         ],
         (0,),
-        (3, 4),
-        16,
-        [place, after_attn, gain_ffn.reshape(1, -1), w_in, w_out]
-        + arrived
-        + pieces,
+        (),
+        10,
+        [place, after_attn, gain_ffn.reshape(1, -1), full_in, full_out] + arrived,
     )
     return evolved.reshape(steps, zone_rows, width)
 

time: 98.2 us -> 82.1 us (0.84)
  waiting for transfers between devices: 48.4 us -> 31.1 us
    ppermute x12 -> x9, waiting for transfers between devices: 13 us -> 0.34 us  [swapped(): lax.ppermute(value, axis, [(source, source ^ bits) for source in range(co...]
    ppermute x12, waiting for transfers between devices: 35.4 us -> 30.8 us  [rotated(): lax.ppermute(value, axis, [(source, (source + steps) % count) for source...]
    unnamed x28 -> x24, local copies, waits for them, and re-layouts: 2.49 us -> 0.42 us
    pallas_call x7 -> x8, Pallas kernels: 13 us -> 13.9 us  [call(): pl.pallas_call(kernel, out_shape=out_shape, in_specs=[pl.BlockSpec(memory...]
    ppermute x12 -> x9, starting transfers between devices: 7.07 us -> 6.74 us  [swapped(): lax.ppermute(value, axis, [(source, source ^ bits) for source in range(co...]
  transfers between devices with their start and end apart: 25 -> 22, of which waited for: 11 -> 9; matrix products, arithmetic and copies ran while one was open for 1% -> 3% of each run, Pallas kernels for 7% -> 8%
where the time goes in v7:
time: 82.1 us; the launch traced here: 81.3 us
  starting transfers between devices  32.9 us (40%)
  waiting for transfers between devices  31.1 us (38%)
  Pallas kernels  13.9 us (17%)
  local copies, waits for them, and re-layouts  2.04 us (2%)
  other arithmetic  1.05 us (1%)
    ppermute x12, waiting for transfers between devices, rotated(): lax.ppermute(value, axis, [(source, (source + steps) % count) for source...  30.8 us
    ppermute x12, starting transfers between devices, rotated(): lax.ppermute(value, axis, [(source, (source + steps) % count) for source...  21.2 us
    pallas_call x8, Pallas kernels, call(): pl.pallas_call(kernel, out_shape=out_shape, in_specs=[pl.BlockSpec(memory...  13.9 us
    ppermute x9, starting transfers between devices, swapped(): lax.ppermute(value, axis, [(source, source ^ bits) for source in range(co...  6.74 us
    ppermute x1, starting transfers between devices, shifted(): lax.ppermute(value, axis, [(source, source + steps) for source in range(c...  4.99 us
  transfers between devices with their start and end apart: 22, of which 9 were waited for; matrix products, arithmetic and copies ran while one was open for 3% of the time, Pallas kernels for 8%

profile of v7, /device:TPU:0, one launch (start us, length us, event | category | flops | bytes accessed | tf_op | source)
XLA Modules:
  0.0 81.3 jit_solution(1689710278179548745)
XLA Ops:
  0.0 5.0 %collective-permute-start = (bf16[4,128,512]{2,1,0:T(8,128)(2,1)}, bf16[4,128,512]{2,1,0:T(8,128)(2,1)S(1)}, u32[]{:S(2)}, u32[]{:S(2)}) collective-permute-start(bf16[4,128,512]{2,1,0:T(8,128)(2,1)} %states.3), channel_id=1, source_target_pairs={{0,8},{4,12},{8,16},{12,20},{16,24},{20,28},{1,9},{5,13},{9,17},{1... | collective-permute-start | bytes 1572872 | tf_op jit(solution)/shard_map/ppermute | solution.py:22
  6.0 2.7 %collective-permute-start.2 = (bf16[128,512]{1,0:T(8,128)(2,1)S(1)}, bf16[128,512]{1,0:T(8,128)(2,1)S(1)}, u32[]{:S(2)}, u32[]{:S(2)}) collective-permute-start(bf16[128,512]{1,0:T(8,128)(2,1)S(1)} %fusion), channel_id=1, source_target_pairs={{0,2},{1,3},{2,0},{3,1},{4,6},{5,7},{6,4},{7,5},{8,10},{9,11},{10,... | collective-permute-start | bytes 393224 | tf_op jit(solution)/shard_map/ppermute | solution.py:27
  8.7 1.6 %collective-permute-start.1 = (bf16[128,512]{1,0:T(8,128)(2,1)S(1)}, bf16[128,512]{1,0:T(8,128)(2,1)S(1)}, u32[]{:S(2)}, u32[]{:S(2)}) collective-permute-start(bf16[128,512]{1,0:T(8,128)(2,1)S(1)} %fusion), channel_id=1, source_target_pairs={{0,1},{1,2},{2,3},{3,0},{4,5},{5,6},{6,7},{7,4},{8,9},{9,10},{10,1... | collective-permute-start | bytes 393224 | tf_op jit(solution)/shard_map/ppermute | solution.py:27
  10.2 2.2 %collective-permute-start.3 = (bf16[128,512]{1,0:T(8,128)(2,1)S(1)}, bf16[128,512]{1,0:T(8,128)(2,1)S(1)}, u32[]{:S(2)}, u32[]{:S(2)}) collective-permute-start(bf16[128,512]{1,0:T(8,128)(2,1)S(1)} %fusion), channel_id=1, source_target_pairs={{0,3},{1,0},{2,1},{3,2},{4,7},{5,4},{6,5},{7,6},{8,11},{9,8},{10,9... | collective-permute-start | bytes 393224 | tf_op jit(solution)/shard_map/ppermute | solution.py:27
  14.1 4.6 %collective-permute-done.2.refs_1_ = bf16[128,512]{1,0:T(8,128)(2,1)S(1)} collective-permute-done((bf16[128,512]{1,0:T(8,128)(2,1)S(1)}, bf16[128,512]{1,0:T(8,128)(2,1)S(1)}, u32[]{:S(2)}, u32[]{:S(2)}) %collective-permute-start.2) | collective-permute-done | bytes 131104 | tf_op jit(solution)/shard_map/ppermute | solution.py:27
  19.2 1.5 %collective-permute-start.4 = (bf16[3,64,512]{2,1,0:T(8,128)(2,1)S(1)}, bf16[3,64,512]{2,1,0:T(8,128)(2,1)S(1)}, u32[]{:S(2)}, u32[]{:S(2)}) collective-permute-start(bf16[3,64,512]{2,1,0:T(8,128)(2,1)S(1)} %get-tuple-element.28.upper), channel_id=1, source_target_pairs={{0,8},{4,12},{8,0},{12,4},{16,24},{20,28},{24,16},{28,20},{1,9},{5... | collective-permute-start | bytes 589832 | tf_op jit(solution)/shard_map/ppermute | solution.py:32
  20.8 3.2 %collective-permute-start.8 = (bf16[256,256]{1,0:T(8,128)(2,1)S(1)}, bf16[256,256]{1,0:T(8,128)(2,1)S(1)}, u32[]{:S(2)}, u32[]{:S(2)}) collective-permute-start(bf16[256,256]{1,0:T(8,128)(2,1)S(1)} %get-tuple-element.30), channel_id=1, source_target_pairs={{0,3},{1,0},{2,1},{3,2},{4,7},{5,4},{6,5},{7,6},{8,11},{9,8},{10,9... | collective-permute-start | bytes 393224 | tf_op jit(solution)/shard_map/ppermute | solution.py:27
  24.6 2.0 %collective-permute-start.6 = (bf16[256,256]{1,0:T(8,128)(2,1)S(1)}, bf16[256,256]{1,0:T(8,128)(2,1)S(1)}, u32[]{:S(2)}, u32[]{:S(2)}) collective-permute-start(bf16[256,256]{1,0:T(8,128)(2,1)S(1)} %get-tuple-element.30), channel_id=1, source_target_pairs={{0,1},{1,2},{2,3},{3,0},{4,5},{5,6},{6,7},{7,4},{8,9},{9,10},{10,1... | collective-permute-start | bytes 393224 | tf_op jit(solution)/shard_map/ppermute | solution.py:27
  26.7 1.2 %collective-permute-done.8.refs_2_ = bf16[256,256]{1,0:T(8,128)(2,1)S(1)} collective-permute-done((bf16[256,256]{1,0:T(8,128)(2,1)S(1)}, bf16[256,256]{1,0:T(8,128)(2,1)S(1)}, u32[]{:S(2)}, u32[]{:S(2)}) %collective-permute-start.8) | collective-permute-done | bytes 131104 | tf_op jit(solution)/shard_map/ppermute | solution.py:27
  27.9 8.5 %collective-permute-done.7.refs_1_ = bf16[256,256]{1,0:T(8,128)(2,1)S(1)} collective-permute-done((bf16[256,256]{1,0:T(8,128)(2,1)S(1)}, bf16[256,256]{1,0:T(8,128)(2,1)S(1)}, u32[]{:S(2)}, u32[]{:S(2)}) %collective-permute-start.7) | collective-permute-done | bytes 131104 | tf_op jit(solution)/shard_map/ppermute | solution.py:27
  37.7 1.7 %collective-permute-start.11 = (bf16[3,128,256]{2,1,0:T(8,128)(2,1)S(1)}, bf16[3,128,256]{2,1,0:T(8,128)(2,1)S(1)}, u32[]{:S(2)}, u32[]{:S(2)}) collective-permute-start(bf16[3,128,256]{2,1,0:T(8,128)(2,1)S(1)} %get-tuple-element.35.refs_0_), channel_id=1, source_target_pairs={{0,8},{4,12},{8,0},{12,4},{16,24},{20,28},{24,16},{28,20},{1,9},{5... | collective-permute-start | bytes 589832 | tf_op jit(solution)/shard_map/ppermute | solution.py:32
  41.3 5.0 %shard_map.121 = (bf16[512,512]{1,0:T(8,128)(2,1)S(1)}, bf16[512,512]{1,0:T(8,128)(2,1)S(1)}) custom-call(s32[2]{0:T(128)S(1)} %pad_add_fusion.place, s32[1,2]{1,0:T(1,128)S(1)} %copy-done.10, bf16[1536,512]{1,0:T(8,128)(2,1)S(1)} %shard_map.120.normed, bf16[128,1536]{1,0:T(8,128)(2,1)S(1)} %copy-done.1, bf16[128,512]{1,0:T(8,128)(2,1)S(1)} %copy-done.4, ...), custom_call_target="tpu_custom_call" | custom-call | tf_op jit(solution)/shard_map/pallas_call | solution.py:324
  46.3 1.2 %shard_map.122 = (f32[512,512]{1,0:T(8,128)S(1)}, bf16[512,128]{1,0:T(8,128)(2,1)S(1)}, bf16[512,128]{1,0:T(8,128)(2,1)S(1)}, bf16[512,128]{1,0:T(8,128)(2,1)S(1...) custom-call(s32[2]{0:T(128)S(1)} %pad_add_fusion.place, ...), custom_call_target="tpu_custom_call" | custom-call | tf_op jit(solution)/shard_map/pallas_call | solution.py:324
  47.6 1.7 %collective-permute-start.16 = (bf16[2,3,128,256]{3,2,1,0:T(8,128)(2,1)S(1)}, bf16[2,3,128,256]{3,2,1,0:T(8,128)(2,1)S(1)}, u32[]{:S(2)}, u32[]{:S(2)}) collective-permute-start(bf16[2,3,128,256]{3,2,1,0:T(8,128)(2,1)S(1)} %get-tuple-element.42.refs_4_), channel_id=1, source_target_pairs={{0,16},{4,20},{8,24},{12,28},{16,0},{20,4},{24,8},{28,12},{1,17},{... | collective-permute-start | bytes 1179656 | tf_op jit(solution)/shard_map/ppermute | solution.py:32
  51.0 2.9 %collective-permute-start.15 = (bf16[512,128]{1,0:T(8,128)(2,1)S(1)}, bf16[512,128]{1,0:T(8,128)(2,1)S(1)}, u32[]{:S(2)}, u32[]{:S(2)}) collective-permute-start(bf16[512,128]{1,0:T(8,128)(2,1)S(1)} %get-tuple-element.41), channel_id=1, source_target_pairs={{0,3},{1,0},{2,1},{3,2},{4,7},{5,4},{6,5},{7,6},{8,11},{9,8},{10,9... | collective-permute-start | bytes 393224 | tf_op jit(solution)/shard_map/ppermute | solution.py:27
  53.9 4.2 %collective-permute-done.13.refs_1_ = bf16[512,128]{1,0:T(8,128)(2,1)S(1)} collective-permute-done((bf16[512,128]{1,0:T(8,128)(2,1)S(1)}, bf16[512,128]{1,0:T(8,128)(2,1)S(1)}, u32[]{:S(2)}, u32[]{:S(2)}) %collective-permute-start.13) | collective-permute-done | bytes 131104 | tf_op jit(solution)/shard_map/ppermute | solution.py:27
  58.1 4.3 %collective-permute-done.14.refs_2_ = bf16[512,128]{1,0:T(8,128)(2,1)S(1)} collective-permute-done((bf16[512,128]{1,0:T(8,128)(2,1)S(1)}, bf16[512,128]{1,0:T(8,128)(2,1)S(1)}, u32[]{:S(2)}, u32[]{:S(2)}) %collective-permute-start.14) | collective-permute-done | bytes 131104 | tf_op jit(solution)/shard_map/ppermute | solution.py:27
  62.4 1.2 %shard_map.123 = (bf16[512,128]{1,0:T(8,128)(2,1)S(1)}, bf16[512,128]{1,0:T(8,128)(2,1)S(1)}, bf16[512,128]{1,0:T(8,128)(2,1)S(1)}, bf16[512,128]{1,0:T(8,128)(2,1)S(1)}, bf16[8,3,128,256]{3,2,1,0:T(8,128)(2,1)S(1)}) custom-call(s32[2]{0:T(128)S(1)} %pad_add_fusion.place, s32[4,3]{1,0:T(4,128)S(1)} %copy-done.9, s32[4]{0:T(128)S(1)} %copy-done.11, ...), custom_call_target="tpu_custom_call" | custom-call | tf_op jit(solution)/shard_map/pallas_call | solution.py:324
  63.7 2.4 %collective-permute-start.19 = (bf16[512,128]{1,0:T(8,128)(2,1)S(1)}, bf16[512,128]{1,0:T(8,128)(2,1)S(1)}, u32[]{:S(2)}, u32[]{:S(2)}) collective-permute-start(bf16[512,128]{1,0:T(8,128)(2,1)S(1)} %get-tuple-element.48), channel_id=1, source_target_pairs={{0,1},{1,2},{2,3},{3,0},{4,5},{5,6},{6,7},{7,4},{8,9},{9,10},{10,1... | collective-permute-start | bytes 393224 | tf_op jit(solution)/shard_map/ppermute | solution.py:27
  66.0 1.1 %collective-permute-start.20 = (bf16[512,128]{1,0:T(8,128)(2,1)S(1)}, bf16[512,128]{1,0:T(8,128)(2,1)S(1)}, u32[]{:S(2)}, u32[]{:S(2)}) collective-permute-start(bf16[512,128]{1,0:T(8,128)(2,1)S(1)} %get-tuple-element.49), channel_id=1, source_target_pairs={{0,2},{1,3},{2,0},{3,1},{4,6},{5,7},{6,4},{7,5},{8,10},{9,11},{10,... | collective-permute-start | bytes 393224 | tf_op jit(solution)/shard_map/ppermute | solution.py:27
  67.2 1.3 %collective-permute-start.21 = (bf16[512,128]{1,0:T(8,128)(2,1)S(1)}, bf16[512,128]{1,0:T(8,128)(2,1)S(1)}, u32[]{:S(2)}, u32[]{:S(2)}) collective-permute-start(bf16[512,128]{1,0:T(8,128)(2,1)S(1)} %get-tuple-element.50), channel_id=1, source_target_pairs={{0,3},{1,0},{2,1},{3,2},{4,7},{5,4},{6,5},{7,6},{8,11},{9,8},{10,9... | collective-permute-start | bytes 393224 | tf_op jit(solution)/shard_map/ppermute | solution.py:27
  69.5 2.4 %collective-permute-done.19.refs_1_ = bf16[512,128]{1,0:T(8,128)(2,1)S(1)} collective-permute-done((bf16[512,128]{1,0:T(8,128)(2,1)S(1)}, bf16[512,128]{1,0:T(8,128)(2,1)S(1)}, u32[]{:S(2)}, u32[]{:S(2)}) %collective-permute-start.19) | collective-permute-done | bytes 131104 | tf_op jit(solution)/shard_map/ppermute | solution.py:27
  71.9 5.1 %collective-permute-done.20.refs_2_ = bf16[512,128]{1,0:T(8,128)(2,1)S(1)} collective-permute-done((bf16[512,128]{1,0:T(8,128)(2,1)S(1)}, bf16[512,128]{1,0:T(8,128)(2,1)S(1)}, u32[]{:S(2)}, u32[]{:S(2)}) %collective-permute-start.20) | collective-permute-done | bytes 131104 | tf_op jit(solution)/shard_map/ppermute | solution.py:27
  77.1 4.2 %shard_map.125 = bf16[512,512]{1,0:T(8,128)(2,1)} custom-call(s32[2]{0:T(128)S(1)} %pad_add_fusion.place, f32[512,512]{1,0:T(8,128)S(1)} %get-tuple-element.37.after_attn, f32[1,512]{1,0:T(1,128)S(1)} %bitcast.6, bf16[8,512,256]{2,1,0:T(8,128)(2,1)S(1)} %get-tuple-element.45.w_in, bf16[2048,512]{1,0:T(8,128)(2,1)S(1)} %get-tuple-element.46.w_out, ...), custom_call_target="tpu_custom_call" | custom-call | tf_op jit(solution)/shard_map/pallas_call | solution.py:324
  (57 shorter events, 9.7 us)
Async XLA Ops:
  0.0 36.5 %copy-start = (bf16[4,128,512]{2,1,0:T(8,128)(2,1)S(1)}, bf16[4,128,512]{2,1,0:T(8,128)(2,1)}, u32[]{:S(2)}) copy-start(bf16[4,128,512]{2,1,0:T(8,128)(2,1)} %states.3) | copy-start | bytes 1572868
  0.0 19.1 %collective-permute-start = (bf16[4,128,512]{2,1,0:T(8,128)(2,1)}, bf16[4,128,512]{2,1,0:T(8,128)(2,1)S(1)}, u32[]{:S(2)}, u32[]{:S(2)}) collective-permute-start(bf16[4,128,512]{2,1,0:T(8,128)(2,1)} %states.3), channel_id=1, source_target_pairs={{0,8},{4,12},{8,16},{12,20},{16,24},{20,28},{1,9},{5,13},{9,17},{1... | collective-permute-start | bytes 1572872 | tf_op jit(solution)/shard_map/ppermute | solution.py:22
  6.0 12.7 %collective-permute-start.2 = (bf16[128,512]{1,0:T(8,128)(2,1)S(1)}, bf16[128,512]{1,0:T(8,128)(2,1)S(1)}, u32[]{:S(2)}, u32[]{:S(2)}) collective-permute-start(bf16[128,512]{1,0:T(8,128)(2,1)S(1)} %fusion), channel_id=1, source_target_pairs={{0,2},{1,3},{2,0},{3,1},{4,6},{5,7},{6,4},{7,5},{8,10},{9,11},{10,... | collective-permute-start | bytes 393224 | tf_op jit(solution)/shard_map/ppermute | solution.py:27
  8.7 10.1 %collective-permute-start.1 = (bf16[128,512]{1,0:T(8,128)(2,1)S(1)}, bf16[128,512]{1,0:T(8,128)(2,1)S(1)}, u32[]{:S(2)}, u32[]{:S(2)}) collective-permute-start(bf16[128,512]{1,0:T(8,128)(2,1)S(1)} %fusion), channel_id=1, source_target_pairs={{0,1},{1,2},{2,3},{3,0},{4,5},{5,6},{6,7},{7,4},{8,9},{9,10},{10,1... | collective-permute-start | bytes 393224 | tf_op jit(solution)/shard_map/ppermute | solution.py:27
  10.2 8.9 %collective-permute-start.3 = (bf16[128,512]{1,0:T(8,128)(2,1)S(1)}, bf16[128,512]{1,0:T(8,128)(2,1)S(1)}, u32[]{:S(2)}, u32[]{:S(2)}) collective-permute-start(bf16[128,512]{1,0:T(8,128)(2,1)S(1)} %fusion), channel_id=1, source_target_pairs={{0,3},{1,0},{2,1},{3,2},{4,7},{5,4},{6,5},{7,6},{8,11},{9,8},{10,9... | collective-permute-start | bytes 393224 | tf_op jit(solution)/shard_map/ppermute | solution.py:27
  14.1 26.1 %copy-start.7 = (f32[512]{0:T(512)S(1)}, f32[512]{0:T(512)}, u32[]{:S(2)}) copy-start(f32[512]{0:T(512)} %param.13) | copy-start | bytes 6148
  19.2 17.3 %collective-permute-start.4 = (bf16[3,64,512]{2,1,0:T(8,128)(2,1)S(1)}, bf16[3,64,512]{2,1,0:T(8,128)(2,1)S(1)}, u32[]{:S(2)}, u32[]{:S(2)}) collective-permute-start(bf16[3,64,512]{2,1,0:T(8,128)(2,1)S(1)} %get-tuple-element.28.upper), channel_id=1, source_target_pairs={{0,8},{4,12},{8,0},{12,4},{16,24},{20,28},{24,16},{28,20},{1,9},{5... | collective-permute-start | bytes 589832 | tf_op jit(solution)/shard_map/ppermute | solution.py:32
  20.7 15.7 %collective-permute-start.5 = (bf16[3,64,512]{2,1,0:T(8,128)(2,1)S(1)}, bf16[3,64,512]{2,1,0:T(8,128)(2,1)S(1)}, u32[]{:S(2)}, u32[]{:S(2)}) collective-permute-start(bf16[3,64,512]{2,1,0:T(8,128)(2,1)S(1)} %get-tuple-element.29.lower), channel_id=1, source_target_pairs={{0,16},{4,20},{8,24},{12,28},{16,0},{20,4},{24,8},{28,12},{1,17},{... | collective-permute-start | bytes 589832 | tf_op jit(solution)/shard_map/ppermute | solution.py:32
  20.8 7.1 %collective-permute-start.8 = (bf16[256,256]{1,0:T(8,128)(2,1)S(1)}, bf16[256,256]{1,0:T(8,128)(2,1)S(1)}, u32[]{:S(2)}, u32[]{:S(2)}) collective-permute-start(bf16[256,256]{1,0:T(8,128)(2,1)S(1)} %get-tuple-element.30), channel_id=1, source_target_pairs={{0,3},{1,0},{2,1},{3,2},{4,7},{5,4},{6,5},{7,6},{8,11},{9,8},{10,9... | collective-permute-start | bytes 393224 | tf_op jit(solution)/shard_map/ppermute | solution.py:27
  24.1 12.4 %collective-permute-start.7 = (bf16[256,256]{1,0:T(8,128)(2,1)S(1)}, bf16[256,256]{1,0:T(8,128)(2,1)S(1)}, u32[]{:S(2)}, u32[]{:S(2)}) collective-permute-start(bf16[256,256]{1,0:T(8,128)(2,1)S(1)} %get-tuple-element.30), channel_id=1, source_target_pairs={{0,2},{1,3},{2,0},{3,1},{4,6},{5,7},{6,4},{7,5},{8,10},{9,11},{10,... | collective-permute-start | bytes 393224 | tf_op jit(solution)/shard_map/ppermute | solution.py:27
  24.6 11.8 %collective-permute-start.6 = (bf16[256,256]{1,0:T(8,128)(2,1)S(1)}, bf16[256,256]{1,0:T(8,128)(2,1)S(1)}, u32[]{:S(2)}, u32[]{:S(2)}) collective-permute-start(bf16[256,256]{1,0:T(8,128)(2,1)S(1)} %get-tuple-element.30), channel_id=1, source_target_pairs={{0,1},{1,2},{2,3},{3,0},{4,5},{5,6},{6,7},{7,4},{8,9},{9,10},{10,1... | collective-permute-start | bytes 393224 | tf_op jit(solution)/shard_map/ppermute | solution.py:27
  37.1 3.8 %collective-permute-start.10 = (bf16[2,3,128,512]{3,2,1,0:T(8,128)(2,1)S(1)}, bf16[2,3,128,512]{3,2,1,0:T(8,128)(2,1)S(1)}, u32[]{:S(2)}, u32[]{:S(2)}) collective-permute-start(bf16[2,3,128,512]{3,2,1,0:T(8,128)(2,1)S(1)} %get-tuple-element.32.refs_0_), channel_id=1, source_target_pairs={{0,4},{4,0},{8,12},{12,8},{16,20},{20,16},{24,28},{28,24},{1,5},{5... | collective-permute-start | bytes 2359304 | tf_op jit(solution)/shard_map/ppermute | solution.py:32
  37.2 3.0 %collective-permute-start.9 = (bf16[4,128,512]{2,1,0:T(8,128)(2,1)S(1)}, bf16[4,128,512]{2,1,0:T(8,128)(2,1)S(1)}, u32[]{:S(2)}, u32[]{:S(2)}) collective-permute-start(bf16[4,128,512]{2,1,0:T(8,128)(2,1)S(1)} %get-tuple-element.31), channel_id=1, source_target_pairs={{0,4},{4,0},{8,12},{12,8},{16,20},{20,16},{24,28},{28,24},{1,5},{5... | collective-permute-start | bytes 1572872 | tf_op jit(solution)/shard_map/ppermute | solution.py:32
  37.7 8.6 %collective-permute-start.11 = (bf16[3,128,256]{2,1,0:T(8,128)(2,1)S(1)}, bf16[3,128,256]{2,1,0:T(8,128)(2,1)S(1)}, u32[]{:S(2)}, u32[]{:S(2)}) collective-permute-start(bf16[3,128,256]{2,1,0:T(8,128)(2,1)S(1)} %get-tuple-element.35.refs_0_), channel_id=1, source_target_pairs={{0,8},{4,12},{8,0},{12,4},{16,24},{20,28},{24,16},{28,20},{1,9},{5... | collective-permute-start | bytes 589832 | tf_op jit(solution)/shard_map/ppermute | solution.py:32
  39.4 6.9 %collective-permute-start.12 = (bf16[3,128,256]{2,1,0:T(8,128)(2,1)S(1)}, bf16[3,128,256]{2,1,0:T(8,128)(2,1)S(1)}, u32[]{:S(2)}, u32[]{:S(2)}) collective-permute-start(bf16[3,128,256]{2,1,0:T(8,128)(2,1)S(1)} %get-tuple-element.36.refs_2_), channel_id=1, source_target_pairs={{0,16},{4,20},{8,24},{12,28},{16,0},{20,4},{24,8},{28,12},{1,17},{... | collective-permute-start | bytes 589832 | tf_op jit(solution)/shard_map/ppermute | solution.py:32
  47.6 14.8 %collective-permute-start.16 = (bf16[2,3,128,256]{3,2,1,0:T(8,128)(2,1)S(1)}, bf16[2,3,128,256]{3,2,1,0:T(8,128)(2,1)S(1)}, u32[]{:S(2)}, u32[]{:S(2)}) collective-permute-start(bf16[2,3,128,256]{3,2,1,0:T(8,128)(2,1)S(1)} %get-tuple-element.42.refs_4_), channel_id=1, source_target_pairs={{0,16},{4,20},{8,24},{12,28},{16,0},{20,4},{24,8},{28,12},{1,17},{... | collective-permute-start | bytes 1179656 | tf_op jit(solution)/shard_map/ppermute | solution.py:32
  49.3 13.1 %collective-permute-start.17 = (bf16[2,3,128,256]{3,2,1,0:T(8,128)(2,1)S(1)}, bf16[2,3,128,256]{3,2,1,0:T(8,128)(2,1)S(1)}, u32[]{:S(2)}, u32[]{:S(2)}) collective-permute-start(bf16[2,3,128,256]{3,2,1,0:T(8,128)(2,1)S(1)} %get-tuple-element.43.refs_6_), channel_id=1, source_target_pairs={{0,8},{4,12},{8,0},{12,4},{16,24},{20,28},{24,16},{28,20},{1,9},{5... | collective-permute-start | bytes 1179656 | tf_op jit(solution)/shard_map/ppermute | solution.py:32
  49.8 8.3 %collective-permute-start.13 = (bf16[512,128]{1,0:T(8,128)(2,1)S(1)}, bf16[512,128]{1,0:T(8,128)(2,1)S(1)}, u32[]{:S(2)}, u32[]{:S(2)}) collective-permute-start(bf16[512,128]{1,0:T(8,128)(2,1)S(1)} %get-tuple-element.39), channel_id=1, source_target_pairs={{0,1},{1,2},{2,3},{3,0},{4,5},{5,6},{6,7},{7,4},{8,9},{9,10},{10,1... | collective-permute-start | bytes 393224 | tf_op jit(solution)/shard_map/ppermute | solution.py:27
  49.8 12.5 %collective-permute-start.14 = (bf16[512,128]{1,0:T(8,128)(2,1)S(1)}, bf16[512,128]{1,0:T(8,128)(2,1)S(1)}, u32[]{:S(2)}, u32[]{:S(2)}) collective-permute-start(bf16[512,128]{1,0:T(8,128)(2,1)S(1)} %get-tuple-element.40), channel_id=1, source_target_pairs={{0,2},{1,3},{2,0},{3,1},{4,6},{5,7},{6,4},{7,5},{8,10},{9,11},{10,... | collective-permute-start | bytes 393224 | tf_op jit(solution)/shard_map/ppermute | solution.py:27
  51.0 11.4 %collective-permute-start.15 = (bf16[512,128]{1,0:T(8,128)(2,1)S(1)}, bf16[512,128]{1,0:T(8,128)(2,1)S(1)}, u32[]{:S(2)}, u32[]{:S(2)}) collective-permute-start(bf16[512,128]{1,0:T(8,128)(2,1)S(1)} %get-tuple-element.41), channel_id=1, source_target_pairs={{0,3},{1,0},{2,1},{3,2},{4,7},{5,4},{6,5},{7,6},{8,11},{9,8},{10,9... | collective-permute-start | bytes 393224 | tf_op jit(solution)/shard_map/ppermute | solution.py:27
  63.6 4.9 %collective-permute-start.18 = (bf16[8,3,128,256]{3,2,1,0:T(8,128)(2,1)S(1)}, bf16[8,3,128,256]{3,2,1,0:T(8,128)(2,1)S(1)}, u32[]{:S(2)}, u32[]{:S(2)}) collective-permute-start(bf16[8,3,128,256]{3,2,1,0:T(8,128)(2,1)S(1)} %get-tuple-element.44.refs_0_), channel_id=1, source_target_pairs={{0,4},{4,0},{8,12},{12,8},{16,20},{20,16},{24,28},{28,24},{1,5},{5... | collective-permute-start | bytes 4718600 | tf_op jit(solution)/shard_map/ppermute | solution.py:32
  63.7 8.2 %collective-permute-start.19 = (bf16[512,128]{1,0:T(8,128)(2,1)S(1)}, bf16[512,128]{1,0:T(8,128)(2,1)S(1)}, u32[]{:S(2)}, u32[]{:S(2)}) collective-permute-start(bf16[512,128]{1,0:T(8,128)(2,1)S(1)} %get-tuple-element.48), channel_id=1, source_target_pairs={{0,1},{1,2},{2,3},{3,0},{4,5},{5,6},{6,7},{7,4},{8,9},{9,10},{10,1... | collective-permute-start | bytes 393224 | tf_op jit(solution)/shard_map/ppermute | solution.py:27
  66.0 11.0 %collective-permute-start.20 = (bf16[512,128]{1,0:T(8,128)(2,1)S(1)}, bf16[512,128]{1,0:T(8,128)(2,1)S(1)}, u32[]{:S(2)}, u32[]{:S(2)}) collective-permute-start(bf16[512,128]{1,0:T(8,128)(2,1)S(1)} %get-tuple-element.49), channel_id=1, source_target_pairs={{0,2},{1,3},{2,0},{3,1},{4,6},{5,7},{6,4},{7,5},{8,10},{9,11},{10,... | collective-permute-start | bytes 393224 | tf_op jit(solution)/shard_map/ppermute | solution.py:27
  67.2 9.9 %collective-permute-start.21 = (bf16[512,128]{1,0:T(8,128)(2,1)S(1)}, bf16[512,128]{1,0:T(8,128)(2,1)S(1)}, u32[]{:S(2)}, u32[]{:S(2)}) collective-permute-start(bf16[512,128]{1,0:T(8,128)(2,1)S(1)} %get-tuple-element.50), channel_id=1, source_target_pairs={{0,3},{1,0},{2,1},{3,2},{4,7},{5,4},{6,5},{7,6},{8,11},{9,8},{10,9... | collective-permute-start | bytes 393224 | tf_op jit(solution)/shard_map/ppermute | solution.py:27
  (10 other events, 108.6 us)

commit v8 on v7

--- a/solution.py
+++ b/solution.py
@@ -22,24 +22,23 @@
     return lax.ppermute(value, axis, [(source, source + steps) for source in range(count - steps)])
 
 
-def rotated(value, axis, steps):
-    count = lax.axis_size(axis)
-    return lax.ppermute(value, axis, [(source, (source + steps) % count) for source in range(count)])
-
-
 def swapped(value, axis, bits):
     count = lax.axis_size(axis)
     return lax.ppermute(value, axis, [(source, source ^ bits) for source in range(count)])
 
 
+def steps_over(count):
+    half = count // 2
+    return tuple(range(half, count)) + tuple(range(1, half))
+
+
 def rms_scale(values, gain):
     mean_sq = jnp.mean(values * values, axis=-1, keepdims=True)
     return values * lax.rsqrt(mean_sq + 1e-06) * gain
 
 
 def quarter_of(block):
-    parity = lax.rem(lax.div(block, 2) + lax.div(block, 4), 2)
-    return lax.rem(block, 2) + 2 * parity
+    return lax.rem(block, 2) + 2 * lax.rem(lax.div(block, 4), 2)
 
 
 def row_sum(value):
@@ -56,22 +55,18 @@
             normed[row : row + zone_rows, :] = rms_scale(block[step].astype(F32), gain).astype(BF16)
 
 
-def split_kernel(packed, before, *refs):
-    arrived, (upper, lower, packed_out) = refs[:-3], refs[-3:]
-    half = upper.shape[1]
+def split_kernel(place, packed, states, before, *refs):
+    arrived, (direct, packed_out, last) = refs[:-3], refs[-3:]
     for index, piece in enumerate(arrived):
-        upper[index] = piece[:half, :]
-        lower[index] = piece[half:, :]
+        direct[index] = piece[...]
     packed_out[...] = packed[...]
-
-
-def gather_kernel(place, states, before, upper, lower, over_x, over_y, *refs):
-    across, (quarters, last, first_out, second_out) = refs[:-4], refs[-4:]
-    half = upper.shape[1]
-    for index, (top, bottom) in enumerate(((upper, lower), (over_x, over_y))):
-        quarters[index, :, :half, :] = top[...]
-        quarters[index, :, half:, :] = bottom[...]
     last[...] = jnp.where(lax.rem(place[0], 2) == 1, before[...], states[...])
+
+
+def gather_kernel(normed, direct, over, *refs):
+    across, (quarters, first_out, second_out) = refs[:-3], refs[-3:]
+    quarters[0] = direct[...]
+    quarters[1] = over[...]
     split = first_out.shape[1]
     for index, piece in enumerate(across):
         first_out[index] = piece[:split, :]
@@ -100,12 +95,11 @@
     for copy in copies:
         copy.start()
     my_quarter = quarter_of(my_block)
-    for step in range(1, zones):
-        source = lax.rem(my_zone - step + zones, zones)
-        rows = pl.ds(pl.multiple_of(source * shard, shard), shard)
+    for place_in, step in enumerate(steps_over(zones)):
+        rows = pl.ds(pl.multiple_of((my_zone ^ step) * shard, shard), shard)
         for core, pair in enumerate(quarters):
             for index in range(2):
-                weights[my_quarter ^ (core + 2 * index), rows, :] = pair[index, step - 1]
+                weights[my_quarter ^ (core + 2 * index), rows, :] = pair[index, place_in]
     for copy in copies:
         copy.wait()
     attn_out[...] = weights[3]
@@ -208,8 +202,8 @@
         mixin = rms_scale(after, gain).astype(BF16)
         for index in range(zones):
             parts[index, rows, :] = mixin[:, index * part : (index + 1) * part]
-    for step in range(zones):
-        outs[step][...] = parts[lax.rem(my_zone + step, zones)]
+    for index, step in enumerate((0,) + steps_over(zones)):
+        outs[index][...] = parts[my_zone ^ step]
 
 
 def mixing_kernel(steps, zones, place, neighbours, degree, mix, *refs):
@@ -220,11 +214,11 @@
     part = items.shape[-1]
     my_zone = place[1]
     group = 2 if part % LANES == 0 and steps % 2 == 0 else 1
-    for step in range(zones):
-        items[lax.rem(my_zone - step + zones, zones)] = arrived[step][...]
-
-    for target in range(zones):
-        block = lax.rem(my_zone + target, zones)
+    for index, step in enumerate((0,) + steps_over(zones)):
+        items[my_zone ^ step] = arrived[index][...]
+
+    for target, target_step in enumerate((0,) + steps_over(zones)):
+        block = my_zone ^ target_step
         left = []
         for slot in range(slots):
             tile = mix[block, slot]
@@ -274,26 +268,26 @@
         for index in range(4):
             slot_in = lax.rem(my_block, SPREAD) ^ (IN_BITS[index] + core)
             slot_out = lax.rem(my_block, SPREAD) ^ (OUT_BITS[index] + core)
-            for step in range(1, zones):
-                source = lax.rem(my_zone - step + zones, zones)
+            for place_in, step in enumerate(steps_over(zones)):
+                source = my_zone ^ step
                 rows = pl.ds(pl.multiple_of(source * in_shard, in_shard), in_shard)
-                w_in[slot_in, rows, :] = pieces[index, step - 1]
+                w_in[slot_in, rows, :] = pieces[index, place_in]
                 first = pl.multiple_of(source * out_shard + slot_out * out_rows, out_rows)
                 for fold in range(width // in_cols):
                     cols = slice(fold * in_cols, (fold + 1) * in_cols)
                     rows = slice(fold * out_rows, (fold + 1) * out_rows)
-                    w_out[pl.ds(first, out_rows), cols] = pieces[4 + index, step - 1, rows, :]
+                    w_out[pl.ds(first, out_rows), cols] = pieces[4 + index, place_in, rows, :]
     for copy in copies:
         copy.wait()
 
 
 def ffn_kernel(zones, place, after_attn, gain_ffn, w_in, w_out, *refs):
-    arrived, (out, after_mix, ffn_in, parts) = refs[:zones], refs[zones:]
+    arrived, (out, after_mix, ffn_in, parts, hidden) = refs[:zones], refs[zones:]
     rows_all, width = after_attn.shape
     my_zone = place[1]
     in_cols = w_in.shape[2]
-    for step in range(zones):
-        parts[lax.rem(my_zone - step + zones, zones)] = arrived[step][...]
+    for index, step in enumerate((0,) + steps_over(zones)):
+        parts[my_zone ^ step] = arrived[index][...]
 
     gain = gain_ffn[...]
     span = 128
@@ -307,16 +301,12 @@
     span = 256
     for first in range(0, rows_all, span):
         rows = slice(first, first + span)
-        total = after_mix[rows, :]
         for index in range(SPREAD):
-            hidden_part = jnp.dot(ffn_in[rows, :], w_in[index], preferred_element_type=F32)
-            hidden_part = jax.nn.gelu(hidden_part, approximate=True).astype(BF16)
-            total = total + jnp.dot(
-                hidden_part,
-                w_out[index * in_cols : (index + 1) * in_cols, :],
-                preferred_element_type=F32,
-            )
-        out[rows, :] = total.astype(BF16)
+            grown = jnp.dot(ffn_in[rows, :], w_in[index], preferred_element_type=F32)
+            cols = slice(index * in_cols, (index + 1) * in_cols)
+            hidden[rows, cols] = jax.nn.gelu(grown, approximate=True).astype(BF16)
+        shrunk = jnp.dot(hidden[rows, :], w_out[...], preferred_element_type=F32)
+        out[rows, :] = (after_mix[rows, :] + shrunk).astype(BF16)
 
 
 def call(kernel, out_shape, scratch, smem, hbm, limit, args):
@@ -359,13 +349,13 @@
     in_cols = hidden // SPREAD
     out_rows = w_out.shape[0] // SPREAD
     part = width // zones
-    rotations = range(1, zones)
+    exchanges = steps_over(zones)
 
     before = shifted(states, "tm", 2)
     first = lax.dynamic_slice_in_dim(
         jnp.concatenate([w_qkv, w_out_attn], axis=1), quarter_of(my_block) * width, width, axis=1
     )
-    direct = [rotated(first, "zone", step) for step in rotations]
+    direct = [swapped(first, "zone", step) for step in exchanges]
     slot = my_block % SPREAD
     slice_in = lax.dynamic_slice_in_dim(w_in, slot * in_cols, in_cols, axis=1)
     slice_out = lax.dynamic_slice_in_dim(w_out, slot * out_rows, out_rows, axis=0)
@@ -374,35 +364,22 @@
     packed = jnp.concatenate(
         [slice_in] + [slice_out[:, at : at + in_cols] for at in range(0, width, in_cols)], axis=0
     )
-    half = first.shape[0] // 2
-    half_shape = jax.ShapeDtypeStruct((zones - 1, half, width), BF16)
-    upper, lower, packed = call(
+    direct, packed, last = call(
         split_kernel,
-        (half_shape, half_shape, jax.ShapeDtypeStruct(packed.shape, BF16)),
-        [],
-        (),
-        (),
-        4,
-        [packed, before] + direct,
-    )
-    over_x, over_y = swapped(upper, "tm", 2), swapped(lower, "tm", 4)
-    across = [rotated(packed, "zone", step) for step in rotations]
-    quarters, last, part_in, part_out = call(
-        gather_kernel,
         (
-            jax.ShapeDtypeStruct((2, zones - 1) + first.shape, BF16),
+            jax.ShapeDtypeStruct((zones - 1,) + first.shape, BF16),
+            jax.ShapeDtypeStruct(packed.shape, BF16),
             jax.ShapeDtypeStruct(states.shape, BF16),
-        )
-        + tuple(jax.ShapeDtypeStruct((zones - 1, size, in_cols), BF16) for size in sizes),
+        ),
         [],
         (0,),
         (),
         4,
-        [place, states, before, upper, lower, over_x, over_y] + across,
-    )
-    quarters = [quarters, swapped(quarters, "tm", 1)]
+        [place, packed, states, before] + direct,
+    )
+    over = swapped(direct, "tm", 4)
     last = swapped(last, "tm", 1)
-    over_in, over_out = swapped(part_in, "tm", 2), swapped(part_out, "tm", 4)
+    across = [swapped(packed, "zone", step) for step in exchanges]
     normed = call(
         norm_kernel,
         jax.ShapeDtypeStruct((key_count * zone_rows, width), BF16),
@@ -413,6 +390,18 @@
         [before, last, states, gain_attn.reshape(1, -1)],
     )
 
+    quarters, part_in, part_out = call(
+        gather_kernel,
+        (jax.ShapeDtypeStruct((2,) + direct.shape, BF16),)
+        + tuple(jax.ShapeDtypeStruct((zones - 1, size, in_cols), BF16) for size in sizes),
+        [],
+        (),
+        (),
+        4,
+        [normed, direct, over] + across,
+    )
+    quarters = [quarters, swapped(quarters, "tm", 1)]
+    over_in, over_out = swapped(part_in, "tm", 2), swapped(part_out, "tm", 4)
     context, w_attn = call(
         functools.partial(attention_kernel, zones, reach, steps),
         (
@@ -445,7 +434,9 @@
         [place, states, context, w_attn, gain_mix.reshape(1, -1)]
         + [part_in, over_in, part_out, over_out],
     )
-    arrived = [chunks[0]] + [rotated(chunks[step], "zone", step) for step in rotations]
+    arrived = [chunks[0]] + [
+        swapped(value, "zone", step) for value, step in zip(chunks[1:], exchanges)
+    ]
 
     pairs = [pair_in, swapped(pair_in, "tm", 4), pair_out, swapped(pair_out, "tm", 2)]
 
@@ -471,7 +462,9 @@
         8,
         [place, w_in, w_out, gathered, swapped(gathered, "tm", 1)],
     )
-    arrived = [spatial[0]] + [rotated(spatial[step], "zone", step) for step in rotations]
+    arrived = [spatial[0]] + [
+        swapped(value, "zone", step) for value, step in zip(spatial[1:], exchanges)
+    ]
     evolved = call(
         functools.partial(ffn_kernel, zones),
         jax.ShapeDtypeStruct((rows, width), BF16),
@@ -479,6 +472,7 @@
             pltpu.VMEM((rows, width), F32),
             pltpu.VMEM((rows, width), BF16),
             pltpu.VMEM((zones, rows, part), BF16),
+            pltpu.VMEM((rows, hidden), BF16),
         ],
         (0,),
         (),

time: 82.1 us -> 81 us (0.987)
  starting transfers between devices: 32.9 us -> 27 us
  waiting for transfers between devices: 31.1 us -> 36.8 us
    ppermute x9 -> x20, waiting for transfers between devices: 0.34 us -> 36.8 us  [swapped(): lax.ppermute(value, axis, [(source, source ^ bits) for source in range(co...]
    ppermute x12 -> x0, waiting for transfers between devices: 30.8 us -> none  [rotated(): lax.ppermute(value, axis, [(source, (source + steps) % count) for source...]
    ppermute x12 -> x0, starting transfers between devices: 21.2 us -> none  [rotated(): lax.ppermute(value, axis, [(source, (source + steps) % count) for source...]
    ppermute x9 -> x20, starting transfers between devices: 6.74 us -> 22 us  [swapped(): lax.ppermute(value, axis, [(source, source ^ bits) for source in range(co...]
  transfers between devices with their start and end apart: 22 -> 21, of which waited for: 9 -> 10; matrix products, arithmetic and copies ran while one was open for 3% -> 3% of each run, Pallas kernels for 8% -> 8%
where the time goes in v8:
time: 81 us; the launch traced here: 80.7 us
  waiting for transfers between devices  36.8 us (45%)
  starting transfers between devices  27 us (33%)
  Pallas kernels  13.9 us (17%)
  local copies, waits for them, and re-layouts  1.69 us (2%)
  other arithmetic  1.05 us (1%)
    ppermute x20, waiting for transfers between devices, swapped(): lax.ppermute(value, axis, [(source, source ^ bits) for source in range(co...  36.8 us
    ppermute x20, starting transfers between devices, swapped(): lax.ppermute(value, axis, [(source, source ^ bits) for source in range(co...  22 us
    pallas_call x8, Pallas kernels, call(): pl.pallas_call(kernel, out_shape=out_shape, in_specs=[pl.BlockSpec(memory...  13.9 us
    ppermute x1, starting transfers between devices, shifted(): lax.ppermute(value, axis, [(source, source + steps) for source in range(c...  4.99 us
  transfers between devices with their start and end apart: 21, of which 10 were waited for; matrix products, arithmetic and copies ran while one was open for 3% of the time, Pallas kernels for 8%

profile of v8, /device:TPU:0, one launch (start us, length us, event | category | flops | bytes accessed | tf_op | source)
XLA Modules:
  0.0 80.7 jit_solution(9330803704949392955)
XLA Ops:
  0.0 5.0 %collective-permute-start = (bf16[4,128,512]{2,1,0:T(8,128)(2,1)}, bf16[4,128,512]{2,1,0:T(8,128)(2,1)S(1)}, u32[]{:S(2)}, u32[]{:S(2)}) collective-permute-start(bf16[4,128,512]{2,1,0:T(8,128)(2,1)} %states.3), channel_id=1, source_target_pairs={{0,8},{4,12},{8,16},{12,20},{16,24},{20,28},{1,9},{5,13},{9,17},{1... | collective-permute-start | bytes 1572872 | tf_op jit(solution)/shard_map/ppermute | solution.py:22
  5.0 1.0 %fusion = bf16[128,512]{1,0:T(8,128)(2,1)S(1)} fusion(s32[]{:T(128)S(6)} %select_n.19, bf16[128,1536]{1,0:T(8,128)(2,1)} %own_qkv.1, bf16[128,512]{1,0:T(8,128)(2,1)} %own_attn.1), kind=kLoop, calls=%fused_computation.2 | loop fusion | flops 262144 | bytes 655364 | tf_op jit(solution)/shard_map/concatenate | solution.py:356
  6.0 3.7 %collective-permute-start.2 = (bf16[128,512]{1,0:T(8,128)(2,1)S(1)}, bf16[128,512]{1,0:T(8,128)(2,1)S(1)}, u32[]{:S(2)}, u32[]{:S(2)}) collective-permute-start(bf16[128,512]{1,0:T(8,128)(2,1)S(1)} %fusion), channel_id=1, source_target_pairs={{0,3},{1,2},{2,1},{3,0},{4,7},{5,6},{6,5},{7,4},{8,11},{9,10},{10,... | collective-permute-start | bytes 393224 | tf_op jit(solution)/shard_map/ppermute | solution.py:27
  12.2 2.2 %collective-permute-done.2.refs_1_ = bf16[128,512]{1,0:T(8,128)(2,1)S(1)} collective-permute-done((bf16[128,512]{1,0:T(8,128)(2,1)S(1)}, bf16[128,512]{1,0:T(8,128)(2,1)S(1)}, u32[]{:S(2)}, u32[]{:S(2)}) %collective-permute-start.2) | collective-permute-done | bytes 131104 | tf_op jit(solution)/shard_map/ppermute | solution.py:27
  14.3 6.1 %collective-permute-done.1.refs_0_ = bf16[128,512]{1,0:T(8,128)(2,1)S(1)} collective-permute-done((bf16[128,512]{1,0:T(8,128)(2,1)S(1)}, bf16[128,512]{1,0:T(8,128)(2,1)S(1)}, u32[]{:S(2)}, u32[]{:S(2)}) %collective-permute-start.1) | collective-permute-done | bytes 131104 | tf_op jit(solution)/shard_map/ppermute | solution.py:27
  21.2 1.6 %collective-permute-start.5 = (bf16[3,128,512]{2,1,0:T(8,128)(2,1)S(1)}, bf16[3,128,512]{2,1,0:T(8,128)(2,1)S(1)}, u32[]{:S(2)}, u32[]{:S(2)}) collective-permute-start(bf16[3,128,512]{2,1,0:T(8,128)(2,1)S(1)} %get-tuple-element.28.direct), channel_id=1, source_target_pairs={{0,16},{4,20},{8,24},{12,28},{16,0},{20,4},{24,8},{28,12},{1,17},{... | collective-permute-start | bytes 1179656 | tf_op jit(solution)/shard_map/ppermute | solution.py:27
  22.8 2.5 %collective-permute-start.7 = (bf16[256,256]{1,0:T(8,128)(2,1)S(1)}, bf16[256,256]{1,0:T(8,128)(2,1)S(1)}, u32[]{:S(2)}, u32[]{:S(2)}) collective-permute-start(bf16[256,256]{1,0:T(8,128)(2,1)S(1)} %get-tuple-element.29), channel_id=1, source_target_pairs={{0,3},{1,2},{2,1},{3,0},{4,7},{5,6},{6,5},{7,4},{8,11},{9,10},{10,... | collective-permute-start | bytes 393224 | tf_op jit(solution)/shard_map/ppermute | solution.py:27
  25.2 1.0 %collective-permute-start.6 = (bf16[256,256]{1,0:T(8,128)(2,1)S(1)}, bf16[256,256]{1,0:T(8,128)(2,1)S(1)}, u32[]{:S(2)}, u32[]{:S(2)}) collective-permute-start(bf16[256,256]{1,0:T(8,128)(2,1)S(1)} %get-tuple-element.29), channel_id=1, source_target_pairs={{0,2},{1,3},{2,0},{3,1},{4,6},{5,7},{6,4},{7,5},{8,10},{9,11},{10,... | collective-permute-start | bytes 393224 | tf_op jit(solution)/shard_map/ppermute | solution.py:27
  26.9 1.4 %collective-permute-done.8.refs_2_ = bf16[256,256]{1,0:T(8,128)(2,1)S(1)} collective-permute-done((bf16[256,256]{1,0:T(8,128)(2,1)S(1)}, bf16[256,256]{1,0:T(8,128)(2,1)S(1)}, u32[]{:S(2)}, u32[]{:S(2)}) %collective-permute-start.8) | collective-permute-done | bytes 131104 | tf_op jit(solution)/shard_map/ppermute | solution.py:27
  28.3 4.1 %collective-permute-done.7.refs_1_ = bf16[256,256]{1,0:T(8,128)(2,1)S(1)} collective-permute-done((bf16[256,256]{1,0:T(8,128)(2,1)S(1)}, bf16[256,256]{1,0:T(8,128)(2,1)S(1)}, u32[]{:S(2)}, u32[]{:S(2)}) %collective-permute-start.7) | collective-permute-done | bytes 131104 | tf_op jit(solution)/shard_map/ppermute | solution.py:27
  32.4 5.5 %collective-permute-done.6.refs_0_ = bf16[256,256]{1,0:T(8,128)(2,1)S(1)} collective-permute-done((bf16[256,256]{1,0:T(8,128)(2,1)S(1)}, bf16[256,256]{1,0:T(8,128)(2,1)S(1)}, u32[]{:S(2)}, u32[]{:S(2)}) %collective-permute-start.6) | collective-permute-done | bytes 131104 | tf_op jit(solution)/shard_map/ppermute | solution.py:27
  38.4 1.8 %collective-permute-start.11 = (bf16[3,128,256]{2,1,0:T(8,128)(2,1)S(1)}, bf16[3,128,256]{2,1,0:T(8,128)(2,1)S(1)}, u32[]{:S(2)}, u32[]{:S(2)}) collective-permute-start(bf16[3,128,256]{2,1,0:T(8,128)(2,1)S(1)} %get-tuple-element.34.refs_2_), channel_id=1, source_target_pairs={{0,16},{4,20},{8,24},{12,28},{16,0},{20,4},{24,8},{28,12},{1,17},{... | collective-permute-start | bytes 589832 | tf_op jit(solution)/shard_map/ppermute | solution.py:27
  40.4 5.0 %shard_map.121 = (bf16[512,512]{1,0:T(8,128)(2,1)S(1)}, bf16[512,512]{1,0:T(8,128)(2,1)S(1)}) custom-call(s32[2]{0:T(128)S(1)} %pad_add_fusion.place, s32[1,2]{1,0:T(1,128)S(1)} %copy-done.10, bf16[1536,512]{1,0:T(8,128)(2,1)S(1)} %shard_map.119.normed, bf16[128,1536]{1,0:T(8,128)(2,1)S(1)} %copy-done.1, bf16[128,512]{1,0:T(8,128)(2,1)S(1)} %copy-done.4, ...), custom_call_target="tpu_custom_call" | custom-call | tf_op jit(solution)/shard_map/pallas_call | solution.py:314
  45.4 1.2 %shard_map.122 = (f32[512,512]{1,0:T(8,128)S(1)}, bf16[512,128]{1,0:T(8,128)(2,1)S(1)}, bf16[512,128]{1,0:T(8,128)(2,1)S(1)}, bf16[512,128]{1,0:T(8,128)(2,1)S(1...) custom-call(s32[2]{0:T(128)S(1)} %pad_add_fusion.place, ...), custom_call_target="tpu_custom_call" | custom-call | tf_op jit(solution)/shard_map/pallas_call | solution.py:314
  46.6 1.8 %collective-permute-start.15 = (bf16[2,3,128,256]{3,2,1,0:T(8,128)(2,1)S(1)}, bf16[2,3,128,256]{3,2,1,0:T(8,128)(2,1)S(1)}, u32[]{:S(2)}, u32[]{:S(2)}) collective-permute-start(bf16[2,3,128,256]{3,2,1,0:T(8,128)(2,1)S(1)} %get-tuple-element.40.refs_4_), channel_id=1, source_target_pairs={{0,16},{4,20},{8,24},{12,28},{16,0},{20,4},{24,8},{28,12},{1,17},{... | collective-permute-start | bytes 1179656 | tf_op jit(solution)/shard_map/ppermute | solution.py:27
  49.0 2.5 %collective-permute-start.13 = (bf16[512,128]{1,0:T(8,128)(2,1)S(1)}, bf16[512,128]{1,0:T(8,128)(2,1)S(1)}, u32[]{:S(2)}, u32[]{:S(2)}) collective-permute-start(bf16[512,128]{1,0:T(8,128)(2,1)S(1)} %get-tuple-element.38), channel_id=1, source_target_pairs={{0,3},{1,2},{2,1},{3,0},{4,7},{5,6},{6,5},{7,4},{8,11},{9,10},{10,... | collective-permute-start | bytes 393224 | tf_op jit(solution)/shard_map/ppermute | solution.py:27
  51.5 1.0 %collective-permute-start.14 = (bf16[512,128]{1,0:T(8,128)(2,1)S(1)}, bf16[512,128]{1,0:T(8,128)(2,1)S(1)}, u32[]{:S(2)}, u32[]{:S(2)}) collective-permute-start(bf16[512,128]{1,0:T(8,128)(2,1)S(1)} %get-tuple-element.39), channel_id=1, source_target_pairs={{0,1},{1,0},{2,3},{3,2},{4,5},{5,4},{6,7},{7,6},{8,9},{9,8},{10,11... | collective-permute-start | bytes 393224 | tf_op jit(solution)/shard_map/ppermute | solution.py:27
  52.5 7.7 %collective-permute-done.12.refs_1_ = bf16[512,128]{1,0:T(8,128)(2,1)S(1)} collective-permute-done((bf16[512,128]{1,0:T(8,128)(2,1)S(1)}, bf16[512,128]{1,0:T(8,128)(2,1)S(1)}, u32[]{:S(2)}, u32[]{:S(2)}) %collective-permute-start.12) | collective-permute-done | bytes 131104 | tf_op jit(solution)/shard_map/ppermute | solution.py:27
  60.1 1.3 %collective-permute-done.14.refs_3_ = bf16[512,128]{1,0:T(8,128)(2,1)S(1)} collective-permute-done((bf16[512,128]{1,0:T(8,128)(2,1)S(1)}, bf16[512,128]{1,0:T(8,128)(2,1)S(1)}, u32[]{:S(2)}, u32[]{:S(2)}) %collective-permute-start.14) | collective-permute-done | bytes 131104 | tf_op jit(solution)/shard_map/ppermute | solution.py:27
  61.4 1.2 %shard_map.123 = (bf16[512,128]{1,0:T(8,128)(2,1)S(1)}, bf16[512,128]{1,0:T(8,128)(2,1)S(1)}, bf16[512,128]{1,0:T(8,128)(2,1)S(1)}, bf16[512,128]{1,0:T(8,128)(2,1)S(1)}, bf16[8,3,128,256]{3,2,1,0:T(8,128)(2,1)S(1)}) custom-call(s32[2]{0:T(128)S(1)} %pad_add_fusion.place, s32[4,3]{1,0:T(4,128)S(1)} %copy-done.9, s32[4]{0:T(128)S(1)} %copy-done.11, ...), custom_call_target="tpu_custom_call" | custom-call | tf_op jit(solution)/shard_map/pallas_call | solution.py:314
  62.7 2.0 %collective-permute-start.18 = (bf16[512,128]{1,0:T(8,128)(2,1)S(1)}, bf16[512,128]{1,0:T(8,128)(2,1)S(1)}, u32[]{:S(2)}, u32[]{:S(2)}) collective-permute-start(bf16[512,128]{1,0:T(8,128)(2,1)S(1)} %get-tuple-element.46), channel_id=1, source_target_pairs={{0,2},{1,3},{2,0},{3,1},{4,6},{5,7},{6,4},{7,5},{8,10},{9,11},{10,... | collective-permute-start | bytes 393224 | tf_op jit(solution)/shard_map/ppermute | solution.py:27
  64.7 2.5 %collective-permute-start.19 = (bf16[512,128]{1,0:T(8,128)(2,1)S(1)}, bf16[512,128]{1,0:T(8,128)(2,1)S(1)}, u32[]{:S(2)}, u32[]{:S(2)}) collective-permute-start(bf16[512,128]{1,0:T(8,128)(2,1)S(1)} %get-tuple-element.47), channel_id=1, source_target_pairs={{0,3},{1,2},{2,1},{3,0},{4,7},{5,6},{6,5},{7,4},{8,11},{9,10},{10,... | collective-permute-start | bytes 393224 | tf_op jit(solution)/shard_map/ppermute | solution.py:27
  68.1 7.5 %collective-permute-done.18.refs_1_ = bf16[512,128]{1,0:T(8,128)(2,1)S(1)} collective-permute-done((bf16[512,128]{1,0:T(8,128)(2,1)S(1)}, bf16[512,128]{1,0:T(8,128)(2,1)S(1)}, u32[]{:S(2)}, u32[]{:S(2)}) %collective-permute-start.18) | collective-permute-done | bytes 131104 | tf_op jit(solution)/shard_map/ppermute | solution.py:27
  76.5 4.2 %shard_map.125 = bf16[512,512]{1,0:T(8,128)(2,1)} custom-call(s32[2]{0:T(128)S(1)} %pad_add_fusion.place, f32[512,512]{1,0:T(8,128)S(1)} %get-tuple-element.35.after_attn, f32[1,512]{1,0:T(1,128)S(1)} %bitcast.6, bf16[8,512,256]{2,1,0:T(8,128)(2,1)S(1)} %get-tuple-element.43.w_in, bf16[2048,512]{1,0:T(8,128)(2,1)S(1)} %get-tuple-element.44.w_out, ...), custom_call_target="tpu_custom_call" | custom-call | tf_op jit(solution)/shard_map/pallas_call | solution.py:314
  (55 shorter events, 7.1 us)
Async XLA Ops:
  0.0 26.2 %copy-start.7 = (f32[512]{0:T(512)S(1)}, f32[512]{0:T(512)}, u32[]{:S(2)}) copy-start(f32[512]{0:T(512)} %param.13) | copy-start | bytes 6148
  0.0 20.5 %collective-permute-start = (bf16[4,128,512]{2,1,0:T(8,128)(2,1)}, bf16[4,128,512]{2,1,0:T(8,128)(2,1)S(1)}, u32[]{:S(2)}, u32[]{:S(2)}) collective-permute-start(bf16[4,128,512]{2,1,0:T(8,128)(2,1)} %states.3), channel_id=1, source_target_pairs={{0,8},{4,12},{8,16},{12,20},{16,24},{20,28},{1,9},{5,13},{9,17},{1... | collective-permute-start | bytes 1572872 | tf_op jit(solution)/shard_map/ppermute | solution.py:22
  6.0 8.3 %collective-permute-start.2 = (bf16[128,512]{1,0:T(8,128)(2,1)S(1)}, bf16[128,512]{1,0:T(8,128)(2,1)S(1)}, u32[]{:S(2)}, u32[]{:S(2)}) collective-permute-start(bf16[128,512]{1,0:T(8,128)(2,1)S(1)} %fusion), channel_id=1, source_target_pairs={{0,3},{1,2},{2,1},{3,0},{4,7},{5,6},{6,5},{7,4},{8,11},{9,10},{10,... | collective-permute-start | bytes 393224 | tf_op jit(solution)/shard_map/ppermute | solution.py:27
  9.7 10.8 %collective-permute-start.1 = (bf16[128,512]{1,0:T(8,128)(2,1)S(1)}, bf16[128,512]{1,0:T(8,128)(2,1)S(1)}, u32[]{:S(2)}, u32[]{:S(2)}) collective-permute-start(bf16[128,512]{1,0:T(8,128)(2,1)S(1)} %fusion), channel_id=1, source_target_pairs={{0,2},{1,3},{2,0},{3,1},{4,6},{5,7},{6,4},{7,5},{8,10},{9,11},{10,... | collective-permute-start | bytes 393224 | tf_op jit(solution)/shard_map/ppermute | solution.py:27
  9.7 10.8 %collective-permute-start.3 = (bf16[128,512]{1,0:T(8,128)(2,1)S(1)}, bf16[128,512]{1,0:T(8,128)(2,1)S(1)}, u32[]{:S(2)}, u32[]{:S(2)}) collective-permute-start(bf16[128,512]{1,0:T(8,128)(2,1)S(1)} %fusion), channel_id=1, source_target_pairs={{0,1},{1,0},{2,3},{3,2},{4,5},{5,4},{6,7},{7,6},{8,9},{9,8},{10,11... | collective-permute-start | bytes 393224 | tf_op jit(solution)/shard_map/ppermute | solution.py:27
  21.1 5.1 %collective-permute-start.4 = (bf16[4,128,512]{2,1,0:T(8,128)(2,1)S(1)}, bf16[4,128,512]{2,1,0:T(8,128)(2,1)S(1)}, u32[]{:S(2)}, u32[]{:S(2)}) collective-permute-start(bf16[4,128,512]{2,1,0:T(8,128)(2,1)S(1)} %get-tuple-element.27), channel_id=1, source_target_pairs={{0,4},{4,0},{8,12},{12,8},{16,20},{20,16},{24,28},{28,24},{1,5},{5... | collective-permute-start | bytes 1572872 | tf_op jit(solution)/shard_map/ppermute | solution.py:27
  21.2 16.7 %collective-permute-start.5 = (bf16[3,128,512]{2,1,0:T(8,128)(2,1)S(1)}, bf16[3,128,512]{2,1,0:T(8,128)(2,1)S(1)}, u32[]{:S(2)}, u32[]{:S(2)}) collective-permute-start(bf16[3,128,512]{2,1,0:T(8,128)(2,1)S(1)} %get-tuple-element.28.direct), channel_id=1, source_target_pairs={{0,16},{4,20},{8,24},{12,28},{16,0},{20,4},{24,8},{28,12},{1,17},{... | collective-permute-start | bytes 1179656 | tf_op jit(solution)/shard_map/ppermute | solution.py:27
  22.7 5.6 %collective-permute-start.8 = (bf16[256,256]{1,0:T(8,128)(2,1)S(1)}, bf16[256,256]{1,0:T(8,128)(2,1)S(1)}, u32[]{:S(2)}, u32[]{:S(2)}) collective-permute-start(bf16[256,256]{1,0:T(8,128)(2,1)S(1)} %get-tuple-element.29), channel_id=1, source_target_pairs={{0,1},{1,0},{2,3},{3,2},{4,5},{5,4},{6,7},{7,6},{8,9},{9,8},{10,11... | collective-permute-start | bytes 393224 | tf_op jit(solution)/shard_map/ppermute | solution.py:27
  22.8 9.7 %collective-permute-start.7 = (bf16[256,256]{1,0:T(8,128)(2,1)S(1)}, bf16[256,256]{1,0:T(8,128)(2,1)S(1)}, u32[]{:S(2)}, u32[]{:S(2)}) collective-permute-start(bf16[256,256]{1,0:T(8,128)(2,1)S(1)} %get-tuple-element.29), channel_id=1, source_target_pairs={{0,3},{1,2},{2,1},{3,0},{4,7},{5,6},{6,5},{7,4},{8,11},{9,10},{10,... | collective-permute-start | bytes 393224 | tf_op jit(solution)/shard_map/ppermute | solution.py:27
  25.2 12.7 %collective-permute-start.6 = (bf16[256,256]{1,0:T(8,128)(2,1)S(1)}, bf16[256,256]{1,0:T(8,128)(2,1)S(1)}, u32[]{:S(2)}, u32[]{:S(2)}) collective-permute-start(bf16[256,256]{1,0:T(8,128)(2,1)S(1)} %get-tuple-element.29), channel_id=1, source_target_pairs={{0,2},{1,3},{2,0},{3,1},{4,6},{5,7},{6,4},{7,5},{8,10},{9,11},{10,... | collective-permute-start | bytes 393224 | tf_op jit(solution)/shard_map/ppermute | solution.py:27
  38.0 2.4 %collective-permute-start.9 = (bf16[2,3,128,512]{3,2,1,0:T(8,128)(2,1)S(1)}, bf16[2,3,128,512]{3,2,1,0:T(8,128)(2,1)S(1)}, u32[]{:S(2)}, u32[]{:S(2)}) collective-permute-start(bf16[2,3,128,512]{3,2,1,0:T(8,128)(2,1)S(1)} %get-tuple-element.30.refs_0_), channel_id=1, source_target_pairs={{0,4},{4,0},{8,12},{12,8},{16,20},{20,16},{24,28},{28,24},{1,5},{5... | collective-permute-start | bytes 2359304 | tf_op jit(solution)/shard_map/ppermute | solution.py:27
  38.1 7.3 %collective-permute-start.10 = (bf16[3,128,256]{2,1,0:T(8,128)(2,1)S(1)}, bf16[3,128,256]{2,1,0:T(8,128)(2,1)S(1)}, u32[]{:S(2)}, u32[]{:S(2)}) collective-permute-start(bf16[3,128,256]{2,1,0:T(8,128)(2,1)S(1)} %get-tuple-element.33.refs_0_), channel_id=1, source_target_pairs={{0,8},{4,12},{8,0},{12,4},{16,24},{20,28},{24,16},{28,20},{1,9},{5... | collective-permute-start | bytes 589832 | tf_op jit(solution)/shard_map/ppermute | solution.py:27
  38.4 7.0 %collective-permute-start.11 = (bf16[3,128,256]{2,1,0:T(8,128)(2,1)S(1)}, bf16[3,128,256]{2,1,0:T(8,128)(2,1)S(1)}, u32[]{:S(2)}, u32[]{:S(2)}) collective-permute-start(bf16[3,128,256]{2,1,0:T(8,128)(2,1)S(1)} %get-tuple-element.34.refs_2_), channel_id=1, source_target_pairs={{0,16},{4,20},{8,24},{12,28},{16,0},{20,4},{24,8},{28,12},{1,17},{... | collective-permute-start | bytes 589832 | tf_op jit(solution)/shard_map/ppermute | solution.py:27
  46.6 20.5 %copy-start.2 = (bf16[512,512]{1,0:T(8,128)(2,1)S(1)}, bf16[512,512]{1,0:T(8,128)(2,1)}, u32[]{:S(2)}) copy-start(bf16[512,512]{1,0:T(8,128)(2,1)} %own_out.1) | copy-start | bytes 1572868
  46.6 20.5 %copy-start.3 = (bf16[128,2048]{1,0:T(8,128)(2,1)S(1)}, bf16[128,2048]{1,0:T(8,128)(2,1)}, u32[]{:S(2)}) copy-start(bf16[128,2048]{1,0:T(8,128)(2,1)} %own_in.1) | copy-start | bytes 1572868
  46.6 14.8 %collective-permute-start.15 = (bf16[2,3,128,256]{3,2,1,0:T(8,128)(2,1)S(1)}, bf16[2,3,128,256]{3,2,1,0:T(8,128)(2,1)S(1)}, u32[]{:S(2)}, u32[]{:S(2)}) collective-permute-start(bf16[2,3,128,256]{3,2,1,0:T(8,128)(2,1)S(1)} %get-tuple-element.40.refs_4_), channel_id=1, source_target_pairs={{0,16},{4,20},{8,24},{12,28},{16,0},{20,4},{24,8},{28,12},{1,17},{... | collective-permute-start | bytes 1179656 | tf_op jit(solution)/shard_map/ppermute | solution.py:27
  48.4 13.0 %collective-permute-start.16 = (bf16[2,3,128,256]{3,2,1,0:T(8,128)(2,1)S(1)}, bf16[2,3,128,256]{3,2,1,0:T(8,128)(2,1)S(1)}, u32[]{:S(2)}, u32[]{:S(2)}) collective-permute-start(bf16[2,3,128,256]{3,2,1,0:T(8,128)(2,1)S(1)} %get-tuple-element.41.refs_6_), channel_id=1, source_target_pairs={{0,8},{4,12},{8,0},{12,4},{16,24},{20,28},{24,16},{28,20},{1,9},{5... | collective-permute-start | bytes 1179656 | tf_op jit(solution)/shard_map/ppermute | solution.py:27
  49.0 11.1 %collective-permute-start.12 = (bf16[512,128]{1,0:T(8,128)(2,1)S(1)}, bf16[512,128]{1,0:T(8,128)(2,1)S(1)}, u32[]{:S(2)}, u32[]{:S(2)}) collective-permute-start(bf16[512,128]{1,0:T(8,128)(2,1)S(1)} %get-tuple-element.37), channel_id=1, source_target_pairs={{0,2},{1,3},{2,0},{3,1},{4,6},{5,7},{6,4},{7,5},{8,10},{9,11},{10,... | collective-permute-start | bytes 393224 | tf_op jit(solution)/shard_map/ppermute | solution.py:27
  49.0 11.1 %collective-permute-start.13 = (bf16[512,128]{1,0:T(8,128)(2,1)S(1)}, bf16[512,128]{1,0:T(8,128)(2,1)S(1)}, u32[]{:S(2)}, u32[]{:S(2)}) collective-permute-start(bf16[512,128]{1,0:T(8,128)(2,1)S(1)} %get-tuple-element.38), channel_id=1, source_target_pairs={{0,3},{1,2},{2,1},{3,0},{4,7},{5,6},{6,5},{7,4},{8,11},{9,10},{10,... | collective-permute-start | bytes 393224 | tf_op jit(solution)/shard_map/ppermute | solution.py:27
  51.5 9.9 %collective-permute-start.14 = (bf16[512,128]{1,0:T(8,128)(2,1)S(1)}, bf16[512,128]{1,0:T(8,128)(2,1)S(1)}, u32[]{:S(2)}, u32[]{:S(2)}) collective-permute-start(bf16[512,128]{1,0:T(8,128)(2,1)S(1)} %get-tuple-element.39), channel_id=1, source_target_pairs={{0,1},{1,0},{2,3},{3,2},{4,5},{5,4},{6,7},{7,6},{8,9},{9,8},{10,11... | collective-permute-start | bytes 393224 | tf_op jit(solution)/shard_map/ppermute | solution.py:27
  62.6 4.5 %collective-permute-start.17 = (bf16[8,3,128,256]{3,2,1,0:T(8,128)(2,1)S(1)}, bf16[8,3,128,256]{3,2,1,0:T(8,128)(2,1)S(1)}, u32[]{:S(2)}, u32[]{:S(2)}) collective-permute-start(bf16[8,3,128,256]{3,2,1,0:T(8,128)(2,1)S(1)} %get-tuple-element.42.refs_0_), channel_id=1, source_target_pairs={{0,4},{4,0},{8,12},{12,8},{16,20},{20,16},{24,28},{28,24},{1,5},{5... | collective-permute-start | bytes 4718600 | tf_op jit(solution)/shard_map/ppermute | solution.py:27
  62.7 12.9 %collective-permute-start.18 = (bf16[512,128]{1,0:T(8,128)(2,1)S(1)}, bf16[512,128]{1,0:T(8,128)(2,1)S(1)}, u32[]{:S(2)}, u32[]{:S(2)}) collective-permute-start(bf16[512,128]{1,0:T(8,128)(2,1)S(1)} %get-tuple-element.46), channel_id=1, source_target_pairs={{0,2},{1,3},{2,0},{3,1},{4,6},{5,7},{6,4},{7,5},{8,10},{9,11},{10,... | collective-permute-start | bytes 393224 | tf_op jit(solution)/shard_map/ppermute | solution.py:27
  64.7 11.0 %collective-permute-start.19 = (bf16[512,128]{1,0:T(8,128)(2,1)S(1)}, bf16[512,128]{1,0:T(8,128)(2,1)S(1)}, u32[]{:S(2)}, u32[]{:S(2)}) collective-permute-start(bf16[512,128]{1,0:T(8,128)(2,1)S(1)} %get-tuple-element.47), channel_id=1, source_target_pairs={{0,3},{1,2},{2,1},{3,0},{4,7},{5,6},{6,5},{7,4},{8,11},{9,10},{10,... | collective-permute-start | bytes 393224 | tf_op jit(solution)/shard_map/ppermute | solution.py:27
  67.1 9.4 %collective-permute-start.20 = (bf16[512,128]{1,0:T(8,128)(2,1)S(1)}, bf16[512,128]{1,0:T(8,128)(2,1)S(1)}, u32[]{:S(2)}, u32[]{:S(2)}) collective-permute-start(bf16[512,128]{1,0:T(8,128)(2,1)S(1)} %get-tuple-element.48), channel_id=1, source_target_pairs={{0,1},{1,0},{2,3},{3,2},{4,5},{5,4},{6,7},{7,6},{8,9},{9,8},{10,11... | collective-permute-start | bytes 393224 | tf_op jit(solution)/shard_map/ppermute | solution.py:27
  (9 other events, 125.5 us)

commit v9 on v8

--- a/solution.py
+++ b/solution.py
@@ -9,8 +9,6 @@
 
 HEADS = 4
 SPREAD = 8
-IN_BITS = (0, 2, 4, 6)
-OUT_BITS = (0, 4, 2, 6)
 LANES = 128
 F32 = jnp.float32
 BF16 = jnp.bfloat16
@@ -27,6 +25,12 @@
     return lax.ppermute(value, axis, [(source, source ^ bits) for source in range(count)])
 
 
+def crossed(value, axis, even_bits, odd_bits):
+    count = lax.axis_size(axis)
+    pairs = [(source, source ^ (odd_bits if source % 2 else even_bits)) for source in range(count)]
+    return lax.ppermute(value, axis, pairs)
+
+
 def steps_over(count):
     half = count // 2
     return tuple(range(half, count)) + tuple(range(1, half))
@@ -38,7 +42,8 @@
 
 
 def quarter_of(block):
-    return lax.rem(block, 2) + 2 * lax.rem(lax.div(block, 4), 2)
+    core = lax.rem(block, 2)
+    return (1 - core) * lax.rem(lax.div(block, 2), 2) + core * (2 + lax.rem(lax.div(block, 4), 2))
 
 
 def row_sum(value):
@@ -55,26 +60,27 @@
             normed[row : row + zone_rows, :] = rms_scale(block[step].astype(F32), gain).astype(BF16)
 
 
-def split_kernel(place, packed, states, before, *refs):
-    arrived, (direct, packed_out, last) = refs[:-3], refs[-3:]
+def split_kernel(place, packed, beside, states, before, *refs):
+    arrived, (direct, upper, lower, doubled, last) = refs[:-5], refs[-5:]
+    half = upper.shape[1]
     for index, piece in enumerate(arrived):
         direct[index] = piece[...]
-    packed_out[...] = packed[...]
+        upper[index] = piece[:half, :]
+        lower[index] = piece[half:, :]
+    doubled[0] = packed[...]
+    doubled[1] = beside[...]
     last[...] = jnp.where(lax.rem(place[0], 2) == 1, before[...], states[...])
 
 
-def gather_kernel(normed, direct, over, *refs):
-    across, (quarters, first_out, second_out) = refs[:-3], refs[-3:]
-    quarters[0] = direct[...]
-    quarters[1] = over[...]
-    split = first_out.shape[1]
-    for index, piece in enumerate(across):
-        first_out[index] = piece[:split, :]
-        second_out[index] = piece[split:, :]
+def stack_kernel(doubled, arrived, *refs):
+    out = refs[-1]
+    near = doubled.shape[0]
+    out[: near - 1] = doubled[1:]
+    out[near - 1 :] = arrived[...]
 
 
 def attention_kernel(zones, reach, steps, place, pattern, normed, own_qkv, own_attn, *refs):
-    quarters, (context_out, attn_out, weights, w_turned, projected, context, sems) = refs[:-7], refs[-7:]
+    pieces, (context_out, attn_out, weights, w_turned, projected, context, sems) = refs[:-7], refs[-7:]
     key_count = (reach + 1) * steps
     zone_rows = normed.shape[0] // key_count
     width = normed.shape[1]
@@ -94,12 +100,15 @@
     copies.append(pltpu.make_async_copy(own_attn, weights.at[3, own_rows, :], sems.at[3]))
     for copy in copies:
         copy.start()
-    my_quarter = quarter_of(my_block)
+    half = shard // 2
+    mine, other = quarter_of(my_block), quarter_of(my_block ^ 1)
     for place_in, step in enumerate(steps_over(zones)):
-        rows = pl.ds(pl.multiple_of((my_zone ^ step) * shard, shard), shard)
-        for core, pair in enumerate(quarters):
-            for index in range(2):
-                weights[my_quarter ^ (core + 2 * index), rows, :] = pair[index, place_in]
+        start = (my_zone ^ step) * shard
+        for piece, quarter, low in zip(
+            pieces, (mine, mine ^ 1, mine ^ 1, other, other ^ 1, other ^ 1), (0, 0, half, 0, 0, half)
+        ):
+            rows = pl.ds(pl.multiple_of(start + low, half), piece.shape[1])
+            weights[quarter, rows, :] = piece[place_in]
     for copy in copies:
         copy.wait()
     attn_out[...] = weights[3]
@@ -186,11 +195,11 @@
 
 
 def project_kernel(place, states, context, w_attn, gain_mix, *refs):
-    halves, (after_out, *outs, pair_in, pair_out, parts) = refs[:4], refs[4:]
+    halves, (after_out, *outs, pair, parts) = refs[:2], refs[2:]
     steps, zone_rows, _ = states.shape
     zones, _, part = parts.shape
     for index, value in enumerate(halves):
-        (pair_in, pair_out)[index // 2][index % 2] = value[...]
+        pair[index] = value[...]
     my_zone = place[1]
     gain = gain_mix[...]
     for step in range(steps):
@@ -207,7 +216,7 @@
 
 
 def mixing_kernel(steps, zones, place, neighbours, degree, mix, *refs):
-    arrived, pairs, (*outs, gathered, items) = refs[:zones], refs[zones : zones + 4], refs[zones + 4 :]
+    arrived, pairs, (*outs, gathered, items) = refs[:zones], refs[zones : zones + 2], refs[zones + 2 :]
     for index, pair in enumerate(pairs):
         gathered[2 * index : 2 * index + 2] = pair[...]
     _, slots, zone_rows, _ = mix.shape
@@ -264,19 +273,20 @@
     copies.append(pltpu.make_async_copy(own_out, w_out.at[own_rows, :], sems.at[SPREAD]))
     for copy in copies:
         copy.start()
-    for core, pieces in enumerate(gathered):
-        for index in range(4):
-            slot_in = lax.rem(my_block, SPREAD) ^ (IN_BITS[index] + core)
-            slot_out = lax.rem(my_block, SPREAD) ^ (OUT_BITS[index] + core)
-            for place_in, step in enumerate(steps_over(zones)):
+    for pieces, block in zip(gathered, (my_block, my_block ^ 1)):
+        near = 2 + 2 * lax.rem(block, 2)
+        for index, bits in enumerate((0, near, 6 - near, 6)):
+            slot = lax.rem(block, SPREAD) ^ bits
+            for step in range(1, zones):
                 source = my_zone ^ step
+                piece = pieces.at[index, step - 1]
                 rows = pl.ds(pl.multiple_of(source * in_shard, in_shard), in_shard)
-                w_in[slot_in, rows, :] = pieces[index, place_in]
-                first = pl.multiple_of(source * out_shard + slot_out * out_rows, out_rows)
+                w_in[slot, rows, :] = piece[:in_shard, :]
+                first = pl.multiple_of(source * out_shard + slot * out_rows, out_rows)
                 for fold in range(width // in_cols):
                     cols = slice(fold * in_cols, (fold + 1) * in_cols)
-                    rows = slice(fold * out_rows, (fold + 1) * out_rows)
-                    w_out[pl.ds(first, out_rows), cols] = pieces[4 + index, place_in, rows, :]
+                    low = in_shard + fold * out_rows
+                    w_out[pl.ds(first, out_rows), cols] = piece[low : low + out_rows, :]
     for copy in copies:
         copy.wait()
 
@@ -359,27 +369,29 @@
     slot = my_block % SPREAD
     slice_in = lax.dynamic_slice_in_dim(w_in, slot * in_cols, in_cols, axis=1)
     slice_out = lax.dynamic_slice_in_dim(w_out, slot * out_rows, out_rows, axis=0)
-    in_shard = w_in.shape[0]
-    sizes = (in_shard, out_rows * (width // in_cols))
     packed = jnp.concatenate(
         [slice_in] + [slice_out[:, at : at + in_cols] for at in range(0, width, in_cols)], axis=0
     )
-    direct, packed, last = call(
+    beside = swapped(packed, "zone", 1)
+    half_shape = jax.ShapeDtypeStruct((zones - 1, first.shape[0] // 2, width), BF16)
+    direct, upper, lower, doubled, last = call(
         split_kernel,
         (
             jax.ShapeDtypeStruct((zones - 1,) + first.shape, BF16),
-            jax.ShapeDtypeStruct(packed.shape, BF16),
+            half_shape,
+            half_shape,
+            jax.ShapeDtypeStruct((2,) + packed.shape, BF16),
             jax.ShapeDtypeStruct(states.shape, BF16),
         ),
         [],
         (0,),
         (),
         4,
-        [place, packed, states, before] + direct,
-    )
-    over = swapped(direct, "tm", 4)
+        [place, packed, beside, states, before] + direct,
+    )
+    over = [crossed(value, "tm", 2, 4) for value in (upper, lower)]
     last = swapped(last, "tm", 1)
-    across = [swapped(packed, "zone", step) for step in exchanges]
+    pieces = [direct] + over + [swapped(value, "tm", 1) for value in [direct] + over]
     normed = call(
         norm_kernel,
         jax.ShapeDtypeStruct((key_count * zone_rows, width), BF16),
@@ -389,19 +401,21 @@
         4,
         [before, last, states, gain_attn.reshape(1, -1)],
     )
-
-    quarters, part_in, part_out = call(
-        gather_kernel,
-        (jax.ShapeDtypeStruct((2,) + direct.shape, BF16),)
-        + tuple(jax.ShapeDtypeStruct((zones - 1, size, in_cols), BF16) for size in sizes),
+    bits = 2
+    while 2 * bits < zones:
+        doubled = jnp.concatenate([doubled, swapped(doubled, "zone", bits)], axis=0)
+        bits *= 2
+    across = call(
+        stack_kernel,
+        jax.ShapeDtypeStruct((zones - 1,) + packed.shape, BF16),
         [],
         (),
         (),
         4,
-        [normed, direct, over] + across,
-    )
-    quarters = [quarters, swapped(quarters, "tm", 1)]
-    over_in, over_out = swapped(part_in, "tm", 2), swapped(part_out, "tm", 4)
+        [doubled, swapped(doubled, "zone", bits), normed] + pieces[3:],
+    )
+    nearest = crossed(across, "tm", 2, 4)
+
     context, w_attn = call(
         functools.partial(attention_kernel, zones, reach, steps),
         (
@@ -418,37 +432,35 @@
         (0, 1),
         (3, 4),
         22,
-        [place, pattern, normed, w_qkv, w_out_attn] + quarters,
+        [place, pattern, normed, w_qkv, w_out_attn] + pieces,
     )
 
     chunk = jax.ShapeDtypeStruct((rows, part), BF16)
-    after_attn, *chunks, pair_in, pair_out = call(
+    after_attn, *chunks, pair = call(
         project_kernel,
         (jax.ShapeDtypeStruct((rows, width), F32),)
         + (chunk,) * zones
-        + tuple(jax.ShapeDtypeStruct((2, zones - 1, size, in_cols), BF16) for size in sizes),
+        + (jax.ShapeDtypeStruct((2,) + across.shape, BF16),),
         [pltpu.VMEM((zones, rows, part), BF16)],
         (0,),
         (),
         8,
         [place, states, context, w_attn, gain_mix.reshape(1, -1)]
-        + [part_in, over_in, part_out, over_out],
+        + [across, nearest],
     )
     arrived = [chunks[0]] + [
         swapped(value, "zone", step) for value, step in zip(chunks[1:], exchanges)
     ]
 
-    pairs = [pair_in, swapped(pair_in, "tm", 4), pair_out, swapped(pair_out, "tm", 2)]
-
     *spatial, gathered = call(
         functools.partial(mixing_kernel, steps, zones),
         (chunk,) * zones
-        + (jax.ShapeDtypeStruct((SPREAD, zones - 1, in_shard, in_cols), BF16),),
+        + (jax.ShapeDtypeStruct((4,) + across.shape, BF16),),
         [pltpu.VMEM((zones, rows, part), BF16)],
         (0, 1, 2),
         (),
         8,
-        [place, neighbours, degree, mix] + arrived + pairs,
+        [place, neighbours, degree, mix] + arrived + [pair, crossed(pair, "tm", 4, 2)],
     )
     full_in, full_out = call(
         functools.partial(order_kernel, zones),

time: 81 us -> 81.5 us (level)
  waiting for transfers between devices: 36.8 us -> 39.1 us
  starting transfers between devices: 27 us -> 25.3 us
    ppermute x20 -> x16, starting transfers between devices: 22 us -> 15.1 us  [swapped(): lax.ppermute(value, axis, [(source, source ^ bits) for source in range(co...]
    ppermute x0 -> x4, waiting for transfers between devices: none -> 5.73 us  [crossed(): return lax.ppermute(value, axis, pairs)]
    ppermute x0 -> x4, starting transfers between devices: none -> 5.19 us  [crossed(): return lax.ppermute(value, axis, pairs)]
    ppermute x20 -> x16, waiting for transfers between devices: 36.8 us -> 33.3 us  [swapped(): lax.ppermute(value, axis, [(source, source ^ bits) for source in range(co...]
  transfers between devices with their start and end apart: 21 -> 21, of which waited for: 10 -> 11; matrix products, arithmetic and copies ran while one was open for 3% -> 3% of each run, Pallas kernels for 8% -> 8%
where the time goes in v9:
time: 81.5 us; the launch traced here: 81.2 us
  waiting for transfers between devices  39.1 us (48%)
  starting transfers between devices  25.3 us (31%)
  Pallas kernels  13.8 us (17%)
  local copies, waits for them, and re-layouts  1.69 us (2%)
  other arithmetic  1.05 us (1%)
    ppermute x16, waiting for transfers between devices, swapped(): lax.ppermute(value, axis, [(source, source ^ bits) for source in range(co...  33.3 us
    ppermute x16, starting transfers between devices, swapped(): lax.ppermute(value, axis, [(source, source ^ bits) for source in range(co...  15.1 us
    pallas_call x8, Pallas kernels, call(): pl.pallas_call(kernel, out_shape=out_shape, in_specs=[pl.BlockSpec(memory...  13.8 us
    ppermute x4, waiting for transfers between devices, crossed(): return lax.ppermute(value, axis, pairs)  5.73 us
    ppermute x4, starting transfers between devices, crossed(): return lax.ppermute(value, axis, pairs)  5.19 us
    ppermute x1, starting transfers between devices, shifted(): lax.ppermute(value, axis, [(source, source + steps) for source in range(c...  4.99 us
  transfers between devices with their start and end apart: 21, of which 11 were waited for; matrix products, arithmetic and copies ran while one was open for 3% of the time, Pallas kernels for 8%

profile of v9, /device:TPU:0, one launch (start us, length us, event | category | flops | bytes accessed | tf_op | source)
XLA Modules:
  0.0 81.2 jit_solution(10946808207240100337)
XLA Ops:
  0.0 5.0 %collective-permute-start = (bf16[4,128,512]{2,1,0:T(8,128)(2,1)}, bf16[4,128,512]{2,1,0:T(8,128)(2,1)S(1)}, u32[]{:S(2)}, u32[]{:S(2)}) collective-permute-start(bf16[4,128,512]{2,1,0:T(8,128)(2,1)} %states.3), channel_id=1, source_target_pairs={{0,8},{4,12},{8,16},{12,20},{16,24},{20,28},{1,9},{5,13},{9,17},{1... | collective-permute-start | bytes 1572872 | tf_op jit(solution)/shard_map/ppermute | solution.py:20
  6.0 3.7 %collective-permute-start.3 = (bf16[128,512]{1,0:T(8,128)(2,1)S(1)}, bf16[128,512]{1,0:T(8,128)(2,1)S(1)}, u32[]{:S(2)}, u32[]{:S(2)}) collective-permute-start(bf16[128,512]{1,0:T(8,128)(2,1)S(1)} %fusion), channel_id=1, source_target_pairs={{0,3},{1,2},{2,1},{3,0},{4,7},{5,6},{6,5},{7,4},{8,11},{9,10},{10,... | collective-permute-start | bytes 393224 | tf_op jit(solution)/shard_map/ppermute | solution.py:25
  12.1 1.3 %collective-permute-start.1 = (bf16[256,256]{1,0:T(8,128)(2,1)S(1)}, bf16[256,256]{1,0:T(8,128)(2,1)S(1)}, u32[]{:S(2)}, u32[]{:S(2)}) collective-permute-start(bf16[256,256]{1,0:T(8,128)(2,1)S(1)} %pad_maximum_fusion.packed), channel_id=1, source_target_pairs={{0,1},{1,0},{2,3},{3,2},{4,5},{5,4},{6,7},{7,6},{8,9},{9,8},{10,11... | collective-permute-start | bytes 393224 | tf_op jit(solution)/shard_map/ppermute | solution.py:25
  14.3 6.2 %collective-permute-done.2.refs_0_ = bf16[128,512]{1,0:T(8,128)(2,1)S(1)} collective-permute-done((bf16[128,512]{1,0:T(8,128)(2,1)S(1)}, bf16[128,512]{1,0:T(8,128)(2,1)S(1)}, u32[]{:S(2)}, u32[]{:S(2)}) %collective-permute-start.2) | collective-permute-done | bytes 131104 | tf_op jit(solution)/shard_map/ppermute | solution.py:25
  22.2 1.5 %collective-permute-start.6 = (bf16[3,64,512]{2,1,0:T(8,128)(2,1)S(1)}, bf16[3,64,512]{2,1,0:T(8,128)(2,1)S(1)}, u32[]{:S(2)}, u32[]{:S(2)}) collective-permute-start(bf16[3,64,512]{2,1,0:T(8,128)(2,1)S(1)} %get-tuple-element.27), channel_id=1, source_target_pairs={{0,8},{4,20},{8,0},{12,28},{16,24},{20,4},{24,16},{28,12},{1,9},{5... | collective-permute-start | bytes 589832 | tf_op jit(solution)/shard_map/ppermute | solution.py:31
  24.3 1.3 %collective-permute-start.11 = (bf16[2,256,256]{2,1,0:T(8,128)(2,1)S(1)}, bf16[2,256,256]{2,1,0:T(8,128)(2,1)S(1)}, u32[]{:S(2)}, u32[]{:S(2)}) collective-permute-start(bf16[2,256,256]{2,1,0:T(8,128)(2,1)S(1)} %get-tuple-element.31.doubled), channel_id=1, source_target_pairs={{0,2},{1,3},{2,0},{3,1},{4,6},{5,7},{6,4},{7,5},{8,10},{9,11},{10,... | collective-permute-start | bytes 786440 | tf_op jit(solution)/shard_map/ppermute | solution.py:25
  25.5 2.4 %collective-permute-done.6.refs_1_ = bf16[3,64,512]{2,1,0:T(8,128)(2,1)S(1)} collective-permute-done((bf16[3,64,512]{2,1,0:T(8,128)(2,1)S(1)}, bf16[3,64,512]{2,1,0:T(8,128)(2,1)S(1)}, u32[]{:S(2)}, u32[]{:S(2)}) %collective-permute-start.6) | collective-permute-done | bytes 196640 | tf_op jit(solution)/shard_map/ppermute | solution.py:31
  27.9 2.1 %collective-permute-done.7.refs_2_ = bf16[3,64,512]{2,1,0:T(8,128)(2,1)S(1)} collective-permute-done((bf16[3,64,512]{2,1,0:T(8,128)(2,1)S(1)}, bf16[3,64,512]{2,1,0:T(8,128)(2,1)S(1)}, u32[]{:S(2)}, u32[]{:S(2)}) %collective-permute-start.7) | collective-permute-done | bytes 196640 | tf_op jit(solution)/shard_map/ppermute | solution.py:31
  30.7 8.8 %collective-permute-done.11.arrived = bf16[2,256,256]{2,1,0:T(8,128)(2,1)S(1)} collective-permute-done((bf16[2,256,256]{2,1,0:T(8,128)(2,1)S(1)}, bf16[2,256,256]{2,1,0:T(8,128)(2,1)S(1)}, u32[]{:S(2)}, u32[]{:S(2)}) %collective-permute-start.11) | collective-permute-done | bytes 262176 | tf_op jit(solution)/shard_map/ppermute | solution.py:25
  39.6 1.5 %collective-permute-start.12 = (bf16[3,256,256]{2,1,0:T(8,128)(2,1)S(1)}, bf16[3,256,256]{2,1,0:T(8,128)(2,1)S(1)}, u32[]{:S(2)}, u32[]{:S(2)}) collective-permute-start(bf16[3,256,256]{2,1,0:T(8,128)(2,1)S(1)} %shard_map.121.refs_0_), channel_id=1, source_target_pairs={{0,8},{4,20},{8,0},{12,28},{16,24},{20,4},{24,16},{28,12},{1,9},{5... | collective-permute-start | bytes 1179656 | tf_op jit(solution)/shard_map/ppermute | solution.py:31
  41.1 5.0 %shard_map.120 = (bf16[512,512]{1,0:T(8,128)(2,1)S(1)}, bf16[512,512]{1,0:T(8,128)(2,1)S(1)}) custom-call(s32[2]{0:T(128)S(1)} %pad_add_fusion.place, s32[1,2]{1,0:T(1,128)S(1)} %copy-done.10, bf16[1536,512]{1,0:T(8,128)(2,1)S(1)} %shard_map.119.normed.refs_0_, bf16[128,1536]{1,0:T(8,128)(2,1)S(1)} %copy-done.1, bf16[128,512]{1,0:T(8,128)(2,1)S(1)} %copy-done.4, ...), custom_call_target="tpu_custom_call" | custom-call | tf_op jit(solution)/shard_map/pallas_call | solution.py:324
  46.1 1.3 %collective-permute-done.12.refs_1_ = bf16[3,256,256]{2,1,0:T(8,128)(2,1)S(1)} collective-permute-done((bf16[3,256,256]{2,1,0:T(8,128)(2,1)S(1)}, bf16[3,256,256]{2,1,0:T(8,128)(2,1)S(1)}, u32[]{:S(2)}, u32[]{:S(2)}) %collective-permute-start.12) | collective-permute-done | bytes 393248 | tf_op jit(solution)/shard_map/ppermute | solution.py:31
  47.4 1.2 %shard_map.122 = (f32[512,512]{1,0:T(8,128)S(1)}, bf16[512,128]{1,0:T(8,128)(2,1)S(1)}, bf16[512,128]{1,0:T(8,128)(2,1)S(1)}, bf16[512,128]{1,0:T(8,128)(2,1)S(1...) custom-call(s32[2]{0:T(128)S(1)} %pad_add_fusion.place, bf16[4,128,512]{2,1,0:T(8,128)(2,1)S(1)} %copy-done, ...), custom_call_target="tpu_custom_call" | custom-call | tf_op jit(solution)/shard_map/pallas_call | solution.py:324
  48.6 1.6 %collective-permute-start.16 = (bf16[2,3,256,256]{3,2,1,0:T(8,128)(2,1)S(1)}, bf16[2,3,256,256]{3,2,1,0:T(8,128)(2,1)S(1)}, u32[]{:S(2)}, u32[]{:S(2)}) collective-permute-start(bf16[2,3,256,256]{3,2,1,0:T(8,128)(2,1)S(1)} %get-tuple-element.37.refs_4_), channel_id=1, source_target_pairs={{0,16},{4,12},{8,24},{12,4},{16,0},{20,28},{24,8},{28,20},{1,17},{... | collective-permute-start | bytes 2359304 | tf_op jit(solution)/shard_map/ppermute | solution.py:31
  50.2 2.2 %collective-permute-start.14 = (bf16[512,128]{1,0:T(8,128)(2,1)S(1)}, bf16[512,128]{1,0:T(8,128)(2,1)S(1)}, u32[]{:S(2)}, u32[]{:S(2)}) collective-permute-start(bf16[512,128]{1,0:T(8,128)(2,1)S(1)} %get-tuple-element.35), channel_id=1, source_target_pairs={{0,3},{1,2},{2,1},{3,0},{4,7},{5,6},{6,5},{7,4},{8,11},{9,10},{10,... | collective-permute-start | bytes 393224 | tf_op jit(solution)/shard_map/ppermute | solution.py:25
  52.4 1.3 %collective-permute-start.15 = (bf16[512,128]{1,0:T(8,128)(2,1)S(1)}, bf16[512,128]{1,0:T(8,128)(2,1)S(1)}, u32[]{:S(2)}, u32[]{:S(2)}) collective-permute-start(bf16[512,128]{1,0:T(8,128)(2,1)S(1)} %get-tuple-element.36), channel_id=1, source_target_pairs={{0,1},{1,0},{2,3},{3,2},{4,5},{5,4},{6,7},{7,6},{8,9},{9,8},{10,11... | collective-permute-start | bytes 393224 | tf_op jit(solution)/shard_map/ppermute | solution.py:25
  53.7 7.0 %collective-permute-done.13.refs_1_ = bf16[512,128]{1,0:T(8,128)(2,1)S(1)} collective-permute-done((bf16[512,128]{1,0:T(8,128)(2,1)S(1)}, bf16[512,128]{1,0:T(8,128)(2,1)S(1)}, u32[]{:S(2)}, u32[]{:S(2)}) %collective-permute-start.13) | collective-permute-done | bytes 131104 | tf_op jit(solution)/shard_map/ppermute | solution.py:25
  60.6 1.3 %collective-permute-done.15.refs_3_ = bf16[512,128]{1,0:T(8,128)(2,1)S(1)} collective-permute-done((bf16[512,128]{1,0:T(8,128)(2,1)S(1)}, bf16[512,128]{1,0:T(8,128)(2,1)S(1)}, u32[]{:S(2)}, u32[]{:S(2)}) %collective-permute-start.15) | collective-permute-done | bytes 131104 | tf_op jit(solution)/shard_map/ppermute | solution.py:25
  61.9 1.2 %shard_map.123 = (bf16[512,128]{1,0:T(8,128)(2,1)S(1)}, bf16[512,128]{1,0:T(8,128)(2,1)S(1)}, bf16[512,128]{1,0:T(8,128)(2,1)S(1)}, bf16[512,128]{1,0:T(8,128)(2,1)S(1)}, bf16[4,3,256,256]{3,2,1,0:T(8,128)(2,1)S(1)}) custom-call(s32[2]{0:T(128)S(1)} %pad_add_fusion.place, s32[4,3]{1,0:T(4,128)S(1)} %copy-done.9, s32[4]{0:T(128)S(1)} %copy-done.11, ...), custom_call_target="tpu_custom_call" | custom-call | tf_op jit(solution)/shard_map/pallas_call | solution.py:324
  63.2 1.9 %collective-permute-start.18 = (bf16[512,128]{1,0:T(8,128)(2,1)S(1)}, bf16[512,128]{1,0:T(8,128)(2,1)S(1)}, u32[]{:S(2)}, u32[]{:S(2)}) collective-permute-start(bf16[512,128]{1,0:T(8,128)(2,1)S(1)} %get-tuple-element.42), channel_id=1, source_target_pairs={{0,2},{1,3},{2,0},{3,1},{4,6},{5,7},{6,4},{7,5},{8,10},{9,11},{10,... | collective-permute-start | bytes 393224 | tf_op jit(solution)/shard_map/ppermute | solution.py:25
  65.1 2.5 %collective-permute-start.19 = (bf16[512,128]{1,0:T(8,128)(2,1)S(1)}, bf16[512,128]{1,0:T(8,128)(2,1)S(1)}, u32[]{:S(2)}, u32[]{:S(2)}) collective-permute-start(bf16[512,128]{1,0:T(8,128)(2,1)S(1)} %get-tuple-element.43), channel_id=1, source_target_pairs={{0,3},{1,2},{2,1},{3,0},{4,7},{5,6},{6,5},{7,4},{8,11},{9,10},{10,... | collective-permute-start | bytes 393224 | tf_op jit(solution)/shard_map/ppermute | solution.py:25
  67.7 1.0 %shard_map.124 = (bf16[8,512,256]{2,1,0:T(8,128)(2,1)S(1)}, bf16[2048,512]{1,0:T(8,128)(2,1)S(1)}) custom-call(s32[2]{0:T(128)S(1)} %pad_add_fusion.place, bf16[128,2048]{1,0:T(8,128)(2,1)S(1)} %copy-done.3, bf16[512,512]{1,0:T(8,128)(2,1)S(1)} %copy-done.2, bf16[4,3,256,256]{3,2,1,0:T(8,128)(2,1)S(1)} %get-tuple-element.38.refs_0_, ...), custom_call_target="tpu_custom_call" | custom-call | tf_op jit(solution)/shard_map/pallas_call | solution.py:324
  68.6 7.5 %collective-permute-done.18.refs_1_ = bf16[512,128]{1,0:T(8,128)(2,1)S(1)} collective-permute-done((bf16[512,128]{1,0:T(8,128)(2,1)S(1)}, bf16[512,128]{1,0:T(8,128)(2,1)S(1)}, u32[]{:S(2)}, u32[]{:S(2)}) %collective-permute-start.18) | collective-permute-done | bytes 131104 | tf_op jit(solution)/shard_map/ppermute | solution.py:25
  77.0 4.2 %shard_map.125 = bf16[512,512]{1,0:T(8,128)(2,1)} custom-call(s32[2]{0:T(128)S(1)} %pad_add_fusion.place, f32[512,512]{1,0:T(8,128)S(1)} %get-tuple-element.32.after_attn, f32[1,512]{1,0:T(1,128)S(1)} %bitcast.6, bf16[8,512,256]{2,1,0:T(8,128)(2,1)S(1)} %get-tuple-element.39.w_in, bf16[2048,512]{1,0:T(8,128)(2,1)S(1)} %get-tuple-element.40.w_out, ...), custom_call_target="tpu_custom_call" | custom-call | tf_op jit(solution)/shard_map/pallas_call | solution.py:324
  (55 shorter events, 8.2 us)
Async XLA Ops:
  0.0 21.4 %copy-start = (bf16[4,128,512]{2,1,0:T(8,128)(2,1)S(1)}, bf16[4,128,512]{2,1,0:T(8,128)(2,1)}, u32[]{:S(2)}) copy-start(bf16[4,128,512]{2,1,0:T(8,128)(2,1)} %states.3) | copy-start | bytes 1572868
  0.0 30.0 %copy-start.7 = (f32[512]{0:T(512)S(1)}, f32[512]{0:T(512)}, u32[]{:S(2)}) copy-start(f32[512]{0:T(512)} %param.13) | copy-start | bytes 6148
  0.0 21.4 %collective-permute-start = (bf16[4,128,512]{2,1,0:T(8,128)(2,1)}, bf16[4,128,512]{2,1,0:T(8,128)(2,1)S(1)}, u32[]{:S(2)}, u32[]{:S(2)}) collective-permute-start(bf16[4,128,512]{2,1,0:T(8,128)(2,1)} %states.3), channel_id=1, source_target_pairs={{0,8},{4,12},{8,16},{12,20},{16,24},{20,28},{1,9},{5,13},{9,17},{1... | collective-permute-start | bytes 1572872 | tf_op jit(solution)/shard_map/ppermute | solution.py:20
  6.0 8.3 %collective-permute-start.3 = (bf16[128,512]{1,0:T(8,128)(2,1)S(1)}, bf16[128,512]{1,0:T(8,128)(2,1)S(1)}, u32[]{:S(2)}, u32[]{:S(2)}) collective-permute-start(bf16[128,512]{1,0:T(8,128)(2,1)S(1)} %fusion), channel_id=1, source_target_pairs={{0,3},{1,2},{2,1},{3,0},{4,7},{5,6},{6,5},{7,4},{8,11},{9,10},{10,... | collective-permute-start | bytes 393224 | tf_op jit(solution)/shard_map/ppermute | solution.py:25
  9.7 10.9 %collective-permute-start.2 = (bf16[128,512]{1,0:T(8,128)(2,1)S(1)}, bf16[128,512]{1,0:T(8,128)(2,1)S(1)}, u32[]{:S(2)}, u32[]{:S(2)}) collective-permute-start(bf16[128,512]{1,0:T(8,128)(2,1)S(1)} %fusion), channel_id=1, source_target_pairs={{0,2},{1,3},{2,0},{3,1},{4,6},{5,7},{6,4},{7,5},{8,10},{9,11},{10,... | collective-permute-start | bytes 393224 | tf_op jit(solution)/shard_map/ppermute | solution.py:25
  9.7 10.9 %collective-permute-start.4 = (bf16[128,512]{1,0:T(8,128)(2,1)S(1)}, bf16[128,512]{1,0:T(8,128)(2,1)S(1)}, u32[]{:S(2)}, u32[]{:S(2)}) collective-permute-start(bf16[128,512]{1,0:T(8,128)(2,1)S(1)} %fusion), channel_id=1, source_target_pairs={{0,1},{1,0},{2,3},{3,2},{4,5},{5,4},{6,7},{7,6},{8,9},{9,8},{10,11... | collective-permute-start | bytes 393224 | tf_op jit(solution)/shard_map/ppermute | solution.py:25
  12.1 9.3 %collective-permute-start.1 = (bf16[256,256]{1,0:T(8,128)(2,1)S(1)}, bf16[256,256]{1,0:T(8,128)(2,1)S(1)}, u32[]{:S(2)}, u32[]{:S(2)}) collective-permute-start(bf16[256,256]{1,0:T(8,128)(2,1)S(1)} %pad_maximum_fusion.packed), channel_id=1, source_target_pairs={{0,1},{1,0},{2,3},{3,2},{4,5},{5,4},{6,7},{7,6},{8,9},{9,8},{10,11... | collective-permute-start | bytes 393224 | tf_op jit(solution)/shard_map/ppermute | solution.py:25
  22.1 7.9 %collective-permute-start.5 = (bf16[4,128,512]{2,1,0:T(8,128)(2,1)S(1)}, bf16[4,128,512]{2,1,0:T(8,128)(2,1)S(1)}, u32[]{:S(2)}, u32[]{:S(2)}) collective-permute-start(bf16[4,128,512]{2,1,0:T(8,128)(2,1)S(1)} %get-tuple-element.25), channel_id=1, source_target_pairs={{0,4},{4,0},{8,12},{12,8},{16,20},{20,16},{24,28},{28,24},{1,5},{5... | collective-permute-start | bytes 1572872 | tf_op jit(solution)/shard_map/ppermute | solution.py:25
  22.2 5.7 %collective-permute-start.6 = (bf16[3,64,512]{2,1,0:T(8,128)(2,1)S(1)}, bf16[3,64,512]{2,1,0:T(8,128)(2,1)S(1)}, u32[]{:S(2)}, u32[]{:S(2)}) collective-permute-start(bf16[3,64,512]{2,1,0:T(8,128)(2,1)S(1)} %get-tuple-element.27), channel_id=1, source_target_pairs={{0,8},{4,20},{8,0},{12,28},{16,24},{20,4},{24,16},{28,12},{1,9},{5... | collective-permute-start | bytes 589832 | tf_op jit(solution)/shard_map/ppermute | solution.py:31
  23.7 6.3 %collective-permute-start.7 = (bf16[3,64,512]{2,1,0:T(8,128)(2,1)S(1)}, bf16[3,64,512]{2,1,0:T(8,128)(2,1)S(1)}, u32[]{:S(2)}, u32[]{:S(2)}) collective-permute-start(bf16[3,64,512]{2,1,0:T(8,128)(2,1)S(1)} %get-tuple-element.28), channel_id=1, source_target_pairs={{0,8},{4,20},{8,0},{12,28},{16,24},{20,4},{24,16},{28,12},{1,9},{5... | collective-permute-start | bytes 589832 | tf_op jit(solution)/shard_map/ppermute | solution.py:31
  24.3 15.2 %collective-permute-start.8 = (bf16[3,128,512]{2,1,0:T(8,128)(2,1)S(1)}, bf16[3,128,512]{2,1,0:T(8,128)(2,1)S(1)}, u32[]{:S(2)}, u32[]{:S(2)}) collective-permute-start(bf16[3,128,512]{2,1,0:T(8,128)(2,1)S(1)} %get-tuple-element.26.refs_0_), channel_id=1, source_target_pairs={{0,4},{4,0},{8,12},{12,8},{16,20},{20,16},{24,28},{28,24},{1,5},{5... | collective-permute-start | bytes 1179656 | tf_op jit(solution)/shard_map/ppermute | solution.py:25
  24.3 15.2 %collective-permute-start.11 = (bf16[2,256,256]{2,1,0:T(8,128)(2,1)S(1)}, bf16[2,256,256]{2,1,0:T(8,128)(2,1)S(1)}, u32[]{:S(2)}, u32[]{:S(2)}) collective-permute-start(bf16[2,256,256]{2,1,0:T(8,128)(2,1)S(1)} %get-tuple-element.31.doubled), channel_id=1, source_target_pairs={{0,2},{1,3},{2,0},{3,1},{4,6},{5,7},{6,4},{7,5},{8,10},{9,11},{10,... | collective-permute-start | bytes 786440 | tf_op jit(solution)/shard_map/ppermute | solution.py:25
  27.9 11.6 %collective-permute-start.9 = (bf16[3,64,512]{2,1,0:T(8,128)(2,1)S(1)}, bf16[3,64,512]{2,1,0:T(8,128)(2,1)S(1)}, u32[]{:S(2)}, u32[]{:S(2)}) collective-permute-start(bf16[3,64,512]{2,1,0:T(8,128)(2,1)S(1)} %collective-permute-done.6.refs_1_), channel_id=1, source_target_pairs={{0,4},{4,0},{8,12},{12,8},{16,20},{20,16},{24,28},{28,24},{1,5},{5... | collective-permute-start | bytes 589832 | tf_op jit(solution)/shard_map/ppermute | solution.py:25
  30.0 9.5 %collective-permute-start.10 = (bf16[3,64,512]{2,1,0:T(8,128)(2,1)S(1)}, bf16[3,64,512]{2,1,0:T(8,128)(2,1)S(1)}, u32[]{:S(2)}, u32[]{:S(2)}) collective-permute-start(bf16[3,64,512]{2,1,0:T(8,128)(2,1)S(1)} %collective-permute-done.7.refs_2_), channel_id=1, source_target_pairs={{0,4},{4,0},{8,12},{12,8},{16,20},{20,16},{24,28},{28,24},{1,5},{5... | collective-permute-start | bytes 589832 | tf_op jit(solution)/shard_map/ppermute | solution.py:25
  39.6 7.8 %collective-permute-start.12 = (bf16[3,256,256]{2,1,0:T(8,128)(2,1)S(1)}, bf16[3,256,256]{2,1,0:T(8,128)(2,1)S(1)}, u32[]{:S(2)}, u32[]{:S(2)}) collective-permute-start(bf16[3,256,256]{2,1,0:T(8,128)(2,1)S(1)} %shard_map.121.refs_0_), channel_id=1, source_target_pairs={{0,8},{4,20},{8,0},{12,28},{16,24},{20,4},{24,16},{28,12},{1,9},{5... | collective-permute-start | bytes 1179656 | tf_op jit(solution)/shard_map/ppermute | solution.py:31
  48.6 19.1 %copy-start.2 = (bf16[512,512]{1,0:T(8,128)(2,1)S(1)}, bf16[512,512]{1,0:T(8,128)(2,1)}, u32[]{:S(2)}) copy-start(bf16[512,512]{1,0:T(8,128)(2,1)} %own_out.1) | copy-start | bytes 1572868
  48.6 13.3 %collective-permute-start.16 = (bf16[2,3,256,256]{3,2,1,0:T(8,128)(2,1)S(1)}, bf16[2,3,256,256]{3,2,1,0:T(8,128)(2,1)S(1)}, u32[]{:S(2)}, u32[]{:S(2)}) collective-permute-start(bf16[2,3,256,256]{3,2,1,0:T(8,128)(2,1)S(1)} %get-tuple-element.37.refs_4_), channel_id=1, source_target_pairs={{0,16},{4,12},{8,24},{12,4},{16,0},{20,28},{24,8},{28,20},{1,17},{... | collective-permute-start | bytes 2359304 | tf_op jit(solution)/shard_map/ppermute | solution.py:31
  50.2 10.5 %collective-permute-start.13 = (bf16[512,128]{1,0:T(8,128)(2,1)S(1)}, bf16[512,128]{1,0:T(8,128)(2,1)S(1)}, u32[]{:S(2)}, u32[]{:S(2)}) collective-permute-start(bf16[512,128]{1,0:T(8,128)(2,1)S(1)} %get-tuple-element.34), channel_id=1, source_target_pairs={{0,2},{1,3},{2,0},{3,1},{4,6},{5,7},{6,4},{7,5},{8,10},{9,11},{10,... | collective-permute-start | bytes 393224 | tf_op jit(solution)/shard_map/ppermute | solution.py:25
  50.2 10.5 %collective-permute-start.14 = (bf16[512,128]{1,0:T(8,128)(2,1)S(1)}, bf16[512,128]{1,0:T(8,128)(2,1)S(1)}, u32[]{:S(2)}, u32[]{:S(2)}) collective-permute-start(bf16[512,128]{1,0:T(8,128)(2,1)S(1)} %get-tuple-element.35), channel_id=1, source_target_pairs={{0,3},{1,2},{2,1},{3,0},{4,7},{5,6},{6,5},{7,4},{8,11},{9,10},{10,... | collective-permute-start | bytes 393224 | tf_op jit(solution)/shard_map/ppermute | solution.py:25
  52.4 9.5 %collective-permute-start.15 = (bf16[512,128]{1,0:T(8,128)(2,1)S(1)}, bf16[512,128]{1,0:T(8,128)(2,1)S(1)}, u32[]{:S(2)}, u32[]{:S(2)}) collective-permute-start(bf16[512,128]{1,0:T(8,128)(2,1)S(1)} %get-tuple-element.36), channel_id=1, source_target_pairs={{0,1},{1,0},{2,3},{3,2},{4,5},{5,4},{6,7},{7,6},{8,9},{9,8},{10,11... | collective-permute-start | bytes 393224 | tf_op jit(solution)/shard_map/ppermute | solution.py:25
  63.1 4.5 %collective-permute-start.17 = (bf16[4,3,256,256]{3,2,1,0:T(8,128)(2,1)S(1)}, bf16[4,3,256,256]{3,2,1,0:T(8,128)(2,1)S(1)}, u32[]{:S(2)}, u32[]{:S(2)}) collective-permute-start(bf16[4,3,256,256]{3,2,1,0:T(8,128)(2,1)S(1)} %get-tuple-element.38.refs_0_), channel_id=1, source_target_pairs={{0,4},{4,0},{8,12},{12,8},{16,20},{20,16},{24,28},{28,24},{1,5},{5... | collective-permute-start | bytes 4718600 | tf_op jit(solution)/shard_map/ppermute | solution.py:25
  63.2 12.9 %collective-permute-start.18 = (bf16[512,128]{1,0:T(8,128)(2,1)S(1)}, bf16[512,128]{1,0:T(8,128)(2,1)S(1)}, u32[]{:S(2)}, u32[]{:S(2)}) collective-permute-start(bf16[512,128]{1,0:T(8,128)(2,1)S(1)} %get-tuple-element.42), channel_id=1, source_target_pairs={{0,2},{1,3},{2,0},{3,1},{4,6},{5,7},{6,4},{7,5},{8,10},{9,11},{10,... | collective-permute-start | bytes 393224 | tf_op jit(solution)/shard_map/ppermute | solution.py:25
  65.1 11.0 %collective-permute-start.19 = (bf16[512,128]{1,0:T(8,128)(2,1)S(1)}, bf16[512,128]{1,0:T(8,128)(2,1)S(1)}, u32[]{:S(2)}, u32[]{:S(2)}) collective-permute-start(bf16[512,128]{1,0:T(8,128)(2,1)S(1)} %get-tuple-element.43), channel_id=1, source_target_pairs={{0,3},{1,2},{2,1},{3,0},{4,7},{5,6},{6,5},{7,4},{8,11},{9,10},{10,... | collective-permute-start | bytes 393224 | tf_op jit(solution)/shard_map/ppermute | solution.py:25
  67.6 9.4 %collective-permute-start.20 = (bf16[512,128]{1,0:T(8,128)(2,1)S(1)}, bf16[512,128]{1,0:T(8,128)(2,1)S(1)}, u32[]{:S(2)}, u32[]{:S(2)}) collective-permute-start(bf16[512,128]{1,0:T(8,128)(2,1)S(1)} %get-tuple-element.44), channel_id=1, source_target_pairs={{0,1},{1,0},{2,3},{3,2},{4,5},{5,4},{6,7},{7,6},{8,9},{9,8},{10,11... | collective-permute-start | bytes 393224 | tf_op jit(solution)/shard_map/ppermute | solution.py:25
  (9 other events, 115.0 us)

commit v10 on v9

--- a/solution.py
+++ b/solution.py
@@ -58,6 +58,24 @@
         for step in range(steps):
             row = (index * steps + step) * zone_rows
             normed[row : row + zone_rows, :] = rms_scale(block[step].astype(F32), gain).astype(BF16)
+
+
+def group_kernel(zones, place, w_in, w_out, own_in, packed):
+    in_shard, hidden = w_in.shape
+    out_rows = w_out.shape[0] // SPREAD
+    in_cols = hidden // SPREAD
+    width = w_out.shape[1]
+    for index in range(SPREAD):
+        for source in range(zones):
+            low = (source * SPREAD + index) * out_rows
+            to = slice(source * out_rows, (source + 1) * out_rows)
+            own_in[index, :, to] = w_in[:, low : low + out_rows]
+    slot = lax.rem(place[0], SPREAD)
+    packed[:in_shard, :] = own_in[slot]
+    rows = pl.ds(pl.multiple_of(slot * out_rows, out_rows), out_rows)
+    for fold in range(width // in_cols):
+        low = in_shard + fold * out_rows
+        packed[low : low + out_rows, :] = w_out[rows, fold * in_cols : (fold + 1) * in_cols]
 
 
 def split_kernel(place, packed, beside, states, before, *refs):
@@ -194,12 +212,10 @@
         context_out[rows, :] = context[:, rows].T.astype(BF16)
 
 
-def project_kernel(place, states, context, w_attn, gain_mix, *refs):
-    halves, (after_out, *outs, pair, parts) = refs[:2], refs[2:]
+def project_kernel(place, states, context, w_attn, gain_mix, after_out, *refs):
+    *outs, parts = refs
     steps, zone_rows, _ = states.shape
     zones, _, part = parts.shape
-    for index, value in enumerate(halves):
-        pair[index] = value[...]
     my_zone = place[1]
     gain = gain_mix[...]
     for step in range(steps):
@@ -216,9 +232,9 @@
 
 
 def mixing_kernel(steps, zones, place, neighbours, degree, mix, *refs):
-    arrived, pairs, (*outs, gathered, items) = refs[:zones], refs[zones : zones + 2], refs[zones + 2 :]
-    for index, pair in enumerate(pairs):
-        gathered[2 * index : 2 * index + 2] = pair[...]
+    arrived, halves, (*outs, pair, items) = refs[:zones], refs[zones : zones + 2], refs[zones + 2 :]
+    for index, value in enumerate(halves):
+        pair[index] = value[...]
     _, slots, zone_rows, _ = mix.shape
     part = items.shape[-1]
     my_zone = place[1]
@@ -252,53 +268,57 @@
                 outs[target][rows, :] = result[:, index * part : (index + 1) * part].astype(BF16)
 
 
-def order_kernel(zones, place, own_in, own_out, *refs):
-    gathered, (w_in, w_out, sems) = refs[:2], refs[2:]
-    width = own_out.shape[1]
-    my_block, my_zone = place[0], place[1]
-    in_shard, hidden = own_in.shape
-    out_shard = own_out.shape[0]
-    in_cols, out_rows = hidden // SPREAD, out_shard // SPREAD
-
+def slots_of(block):
+    near = 2 + 2 * lax.rem(block, 2)
+    return [lax.rem(block, SPREAD) ^ bits for bits in (0, near, 6 - near, 6)]
+
+
+def fill_slots(zones, place, own_in, own_out, slots, pieces, w_in, w_out, sems):
+    my_zone = place[1]
+    in_shard = own_in.shape[1]
+    out_rows = own_out.shape[0] // SPREAD
+    in_cols, width = own_in.shape[2], own_out.shape[1]
     own_rows = pl.ds(pl.multiple_of(my_zone * in_shard, in_shard), in_shard)
-    copies = [
-        pltpu.make_async_copy(
-            own_in.at[:, index * in_cols : (index + 1) * in_cols],
-            w_in.at[index, own_rows, :],
-            sems.at[index],
-        )
-        for index in range(SPREAD)
-    ]
-    own_rows = pl.ds(pl.multiple_of(my_zone * out_shard, out_shard), out_shard)
-    copies.append(pltpu.make_async_copy(own_out, w_out.at[own_rows, :], sems.at[SPREAD]))
+    own_out_rows = pl.ds(pl.multiple_of(my_zone * out_rows, out_rows), out_rows)
+    copies = []
+    for index, slot in enumerate(slots):
+        from_rows = pl.ds(pl.multiple_of(slot * out_rows, out_rows), out_rows)
+        copies += [
+            pltpu.make_async_copy(own_in.at[slot], w_in.at[index, own_rows, :], sems.at[2 * index]),
+            pltpu.make_async_copy(
+                own_out.at[from_rows, :], w_out.at[index, own_out_rows, :], sems.at[2 * index + 1]
+            ),
+        ]
     for copy in copies:
         copy.start()
-    for pieces, block in zip(gathered, (my_block, my_block ^ 1)):
-        near = 2 + 2 * lax.rem(block, 2)
-        for index, bits in enumerate((0, near, 6 - near, 6)):
-            slot = lax.rem(block, SPREAD) ^ bits
-            for step in range(1, zones):
-                source = my_zone ^ step
-                piece = pieces.at[index, step - 1]
-                rows = pl.ds(pl.multiple_of(source * in_shard, in_shard), in_shard)
-                w_in[slot, rows, :] = piece[:in_shard, :]
-                first = pl.multiple_of(source * out_shard + slot * out_rows, out_rows)
-                for fold in range(width // in_cols):
-                    cols = slice(fold * in_cols, (fold + 1) * in_cols)
-                    low = in_shard + fold * out_rows
-                    w_out[pl.ds(first, out_rows), cols] = piece[low : low + out_rows, :]
+    for index, piece in enumerate(pieces):
+        for step in range(1, zones):
+            source = my_zone ^ step
+            part = piece[step - 1]
+            rows = pl.ds(pl.multiple_of(source * in_shard, in_shard), in_shard)
+            w_in[index, rows, :] = part[:in_shard, :]
+            rows = pl.ds(pl.multiple_of(source * out_rows, out_rows), out_rows)
+            for fold in range(width // in_cols):
+                low = in_shard + fold * out_rows
+                w_out[index, rows, fold * in_cols : (fold + 1) * in_cols] = part[low : low + out_rows, :]
     for copy in copies:
         copy.wait()
 
 
-def ffn_kernel(zones, place, after_attn, gain_ffn, w_in, w_out, *refs):
-    arrived, (out, after_mix, ffn_in, parts, hidden) = refs[:zones], refs[zones:]
+def order_kernel(zones, place, own_in, own_out, pair, far, swapped_pair, w_in, w_out, sems):
+    my_block = place[0]
+    slots = slots_of(my_block) + slots_of(my_block ^ 1)[:2]
+    pieces = [group.at[index] for group in (pair, far, swapped_pair) for index in range(2)]
+    fill_slots(zones, place, own_in, own_out, slots, pieces, w_in, w_out, sems)
+
+
+def after_kernel(zones, place, after_attn, gain_ffn, ready, far, *refs):
+    arrived, (after_mix, ffn_in, far_out, parts) = refs[:zones], refs[zones:]
     rows_all, width = after_attn.shape
     my_zone = place[1]
-    in_cols = w_in.shape[2]
+    far_out[...] = far[...]
     for index, step in enumerate((0,) + steps_over(zones)):
         parts[my_zone ^ step] = arrived[index][...]
-
     gain = gain_ffn[...]
     span = 128
     part = parts.shape[-1]
@@ -308,15 +328,31 @@
             cols = slice(index * part, (index + 1) * part)
             after_mix[rows, cols] = after_attn[rows, cols] + parts[index, rows, :].astype(F32)
         ffn_in[rows, :] = rms_scale(after_mix[rows, :], gain).astype(BF16)
+
+
+def ffn_rows(ffn_in, w_in, w_out, total):
+    for index in range(w_in.shape[0]):
+        grown = jnp.dot(ffn_in, w_in[index], preferred_element_type=F32)
+        grown = jax.nn.gelu(grown, approximate=True).astype(BF16)
+        total = total + jnp.dot(grown, w_out[index], preferred_element_type=F32)
+    return total
+
+
+def ffn_kernel(after_mix, ffn_in, w_in, w_out, out):
     span = 256
-    for first in range(0, rows_all, span):
+    for first in range(0, after_mix.shape[0], span):
         rows = slice(first, first + span)
-        for index in range(SPREAD):
-            grown = jnp.dot(ffn_in[rows, :], w_in[index], preferred_element_type=F32)
-            cols = slice(index * in_cols, (index + 1) * in_cols)
-            hidden[rows, cols] = jax.nn.gelu(grown, approximate=True).astype(BF16)
-        shrunk = jnp.dot(hidden[rows, :], w_out[...], preferred_element_type=F32)
-        out[rows, :] = (after_mix[rows, :] + shrunk).astype(BF16)
+        out[rows, :] = ffn_rows(ffn_in[rows, :], w_in, w_out, after_mix[rows, :])
+
+
+def last_kernel(zones, place, own_in, own_out, total, ffn_in, swapped_far, out, w_in, w_out, sems):
+    slots = slots_of(place[0] ^ 1)[2:]
+    pieces = [swapped_far.at[index] for index in range(2)]
+    fill_slots(zones, place, own_in, own_out, slots, pieces, w_in, w_out, sems)
+    span = 256
+    for first in range(0, total.shape[0], span):
+        rows = slice(first, first + span)
+        out[rows, :] = ffn_rows(ffn_in[rows, :], w_in, w_out, total[rows, :]).astype(BF16)
 
 
 def call(kernel, out_shape, scratch, smem, hbm, limit, args):
@@ -366,11 +402,18 @@
         jnp.concatenate([w_qkv, w_out_attn], axis=1), quarter_of(my_block) * width, width, axis=1
     )
     direct = [swapped(first, "zone", step) for step in exchanges]
-    slot = my_block % SPREAD
-    slice_in = lax.dynamic_slice_in_dim(w_in, slot * in_cols, in_cols, axis=1)
-    slice_out = lax.dynamic_slice_in_dim(w_out, slot * out_rows, out_rows, axis=0)
-    packed = jnp.concatenate(
-        [slice_in] + [slice_out[:, at : at + in_cols] for at in range(0, width, in_cols)], axis=0
+    packed_rows = w_in.shape[0] + out_rows * (width // in_cols)
+    own_in, packed = call(
+        functools.partial(group_kernel, zones),
+        (
+            jax.ShapeDtypeStruct((SPREAD, w_in.shape[0], in_cols), BF16),
+            jax.ShapeDtypeStruct((packed_rows, in_cols), BF16),
+        ),
+        [],
+        (0,),
+        (),
+        4,
+        [place, w_in, w_out],
     )
     beside = swapped(packed, "zone", 1)
     half_shape = jax.ShapeDtypeStruct((zones - 1, first.shape[0] // 2, width), BF16)
@@ -405,17 +448,6 @@
     while 2 * bits < zones:
         doubled = jnp.concatenate([doubled, swapped(doubled, "zone", bits)], axis=0)
         bits *= 2
-    across = call(
-        stack_kernel,
-        jax.ShapeDtypeStruct((zones - 1,) + packed.shape, BF16),
-        [],
-        (),
-        (),
-        4,
-        [doubled, swapped(doubled, "zone", bits), normed] + pieces[3:],
-    )
-    nearest = crossed(across, "tm", 2, 4)
-
     context, w_attn = call(
         functools.partial(attention_kernel, zones, reach, steps),
         (
@@ -436,60 +468,91 @@
     )
 
     chunk = jax.ShapeDtypeStruct((rows, part), BF16)
-    after_attn, *chunks, pair = call(
+    after_attn, *chunks = call(
         project_kernel,
         (jax.ShapeDtypeStruct((rows, width), F32),)
-        + (chunk,) * zones
-        + (jax.ShapeDtypeStruct((2,) + across.shape, BF16),),
+        + (chunk,) * zones,
         [pltpu.VMEM((zones, rows, part), BF16)],
         (0,),
         (),
         8,
-        [place, states, context, w_attn, gain_mix.reshape(1, -1)]
-        + [across, nearest],
-    )
+        [place, states, context, w_attn, gain_mix.reshape(1, -1)],
+    )
+    across = call(
+        stack_kernel,
+        jax.ShapeDtypeStruct((zones - 1,) + packed.shape, BF16),
+        [],
+        (),
+        (),
+        4,
+        [doubled, swapped(doubled, "zone", bits), after_attn],
+    )
+    nearest = crossed(across, "tm", 2, 4)
+
     arrived = [chunks[0]] + [
         swapped(value, "zone", step) for value, step in zip(chunks[1:], exchanges)
     ]
 
-    *spatial, gathered = call(
+    *spatial, pair = call(
         functools.partial(mixing_kernel, steps, zones),
         (chunk,) * zones
-        + (jax.ShapeDtypeStruct((4,) + across.shape, BF16),),
+        + (jax.ShapeDtypeStruct((2,) + across.shape, BF16),),
         [pltpu.VMEM((zones, rows, part), BF16)],
         (0, 1, 2),
         (),
         8,
-        [place, neighbours, degree, mix] + arrived + [pair, crossed(pair, "tm", 4, 2)],
-    )
+        [place, neighbours, degree, mix] + arrived + [across, nearest],
+    )
+    far = crossed(pair, "tm", 4, 2)
     full_in, full_out = call(
         functools.partial(order_kernel, zones),
         (
-            jax.ShapeDtypeStruct((SPREAD, width, in_cols), BF16),
-            jax.ShapeDtypeStruct((hidden, width), BF16),
+            jax.ShapeDtypeStruct((6, width, in_cols), BF16),
+            jax.ShapeDtypeStruct((6, in_cols, width), BF16),
         ),
-        [pltpu.SemaphoreType.DMA((SPREAD + 1,))],
+        [pltpu.SemaphoreType.DMA((12,))],
         (0,),
         (1, 2),
         8,
-        [place, w_in, w_out, gathered, swapped(gathered, "tm", 1)],
+        [place, own_in, w_out, pair, far, swapped(pair, "tm", 1)],
     )
     arrived = [spatial[0]] + [
         swapped(value, "zone", step) for value, step in zip(spatial[1:], exchanges)
     ]
+    after_mix, ffn_in, far = call(
+        functools.partial(after_kernel, zones),
+        (
+            jax.ShapeDtypeStruct((rows, width), F32),
+            jax.ShapeDtypeStruct((rows, width), BF16),
+            jax.ShapeDtypeStruct(far.shape, BF16),
+        ),
+        [pltpu.VMEM((zones, rows, part), BF16)],
+        (0,),
+        (),
+        8,
+        [place, after_attn, gain_ffn.reshape(1, -1), full_out, far] + arrived,
+    )
+    total = call(
+        ffn_kernel,
+        jax.ShapeDtypeStruct((rows, width), F32),
+        [],
+        (),
+        (),
+        8,
+        [after_mix, ffn_in, full_in, full_out],
+    )
     evolved = call(
-        functools.partial(ffn_kernel, zones),
+        functools.partial(last_kernel, zones),
         jax.ShapeDtypeStruct((rows, width), BF16),
         [
-            pltpu.VMEM((rows, width), F32),
-            pltpu.VMEM((rows, width), BF16),
-            pltpu.VMEM((zones, rows, part), BF16),
-            pltpu.VMEM((rows, hidden), BF16),
+            pltpu.VMEM((2, width, in_cols), BF16),
+            pltpu.VMEM((2, in_cols, width), BF16),
+            pltpu.SemaphoreType.DMA((4,)),
         ],
         (0,),
-        (),
-        10,
-        [place, after_attn, gain_ffn.reshape(1, -1), full_in, full_out] + arrived,
+        (1, 2),
+        8,
+        [place, own_in, w_out, total, ffn_in, swapped(far, "tm", 1)],
     )
     return evolved.reshape(steps, zone_rows, width)
 

time: 81.5 us -> 75.1 us (0.921)
  waiting for transfers between devices: 39.1 us -> 30.1 us
  Pallas kernels: 13.8 us -> 16.9 us
  starting transfers between devices: 25.3 us -> 24.4 us
    ppermute x16 -> x17, waiting for transfers between devices: 33.3 us -> 18.6 us  [swapped(): lax.ppermute(value, axis, [(source, source ^ bits) for source in range(co...]
    ppermute x4, waiting for transfers between devices: 5.73 us -> 11.5 us  [crossed(): return lax.ppermute(value, axis, pairs)]
    pallas_call x8 -> x11, Pallas kernels: 13.8 us -> 16.9 us  [call(): pl.pallas_call(kernel, out_shape=out_shape, in_specs=[pl.BlockSpec(memory...]
    unnamed x24 -> x26, local copies, waits for them, and re-layouts: 0.07 us -> 2.14 us
    ppermute x4, starting transfers between devices: 5.19 us -> 4.22 us  [crossed(): return lax.ppermute(value, axis, pairs)]
    dynamic_slice x1 -> x0, local copies, waits for them, and re-layouts: 0.84 us -> none  [on_device(): slice_in = lax.dynamic_slice_in_dim(w_in, slot * in_cols, in_cols, axis=1)]
    ppermute x16 -> x17, starting transfers between devices: 15.1 us -> 15.2 us  [swapped(): lax.ppermute(value, axis, [(source, source ^ bits) for source in range(co...]
  transfers between devices with their start and end apart: 21 -> 22, of which waited for: 11 -> 10; matrix products, arithmetic and copies ran while one was open for 3% -> 1% of each run, Pallas kernels for 8% -> 15%
where the time goes in v10:
time: 75.1 us; the launch traced here: 74.8 us
  waiting for transfers between devices  30.1 us (40%)
  starting transfers between devices  24.4 us (32%)
  Pallas kernels  16.9 us (23%)
  local copies, waits for them, and re-layouts  2.14 us (3%)
  other arithmetic  1.04 us (1%)
    ppermute x17, waiting for transfers between devices, swapped(): lax.ppermute(value, axis, [(source, source ^ bits) for source in range(co...  18.6 us
    pallas_call x11, Pallas kernels, call(): pl.pallas_call(kernel, out_shape=out_shape, in_specs=[pl.BlockSpec(memory...  16.9 us
    ppermute x17, starting transfers between devices, swapped(): lax.ppermute(value, axis, [(source, source ^ bits) for source in range(co...  15.2 us
    ppermute x4, waiting for transfers between devices, crossed(): return lax.ppermute(value, axis, pairs)  11.5 us
    ppermute x1, starting transfers between devices, shifted(): lax.ppermute(value, axis, [(source, source + steps) for source in range(c...  4.99 us
    ppermute x4, starting transfers between devices, crossed(): return lax.ppermute(value, axis, pairs)  4.22 us
    unnamed x26, local copies, waits for them, and re-layouts  2.14 us
  transfers between devices with their start and end apart: 22, of which 10 were waited for; matrix products, arithmetic and copies ran while one was open for 1% of the time, Pallas kernels for 15%

profile of v10, /device:TPU:0, one launch (start us, length us, event | category | flops | bytes accessed | tf_op | source)
XLA Modules:
  0.0 74.8 jit_solution(7245739704039708744)
XLA Ops:
  0.0 5.0 %collective-permute-start = (bf16[4,128,512]{2,1,0:T(8,128)(2,1)}, bf16[4,128,512]{2,1,0:T(8,128)(2,1)S(1)}, u32[]{:S(2)}, u32[]{:S(2)}) collective-permute-start(bf16[4,128,512]{2,1,0:T(8,128)(2,1)} %states.3), channel_id=1, source_target_pairs={{0,8},{4,12},{8,16},{12,20},{16,24},{20,28},{1,9},{5,13},{9,17},{1... | collective-permute-start | bytes 1572872 | tf_op jit(solution)/shard_map/ppermute | solution.py:20
  6.0 3.7 %collective-permute-start.3 = (bf16[128,512]{1,0:T(8,128)(2,1)S(1)}, bf16[128,512]{1,0:T(8,128)(2,1)S(1)}, u32[]{:S(2)}, u32[]{:S(2)}) collective-permute-start(bf16[128,512]{1,0:T(8,128)(2,1)S(1)} %fusion), channel_id=1, source_target_pairs={{0,3},{1,2},{2,1},{3,0},{4,7},{5,6},{6,5},{7,4},{8,11},{9,10},{10,... | collective-permute-start | bytes 393224 | tf_op jit(solution)/shard_map/ppermute | solution.py:25
  10.5 1.0 %copy-done.1 = bf16[512,512]{1,0:T(8,128)(2,1)S(1)} copy-done((bf16[512,512]{1,0:T(8,128)(2,1)S(1)}, bf16[512,512]{1,0:T(8,128)(2,1)}, u32[]{:S(2)}) %copy-start.1) | copy-done | bytes 524312
  13.5 1.3 %collective-permute-start.1 = (bf16[256,256]{1,0:T(8,128)(2,1)S(1)}, bf16[256,256]{1,0:T(8,128)(2,1)S(1)}, u32[]{:S(2)}, u32[]{:S(2)}) collective-permute-start(bf16[256,256]{1,0:T(8,128)(2,1)S(1)} %get-tuple-element.30.packed), channel_id=1, source_target_pairs={{0,1},{1,0},{2,3},{3,2},{4,5},{5,4},{6,7},{7,6},{8,9},{9,8},{10,11... | collective-permute-start | bytes 393224 | tf_op jit(solution)/shard_map/ppermute | solution.py:25
  14.8 5.8 %collective-permute-done.2.refs_0_ = bf16[128,512]{1,0:T(8,128)(2,1)S(1)} collective-permute-done((bf16[128,512]{1,0:T(8,128)(2,1)S(1)}, bf16[128,512]{1,0:T(8,128)(2,1)S(1)}, u32[]{:S(2)}, u32[]{:S(2)}) %collective-permute-start.2) | collective-permute-done | bytes 131104 | tf_op jit(solution)/shard_map/ppermute | solution.py:25
  22.2 1.5 %collective-permute-start.6 = (bf16[3,64,512]{2,1,0:T(8,128)(2,1)S(1)}, bf16[3,64,512]{2,1,0:T(8,128)(2,1)S(1)}, u32[]{:S(2)}, u32[]{:S(2)}) collective-permute-start(bf16[3,64,512]{2,1,0:T(8,128)(2,1)S(1)} %get-tuple-element.33), channel_id=1, source_target_pairs={{0,8},{4,20},{8,0},{12,28},{16,24},{20,4},{24,16},{28,12},{1,9},{5... | collective-permute-start | bytes 589832 | tf_op jit(solution)/shard_map/ppermute | solution.py:31
  24.3 1.3 %collective-permute-start.14 = (bf16[2,256,256]{2,1,0:T(8,128)(2,1)S(1)}, bf16[2,256,256]{2,1,0:T(8,128)(2,1)S(1)}, u32[]{:S(2)}, u32[]{:S(2)}) collective-permute-start(bf16[2,256,256]{2,1,0:T(8,128)(2,1)S(1)} %get-tuple-element.42.doubled), channel_id=1, source_target_pairs={{0,2},{1,3},{2,0},{3,1},{4,6},{5,7},{6,4},{7,5},{8,10},{9,11},{10,... | collective-permute-start | bytes 786440 | tf_op jit(solution)/shard_map/ppermute | solution.py:25
  25.6 2.4 %collective-permute-done.6.refs_1_ = bf16[3,64,512]{2,1,0:T(8,128)(2,1)S(1)} collective-permute-done((bf16[3,64,512]{2,1,0:T(8,128)(2,1)S(1)}, bf16[3,64,512]{2,1,0:T(8,128)(2,1)S(1)}, u32[]{:S(2)}, u32[]{:S(2)}) %collective-permute-start.6) | collective-permute-done | bytes 196640 | tf_op jit(solution)/shard_map/ppermute | solution.py:31
  27.9 2.1 %collective-permute-done.7.refs_2_ = bf16[3,64,512]{2,1,0:T(8,128)(2,1)S(1)} collective-permute-done((bf16[3,64,512]{2,1,0:T(8,128)(2,1)S(1)}, bf16[3,64,512]{2,1,0:T(8,128)(2,1)S(1)}, u32[]{:S(2)}, u32[]{:S(2)}) %collective-permute-start.7) | collective-permute-done | bytes 196640 | tf_op jit(solution)/shard_map/ppermute | solution.py:31
  31.5 5.0 %shard_map.121 = (bf16[512,512]{1,0:T(8,128)(2,1)S(1)}, bf16[512,512]{1,0:T(8,128)(2,1)S(1)}) custom-call(s32[2]{0:T(128)S(1)} %pad_add_fusion.place, s32[1,2]{1,0:T(1,128)S(1)} %copy-done.11, bf16[1536,512]{1,0:T(8,128)(2,1)S(1)} %shard_map.120.normed, bf16[128,1536]{1,0:T(8,128)(2,1)S(1)} %copy-done.3, bf16[128,512]{1,0:T(8,128)(2,1)S(1)} %copy-done.4, ...), custom_call_target="tpu_custom_call" | custom-call | tf_op jit(solution)/shard_map/pallas_call | solution.py:360
  36.5 1.1 %shard_map.122 = (f32[512,512]{1,0:T(8,128)S(1)}, bf16[512,128]{1,0:T(8,128)(2,1)S(1)}, bf16[512,128]{1,0:T(8,128)(2,1)S(1)}, bf16[512,128]{1,0:T(8,128)(2,1)S(1)}, bf16[512,128]{1,0:T(8,128)(2,1)S(1)}) custom-call(s32[2]{0:T(128)S(1)} %pad_add_fusion.place, bf16[4,128,512]{2,1,0:T(8,128)(2,1)S(1)} %copy-done, ...), custom_call_target="tpu_custom_call" | custom-call | tf_op jit(solution)/shard_map/pallas_call | solution.py:360
  37.7 1.8 %collective-permute-done.14.arrived = bf16[2,256,256]{2,1,0:T(8,128)(2,1)S(1)} collective-permute-done((bf16[2,256,256]{2,1,0:T(8,128)(2,1)S(1)}, bf16[2,256,256]{2,1,0:T(8,128)(2,1)S(1)}, u32[]{:S(2)}, u32[]{:S(2)}) %collective-permute-start.14) | collective-permute-done | bytes 262176 | tf_op jit(solution)/shard_map/ppermute | solution.py:25
  39.5 1.5 %collective-permute-start.15 = (bf16[3,256,256]{2,1,0:T(8,128)(2,1)S(1)}, bf16[3,256,256]{2,1,0:T(8,128)(2,1)S(1)}, u32[]{:S(2)}, u32[]{:S(2)}) collective-permute-start(bf16[3,256,256]{2,1,0:T(8,128)(2,1)S(1)} %shard_map.123.refs_4_), channel_id=1, source_target_pairs={{0,8},{4,20},{8,0},{12,28},{16,24},{20,4},{24,16},{28,12},{1,9},{5... | collective-permute-start | bytes 1179656 | tf_op jit(solution)/shard_map/ppermute | solution.py:31
  41.1 2.2 %collective-permute-start.12 = (bf16[512,128]{1,0:T(8,128)(2,1)S(1)}, bf16[512,128]{1,0:T(8,128)(2,1)S(1)}, u32[]{:S(2)}, u32[]{:S(2)}) collective-permute-start(bf16[512,128]{1,0:T(8,128)(2,1)S(1)} %get-tuple-element.40), channel_id=1, source_target_pairs={{0,3},{1,2},{2,1},{3,0},{4,7},{5,6},{6,5},{7,4},{8,11},{9,10},{10,... | collective-permute-start | bytes 393224 | tf_op jit(solution)/shard_map/ppermute | solution.py:25
  43.3 1.3 %collective-permute-start.13 = (bf16[512,128]{1,0:T(8,128)(2,1)S(1)}, bf16[512,128]{1,0:T(8,128)(2,1)S(1)}, u32[]{:S(2)}, u32[]{:S(2)}) collective-permute-start(bf16[512,128]{1,0:T(8,128)(2,1)S(1)} %get-tuple-element.41), channel_id=1, source_target_pairs={{0,1},{1,0},{2,3},{3,2},{4,5},{5,4},{6,7},{7,6},{8,9},{9,8},{10,11... | collective-permute-start | bytes 393224 | tf_op jit(solution)/shard_map/ppermute | solution.py:25
  44.6 7.9 %collective-permute-done.11.refs_1_ = bf16[512,128]{1,0:T(8,128)(2,1)S(1)} collective-permute-done((bf16[512,128]{1,0:T(8,128)(2,1)S(1)}, bf16[512,128]{1,0:T(8,128)(2,1)S(1)}, u32[]{:S(2)}, u32[]{:S(2)}) %collective-permute-start.11) | collective-permute-done | bytes 131104 | tf_op jit(solution)/shard_map/ppermute | solution.py:25
  52.5 1.2 %collective-permute-done.13.refs_3_ = bf16[512,128]{1,0:T(8,128)(2,1)S(1)} collective-permute-done((bf16[512,128]{1,0:T(8,128)(2,1)S(1)}, bf16[512,128]{1,0:T(8,128)(2,1)S(1)}, u32[]{:S(2)}, u32[]{:S(2)}) %collective-permute-start.13) | collective-permute-done | bytes 131104 | tf_op jit(solution)/shard_map/ppermute | solution.py:25
  53.7 1.1 %shard_map.124 = (bf16[512,128]{1,0:T(8,128)(2,1)S(1)}, bf16[512,128]{1,0:T(8,128)(2,1)S(1)}, bf16[512,128]{1,0:T(8,128)(2,1)S(1)}, bf16[512,128]{1,0:T(8,128)(2,1)S(1)}, bf16[2,3,256,256]{3,2,1,0:T(8,128)(2,1)S(1)}) custom-call(s32[2]{0:T(128)S(1)} %pad_add_fusion.place, s32[4,3]{1,0:T(4,128)S(1)} %copy-done.8, s32[4]{0:T(128)S(1)} %copy-done.12, ...), custom_call_target="tpu_custom_call" | custom-call | tf_op jit(solution)/shard_map/pallas_call | solution.py:360
  55.5 1.9 %collective-permute-start.18 = (bf16[512,128]{1,0:T(8,128)(2,1)S(1)}, bf16[512,128]{1,0:T(8,128)(2,1)S(1)}, u32[]{:S(2)}, u32[]{:S(2)}) collective-permute-start(bf16[512,128]{1,0:T(8,128)(2,1)S(1)} %get-tuple-element.46), channel_id=1, source_target_pairs={{0,2},{1,3},{2,0},{3,1},{4,6},{5,7},{6,4},{7,5},{8,10},{9,11},{10,... | collective-permute-start | bytes 393224 | tf_op jit(solution)/shard_map/ppermute | solution.py:25
  57.4 2.5 %collective-permute-start.19 = (bf16[512,128]{1,0:T(8,128)(2,1)S(1)}, bf16[512,128]{1,0:T(8,128)(2,1)S(1)}, u32[]{:S(2)}, u32[]{:S(2)}) collective-permute-start(bf16[512,128]{1,0:T(8,128)(2,1)S(1)} %get-tuple-element.47), channel_id=1, source_target_pairs={{0,3},{1,2},{2,1},{3,0},{4,7},{5,6},{6,5},{7,4},{8,11},{9,10},{10,... | collective-permute-start | bytes 393224 | tf_op jit(solution)/shard_map/ppermute | solution.py:25
  60.0 7.0 %collective-permute-done.16.far = bf16[2,3,256,256]{3,2,1,0:T(8,128)(2,1)S(1)} collective-permute-done((bf16[2,3,256,256]{3,2,1,0:T(8,128)(2,1)S(1)}, bf16[2,3,256,256]{3,2,1,0:T(8,128)(2,1)S(1)}, u32[]{:S(2)}, u32[]{:S(2)}) %collective-permute-start.16) | collective-permute-done | bytes 786464 | tf_op jit(solution)/shard_map/ppermute | solution.py:31
  67.0 1.9 %shard_map.125 = (bf16[6,512,256]{2,1,0:T(8,128)(2,1)S(1)}, bf16[6,256,512]{2,1,0:T(8,128)(2,1)S(1)}) custom-call(s32[2]{0:T(128)S(1)} %pad_add_fusion.place, bf16[8,128,256]{2,1,0:T(8,128)(2,1)S(1)} %get-tuple-element.29.own_in, bf16[512,512]{1,0:T(8,128)(2,1)S(1)} %copy-done.2, bf16[2,3,256,256]{3,2,1,0:T(8,128)(2,1)S(1)} %get-tuple-element.43.pair, ...), custom_call_target="tpu_custom_call" | custom-call | tf_op jit(solution)/shard_map/pallas_call | solution.py:360
  69.9 2.0 %shard_map.127.total = f32[512,512]{1,0:T(8,128)S(1)} custom-call(f32[512,512]{1,0:T(8,128)S(1)} %get-tuple-element.49.after_mix, bf16[512,512]{1,0:T(8,128)(2,1)S(1)} %get-tuple-element.50.ffn_in, bf16[6,512,256]{2,1,0:T(8,128)(2,1)S(1)} %get-tuple-element.51.w_in, bf16[6,256,512]{2,1,0:T(8,128)(2,1)S(1)} %get-tuple-element.44.ready.w_out), custom_call_target="tpu_custom_call" | custom-call | tf_op jit(solution)/shard_map/pallas_call | solution.py:360
  72.1 2.7 %shard_map.128 = bf16[512,512]{1,0:T(8,128)(2,1)} custom-call(s32[2]{0:T(128)S(1)} %pad_add_fusion.place, bf16[8,128,256]{2,1,0:T(8,128)(2,1)S(1)} %get-tuple-element.29.own_in, bf16[512,512]{1,0:T(8,128)(2,1)S(1)} %copy-done.2, f32[512,512]{1,0:T(8,128)S(1)} %shard_map.127.total, bf16[512,512]{1,0:T(8,128)(2,1)S(1)} %get-tuple-element.50.ffn_in, ...), custom_call_target="tpu_custom_call" | custom-call | tf_op jit(solution)/shard_map/pallas_call | solution.py:360
  (59 shorter events, 9.2 us)
Async XLA Ops:
  0.0 21.4 %collective-permute-start = (bf16[4,128,512]{2,1,0:T(8,128)(2,1)}, bf16[4,128,512]{2,1,0:T(8,128)(2,1)S(1)}, u32[]{:S(2)}, u32[]{:S(2)}) collective-permute-start(bf16[4,128,512]{2,1,0:T(8,128)(2,1)} %states.3), channel_id=1, source_target_pairs={{0,8},{4,12},{8,16},{12,20},{16,24},{20,28},{1,9},{5,13},{9,17},{1... | collective-permute-start | bytes 1572872 | tf_op jit(solution)/shard_map/ppermute | solution.py:20
  5.0 25.0 %copy-start.10 = (f32[512]{0:T(512)S(1)}, f32[512]{0:T(512)}, u32[]{:S(2)}) copy-start(f32[512]{0:T(512)} %param.13) | copy-start | bytes 6148
  6.0 8.8 %collective-permute-start.3 = (bf16[128,512]{1,0:T(8,128)(2,1)S(1)}, bf16[128,512]{1,0:T(8,128)(2,1)S(1)}, u32[]{:S(2)}, u32[]{:S(2)}) collective-permute-start(bf16[128,512]{1,0:T(8,128)(2,1)S(1)} %fusion), channel_id=1, source_target_pairs={{0,3},{1,2},{2,1},{3,0},{4,7},{5,6},{6,5},{7,4},{8,11},{9,10},{10,... | collective-permute-start | bytes 393224 | tf_op jit(solution)/shard_map/ppermute | solution.py:25
  9.7 10.9 %collective-permute-start.2 = (bf16[128,512]{1,0:T(8,128)(2,1)S(1)}, bf16[128,512]{1,0:T(8,128)(2,1)S(1)}, u32[]{:S(2)}, u32[]{:S(2)}) collective-permute-start(bf16[128,512]{1,0:T(8,128)(2,1)S(1)} %fusion), channel_id=1, source_target_pairs={{0,2},{1,3},{2,0},{3,1},{4,6},{5,7},{6,4},{7,5},{8,10},{9,11},{10,... | collective-permute-start | bytes 393224 | tf_op jit(solution)/shard_map/ppermute | solution.py:25
  9.7 10.9 %collective-permute-start.4 = (bf16[128,512]{1,0:T(8,128)(2,1)S(1)}, bf16[128,512]{1,0:T(8,128)(2,1)S(1)}, u32[]{:S(2)}, u32[]{:S(2)}) collective-permute-start(bf16[128,512]{1,0:T(8,128)(2,1)S(1)} %fusion), channel_id=1, source_target_pairs={{0,1},{1,0},{2,3},{3,2},{4,5},{5,4},{6,7},{7,6},{8,9},{9,8},{10,11... | collective-permute-start | bytes 393224 | tf_op jit(solution)/shard_map/ppermute | solution.py:25
  13.5 7.9 %collective-permute-start.1 = (bf16[256,256]{1,0:T(8,128)(2,1)S(1)}, bf16[256,256]{1,0:T(8,128)(2,1)S(1)}, u32[]{:S(2)}, u32[]{:S(2)}) collective-permute-start(bf16[256,256]{1,0:T(8,128)(2,1)S(1)} %get-tuple-element.30.packed), channel_id=1, source_target_pairs={{0,1},{1,0},{2,3},{3,2},{4,5},{5,4},{6,7},{7,6},{8,9},{9,8},{10,11... | collective-permute-start | bytes 393224 | tf_op jit(solution)/shard_map/ppermute | solution.py:25
  22.1 7.9 %collective-permute-start.5 = (bf16[4,128,512]{2,1,0:T(8,128)(2,1)S(1)}, bf16[4,128,512]{2,1,0:T(8,128)(2,1)S(1)}, u32[]{:S(2)}, u32[]{:S(2)}) collective-permute-start(bf16[4,128,512]{2,1,0:T(8,128)(2,1)S(1)} %get-tuple-element.31), channel_id=1, source_target_pairs={{0,4},{4,0},{8,12},{12,8},{16,20},{20,16},{24,28},{28,24},{1,5},{5... | collective-permute-start | bytes 1572872 | tf_op jit(solution)/shard_map/ppermute | solution.py:25
  22.2 5.7 %collective-permute-start.6 = (bf16[3,64,512]{2,1,0:T(8,128)(2,1)S(1)}, bf16[3,64,512]{2,1,0:T(8,128)(2,1)S(1)}, u32[]{:S(2)}, u32[]{:S(2)}) collective-permute-start(bf16[3,64,512]{2,1,0:T(8,128)(2,1)S(1)} %get-tuple-element.33), channel_id=1, source_target_pairs={{0,8},{4,20},{8,0},{12,28},{16,24},{20,4},{24,16},{28,12},{1,9},{5... | collective-permute-start | bytes 589832 | tf_op jit(solution)/shard_map/ppermute | solution.py:31
  23.7 6.3 %collective-permute-start.7 = (bf16[3,64,512]{2,1,0:T(8,128)(2,1)S(1)}, bf16[3,64,512]{2,1,0:T(8,128)(2,1)S(1)}, u32[]{:S(2)}, u32[]{:S(2)}) collective-permute-start(bf16[3,64,512]{2,1,0:T(8,128)(2,1)S(1)} %get-tuple-element.34), channel_id=1, source_target_pairs={{0,8},{4,20},{8,0},{12,28},{16,24},{20,4},{24,16},{28,12},{1,9},{5... | collective-permute-start | bytes 589832 | tf_op jit(solution)/shard_map/ppermute | solution.py:31
  24.3 7.2 %collective-permute-start.8 = (bf16[3,128,512]{2,1,0:T(8,128)(2,1)S(1)}, bf16[3,128,512]{2,1,0:T(8,128)(2,1)S(1)}, u32[]{:S(2)}, u32[]{:S(2)}) collective-permute-start(bf16[3,128,512]{2,1,0:T(8,128)(2,1)S(1)} %get-tuple-element.32.refs_0_), channel_id=1, source_target_pairs={{0,4},{4,0},{8,12},{12,8},{16,20},{20,16},{24,28},{28,24},{1,5},{5... | collective-permute-start | bytes 1179656 | tf_op jit(solution)/shard_map/ppermute | solution.py:25
  24.3 15.2 %collective-permute-start.14 = (bf16[2,256,256]{2,1,0:T(8,128)(2,1)S(1)}, bf16[2,256,256]{2,1,0:T(8,128)(2,1)S(1)}, u32[]{:S(2)}, u32[]{:S(2)}) collective-permute-start(bf16[2,256,256]{2,1,0:T(8,128)(2,1)S(1)} %get-tuple-element.42.doubled), channel_id=1, source_target_pairs={{0,2},{1,3},{2,0},{3,1},{4,6},{5,7},{6,4},{7,5},{8,10},{9,11},{10,... | collective-permute-start | bytes 786440 | tf_op jit(solution)/shard_map/ppermute | solution.py:25
  27.9 2.8 %collective-permute-start.9 = (bf16[3,64,512]{2,1,0:T(8,128)(2,1)S(1)}, bf16[3,64,512]{2,1,0:T(8,128)(2,1)S(1)}, u32[]{:S(2)}, u32[]{:S(2)}) collective-permute-start(bf16[3,64,512]{2,1,0:T(8,128)(2,1)S(1)} %collective-permute-done.6.refs_1_), channel_id=1, source_target_pairs={{0,4},{4,0},{8,12},{12,8},{16,20},{20,16},{24,28},{28,24},{1,5},{5... | collective-permute-start | bytes 589832 | tf_op jit(solution)/shard_map/ppermute | solution.py:25
  30.0 1.4 %collective-permute-start.10 = (bf16[3,64,512]{2,1,0:T(8,128)(2,1)S(1)}, bf16[3,64,512]{2,1,0:T(8,128)(2,1)S(1)}, u32[]{:S(2)}, u32[]{:S(2)}) collective-permute-start(bf16[3,64,512]{2,1,0:T(8,128)(2,1)S(1)} %collective-permute-done.7.refs_2_), channel_id=1, source_target_pairs={{0,4},{4,0},{8,12},{12,8},{16,20},{20,16},{24,28},{28,24},{1,5},{5... | collective-permute-start | bytes 589832 | tf_op jit(solution)/shard_map/ppermute | solution.py:25
  39.5 27.5 %copy-start.2 = (bf16[512,512]{1,0:T(8,128)(2,1)S(1)}, bf16[512,512]{1,0:T(8,128)(2,1)}, u32[]{:S(2)}) copy-start(bf16[512,512]{1,0:T(8,128)(2,1)} %own_out.3) | copy-start | bytes 1572868
  39.5 14.2 %collective-permute-start.15 = (bf16[3,256,256]{2,1,0:T(8,128)(2,1)S(1)}, bf16[3,256,256]{2,1,0:T(8,128)(2,1)S(1)}, u32[]{:S(2)}, u32[]{:S(2)}) collective-permute-start(bf16[3,256,256]{2,1,0:T(8,128)(2,1)S(1)} %shard_map.123.refs_4_), channel_id=1, source_target_pairs={{0,8},{4,20},{8,0},{12,28},{16,24},{20,4},{24,16},{28,12},{1,9},{5... | collective-permute-start | bytes 1179656 | tf_op jit(solution)/shard_map/ppermute | solution.py:31
  41.1 11.4 %collective-permute-start.11 = (bf16[512,128]{1,0:T(8,128)(2,1)S(1)}, bf16[512,128]{1,0:T(8,128)(2,1)S(1)}, u32[]{:S(2)}, u32[]{:S(2)}) collective-permute-start(bf16[512,128]{1,0:T(8,128)(2,1)S(1)} %get-tuple-element.39), channel_id=1, source_target_pairs={{0,2},{1,3},{2,0},{3,1},{4,6},{5,7},{6,4},{7,5},{8,10},{9,11},{10,... | collective-permute-start | bytes 393224 | tf_op jit(solution)/shard_map/ppermute | solution.py:25
  41.1 11.4 %collective-permute-start.12 = (bf16[512,128]{1,0:T(8,128)(2,1)S(1)}, bf16[512,128]{1,0:T(8,128)(2,1)S(1)}, u32[]{:S(2)}, u32[]{:S(2)}) collective-permute-start(bf16[512,128]{1,0:T(8,128)(2,1)S(1)} %get-tuple-element.40), channel_id=1, source_target_pairs={{0,3},{1,2},{2,1},{3,0},{4,7},{5,6},{6,5},{7,4},{8,11},{9,10},{10,... | collective-permute-start | bytes 393224 | tf_op jit(solution)/shard_map/ppermute | solution.py:25
  43.3 10.4 %collective-permute-start.13 = (bf16[512,128]{1,0:T(8,128)(2,1)S(1)}, bf16[512,128]{1,0:T(8,128)(2,1)S(1)}, u32[]{:S(2)}, u32[]{:S(2)}) collective-permute-start(bf16[512,128]{1,0:T(8,128)(2,1)S(1)} %get-tuple-element.41), channel_id=1, source_target_pairs={{0,1},{1,0},{2,3},{3,2},{4,5},{5,4},{6,7},{7,6},{8,9},{9,8},{10,11... | collective-permute-start | bytes 393224 | tf_op jit(solution)/shard_map/ppermute | solution.py:25
  54.9 5.1 %collective-permute-start.17 = (bf16[2,3,256,256]{3,2,1,0:T(8,128)(2,1)S(1)}, bf16[2,3,256,256]{3,2,1,0:T(8,128)(2,1)S(1)}, u32[]{:S(2)}, u32[]{:S(2)}) collective-permute-start(bf16[2,3,256,256]{3,2,1,0:T(8,128)(2,1)S(1)} %get-tuple-element.43.pair), channel_id=1, source_target_pairs={{0,4},{4,0},{8,12},{12,8},{16,20},{20,16},{24,28},{28,24},{1,5},{5... | collective-permute-start | bytes 2359304 | tf_op jit(solution)/shard_map/ppermute | solution.py:25
  54.9 12.1 %collective-permute-start.16 = (bf16[2,3,256,256]{3,2,1,0:T(8,128)(2,1)S(1)}, bf16[2,3,256,256]{3,2,1,0:T(8,128)(2,1)S(1)}, u32[]{:S(2)}, u32[]{:S(2)}) collective-permute-start(bf16[2,3,256,256]{3,2,1,0:T(8,128)(2,1)S(1)} %get-tuple-element.43.pair), channel_id=1, source_target_pairs={{0,16},{4,12},{8,24},{12,4},{16,0},{20,28},{24,8},{28,20},{1,17},{... | collective-permute-start | bytes 2359304 | tf_op jit(solution)/shard_map/ppermute | solution.py:31
  55.5 13.3 %collective-permute-start.18 = (bf16[512,128]{1,0:T(8,128)(2,1)S(1)}, bf16[512,128]{1,0:T(8,128)(2,1)S(1)}, u32[]{:S(2)}, u32[]{:S(2)}) collective-permute-start(bf16[512,128]{1,0:T(8,128)(2,1)S(1)} %get-tuple-element.46), channel_id=1, source_target_pairs={{0,2},{1,3},{2,0},{3,1},{4,6},{5,7},{6,4},{7,5},{8,10},{9,11},{10,... | collective-permute-start | bytes 393224 | tf_op jit(solution)/shard_map/ppermute | solution.py:25
  57.4 11.4 %collective-permute-start.19 = (bf16[512,128]{1,0:T(8,128)(2,1)S(1)}, bf16[512,128]{1,0:T(8,128)(2,1)S(1)}, u32[]{:S(2)}, u32[]{:S(2)}) collective-permute-start(bf16[512,128]{1,0:T(8,128)(2,1)S(1)} %get-tuple-element.47), channel_id=1, source_target_pairs={{0,3},{1,2},{2,1},{3,0},{4,7},{5,6},{6,5},{7,4},{8,11},{9,10},{10,... | collective-permute-start | bytes 393224 | tf_op jit(solution)/shard_map/ppermute | solution.py:25
  60.0 8.9 %collective-permute-start.20 = (bf16[512,128]{1,0:T(8,128)(2,1)S(1)}, bf16[512,128]{1,0:T(8,128)(2,1)S(1)}, u32[]{:S(2)}, u32[]{:S(2)}) collective-permute-start(bf16[512,128]{1,0:T(8,128)(2,1)S(1)} %get-tuple-element.48), channel_id=1, source_target_pairs={{0,1},{1,0},{2,3},{3,2},{4,5},{5,4},{6,7},{7,6},{8,9},{9,8},{10,11... | collective-permute-start | bytes 393224 | tf_op jit(solution)/shard_map/ppermute | solution.py:25
  69.8 2.4 %collective-permute-start.21 = (bf16[2,3,256,256]{3,2,1,0:T(8,128)(2,1)S(1)}, bf16[2,3,256,256]{3,2,1,0:T(8,128)(2,1)S(1)}, u32[]{:S(2)}, u32[]{:S(2)}) collective-permute-start(bf16[2,3,256,256]{3,2,1,0:T(8,128)(2,1)S(1)} %get-tuple-element.52), channel_id=1, source_target_pairs={{0,4},{4,0},{8,12},{12,8},{16,20},{20,16},{24,28},{28,24},{1,5},{5... | collective-permute-start | bytes 2359304 | tf_op jit(solution)/shard_map/ppermute | solution.py:25
  (11 other events, 87.1 us)

commit v11 on v10

--- a/solution.py
+++ b/solution.py
@@ -130,25 +130,28 @@
     for copy in copies:
         copy.wait()
     attn_out[...] = weights[3]
-    for index in range(3):
-        for block in range(width // LANES):
-            first = block * LANES
-            rows = slice(index * width + first, index * width + first + LANES)
-            w_turned[rows, :] = weights[index, :, first : first + LANES].T
-
-    def project(first, last, weight_rows):
-        return lax.dot_general(
-            w_turned[weight_rows, :],
-            normed[first:last, :],
+    group = 3 * head_size
+    for head in range(HEADS):
+        for kind in range(3):
+            rows = slice(head * group + kind * head_size, head * group + (kind + 1) * head_size)
+            w_turned[rows, :] = weights[kind, :, head * head_size : (head + 1) * head_size].T
+
+    def project(head, first, span):
+        skip = 0 if first >= reach * steps * zone_rows else head_size
+        projected[head, skip:, first : first + span] = lax.dot_general(
+            w_turned[head * group + skip : (head + 1) * group, :],
+            normed[first : first + span, :],
             (((1,), (1,)), ((), ())),
             preferred_element_type=F32,
-        ).astype(BF16).astype(F32)
+        )
 
     span = 2 * zone_rows
-    for first in range(0, key_count * zone_rows, span):
-        own = first >= reach * steps * zone_rows
-        rows = slice(0 if own else width, 3 * width)
-        projected[rows, first : first + span] = project(first, first + span, rows)
+    pending = [(head, first) for head in range(HEADS) for first in range(0, key_count * zone_rows, span)]
+
+    def project_some(count):
+        for _ in range(min(count, len(pending))):
+            head, first = pending.pop(0)
+            project(head, first, span)
 
     allowed_back = [
         (pattern[0, back - 1] == 1) & (my_block >= back) for back in range(reach, 0, -1)
@@ -158,54 +161,55 @@
     def usable(query):
         return range(reach * steps + query + 1)
 
-    def head_body(head, carry):
-        base = head * head_size
-
+    def attend(head, queries):
         def tile(kind, chunk, key):
-            row = pl.multiple_of(kind * width + base + chunk * 8, 8)
-            return projected[pl.ds(row, 8), key * zone_rows : (key + 1) * zone_rows]
-
-        for pair in range(0, steps, 2):
-            queries = range(pair, min(pair + 2, steps))
+            row = kind * head_size + chunk * 8
+            return projected[head, row : row + 8, key * zone_rows : (key + 1) * zone_rows]
+
+        sums = {}
+        for chunk in range(chunks):
+            q_tiles = {q: tile(0, chunk, reach * steps + q) for q in queries}
+            for key in usable(queries[-1]):
+                k_tile = tile(1, chunk, key)
+                for q in queries:
+                    if key in usable(q):
+                        term = q_tiles[q] * k_tile
+                        sums[q, key] = term if chunk == 0 else sums[q, key] + term
+        weights_of, scales = {}, {}
+        for q in queries:
+            scores = jnp.concatenate([row_sum(sums[q, key]) for key in usable(q)], axis=0)
+            scores = scores * head_size ** (-0.5)
+            row_id = lax.broadcasted_iota(jnp.int32, scores.shape, 0)
+            allowed = row_id >= reach * steps
+            for index, live in enumerate(allowed_back):
+                inside = (row_id >= index * steps) & (row_id < (index + 1) * steps)
+                allowed = allowed | (inside & live)
+            masked = jnp.where(allowed, scores, -1e30)
+            top = jnp.max(masked, axis=0, keepdims=True)
+            expw = jnp.where(allowed, jnp.exp(masked - top), 0.0)
+            scales[q] = jnp.broadcast_to(1.0 / row_sum(expw), (8, zone_rows))
+            probs = expw.astype(BF16).astype(F32)
+            for key in usable(q):
+                weights_of[q, key] = jnp.broadcast_to(probs[key : key + 1, :], (8, zone_rows))
+        for chunk in range(chunks):
             sums = {}
-            for chunk in range(chunks):
-                q_tiles = {q: tile(0, chunk, reach * steps + q) for q in queries}
-                for key in usable(queries[-1]):
-                    k_tile = tile(1, chunk, key)
-                    for q in queries:
-                        if key in usable(q):
-                            term = q_tiles[q] * k_tile
-                            sums[q, key] = term if chunk == 0 else sums[q, key] + term
-            weights, scales = {}, {}
+            for key in usable(queries[-1]):
+                v_tile = tile(2, chunk, key)
+                for q in queries:
+                    if key in usable(q):
+                        term = weights_of[q, key] * v_tile
+                        sums[q] = term if key == 0 else sums[q] + term
             for q in queries:
-                scores = jnp.concatenate([row_sum(sums[q, key]) for key in usable(q)], axis=0)
-                scores = scores * head_size ** (-0.5)
-                row_id = lax.broadcasted_iota(jnp.int32, scores.shape, 0)
-                allowed = row_id >= reach * steps
-                for index, live in enumerate(allowed_back):
-                    inside = (row_id >= index * steps) & (row_id < (index + 1) * steps)
-                    allowed = allowed | (inside & live)
-                masked = jnp.where(allowed, scores, -1e30)
-                top = jnp.max(masked, axis=0, keepdims=True)
-                expw = jnp.where(allowed, jnp.exp(masked - top), 0.0)
-                scales[q] = jnp.broadcast_to(1.0 / row_sum(expw), (8, zone_rows))
-                probs = expw.astype(BF16).astype(F32)
-                for key in usable(q):
-                    weights[q, key] = jnp.broadcast_to(probs[key : key + 1, :], (8, zone_rows))
-            for chunk in range(chunks):
-                sums = {}
-                for key in usable(queries[-1]):
-                    v_tile = tile(2, chunk, key)
-                    for q in queries:
-                        if key in usable(q):
-                            term = weights[q, key] * v_tile
-                            sums[q] = term if key == 0 else sums[q] + term
-                for q in queries:
-                    row = pl.multiple_of(base + chunk * 8, 8)
-                    context[pl.ds(row, 8), q * zone_rows : (q + 1) * zone_rows] = sums[q] * scales[q]
-        return carry
-
-    lax.fori_loop(0, HEADS, head_body, 0)
+                row = head * head_size + chunk * 8
+                context[row : row + 8, q * zone_rows : (q + 1) * zone_rows] = sums[q] * scales[q]
+
+    spans = key_count * zone_rows // span
+    project_some(spans)
+    pairs = range(0, steps, 2)
+    for head in range(HEADS):
+        for pair in pairs:
+            project_some(-(-spans // len(pairs)))
+            attend(head, range(pair, min(pair + 2, steps)))
 
     for step in range(steps):
         rows = slice(step * zone_rows, (step + 1) * zone_rows)
@@ -273,25 +277,17 @@
     return [lax.rem(block, SPREAD) ^ bits for bits in (0, near, 6 - near, 6)]
 
 
-def fill_slots(zones, place, own_in, own_out, slots, pieces, w_in, w_out, sems):
+def fill_slots(zones, place, own_in, own_out, slots, pieces, w_in, w_out):
     my_zone = place[1]
     in_shard = own_in.shape[1]
     out_rows = own_out.shape[0] // SPREAD
     in_cols, width = own_in.shape[2], own_out.shape[1]
     own_rows = pl.ds(pl.multiple_of(my_zone * in_shard, in_shard), in_shard)
     own_out_rows = pl.ds(pl.multiple_of(my_zone * out_rows, out_rows), out_rows)
-    copies = []
-    for index, slot in enumerate(slots):
+    for index, (slot, piece) in enumerate(zip(slots, pieces)):
         from_rows = pl.ds(pl.multiple_of(slot * out_rows, out_rows), out_rows)
-        copies += [
-            pltpu.make_async_copy(own_in.at[slot], w_in.at[index, own_rows, :], sems.at[2 * index]),
-            pltpu.make_async_copy(
-                own_out.at[from_rows, :], w_out.at[index, own_out_rows, :], sems.at[2 * index + 1]
-            ),
-        ]
-    for copy in copies:
-        copy.start()
-    for index, piece in enumerate(pieces):
+        w_in[index, own_rows, :] = own_in[slot]
+        w_out[index, own_out_rows, :] = own_out[from_rows, :]
         for step in range(1, zones):
             source = my_zone ^ step
             part = piece[step - 1]
@@ -301,15 +297,13 @@
             for fold in range(width // in_cols):
                 low = in_shard + fold * out_rows
                 w_out[index, rows, fold * in_cols : (fold + 1) * in_cols] = part[low : low + out_rows, :]
-    for copy in copies:
-        copy.wait()
-
-
-def order_kernel(zones, place, own_in, own_out, pair, far, swapped_pair, w_in, w_out, sems):
+
+
+def order_kernel(zones, place, own_in, own_out, pair, far, swapped_pair, w_in, w_out):
     my_block = place[0]
     slots = slots_of(my_block) + slots_of(my_block ^ 1)[:2]
     pieces = [group.at[index] for group in (pair, far, swapped_pair) for index in range(2)]
-    fill_slots(zones, place, own_in, own_out, slots, pieces, w_in, w_out, sems)
+    fill_slots(zones, place, own_in, own_out, slots, pieces, w_in, w_out)
 
 
 def after_kernel(zones, place, after_attn, gain_ffn, ready, far, *refs):
@@ -345,10 +339,10 @@
         out[rows, :] = ffn_rows(ffn_in[rows, :], w_in, w_out, after_mix[rows, :])
 
 
-def last_kernel(zones, place, own_in, own_out, total, ffn_in, swapped_far, out, w_in, w_out, sems):
+def last_kernel(zones, place, own_in, own_out, total, ffn_in, swapped_far, out, w_in, w_out):
     slots = slots_of(place[0] ^ 1)[2:]
     pieces = [swapped_far.at[index] for index in range(2)]
-    fill_slots(zones, place, own_in, own_out, slots, pieces, w_in, w_out, sems)
+    fill_slots(zones, place, own_in, own_out, slots, pieces, w_in, w_out)
     span = 256
     for first in range(0, total.shape[0], span):
         rows = slice(first, first + span)
@@ -457,7 +451,7 @@
         [
             pltpu.VMEM((4, width, width), BF16),
             pltpu.VMEM((3 * width, width), BF16),
-            pltpu.VMEM((3 * width, key_count * zone_rows), F32),
+            pltpu.VMEM((HEADS, 3 * (width // HEADS), key_count * zone_rows), F32),
             pltpu.VMEM((width, rows), F32),
             pltpu.SemaphoreType.DMA((4,)),
         ],
@@ -510,9 +504,9 @@
             jax.ShapeDtypeStruct((6, width, in_cols), BF16),
             jax.ShapeDtypeStruct((6, in_cols, width), BF16),
         ),
-        [pltpu.SemaphoreType.DMA((12,))],
+        [],
         (0,),
-        (1, 2),
+        (),
         8,
         [place, own_in, w_out, pair, far, swapped(pair, "tm", 1)],
     )
@@ -547,10 +541,9 @@
         [
             pltpu.VMEM((2, width, in_cols), BF16),
             pltpu.VMEM((2, in_cols, width), BF16),
-            pltpu.SemaphoreType.DMA((4,)),
         ],
         (0,),
-        (1, 2),
+        (),
         8,
         [place, own_in, w_out, total, ffn_in, swapped(far, "tm", 1)],
     )

time: 75.1 us -> 74.6 us (level)
  Pallas kernels: 16.9 us -> 14.8 us
  waiting for transfers between devices: 30.1 us -> 31.7 us
    pallas_call x11, Pallas kernels: 16.9 us -> 14.8 us  [call(): pl.pallas_call(kernel, out_shape=out_shape, in_specs=[pl.BlockSpec(memory...]
    ppermute x17, waiting for transfers between devices: 18.6 us -> 20.2 us  [swapped(): lax.ppermute(value, axis, [(source, source ^ bits) for source in range(co...]
  transfers between devices with their start and end apart: 22 -> 22, of which waited for: 10 -> 12; matrix products, arithmetic and copies ran while one was open for 1% -> 1% of each run, Pallas kernels for 15% -> 13%
where the time goes in v11:
time: 74.6 us; the launch traced here: 74.4 us
  waiting for transfers between devices  31.7 us (42%)
  starting transfers between devices  24.4 us (33%)
  Pallas kernels  14.8 us (20%)
  local copies, waits for them, and re-layouts  2.14 us (3%)
  other arithmetic  1.04 us (1%)
    ppermute x17, waiting for transfers between devices, swapped(): lax.ppermute(value, axis, [(source, source ^ bits) for source in range(co...  20.2 us
    ppermute x17, starting transfers between devices, swapped(): lax.ppermute(value, axis, [(source, source ^ bits) for source in range(co...  15.2 us
    pallas_call x11, Pallas kernels, call(): pl.pallas_call(kernel, out_shape=out_shape, in_specs=[pl.BlockSpec(memory...  14.8 us
    ppermute x4, waiting for transfers between devices, crossed(): return lax.ppermute(value, axis, pairs)  11.5 us
    ppermute x1, starting transfers between devices, shifted(): lax.ppermute(value, axis, [(source, source + steps) for source in range(c...  4.99 us
    ppermute x4, starting transfers between devices, crossed(): return lax.ppermute(value, axis, pairs)  4.22 us
    unnamed x26, local copies, waits for them, and re-layouts  2.14 us
  transfers between devices with their start and end apart: 22, of which 12 were waited for; matrix products, arithmetic and copies ran while one was open for 1% of the time, Pallas kernels for 13%

profile of v11, /device:TPU:0, one launch (start us, length us, event | category | flops | bytes accessed | tf_op | source)
XLA Modules:
  0.0 74.4 jit_solution(13360322596959709963)
XLA Ops:
  0.0 5.0 %collective-permute-start = (bf16[4,128,512]{2,1,0:T(8,128)(2,1)}, bf16[4,128,512]{2,1,0:T(8,128)(2,1)S(1)}, u32[]{:S(2)}, u32[]{:S(2)}) collective-permute-start(bf16[4,128,512]{2,1,0:T(8,128)(2,1)} %states.3), channel_id=1, source_target_pairs={{0,8},{4,12},{8,16},{12,20},{16,24},{20,28},{1,9},{5,13},{9,17},{1... | collective-permute-start | bytes 1572872 | tf_op jit(solution)/shard_map/ppermute | solution.py:20
  6.0 3.7 %collective-permute-start.3 = (bf16[128,512]{1,0:T(8,128)(2,1)S(1)}, bf16[128,512]{1,0:T(8,128)(2,1)S(1)}, u32[]{:S(2)}, u32[]{:S(2)}) collective-permute-start(bf16[128,512]{1,0:T(8,128)(2,1)S(1)} %fusion), channel_id=1, source_target_pairs={{0,3},{1,2},{2,1},{3,0},{4,7},{5,6},{6,5},{7,4},{8,11},{9,10},{10,... | collective-permute-start | bytes 393224 | tf_op jit(solution)/shard_map/ppermute | solution.py:25
  10.5 1.0 %copy-done.1 = bf16[512,512]{1,0:T(8,128)(2,1)S(1)} copy-done((bf16[512,512]{1,0:T(8,128)(2,1)S(1)}, bf16[512,512]{1,0:T(8,128)(2,1)}, u32[]{:S(2)}) %copy-start.1) | copy-done | bytes 524312
  11.6 1.0 %copy-done.5 = bf16[128,2048]{1,0:T(8,128)(2,1)S(1)} copy-done((bf16[128,2048]{1,0:T(8,128)(2,1)S(1)}, bf16[128,2048]{1,0:T(8,128)(2,1)}, u32[]{:S(2)}) %copy-start.5) | copy-done | bytes 524312
  13.5 1.3 %collective-permute-start.1 = (bf16[256,256]{1,0:T(8,128)(2,1)S(1)}, bf16[256,256]{1,0:T(8,128)(2,1)S(1)}, u32[]{:S(2)}, u32[]{:S(2)}) collective-permute-start(bf16[256,256]{1,0:T(8,128)(2,1)S(1)} %get-tuple-element.30.packed), channel_id=1, source_target_pairs={{0,1},{1,0},{2,3},{3,2},{4,5},{5,4},{6,7},{7,6},{8,9},{9,8},{10,11... | collective-permute-start | bytes 393224 | tf_op jit(solution)/shard_map/ppermute | solution.py:25
  14.8 5.8 %collective-permute-done.2.refs_0_ = bf16[128,512]{1,0:T(8,128)(2,1)S(1)} collective-permute-done((bf16[128,512]{1,0:T(8,128)(2,1)S(1)}, bf16[128,512]{1,0:T(8,128)(2,1)S(1)}, u32[]{:S(2)}, u32[]{:S(2)}) %collective-permute-start.2) | collective-permute-done | bytes 131104 | tf_op jit(solution)/shard_map/ppermute | solution.py:25
  22.2 1.5 %collective-permute-start.6 = (bf16[3,64,512]{2,1,0:T(8,128)(2,1)S(1)}, bf16[3,64,512]{2,1,0:T(8,128)(2,1)S(1)}, u32[]{:S(2)}, u32[]{:S(2)}) collective-permute-start(bf16[3,64,512]{2,1,0:T(8,128)(2,1)S(1)} %get-tuple-element.33), channel_id=1, source_target_pairs={{0,8},{4,20},{8,0},{12,28},{16,24},{20,4},{24,16},{28,12},{1,9},{5... | collective-permute-start | bytes 589832 | tf_op jit(solution)/shard_map/ppermute | solution.py:31
  24.3 1.3 %collective-permute-start.14 = (bf16[2,256,256]{2,1,0:T(8,128)(2,1)S(1)}, bf16[2,256,256]{2,1,0:T(8,128)(2,1)S(1)}, u32[]{:S(2)}, u32[]{:S(2)}) collective-permute-start(bf16[2,256,256]{2,1,0:T(8,128)(2,1)S(1)} %get-tuple-element.42.doubled), channel_id=1, source_target_pairs={{0,2},{1,3},{2,0},{3,1},{4,6},{5,7},{6,4},{7,5},{8,10},{9,11},{10,... | collective-permute-start | bytes 786440 | tf_op jit(solution)/shard_map/ppermute | solution.py:25
  25.6 2.4 %collective-permute-done.6.refs_1_ = bf16[3,64,512]{2,1,0:T(8,128)(2,1)S(1)} collective-permute-done((bf16[3,64,512]{2,1,0:T(8,128)(2,1)S(1)}, bf16[3,64,512]{2,1,0:T(8,128)(2,1)S(1)}, u32[]{:S(2)}, u32[]{:S(2)}) %collective-permute-start.6) | collective-permute-done | bytes 196640 | tf_op jit(solution)/shard_map/ppermute | solution.py:31
  27.9 2.1 %collective-permute-done.7.refs_2_ = bf16[3,64,512]{2,1,0:T(8,128)(2,1)S(1)} collective-permute-done((bf16[3,64,512]{2,1,0:T(8,128)(2,1)S(1)}, bf16[3,64,512]{2,1,0:T(8,128)(2,1)S(1)}, u32[]{:S(2)}, u32[]{:S(2)}) %collective-permute-start.7) | collective-permute-done | bytes 196640 | tf_op jit(solution)/shard_map/ppermute | solution.py:31
  31.5 4.4 %shard_map.121 = (bf16[512,512]{1,0:T(8,128)(2,1)S(1)}, bf16[512,512]{1,0:T(8,128)(2,1)S(1)}) custom-call(s32[2]{0:T(128)S(1)} %pad_add_fusion.place, s32[1,2]{1,0:T(1,128)S(1)} %copy-done.11, bf16[1536,512]{1,0:T(8,128)(2,1)S(1)} %shard_map.120.normed, bf16[128,1536]{1,0:T(8,128)(2,1)S(1)} %copy-done.3, bf16[128,512]{1,0:T(8,128)(2,1)S(1)} %copy-done.4, ...), custom_call_target="tpu_custom_call" | custom-call | tf_op jit(solution)/shard_map/pallas_call | solution.py:354
  36.0 1.1 %shard_map.122 = (f32[512,512]{1,0:T(8,128)S(1)}, bf16[512,128]{1,0:T(8,128)(2,1)S(1)}, bf16[512,128]{1,0:T(8,128)(2,1)S(1)}, bf16[512,128]{1,0:T(8,128)(2,1)S(1)}, bf16[512,128]{1,0:T(8,128)(2,1)S(1)}) custom-call(s32[2]{0:T(128)S(1)} %pad_add_fusion.place, bf16[4,128,512]{2,1,0:T(8,128)(2,1)S(1)} %copy-done, ...), custom_call_target="tpu_custom_call" | custom-call | tf_op jit(solution)/shard_map/pallas_call | solution.py:354
  37.1 2.4 %collective-permute-done.14.arrived = bf16[2,256,256]{2,1,0:T(8,128)(2,1)S(1)} collective-permute-done((bf16[2,256,256]{2,1,0:T(8,128)(2,1)S(1)}, bf16[2,256,256]{2,1,0:T(8,128)(2,1)S(1)}, u32[]{:S(2)}, u32[]{:S(2)}) %collective-permute-start.14) | collective-permute-done | bytes 262176 | tf_op jit(solution)/shard_map/ppermute | solution.py:25
  39.5 1.5 %collective-permute-start.15 = (bf16[3,256,256]{2,1,0:T(8,128)(2,1)S(1)}, bf16[3,256,256]{2,1,0:T(8,128)(2,1)S(1)}, u32[]{:S(2)}, u32[]{:S(2)}) collective-permute-start(bf16[3,256,256]{2,1,0:T(8,128)(2,1)S(1)} %shard_map.123.refs_4_), channel_id=1, source_target_pairs={{0,8},{4,20},{8,0},{12,28},{16,24},{20,4},{24,16},{28,12},{1,9},{5... | collective-permute-start | bytes 1179656 | tf_op jit(solution)/shard_map/ppermute | solution.py:31
  41.1 2.2 %collective-permute-start.12 = (bf16[512,128]{1,0:T(8,128)(2,1)S(1)}, bf16[512,128]{1,0:T(8,128)(2,1)S(1)}, u32[]{:S(2)}, u32[]{:S(2)}) collective-permute-start(bf16[512,128]{1,0:T(8,128)(2,1)S(1)} %get-tuple-element.40), channel_id=1, source_target_pairs={{0,3},{1,2},{2,1},{3,0},{4,7},{5,6},{6,5},{7,4},{8,11},{9,10},{10,... | collective-permute-start | bytes 393224 | tf_op jit(solution)/shard_map/ppermute | solution.py:25
  43.3 1.3 %collective-permute-start.13 = (bf16[512,128]{1,0:T(8,128)(2,1)S(1)}, bf16[512,128]{1,0:T(8,128)(2,1)S(1)}, u32[]{:S(2)}, u32[]{:S(2)}) collective-permute-start(bf16[512,128]{1,0:T(8,128)(2,1)S(1)} %get-tuple-element.41), channel_id=1, source_target_pairs={{0,1},{1,0},{2,3},{3,2},{4,5},{5,4},{6,7},{7,6},{8,9},{9,8},{10,11... | collective-permute-start | bytes 393224 | tf_op jit(solution)/shard_map/ppermute | solution.py:25
  44.6 7.9 %collective-permute-done.11.refs_1_ = bf16[512,128]{1,0:T(8,128)(2,1)S(1)} collective-permute-done((bf16[512,128]{1,0:T(8,128)(2,1)S(1)}, bf16[512,128]{1,0:T(8,128)(2,1)S(1)}, u32[]{:S(2)}, u32[]{:S(2)}) %collective-permute-start.11) | collective-permute-done | bytes 131104 | tf_op jit(solution)/shard_map/ppermute | solution.py:25
  52.5 1.2 %collective-permute-done.13.refs_3_ = bf16[512,128]{1,0:T(8,128)(2,1)S(1)} collective-permute-done((bf16[512,128]{1,0:T(8,128)(2,1)S(1)}, bf16[512,128]{1,0:T(8,128)(2,1)S(1)}, u32[]{:S(2)}, u32[]{:S(2)}) %collective-permute-start.13) | collective-permute-done | bytes 131104 | tf_op jit(solution)/shard_map/ppermute | solution.py:25
  53.7 1.1 %shard_map.124 = (bf16[512,128]{1,0:T(8,128)(2,1)S(1)}, bf16[512,128]{1,0:T(8,128)(2,1)S(1)}, bf16[512,128]{1,0:T(8,128)(2,1)S(1)}, bf16[512,128]{1,0:T(8,128)(2,1)S(1)}, bf16[2,3,256,256]{3,2,1,0:T(8,128)(2,1)S(1)}) custom-call(s32[2]{0:T(128)S(1)} %pad_add_fusion.place, s32[4,3]{1,0:T(4,128)S(1)} %copy-done.8, s32[4]{0:T(128)S(1)} %copy-done.12, ...), custom_call_target="tpu_custom_call" | custom-call | tf_op jit(solution)/shard_map/pallas_call | solution.py:354
  55.5 1.9 %collective-permute-start.18 = (bf16[512,128]{1,0:T(8,128)(2,1)S(1)}, bf16[512,128]{1,0:T(8,128)(2,1)S(1)}, u32[]{:S(2)}, u32[]{:S(2)}) collective-permute-start(bf16[512,128]{1,0:T(8,128)(2,1)S(1)} %get-tuple-element.46), channel_id=1, source_target_pairs={{0,2},{1,3},{2,0},{3,1},{4,6},{5,7},{6,4},{7,5},{8,10},{9,11},{10,... | collective-permute-start | bytes 393224 | tf_op jit(solution)/shard_map/ppermute | solution.py:25
  57.4 2.5 %collective-permute-start.19 = (bf16[512,128]{1,0:T(8,128)(2,1)S(1)}, bf16[512,128]{1,0:T(8,128)(2,1)S(1)}, u32[]{:S(2)}, u32[]{:S(2)}) collective-permute-start(bf16[512,128]{1,0:T(8,128)(2,1)S(1)} %get-tuple-element.47), channel_id=1, source_target_pairs={{0,3},{1,2},{2,1},{3,0},{4,7},{5,6},{6,5},{7,4},{8,11},{9,10},{10,... | collective-permute-start | bytes 393224 | tf_op jit(solution)/shard_map/ppermute | solution.py:25
  60.0 7.0 %collective-permute-done.16.far = bf16[2,3,256,256]{3,2,1,0:T(8,128)(2,1)S(1)} collective-permute-done((bf16[2,3,256,256]{3,2,1,0:T(8,128)(2,1)S(1)}, bf16[2,3,256,256]{3,2,1,0:T(8,128)(2,1)S(1)}, u32[]{:S(2)}, u32[]{:S(2)}) %collective-permute-start.16) | collective-permute-done | bytes 786464 | tf_op jit(solution)/shard_map/ppermute | solution.py:31
  69.8 2.0 %shard_map.127.total = f32[512,512]{1,0:T(8,128)S(1)} custom-call(f32[512,512]{1,0:T(8,128)S(1)} %get-tuple-element.49.after_mix, bf16[512,512]{1,0:T(8,128)(2,1)S(1)} %get-tuple-element.50.ffn_in, bf16[6,512,256]{2,1,0:T(8,128)(2,1)S(1)} %get-tuple-element.51.w_in, bf16[6,256,512]{2,1,0:T(8,128)(2,1)S(1)} %get-tuple-element.44.ready.w_out), custom_call_target="tpu_custom_call" | custom-call | tf_op jit(solution)/shard_map/pallas_call | solution.py:354
  72.1 2.3 %shard_map.128 = bf16[512,512]{1,0:T(8,128)(2,1)} custom-call(s32[2]{0:T(128)S(1)} %pad_add_fusion.place, bf16[8,128,256]{2,1,0:T(8,128)(2,1)S(1)} %get-tuple-element.29.own_in, bf16[512,512]{1,0:T(8,128)(2,1)S(1)} %copy-done.2, f32[512,512]{1,0:T(8,128)S(1)} %shard_map.127.total, bf16[512,512]{1,0:T(8,128)(2,1)S(1)} %get-tuple-element.50.ffn_in, ...), custom_call_target="tpu_custom_call" | custom-call | tf_op jit(solution)/shard_map/pallas_call | solution.py:354
  (59 shorter events, 10.0 us)
Async XLA Ops:
  0.0 21.4 %collective-permute-start = (bf16[4,128,512]{2,1,0:T(8,128)(2,1)}, bf16[4,128,512]{2,1,0:T(8,128)(2,1)S(1)}, u32[]{:S(2)}, u32[]{:S(2)}) collective-permute-start(bf16[4,128,512]{2,1,0:T(8,128)(2,1)} %states.3), channel_id=1, source_target_pairs={{0,8},{4,12},{8,16},{12,20},{16,24},{20,28},{1,9},{5,13},{9,17},{1... | collective-permute-start | bytes 1572872 | tf_op jit(solution)/shard_map/ppermute | solution.py:20
  5.0 25.0 %copy-start.10 = (f32[512]{0:T(512)S(1)}, f32[512]{0:T(512)}, u32[]{:S(2)}) copy-start(f32[512]{0:T(512)} %param.13) | copy-start | bytes 6148
  6.0 8.8 %collective-permute-start.3 = (bf16[128,512]{1,0:T(8,128)(2,1)S(1)}, bf16[128,512]{1,0:T(8,128)(2,1)S(1)}, u32[]{:S(2)}, u32[]{:S(2)}) collective-permute-start(bf16[128,512]{1,0:T(8,128)(2,1)S(1)} %fusion), channel_id=1, source_target_pairs={{0,3},{1,2},{2,1},{3,0},{4,7},{5,6},{6,5},{7,4},{8,11},{9,10},{10,... | collective-permute-start | bytes 393224 | tf_op jit(solution)/shard_map/ppermute | solution.py:25
  9.7 10.9 %collective-permute-start.2 = (bf16[128,512]{1,0:T(8,128)(2,1)S(1)}, bf16[128,512]{1,0:T(8,128)(2,1)S(1)}, u32[]{:S(2)}, u32[]{:S(2)}) collective-permute-start(bf16[128,512]{1,0:T(8,128)(2,1)S(1)} %fusion), channel_id=1, source_target_pairs={{0,2},{1,3},{2,0},{3,1},{4,6},{5,7},{6,4},{7,5},{8,10},{9,11},{10,... | collective-permute-start | bytes 393224 | tf_op jit(solution)/shard_map/ppermute | solution.py:25
  9.7 10.9 %collective-permute-start.4 = (bf16[128,512]{1,0:T(8,128)(2,1)S(1)}, bf16[128,512]{1,0:T(8,128)(2,1)S(1)}, u32[]{:S(2)}, u32[]{:S(2)}) collective-permute-start(bf16[128,512]{1,0:T(8,128)(2,1)S(1)} %fusion), channel_id=1, source_target_pairs={{0,1},{1,0},{2,3},{3,2},{4,5},{5,4},{6,7},{7,6},{8,9},{9,8},{10,11... | collective-permute-start | bytes 393224 | tf_op jit(solution)/shard_map/ppermute | solution.py:25
  13.5 7.9 %collective-permute-start.1 = (bf16[256,256]{1,0:T(8,128)(2,1)S(1)}, bf16[256,256]{1,0:T(8,128)(2,1)S(1)}, u32[]{:S(2)}, u32[]{:S(2)}) collective-permute-start(bf16[256,256]{1,0:T(8,128)(2,1)S(1)} %get-tuple-element.30.packed), channel_id=1, source_target_pairs={{0,1},{1,0},{2,3},{3,2},{4,5},{5,4},{6,7},{7,6},{8,9},{9,8},{10,11... | collective-permute-start | bytes 393224 | tf_op jit(solution)/shard_map/ppermute | solution.py:25
  22.1 7.9 %collective-permute-start.5 = (bf16[4,128,512]{2,1,0:T(8,128)(2,1)S(1)}, bf16[4,128,512]{2,1,0:T(8,128)(2,1)S(1)}, u32[]{:S(2)}, u32[]{:S(2)}) collective-permute-start(bf16[4,128,512]{2,1,0:T(8,128)(2,1)S(1)} %get-tuple-element.31), channel_id=1, source_target_pairs={{0,4},{4,0},{8,12},{12,8},{16,20},{20,16},{24,28},{28,24},{1,5},{5... | collective-permute-start | bytes 1572872 | tf_op jit(solution)/shard_map/ppermute | solution.py:25
  22.2 5.7 %collective-permute-start.6 = (bf16[3,64,512]{2,1,0:T(8,128)(2,1)S(1)}, bf16[3,64,512]{2,1,0:T(8,128)(2,1)S(1)}, u32[]{:S(2)}, u32[]{:S(2)}) collective-permute-start(bf16[3,64,512]{2,1,0:T(8,128)(2,1)S(1)} %get-tuple-element.33), channel_id=1, source_target_pairs={{0,8},{4,20},{8,0},{12,28},{16,24},{20,4},{24,16},{28,12},{1,9},{5... | collective-permute-start | bytes 589832 | tf_op jit(solution)/shard_map/ppermute | solution.py:31
  23.7 6.3 %collective-permute-start.7 = (bf16[3,64,512]{2,1,0:T(8,128)(2,1)S(1)}, bf16[3,64,512]{2,1,0:T(8,128)(2,1)S(1)}, u32[]{:S(2)}, u32[]{:S(2)}) collective-permute-start(bf16[3,64,512]{2,1,0:T(8,128)(2,1)S(1)} %get-tuple-element.34), channel_id=1, source_target_pairs={{0,8},{4,20},{8,0},{12,28},{16,24},{20,4},{24,16},{28,12},{1,9},{5... | collective-permute-start | bytes 589832 | tf_op jit(solution)/shard_map/ppermute | solution.py:31
  24.3 7.2 %collective-permute-start.8 = (bf16[3,128,512]{2,1,0:T(8,128)(2,1)S(1)}, bf16[3,128,512]{2,1,0:T(8,128)(2,1)S(1)}, u32[]{:S(2)}, u32[]{:S(2)}) collective-permute-start(bf16[3,128,512]{2,1,0:T(8,128)(2,1)S(1)} %get-tuple-element.32.refs_0_), channel_id=1, source_target_pairs={{0,4},{4,0},{8,12},{12,8},{16,20},{20,16},{24,28},{28,24},{1,5},{5... | collective-permute-start | bytes 1179656 | tf_op jit(solution)/shard_map/ppermute | solution.py:25
  24.3 15.2 %collective-permute-start.14 = (bf16[2,256,256]{2,1,0:T(8,128)(2,1)S(1)}, bf16[2,256,256]{2,1,0:T(8,128)(2,1)S(1)}, u32[]{:S(2)}, u32[]{:S(2)}) collective-permute-start(bf16[2,256,256]{2,1,0:T(8,128)(2,1)S(1)} %get-tuple-element.42.doubled), channel_id=1, source_target_pairs={{0,2},{1,3},{2,0},{3,1},{4,6},{5,7},{6,4},{7,5},{8,10},{9,11},{10,... | collective-permute-start | bytes 786440 | tf_op jit(solution)/shard_map/ppermute | solution.py:25
  27.9 2.8 %collective-permute-start.9 = (bf16[3,64,512]{2,1,0:T(8,128)(2,1)S(1)}, bf16[3,64,512]{2,1,0:T(8,128)(2,1)S(1)}, u32[]{:S(2)}, u32[]{:S(2)}) collective-permute-start(bf16[3,64,512]{2,1,0:T(8,128)(2,1)S(1)} %collective-permute-done.6.refs_1_), channel_id=1, source_target_pairs={{0,4},{4,0},{8,12},{12,8},{16,20},{20,16},{24,28},{28,24},{1,5},{5... | collective-permute-start | bytes 589832 | tf_op jit(solution)/shard_map/ppermute | solution.py:25
  30.0 1.4 %collective-permute-start.10 = (bf16[3,64,512]{2,1,0:T(8,128)(2,1)S(1)}, bf16[3,64,512]{2,1,0:T(8,128)(2,1)S(1)}, u32[]{:S(2)}, u32[]{:S(2)}) collective-permute-start(bf16[3,64,512]{2,1,0:T(8,128)(2,1)S(1)} %collective-permute-done.7.refs_2_), channel_id=1, source_target_pairs={{0,4},{4,0},{8,12},{12,8},{16,20},{20,16},{24,28},{28,24},{1,5},{5... | collective-permute-start | bytes 589832 | tf_op jit(solution)/shard_map/ppermute | solution.py:25
  39.5 27.5 %copy-start.2 = (bf16[512,512]{1,0:T(8,128)(2,1)S(1)}, bf16[512,512]{1,0:T(8,128)(2,1)}, u32[]{:S(2)}) copy-start(bf16[512,512]{1,0:T(8,128)(2,1)} %own_out.3) | copy-start | bytes 1572868
  39.5 14.2 %collective-permute-start.15 = (bf16[3,256,256]{2,1,0:T(8,128)(2,1)S(1)}, bf16[3,256,256]{2,1,0:T(8,128)(2,1)S(1)}, u32[]{:S(2)}, u32[]{:S(2)}) collective-permute-start(bf16[3,256,256]{2,1,0:T(8,128)(2,1)S(1)} %shard_map.123.refs_4_), channel_id=1, source_target_pairs={{0,8},{4,20},{8,0},{12,28},{16,24},{20,4},{24,16},{28,12},{1,9},{5... | collective-permute-start | bytes 1179656 | tf_op jit(solution)/shard_map/ppermute | solution.py:31
  41.1 11.4 %collective-permute-start.11 = (bf16[512,128]{1,0:T(8,128)(2,1)S(1)}, bf16[512,128]{1,0:T(8,128)(2,1)S(1)}, u32[]{:S(2)}, u32[]{:S(2)}) collective-permute-start(bf16[512,128]{1,0:T(8,128)(2,1)S(1)} %get-tuple-element.39), channel_id=1, source_target_pairs={{0,2},{1,3},{2,0},{3,1},{4,6},{5,7},{6,4},{7,5},{8,10},{9,11},{10,... | collective-permute-start | bytes 393224 | tf_op jit(solution)/shard_map/ppermute | solution.py:25
  41.1 11.4 %collective-permute-start.12 = (bf16[512,128]{1,0:T(8,128)(2,1)S(1)}, bf16[512,128]{1,0:T(8,128)(2,1)S(1)}, u32[]{:S(2)}, u32[]{:S(2)}) collective-permute-start(bf16[512,128]{1,0:T(8,128)(2,1)S(1)} %get-tuple-element.40), channel_id=1, source_target_pairs={{0,3},{1,2},{2,1},{3,0},{4,7},{5,6},{6,5},{7,4},{8,11},{9,10},{10,... | collective-permute-start | bytes 393224 | tf_op jit(solution)/shard_map/ppermute | solution.py:25
  43.3 10.5 %collective-permute-start.13 = (bf16[512,128]{1,0:T(8,128)(2,1)S(1)}, bf16[512,128]{1,0:T(8,128)(2,1)S(1)}, u32[]{:S(2)}, u32[]{:S(2)}) collective-permute-start(bf16[512,128]{1,0:T(8,128)(2,1)S(1)} %get-tuple-element.41), channel_id=1, source_target_pairs={{0,1},{1,0},{2,3},{3,2},{4,5},{5,4},{6,7},{7,6},{8,9},{9,8},{10,11... | collective-permute-start | bytes 393224 | tf_op jit(solution)/shard_map/ppermute | solution.py:25
  54.9 5.1 %collective-permute-start.17 = (bf16[2,3,256,256]{3,2,1,0:T(8,128)(2,1)S(1)}, bf16[2,3,256,256]{3,2,1,0:T(8,128)(2,1)S(1)}, u32[]{:S(2)}, u32[]{:S(2)}) collective-permute-start(bf16[2,3,256,256]{3,2,1,0:T(8,128)(2,1)S(1)} %get-tuple-element.43.pair), channel_id=1, source_target_pairs={{0,4},{4,0},{8,12},{12,8},{16,20},{20,16},{24,28},{28,24},{1,5},{5... | collective-permute-start | bytes 2359304 | tf_op jit(solution)/shard_map/ppermute | solution.py:25
  54.9 12.1 %collective-permute-start.16 = (bf16[2,3,256,256]{3,2,1,0:T(8,128)(2,1)S(1)}, bf16[2,3,256,256]{3,2,1,0:T(8,128)(2,1)S(1)}, u32[]{:S(2)}, u32[]{:S(2)}) collective-permute-start(bf16[2,3,256,256]{3,2,1,0:T(8,128)(2,1)S(1)} %get-tuple-element.43.pair), channel_id=1, source_target_pairs={{0,16},{4,12},{8,24},{12,4},{16,0},{20,28},{24,8},{28,20},{1,17},{... | collective-permute-start | bytes 2359304 | tf_op jit(solution)/shard_map/ppermute | solution.py:31
  55.5 12.9 %collective-permute-start.18 = (bf16[512,128]{1,0:T(8,128)(2,1)S(1)}, bf16[512,128]{1,0:T(8,128)(2,1)S(1)}, u32[]{:S(2)}, u32[]{:S(2)}) collective-permute-start(bf16[512,128]{1,0:T(8,128)(2,1)S(1)} %get-tuple-element.46), channel_id=1, source_target_pairs={{0,2},{1,3},{2,0},{3,1},{4,6},{5,7},{6,4},{7,5},{8,10},{9,11},{10,... | collective-permute-start | bytes 393224 | tf_op jit(solution)/shard_map/ppermute | solution.py:25
  57.4 11.0 %collective-permute-start.19 = (bf16[512,128]{1,0:T(8,128)(2,1)S(1)}, bf16[512,128]{1,0:T(8,128)(2,1)S(1)}, u32[]{:S(2)}, u32[]{:S(2)}) collective-permute-start(bf16[512,128]{1,0:T(8,128)(2,1)S(1)} %get-tuple-element.47), channel_id=1, source_target_pairs={{0,3},{1,2},{2,1},{3,0},{4,7},{5,6},{6,5},{7,4},{8,11},{9,10},{10,... | collective-permute-start | bytes 393224 | tf_op jit(solution)/shard_map/ppermute | solution.py:25
  60.0 8.9 %collective-permute-start.20 = (bf16[512,128]{1,0:T(8,128)(2,1)S(1)}, bf16[512,128]{1,0:T(8,128)(2,1)S(1)}, u32[]{:S(2)}, u32[]{:S(2)}) collective-permute-start(bf16[512,128]{1,0:T(8,128)(2,1)S(1)} %get-tuple-element.48), channel_id=1, source_target_pairs={{0,1},{1,0},{2,3},{3,2},{4,5},{5,4},{6,7},{7,6},{8,9},{9,8},{10,11... | collective-permute-start | bytes 393224 | tf_op jit(solution)/shard_map/ppermute | solution.py:25
  69.7 2.4 %collective-permute-start.21 = (bf16[2,3,256,256]{3,2,1,0:T(8,128)(2,1)S(1)}, bf16[2,3,256,256]{3,2,1,0:T(8,128)(2,1)S(1)}, u32[]{:S(2)}, u32[]{:S(2)}) collective-permute-start(bf16[2,3,256,256]{3,2,1,0:T(8,128)(2,1)S(1)} %get-tuple-element.52), channel_id=1, source_target_pairs={{0,4},{4,0},{8,12},{12,8},{16,20},{20,16},{24,28},{28,24},{1,5},{5... | collective-permute-start | bytes 2359304 | tf_op jit(solution)/shard_map/ppermute | solution.py:25
  (11 other events, 88.2 us)

commit v12 on v11

--- a/solution.py
+++ b/solution.py
@@ -131,7 +131,7 @@
         copy.wait()
     attn_out[...] = weights[3]
     group = 3 * head_size
-    for head in range(HEADS):
+    def turn(head):
         for kind in range(3):
             rows = slice(head * group + kind * head_size, head * group + (kind + 1) * head_size)
             w_turned[rows, :] = weights[kind, :, head * head_size : (head + 1) * head_size].T
@@ -151,6 +151,8 @@
     def project_some(count):
         for _ in range(min(count, len(pending))):
             head, first = pending.pop(0)
+            if first == 0:
+                turn(head)
             project(head, first, span)
 
     allowed_back = [
@@ -339,17 +341,22 @@
         out[rows, :] = ffn_rows(ffn_in[rows, :], w_in, w_out, after_mix[rows, :])
 
 
-def last_kernel(zones, place, own_in, own_out, total, ffn_in, swapped_far, out, w_in, w_out):
+def last_kernel(zones, place, own_in, own_out, total, ffn_in, swapped_far, out, w_in, w_out, rows_out, sems):
     slots = slots_of(place[0] ^ 1)[2:]
     pieces = [swapped_far.at[index] for index in range(2)]
     fill_slots(zones, place, own_in, own_out, slots, pieces, w_in, w_out)
-    span = 256
-    for first in range(0, total.shape[0], span):
-        rows = slice(first, first + span)
-        out[rows, :] = ffn_rows(ffn_in[rows, :], w_in, w_out, total[rows, :]).astype(BF16)
-
-
-def call(kernel, out_shape, scratch, smem, hbm, limit, args):
+    span = total.shape[0] // sems.shape[0]
+    copies = []
+    for index in range(sems.shape[0]):
+        rows = slice(index * span, (index + 1) * span)
+        rows_out[rows, :] = ffn_rows(ffn_in[rows, :], w_in, w_out, total[rows, :]).astype(BF16)
+        copies.append(pltpu.make_async_copy(rows_out.at[rows, :], out.at[rows, :], sems.at[index]))
+        copies[-1].start()
+    for copy in copies:
+        copy.wait()
+
+
+def call(kernel, out_shape, scratch, smem, hbm, limit, args, out_space=pltpu.VMEM):
     spaces = {index: pltpu.SMEM for index in smem} | {index: pltpu.HBM for index in hbm}
     return pl.pallas_call(
         kernel,
@@ -357,7 +364,7 @@
         in_specs=[
             pl.BlockSpec(memory_space=spaces.get(index, pltpu.VMEM)) for index in range(len(args))
         ],
-        out_specs=jax.tree.map(lambda _: pl.BlockSpec(memory_space=pltpu.VMEM), out_shape),
+        out_specs=jax.tree.map(lambda _: pl.BlockSpec(memory_space=out_space), out_shape),
         scratch_shapes=scratch,
         cost_estimate=pl.CostEstimate(flops=0, bytes_accessed=0, transcendentals=0),
         compiler_params=pltpu.CompilerParams(vmem_limit_bytes=limit * MIB),
@@ -541,11 +548,14 @@
         [
             pltpu.VMEM((2, width, in_cols), BF16),
             pltpu.VMEM((2, in_cols, width), BF16),
+            pltpu.VMEM((rows, width), BF16),
+            pltpu.SemaphoreType.DMA((4,)),
         ],
         (0,),
         (),
         8,
         [place, own_in, w_out, total, ffn_in, swapped(far, "tm", 1)],
+        pl.ANY,
     )
     return evolved.reshape(steps, zone_rows, width)
 

time: 74.6 us -> 74.5 us (level)
  no operation moved by 1% of the time
where the time goes in v12:
time: 74.5 us; the launch traced here: 74.3 us
  waiting for transfers between devices  31.7 us (43%)
  starting transfers between devices  24.4 us (33%)
  Pallas kernels  14.7 us (20%)
  local copies, waits for them, and re-layouts  2.14 us (3%)
  other arithmetic  1.04 us (1%)
    ppermute x17, waiting for transfers between devices, swapped(): lax.ppermute(value, axis, [(source, source ^ bits) for source in range(co...  20.2 us
    ppermute x17, starting transfers between devices, swapped(): lax.ppermute(value, axis, [(source, source ^ bits) for source in range(co...  15.2 us
    pallas_call x11, Pallas kernels, call(): pl.pallas_call(kernel, out_shape=out_shape, in_specs=[pl.BlockSpec(memory...  14.7 us
    ppermute x4, waiting for transfers between devices, crossed(): return lax.ppermute(value, axis, pairs)  11.5 us
    ppermute x1, starting transfers between devices, shifted(): lax.ppermute(value, axis, [(source, source + steps) for source in range(c...  4.99 us
    ppermute x4, starting transfers between devices, crossed(): return lax.ppermute(value, axis, pairs)  4.22 us
    unnamed x26, local copies, waits for them, and re-layouts  2.14 us
  transfers between devices with their start and end apart: 22, of which 12 were waited for; matrix products, arithmetic and copies ran while one was open for 1% of the time, Pallas kernels for 13%

profile of v12, /device:TPU:0, one launch (start us, length us, event | category | flops | bytes accessed | tf_op | source)
XLA Modules:
  0.0 74.3 jit_solution(14344974077773677378)
XLA Ops:
  0.0 5.0 %collective-permute-start = (bf16[4,128,512]{2,1,0:T(8,128)(2,1)}, bf16[4,128,512]{2,1,0:T(8,128)(2,1)S(1)}, u32[]{:S(2)}, u32[]{:S(2)}) collective-permute-start(bf16[4,128,512]{2,1,0:T(8,128)(2,1)} %states.3), channel_id=1, source_target_pairs={{0,8},{4,12},{8,16},{12,20},{16,24},{20,28},{1,9},{5,13},{9,17},{1... | collective-permute-start | bytes 1572872 | tf_op jit(solution)/shard_map/ppermute | solution.py:20
  6.0 3.7 %collective-permute-start.3 = (bf16[128,512]{1,0:T(8,128)(2,1)S(1)}, bf16[128,512]{1,0:T(8,128)(2,1)S(1)}, u32[]{:S(2)}, u32[]{:S(2)}) collective-permute-start(bf16[128,512]{1,0:T(8,128)(2,1)S(1)} %fusion), channel_id=1, source_target_pairs={{0,3},{1,2},{2,1},{3,0},{4,7},{5,6},{6,5},{7,4},{8,11},{9,10},{10,... | collective-permute-start | bytes 393224 | tf_op jit(solution)/shard_map/ppermute | solution.py:25
  10.5 1.0 %copy-done.1 = bf16[512,512]{1,0:T(8,128)(2,1)S(1)} copy-done((bf16[512,512]{1,0:T(8,128)(2,1)S(1)}, bf16[512,512]{1,0:T(8,128)(2,1)}, u32[]{:S(2)}) %copy-start.1) | copy-done | bytes 524312
  11.6 1.0 %copy-done.5 = bf16[128,2048]{1,0:T(8,128)(2,1)S(1)} copy-done((bf16[128,2048]{1,0:T(8,128)(2,1)S(1)}, bf16[128,2048]{1,0:T(8,128)(2,1)}, u32[]{:S(2)}) %copy-start.5) | copy-done | bytes 524312
  13.5 1.3 %collective-permute-start.1 = (bf16[256,256]{1,0:T(8,128)(2,1)S(1)}, bf16[256,256]{1,0:T(8,128)(2,1)S(1)}, u32[]{:S(2)}, u32[]{:S(2)}) collective-permute-start(bf16[256,256]{1,0:T(8,128)(2,1)S(1)} %get-tuple-element.30.packed), channel_id=1, source_target_pairs={{0,1},{1,0},{2,3},{3,2},{4,5},{5,4},{6,7},{7,6},{8,9},{9,8},{10,11... | collective-permute-start | bytes 393224 | tf_op jit(solution)/shard_map/ppermute | solution.py:25
  14.8 5.8 %collective-permute-done.2.refs_0_ = bf16[128,512]{1,0:T(8,128)(2,1)S(1)} collective-permute-done((bf16[128,512]{1,0:T(8,128)(2,1)S(1)}, bf16[128,512]{1,0:T(8,128)(2,1)S(1)}, u32[]{:S(2)}, u32[]{:S(2)}) %collective-permute-start.2) | collective-permute-done | bytes 131104 | tf_op jit(solution)/shard_map/ppermute | solution.py:25
  22.2 1.5 %collective-permute-start.6 = (bf16[3,64,512]{2,1,0:T(8,128)(2,1)S(1)}, bf16[3,64,512]{2,1,0:T(8,128)(2,1)S(1)}, u32[]{:S(2)}, u32[]{:S(2)}) collective-permute-start(bf16[3,64,512]{2,1,0:T(8,128)(2,1)S(1)} %get-tuple-element.33), channel_id=1, source_target_pairs={{0,8},{4,20},{8,0},{12,28},{16,24},{20,4},{24,16},{28,12},{1,9},{5... | collective-permute-start | bytes 589832 | tf_op jit(solution)/shard_map/ppermute | solution.py:31
  24.3 1.3 %collective-permute-start.14 = (bf16[2,256,256]{2,1,0:T(8,128)(2,1)S(1)}, bf16[2,256,256]{2,1,0:T(8,128)(2,1)S(1)}, u32[]{:S(2)}, u32[]{:S(2)}) collective-permute-start(bf16[2,256,256]{2,1,0:T(8,128)(2,1)S(1)} %get-tuple-element.42.doubled), channel_id=1, source_target_pairs={{0,2},{1,3},{2,0},{3,1},{4,6},{5,7},{6,4},{7,5},{8,10},{9,11},{10,... | collective-permute-start | bytes 786440 | tf_op jit(solution)/shard_map/ppermute | solution.py:25
  25.6 2.4 %collective-permute-done.6.refs_1_ = bf16[3,64,512]{2,1,0:T(8,128)(2,1)S(1)} collective-permute-done((bf16[3,64,512]{2,1,0:T(8,128)(2,1)S(1)}, bf16[3,64,512]{2,1,0:T(8,128)(2,1)S(1)}, u32[]{:S(2)}, u32[]{:S(2)}) %collective-permute-start.6) | collective-permute-done | bytes 196640 | tf_op jit(solution)/shard_map/ppermute | solution.py:31
  27.9 2.1 %collective-permute-done.7.refs_2_ = bf16[3,64,512]{2,1,0:T(8,128)(2,1)S(1)} collective-permute-done((bf16[3,64,512]{2,1,0:T(8,128)(2,1)S(1)}, bf16[3,64,512]{2,1,0:T(8,128)(2,1)S(1)}, u32[]{:S(2)}, u32[]{:S(2)}) %collective-permute-start.7) | collective-permute-done | bytes 196640 | tf_op jit(solution)/shard_map/ppermute | solution.py:31
  31.5 4.4 %shard_map.121 = (bf16[512,512]{1,0:T(8,128)(2,1)S(1)}, bf16[512,512]{1,0:T(8,128)(2,1)S(1)}) custom-call(s32[2]{0:T(128)S(1)} %pad_add_fusion.place, s32[1,2]{1,0:T(1,128)S(1)} %copy-done.11, bf16[1536,512]{1,0:T(8,128)(2,1)S(1)} %shard_map.120.normed, bf16[128,1536]{1,0:T(8,128)(2,1)S(1)} %copy-done.3, bf16[128,512]{1,0:T(8,128)(2,1)S(1)} %copy-done.4, ...), custom_call_target="tpu_custom_call" | custom-call | tf_op jit(solution)/shard_map/pallas_call | solution.py:361
  36.0 1.1 %shard_map.122 = (f32[512,512]{1,0:T(8,128)S(1)}, bf16[512,128]{1,0:T(8,128)(2,1)S(1)}, bf16[512,128]{1,0:T(8,128)(2,1)S(1)}, bf16[512,128]{1,0:T(8,128)(2,1)S(1)}, bf16[512,128]{1,0:T(8,128)(2,1)S(1)}) custom-call(s32[2]{0:T(128)S(1)} %pad_add_fusion.place, bf16[4,128,512]{2,1,0:T(8,128)(2,1)S(1)} %copy-done, ...), custom_call_target="tpu_custom_call" | custom-call | tf_op jit(solution)/shard_map/pallas_call | solution.py:361
  37.1 2.4 %collective-permute-done.14.arrived = bf16[2,256,256]{2,1,0:T(8,128)(2,1)S(1)} collective-permute-done((bf16[2,256,256]{2,1,0:T(8,128)(2,1)S(1)}, bf16[2,256,256]{2,1,0:T(8,128)(2,1)S(1)}, u32[]{:S(2)}, u32[]{:S(2)}) %collective-permute-start.14) | collective-permute-done | bytes 262176 | tf_op jit(solution)/shard_map/ppermute | solution.py:25
  39.5 1.5 %collective-permute-start.15 = (bf16[3,256,256]{2,1,0:T(8,128)(2,1)S(1)}, bf16[3,256,256]{2,1,0:T(8,128)(2,1)S(1)}, u32[]{:S(2)}, u32[]{:S(2)}) collective-permute-start(bf16[3,256,256]{2,1,0:T(8,128)(2,1)S(1)} %shard_map.123.refs_4_), channel_id=1, source_target_pairs={{0,8},{4,20},{8,0},{12,28},{16,24},{20,4},{24,16},{28,12},{1,9},{5... | collective-permute-start | bytes 1179656 | tf_op jit(solution)/shard_map/ppermute | solution.py:31
  41.1 2.2 %collective-permute-start.12 = (bf16[512,128]{1,0:T(8,128)(2,1)S(1)}, bf16[512,128]{1,0:T(8,128)(2,1)S(1)}, u32[]{:S(2)}, u32[]{:S(2)}) collective-permute-start(bf16[512,128]{1,0:T(8,128)(2,1)S(1)} %get-tuple-element.40), channel_id=1, source_target_pairs={{0,3},{1,2},{2,1},{3,0},{4,7},{5,6},{6,5},{7,4},{8,11},{9,10},{10,... | collective-permute-start | bytes 393224 | tf_op jit(solution)/shard_map/ppermute | solution.py:25
  43.3 1.3 %collective-permute-start.13 = (bf16[512,128]{1,0:T(8,128)(2,1)S(1)}, bf16[512,128]{1,0:T(8,128)(2,1)S(1)}, u32[]{:S(2)}, u32[]{:S(2)}) collective-permute-start(bf16[512,128]{1,0:T(8,128)(2,1)S(1)} %get-tuple-element.41), channel_id=1, source_target_pairs={{0,1},{1,0},{2,3},{3,2},{4,5},{5,4},{6,7},{7,6},{8,9},{9,8},{10,11... | collective-permute-start | bytes 393224 | tf_op jit(solution)/shard_map/ppermute | solution.py:25
  44.6 7.9 %collective-permute-done.11.refs_1_ = bf16[512,128]{1,0:T(8,128)(2,1)S(1)} collective-permute-done((bf16[512,128]{1,0:T(8,128)(2,1)S(1)}, bf16[512,128]{1,0:T(8,128)(2,1)S(1)}, u32[]{:S(2)}, u32[]{:S(2)}) %collective-permute-start.11) | collective-permute-done | bytes 131104 | tf_op jit(solution)/shard_map/ppermute | solution.py:25
  52.5 1.2 %collective-permute-done.13.refs_3_ = bf16[512,128]{1,0:T(8,128)(2,1)S(1)} collective-permute-done((bf16[512,128]{1,0:T(8,128)(2,1)S(1)}, bf16[512,128]{1,0:T(8,128)(2,1)S(1)}, u32[]{:S(2)}, u32[]{:S(2)}) %collective-permute-start.13) | collective-permute-done | bytes 131104 | tf_op jit(solution)/shard_map/ppermute | solution.py:25
  53.7 1.1 %shard_map.124 = (bf16[512,128]{1,0:T(8,128)(2,1)S(1)}, bf16[512,128]{1,0:T(8,128)(2,1)S(1)}, bf16[512,128]{1,0:T(8,128)(2,1)S(1)}, bf16[512,128]{1,0:T(8,128)(2,1)S(1)}, bf16[2,3,256,256]{3,2,1,0:T(8,128)(2,1)S(1)}) custom-call(s32[2]{0:T(128)S(1)} %pad_add_fusion.place, s32[4,3]{1,0:T(4,128)S(1)} %copy-done.8, s32[4]{0:T(128)S(1)} %copy-done.12, ...), custom_call_target="tpu_custom_call" | custom-call | tf_op jit(solution)/shard_map/pallas_call | solution.py:361
  55.5 1.9 %collective-permute-start.18 = (bf16[512,128]{1,0:T(8,128)(2,1)S(1)}, bf16[512,128]{1,0:T(8,128)(2,1)S(1)}, u32[]{:S(2)}, u32[]{:S(2)}) collective-permute-start(bf16[512,128]{1,0:T(8,128)(2,1)S(1)} %get-tuple-element.46), channel_id=1, source_target_pairs={{0,2},{1,3},{2,0},{3,1},{4,6},{5,7},{6,4},{7,5},{8,10},{9,11},{10,... | collective-permute-start | bytes 393224 | tf_op jit(solution)/shard_map/ppermute | solution.py:25
  57.4 2.5 %collective-permute-start.19 = (bf16[512,128]{1,0:T(8,128)(2,1)S(1)}, bf16[512,128]{1,0:T(8,128)(2,1)S(1)}, u32[]{:S(2)}, u32[]{:S(2)}) collective-permute-start(bf16[512,128]{1,0:T(8,128)(2,1)S(1)} %get-tuple-element.47), channel_id=1, source_target_pairs={{0,3},{1,2},{2,1},{3,0},{4,7},{5,6},{6,5},{7,4},{8,11},{9,10},{10,... | collective-permute-start | bytes 393224 | tf_op jit(solution)/shard_map/ppermute | solution.py:25
  60.0 7.0 %collective-permute-done.16.far = bf16[2,3,256,256]{3,2,1,0:T(8,128)(2,1)S(1)} collective-permute-done((bf16[2,3,256,256]{3,2,1,0:T(8,128)(2,1)S(1)}, bf16[2,3,256,256]{3,2,1,0:T(8,128)(2,1)S(1)}, u32[]{:S(2)}, u32[]{:S(2)}) %collective-permute-start.16) | collective-permute-done | bytes 786464 | tf_op jit(solution)/shard_map/ppermute | solution.py:31
  69.8 2.0 %shard_map.127.total = f32[512,512]{1,0:T(8,128)S(1)} custom-call(f32[512,512]{1,0:T(8,128)S(1)} %get-tuple-element.49.after_mix, bf16[512,512]{1,0:T(8,128)(2,1)S(1)} %get-tuple-element.50.ffn_in, bf16[6,512,256]{2,1,0:T(8,128)(2,1)S(1)} %get-tuple-element.51.w_in, bf16[6,256,512]{2,1,0:T(8,128)(2,1)S(1)} %get-tuple-element.44.ready.w_out), custom_call_target="tpu_custom_call" | custom-call | tf_op jit(solution)/shard_map/pallas_call | solution.py:361
  72.1 2.2 %shard_map.128 = bf16[512,512]{1,0:T(8,128)(2,1)} custom-call(s32[2]{0:T(128)S(1)} %pad_add_fusion.place, bf16[8,128,256]{2,1,0:T(8,128)(2,1)S(1)} %get-tuple-element.29.own_in, bf16[512,512]{1,0:T(8,128)(2,1)S(1)} %copy-done.2, f32[512,512]{1,0:T(8,128)S(1)} %shard_map.127.total, bf16[512,512]{1,0:T(8,128)(2,1)S(1)} %get-tuple-element.50.ffn_in, ...), custom_call_target="tpu_custom_call" | custom-call | tf_op jit(solution)/shard_map/pallas_call | solution.py:361
  (59 shorter events, 10.0 us)
Async XLA Ops:
  0.0 21.4 %collective-permute-start = (bf16[4,128,512]{2,1,0:T(8,128)(2,1)}, bf16[4,128,512]{2,1,0:T(8,128)(2,1)S(1)}, u32[]{:S(2)}, u32[]{:S(2)}) collective-permute-start(bf16[4,128,512]{2,1,0:T(8,128)(2,1)} %states.3), channel_id=1, source_target_pairs={{0,8},{4,12},{8,16},{12,20},{16,24},{20,28},{1,9},{5,13},{9,17},{1... | collective-permute-start | bytes 1572872 | tf_op jit(solution)/shard_map/ppermute | solution.py:20
  5.0 25.0 %copy-start.10 = (f32[512]{0:T(512)S(1)}, f32[512]{0:T(512)}, u32[]{:S(2)}) copy-start(f32[512]{0:T(512)} %param.13) | copy-start | bytes 6148
  6.0 8.8 %collective-permute-start.3 = (bf16[128,512]{1,0:T(8,128)(2,1)S(1)}, bf16[128,512]{1,0:T(8,128)(2,1)S(1)}, u32[]{:S(2)}, u32[]{:S(2)}) collective-permute-start(bf16[128,512]{1,0:T(8,128)(2,1)S(1)} %fusion), channel_id=1, source_target_pairs={{0,3},{1,2},{2,1},{3,0},{4,7},{5,6},{6,5},{7,4},{8,11},{9,10},{10,... | collective-permute-start | bytes 393224 | tf_op jit(solution)/shard_map/ppermute | solution.py:25
  9.7 10.9 %collective-permute-start.2 = (bf16[128,512]{1,0:T(8,128)(2,1)S(1)}, bf16[128,512]{1,0:T(8,128)(2,1)S(1)}, u32[]{:S(2)}, u32[]{:S(2)}) collective-permute-start(bf16[128,512]{1,0:T(8,128)(2,1)S(1)} %fusion), channel_id=1, source_target_pairs={{0,2},{1,3},{2,0},{3,1},{4,6},{5,7},{6,4},{7,5},{8,10},{9,11},{10,... | collective-permute-start | bytes 393224 | tf_op jit(solution)/shard_map/ppermute | solution.py:25
  9.7 10.9 %collective-permute-start.4 = (bf16[128,512]{1,0:T(8,128)(2,1)S(1)}, bf16[128,512]{1,0:T(8,128)(2,1)S(1)}, u32[]{:S(2)}, u32[]{:S(2)}) collective-permute-start(bf16[128,512]{1,0:T(8,128)(2,1)S(1)} %fusion), channel_id=1, source_target_pairs={{0,1},{1,0},{2,3},{3,2},{4,5},{5,4},{6,7},{7,6},{8,9},{9,8},{10,11... | collective-permute-start | bytes 393224 | tf_op jit(solution)/shard_map/ppermute | solution.py:25
  13.5 7.9 %collective-permute-start.1 = (bf16[256,256]{1,0:T(8,128)(2,1)S(1)}, bf16[256,256]{1,0:T(8,128)(2,1)S(1)}, u32[]{:S(2)}, u32[]{:S(2)}) collective-permute-start(bf16[256,256]{1,0:T(8,128)(2,1)S(1)} %get-tuple-element.30.packed), channel_id=1, source_target_pairs={{0,1},{1,0},{2,3},{3,2},{4,5},{5,4},{6,7},{7,6},{8,9},{9,8},{10,11... | collective-permute-start | bytes 393224 | tf_op jit(solution)/shard_map/ppermute | solution.py:25
  22.1 7.9 %collective-permute-start.5 = (bf16[4,128,512]{2,1,0:T(8,128)(2,1)S(1)}, bf16[4,128,512]{2,1,0:T(8,128)(2,1)S(1)}, u32[]{:S(2)}, u32[]{:S(2)}) collective-permute-start(bf16[4,128,512]{2,1,0:T(8,128)(2,1)S(1)} %get-tuple-element.31), channel_id=1, source_target_pairs={{0,4},{4,0},{8,12},{12,8},{16,20},{20,16},{24,28},{28,24},{1,5},{5... | collective-permute-start | bytes 1572872 | tf_op jit(solution)/shard_map/ppermute | solution.py:25
  22.2 5.7 %collective-permute-start.6 = (bf16[3,64,512]{2,1,0:T(8,128)(2,1)S(1)}, bf16[3,64,512]{2,1,0:T(8,128)(2,1)S(1)}, u32[]{:S(2)}, u32[]{:S(2)}) collective-permute-start(bf16[3,64,512]{2,1,0:T(8,128)(2,1)S(1)} %get-tuple-element.33), channel_id=1, source_target_pairs={{0,8},{4,20},{8,0},{12,28},{16,24},{20,4},{24,16},{28,12},{1,9},{5... | collective-permute-start | bytes 589832 | tf_op jit(solution)/shard_map/ppermute | solution.py:31
  23.7 6.3 %collective-permute-start.7 = (bf16[3,64,512]{2,1,0:T(8,128)(2,1)S(1)}, bf16[3,64,512]{2,1,0:T(8,128)(2,1)S(1)}, u32[]{:S(2)}, u32[]{:S(2)}) collective-permute-start(bf16[3,64,512]{2,1,0:T(8,128)(2,1)S(1)} %get-tuple-element.34), channel_id=1, source_target_pairs={{0,8},{4,20},{8,0},{12,28},{16,24},{20,4},{24,16},{28,12},{1,9},{5... | collective-permute-start | bytes 589832 | tf_op jit(solution)/shard_map/ppermute | solution.py:31
  24.3 7.2 %collective-permute-start.8 = (bf16[3,128,512]{2,1,0:T(8,128)(2,1)S(1)}, bf16[3,128,512]{2,1,0:T(8,128)(2,1)S(1)}, u32[]{:S(2)}, u32[]{:S(2)}) collective-permute-start(bf16[3,128,512]{2,1,0:T(8,128)(2,1)S(1)} %get-tuple-element.32.refs_0_), channel_id=1, source_target_pairs={{0,4},{4,0},{8,12},{12,8},{16,20},{20,16},{24,28},{28,24},{1,5},{5... | collective-permute-start | bytes 1179656 | tf_op jit(solution)/shard_map/ppermute | solution.py:25
  24.3 15.2 %collective-permute-start.14 = (bf16[2,256,256]{2,1,0:T(8,128)(2,1)S(1)}, bf16[2,256,256]{2,1,0:T(8,128)(2,1)S(1)}, u32[]{:S(2)}, u32[]{:S(2)}) collective-permute-start(bf16[2,256,256]{2,1,0:T(8,128)(2,1)S(1)} %get-tuple-element.42.doubled), channel_id=1, source_target_pairs={{0,2},{1,3},{2,0},{3,1},{4,6},{5,7},{6,4},{7,5},{8,10},{9,11},{10,... | collective-permute-start | bytes 786440 | tf_op jit(solution)/shard_map/ppermute | solution.py:25
  27.9 2.8 %collective-permute-start.9 = (bf16[3,64,512]{2,1,0:T(8,128)(2,1)S(1)}, bf16[3,64,512]{2,1,0:T(8,128)(2,1)S(1)}, u32[]{:S(2)}, u32[]{:S(2)}) collective-permute-start(bf16[3,64,512]{2,1,0:T(8,128)(2,1)S(1)} %collective-permute-done.6.refs_1_), channel_id=1, source_target_pairs={{0,4},{4,0},{8,12},{12,8},{16,20},{20,16},{24,28},{28,24},{1,5},{5... | collective-permute-start | bytes 589832 | tf_op jit(solution)/shard_map/ppermute | solution.py:25
  30.0 1.4 %collective-permute-start.10 = (bf16[3,64,512]{2,1,0:T(8,128)(2,1)S(1)}, bf16[3,64,512]{2,1,0:T(8,128)(2,1)S(1)}, u32[]{:S(2)}, u32[]{:S(2)}) collective-permute-start(bf16[3,64,512]{2,1,0:T(8,128)(2,1)S(1)} %collective-permute-done.7.refs_2_), channel_id=1, source_target_pairs={{0,4},{4,0},{8,12},{12,8},{16,20},{20,16},{24,28},{28,24},{1,5},{5... | collective-permute-start | bytes 589832 | tf_op jit(solution)/shard_map/ppermute | solution.py:25
  39.5 27.5 %copy-start.2 = (bf16[512,512]{1,0:T(8,128)(2,1)S(1)}, bf16[512,512]{1,0:T(8,128)(2,1)}, u32[]{:S(2)}) copy-start(bf16[512,512]{1,0:T(8,128)(2,1)} %own_out.3) | copy-start | bytes 1572868
  39.5 14.2 %collective-permute-start.15 = (bf16[3,256,256]{2,1,0:T(8,128)(2,1)S(1)}, bf16[3,256,256]{2,1,0:T(8,128)(2,1)S(1)}, u32[]{:S(2)}, u32[]{:S(2)}) collective-permute-start(bf16[3,256,256]{2,1,0:T(8,128)(2,1)S(1)} %shard_map.123.refs_4_), channel_id=1, source_target_pairs={{0,8},{4,20},{8,0},{12,28},{16,24},{20,4},{24,16},{28,12},{1,9},{5... | collective-permute-start | bytes 1179656 | tf_op jit(solution)/shard_map/ppermute | solution.py:31
  41.1 11.4 %collective-permute-start.11 = (bf16[512,128]{1,0:T(8,128)(2,1)S(1)}, bf16[512,128]{1,0:T(8,128)(2,1)S(1)}, u32[]{:S(2)}, u32[]{:S(2)}) collective-permute-start(bf16[512,128]{1,0:T(8,128)(2,1)S(1)} %get-tuple-element.39), channel_id=1, source_target_pairs={{0,2},{1,3},{2,0},{3,1},{4,6},{5,7},{6,4},{7,5},{8,10},{9,11},{10,... | collective-permute-start | bytes 393224 | tf_op jit(solution)/shard_map/ppermute | solution.py:25
  41.1 11.4 %collective-permute-start.12 = (bf16[512,128]{1,0:T(8,128)(2,1)S(1)}, bf16[512,128]{1,0:T(8,128)(2,1)S(1)}, u32[]{:S(2)}, u32[]{:S(2)}) collective-permute-start(bf16[512,128]{1,0:T(8,128)(2,1)S(1)} %get-tuple-element.40), channel_id=1, source_target_pairs={{0,3},{1,2},{2,1},{3,0},{4,7},{5,6},{6,5},{7,4},{8,11},{9,10},{10,... | collective-permute-start | bytes 393224 | tf_op jit(solution)/shard_map/ppermute | solution.py:25
  43.3 10.5 %collective-permute-start.13 = (bf16[512,128]{1,0:T(8,128)(2,1)S(1)}, bf16[512,128]{1,0:T(8,128)(2,1)S(1)}, u32[]{:S(2)}, u32[]{:S(2)}) collective-permute-start(bf16[512,128]{1,0:T(8,128)(2,1)S(1)} %get-tuple-element.41), channel_id=1, source_target_pairs={{0,1},{1,0},{2,3},{3,2},{4,5},{5,4},{6,7},{7,6},{8,9},{9,8},{10,11... | collective-permute-start | bytes 393224 | tf_op jit(solution)/shard_map/ppermute | solution.py:25
  54.9 5.1 %collective-permute-start.17 = (bf16[2,3,256,256]{3,2,1,0:T(8,128)(2,1)S(1)}, bf16[2,3,256,256]{3,2,1,0:T(8,128)(2,1)S(1)}, u32[]{:S(2)}, u32[]{:S(2)}) collective-permute-start(bf16[2,3,256,256]{3,2,1,0:T(8,128)(2,1)S(1)} %get-tuple-element.43.pair), channel_id=1, source_target_pairs={{0,4},{4,0},{8,12},{12,8},{16,20},{20,16},{24,28},{28,24},{1,5},{5... | collective-permute-start | bytes 2359304 | tf_op jit(solution)/shard_map/ppermute | solution.py:25
  54.9 12.1 %collective-permute-start.16 = (bf16[2,3,256,256]{3,2,1,0:T(8,128)(2,1)S(1)}, bf16[2,3,256,256]{3,2,1,0:T(8,128)(2,1)S(1)}, u32[]{:S(2)}, u32[]{:S(2)}) collective-permute-start(bf16[2,3,256,256]{3,2,1,0:T(8,128)(2,1)S(1)} %get-tuple-element.43.pair), channel_id=1, source_target_pairs={{0,16},{4,12},{8,24},{12,4},{16,0},{20,28},{24,8},{28,20},{1,17},{... | collective-permute-start | bytes 2359304 | tf_op jit(solution)/shard_map/ppermute | solution.py:31
  55.5 12.9 %collective-permute-start.18 = (bf16[512,128]{1,0:T(8,128)(2,1)S(1)}, bf16[512,128]{1,0:T(8,128)(2,1)S(1)}, u32[]{:S(2)}, u32[]{:S(2)}) collective-permute-start(bf16[512,128]{1,0:T(8,128)(2,1)S(1)} %get-tuple-element.46), channel_id=1, source_target_pairs={{0,2},{1,3},{2,0},{3,1},{4,6},{5,7},{6,4},{7,5},{8,10},{9,11},{10,... | collective-permute-start | bytes 393224 | tf_op jit(solution)/shard_map/ppermute | solution.py:25
  57.4 11.0 %collective-permute-start.19 = (bf16[512,128]{1,0:T(8,128)(2,1)S(1)}, bf16[512,128]{1,0:T(8,128)(2,1)S(1)}, u32[]{:S(2)}, u32[]{:S(2)}) collective-permute-start(bf16[512,128]{1,0:T(8,128)(2,1)S(1)} %get-tuple-element.47), channel_id=1, source_target_pairs={{0,3},{1,2},{2,1},{3,0},{4,7},{5,6},{6,5},{7,4},{8,11},{9,10},{10,... | collective-permute-start | bytes 393224 | tf_op jit(solution)/shard_map/ppermute | solution.py:25
  60.0 8.9 %collective-permute-start.20 = (bf16[512,128]{1,0:T(8,128)(2,1)S(1)}, bf16[512,128]{1,0:T(8,128)(2,1)S(1)}, u32[]{:S(2)}, u32[]{:S(2)}) collective-permute-start(bf16[512,128]{1,0:T(8,128)(2,1)S(1)} %get-tuple-element.48), channel_id=1, source_target_pairs={{0,1},{1,0},{2,3},{3,2},{4,5},{5,4},{6,7},{7,6},{8,9},{9,8},{10,11... | collective-permute-start | bytes 393224 | tf_op jit(solution)/shard_map/ppermute | solution.py:25
  69.7 2.4 %collective-permute-start.21 = (bf16[2,3,256,256]{3,2,1,0:T(8,128)(2,1)S(1)}, bf16[2,3,256,256]{3,2,1,0:T(8,128)(2,1)S(1)}, u32[]{:S(2)}, u32[]{:S(2)}) collective-permute-start(bf16[2,3,256,256]{3,2,1,0:T(8,128)(2,1)S(1)} %get-tuple-element.52), channel_id=1, source_target_pairs={{0,4},{4,0},{8,12},{12,8},{16,20},{20,16},{24,28},{28,24},{1,5},{5... | collective-permute-start | bytes 2359304 | tf_op jit(solution)/shard_map/ppermute | solution.py:25
  (11 other events, 88.2 us)

commit v13 on v12

--- a/solution.py
+++ b/solution.py
@@ -326,30 +326,35 @@
         ffn_in[rows, :] = rms_scale(after_mix[rows, :], gain).astype(BF16)
 
 
-def ffn_rows(ffn_in, w_in, w_out, total):
+def grow(ffn_in, w_in, hidden):
+    in_cols = w_in.shape[2]
     for index in range(w_in.shape[0]):
-        grown = jnp.dot(ffn_in, w_in[index], preferred_element_type=F32)
-        grown = jax.nn.gelu(grown, approximate=True).astype(BF16)
-        total = total + jnp.dot(grown, w_out[index], preferred_element_type=F32)
-    return total
-
-
-def ffn_kernel(after_mix, ffn_in, w_in, w_out, out):
-    span = 256
-    for first in range(0, after_mix.shape[0], span):
-        rows = slice(first, first + span)
-        out[rows, :] = ffn_rows(ffn_in[rows, :], w_in, w_out, after_mix[rows, :])
-
-
-def last_kernel(zones, place, own_in, own_out, total, ffn_in, swapped_far, out, w_in, w_out, rows_out, sems):
+        grown = jnp.dot(ffn_in[...], w_in[index], preferred_element_type=F32)
+        hidden[:, index * in_cols : (index + 1) * in_cols] = jax.nn.gelu(
+            grown, approximate=True
+        ).astype(BF16)
+
+
+def ffn_kernel(after_mix, ffn_in, w_in, w_out, out, hidden):
+    grow(ffn_in, w_in, hidden)
+    weights = w_out[...].reshape(hidden.shape[1], w_out.shape[2])
+    out[...] = after_mix[...] + jnp.dot(hidden[...], weights, preferred_element_type=F32)
+
+
+def last_kernel(
+    zones, place, own_in, own_out, total, ffn_in, swapped_far, out, w_in, w_out, hidden, rows_out, sems
+):
     slots = slots_of(place[0] ^ 1)[2:]
     pieces = [swapped_far.at[index] for index in range(2)]
     fill_slots(zones, place, own_in, own_out, slots, pieces, w_in, w_out)
+    grow(ffn_in, w_in, hidden)
+    weights = w_out[...].reshape(hidden.shape[1], w_out.shape[2])
     span = total.shape[0] // sems.shape[0]
     copies = []
     for index in range(sems.shape[0]):
         rows = slice(index * span, (index + 1) * span)
-        rows_out[rows, :] = ffn_rows(ffn_in[rows, :], w_in, w_out, total[rows, :]).astype(BF16)
+        shrunk = jnp.dot(hidden[rows, :], weights, preferred_element_type=F32)
+        rows_out[rows, :] = (total[rows, :] + shrunk).astype(BF16)
         copies.append(pltpu.make_async_copy(rows_out.at[rows, :], out.at[rows, :], sems.at[index]))
         copies[-1].start()
     for copy in copies:
@@ -536,10 +541,10 @@
     total = call(
         ffn_kernel,
         jax.ShapeDtypeStruct((rows, width), F32),
-        [],
-        (),
-        (),
-        8,
+        [pltpu.VMEM((rows, 6 * in_cols), BF16)],
+        (),
+        (),
+        12,
         [after_mix, ffn_in, full_in, full_out],
     )
     evolved = call(
@@ -548,12 +553,13 @@
         [
             pltpu.VMEM((2, width, in_cols), BF16),
             pltpu.VMEM((2, in_cols, width), BF16),
+            pltpu.VMEM((rows, 2 * in_cols), BF16),
             pltpu.VMEM((rows, width), BF16),
-            pltpu.SemaphoreType.DMA((4,)),
+            pltpu.SemaphoreType.DMA((2,)),
         ],
         (0,),
         (),
-        8,
+        12,
         [place, own_in, w_out, total, ffn_in, swapped(far, "tm", 1)],
         pl.ANY,
     )

time: 74.5 us -> 74.6 us (level)
  no operation moved by 1% of the time
where the time goes in v13:
time: 74.6 us; the launch traced here: 74.3 us
  waiting for transfers between devices  31.8 us (43%)
  starting transfers between devices  24.4 us (33%)
  Pallas kernels  14.6 us (20%)
  local copies, waits for them, and re-layouts  2.14 us (3%)
  other arithmetic  1.04 us (1%)
    ppermute x17, waiting for transfers between devices, swapped(): lax.ppermute(value, axis, [(source, source ^ bits) for source in range(co...  20.4 us
    ppermute x17, starting transfers between devices, swapped(): lax.ppermute(value, axis, [(source, source ^ bits) for source in range(co...  15.2 us
    pallas_call x11, Pallas kernels, call(): pl.pallas_call(kernel, out_shape=out_shape, in_specs=[pl.BlockSpec(memory...  14.6 us
    ppermute x4, waiting for transfers between devices, crossed(): return lax.ppermute(value, axis, pairs)  11.5 us
    ppermute x1, starting transfers between devices, shifted(): lax.ppermute(value, axis, [(source, source + steps) for source in range(c...  4.99 us
    ppermute x4, starting transfers between devices, crossed(): return lax.ppermute(value, axis, pairs)  4.22 us
    unnamed x26, local copies, waits for them, and re-layouts  2.14 us
  transfers between devices with their start and end apart: 22, of which 12 were waited for; matrix products, arithmetic and copies ran while one was open for 1% of the time, Pallas kernels for 13%

profile of v13, /device:TPU:0, one launch (start us, length us, event | category | flops | bytes accessed | tf_op | source)
XLA Modules:
  0.0 74.3 jit_solution(13347621247060028052)
XLA Ops:
  0.0 5.0 %collective-permute-start = (bf16[4,128,512]{2,1,0:T(8,128)(2,1)}, bf16[4,128,512]{2,1,0:T(8,128)(2,1)S(1)}, u32[]{:S(2)}, u32[]{:S(2)}) collective-permute-start(bf16[4,128,512]{2,1,0:T(8,128)(2,1)} %states.3), channel_id=1, source_target_pairs={{0,8},{4,12},{8,16},{12,20},{16,24},{20,28},{1,9},{5,13},{9,17},{1... | collective-permute-start | bytes 1572872 | tf_op jit(solution)/shard_map/ppermute | solution.py:20
  6.0 3.7 %collective-permute-start.3 = (bf16[128,512]{1,0:T(8,128)(2,1)S(1)}, bf16[128,512]{1,0:T(8,128)(2,1)S(1)}, u32[]{:S(2)}, u32[]{:S(2)}) collective-permute-start(bf16[128,512]{1,0:T(8,128)(2,1)S(1)} %fusion), channel_id=1, source_target_pairs={{0,3},{1,2},{2,1},{3,0},{4,7},{5,6},{6,5},{7,4},{8,11},{9,10},{10,... | collective-permute-start | bytes 393224 | tf_op jit(solution)/shard_map/ppermute | solution.py:25
  10.5 1.0 %copy-done.1 = bf16[512,512]{1,0:T(8,128)(2,1)S(1)} copy-done((bf16[512,512]{1,0:T(8,128)(2,1)S(1)}, bf16[512,512]{1,0:T(8,128)(2,1)}, u32[]{:S(2)}) %copy-start.1) | copy-done | bytes 524312
  11.6 1.0 %copy-done.5 = bf16[128,2048]{1,0:T(8,128)(2,1)S(1)} copy-done((bf16[128,2048]{1,0:T(8,128)(2,1)S(1)}, bf16[128,2048]{1,0:T(8,128)(2,1)}, u32[]{:S(2)}) %copy-start.5) | copy-done | bytes 524312
  13.5 1.3 %collective-permute-start.1 = (bf16[256,256]{1,0:T(8,128)(2,1)S(1)}, bf16[256,256]{1,0:T(8,128)(2,1)S(1)}, u32[]{:S(2)}, u32[]{:S(2)}) collective-permute-start(bf16[256,256]{1,0:T(8,128)(2,1)S(1)} %get-tuple-element.30.packed), channel_id=1, source_target_pairs={{0,1},{1,0},{2,3},{3,2},{4,5},{5,4},{6,7},{7,6},{8,9},{9,8},{10,11... | collective-permute-start | bytes 393224 | tf_op jit(solution)/shard_map/ppermute | solution.py:25
  14.8 5.8 %collective-permute-done.2.refs_0_ = bf16[128,512]{1,0:T(8,128)(2,1)S(1)} collective-permute-done((bf16[128,512]{1,0:T(8,128)(2,1)S(1)}, bf16[128,512]{1,0:T(8,128)(2,1)S(1)}, u32[]{:S(2)}, u32[]{:S(2)}) %collective-permute-start.2) | collective-permute-done | bytes 131104 | tf_op jit(solution)/shard_map/ppermute | solution.py:25
  22.2 1.5 %collective-permute-start.6 = (bf16[3,64,512]{2,1,0:T(8,128)(2,1)S(1)}, bf16[3,64,512]{2,1,0:T(8,128)(2,1)S(1)}, u32[]{:S(2)}, u32[]{:S(2)}) collective-permute-start(bf16[3,64,512]{2,1,0:T(8,128)(2,1)S(1)} %get-tuple-element.33), channel_id=1, source_target_pairs={{0,8},{4,20},{8,0},{12,28},{16,24},{20,4},{24,16},{28,12},{1,9},{5... | collective-permute-start | bytes 589832 | tf_op jit(solution)/shard_map/ppermute | solution.py:31
  24.3 1.3 %collective-permute-start.14 = (bf16[2,256,256]{2,1,0:T(8,128)(2,1)S(1)}, bf16[2,256,256]{2,1,0:T(8,128)(2,1)S(1)}, u32[]{:S(2)}, u32[]{:S(2)}) collective-permute-start(bf16[2,256,256]{2,1,0:T(8,128)(2,1)S(1)} %get-tuple-element.42.doubled), channel_id=1, source_target_pairs={{0,2},{1,3},{2,0},{3,1},{4,6},{5,7},{6,4},{7,5},{8,10},{9,11},{10,... | collective-permute-start | bytes 786440 | tf_op jit(solution)/shard_map/ppermute | solution.py:25
  25.6 2.4 %collective-permute-done.6.refs_1_ = bf16[3,64,512]{2,1,0:T(8,128)(2,1)S(1)} collective-permute-done((bf16[3,64,512]{2,1,0:T(8,128)(2,1)S(1)}, bf16[3,64,512]{2,1,0:T(8,128)(2,1)S(1)}, u32[]{:S(2)}, u32[]{:S(2)}) %collective-permute-start.6) | collective-permute-done | bytes 196640 | tf_op jit(solution)/shard_map/ppermute | solution.py:31
  27.9 2.1 %collective-permute-done.7.refs_2_ = bf16[3,64,512]{2,1,0:T(8,128)(2,1)S(1)} collective-permute-done((bf16[3,64,512]{2,1,0:T(8,128)(2,1)S(1)}, bf16[3,64,512]{2,1,0:T(8,128)(2,1)S(1)}, u32[]{:S(2)}, u32[]{:S(2)}) %collective-permute-start.7) | collective-permute-done | bytes 196640 | tf_op jit(solution)/shard_map/ppermute | solution.py:31
  31.5 4.4 %shard_map.121 = (bf16[512,512]{1,0:T(8,128)(2,1)S(1)}, bf16[512,512]{1,0:T(8,128)(2,1)S(1)}) custom-call(s32[2]{0:T(128)S(1)} %pad_add_fusion.place, s32[1,2]{1,0:T(1,128)S(1)} %copy-done.11, bf16[1536,512]{1,0:T(8,128)(2,1)S(1)} %shard_map.120.normed, bf16[128,1536]{1,0:T(8,128)(2,1)S(1)} %copy-done.3, bf16[128,512]{1,0:T(8,128)(2,1)S(1)} %copy-done.4, ...), custom_call_target="tpu_custom_call" | custom-call | tf_op jit(solution)/shard_map/pallas_call | solution.py:366
  36.0 1.1 %shard_map.122 = (f32[512,512]{1,0:T(8,128)S(1)}, bf16[512,128]{1,0:T(8,128)(2,1)S(1)}, bf16[512,128]{1,0:T(8,128)(2,1)S(1)}, bf16[512,128]{1,0:T(8,128)(2,1)S(1)}, bf16[512,128]{1,0:T(8,128)(2,1)S(1)}) custom-call(s32[2]{0:T(128)S(1)} %pad_add_fusion.place, bf16[4,128,512]{2,1,0:T(8,128)(2,1)S(1)} %copy-done, ...), custom_call_target="tpu_custom_call" | custom-call | tf_op jit(solution)/shard_map/pallas_call | solution.py:366
  37.1 2.4 %collective-permute-done.14.arrived = bf16[2,256,256]{2,1,0:T(8,128)(2,1)S(1)} collective-permute-done((bf16[2,256,256]{2,1,0:T(8,128)(2,1)S(1)}, bf16[2,256,256]{2,1,0:T(8,128)(2,1)S(1)}, u32[]{:S(2)}, u32[]{:S(2)}) %collective-permute-start.14) | collective-permute-done | bytes 262176 | tf_op jit(solution)/shard_map/ppermute | solution.py:25
  39.5 1.5 %collective-permute-start.15 = (bf16[3,256,256]{2,1,0:T(8,128)(2,1)S(1)}, bf16[3,256,256]{2,1,0:T(8,128)(2,1)S(1)}, u32[]{:S(2)}, u32[]{:S(2)}) collective-permute-start(bf16[3,256,256]{2,1,0:T(8,128)(2,1)S(1)} %shard_map.123.refs_4_), channel_id=1, source_target_pairs={{0,8},{4,20},{8,0},{12,28},{16,24},{20,4},{24,16},{28,12},{1,9},{5... | collective-permute-start | bytes 1179656 | tf_op jit(solution)/shard_map/ppermute | solution.py:31
  41.1 2.2 %collective-permute-start.12 = (bf16[512,128]{1,0:T(8,128)(2,1)S(1)}, bf16[512,128]{1,0:T(8,128)(2,1)S(1)}, u32[]{:S(2)}, u32[]{:S(2)}) collective-permute-start(bf16[512,128]{1,0:T(8,128)(2,1)S(1)} %get-tuple-element.40), channel_id=1, source_target_pairs={{0,3},{1,2},{2,1},{3,0},{4,7},{5,6},{6,5},{7,4},{8,11},{9,10},{10,... | collective-permute-start | bytes 393224 | tf_op jit(solution)/shard_map/ppermute | solution.py:25
  43.3 1.3 %collective-permute-start.13 = (bf16[512,128]{1,0:T(8,128)(2,1)S(1)}, bf16[512,128]{1,0:T(8,128)(2,1)S(1)}, u32[]{:S(2)}, u32[]{:S(2)}) collective-permute-start(bf16[512,128]{1,0:T(8,128)(2,1)S(1)} %get-tuple-element.41), channel_id=1, source_target_pairs={{0,1},{1,0},{2,3},{3,2},{4,5},{5,4},{6,7},{7,6},{8,9},{9,8},{10,11... | collective-permute-start | bytes 393224 | tf_op jit(solution)/shard_map/ppermute | solution.py:25
  44.6 7.9 %collective-permute-done.11.refs_1_ = bf16[512,128]{1,0:T(8,128)(2,1)S(1)} collective-permute-done((bf16[512,128]{1,0:T(8,128)(2,1)S(1)}, bf16[512,128]{1,0:T(8,128)(2,1)S(1)}, u32[]{:S(2)}, u32[]{:S(2)}) %collective-permute-start.11) | collective-permute-done | bytes 131104 | tf_op jit(solution)/shard_map/ppermute | solution.py:25
  52.5 1.2 %collective-permute-done.13.refs_3_ = bf16[512,128]{1,0:T(8,128)(2,1)S(1)} collective-permute-done((bf16[512,128]{1,0:T(8,128)(2,1)S(1)}, bf16[512,128]{1,0:T(8,128)(2,1)S(1)}, u32[]{:S(2)}, u32[]{:S(2)}) %collective-permute-start.13) | collective-permute-done | bytes 131104 | tf_op jit(solution)/shard_map/ppermute | solution.py:25
  53.7 1.1 %shard_map.124 = (bf16[512,128]{1,0:T(8,128)(2,1)S(1)}, bf16[512,128]{1,0:T(8,128)(2,1)S(1)}, bf16[512,128]{1,0:T(8,128)(2,1)S(1)}, bf16[512,128]{1,0:T(8,128)(2,1)S(1)}, bf16[2,3,256,256]{3,2,1,0:T(8,128)(2,1)S(1)}) custom-call(s32[2]{0:T(128)S(1)} %pad_add_fusion.place, s32[4,3]{1,0:T(4,128)S(1)} %copy-done.8, s32[4]{0:T(128)S(1)} %copy-done.12, ...), custom_call_target="tpu_custom_call" | custom-call | tf_op jit(solution)/shard_map/pallas_call | solution.py:366
  55.5 1.9 %collective-permute-start.18 = (bf16[512,128]{1,0:T(8,128)(2,1)S(1)}, bf16[512,128]{1,0:T(8,128)(2,1)S(1)}, u32[]{:S(2)}, u32[]{:S(2)}) collective-permute-start(bf16[512,128]{1,0:T(8,128)(2,1)S(1)} %get-tuple-element.46), channel_id=1, source_target_pairs={{0,2},{1,3},{2,0},{3,1},{4,6},{5,7},{6,4},{7,5},{8,10},{9,11},{10,... | collective-permute-start | bytes 393224 | tf_op jit(solution)/shard_map/ppermute | solution.py:25
  57.4 2.5 %collective-permute-start.19 = (bf16[512,128]{1,0:T(8,128)(2,1)S(1)}, bf16[512,128]{1,0:T(8,128)(2,1)S(1)}, u32[]{:S(2)}, u32[]{:S(2)}) collective-permute-start(bf16[512,128]{1,0:T(8,128)(2,1)S(1)} %get-tuple-element.47), channel_id=1, source_target_pairs={{0,3},{1,2},{2,1},{3,0},{4,7},{5,6},{6,5},{7,4},{8,11},{9,10},{10,... | collective-permute-start | bytes 393224 | tf_op jit(solution)/shard_map/ppermute | solution.py:25
  60.0 7.0 %collective-permute-done.16.far = bf16[2,3,256,256]{3,2,1,0:T(8,128)(2,1)S(1)} collective-permute-done((bf16[2,3,256,256]{3,2,1,0:T(8,128)(2,1)S(1)}, bf16[2,3,256,256]{3,2,1,0:T(8,128)(2,1)S(1)}, u32[]{:S(2)}, u32[]{:S(2)}) %collective-permute-start.16) | collective-permute-done | bytes 786464 | tf_op jit(solution)/shard_map/ppermute | solution.py:31
  69.8 1.9 %shard_map.127.total = f32[512,512]{1,0:T(8,128)S(1)} custom-call(f32[512,512]{1,0:T(8,128)S(1)} %get-tuple-element.49.after_mix, bf16[512,512]{1,0:T(8,128)(2,1)S(1)} %get-tuple-element.50.ffn_in, bf16[6,512,256]{2,1,0:T(8,128)(2,1)S(1)} %get-tuple-element.51.w_in, bf16[6,256,512]{2,1,0:T(8,128)(2,1)S(1)} %get-tuple-element.44.ready.w_out), custom_call_target="tpu_custom_call" | custom-call | tf_op jit(solution)/shard_map/pallas_call | solution.py:366
  72.1 2.2 %shard_map.128 = bf16[512,512]{1,0:T(8,128)(2,1)} custom-call(s32[2]{0:T(128)S(1)} %pad_add_fusion.place, bf16[8,128,256]{2,1,0:T(8,128)(2,1)S(1)} %get-tuple-element.29.own_in, bf16[512,512]{1,0:T(8,128)(2,1)S(1)} %copy-done.2, f32[512,512]{1,0:T(8,128)S(1)} %shard_map.127.total, bf16[512,512]{1,0:T(8,128)(2,1)S(1)} %get-tuple-element.50.ffn_in, ...), custom_call_target="tpu_custom_call" | custom-call | tf_op jit(solution)/shard_map/pallas_call | solution.py:366
  (59 shorter events, 10.1 us)
Async XLA Ops:
  0.0 21.4 %collective-permute-start = (bf16[4,128,512]{2,1,0:T(8,128)(2,1)}, bf16[4,128,512]{2,1,0:T(8,128)(2,1)S(1)}, u32[]{:S(2)}, u32[]{:S(2)}) collective-permute-start(bf16[4,128,512]{2,1,0:T(8,128)(2,1)} %states.3), channel_id=1, source_target_pairs={{0,8},{4,12},{8,16},{12,20},{16,24},{20,28},{1,9},{5,13},{9,17},{1... | collective-permute-start | bytes 1572872 | tf_op jit(solution)/shard_map/ppermute | solution.py:20
  5.0 25.0 %copy-start.10 = (f32[512]{0:T(512)S(1)}, f32[512]{0:T(512)}, u32[]{:S(2)}) copy-start(f32[512]{0:T(512)} %param.13) | copy-start | bytes 6148
  6.0 8.8 %collective-permute-start.3 = (bf16[128,512]{1,0:T(8,128)(2,1)S(1)}, bf16[128,512]{1,0:T(8,128)(2,1)S(1)}, u32[]{:S(2)}, u32[]{:S(2)}) collective-permute-start(bf16[128,512]{1,0:T(8,128)(2,1)S(1)} %fusion), channel_id=1, source_target_pairs={{0,3},{1,2},{2,1},{3,0},{4,7},{5,6},{6,5},{7,4},{8,11},{9,10},{10,... | collective-permute-start | bytes 393224 | tf_op jit(solution)/shard_map/ppermute | solution.py:25
  9.7 10.9 %collective-permute-start.2 = (bf16[128,512]{1,0:T(8,128)(2,1)S(1)}, bf16[128,512]{1,0:T(8,128)(2,1)S(1)}, u32[]{:S(2)}, u32[]{:S(2)}) collective-permute-start(bf16[128,512]{1,0:T(8,128)(2,1)S(1)} %fusion), channel_id=1, source_target_pairs={{0,2},{1,3},{2,0},{3,1},{4,6},{5,7},{6,4},{7,5},{8,10},{9,11},{10,... | collective-permute-start | bytes 393224 | tf_op jit(solution)/shard_map/ppermute | solution.py:25
  9.7 10.9 %collective-permute-start.4 = (bf16[128,512]{1,0:T(8,128)(2,1)S(1)}, bf16[128,512]{1,0:T(8,128)(2,1)S(1)}, u32[]{:S(2)}, u32[]{:S(2)}) collective-permute-start(bf16[128,512]{1,0:T(8,128)(2,1)S(1)} %fusion), channel_id=1, source_target_pairs={{0,1},{1,0},{2,3},{3,2},{4,5},{5,4},{6,7},{7,6},{8,9},{9,8},{10,11... | collective-permute-start | bytes 393224 | tf_op jit(solution)/shard_map/ppermute | solution.py:25
  13.5 7.9 %collective-permute-start.1 = (bf16[256,256]{1,0:T(8,128)(2,1)S(1)}, bf16[256,256]{1,0:T(8,128)(2,1)S(1)}, u32[]{:S(2)}, u32[]{:S(2)}) collective-permute-start(bf16[256,256]{1,0:T(8,128)(2,1)S(1)} %get-tuple-element.30.packed), channel_id=1, source_target_pairs={{0,1},{1,0},{2,3},{3,2},{4,5},{5,4},{6,7},{7,6},{8,9},{9,8},{10,11... | collective-permute-start | bytes 393224 | tf_op jit(solution)/shard_map/ppermute | solution.py:25
  22.1 7.9 %collective-permute-start.5 = (bf16[4,128,512]{2,1,0:T(8,128)(2,1)S(1)}, bf16[4,128,512]{2,1,0:T(8,128)(2,1)S(1)}, u32[]{:S(2)}, u32[]{:S(2)}) collective-permute-start(bf16[4,128,512]{2,1,0:T(8,128)(2,1)S(1)} %get-tuple-element.31), channel_id=1, source_target_pairs={{0,4},{4,0},{8,12},{12,8},{16,20},{20,16},{24,28},{28,24},{1,5},{5... | collective-permute-start | bytes 1572872 | tf_op jit(solution)/shard_map/ppermute | solution.py:25
  22.2 5.7 %collective-permute-start.6 = (bf16[3,64,512]{2,1,0:T(8,128)(2,1)S(1)}, bf16[3,64,512]{2,1,0:T(8,128)(2,1)S(1)}, u32[]{:S(2)}, u32[]{:S(2)}) collective-permute-start(bf16[3,64,512]{2,1,0:T(8,128)(2,1)S(1)} %get-tuple-element.33), channel_id=1, source_target_pairs={{0,8},{4,20},{8,0},{12,28},{16,24},{20,4},{24,16},{28,12},{1,9},{5... | collective-permute-start | bytes 589832 | tf_op jit(solution)/shard_map/ppermute | solution.py:31
  23.7 6.3 %collective-permute-start.7 = (bf16[3,64,512]{2,1,0:T(8,128)(2,1)S(1)}, bf16[3,64,512]{2,1,0:T(8,128)(2,1)S(1)}, u32[]{:S(2)}, u32[]{:S(2)}) collective-permute-start(bf16[3,64,512]{2,1,0:T(8,128)(2,1)S(1)} %get-tuple-element.34), channel_id=1, source_target_pairs={{0,8},{4,20},{8,0},{12,28},{16,24},{20,4},{24,16},{28,12},{1,9},{5... | collective-permute-start | bytes 589832 | tf_op jit(solution)/shard_map/ppermute | solution.py:31
  24.3 7.2 %collective-permute-start.8 = (bf16[3,128,512]{2,1,0:T(8,128)(2,1)S(1)}, bf16[3,128,512]{2,1,0:T(8,128)(2,1)S(1)}, u32[]{:S(2)}, u32[]{:S(2)}) collective-permute-start(bf16[3,128,512]{2,1,0:T(8,128)(2,1)S(1)} %get-tuple-element.32.refs_0_), channel_id=1, source_target_pairs={{0,4},{4,0},{8,12},{12,8},{16,20},{20,16},{24,28},{28,24},{1,5},{5... | collective-permute-start | bytes 1179656 | tf_op jit(solution)/shard_map/ppermute | solution.py:25
  24.3 15.2 %collective-permute-start.14 = (bf16[2,256,256]{2,1,0:T(8,128)(2,1)S(1)}, bf16[2,256,256]{2,1,0:T(8,128)(2,1)S(1)}, u32[]{:S(2)}, u32[]{:S(2)}) collective-permute-start(bf16[2,256,256]{2,1,0:T(8,128)(2,1)S(1)} %get-tuple-element.42.doubled), channel_id=1, source_target_pairs={{0,2},{1,3},{2,0},{3,1},{4,6},{5,7},{6,4},{7,5},{8,10},{9,11},{10,... | collective-permute-start | bytes 786440 | tf_op jit(solution)/shard_map/ppermute | solution.py:25
  27.9 2.8 %collective-permute-start.9 = (bf16[3,64,512]{2,1,0:T(8,128)(2,1)S(1)}, bf16[3,64,512]{2,1,0:T(8,128)(2,1)S(1)}, u32[]{:S(2)}, u32[]{:S(2)}) collective-permute-start(bf16[3,64,512]{2,1,0:T(8,128)(2,1)S(1)} %collective-permute-done.6.refs_1_), channel_id=1, source_target_pairs={{0,4},{4,0},{8,12},{12,8},{16,20},{20,16},{24,28},{28,24},{1,5},{5... | collective-permute-start | bytes 589832 | tf_op jit(solution)/shard_map/ppermute | solution.py:25
  30.0 1.4 %collective-permute-start.10 = (bf16[3,64,512]{2,1,0:T(8,128)(2,1)S(1)}, bf16[3,64,512]{2,1,0:T(8,128)(2,1)S(1)}, u32[]{:S(2)}, u32[]{:S(2)}) collective-permute-start(bf16[3,64,512]{2,1,0:T(8,128)(2,1)S(1)} %collective-permute-done.7.refs_2_), channel_id=1, source_target_pairs={{0,4},{4,0},{8,12},{12,8},{16,20},{20,16},{24,28},{28,24},{1,5},{5... | collective-permute-start | bytes 589832 | tf_op jit(solution)/shard_map/ppermute | solution.py:25
  39.5 27.5 %copy-start.2 = (bf16[512,512]{1,0:T(8,128)(2,1)S(1)}, bf16[512,512]{1,0:T(8,128)(2,1)}, u32[]{:S(2)}) copy-start(bf16[512,512]{1,0:T(8,128)(2,1)} %own_out.3) | copy-start | bytes 1572868
  39.5 14.2 %collective-permute-start.15 = (bf16[3,256,256]{2,1,0:T(8,128)(2,1)S(1)}, bf16[3,256,256]{2,1,0:T(8,128)(2,1)S(1)}, u32[]{:S(2)}, u32[]{:S(2)}) collective-permute-start(bf16[3,256,256]{2,1,0:T(8,128)(2,1)S(1)} %shard_map.123.refs_4_), channel_id=1, source_target_pairs={{0,8},{4,20},{8,0},{12,28},{16,24},{20,4},{24,16},{28,12},{1,9},{5... | collective-permute-start | bytes 1179656 | tf_op jit(solution)/shard_map/ppermute | solution.py:31
  41.1 11.4 %collective-permute-start.11 = (bf16[512,128]{1,0:T(8,128)(2,1)S(1)}, bf16[512,128]{1,0:T(8,128)(2,1)S(1)}, u32[]{:S(2)}, u32[]{:S(2)}) collective-permute-start(bf16[512,128]{1,0:T(8,128)(2,1)S(1)} %get-tuple-element.39), channel_id=1, source_target_pairs={{0,2},{1,3},{2,0},{3,1},{4,6},{5,7},{6,4},{7,5},{8,10},{9,11},{10,... | collective-permute-start | bytes 393224 | tf_op jit(solution)/shard_map/ppermute | solution.py:25
  41.1 11.4 %collective-permute-start.12 = (bf16[512,128]{1,0:T(8,128)(2,1)S(1)}, bf16[512,128]{1,0:T(8,128)(2,1)S(1)}, u32[]{:S(2)}, u32[]{:S(2)}) collective-permute-start(bf16[512,128]{1,0:T(8,128)(2,1)S(1)} %get-tuple-element.40), channel_id=1, source_target_pairs={{0,3},{1,2},{2,1},{3,0},{4,7},{5,6},{6,5},{7,4},{8,11},{9,10},{10,... | collective-permute-start | bytes 393224 | tf_op jit(solution)/shard_map/ppermute | solution.py:25
  43.3 10.5 %collective-permute-start.13 = (bf16[512,128]{1,0:T(8,128)(2,1)S(1)}, bf16[512,128]{1,0:T(8,128)(2,1)S(1)}, u32[]{:S(2)}, u32[]{:S(2)}) collective-permute-start(bf16[512,128]{1,0:T(8,128)(2,1)S(1)} %get-tuple-element.41), channel_id=1, source_target_pairs={{0,1},{1,0},{2,3},{3,2},{4,5},{5,4},{6,7},{7,6},{8,9},{9,8},{10,11... | collective-permute-start | bytes 393224 | tf_op jit(solution)/shard_map/ppermute | solution.py:25
  54.9 5.1 %collective-permute-start.17 = (bf16[2,3,256,256]{3,2,1,0:T(8,128)(2,1)S(1)}, bf16[2,3,256,256]{3,2,1,0:T(8,128)(2,1)S(1)}, u32[]{:S(2)}, u32[]{:S(2)}) collective-permute-start(bf16[2,3,256,256]{3,2,1,0:T(8,128)(2,1)S(1)} %get-tuple-element.43.pair), channel_id=1, source_target_pairs={{0,4},{4,0},{8,12},{12,8},{16,20},{20,16},{24,28},{28,24},{1,5},{5... | collective-permute-start | bytes 2359304 | tf_op jit(solution)/shard_map/ppermute | solution.py:25
  54.9 12.1 %collective-permute-start.16 = (bf16[2,3,256,256]{3,2,1,0:T(8,128)(2,1)S(1)}, bf16[2,3,256,256]{3,2,1,0:T(8,128)(2,1)S(1)}, u32[]{:S(2)}, u32[]{:S(2)}) collective-permute-start(bf16[2,3,256,256]{3,2,1,0:T(8,128)(2,1)S(1)} %get-tuple-element.43.pair), channel_id=1, source_target_pairs={{0,16},{4,12},{8,24},{12,4},{16,0},{20,28},{24,8},{28,20},{1,17},{... | collective-permute-start | bytes 2359304 | tf_op jit(solution)/shard_map/ppermute | solution.py:31
  55.5 12.9 %collective-permute-start.18 = (bf16[512,128]{1,0:T(8,128)(2,1)S(1)}, bf16[512,128]{1,0:T(8,128)(2,1)S(1)}, u32[]{:S(2)}, u32[]{:S(2)}) collective-permute-start(bf16[512,128]{1,0:T(8,128)(2,1)S(1)} %get-tuple-element.46), channel_id=1, source_target_pairs={{0,2},{1,3},{2,0},{3,1},{4,6},{5,7},{6,4},{7,5},{8,10},{9,11},{10,... | collective-permute-start | bytes 393224 | tf_op jit(solution)/shard_map/ppermute | solution.py:25
  57.4 11.0 %collective-permute-start.19 = (bf16[512,128]{1,0:T(8,128)(2,1)S(1)}, bf16[512,128]{1,0:T(8,128)(2,1)S(1)}, u32[]{:S(2)}, u32[]{:S(2)}) collective-permute-start(bf16[512,128]{1,0:T(8,128)(2,1)S(1)} %get-tuple-element.47), channel_id=1, source_target_pairs={{0,3},{1,2},{2,1},{3,0},{4,7},{5,6},{6,5},{7,4},{8,11},{9,10},{10,... | collective-permute-start | bytes 393224 | tf_op jit(solution)/shard_map/ppermute | solution.py:25
  60.0 8.9 %collective-permute-start.20 = (bf16[512,128]{1,0:T(8,128)(2,1)S(1)}, bf16[512,128]{1,0:T(8,128)(2,1)S(1)}, u32[]{:S(2)}, u32[]{:S(2)}) collective-permute-start(bf16[512,128]{1,0:T(8,128)(2,1)S(1)} %get-tuple-element.48), channel_id=1, source_target_pairs={{0,1},{1,0},{2,3},{3,2},{4,5},{5,4},{6,7},{7,6},{8,9},{9,8},{10,11... | collective-permute-start | bytes 393224 | tf_op jit(solution)/shard_map/ppermute | solution.py:25
  69.7 2.4 %collective-permute-start.21 = (bf16[2,3,256,256]{3,2,1,0:T(8,128)(2,1)S(1)}, bf16[2,3,256,256]{3,2,1,0:T(8,128)(2,1)S(1)}, u32[]{:S(2)}, u32[]{:S(2)}) collective-permute-start(bf16[2,3,256,256]{3,2,1,0:T(8,128)(2,1)S(1)} %get-tuple-element.52), channel_id=1, source_target_pairs={{0,4},{4,0},{8,12},{12,8},{16,20},{20,16},{24,28},{28,24},{1,5},{5... | collective-permute-start | bytes 2359304 | tf_op jit(solution)/shard_map/ppermute | solution.py:25
  (11 other events, 88.2 us)

commit v14 on v13

--- a/solution.py
+++ b/solution.py
@@ -98,7 +98,7 @@
 
 
 def attention_kernel(zones, reach, steps, place, pattern, normed, own_qkv, own_attn, *refs):
-    pieces, (context_out, attn_out, weights, w_turned, projected, context, sems) = refs[:-7], refs[-7:]
+    pieces, (context_out, attn_out, weights, w_turned, projected, context) = refs[:-6], refs[-6:]
     key_count = (reach + 1) * steps
     zone_rows = normed.shape[0] // key_count
     width = normed.shape[1]
@@ -107,17 +107,9 @@
     shard = own_qkv.shape[0]
 
     own_rows = pl.ds(pl.multiple_of(my_zone * shard, shard), shard)
-    copies = [
-        pltpu.make_async_copy(
-            own_qkv.at[:, index * width : (index + 1) * width],
-            weights.at[index, own_rows, :],
-            sems.at[index],
-        )
-        for index in range(3)
-    ]
-    copies.append(pltpu.make_async_copy(own_attn, weights.at[3, own_rows, :], sems.at[3]))
-    for copy in copies:
-        copy.start()
+    for index in range(3):
+        weights[index, own_rows, :] = own_qkv[:, index * width : (index + 1) * width]
+    weights[3, own_rows, :] = own_attn[...]
     half = shard // 2
     mine, other = quarter_of(my_block), quarter_of(my_block ^ 1)
     for place_in, step in enumerate(steps_over(zones)):
@@ -127,8 +119,6 @@
         ):
             rows = pl.ds(pl.multiple_of(start + low, half), piece.shape[1])
             weights[quarter, rows, :] = piece[place_in]
-    for copy in copies:
-        copy.wait()
     attn_out[...] = weights[3]
     group = 3 * head_size
     def turn(head):
@@ -465,10 +455,9 @@
             pltpu.VMEM((3 * width, width), BF16),
             pltpu.VMEM((HEADS, 3 * (width // HEADS), key_count * zone_rows), F32),
             pltpu.VMEM((width, rows), F32),
-            pltpu.SemaphoreType.DMA((4,)),
         ],
         (0, 1),
-        (3, 4),
+        (),
         22,
         [place, pattern, normed, w_qkv, w_out_attn] + pieces,
     )

time: 74.6 us -> 74.6 us (level)
  no operation moved by 1% of the time
where the time goes in v14:
time: 74.6 us; the launch traced here: 74.3 us
  waiting for transfers between devices  32.1 us (43%)
  starting transfers between devices  24.4 us (33%)
  Pallas kernels  14.4 us (19%)
  local copies, waits for them, and re-layouts  2.14 us (3%)
  other arithmetic  1.04 us (1%)
    ppermute x17, waiting for transfers between devices, swapped(): lax.ppermute(value, axis, [(source, source ^ bits) for source in range(co...  20.6 us
    ppermute x17, starting transfers between devices, swapped(): lax.ppermute(value, axis, [(source, source ^ bits) for source in range(co...  15.2 us
    pallas_call x11, Pallas kernels, call(): pl.pallas_call(kernel, out_shape=out_shape, in_specs=[pl.BlockSpec(memory...  14.4 us
    ppermute x4, waiting for transfers between devices, crossed(): return lax.ppermute(value, axis, pairs)  11.5 us
    ppermute x1, starting transfers between devices, shifted(): lax.ppermute(value, axis, [(source, source + steps) for source in range(c...  4.99 us
    ppermute x4, starting transfers between devices, crossed(): return lax.ppermute(value, axis, pairs)  4.22 us
    unnamed x26, local copies, waits for them, and re-layouts  2.14 us
  transfers between devices with their start and end apart: 22, of which 12 were waited for; matrix products, arithmetic and copies ran while one was open for 1% of the time, Pallas kernels for 13%

profile of v14, /device:TPU:0, one launch (start us, length us, event | category | flops | bytes accessed | tf_op | source)
XLA Modules:
  0.0 74.3 jit_solution(8893424687197067293)
XLA Ops:
  0.0 5.0 %collective-permute-start = (bf16[4,128,512]{2,1,0:T(8,128)(2,1)}, bf16[4,128,512]{2,1,0:T(8,128)(2,1)S(1)}, u32[]{:S(2)}, u32[]{:S(2)}) collective-permute-start(bf16[4,128,512]{2,1,0:T(8,128)(2,1)} %states.3), channel_id=1, source_target_pairs={{0,8},{4,12},{8,16},{12,20},{16,24},{20,28},{1,9},{5,13},{9,17},{1... | collective-permute-start | bytes 1572872 | tf_op jit(solution)/shard_map/ppermute | solution.py:20
  6.0 3.7 %collective-permute-start.3 = (bf16[128,512]{1,0:T(8,128)(2,1)S(1)}, bf16[128,512]{1,0:T(8,128)(2,1)S(1)}, u32[]{:S(2)}, u32[]{:S(2)}) collective-permute-start(bf16[128,512]{1,0:T(8,128)(2,1)S(1)} %fusion), channel_id=1, source_target_pairs={{0,3},{1,2},{2,1},{3,0},{4,7},{5,6},{6,5},{7,4},{8,11},{9,10},{10,... | collective-permute-start | bytes 393224 | tf_op jit(solution)/shard_map/ppermute | solution.py:25
  10.5 1.0 %copy-done.1 = bf16[512,512]{1,0:T(8,128)(2,1)S(1)} copy-done((bf16[512,512]{1,0:T(8,128)(2,1)S(1)}, bf16[512,512]{1,0:T(8,128)(2,1)}, u32[]{:S(2)}) %copy-start.1) | copy-done | bytes 524312
  11.6 1.0 %copy-done.5 = bf16[128,2048]{1,0:T(8,128)(2,1)S(1)} copy-done((bf16[128,2048]{1,0:T(8,128)(2,1)S(1)}, bf16[128,2048]{1,0:T(8,128)(2,1)}, u32[]{:S(2)}) %copy-start.5) | copy-done | bytes 524312
  13.5 1.3 %collective-permute-start.1 = (bf16[256,256]{1,0:T(8,128)(2,1)S(1)}, bf16[256,256]{1,0:T(8,128)(2,1)S(1)}, u32[]{:S(2)}, u32[]{:S(2)}) collective-permute-start(bf16[256,256]{1,0:T(8,128)(2,1)S(1)} %get-tuple-element.30.packed), channel_id=1, source_target_pairs={{0,1},{1,0},{2,3},{3,2},{4,5},{5,4},{6,7},{7,6},{8,9},{9,8},{10,11... | collective-permute-start | bytes 393224 | tf_op jit(solution)/shard_map/ppermute | solution.py:25
  14.8 5.8 %collective-permute-done.2.refs_0_ = bf16[128,512]{1,0:T(8,128)(2,1)S(1)} collective-permute-done((bf16[128,512]{1,0:T(8,128)(2,1)S(1)}, bf16[128,512]{1,0:T(8,128)(2,1)S(1)}, u32[]{:S(2)}, u32[]{:S(2)}) %collective-permute-start.2) | collective-permute-done | bytes 131104 | tf_op jit(solution)/shard_map/ppermute | solution.py:25
  22.2 1.5 %collective-permute-start.6 = (bf16[3,64,512]{2,1,0:T(8,128)(2,1)S(1)}, bf16[3,64,512]{2,1,0:T(8,128)(2,1)S(1)}, u32[]{:S(2)}, u32[]{:S(2)}) collective-permute-start(bf16[3,64,512]{2,1,0:T(8,128)(2,1)S(1)} %get-tuple-element.33), channel_id=1, source_target_pairs={{0,8},{4,20},{8,0},{12,28},{16,24},{20,4},{24,16},{28,12},{1,9},{5... | collective-permute-start | bytes 589832 | tf_op jit(solution)/shard_map/ppermute | solution.py:31
  24.3 1.3 %collective-permute-start.14 = (bf16[2,256,256]{2,1,0:T(8,128)(2,1)S(1)}, bf16[2,256,256]{2,1,0:T(8,128)(2,1)S(1)}, u32[]{:S(2)}, u32[]{:S(2)}) collective-permute-start(bf16[2,256,256]{2,1,0:T(8,128)(2,1)S(1)} %get-tuple-element.42.doubled), channel_id=1, source_target_pairs={{0,2},{1,3},{2,0},{3,1},{4,6},{5,7},{6,4},{7,5},{8,10},{9,11},{10,... | collective-permute-start | bytes 786440 | tf_op jit(solution)/shard_map/ppermute | solution.py:25
  25.6 2.4 %collective-permute-done.6.refs_1_ = bf16[3,64,512]{2,1,0:T(8,128)(2,1)S(1)} collective-permute-done((bf16[3,64,512]{2,1,0:T(8,128)(2,1)S(1)}, bf16[3,64,512]{2,1,0:T(8,128)(2,1)S(1)}, u32[]{:S(2)}, u32[]{:S(2)}) %collective-permute-start.6) | collective-permute-done | bytes 196640 | tf_op jit(solution)/shard_map/ppermute | solution.py:31
  27.9 2.1 %collective-permute-done.7.refs_2_ = bf16[3,64,512]{2,1,0:T(8,128)(2,1)S(1)} collective-permute-done((bf16[3,64,512]{2,1,0:T(8,128)(2,1)S(1)}, bf16[3,64,512]{2,1,0:T(8,128)(2,1)S(1)}, u32[]{:S(2)}, u32[]{:S(2)}) %collective-permute-start.7) | collective-permute-done | bytes 196640 | tf_op jit(solution)/shard_map/ppermute | solution.py:31
  31.5 4.2 %shard_map.121 = (bf16[512,512]{1,0:T(8,128)(2,1)S(1)}, bf16[512,512]{1,0:T(8,128)(2,1)S(1)}) custom-call(s32[2]{0:T(128)S(1)} %pad_add_fusion.place, s32[1,2]{1,0:T(1,128)S(1)} %copy-done.11, bf16[1536,512]{1,0:T(8,128)(2,1)S(1)} %shard_map.120.normed, bf16[128,1536]{1,0:T(8,128)(2,1)S(1)} %copy-done.3, bf16[128,512]{1,0:T(8,128)(2,1)S(1)} %copy-done.4, ...), custom_call_target="tpu_custom_call" | custom-call | tf_op jit(solution)/shard_map/pallas_call | solution.py:356
  35.7 1.1 %shard_map.122 = (f32[512,512]{1,0:T(8,128)S(1)}, bf16[512,128]{1,0:T(8,128)(2,1)S(1)}, bf16[512,128]{1,0:T(8,128)(2,1)S(1)}, bf16[512,128]{1,0:T(8,128)(2,1)S(1)}, bf16[512,128]{1,0:T(8,128)(2,1)S(1)}) custom-call(s32[2]{0:T(128)S(1)} %pad_add_fusion.place, bf16[4,128,512]{2,1,0:T(8,128)(2,1)S(1)} %copy-done, ...), custom_call_target="tpu_custom_call" | custom-call | tf_op jit(solution)/shard_map/pallas_call | solution.py:356
  36.8 2.7 %collective-permute-done.14.arrived = bf16[2,256,256]{2,1,0:T(8,128)(2,1)S(1)} collective-permute-done((bf16[2,256,256]{2,1,0:T(8,128)(2,1)S(1)}, bf16[2,256,256]{2,1,0:T(8,128)(2,1)S(1)}, u32[]{:S(2)}, u32[]{:S(2)}) %collective-permute-start.14) | collective-permute-done | bytes 262176 | tf_op jit(solution)/shard_map/ppermute | solution.py:25
  39.5 1.5 %collective-permute-start.15 = (bf16[3,256,256]{2,1,0:T(8,128)(2,1)S(1)}, bf16[3,256,256]{2,1,0:T(8,128)(2,1)S(1)}, u32[]{:S(2)}, u32[]{:S(2)}) collective-permute-start(bf16[3,256,256]{2,1,0:T(8,128)(2,1)S(1)} %shard_map.123.refs_4_), channel_id=1, source_target_pairs={{0,8},{4,20},{8,0},{12,28},{16,24},{20,4},{24,16},{28,12},{1,9},{5... | collective-permute-start | bytes 1179656 | tf_op jit(solution)/shard_map/ppermute | solution.py:31
  41.1 2.2 %collective-permute-start.12 = (bf16[512,128]{1,0:T(8,128)(2,1)S(1)}, bf16[512,128]{1,0:T(8,128)(2,1)S(1)}, u32[]{:S(2)}, u32[]{:S(2)}) collective-permute-start(bf16[512,128]{1,0:T(8,128)(2,1)S(1)} %get-tuple-element.40), channel_id=1, source_target_pairs={{0,3},{1,2},{2,1},{3,0},{4,7},{5,6},{6,5},{7,4},{8,11},{9,10},{10,... | collective-permute-start | bytes 393224 | tf_op jit(solution)/shard_map/ppermute | solution.py:25
  43.3 1.3 %collective-permute-start.13 = (bf16[512,128]{1,0:T(8,128)(2,1)S(1)}, bf16[512,128]{1,0:T(8,128)(2,1)S(1)}, u32[]{:S(2)}, u32[]{:S(2)}) collective-permute-start(bf16[512,128]{1,0:T(8,128)(2,1)S(1)} %get-tuple-element.41), channel_id=1, source_target_pairs={{0,1},{1,0},{2,3},{3,2},{4,5},{5,4},{6,7},{7,6},{8,9},{9,8},{10,11... | collective-permute-start | bytes 393224 | tf_op jit(solution)/shard_map/ppermute | solution.py:25
  44.6 7.9 %collective-permute-done.11.refs_1_ = bf16[512,128]{1,0:T(8,128)(2,1)S(1)} collective-permute-done((bf16[512,128]{1,0:T(8,128)(2,1)S(1)}, bf16[512,128]{1,0:T(8,128)(2,1)S(1)}, u32[]{:S(2)}, u32[]{:S(2)}) %collective-permute-start.11) | collective-permute-done | bytes 131104 | tf_op jit(solution)/shard_map/ppermute | solution.py:25
  52.5 1.2 %collective-permute-done.13.refs_3_ = bf16[512,128]{1,0:T(8,128)(2,1)S(1)} collective-permute-done((bf16[512,128]{1,0:T(8,128)(2,1)S(1)}, bf16[512,128]{1,0:T(8,128)(2,1)S(1)}, u32[]{:S(2)}, u32[]{:S(2)}) %collective-permute-start.13) | collective-permute-done | bytes 131104 | tf_op jit(solution)/shard_map/ppermute | solution.py:25
  53.7 1.1 %shard_map.124 = (bf16[512,128]{1,0:T(8,128)(2,1)S(1)}, bf16[512,128]{1,0:T(8,128)(2,1)S(1)}, bf16[512,128]{1,0:T(8,128)(2,1)S(1)}, bf16[512,128]{1,0:T(8,128)(2,1)S(1)}, bf16[2,3,256,256]{3,2,1,0:T(8,128)(2,1)S(1)}) custom-call(s32[2]{0:T(128)S(1)} %pad_add_fusion.place, s32[4,3]{1,0:T(4,128)S(1)} %copy-done.8, s32[4]{0:T(128)S(1)} %copy-done.12, ...), custom_call_target="tpu_custom_call" | custom-call | tf_op jit(solution)/shard_map/pallas_call | solution.py:356
  55.5 1.9 %collective-permute-start.18 = (bf16[512,128]{1,0:T(8,128)(2,1)S(1)}, bf16[512,128]{1,0:T(8,128)(2,1)S(1)}, u32[]{:S(2)}, u32[]{:S(2)}) collective-permute-start(bf16[512,128]{1,0:T(8,128)(2,1)S(1)} %get-tuple-element.46), channel_id=1, source_target_pairs={{0,2},{1,3},{2,0},{3,1},{4,6},{5,7},{6,4},{7,5},{8,10},{9,11},{10,... | collective-permute-start | bytes 393224 | tf_op jit(solution)/shard_map/ppermute | solution.py:25
  57.4 2.5 %collective-permute-start.19 = (bf16[512,128]{1,0:T(8,128)(2,1)S(1)}, bf16[512,128]{1,0:T(8,128)(2,1)S(1)}, u32[]{:S(2)}, u32[]{:S(2)}) collective-permute-start(bf16[512,128]{1,0:T(8,128)(2,1)S(1)} %get-tuple-element.47), channel_id=1, source_target_pairs={{0,3},{1,2},{2,1},{3,0},{4,7},{5,6},{6,5},{7,4},{8,11},{9,10},{10,... | collective-permute-start | bytes 393224 | tf_op jit(solution)/shard_map/ppermute | solution.py:25
  60.0 7.0 %collective-permute-done.16.far = bf16[2,3,256,256]{3,2,1,0:T(8,128)(2,1)S(1)} collective-permute-done((bf16[2,3,256,256]{3,2,1,0:T(8,128)(2,1)S(1)}, bf16[2,3,256,256]{3,2,1,0:T(8,128)(2,1)S(1)}, u32[]{:S(2)}, u32[]{:S(2)}) %collective-permute-start.16) | collective-permute-done | bytes 786464 | tf_op jit(solution)/shard_map/ppermute | solution.py:31
  69.8 1.9 %shard_map.127.total = f32[512,512]{1,0:T(8,128)S(1)} custom-call(f32[512,512]{1,0:T(8,128)S(1)} %get-tuple-element.49.after_mix, bf16[512,512]{1,0:T(8,128)(2,1)S(1)} %get-tuple-element.50.ffn_in, bf16[6,512,256]{2,1,0:T(8,128)(2,1)S(1)} %get-tuple-element.51.w_in, bf16[6,256,512]{2,1,0:T(8,128)(2,1)S(1)} %get-tuple-element.44.ready.w_out), custom_call_target="tpu_custom_call" | custom-call | tf_op jit(solution)/shard_map/pallas_call | solution.py:356
  72.1 2.2 %shard_map.128 = bf16[512,512]{1,0:T(8,128)(2,1)} custom-call(s32[2]{0:T(128)S(1)} %pad_add_fusion.place, bf16[8,128,256]{2,1,0:T(8,128)(2,1)S(1)} %get-tuple-element.29.own_in, bf16[512,512]{1,0:T(8,128)(2,1)S(1)} %copy-done.2, f32[512,512]{1,0:T(8,128)S(1)} %shard_map.127.total, bf16[512,512]{1,0:T(8,128)(2,1)S(1)} %get-tuple-element.50.ffn_in, ...), custom_call_target="tpu_custom_call" | custom-call | tf_op jit(solution)/shard_map/pallas_call | solution.py:356
  (59 shorter events, 10.1 us)
Async XLA Ops:
  0.0 21.4 %collective-permute-start = (bf16[4,128,512]{2,1,0:T(8,128)(2,1)}, bf16[4,128,512]{2,1,0:T(8,128)(2,1)S(1)}, u32[]{:S(2)}, u32[]{:S(2)}) collective-permute-start(bf16[4,128,512]{2,1,0:T(8,128)(2,1)} %states.3), channel_id=1, source_target_pairs={{0,8},{4,12},{8,16},{12,20},{16,24},{20,28},{1,9},{5,13},{9,17},{1... | collective-permute-start | bytes 1572872 | tf_op jit(solution)/shard_map/ppermute | solution.py:20
  5.0 25.0 %copy-start.10 = (f32[512]{0:T(512)S(1)}, f32[512]{0:T(512)}, u32[]{:S(2)}) copy-start(f32[512]{0:T(512)} %param.13) | copy-start | bytes 6148
  6.0 8.8 %collective-permute-start.3 = (bf16[128,512]{1,0:T(8,128)(2,1)S(1)}, bf16[128,512]{1,0:T(8,128)(2,1)S(1)}, u32[]{:S(2)}, u32[]{:S(2)}) collective-permute-start(bf16[128,512]{1,0:T(8,128)(2,1)S(1)} %fusion), channel_id=1, source_target_pairs={{0,3},{1,2},{2,1},{3,0},{4,7},{5,6},{6,5},{7,4},{8,11},{9,10},{10,... | collective-permute-start | bytes 393224 | tf_op jit(solution)/shard_map/ppermute | solution.py:25
  9.7 10.9 %collective-permute-start.2 = (bf16[128,512]{1,0:T(8,128)(2,1)S(1)}, bf16[128,512]{1,0:T(8,128)(2,1)S(1)}, u32[]{:S(2)}, u32[]{:S(2)}) collective-permute-start(bf16[128,512]{1,0:T(8,128)(2,1)S(1)} %fusion), channel_id=1, source_target_pairs={{0,2},{1,3},{2,0},{3,1},{4,6},{5,7},{6,4},{7,5},{8,10},{9,11},{10,... | collective-permute-start | bytes 393224 | tf_op jit(solution)/shard_map/ppermute | solution.py:25
  9.7 10.9 %collective-permute-start.4 = (bf16[128,512]{1,0:T(8,128)(2,1)S(1)}, bf16[128,512]{1,0:T(8,128)(2,1)S(1)}, u32[]{:S(2)}, u32[]{:S(2)}) collective-permute-start(bf16[128,512]{1,0:T(8,128)(2,1)S(1)} %fusion), channel_id=1, source_target_pairs={{0,1},{1,0},{2,3},{3,2},{4,5},{5,4},{6,7},{7,6},{8,9},{9,8},{10,11... | collective-permute-start | bytes 393224 | tf_op jit(solution)/shard_map/ppermute | solution.py:25
  13.5 7.9 %collective-permute-start.1 = (bf16[256,256]{1,0:T(8,128)(2,1)S(1)}, bf16[256,256]{1,0:T(8,128)(2,1)S(1)}, u32[]{:S(2)}, u32[]{:S(2)}) collective-permute-start(bf16[256,256]{1,0:T(8,128)(2,1)S(1)} %get-tuple-element.30.packed), channel_id=1, source_target_pairs={{0,1},{1,0},{2,3},{3,2},{4,5},{5,4},{6,7},{7,6},{8,9},{9,8},{10,11... | collective-permute-start | bytes 393224 | tf_op jit(solution)/shard_map/ppermute | solution.py:25
  22.1 7.9 %collective-permute-start.5 = (bf16[4,128,512]{2,1,0:T(8,128)(2,1)S(1)}, bf16[4,128,512]{2,1,0:T(8,128)(2,1)S(1)}, u32[]{:S(2)}, u32[]{:S(2)}) collective-permute-start(bf16[4,128,512]{2,1,0:T(8,128)(2,1)S(1)} %get-tuple-element.31), channel_id=1, source_target_pairs={{0,4},{4,0},{8,12},{12,8},{16,20},{20,16},{24,28},{28,24},{1,5},{5... | collective-permute-start | bytes 1572872 | tf_op jit(solution)/shard_map/ppermute | solution.py:25
  22.2 5.7 %collective-permute-start.6 = (bf16[3,64,512]{2,1,0:T(8,128)(2,1)S(1)}, bf16[3,64,512]{2,1,0:T(8,128)(2,1)S(1)}, u32[]{:S(2)}, u32[]{:S(2)}) collective-permute-start(bf16[3,64,512]{2,1,0:T(8,128)(2,1)S(1)} %get-tuple-element.33), channel_id=1, source_target_pairs={{0,8},{4,20},{8,0},{12,28},{16,24},{20,4},{24,16},{28,12},{1,9},{5... | collective-permute-start | bytes 589832 | tf_op jit(solution)/shard_map/ppermute | solution.py:31
  23.7 6.3 %collective-permute-start.7 = (bf16[3,64,512]{2,1,0:T(8,128)(2,1)S(1)}, bf16[3,64,512]{2,1,0:T(8,128)(2,1)S(1)}, u32[]{:S(2)}, u32[]{:S(2)}) collective-permute-start(bf16[3,64,512]{2,1,0:T(8,128)(2,1)S(1)} %get-tuple-element.34), channel_id=1, source_target_pairs={{0,8},{4,20},{8,0},{12,28},{16,24},{20,4},{24,16},{28,12},{1,9},{5... | collective-permute-start | bytes 589832 | tf_op jit(solution)/shard_map/ppermute | solution.py:31
  24.3 7.2 %collective-permute-start.8 = (bf16[3,128,512]{2,1,0:T(8,128)(2,1)S(1)}, bf16[3,128,512]{2,1,0:T(8,128)(2,1)S(1)}, u32[]{:S(2)}, u32[]{:S(2)}) collective-permute-start(bf16[3,128,512]{2,1,0:T(8,128)(2,1)S(1)} %get-tuple-element.32.refs_0_), channel_id=1, source_target_pairs={{0,4},{4,0},{8,12},{12,8},{16,20},{20,16},{24,28},{28,24},{1,5},{5... | collective-permute-start | bytes 1179656 | tf_op jit(solution)/shard_map/ppermute | solution.py:25
  24.3 15.2 %collective-permute-start.14 = (bf16[2,256,256]{2,1,0:T(8,128)(2,1)S(1)}, bf16[2,256,256]{2,1,0:T(8,128)(2,1)S(1)}, u32[]{:S(2)}, u32[]{:S(2)}) collective-permute-start(bf16[2,256,256]{2,1,0:T(8,128)(2,1)S(1)} %get-tuple-element.42.doubled), channel_id=1, source_target_pairs={{0,2},{1,3},{2,0},{3,1},{4,6},{5,7},{6,4},{7,5},{8,10},{9,11},{10,... | collective-permute-start | bytes 786440 | tf_op jit(solution)/shard_map/ppermute | solution.py:25
  27.9 2.8 %collective-permute-start.9 = (bf16[3,64,512]{2,1,0:T(8,128)(2,1)S(1)}, bf16[3,64,512]{2,1,0:T(8,128)(2,1)S(1)}, u32[]{:S(2)}, u32[]{:S(2)}) collective-permute-start(bf16[3,64,512]{2,1,0:T(8,128)(2,1)S(1)} %collective-permute-done.6.refs_1_), channel_id=1, source_target_pairs={{0,4},{4,0},{8,12},{12,8},{16,20},{20,16},{24,28},{28,24},{1,5},{5... | collective-permute-start | bytes 589832 | tf_op jit(solution)/shard_map/ppermute | solution.py:25
  30.0 1.4 %collective-permute-start.10 = (bf16[3,64,512]{2,1,0:T(8,128)(2,1)S(1)}, bf16[3,64,512]{2,1,0:T(8,128)(2,1)S(1)}, u32[]{:S(2)}, u32[]{:S(2)}) collective-permute-start(bf16[3,64,512]{2,1,0:T(8,128)(2,1)S(1)} %collective-permute-done.7.refs_2_), channel_id=1, source_target_pairs={{0,4},{4,0},{8,12},{12,8},{16,20},{20,16},{24,28},{28,24},{1,5},{5... | collective-permute-start | bytes 589832 | tf_op jit(solution)/shard_map/ppermute | solution.py:25
  39.5 27.5 %copy-start.2 = (bf16[512,512]{1,0:T(8,128)(2,1)S(1)}, bf16[512,512]{1,0:T(8,128)(2,1)}, u32[]{:S(2)}) copy-start(bf16[512,512]{1,0:T(8,128)(2,1)} %own_out.3) | copy-start | bytes 1572868
  39.5 14.2 %collective-permute-start.15 = (bf16[3,256,256]{2,1,0:T(8,128)(2,1)S(1)}, bf16[3,256,256]{2,1,0:T(8,128)(2,1)S(1)}, u32[]{:S(2)}, u32[]{:S(2)}) collective-permute-start(bf16[3,256,256]{2,1,0:T(8,128)(2,1)S(1)} %shard_map.123.refs_4_), channel_id=1, source_target_pairs={{0,8},{4,20},{8,0},{12,28},{16,24},{20,4},{24,16},{28,12},{1,9},{5... | collective-permute-start | bytes 1179656 | tf_op jit(solution)/shard_map/ppermute | solution.py:31
  41.1 11.4 %collective-permute-start.11 = (bf16[512,128]{1,0:T(8,128)(2,1)S(1)}, bf16[512,128]{1,0:T(8,128)(2,1)S(1)}, u32[]{:S(2)}, u32[]{:S(2)}) collective-permute-start(bf16[512,128]{1,0:T(8,128)(2,1)S(1)} %get-tuple-element.39), channel_id=1, source_target_pairs={{0,2},{1,3},{2,0},{3,1},{4,6},{5,7},{6,4},{7,5},{8,10},{9,11},{10,... | collective-permute-start | bytes 393224 | tf_op jit(solution)/shard_map/ppermute | solution.py:25
  41.1 11.4 %collective-permute-start.12 = (bf16[512,128]{1,0:T(8,128)(2,1)S(1)}, bf16[512,128]{1,0:T(8,128)(2,1)S(1)}, u32[]{:S(2)}, u32[]{:S(2)}) collective-permute-start(bf16[512,128]{1,0:T(8,128)(2,1)S(1)} %get-tuple-element.40), channel_id=1, source_target_pairs={{0,3},{1,2},{2,1},{3,0},{4,7},{5,6},{6,5},{7,4},{8,11},{9,10},{10,... | collective-permute-start | bytes 393224 | tf_op jit(solution)/shard_map/ppermute | solution.py:25
  43.3 10.5 %collective-permute-start.13 = (bf16[512,128]{1,0:T(8,128)(2,1)S(1)}, bf16[512,128]{1,0:T(8,128)(2,1)S(1)}, u32[]{:S(2)}, u32[]{:S(2)}) collective-permute-start(bf16[512,128]{1,0:T(8,128)(2,1)S(1)} %get-tuple-element.41), channel_id=1, source_target_pairs={{0,1},{1,0},{2,3},{3,2},{4,5},{5,4},{6,7},{7,6},{8,9},{9,8},{10,11... | collective-permute-start | bytes 393224 | tf_op jit(solution)/shard_map/ppermute | solution.py:25
  54.9 5.1 %collective-permute-start.17 = (bf16[2,3,256,256]{3,2,1,0:T(8,128)(2,1)S(1)}, bf16[2,3,256,256]{3,2,1,0:T(8,128)(2,1)S(1)}, u32[]{:S(2)}, u32[]{:S(2)}) collective-permute-start(bf16[2,3,256,256]{3,2,1,0:T(8,128)(2,1)S(1)} %get-tuple-element.43.pair), channel_id=1, source_target_pairs={{0,4},{4,0},{8,12},{12,8},{16,20},{20,16},{24,28},{28,24},{1,5},{5... | collective-permute-start | bytes 2359304 | tf_op jit(solution)/shard_map/ppermute | solution.py:25
  54.9 12.1 %collective-permute-start.16 = (bf16[2,3,256,256]{3,2,1,0:T(8,128)(2,1)S(1)}, bf16[2,3,256,256]{3,2,1,0:T(8,128)(2,1)S(1)}, u32[]{:S(2)}, u32[]{:S(2)}) collective-permute-start(bf16[2,3,256,256]{3,2,1,0:T(8,128)(2,1)S(1)} %get-tuple-element.43.pair), channel_id=1, source_target_pairs={{0,16},{4,12},{8,24},{12,4},{16,0},{20,28},{24,8},{28,20},{1,17},{... | collective-permute-start | bytes 2359304 | tf_op jit(solution)/shard_map/ppermute | solution.py:31
  55.5 12.9 %collective-permute-start.18 = (bf16[512,128]{1,0:T(8,128)(2,1)S(1)}, bf16[512,128]{1,0:T(8,128)(2,1)S(1)}, u32[]{:S(2)}, u32[]{:S(2)}) collective-permute-start(bf16[512,128]{1,0:T(8,128)(2,1)S(1)} %get-tuple-element.46), channel_id=1, source_target_pairs={{0,2},{1,3},{2,0},{3,1},{4,6},{5,7},{6,4},{7,5},{8,10},{9,11},{10,... | collective-permute-start | bytes 393224 | tf_op jit(solution)/shard_map/ppermute | solution.py:25
  57.4 11.0 %collective-permute-start.19 = (bf16[512,128]{1,0:T(8,128)(2,1)S(1)}, bf16[512,128]{1,0:T(8,128)(2,1)S(1)}, u32[]{:S(2)}, u32[]{:S(2)}) collective-permute-start(bf16[512,128]{1,0:T(8,128)(2,1)S(1)} %get-tuple-element.47), channel_id=1, source_target_pairs={{0,3},{1,2},{2,1},{3,0},{4,7},{5,6},{6,5},{7,4},{8,11},{9,10},{10,... | collective-permute-start | bytes 393224 | tf_op jit(solution)/shard_map/ppermute | solution.py:25
  60.0 8.9 %collective-permute-start.20 = (bf16[512,128]{1,0:T(8,128)(2,1)S(1)}, bf16[512,128]{1,0:T(8,128)(2,1)S(1)}, u32[]{:S(2)}, u32[]{:S(2)}) collective-permute-start(bf16[512,128]{1,0:T(8,128)(2,1)S(1)} %get-tuple-element.48), channel_id=1, source_target_pairs={{0,1},{1,0},{2,3},{3,2},{4,5},{5,4},{6,7},{7,6},{8,9},{9,8},{10,11... | collective-permute-start | bytes 393224 | tf_op jit(solution)/shard_map/ppermute | solution.py:25
  69.7 2.4 %collective-permute-start.21 = (bf16[2,3,256,256]{3,2,1,0:T(8,128)(2,1)S(1)}, bf16[2,3,256,256]{3,2,1,0:T(8,128)(2,1)S(1)}, u32[]{:S(2)}, u32[]{:S(2)}) collective-permute-start(bf16[2,3,256,256]{3,2,1,0:T(8,128)(2,1)S(1)} %get-tuple-element.52), channel_id=1, source_target_pairs={{0,4},{4,0},{8,12},{12,8},{16,20},{20,16},{24,28},{28,24},{1,5},{5... | collective-permute-start | bytes 2359304 | tf_op jit(solution)/shard_map/ppermute | solution.py:25
  (11 other events, 88.7 us)

commit v15 on v14

--- a/solution.py
+++ b/solution.py
@@ -58,6 +58,17 @@
         for step in range(steps):
             row = (index * steps + step) * zone_rows
             normed[row : row + zone_rows, :] = rms_scale(block[step].astype(F32), gain).astype(BF16)
+
+
+def open_kernel(place, states, w_qkv, w_attn, states_out, first):
+    states_out[...] = states[...]
+    width = w_attn.shape[1]
+    quarter = quarter_of(place[0])
+    for index in range(4):
+
+        @pl.when(quarter == index)
+        def _():
+            first[...] = w_attn[...] if index == 3 else w_qkv[:, index * width : (index + 1) * width]
 
 
 def group_kernel(zones, place, w_in, w_out, own_in, packed):
@@ -393,10 +404,19 @@
     part = width // zones
     exchanges = steps_over(zones)
 
+    states, first = call(
+        open_kernel,
+        (
+            jax.ShapeDtypeStruct(states.shape, BF16),
+            jax.ShapeDtypeStruct(w_out_attn.shape, BF16),
+        ),
+        [],
+        (0,),
+        (),
+        6,
+        [place, states, w_qkv, w_out_attn],
+    )
     before = shifted(states, "tm", 2)
-    first = lax.dynamic_slice_in_dim(
-        jnp.concatenate([w_qkv, w_out_attn], axis=1), quarter_of(my_block) * width, width, axis=1
-    )
     direct = [swapped(first, "zone", step) for step in exchanges]
     packed_rows = w_in.shape[0] + out_rows * (width // in_cols)
     own_in, packed = call(

time: 74.6 us -> 76.9 us (1.031)
  local copies, waits for them, and re-layouts: 2.14 us -> 5.08 us
  other arithmetic: 1.04 us -> 0.07 us
  starting transfers between devices: 24.4 us -> 23.6 us
    unnamed x26 -> x30, local copies, waits for them, and re-layouts: 2.14 us -> 5.08 us
    ppermute x4, waiting for transfers between devices: 11.5 us -> 12.5 us  [crossed(): return lax.ppermute(value, axis, pairs)]
    concatenate x1 -> x0, other arithmetic: 0.97 us -> none  [on_device(): jnp.concatenate([w_qkv, w_out_attn], axis=1)]
    pallas_call x11 -> x12, Pallas kernels: 14.4 us -> 15 us  [call(): pl.pallas_call(kernel, out_shape=out_shape, in_specs=[pl.BlockSpec(memory...]
  transfers between devices with their start and end apart: 22 -> 22, of which waited for: 12 -> 12; matrix products, arithmetic and copies ran while one was open for 1% -> 0% of each run, Pallas kernels for 13% -> 12%
where the time goes in v15:
time: 76.9 us; the launch traced here: 76.5 us
  waiting for transfers between devices  32.6 us (42%)
  starting transfers between devices  23.6 us (31%)
  Pallas kernels  15 us (20%)
  local copies, waits for them, and re-layouts  5.08 us (7%)
    ppermute x17, waiting for transfers between devices, swapped(): lax.ppermute(value, axis, [(source, source ^ bits) for source in range(co...  20.1 us
    pallas_call x12, Pallas kernels, call(): pl.pallas_call(kernel, out_shape=out_shape, in_specs=[pl.BlockSpec(memory...  15 us
    ppermute x17, starting transfers between devices, swapped(): lax.ppermute(value, axis, [(source, source ^ bits) for source in range(co...  14.5 us
    ppermute x4, waiting for transfers between devices, crossed(): return lax.ppermute(value, axis, pairs)  12.5 us
    unnamed x30, local copies, waits for them, and re-layouts  5.08 us
    ppermute x1, starting transfers between devices, shifted(): lax.ppermute(value, axis, [(source, source + steps) for source in range(c...  4.87 us
    ppermute x4, starting transfers between devices, crossed(): return lax.ppermute(value, axis, pairs)  4.22 us
  transfers between devices with their start and end apart: 22, of which 12 were waited for; matrix products, arithmetic and copies ran while one was open for 0% of the time, Pallas kernels for 12%

profile of v15, /device:TPU:0, one launch (start us, length us, event | category | flops | bytes accessed | tf_op | source)
XLA Modules:
  0.0 76.5 jit_solution(428012049889145186)
XLA Ops:
  1.1 1.0 %copy-done.4 = bf16[4,128,512]{2,1,0:T(8,128)(2,1)S(1)} copy-done((bf16[4,128,512]{2,1,0:T(8,128)(2,1)S(1)}, bf16[4,128,512]{2,1,0:T(8,128)(2,1)}, u32[]{:S(2)}) %copy-start.4) | copy-done | bytes 524312
  3.6 4.9 %collective-permute-start = (bf16[4,128,512]{2,1,0:T(8,128)(2,1)S(1)}, bf16[4,128,512]{2,1,0:T(8,128)(2,1)S(1)}, u32[]{:S(2)}, u32[]{:S(2)}) collective-permute-start(bf16[4,128,512]{2,1,0:T(8,128)(2,1)S(1)} %get-tuple-element.32.states.refs_2_), channel_id=1, source_target_pairs={{0,8},{4,12},{8,16},{12,20},{16,24},{20,28},{1,9},{5,13},{9,17},{1... | collective-permute-start | bytes 1572872 | tf_op jit(solution)/shard_map/ppermute | solution.py:20
  8.5 1.6 %collective-permute-start.4 = (bf16[128,512]{1,0:T(8,128)(2,1)S(1)}, bf16[128,512]{1,0:T(8,128)(2,1)S(1)}, u32[]{:S(2)}, u32[]{:S(2)}) collective-permute-start(bf16[128,512]{1,0:T(8,128)(2,1)S(1)} %get-tuple-element.34), channel_id=1, source_target_pairs={{0,1},{1,0},{2,3},{3,2},{4,5},{5,4},{6,7},{7,6},{8,9},{9,8},{10,11... | collective-permute-start | bytes 393224 | tf_op jit(solution)/shard_map/ppermute | solution.py:25
  10.2 2.5 %collective-permute-start.3 = (bf16[128,512]{1,0:T(8,128)(2,1)S(1)}, bf16[128,512]{1,0:T(8,128)(2,1)S(1)}, u32[]{:S(2)}, u32[]{:S(2)}) collective-permute-start(bf16[128,512]{1,0:T(8,128)(2,1)S(1)} %get-tuple-element.34), channel_id=1, source_target_pairs={{0,3},{1,2},{2,1},{3,0},{4,7},{5,6},{6,5},{7,4},{8,11},{9,10},{10,... | collective-permute-start | bytes 393224 | tf_op jit(solution)/shard_map/ppermute | solution.py:25
  15.7 1.9 %collective-permute-start.1 = (bf16[256,256]{1,0:T(8,128)(2,1)S(1)}, bf16[256,256]{1,0:T(8,128)(2,1)S(1)}, u32[]{:S(2)}, u32[]{:S(2)}) collective-permute-start(bf16[256,256]{1,0:T(8,128)(2,1)S(1)} %get-tuple-element.33.packed), channel_id=1, source_target_pairs={{0,1},{1,0},{2,3},{3,2},{4,5},{5,4},{6,7},{7,6},{8,9},{9,8},{10,11... | collective-permute-start | bytes 393224 | tf_op jit(solution)/shard_map/ppermute | solution.py:25
  17.6 2.3 %collective-permute-done.3.refs_1_ = bf16[128,512]{1,0:T(8,128)(2,1)S(1)} collective-permute-done((bf16[128,512]{1,0:T(8,128)(2,1)S(1)}, bf16[128,512]{1,0:T(8,128)(2,1)S(1)}, u32[]{:S(2)}, u32[]{:S(2)}) %collective-permute-start.3) | collective-permute-done | bytes 131104 | tf_op jit(solution)/shard_map/ppermute | solution.py:25
  19.9 4.2 %collective-permute-done.2.refs_0_ = bf16[128,512]{1,0:T(8,128)(2,1)S(1)} collective-permute-done((bf16[128,512]{1,0:T(8,128)(2,1)S(1)}, bf16[128,512]{1,0:T(8,128)(2,1)S(1)}, u32[]{:S(2)}, u32[]{:S(2)}) %collective-permute-start.2) | collective-permute-done | bytes 131104 | tf_op jit(solution)/shard_map/ppermute | solution.py:25
  24.9 1.5 %collective-permute-start.6 = (bf16[3,64,512]{2,1,0:T(8,128)(2,1)S(1)}, bf16[3,64,512]{2,1,0:T(8,128)(2,1)S(1)}, u32[]{:S(2)}, u32[]{:S(2)}) collective-permute-start(bf16[3,64,512]{2,1,0:T(8,128)(2,1)S(1)} %get-tuple-element.37), channel_id=1, source_target_pairs={{0,8},{4,20},{8,0},{12,28},{16,24},{20,4},{24,16},{28,12},{1,9},{5... | collective-permute-start | bytes 589832 | tf_op jit(solution)/shard_map/ppermute | solution.py:31
  27.4 3.2 %collective-permute-done.6.refs_1_ = bf16[3,64,512]{2,1,0:T(8,128)(2,1)S(1)} collective-permute-done((bf16[3,64,512]{2,1,0:T(8,128)(2,1)S(1)}, bf16[3,64,512]{2,1,0:T(8,128)(2,1)S(1)}, u32[]{:S(2)}, u32[]{:S(2)}) %collective-permute-start.6) | collective-permute-done | bytes 196640 | tf_op jit(solution)/shard_map/ppermute | solution.py:31
  30.6 2.1 %collective-permute-done.7.refs_2_ = bf16[3,64,512]{2,1,0:T(8,128)(2,1)S(1)} collective-permute-done((bf16[3,64,512]{2,1,0:T(8,128)(2,1)S(1)}, bf16[3,64,512]{2,1,0:T(8,128)(2,1)S(1)}, u32[]{:S(2)}, u32[]{:S(2)}) %collective-permute-start.7) | collective-permute-done | bytes 196640 | tf_op jit(solution)/shard_map/ppermute | solution.py:31
  34.2 4.2 %shard_map.122 = (bf16[512,512]{1,0:T(8,128)(2,1)S(1)}, bf16[512,512]{1,0:T(8,128)(2,1)S(1)}) custom-call(s32[2]{0:T(128)S(1)} %pad_add_fusion.place, s32[1,2]{1,0:T(1,128)S(1)} %copy-done.13, bf16[1536,512]{1,0:T(8,128)(2,1)S(1)} %shard_map.121.normed, bf16[128,1536]{1,0:T(8,128)(2,1)S(1)} %copy-done.3, bf16[128,512]{1,0:T(8,128)(2,1)S(1)} %copy-done.7, ...), custom_call_target="tpu_custom_call" | custom-call | tf_op jit(solution)/shard_map/pallas_call | solution.py:367
  38.4 1.1 %shard_map.123 = (f32[512,512]{1,0:T(8,128)S(1)}, bf16[512,128]{1,0:T(8,128)(2,1)S(1)}, bf16[512,128]{1,0:T(8,128)(2,1)S(1)}, bf16[512,128]{1,0:T(8,128)(2,1)S(1)}, bf16[512,128]{1,0:T(8,128)(2,1)S(1)}) custom-call(s32[2]{0:T(128)S(1)} %pad_add_fusion.place, bf16[4,128,512]{2,1,0:T(8,128)(2,1)S(1)} %get-tuple-element.32.states.refs_2_, ...), custom_call_target="tpu_custom_call" | custom-call | tf_op jit(solution)/shard_map/pallas_call | solution.py:367
  39.5 2.7 %collective-permute-done.14.arrived = bf16[2,256,256]{2,1,0:T(8,128)(2,1)S(1)} collective-permute-done((bf16[2,256,256]{2,1,0:T(8,128)(2,1)S(1)}, bf16[2,256,256]{2,1,0:T(8,128)(2,1)S(1)}, u32[]{:S(2)}, u32[]{:S(2)}) %collective-permute-start.14) | collective-permute-done | bytes 262176 | tf_op jit(solution)/shard_map/ppermute | solution.py:25
  42.2 1.5 %collective-permute-start.15 = (bf16[3,256,256]{2,1,0:T(8,128)(2,1)S(1)}, bf16[3,256,256]{2,1,0:T(8,128)(2,1)S(1)}, u32[]{:S(2)}, u32[]{:S(2)}) collective-permute-start(bf16[3,256,256]{2,1,0:T(8,128)(2,1)S(1)} %shard_map.124.refs_4_), channel_id=1, source_target_pairs={{0,8},{4,20},{8,0},{12,28},{16,24},{20,4},{24,16},{28,12},{1,9},{5... | collective-permute-start | bytes 1179656 | tf_op jit(solution)/shard_map/ppermute | solution.py:31
  43.8 1.3 %collective-permute-start.12 = (bf16[512,128]{1,0:T(8,128)(2,1)S(1)}, bf16[512,128]{1,0:T(8,128)(2,1)S(1)}, u32[]{:S(2)}, u32[]{:S(2)}) collective-permute-start(bf16[512,128]{1,0:T(8,128)(2,1)S(1)} %get-tuple-element.44), channel_id=1, source_target_pairs={{0,3},{1,2},{2,1},{3,0},{4,7},{5,6},{6,5},{7,4},{8,11},{9,10},{10,... | collective-permute-start | bytes 393224 | tf_op jit(solution)/shard_map/ppermute | solution.py:25
  45.1 2.1 %collective-permute-start.13 = (bf16[512,128]{1,0:T(8,128)(2,1)S(1)}, bf16[512,128]{1,0:T(8,128)(2,1)S(1)}, u32[]{:S(2)}, u32[]{:S(2)}) collective-permute-start(bf16[512,128]{1,0:T(8,128)(2,1)S(1)} %get-tuple-element.45), channel_id=1, source_target_pairs={{0,1},{1,0},{2,3},{3,2},{4,5},{5,4},{6,7},{7,6},{8,9},{9,8},{10,11... | collective-permute-start | bytes 393224 | tf_op jit(solution)/shard_map/ppermute | solution.py:25
  47.2 7.1 %collective-permute-done.11.refs_1_ = bf16[512,128]{1,0:T(8,128)(2,1)S(1)} collective-permute-done((bf16[512,128]{1,0:T(8,128)(2,1)S(1)}, bf16[512,128]{1,0:T(8,128)(2,1)S(1)}, u32[]{:S(2)}, u32[]{:S(2)}) %collective-permute-start.11) | collective-permute-done | bytes 131104 | tf_op jit(solution)/shard_map/ppermute | solution.py:25
  54.3 1.4 %collective-permute-done.13.refs_3_ = bf16[512,128]{1,0:T(8,128)(2,1)S(1)} collective-permute-done((bf16[512,128]{1,0:T(8,128)(2,1)S(1)}, bf16[512,128]{1,0:T(8,128)(2,1)S(1)}, u32[]{:S(2)}, u32[]{:S(2)}) %collective-permute-start.13) | collective-permute-done | bytes 131104 | tf_op jit(solution)/shard_map/ppermute | solution.py:25
  55.8 1.1 %shard_map.125 = (bf16[512,128]{1,0:T(8,128)(2,1)S(1)}, bf16[512,128]{1,0:T(8,128)(2,1)S(1)}, bf16[512,128]{1,0:T(8,128)(2,1)S(1)}, bf16[512,128]{1,0:T(8,128)(2,1)S(1)}, bf16[2,3,256,256]{3,2,1,0:T(8,128)(2,1)S(1)}) custom-call(s32[2]{0:T(128)S(1)} %pad_add_fusion.place, s32[4,3]{1,0:T(4,128)S(1)} %copy-done.10, s32[4]{0:T(128)S(1)} %copy-done.14, ...), custom_call_target="tpu_custom_call" | custom-call | tf_op jit(solution)/shard_map/pallas_call | solution.py:367
  57.6 2.9 %collective-permute-start.18 = (bf16[512,128]{1,0:T(8,128)(2,1)S(1)}, bf16[512,128]{1,0:T(8,128)(2,1)S(1)}, u32[]{:S(2)}, u32[]{:S(2)}) collective-permute-start(bf16[512,128]{1,0:T(8,128)(2,1)S(1)} %get-tuple-element.50), channel_id=1, source_target_pairs={{0,2},{1,3},{2,0},{3,1},{4,6},{5,7},{6,4},{7,5},{8,10},{9,11},{10,... | collective-permute-start | bytes 393224 | tf_op jit(solution)/shard_map/ppermute | solution.py:25
  60.5 1.3 %collective-permute-start.19 = (bf16[512,128]{1,0:T(8,128)(2,1)S(1)}, bf16[512,128]{1,0:T(8,128)(2,1)S(1)}, u32[]{:S(2)}, u32[]{:S(2)}) collective-permute-start(bf16[512,128]{1,0:T(8,128)(2,1)S(1)} %get-tuple-element.51), channel_id=1, source_target_pairs={{0,3},{1,2},{2,1},{3,0},{4,7},{5,6},{6,5},{7,4},{8,11},{9,10},{10,... | collective-permute-start | bytes 393224 | tf_op jit(solution)/shard_map/ppermute | solution.py:25
  61.8 7.2 %collective-permute-done.16.far = bf16[2,3,256,256]{3,2,1,0:T(8,128)(2,1)S(1)} collective-permute-done((bf16[2,3,256,256]{3,2,1,0:T(8,128)(2,1)S(1)}, bf16[2,3,256,256]{3,2,1,0:T(8,128)(2,1)S(1)}, u32[]{:S(2)}, u32[]{:S(2)}) %collective-permute-start.16) | collective-permute-done | bytes 786464 | tf_op jit(solution)/shard_map/ppermute | solution.py:31
  72.0 1.9 %shard_map.128.total = f32[512,512]{1,0:T(8,128)S(1)} custom-call(f32[512,512]{1,0:T(8,128)S(1)} %get-tuple-element.53.after_mix, bf16[512,512]{1,0:T(8,128)(2,1)S(1)} %get-tuple-element.54.ffn_in, bf16[6,512,256]{2,1,0:T(8,128)(2,1)S(1)} %get-tuple-element.55.w_in, bf16[6,256,512]{2,1,0:T(8,128)(2,1)S(1)} %get-tuple-element.48.ready.w_out), custom_call_target="tpu_custom_call" | custom-call | tf_op jit(solution)/shard_map/pallas_call | solution.py:367
  74.3 2.2 %shard_map.129 = bf16[512,512]{1,0:T(8,128)(2,1)} custom-call(s32[2]{0:T(128)S(1)} %pad_add_fusion.place, bf16[8,128,256]{2,1,0:T(8,128)(2,1)S(1)} %get-tuple-element.31.own_in, bf16[512,512]{1,0:T(8,128)(2,1)S(1)} %copy-done.1, f32[512,512]{1,0:T(8,128)S(1)} %shard_map.128.total, bf16[512,512]{1,0:T(8,128)(2,1)S(1)} %get-tuple-element.54.ffn_in, ...), custom_call_target="tpu_custom_call" | custom-call | tf_op jit(solution)/shard_map/pallas_call | solution.py:367
  (63 shorter events, 12.9 us)
Async XLA Ops:
  3.6 29.1 %copy-start.12 = (f32[512]{0:T(512)S(1)}, f32[512]{0:T(512)}, u32[]{:S(2)}) copy-start(f32[512]{0:T(512)} %param.13) | copy-start | bytes 6148
  3.6 20.5 %collective-permute-start = (bf16[4,128,512]{2,1,0:T(8,128)(2,1)S(1)}, bf16[4,128,512]{2,1,0:T(8,128)(2,1)S(1)}, u32[]{:S(2)}, u32[]{:S(2)}) collective-permute-start(bf16[4,128,512]{2,1,0:T(8,128)(2,1)S(1)} %get-tuple-element.32.states.refs_2_), channel_id=1, source_target_pairs={{0,8},{4,12},{8,16},{12,20},{16,24},{20,28},{1,9},{5,13},{9,17},{1... | collective-permute-start | bytes 1572872 | tf_op jit(solution)/shard_map/ppermute | solution.py:20
  8.5 9.1 %collective-permute-start.4 = (bf16[128,512]{1,0:T(8,128)(2,1)S(1)}, bf16[128,512]{1,0:T(8,128)(2,1)S(1)}, u32[]{:S(2)}, u32[]{:S(2)}) collective-permute-start(bf16[128,512]{1,0:T(8,128)(2,1)S(1)} %get-tuple-element.34), channel_id=1, source_target_pairs={{0,1},{1,0},{2,3},{3,2},{4,5},{5,4},{6,7},{7,6},{8,9},{9,8},{10,11... | collective-permute-start | bytes 393224 | tf_op jit(solution)/shard_map/ppermute | solution.py:25
  10.2 9.8 %collective-permute-start.3 = (bf16[128,512]{1,0:T(8,128)(2,1)S(1)}, bf16[128,512]{1,0:T(8,128)(2,1)S(1)}, u32[]{:S(2)}, u32[]{:S(2)}) collective-permute-start(bf16[128,512]{1,0:T(8,128)(2,1)S(1)} %get-tuple-element.34), channel_id=1, source_target_pairs={{0,3},{1,2},{2,1},{3,0},{4,7},{5,6},{6,5},{7,4},{8,11},{9,10},{10,... | collective-permute-start | bytes 393224 | tf_op jit(solution)/shard_map/ppermute | solution.py:25
  12.6 11.5 %collective-permute-start.2 = (bf16[128,512]{1,0:T(8,128)(2,1)S(1)}, bf16[128,512]{1,0:T(8,128)(2,1)S(1)}, u32[]{:S(2)}, u32[]{:S(2)}) collective-permute-start(bf16[128,512]{1,0:T(8,128)(2,1)S(1)} %get-tuple-element.34), channel_id=1, source_target_pairs={{0,2},{1,3},{2,0},{3,1},{4,6},{5,7},{6,4},{7,5},{8,10},{9,11},{10,... | collective-permute-start | bytes 393224 | tf_op jit(solution)/shard_map/ppermute | solution.py:25
  15.7 8.4 %collective-permute-start.1 = (bf16[256,256]{1,0:T(8,128)(2,1)S(1)}, bf16[256,256]{1,0:T(8,128)(2,1)S(1)}, u32[]{:S(2)}, u32[]{:S(2)}) collective-permute-start(bf16[256,256]{1,0:T(8,128)(2,1)S(1)} %get-tuple-element.33.packed), channel_id=1, source_target_pairs={{0,1},{1,0},{2,3},{3,2},{4,5},{5,4},{6,7},{7,6},{8,9},{9,8},{10,11... | collective-permute-start | bytes 393224 | tf_op jit(solution)/shard_map/ppermute | solution.py:25
  24.8 7.9 %collective-permute-start.5 = (bf16[4,128,512]{2,1,0:T(8,128)(2,1)S(1)}, bf16[4,128,512]{2,1,0:T(8,128)(2,1)S(1)}, u32[]{:S(2)}, u32[]{:S(2)}) collective-permute-start(bf16[4,128,512]{2,1,0:T(8,128)(2,1)S(1)} %get-tuple-element.35), channel_id=1, source_target_pairs={{0,4},{4,0},{8,12},{12,8},{16,20},{20,16},{24,28},{28,24},{1,5},{5... | collective-permute-start | bytes 1572872 | tf_op jit(solution)/shard_map/ppermute | solution.py:25
  24.9 5.7 %collective-permute-start.6 = (bf16[3,64,512]{2,1,0:T(8,128)(2,1)S(1)}, bf16[3,64,512]{2,1,0:T(8,128)(2,1)S(1)}, u32[]{:S(2)}, u32[]{:S(2)}) collective-permute-start(bf16[3,64,512]{2,1,0:T(8,128)(2,1)S(1)} %get-tuple-element.37), channel_id=1, source_target_pairs={{0,8},{4,20},{8,0},{12,28},{16,24},{20,4},{24,16},{28,12},{1,9},{5... | collective-permute-start | bytes 589832 | tf_op jit(solution)/shard_map/ppermute | solution.py:31
  26.4 6.3 %collective-permute-start.7 = (bf16[3,64,512]{2,1,0:T(8,128)(2,1)S(1)}, bf16[3,64,512]{2,1,0:T(8,128)(2,1)S(1)}, u32[]{:S(2)}, u32[]{:S(2)}) collective-permute-start(bf16[3,64,512]{2,1,0:T(8,128)(2,1)S(1)} %get-tuple-element.38), channel_id=1, source_target_pairs={{0,8},{4,20},{8,0},{12,28},{16,24},{20,4},{24,16},{28,12},{1,9},{5... | collective-permute-start | bytes 589832 | tf_op jit(solution)/shard_map/ppermute | solution.py:31
  27.0 7.2 %collective-permute-start.8 = (bf16[3,128,512]{2,1,0:T(8,128)(2,1)S(1)}, bf16[3,128,512]{2,1,0:T(8,128)(2,1)S(1)}, u32[]{:S(2)}, u32[]{:S(2)}) collective-permute-start(bf16[3,128,512]{2,1,0:T(8,128)(2,1)S(1)} %get-tuple-element.36.refs_0_), channel_id=1, source_target_pairs={{0,4},{4,0},{8,12},{12,8},{16,20},{20,16},{24,28},{28,24},{1,5},{5... | collective-permute-start | bytes 1179656 | tf_op jit(solution)/shard_map/ppermute | solution.py:25
  27.0 15.2 %collective-permute-start.14 = (bf16[2,256,256]{2,1,0:T(8,128)(2,1)S(1)}, bf16[2,256,256]{2,1,0:T(8,128)(2,1)S(1)}, u32[]{:S(2)}, u32[]{:S(2)}) collective-permute-start(bf16[2,256,256]{2,1,0:T(8,128)(2,1)S(1)} %get-tuple-element.46.doubled), channel_id=1, source_target_pairs={{0,2},{1,3},{2,0},{3,1},{4,6},{5,7},{6,4},{7,5},{8,10},{9,11},{10,... | collective-permute-start | bytes 786440 | tf_op jit(solution)/shard_map/ppermute | solution.py:25
  30.6 2.8 %collective-permute-start.9 = (bf16[3,64,512]{2,1,0:T(8,128)(2,1)S(1)}, bf16[3,64,512]{2,1,0:T(8,128)(2,1)S(1)}, u32[]{:S(2)}, u32[]{:S(2)}) collective-permute-start(bf16[3,64,512]{2,1,0:T(8,128)(2,1)S(1)} %collective-permute-done.6.refs_1_), channel_id=1, source_target_pairs={{0,4},{4,0},{8,12},{12,8},{16,20},{20,16},{24,28},{28,24},{1,5},{5... | collective-permute-start | bytes 589832 | tf_op jit(solution)/shard_map/ppermute | solution.py:25
  32.7 1.4 %collective-permute-start.10 = (bf16[3,64,512]{2,1,0:T(8,128)(2,1)S(1)}, bf16[3,64,512]{2,1,0:T(8,128)(2,1)S(1)}, u32[]{:S(2)}, u32[]{:S(2)}) collective-permute-start(bf16[3,64,512]{2,1,0:T(8,128)(2,1)S(1)} %collective-permute-done.7.refs_2_), channel_id=1, source_target_pairs={{0,4},{4,0},{8,12},{12,8},{16,20},{20,16},{24,28},{28,24},{1,5},{5... | collective-permute-start | bytes 589832 | tf_op jit(solution)/shard_map/ppermute | solution.py:25
  42.2 26.8 %copy-start.1 = (bf16[512,512]{1,0:T(8,128)(2,1)S(1)}, bf16[512,512]{1,0:T(8,128)(2,1)}, u32[]{:S(2)}) copy-start(bf16[512,512]{1,0:T(8,128)(2,1)} %own_out.3) | copy-start | bytes 1572868
  42.2 13.5 %collective-permute-start.15 = (bf16[3,256,256]{2,1,0:T(8,128)(2,1)S(1)}, bf16[3,256,256]{2,1,0:T(8,128)(2,1)S(1)}, u32[]{:S(2)}, u32[]{:S(2)}) collective-permute-start(bf16[3,256,256]{2,1,0:T(8,128)(2,1)S(1)} %shard_map.124.refs_4_), channel_id=1, source_target_pairs={{0,8},{4,20},{8,0},{12,28},{16,24},{20,4},{24,16},{28,12},{1,9},{5... | collective-permute-start | bytes 1179656 | tf_op jit(solution)/shard_map/ppermute | solution.py:31
  43.8 10.6 %collective-permute-start.11 = (bf16[512,128]{1,0:T(8,128)(2,1)S(1)}, bf16[512,128]{1,0:T(8,128)(2,1)S(1)}, u32[]{:S(2)}, u32[]{:S(2)}) collective-permute-start(bf16[512,128]{1,0:T(8,128)(2,1)S(1)} %get-tuple-element.43), channel_id=1, source_target_pairs={{0,2},{1,3},{2,0},{3,1},{4,6},{5,7},{6,4},{7,5},{8,10},{9,11},{10,... | collective-permute-start | bytes 393224 | tf_op jit(solution)/shard_map/ppermute | solution.py:25
  43.8 10.6 %collective-permute-start.12 = (bf16[512,128]{1,0:T(8,128)(2,1)S(1)}, bf16[512,128]{1,0:T(8,128)(2,1)S(1)}, u32[]{:S(2)}, u32[]{:S(2)}) collective-permute-start(bf16[512,128]{1,0:T(8,128)(2,1)S(1)} %get-tuple-element.44), channel_id=1, source_target_pairs={{0,3},{1,2},{2,1},{3,0},{4,7},{5,6},{6,5},{7,4},{8,11},{9,10},{10,... | collective-permute-start | bytes 393224 | tf_op jit(solution)/shard_map/ppermute | solution.py:25
  45.1 10.7 %collective-permute-start.13 = (bf16[512,128]{1,0:T(8,128)(2,1)S(1)}, bf16[512,128]{1,0:T(8,128)(2,1)S(1)}, u32[]{:S(2)}, u32[]{:S(2)}) collective-permute-start(bf16[512,128]{1,0:T(8,128)(2,1)S(1)} %get-tuple-element.45), channel_id=1, source_target_pairs={{0,1},{1,0},{2,3},{3,2},{4,5},{5,4},{6,7},{7,6},{8,9},{9,8},{10,11... | collective-permute-start | bytes 393224 | tf_op jit(solution)/shard_map/ppermute | solution.py:25
  56.9 4.9 %collective-permute-start.17 = (bf16[2,3,256,256]{3,2,1,0:T(8,128)(2,1)S(1)}, bf16[2,3,256,256]{3,2,1,0:T(8,128)(2,1)S(1)}, u32[]{:S(2)}, u32[]{:S(2)}) collective-permute-start(bf16[2,3,256,256]{3,2,1,0:T(8,128)(2,1)S(1)} %get-tuple-element.47.pair), channel_id=1, source_target_pairs={{0,4},{4,0},{8,12},{12,8},{16,20},{20,16},{24,28},{28,24},{1,5},{5... | collective-permute-start | bytes 2359304 | tf_op jit(solution)/shard_map/ppermute | solution.py:25
  57.0 12.1 %collective-permute-start.16 = (bf16[2,3,256,256]{3,2,1,0:T(8,128)(2,1)S(1)}, bf16[2,3,256,256]{3,2,1,0:T(8,128)(2,1)S(1)}, u32[]{:S(2)}, u32[]{:S(2)}) collective-permute-start(bf16[2,3,256,256]{3,2,1,0:T(8,128)(2,1)S(1)} %get-tuple-element.47.pair), channel_id=1, source_target_pairs={{0,16},{4,12},{8,24},{12,4},{16,0},{20,28},{24,8},{28,20},{1,17},{... | collective-permute-start | bytes 2359304 | tf_op jit(solution)/shard_map/ppermute | solution.py:31
  57.6 12.9 %collective-permute-start.18 = (bf16[512,128]{1,0:T(8,128)(2,1)S(1)}, bf16[512,128]{1,0:T(8,128)(2,1)S(1)}, u32[]{:S(2)}, u32[]{:S(2)}) collective-permute-start(bf16[512,128]{1,0:T(8,128)(2,1)S(1)} %get-tuple-element.50), channel_id=1, source_target_pairs={{0,2},{1,3},{2,0},{3,1},{4,6},{5,7},{6,4},{7,5},{8,10},{9,11},{10,... | collective-permute-start | bytes 393224 | tf_op jit(solution)/shard_map/ppermute | solution.py:25
  60.5 10.0 %collective-permute-start.19 = (bf16[512,128]{1,0:T(8,128)(2,1)S(1)}, bf16[512,128]{1,0:T(8,128)(2,1)S(1)}, u32[]{:S(2)}, u32[]{:S(2)}) collective-permute-start(bf16[512,128]{1,0:T(8,128)(2,1)S(1)} %get-tuple-element.51), channel_id=1, source_target_pairs={{0,3},{1,2},{2,1},{3,0},{4,7},{5,6},{6,5},{7,4},{8,11},{9,10},{10,... | collective-permute-start | bytes 393224 | tf_op jit(solution)/shard_map/ppermute | solution.py:25
  61.8 9.2 %collective-permute-start.20 = (bf16[512,128]{1,0:T(8,128)(2,1)S(1)}, bf16[512,128]{1,0:T(8,128)(2,1)S(1)}, u32[]{:S(2)}, u32[]{:S(2)}) collective-permute-start(bf16[512,128]{1,0:T(8,128)(2,1)S(1)} %get-tuple-element.52), channel_id=1, source_target_pairs={{0,1},{1,0},{2,3},{3,2},{4,5},{5,4},{6,7},{7,6},{8,9},{9,8},{10,11... | collective-permute-start | bytes 393224 | tf_op jit(solution)/shard_map/ppermute | solution.py:25
  71.9 2.4 %collective-permute-start.21 = (bf16[2,3,256,256]{3,2,1,0:T(8,128)(2,1)S(1)}, bf16[2,3,256,256]{3,2,1,0:T(8,128)(2,1)S(1)}, u32[]{:S(2)}, u32[]{:S(2)}) collective-permute-start(bf16[2,3,256,256]{3,2,1,0:T(8,128)(2,1)S(1)} %get-tuple-element.56), channel_id=1, source_target_pairs={{0,4},{4,0},{8,12},{12,8},{16,20},{20,16},{24,28},{28,24},{1,5},{5... | collective-permute-start | bytes 2359304 | tf_op jit(solution)/shard_map/ppermute | solution.py:25
  (13 other events, 68.4 us)

commit v16 on v14

--- a/solution.py
+++ b/solution.py
@@ -298,11 +298,23 @@
     fill_slots(zones, place, own_in, own_out, slots, pieces, w_in, w_out)
 
 
-def after_kernel(zones, place, after_attn, gain_ffn, ready, far, *refs):
-    arrived, (after_mix, ffn_in, far_out, parts) = refs[:zones], refs[zones:]
+def relay_kernel(ready, far, *refs):
+    refs[-1][...] = far[...]
+
+
+def grow(ffn_in, w_in, hidden):
+    in_cols = w_in.shape[2]
+    for index in range(w_in.shape[0]):
+        grown = jnp.dot(ffn_in[...], w_in[index], preferred_element_type=F32)
+        hidden[:, index * in_cols : (index + 1) * in_cols] = jax.nn.gelu(
+            grown, approximate=True
+        ).astype(BF16)
+
+
+def ffn_kernel(zones, place, after_attn, gain_ffn, w_in, w_out, *refs):
+    arrived, (total, ffn_in, parts, hidden) = refs[:zones], refs[zones:]
     rows_all, width = after_attn.shape
     my_zone = place[1]
-    far_out[...] = far[...]
     for index, step in enumerate((0,) + steps_over(zones)):
         parts[my_zone ^ step] = arrived[index][...]
     gain = gain_ffn[...]
@@ -312,23 +324,11 @@
         rows = slice(first, first + span)
         for index in range(zones):
             cols = slice(index * part, (index + 1) * part)
-            after_mix[rows, cols] = after_attn[rows, cols] + parts[index, rows, :].astype(F32)
-        ffn_in[rows, :] = rms_scale(after_mix[rows, :], gain).astype(BF16)
-
-
-def grow(ffn_in, w_in, hidden):
-    in_cols = w_in.shape[2]
-    for index in range(w_in.shape[0]):
-        grown = jnp.dot(ffn_in[...], w_in[index], preferred_element_type=F32)
-        hidden[:, index * in_cols : (index + 1) * in_cols] = jax.nn.gelu(
-            grown, approximate=True
-        ).astype(BF16)
-
-
-def ffn_kernel(after_mix, ffn_in, w_in, w_out, out, hidden):
+            total[rows, cols] = after_attn[rows, cols] + parts[index, rows, :].astype(F32)
+        ffn_in[rows, :] = rms_scale(total[rows, :], gain).astype(BF16)
     grow(ffn_in, w_in, hidden)
     weights = w_out[...].reshape(hidden.shape[1], w_out.shape[2])
-    out[...] = after_mix[...] + jnp.dot(hidden[...], weights, preferred_element_type=F32)
+    total[...] += jnp.dot(hidden[...], weights, preferred_element_type=F32)
 
 
 def last_kernel(
@@ -514,27 +514,23 @@
     arrived = [spatial[0]] + [
         swapped(value, "zone", step) for value, step in zip(spatial[1:], exchanges)
     ]
-    after_mix, ffn_in, far = call(
-        functools.partial(after_kernel, zones),
-        (
-            jax.ShapeDtypeStruct((rows, width), F32),
-            jax.ShapeDtypeStruct((rows, width), BF16),
-            jax.ShapeDtypeStruct(far.shape, BF16),
-        ),
-        [pltpu.VMEM((zones, rows, part), BF16)],
+    far = call(
+        relay_kernel,
+        jax.ShapeDtypeStruct(far.shape, BF16),
+        [],
+        (),
+        (),
+        4,
+        [full_out, far] + arrived[1:],
+    )
+    total, ffn_in = call(
+        functools.partial(ffn_kernel, zones),
+        (jax.ShapeDtypeStruct((rows, width), F32), jax.ShapeDtypeStruct((rows, width), BF16)),
+        [pltpu.VMEM((zones, rows, part), BF16), pltpu.VMEM((rows, 6 * in_cols), BF16)],
         (0,),
         (),
-        8,
-        [place, after_attn, gain_ffn.reshape(1, -1), full_out, far] + arrived,
-    )
-    total = call(
-        ffn_kernel,
-        jax.ShapeDtypeStruct((rows, width), F32),
-        [pltpu.VMEM((rows, 6 * in_cols), BF16)],
-        (),
-        (),
         12,
-        [after_mix, ffn_in, full_in, full_out],
+        [place, after_attn, gain_ffn.reshape(1, -1), full_in, full_out] + arrived,
     )
     evolved = call(
         functools.partial(last_kernel, zones),
@@ -544,7 +540,7 @@
             pltpu.VMEM((2, in_cols, width), BF16),
             pltpu.VMEM((rows, 2 * in_cols), BF16),
             pltpu.VMEM((rows, width), BF16),
-            pltpu.SemaphoreType.DMA((2,)),
+            pltpu.SemaphoreType.DMA((4,)),
         ],
         (0,),
         (),

time: 74.6 us -> 74.7 us (level)
  transfers between devices with their start and end apart: 22 -> 22, of which waited for: 12 -> 11; matrix products, arithmetic and copies ran while one was open for 1% -> 1% of each run, Pallas kernels for 13% -> 14%
where the time goes in v16:
time: 74.7 us; the launch traced here: 74.4 us
  waiting for transfers between devices  31.8 us (43%)
  starting transfers between devices  24.4 us (33%)
  Pallas kernels  14.2 us (19%)
  local copies, waits for them, and re-layouts  2.69 us (4%)
  other arithmetic  1.04 us (1%)
    ppermute x17, waiting for transfers between devices, swapped(): lax.ppermute(value, axis, [(source, source ^ bits) for source in range(co...  20.3 us
    ppermute x17, starting transfers between devices, swapped(): lax.ppermute(value, axis, [(source, source ^ bits) for source in range(co...  15.2 us
    pallas_call x11, Pallas kernels, call(): pl.pallas_call(kernel, out_shape=out_shape, in_specs=[pl.BlockSpec(memory...  14.2 us
    ppermute x4, waiting for transfers between devices, crossed(): return lax.ppermute(value, axis, pairs)  11.5 us
    ppermute x1, starting transfers between devices, shifted(): lax.ppermute(value, axis, [(source, source + steps) for source in range(c...  4.99 us
    ppermute x4, starting transfers between devices, crossed(): return lax.ppermute(value, axis, pairs)  4.22 us
    unnamed x26, local copies, waits for them, and re-layouts  2.69 us
  transfers between devices with their start and end apart: 22, of which 11 were waited for; matrix products, arithmetic and copies ran while one was open for 1% of the time, Pallas kernels for 14%

profile of v16, /device:TPU:0, one launch (start us, length us, event | category | flops | bytes accessed | tf_op | source)
XLA Modules:
  0.0 74.4 jit_solution(12696088692281241942)
XLA Ops:
  0.0 5.0 %collective-permute-start = (bf16[4,128,512]{2,1,0:T(8,128)(2,1)}, bf16[4,128,512]{2,1,0:T(8,128)(2,1)S(1)}, u32[]{:S(2)}, u32[]{:S(2)}) collective-permute-start(bf16[4,128,512]{2,1,0:T(8,128)(2,1)} %states.3), channel_id=1, source_target_pairs={{0,8},{4,12},{8,16},{12,20},{16,24},{20,28},{1,9},{5,13},{9,17},{1... | collective-permute-start | bytes 1572872 | tf_op jit(solution)/shard_map/ppermute | solution.py:20
  6.0 3.7 %collective-permute-start.3 = (bf16[128,512]{1,0:T(8,128)(2,1)S(1)}, bf16[128,512]{1,0:T(8,128)(2,1)S(1)}, u32[]{:S(2)}, u32[]{:S(2)}) collective-permute-start(bf16[128,512]{1,0:T(8,128)(2,1)S(1)} %fusion), channel_id=1, source_target_pairs={{0,3},{1,2},{2,1},{3,0},{4,7},{5,6},{6,5},{7,4},{8,11},{9,10},{10,... | collective-permute-start | bytes 393224 | tf_op jit(solution)/shard_map/ppermute | solution.py:25
  10.5 1.0 %copy-done.1 = bf16[512,512]{1,0:T(8,128)(2,1)S(1)} copy-done((bf16[512,512]{1,0:T(8,128)(2,1)S(1)}, bf16[512,512]{1,0:T(8,128)(2,1)}, u32[]{:S(2)}) %copy-start.1) | copy-done | bytes 524312
  11.6 1.0 %copy-done.5 = bf16[128,2048]{1,0:T(8,128)(2,1)S(1)} copy-done((bf16[128,2048]{1,0:T(8,128)(2,1)S(1)}, bf16[128,2048]{1,0:T(8,128)(2,1)}, u32[]{:S(2)}) %copy-start.5) | copy-done | bytes 524312
  13.5 1.3 %collective-permute-start.1 = (bf16[256,256]{1,0:T(8,128)(2,1)S(1)}, bf16[256,256]{1,0:T(8,128)(2,1)S(1)}, u32[]{:S(2)}, u32[]{:S(2)}) collective-permute-start(bf16[256,256]{1,0:T(8,128)(2,1)S(1)} %get-tuple-element.29.packed), channel_id=1, source_target_pairs={{0,1},{1,0},{2,3},{3,2},{4,5},{5,4},{6,7},{7,6},{8,9},{9,8},{10,11... | collective-permute-start | bytes 393224 | tf_op jit(solution)/shard_map/ppermute | solution.py:25
  14.8 5.8 %collective-permute-done.2.refs_0_ = bf16[128,512]{1,0:T(8,128)(2,1)S(1)} collective-permute-done((bf16[128,512]{1,0:T(8,128)(2,1)S(1)}, bf16[128,512]{1,0:T(8,128)(2,1)S(1)}, u32[]{:S(2)}, u32[]{:S(2)}) %collective-permute-start.2) | collective-permute-done | bytes 131104 | tf_op jit(solution)/shard_map/ppermute | solution.py:25
  22.2 1.5 %collective-permute-start.6 = (bf16[3,64,512]{2,1,0:T(8,128)(2,1)S(1)}, bf16[3,64,512]{2,1,0:T(8,128)(2,1)S(1)}, u32[]{:S(2)}, u32[]{:S(2)}) collective-permute-start(bf16[3,64,512]{2,1,0:T(8,128)(2,1)S(1)} %get-tuple-element.32), channel_id=1, source_target_pairs={{0,8},{4,20},{8,0},{12,28},{16,24},{20,4},{24,16},{28,12},{1,9},{5... | collective-permute-start | bytes 589832 | tf_op jit(solution)/shard_map/ppermute | solution.py:31
  24.3 1.3 %collective-permute-start.14 = (bf16[2,256,256]{2,1,0:T(8,128)(2,1)S(1)}, bf16[2,256,256]{2,1,0:T(8,128)(2,1)S(1)}, u32[]{:S(2)}, u32[]{:S(2)}) collective-permute-start(bf16[2,256,256]{2,1,0:T(8,128)(2,1)S(1)} %get-tuple-element.41.doubled), channel_id=1, source_target_pairs={{0,2},{1,3},{2,0},{3,1},{4,6},{5,7},{6,4},{7,5},{8,10},{9,11},{10,... | collective-permute-start | bytes 786440 | tf_op jit(solution)/shard_map/ppermute | solution.py:25
  25.6 2.4 %collective-permute-done.6.refs_1_ = bf16[3,64,512]{2,1,0:T(8,128)(2,1)S(1)} collective-permute-done((bf16[3,64,512]{2,1,0:T(8,128)(2,1)S(1)}, bf16[3,64,512]{2,1,0:T(8,128)(2,1)S(1)}, u32[]{:S(2)}, u32[]{:S(2)}) %collective-permute-start.6) | collective-permute-done | bytes 196640 | tf_op jit(solution)/shard_map/ppermute | solution.py:31
  27.9 2.1 %collective-permute-done.7.refs_2_ = bf16[3,64,512]{2,1,0:T(8,128)(2,1)S(1)} collective-permute-done((bf16[3,64,512]{2,1,0:T(8,128)(2,1)S(1)}, bf16[3,64,512]{2,1,0:T(8,128)(2,1)S(1)}, u32[]{:S(2)}, u32[]{:S(2)}) %collective-permute-start.7) | collective-permute-done | bytes 196640 | tf_op jit(solution)/shard_map/ppermute | solution.py:31
  31.5 4.2 %shard_map.121 = (bf16[512,512]{1,0:T(8,128)(2,1)S(1)}, bf16[512,512]{1,0:T(8,128)(2,1)S(1)}) custom-call(s32[2]{0:T(128)S(1)} %pad_add_fusion.place, s32[1,2]{1,0:T(1,128)S(1)} %copy-done.11, bf16[1536,512]{1,0:T(8,128)(2,1)S(1)} %shard_map.120.normed, bf16[128,1536]{1,0:T(8,128)(2,1)S(1)} %copy-done.3, bf16[128,512]{1,0:T(8,128)(2,1)S(1)} %copy-done.4, ...), custom_call_target="tpu_custom_call" | custom-call | tf_op jit(solution)/shard_map/pallas_call | solution.py:356
  35.7 1.1 %shard_map.122 = (f32[512,512]{1,0:T(8,128)S(1)}, bf16[512,128]{1,0:T(8,128)(2,1)S(1)}, bf16[512,128]{1,0:T(8,128)(2,1)S(1)}, bf16[512,128]{1,0:T(8,128)(2,1)S(1)}, bf16[512,128]{1,0:T(8,128)(2,1)S(1)}) custom-call(s32[2]{0:T(128)S(1)} %pad_add_fusion.place, bf16[4,128,512]{2,1,0:T(8,128)(2,1)S(1)} %copy-done, ...), custom_call_target="tpu_custom_call" | custom-call | tf_op jit(solution)/shard_map/pallas_call | solution.py:356
  36.8 2.7 %collective-permute-done.14.arrived = bf16[2,256,256]{2,1,0:T(8,128)(2,1)S(1)} collective-permute-done((bf16[2,256,256]{2,1,0:T(8,128)(2,1)S(1)}, bf16[2,256,256]{2,1,0:T(8,128)(2,1)S(1)}, u32[]{:S(2)}, u32[]{:S(2)}) %collective-permute-start.14) | collective-permute-done | bytes 262176 | tf_op jit(solution)/shard_map/ppermute | solution.py:25
  39.5 1.5 %collective-permute-start.15 = (bf16[3,256,256]{2,1,0:T(8,128)(2,1)S(1)}, bf16[3,256,256]{2,1,0:T(8,128)(2,1)S(1)}, u32[]{:S(2)}, u32[]{:S(2)}) collective-permute-start(bf16[3,256,256]{2,1,0:T(8,128)(2,1)S(1)} %shard_map.123.refs_4_), channel_id=1, source_target_pairs={{0,8},{4,20},{8,0},{12,28},{16,24},{20,4},{24,16},{28,12},{1,9},{5... | collective-permute-start | bytes 1179656 | tf_op jit(solution)/shard_map/ppermute | solution.py:31
  41.1 2.2 %collective-permute-start.12 = (bf16[512,128]{1,0:T(8,128)(2,1)S(1)}, bf16[512,128]{1,0:T(8,128)(2,1)S(1)}, u32[]{:S(2)}, u32[]{:S(2)}) collective-permute-start(bf16[512,128]{1,0:T(8,128)(2,1)S(1)} %get-tuple-element.39), channel_id=1, source_target_pairs={{0,3},{1,2},{2,1},{3,0},{4,7},{5,6},{6,5},{7,4},{8,11},{9,10},{10,... | collective-permute-start | bytes 393224 | tf_op jit(solution)/shard_map/ppermute | solution.py:25
  43.3 1.3 %collective-permute-start.13 = (bf16[512,128]{1,0:T(8,128)(2,1)S(1)}, bf16[512,128]{1,0:T(8,128)(2,1)S(1)}, u32[]{:S(2)}, u32[]{:S(2)}) collective-permute-start(bf16[512,128]{1,0:T(8,128)(2,1)S(1)} %get-tuple-element.40), channel_id=1, source_target_pairs={{0,1},{1,0},{2,3},{3,2},{4,5},{5,4},{6,7},{7,6},{8,9},{9,8},{10,11... | collective-permute-start | bytes 393224 | tf_op jit(solution)/shard_map/ppermute | solution.py:25
  44.6 7.9 %collective-permute-done.11.refs_1_ = bf16[512,128]{1,0:T(8,128)(2,1)S(1)} collective-permute-done((bf16[512,128]{1,0:T(8,128)(2,1)S(1)}, bf16[512,128]{1,0:T(8,128)(2,1)S(1)}, u32[]{:S(2)}, u32[]{:S(2)}) %collective-permute-start.11) | collective-permute-done | bytes 131104 | tf_op jit(solution)/shard_map/ppermute | solution.py:25
  52.5 1.2 %collective-permute-done.13.refs_3_ = bf16[512,128]{1,0:T(8,128)(2,1)S(1)} collective-permute-done((bf16[512,128]{1,0:T(8,128)(2,1)S(1)}, bf16[512,128]{1,0:T(8,128)(2,1)S(1)}, u32[]{:S(2)}, u32[]{:S(2)}) %collective-permute-start.13) | collective-permute-done | bytes 131104 | tf_op jit(solution)/shard_map/ppermute | solution.py:25
  53.7 1.1 %shard_map.124 = (bf16[512,128]{1,0:T(8,128)(2,1)S(1)}, bf16[512,128]{1,0:T(8,128)(2,1)S(1)}, bf16[512,128]{1,0:T(8,128)(2,1)S(1)}, bf16[512,128]{1,0:T(8,128)(2,1)S(1)}, bf16[2,3,256,256]{3,2,1,0:T(8,128)(2,1)S(1)}) custom-call(s32[2]{0:T(128)S(1)} %pad_add_fusion.place, s32[4,3]{1,0:T(4,128)S(1)} %copy-done.8, s32[4]{0:T(128)S(1)} %copy-done.12, ...), custom_call_target="tpu_custom_call" | custom-call | tf_op jit(solution)/shard_map/pallas_call | solution.py:356
  55.5 1.9 %collective-permute-start.18 = (bf16[512,128]{1,0:T(8,128)(2,1)S(1)}, bf16[512,128]{1,0:T(8,128)(2,1)S(1)}, u32[]{:S(2)}, u32[]{:S(2)}) collective-permute-start(bf16[512,128]{1,0:T(8,128)(2,1)S(1)} %get-tuple-element.46), channel_id=1, source_target_pairs={{0,2},{1,3},{2,0},{3,1},{4,6},{5,7},{6,4},{7,5},{8,10},{9,11},{10,... | collective-permute-start | bytes 393224 | tf_op jit(solution)/shard_map/ppermute | solution.py:25
  57.4 2.5 %collective-permute-start.19 = (bf16[512,128]{1,0:T(8,128)(2,1)S(1)}, bf16[512,128]{1,0:T(8,128)(2,1)S(1)}, u32[]{:S(2)}, u32[]{:S(2)}) collective-permute-start(bf16[512,128]{1,0:T(8,128)(2,1)S(1)} %get-tuple-element.47), channel_id=1, source_target_pairs={{0,3},{1,2},{2,1},{3,0},{4,7},{5,6},{6,5},{7,4},{8,11},{9,10},{10,... | collective-permute-start | bytes 393224 | tf_op jit(solution)/shard_map/ppermute | solution.py:25
  60.0 7.0 %collective-permute-done.16.far = bf16[2,3,256,256]{3,2,1,0:T(8,128)(2,1)S(1)} collective-permute-done((bf16[2,3,256,256]{3,2,1,0:T(8,128)(2,1)S(1)}, bf16[2,3,256,256]{3,2,1,0:T(8,128)(2,1)S(1)}, u32[]{:S(2)}, u32[]{:S(2)}) %collective-permute-start.16) | collective-permute-done | bytes 786464 | tf_op jit(solution)/shard_map/ppermute | solution.py:31
  69.5 2.6 %shard_map.126 = (f32[512,512]{1,0:T(8,128)S(1)}, bf16[512,512]{1,0:T(8,128)(2,1)S(1)}) custom-call(s32[2]{0:T(128)S(1)} %pad_add_fusion.place, f32[512,512]{1,0:T(8,128)S(1)} %get-tuple-element.36.refs_0_.after_attn, f32[1,512]{1,0:T(1,128)S(1)} %bitcast.7, bf16[6,512,256]{2,1,0:T(8,128)(2,1)S(1)} %get-tuple-element.43.w_in, ...), custom_call_target="tpu_custom_call" | custom-call | tf_op jit(solution)/shard_map/pallas_call | solution.py:356
  72.2 2.2 %shard_map.128 = bf16[512,512]{1,0:T(8,128)(2,1)} custom-call(s32[2]{0:T(128)S(1)} %pad_add_fusion.place, bf16[8,128,256]{2,1,0:T(8,128)(2,1)S(1)} %get-tuple-element.28.own_in, bf16[512,512]{1,0:T(8,128)(2,1)S(1)} %copy-done.2, f32[512,512]{1,0:T(8,128)S(1)} %get-tuple-element.49.total, bf16[512,512]{1,0:T(8,128)(2,1)S(1)} %get-tuple-element.50.ffn_in, ...), custom_call_target="tpu_custom_call" | custom-call | tf_op jit(solution)/shard_map/pallas_call | solution.py:356
  (59 shorter events, 9.5 us)
Async XLA Ops:
  0.0 21.4 %collective-permute-start = (bf16[4,128,512]{2,1,0:T(8,128)(2,1)}, bf16[4,128,512]{2,1,0:T(8,128)(2,1)S(1)}, u32[]{:S(2)}, u32[]{:S(2)}) collective-permute-start(bf16[4,128,512]{2,1,0:T(8,128)(2,1)} %states.3), channel_id=1, source_target_pairs={{0,8},{4,12},{8,16},{12,20},{16,24},{20,28},{1,9},{5,13},{9,17},{1... | collective-permute-start | bytes 1572872 | tf_op jit(solution)/shard_map/ppermute | solution.py:20
  5.0 25.0 %copy-start.10 = (f32[512]{0:T(512)S(1)}, f32[512]{0:T(512)}, u32[]{:S(2)}) copy-start(f32[512]{0:T(512)} %param.13) | copy-start | bytes 6148
  6.0 8.8 %collective-permute-start.3 = (bf16[128,512]{1,0:T(8,128)(2,1)S(1)}, bf16[128,512]{1,0:T(8,128)(2,1)S(1)}, u32[]{:S(2)}, u32[]{:S(2)}) collective-permute-start(bf16[128,512]{1,0:T(8,128)(2,1)S(1)} %fusion), channel_id=1, source_target_pairs={{0,3},{1,2},{2,1},{3,0},{4,7},{5,6},{6,5},{7,4},{8,11},{9,10},{10,... | collective-permute-start | bytes 393224 | tf_op jit(solution)/shard_map/ppermute | solution.py:25
  9.7 10.9 %collective-permute-start.2 = (bf16[128,512]{1,0:T(8,128)(2,1)S(1)}, bf16[128,512]{1,0:T(8,128)(2,1)S(1)}, u32[]{:S(2)}, u32[]{:S(2)}) collective-permute-start(bf16[128,512]{1,0:T(8,128)(2,1)S(1)} %fusion), channel_id=1, source_target_pairs={{0,2},{1,3},{2,0},{3,1},{4,6},{5,7},{6,4},{7,5},{8,10},{9,11},{10,... | collective-permute-start | bytes 393224 | tf_op jit(solution)/shard_map/ppermute | solution.py:25
  9.7 10.9 %collective-permute-start.4 = (bf16[128,512]{1,0:T(8,128)(2,1)S(1)}, bf16[128,512]{1,0:T(8,128)(2,1)S(1)}, u32[]{:S(2)}, u32[]{:S(2)}) collective-permute-start(bf16[128,512]{1,0:T(8,128)(2,1)S(1)} %fusion), channel_id=1, source_target_pairs={{0,1},{1,0},{2,3},{3,2},{4,5},{5,4},{6,7},{7,6},{8,9},{9,8},{10,11... | collective-permute-start | bytes 393224 | tf_op jit(solution)/shard_map/ppermute | solution.py:25
  13.5 7.9 %collective-permute-start.1 = (bf16[256,256]{1,0:T(8,128)(2,1)S(1)}, bf16[256,256]{1,0:T(8,128)(2,1)S(1)}, u32[]{:S(2)}, u32[]{:S(2)}) collective-permute-start(bf16[256,256]{1,0:T(8,128)(2,1)S(1)} %get-tuple-element.29.packed), channel_id=1, source_target_pairs={{0,1},{1,0},{2,3},{3,2},{4,5},{5,4},{6,7},{7,6},{8,9},{9,8},{10,11... | collective-permute-start | bytes 393224 | tf_op jit(solution)/shard_map/ppermute | solution.py:25
  22.1 7.9 %collective-permute-start.5 = (bf16[4,128,512]{2,1,0:T(8,128)(2,1)S(1)}, bf16[4,128,512]{2,1,0:T(8,128)(2,1)S(1)}, u32[]{:S(2)}, u32[]{:S(2)}) collective-permute-start(bf16[4,128,512]{2,1,0:T(8,128)(2,1)S(1)} %get-tuple-element.30), channel_id=1, source_target_pairs={{0,4},{4,0},{8,12},{12,8},{16,20},{20,16},{24,28},{28,24},{1,5},{5... | collective-permute-start | bytes 1572872 | tf_op jit(solution)/shard_map/ppermute | solution.py:25
  22.2 5.7 %collective-permute-start.6 = (bf16[3,64,512]{2,1,0:T(8,128)(2,1)S(1)}, bf16[3,64,512]{2,1,0:T(8,128)(2,1)S(1)}, u32[]{:S(2)}, u32[]{:S(2)}) collective-permute-start(bf16[3,64,512]{2,1,0:T(8,128)(2,1)S(1)} %get-tuple-element.32), channel_id=1, source_target_pairs={{0,8},{4,20},{8,0},{12,28},{16,24},{20,4},{24,16},{28,12},{1,9},{5... | collective-permute-start | bytes 589832 | tf_op jit(solution)/shard_map/ppermute | solution.py:31
  23.7 6.3 %collective-permute-start.7 = (bf16[3,64,512]{2,1,0:T(8,128)(2,1)S(1)}, bf16[3,64,512]{2,1,0:T(8,128)(2,1)S(1)}, u32[]{:S(2)}, u32[]{:S(2)}) collective-permute-start(bf16[3,64,512]{2,1,0:T(8,128)(2,1)S(1)} %get-tuple-element.33), channel_id=1, source_target_pairs={{0,8},{4,20},{8,0},{12,28},{16,24},{20,4},{24,16},{28,12},{1,9},{5... | collective-permute-start | bytes 589832 | tf_op jit(solution)/shard_map/ppermute | solution.py:31
  24.3 7.2 %collective-permute-start.8 = (bf16[3,128,512]{2,1,0:T(8,128)(2,1)S(1)}, bf16[3,128,512]{2,1,0:T(8,128)(2,1)S(1)}, u32[]{:S(2)}, u32[]{:S(2)}) collective-permute-start(bf16[3,128,512]{2,1,0:T(8,128)(2,1)S(1)} %get-tuple-element.31.refs_0_), channel_id=1, source_target_pairs={{0,4},{4,0},{8,12},{12,8},{16,20},{20,16},{24,28},{28,24},{1,5},{5... | collective-permute-start | bytes 1179656 | tf_op jit(solution)/shard_map/ppermute | solution.py:25
  24.3 15.2 %collective-permute-start.14 = (bf16[2,256,256]{2,1,0:T(8,128)(2,1)S(1)}, bf16[2,256,256]{2,1,0:T(8,128)(2,1)S(1)}, u32[]{:S(2)}, u32[]{:S(2)}) collective-permute-start(bf16[2,256,256]{2,1,0:T(8,128)(2,1)S(1)} %get-tuple-element.41.doubled), channel_id=1, source_target_pairs={{0,2},{1,3},{2,0},{3,1},{4,6},{5,7},{6,4},{7,5},{8,10},{9,11},{10,... | collective-permute-start | bytes 786440 | tf_op jit(solution)/shard_map/ppermute | solution.py:25
  27.9 2.8 %collective-permute-start.9 = (bf16[3,64,512]{2,1,0:T(8,128)(2,1)S(1)}, bf16[3,64,512]{2,1,0:T(8,128)(2,1)S(1)}, u32[]{:S(2)}, u32[]{:S(2)}) collective-permute-start(bf16[3,64,512]{2,1,0:T(8,128)(2,1)S(1)} %collective-permute-done.6.refs_1_), channel_id=1, source_target_pairs={{0,4},{4,0},{8,12},{12,8},{16,20},{20,16},{24,28},{28,24},{1,5},{5... | collective-permute-start | bytes 589832 | tf_op jit(solution)/shard_map/ppermute | solution.py:25
  30.0 1.4 %collective-permute-start.10 = (bf16[3,64,512]{2,1,0:T(8,128)(2,1)S(1)}, bf16[3,64,512]{2,1,0:T(8,128)(2,1)S(1)}, u32[]{:S(2)}, u32[]{:S(2)}) collective-permute-start(bf16[3,64,512]{2,1,0:T(8,128)(2,1)S(1)} %collective-permute-done.7.refs_2_), channel_id=1, source_target_pairs={{0,4},{4,0},{8,12},{12,8},{16,20},{20,16},{24,28},{28,24},{1,5},{5... | collective-permute-start | bytes 589832 | tf_op jit(solution)/shard_map/ppermute | solution.py:25
  39.5 27.5 %copy-start.2 = (bf16[512,512]{1,0:T(8,128)(2,1)S(1)}, bf16[512,512]{1,0:T(8,128)(2,1)}, u32[]{:S(2)}) copy-start(bf16[512,512]{1,0:T(8,128)(2,1)} %own_out.3) | copy-start | bytes 1572868
  39.5 14.2 %collective-permute-start.15 = (bf16[3,256,256]{2,1,0:T(8,128)(2,1)S(1)}, bf16[3,256,256]{2,1,0:T(8,128)(2,1)S(1)}, u32[]{:S(2)}, u32[]{:S(2)}) collective-permute-start(bf16[3,256,256]{2,1,0:T(8,128)(2,1)S(1)} %shard_map.123.refs_4_), channel_id=1, source_target_pairs={{0,8},{4,20},{8,0},{12,28},{16,24},{20,4},{24,16},{28,12},{1,9},{5... | collective-permute-start | bytes 1179656 | tf_op jit(solution)/shard_map/ppermute | solution.py:31
  41.1 11.4 %collective-permute-start.11 = (bf16[512,128]{1,0:T(8,128)(2,1)S(1)}, bf16[512,128]{1,0:T(8,128)(2,1)S(1)}, u32[]{:S(2)}, u32[]{:S(2)}) collective-permute-start(bf16[512,128]{1,0:T(8,128)(2,1)S(1)} %get-tuple-element.38), channel_id=1, source_target_pairs={{0,2},{1,3},{2,0},{3,1},{4,6},{5,7},{6,4},{7,5},{8,10},{9,11},{10,... | collective-permute-start | bytes 393224 | tf_op jit(solution)/shard_map/ppermute | solution.py:25
  41.1 11.4 %collective-permute-start.12 = (bf16[512,128]{1,0:T(8,128)(2,1)S(1)}, bf16[512,128]{1,0:T(8,128)(2,1)S(1)}, u32[]{:S(2)}, u32[]{:S(2)}) collective-permute-start(bf16[512,128]{1,0:T(8,128)(2,1)S(1)} %get-tuple-element.39), channel_id=1, source_target_pairs={{0,3},{1,2},{2,1},{3,0},{4,7},{5,6},{6,5},{7,4},{8,11},{9,10},{10,... | collective-permute-start | bytes 393224 | tf_op jit(solution)/shard_map/ppermute | solution.py:25
  43.3 10.5 %collective-permute-start.13 = (bf16[512,128]{1,0:T(8,128)(2,1)S(1)}, bf16[512,128]{1,0:T(8,128)(2,1)S(1)}, u32[]{:S(2)}, u32[]{:S(2)}) collective-permute-start(bf16[512,128]{1,0:T(8,128)(2,1)S(1)} %get-tuple-element.40), channel_id=1, source_target_pairs={{0,1},{1,0},{2,3},{3,2},{4,5},{5,4},{6,7},{7,6},{8,9},{9,8},{10,11... | collective-permute-start | bytes 393224 | tf_op jit(solution)/shard_map/ppermute | solution.py:25
  54.9 5.1 %collective-permute-start.17 = (bf16[2,3,256,256]{3,2,1,0:T(8,128)(2,1)S(1)}, bf16[2,3,256,256]{3,2,1,0:T(8,128)(2,1)S(1)}, u32[]{:S(2)}, u32[]{:S(2)}) collective-permute-start(bf16[2,3,256,256]{3,2,1,0:T(8,128)(2,1)S(1)} %get-tuple-element.42.pair), channel_id=1, source_target_pairs={{0,4},{4,0},{8,12},{12,8},{16,20},{20,16},{24,28},{28,24},{1,5},{5... | collective-permute-start | bytes 2359304 | tf_op jit(solution)/shard_map/ppermute | solution.py:25
  54.9 12.1 %collective-permute-start.16 = (bf16[2,3,256,256]{3,2,1,0:T(8,128)(2,1)S(1)}, bf16[2,3,256,256]{3,2,1,0:T(8,128)(2,1)S(1)}, u32[]{:S(2)}, u32[]{:S(2)}) collective-permute-start(bf16[2,3,256,256]{3,2,1,0:T(8,128)(2,1)S(1)} %get-tuple-element.42.pair), channel_id=1, source_target_pairs={{0,16},{4,12},{8,24},{12,4},{16,0},{20,28},{24,8},{28,20},{1,17},{... | collective-permute-start | bytes 2359304 | tf_op jit(solution)/shard_map/ppermute | solution.py:31
  55.5 12.9 %collective-permute-start.18 = (bf16[512,128]{1,0:T(8,128)(2,1)S(1)}, bf16[512,128]{1,0:T(8,128)(2,1)S(1)}, u32[]{:S(2)}, u32[]{:S(2)}) collective-permute-start(bf16[512,128]{1,0:T(8,128)(2,1)S(1)} %get-tuple-element.46), channel_id=1, source_target_pairs={{0,2},{1,3},{2,0},{3,1},{4,6},{5,7},{6,4},{7,5},{8,10},{9,11},{10,... | collective-permute-start | bytes 393224 | tf_op jit(solution)/shard_map/ppermute | solution.py:25
  57.4 11.0 %collective-permute-start.19 = (bf16[512,128]{1,0:T(8,128)(2,1)S(1)}, bf16[512,128]{1,0:T(8,128)(2,1)S(1)}, u32[]{:S(2)}, u32[]{:S(2)}) collective-permute-start(bf16[512,128]{1,0:T(8,128)(2,1)S(1)} %get-tuple-element.47), channel_id=1, source_target_pairs={{0,3},{1,2},{2,1},{3,0},{4,7},{5,6},{6,5},{7,4},{8,11},{9,10},{10,... | collective-permute-start | bytes 393224 | tf_op jit(solution)/shard_map/ppermute | solution.py:25
  60.0 8.9 %collective-permute-start.20 = (bf16[512,128]{1,0:T(8,128)(2,1)S(1)}, bf16[512,128]{1,0:T(8,128)(2,1)S(1)}, u32[]{:S(2)}, u32[]{:S(2)}) collective-permute-start(bf16[512,128]{1,0:T(8,128)(2,1)S(1)} %get-tuple-element.48), channel_id=1, source_target_pairs={{0,1},{1,0},{2,3},{3,2},{4,5},{5,4},{6,7},{7,6},{8,9},{9,8},{10,11... | collective-permute-start | bytes 393224 | tf_op jit(solution)/shard_map/ppermute | solution.py:25
  68.9 3.2 %collective-permute-start.21 = (bf16[2,3,256,256]{3,2,1,0:T(8,128)(2,1)S(1)}, bf16[2,3,256,256]{3,2,1,0:T(8,128)(2,1)S(1)}, u32[]{:S(2)}, u32[]{:S(2)}) collective-permute-start(bf16[2,3,256,256]{3,2,1,0:T(8,128)(2,1)S(1)} %shard_map.127), channel_id=1, source_target_pairs={{0,4},{4,0},{8,12},{12,8},{16,20},{20,16},{24,28},{28,24},{1,5},{5... | collective-permute-start | bytes 2359304 | tf_op jit(solution)/shard_map/ppermute | solution.py:25
  (11 other events, 87.6 us)

commit v17 on v16

--- a/solution.py
+++ b/solution.py
@@ -291,7 +291,8 @@
                 w_out[index, rows, fold * in_cols : (fold + 1) * in_cols] = part[low : low + out_rows, :]
 
 
-def order_kernel(zones, place, own_in, own_out, pair, far, swapped_pair, w_in, w_out):
+def order_kernel(zones, place, gain, own_in, own_out, pair, far, swapped_pair, w_in, w_out, gain_out):
+    gain_out[...] = gain[...]
     my_block = place[0]
     slots = slots_of(my_block) + slots_of(my_block ^ 1)[:2]
     pieces = [group.at[index] for group in (pair, far, swapped_pair) for index in range(2)]
@@ -499,17 +500,18 @@
         [place, neighbours, degree, mix] + arrived + [across, nearest],
     )
     far = crossed(pair, "tm", 4, 2)
-    full_in, full_out = call(
+    full_in, full_out, gain = call(
         functools.partial(order_kernel, zones),
         (
             jax.ShapeDtypeStruct((6, width, in_cols), BF16),
             jax.ShapeDtypeStruct((6, in_cols, width), BF16),
+            jax.ShapeDtypeStruct((1, width), F32),
         ),
         [],
         (0,),
         (),
         8,
-        [place, own_in, w_out, pair, far, swapped(pair, "tm", 1)],
+        [place, gain_ffn.reshape(1, -1), own_in, w_out, pair, far, swapped(pair, "tm", 1)],
     )
     arrived = [spatial[0]] + [
         swapped(value, "zone", step) for value, step in zip(spatial[1:], exchanges)
@@ -530,7 +532,7 @@
         (0,),
         (),
         12,
-        [place, after_attn, gain_ffn.reshape(1, -1), full_in, full_out] + arrived,
+        [place, after_attn, gain, full_in, full_out] + arrived,
     )
     evolved = call(
         functools.partial(last_kernel, zones),

time: 74.7 us -> 74.1 us (level)
  no operation moved by 1% of the time
where the time goes in v17:
time: 74.1 us; the launch traced here: 73.9 us
  waiting for transfers between devices  31.8 us (43%)
  starting transfers between devices  24.4 us (33%)
  Pallas kernels  14.3 us (19%)
  local copies, waits for them, and re-layouts  2.14 us (3%)
  other arithmetic  1.04 us (1%)
    ppermute x17, waiting for transfers between devices, swapped(): lax.ppermute(value, axis, [(source, source ^ bits) for source in range(co...  20.3 us
    ppermute x17, starting transfers between devices, swapped(): lax.ppermute(value, axis, [(source, source ^ bits) for source in range(co...  15.2 us
    pallas_call x11, Pallas kernels, call(): pl.pallas_call(kernel, out_shape=out_shape, in_specs=[pl.BlockSpec(memory...  14.3 us
    ppermute x4, waiting for transfers between devices, crossed(): return lax.ppermute(value, axis, pairs)  11.5 us
    ppermute x1, starting transfers between devices, shifted(): lax.ppermute(value, axis, [(source, source + steps) for source in range(c...  4.99 us
    ppermute x4, starting transfers between devices, crossed(): return lax.ppermute(value, axis, pairs)  4.22 us
    unnamed x26, local copies, waits for them, and re-layouts  2.14 us
  transfers between devices with their start and end apart: 22, of which 11 were waited for; matrix products, arithmetic and copies ran while one was open for 1% of the time, Pallas kernels for 14%

profile of v17, /device:TPU:0, one launch (start us, length us, event | category | flops | bytes accessed | tf_op | source)
XLA Modules:
  0.0 73.9 jit_solution(9624062615873746361)
XLA Ops:
  0.0 5.0 %collective-permute-start = (bf16[4,128,512]{2,1,0:T(8,128)(2,1)}, bf16[4,128,512]{2,1,0:T(8,128)(2,1)S(1)}, u32[]{:S(2)}, u32[]{:S(2)}) collective-permute-start(bf16[4,128,512]{2,1,0:T(8,128)(2,1)} %states.3), channel_id=1, source_target_pairs={{0,8},{4,12},{8,16},{12,20},{16,24},{20,28},{1,9},{5,13},{9,17},{1... | collective-permute-start | bytes 1572872 | tf_op jit(solution)/shard_map/ppermute | solution.py:20
  6.0 3.7 %collective-permute-start.3 = (bf16[128,512]{1,0:T(8,128)(2,1)S(1)}, bf16[128,512]{1,0:T(8,128)(2,1)S(1)}, u32[]{:S(2)}, u32[]{:S(2)}) collective-permute-start(bf16[128,512]{1,0:T(8,128)(2,1)S(1)} %fusion), channel_id=1, source_target_pairs={{0,3},{1,2},{2,1},{3,0},{4,7},{5,6},{6,5},{7,4},{8,11},{9,10},{10,... | collective-permute-start | bytes 393224 | tf_op jit(solution)/shard_map/ppermute | solution.py:25
  10.5 1.0 %copy-done = bf16[512,512]{1,0:T(8,128)(2,1)S(1)} copy-done((bf16[512,512]{1,0:T(8,128)(2,1)S(1)}, bf16[512,512]{1,0:T(8,128)(2,1)}, u32[]{:S(2)}) %copy-start) | copy-done | bytes 524312
  11.6 1.0 %copy-done.5 = bf16[128,2048]{1,0:T(8,128)(2,1)S(1)} copy-done((bf16[128,2048]{1,0:T(8,128)(2,1)S(1)}, bf16[128,2048]{1,0:T(8,128)(2,1)}, u32[]{:S(2)}) %copy-start.5) | copy-done | bytes 524312
  13.5 1.3 %collective-permute-start.1 = (bf16[256,256]{1,0:T(8,128)(2,1)S(1)}, bf16[256,256]{1,0:T(8,128)(2,1)S(1)}, u32[]{:S(2)}, u32[]{:S(2)}) collective-permute-start(bf16[256,256]{1,0:T(8,128)(2,1)S(1)} %get-tuple-element.30.packed), channel_id=1, source_target_pairs={{0,1},{1,0},{2,3},{3,2},{4,5},{5,4},{6,7},{7,6},{8,9},{9,8},{10,11... | collective-permute-start | bytes 393224 | tf_op jit(solution)/shard_map/ppermute | solution.py:25
  14.8 5.8 %collective-permute-done.2.refs_0_ = bf16[128,512]{1,0:T(8,128)(2,1)S(1)} collective-permute-done((bf16[128,512]{1,0:T(8,128)(2,1)S(1)}, bf16[128,512]{1,0:T(8,128)(2,1)S(1)}, u32[]{:S(2)}, u32[]{:S(2)}) %collective-permute-start.2) | collective-permute-done | bytes 131104 | tf_op jit(solution)/shard_map/ppermute | solution.py:25
  22.2 1.5 %collective-permute-start.6 = (bf16[3,64,512]{2,1,0:T(8,128)(2,1)S(1)}, bf16[3,64,512]{2,1,0:T(8,128)(2,1)S(1)}, u32[]{:S(2)}, u32[]{:S(2)}) collective-permute-start(bf16[3,64,512]{2,1,0:T(8,128)(2,1)S(1)} %get-tuple-element.33), channel_id=1, source_target_pairs={{0,8},{4,20},{8,0},{12,28},{16,24},{20,4},{24,16},{28,12},{1,9},{5... | collective-permute-start | bytes 589832 | tf_op jit(solution)/shard_map/ppermute | solution.py:31
  24.3 1.3 %collective-permute-start.14 = (bf16[2,256,256]{2,1,0:T(8,128)(2,1)S(1)}, bf16[2,256,256]{2,1,0:T(8,128)(2,1)S(1)}, u32[]{:S(2)}, u32[]{:S(2)}) collective-permute-start(bf16[2,256,256]{2,1,0:T(8,128)(2,1)S(1)} %get-tuple-element.42.doubled), channel_id=1, source_target_pairs={{0,2},{1,3},{2,0},{3,1},{4,6},{5,7},{6,4},{7,5},{8,10},{9,11},{10,... | collective-permute-start | bytes 786440 | tf_op jit(solution)/shard_map/ppermute | solution.py:25
  25.6 2.4 %collective-permute-done.6.refs_1_ = bf16[3,64,512]{2,1,0:T(8,128)(2,1)S(1)} collective-permute-done((bf16[3,64,512]{2,1,0:T(8,128)(2,1)S(1)}, bf16[3,64,512]{2,1,0:T(8,128)(2,1)S(1)}, u32[]{:S(2)}, u32[]{:S(2)}) %collective-permute-start.6) | collective-permute-done | bytes 196640 | tf_op jit(solution)/shard_map/ppermute | solution.py:31
  27.9 2.1 %collective-permute-done.7.refs_2_ = bf16[3,64,512]{2,1,0:T(8,128)(2,1)S(1)} collective-permute-done((bf16[3,64,512]{2,1,0:T(8,128)(2,1)S(1)}, bf16[3,64,512]{2,1,0:T(8,128)(2,1)S(1)}, u32[]{:S(2)}, u32[]{:S(2)}) %collective-permute-start.7) | collective-permute-done | bytes 196640 | tf_op jit(solution)/shard_map/ppermute | solution.py:31
  31.5 4.2 %shard_map.121 = (bf16[512,512]{1,0:T(8,128)(2,1)S(1)}, bf16[512,512]{1,0:T(8,128)(2,1)S(1)}) custom-call(s32[2]{0:T(128)S(1)} %pad_add_fusion.place, s32[1,2]{1,0:T(1,128)S(1)} %copy-done.11, bf16[1536,512]{1,0:T(8,128)(2,1)S(1)} %shard_map.120.normed, bf16[128,1536]{1,0:T(8,128)(2,1)S(1)} %copy-done.3, bf16[128,512]{1,0:T(8,128)(2,1)S(1)} %copy-done.4, ...), custom_call_target="tpu_custom_call" | custom-call | tf_op jit(solution)/shard_map/pallas_call | solution.py:357
  35.7 1.1 %shard_map.122 = (f32[512,512]{1,0:T(8,128)S(1)}, bf16[512,128]{1,0:T(8,128)(2,1)S(1)}, bf16[512,128]{1,0:T(8,128)(2,1)S(1)}, bf16[512,128]{1,0:T(8,128)(2,1)S(1)}, bf16[512,128]{1,0:T(8,128)(2,1)S(1)}) custom-call(s32[2]{0:T(128)S(1)} %pad_add_fusion.place, bf16[4,128,512]{2,1,0:T(8,128)(2,1)S(1)} %copy-done.2, ...), custom_call_target="tpu_custom_call" | custom-call | tf_op jit(solution)/shard_map/pallas_call | solution.py:357
  36.8 2.7 %collective-permute-done.14.arrived = bf16[2,256,256]{2,1,0:T(8,128)(2,1)S(1)} collective-permute-done((bf16[2,256,256]{2,1,0:T(8,128)(2,1)S(1)}, bf16[2,256,256]{2,1,0:T(8,128)(2,1)S(1)}, u32[]{:S(2)}, u32[]{:S(2)}) %collective-permute-start.14) | collective-permute-done | bytes 262176 | tf_op jit(solution)/shard_map/ppermute | solution.py:25
  39.5 1.5 %collective-permute-start.15 = (bf16[3,256,256]{2,1,0:T(8,128)(2,1)S(1)}, bf16[3,256,256]{2,1,0:T(8,128)(2,1)S(1)}, u32[]{:S(2)}, u32[]{:S(2)}) collective-permute-start(bf16[3,256,256]{2,1,0:T(8,128)(2,1)S(1)} %shard_map.123.refs_4_), channel_id=1, source_target_pairs={{0,8},{4,20},{8,0},{12,28},{16,24},{20,4},{24,16},{28,12},{1,9},{5... | collective-permute-start | bytes 1179656 | tf_op jit(solution)/shard_map/ppermute | solution.py:31
  41.1 2.2 %collective-permute-start.12 = (bf16[512,128]{1,0:T(8,128)(2,1)S(1)}, bf16[512,128]{1,0:T(8,128)(2,1)S(1)}, u32[]{:S(2)}, u32[]{:S(2)}) collective-permute-start(bf16[512,128]{1,0:T(8,128)(2,1)S(1)} %get-tuple-element.40), channel_id=1, source_target_pairs={{0,3},{1,2},{2,1},{3,0},{4,7},{5,6},{6,5},{7,4},{8,11},{9,10},{10,... | collective-permute-start | bytes 393224 | tf_op jit(solution)/shard_map/ppermute | solution.py:25
  43.3 1.3 %collective-permute-start.13 = (bf16[512,128]{1,0:T(8,128)(2,1)S(1)}, bf16[512,128]{1,0:T(8,128)(2,1)S(1)}, u32[]{:S(2)}, u32[]{:S(2)}) collective-permute-start(bf16[512,128]{1,0:T(8,128)(2,1)S(1)} %get-tuple-element.41), channel_id=1, source_target_pairs={{0,1},{1,0},{2,3},{3,2},{4,5},{5,4},{6,7},{7,6},{8,9},{9,8},{10,11... | collective-permute-start | bytes 393224 | tf_op jit(solution)/shard_map/ppermute | solution.py:25
  44.6 7.9 %collective-permute-done.11.refs_1_ = bf16[512,128]{1,0:T(8,128)(2,1)S(1)} collective-permute-done((bf16[512,128]{1,0:T(8,128)(2,1)S(1)}, bf16[512,128]{1,0:T(8,128)(2,1)S(1)}, u32[]{:S(2)}, u32[]{:S(2)}) %collective-permute-start.11) | collective-permute-done | bytes 131104 | tf_op jit(solution)/shard_map/ppermute | solution.py:25
  52.5 1.2 %collective-permute-done.13.refs_3_ = bf16[512,128]{1,0:T(8,128)(2,1)S(1)} collective-permute-done((bf16[512,128]{1,0:T(8,128)(2,1)S(1)}, bf16[512,128]{1,0:T(8,128)(2,1)S(1)}, u32[]{:S(2)}, u32[]{:S(2)}) %collective-permute-start.13) | collective-permute-done | bytes 131104 | tf_op jit(solution)/shard_map/ppermute | solution.py:25
  53.7 1.1 %shard_map.124 = (bf16[512,128]{1,0:T(8,128)(2,1)S(1)}, bf16[512,128]{1,0:T(8,128)(2,1)S(1)}, bf16[512,128]{1,0:T(8,128)(2,1)S(1)}, bf16[512,128]{1,0:T(8,128)(2,1)S(1)}, bf16[2,3,256,256]{3,2,1,0:T(8,128)(2,1)S(1)}) custom-call(s32[2]{0:T(128)S(1)} %pad_add_fusion.place, s32[4,3]{1,0:T(4,128)S(1)} %copy-done.8, s32[4]{0:T(128)S(1)} %copy-done.12, ...), custom_call_target="tpu_custom_call" | custom-call | tf_op jit(solution)/shard_map/pallas_call | solution.py:357
  55.5 1.9 %collective-permute-start.18 = (bf16[512,128]{1,0:T(8,128)(2,1)S(1)}, bf16[512,128]{1,0:T(8,128)(2,1)S(1)}, u32[]{:S(2)}, u32[]{:S(2)}) collective-permute-start(bf16[512,128]{1,0:T(8,128)(2,1)S(1)} %get-tuple-element.48), channel_id=1, source_target_pairs={{0,2},{1,3},{2,0},{3,1},{4,6},{5,7},{6,4},{7,5},{8,10},{9,11},{10,... | collective-permute-start | bytes 393224 | tf_op jit(solution)/shard_map/ppermute | solution.py:25
  57.4 2.5 %collective-permute-start.19 = (bf16[512,128]{1,0:T(8,128)(2,1)S(1)}, bf16[512,128]{1,0:T(8,128)(2,1)S(1)}, u32[]{:S(2)}, u32[]{:S(2)}) collective-permute-start(bf16[512,128]{1,0:T(8,128)(2,1)S(1)} %get-tuple-element.49), channel_id=1, source_target_pairs={{0,3},{1,2},{2,1},{3,0},{4,7},{5,6},{6,5},{7,4},{8,11},{9,10},{10,... | collective-permute-start | bytes 393224 | tf_op jit(solution)/shard_map/ppermute | solution.py:25
  60.0 7.0 %collective-permute-done.16.far = bf16[2,3,256,256]{3,2,1,0:T(8,128)(2,1)S(1)} collective-permute-done((bf16[2,3,256,256]{3,2,1,0:T(8,128)(2,1)S(1)}, bf16[2,3,256,256]{3,2,1,0:T(8,128)(2,1)S(1)}, u32[]{:S(2)}, u32[]{:S(2)}) %collective-permute-start.16) | collective-permute-done | bytes 786464 | tf_op jit(solution)/shard_map/ppermute | solution.py:31
  69.0 2.6 %shard_map.126 = (f32[512,512]{1,0:T(8,128)S(1)}, bf16[512,512]{1,0:T(8,128)(2,1)S(1)}) custom-call(s32[2]{0:T(128)S(1)} %pad_add_fusion.place, f32[512,512]{1,0:T(8,128)S(1)} %get-tuple-element.37.refs_0_.after_attn, f32[1,512]{1,0:T(1,128)S(1)} %get-tuple-element.44.gain_ffn, bf16[6,512,256]{2,1,0:T(8,128)(2,1)S(1)} %get-tuple-element.45.w_in, ...), custom_call_target="tpu_custom_call" | custom-call | tf_op jit(solution)/shard_map/pallas_call | solution.py:357
  71.6 2.2 %shard_map.128 = bf16[512,512]{1,0:T(8,128)(2,1)} custom-call(s32[2]{0:T(128)S(1)} %pad_add_fusion.place, bf16[8,128,256]{2,1,0:T(8,128)(2,1)S(1)} %get-tuple-element.29.own_in, bf16[512,512]{1,0:T(8,128)(2,1)S(1)} %copy-done.1, f32[512,512]{1,0:T(8,128)S(1)} %get-tuple-element.51.total, bf16[512,512]{1,0:T(8,128)(2,1)S(1)} %get-tuple-element.52.ffn_in, ...), custom_call_target="tpu_custom_call" | custom-call | tf_op jit(solution)/shard_map/pallas_call | solution.py:357
  (59 shorter events, 9.0 us)
Async XLA Ops:
  0.0 21.4 %collective-permute-start = (bf16[4,128,512]{2,1,0:T(8,128)(2,1)}, bf16[4,128,512]{2,1,0:T(8,128)(2,1)S(1)}, u32[]{:S(2)}, u32[]{:S(2)}) collective-permute-start(bf16[4,128,512]{2,1,0:T(8,128)(2,1)} %states.3), channel_id=1, source_target_pairs={{0,8},{4,12},{8,16},{12,20},{16,24},{20,28},{1,9},{5,13},{9,17},{1... | collective-permute-start | bytes 1572872 | tf_op jit(solution)/shard_map/ppermute | solution.py:20
  6.0 8.8 %collective-permute-start.3 = (bf16[128,512]{1,0:T(8,128)(2,1)S(1)}, bf16[128,512]{1,0:T(8,128)(2,1)S(1)}, u32[]{:S(2)}, u32[]{:S(2)}) collective-permute-start(bf16[128,512]{1,0:T(8,128)(2,1)S(1)} %fusion), channel_id=1, source_target_pairs={{0,3},{1,2},{2,1},{3,0},{4,7},{5,6},{6,5},{7,4},{8,11},{9,10},{10,... | collective-permute-start | bytes 393224 | tf_op jit(solution)/shard_map/ppermute | solution.py:25
  9.7 10.9 %collective-permute-start.2 = (bf16[128,512]{1,0:T(8,128)(2,1)S(1)}, bf16[128,512]{1,0:T(8,128)(2,1)S(1)}, u32[]{:S(2)}, u32[]{:S(2)}) collective-permute-start(bf16[128,512]{1,0:T(8,128)(2,1)S(1)} %fusion), channel_id=1, source_target_pairs={{0,2},{1,3},{2,0},{3,1},{4,6},{5,7},{6,4},{7,5},{8,10},{9,11},{10,... | collective-permute-start | bytes 393224 | tf_op jit(solution)/shard_map/ppermute | solution.py:25
  9.7 10.9 %collective-permute-start.4 = (bf16[128,512]{1,0:T(8,128)(2,1)S(1)}, bf16[128,512]{1,0:T(8,128)(2,1)S(1)}, u32[]{:S(2)}, u32[]{:S(2)}) collective-permute-start(bf16[128,512]{1,0:T(8,128)(2,1)S(1)} %fusion), channel_id=1, source_target_pairs={{0,1},{1,0},{2,3},{3,2},{4,5},{5,4},{6,7},{7,6},{8,9},{9,8},{10,11... | collective-permute-start | bytes 393224 | tf_op jit(solution)/shard_map/ppermute | solution.py:25
  13.5 7.9 %collective-permute-start.1 = (bf16[256,256]{1,0:T(8,128)(2,1)S(1)}, bf16[256,256]{1,0:T(8,128)(2,1)S(1)}, u32[]{:S(2)}, u32[]{:S(2)}) collective-permute-start(bf16[256,256]{1,0:T(8,128)(2,1)S(1)} %get-tuple-element.30.packed), channel_id=1, source_target_pairs={{0,1},{1,0},{2,3},{3,2},{4,5},{5,4},{6,7},{7,6},{8,9},{9,8},{10,11... | collective-permute-start | bytes 393224 | tf_op jit(solution)/shard_map/ppermute | solution.py:25
  22.1 7.9 %collective-permute-start.5 = (bf16[4,128,512]{2,1,0:T(8,128)(2,1)S(1)}, bf16[4,128,512]{2,1,0:T(8,128)(2,1)S(1)}, u32[]{:S(2)}, u32[]{:S(2)}) collective-permute-start(bf16[4,128,512]{2,1,0:T(8,128)(2,1)S(1)} %get-tuple-element.31), channel_id=1, source_target_pairs={{0,4},{4,0},{8,12},{12,8},{16,20},{20,16},{24,28},{28,24},{1,5},{5... | collective-permute-start | bytes 1572872 | tf_op jit(solution)/shard_map/ppermute | solution.py:25
  22.2 5.7 %collective-permute-start.6 = (bf16[3,64,512]{2,1,0:T(8,128)(2,1)S(1)}, bf16[3,64,512]{2,1,0:T(8,128)(2,1)S(1)}, u32[]{:S(2)}, u32[]{:S(2)}) collective-permute-start(bf16[3,64,512]{2,1,0:T(8,128)(2,1)S(1)} %get-tuple-element.33), channel_id=1, source_target_pairs={{0,8},{4,20},{8,0},{12,28},{16,24},{20,4},{24,16},{28,12},{1,9},{5... | collective-permute-start | bytes 589832 | tf_op jit(solution)/shard_map/ppermute | solution.py:31
  23.7 6.3 %collective-permute-start.7 = (bf16[3,64,512]{2,1,0:T(8,128)(2,1)S(1)}, bf16[3,64,512]{2,1,0:T(8,128)(2,1)S(1)}, u32[]{:S(2)}, u32[]{:S(2)}) collective-permute-start(bf16[3,64,512]{2,1,0:T(8,128)(2,1)S(1)} %get-tuple-element.34), channel_id=1, source_target_pairs={{0,8},{4,20},{8,0},{12,28},{16,24},{20,4},{24,16},{28,12},{1,9},{5... | collective-permute-start | bytes 589832 | tf_op jit(solution)/shard_map/ppermute | solution.py:31
  24.3 7.2 %collective-permute-start.8 = (bf16[3,128,512]{2,1,0:T(8,128)(2,1)S(1)}, bf16[3,128,512]{2,1,0:T(8,128)(2,1)S(1)}, u32[]{:S(2)}, u32[]{:S(2)}) collective-permute-start(bf16[3,128,512]{2,1,0:T(8,128)(2,1)S(1)} %get-tuple-element.32.refs_0_), channel_id=1, source_target_pairs={{0,4},{4,0},{8,12},{12,8},{16,20},{20,16},{24,28},{28,24},{1,5},{5... | collective-permute-start | bytes 1179656 | tf_op jit(solution)/shard_map/ppermute | solution.py:25
  24.3 15.2 %collective-permute-start.14 = (bf16[2,256,256]{2,1,0:T(8,128)(2,1)S(1)}, bf16[2,256,256]{2,1,0:T(8,128)(2,1)S(1)}, u32[]{:S(2)}, u32[]{:S(2)}) collective-permute-start(bf16[2,256,256]{2,1,0:T(8,128)(2,1)S(1)} %get-tuple-element.42.doubled), channel_id=1, source_target_pairs={{0,2},{1,3},{2,0},{3,1},{4,6},{5,7},{6,4},{7,5},{8,10},{9,11},{10,... | collective-permute-start | bytes 786440 | tf_op jit(solution)/shard_map/ppermute | solution.py:25
  27.9 2.8 %collective-permute-start.9 = (bf16[3,64,512]{2,1,0:T(8,128)(2,1)S(1)}, bf16[3,64,512]{2,1,0:T(8,128)(2,1)S(1)}, u32[]{:S(2)}, u32[]{:S(2)}) collective-permute-start(bf16[3,64,512]{2,1,0:T(8,128)(2,1)S(1)} %collective-permute-done.6.refs_1_), channel_id=1, source_target_pairs={{0,4},{4,0},{8,12},{12,8},{16,20},{20,16},{24,28},{28,24},{1,5},{5... | collective-permute-start | bytes 589832 | tf_op jit(solution)/shard_map/ppermute | solution.py:25
  30.0 1.4 %collective-permute-start.10 = (bf16[3,64,512]{2,1,0:T(8,128)(2,1)S(1)}, bf16[3,64,512]{2,1,0:T(8,128)(2,1)S(1)}, u32[]{:S(2)}, u32[]{:S(2)}) collective-permute-start(bf16[3,64,512]{2,1,0:T(8,128)(2,1)S(1)} %collective-permute-done.7.refs_2_), channel_id=1, source_target_pairs={{0,4},{4,0},{8,12},{12,8},{16,20},{20,16},{24,28},{28,24},{1,5},{5... | collective-permute-start | bytes 589832 | tf_op jit(solution)/shard_map/ppermute | solution.py:25
  39.5 27.5 %copy-start.1 = (bf16[512,512]{1,0:T(8,128)(2,1)S(1)}, bf16[512,512]{1,0:T(8,128)(2,1)}, u32[]{:S(2)}) copy-start(bf16[512,512]{1,0:T(8,128)(2,1)} %own_out.3) | copy-start | bytes 1572868
  39.5 27.5 %copy-start.9 = (f32[512]{0:T(512)S(1)}, f32[512]{0:T(512)}, u32[]{:S(2)}) copy-start(f32[512]{0:T(512)} %param.21) | copy-start | bytes 6148
  39.5 14.2 %collective-permute-start.15 = (bf16[3,256,256]{2,1,0:T(8,128)(2,1)S(1)}, bf16[3,256,256]{2,1,0:T(8,128)(2,1)S(1)}, u32[]{:S(2)}, u32[]{:S(2)}) collective-permute-start(bf16[3,256,256]{2,1,0:T(8,128)(2,1)S(1)} %shard_map.123.refs_4_), channel_id=1, source_target_pairs={{0,8},{4,20},{8,0},{12,28},{16,24},{20,4},{24,16},{28,12},{1,9},{5... | collective-permute-start | bytes 1179656 | tf_op jit(solution)/shard_map/ppermute | solution.py:31
  41.1 11.4 %collective-permute-start.11 = (bf16[512,128]{1,0:T(8,128)(2,1)S(1)}, bf16[512,128]{1,0:T(8,128)(2,1)S(1)}, u32[]{:S(2)}, u32[]{:S(2)}) collective-permute-start(bf16[512,128]{1,0:T(8,128)(2,1)S(1)} %get-tuple-element.39), channel_id=1, source_target_pairs={{0,2},{1,3},{2,0},{3,1},{4,6},{5,7},{6,4},{7,5},{8,10},{9,11},{10,... | collective-permute-start | bytes 393224 | tf_op jit(solution)/shard_map/ppermute | solution.py:25
  41.1 11.4 %collective-permute-start.12 = (bf16[512,128]{1,0:T(8,128)(2,1)S(1)}, bf16[512,128]{1,0:T(8,128)(2,1)S(1)}, u32[]{:S(2)}, u32[]{:S(2)}) collective-permute-start(bf16[512,128]{1,0:T(8,128)(2,1)S(1)} %get-tuple-element.40), channel_id=1, source_target_pairs={{0,3},{1,2},{2,1},{3,0},{4,7},{5,6},{6,5},{7,4},{8,11},{9,10},{10,... | collective-permute-start | bytes 393224 | tf_op jit(solution)/shard_map/ppermute | solution.py:25
  43.3 10.5 %collective-permute-start.13 = (bf16[512,128]{1,0:T(8,128)(2,1)S(1)}, bf16[512,128]{1,0:T(8,128)(2,1)S(1)}, u32[]{:S(2)}, u32[]{:S(2)}) collective-permute-start(bf16[512,128]{1,0:T(8,128)(2,1)S(1)} %get-tuple-element.41), channel_id=1, source_target_pairs={{0,1},{1,0},{2,3},{3,2},{4,5},{5,4},{6,7},{7,6},{8,9},{9,8},{10,11... | collective-permute-start | bytes 393224 | tf_op jit(solution)/shard_map/ppermute | solution.py:25
  54.9 5.1 %collective-permute-start.17 = (bf16[2,3,256,256]{3,2,1,0:T(8,128)(2,1)S(1)}, bf16[2,3,256,256]{3,2,1,0:T(8,128)(2,1)S(1)}, u32[]{:S(2)}, u32[]{:S(2)}) collective-permute-start(bf16[2,3,256,256]{3,2,1,0:T(8,128)(2,1)S(1)} %get-tuple-element.43.pair), channel_id=1, source_target_pairs={{0,4},{4,0},{8,12},{12,8},{16,20},{20,16},{24,28},{28,24},{1,5},{5... | collective-permute-start | bytes 2359304 | tf_op jit(solution)/shard_map/ppermute | solution.py:25
  54.9 12.1 %collective-permute-start.16 = (bf16[2,3,256,256]{3,2,1,0:T(8,128)(2,1)S(1)}, bf16[2,3,256,256]{3,2,1,0:T(8,128)(2,1)S(1)}, u32[]{:S(2)}, u32[]{:S(2)}) collective-permute-start(bf16[2,3,256,256]{3,2,1,0:T(8,128)(2,1)S(1)} %get-tuple-element.43.pair), channel_id=1, source_target_pairs={{0,16},{4,12},{8,24},{12,4},{16,0},{20,28},{24,8},{28,20},{1,17},{... | collective-permute-start | bytes 2359304 | tf_op jit(solution)/shard_map/ppermute | solution.py:31
  55.5 12.9 %collective-permute-start.18 = (bf16[512,128]{1,0:T(8,128)(2,1)S(1)}, bf16[512,128]{1,0:T(8,128)(2,1)S(1)}, u32[]{:S(2)}, u32[]{:S(2)}) collective-permute-start(bf16[512,128]{1,0:T(8,128)(2,1)S(1)} %get-tuple-element.48), channel_id=1, source_target_pairs={{0,2},{1,3},{2,0},{3,1},{4,6},{5,7},{6,4},{7,5},{8,10},{9,11},{10,... | collective-permute-start | bytes 393224 | tf_op jit(solution)/shard_map/ppermute | solution.py:25
  57.4 11.0 %collective-permute-start.19 = (bf16[512,128]{1,0:T(8,128)(2,1)S(1)}, bf16[512,128]{1,0:T(8,128)(2,1)S(1)}, u32[]{:S(2)}, u32[]{:S(2)}) collective-permute-start(bf16[512,128]{1,0:T(8,128)(2,1)S(1)} %get-tuple-element.49), channel_id=1, source_target_pairs={{0,3},{1,2},{2,1},{3,0},{4,7},{5,6},{6,5},{7,4},{8,11},{9,10},{10,... | collective-permute-start | bytes 393224 | tf_op jit(solution)/shard_map/ppermute | solution.py:25
  60.0 8.9 %collective-permute-start.20 = (bf16[512,128]{1,0:T(8,128)(2,1)S(1)}, bf16[512,128]{1,0:T(8,128)(2,1)S(1)}, u32[]{:S(2)}, u32[]{:S(2)}) collective-permute-start(bf16[512,128]{1,0:T(8,128)(2,1)S(1)} %get-tuple-element.50), channel_id=1, source_target_pairs={{0,1},{1,0},{2,3},{3,2},{4,5},{5,4},{6,7},{7,6},{8,9},{9,8},{10,11... | collective-permute-start | bytes 393224 | tf_op jit(solution)/shard_map/ppermute | solution.py:25
  68.9 2.7 %collective-permute-start.21 = (bf16[2,3,256,256]{3,2,1,0:T(8,128)(2,1)S(1)}, bf16[2,3,256,256]{3,2,1,0:T(8,128)(2,1)S(1)}, u32[]{:S(2)}, u32[]{:S(2)}) collective-permute-start(bf16[2,3,256,256]{3,2,1,0:T(8,128)(2,1)S(1)} %shard_map.127), channel_id=1, source_target_pairs={{0,4},{4,0},{8,12},{12,8},{16,20},{20,16},{24,28},{28,24},{1,5},{5... | collective-permute-start | bytes 2359304 | tf_op jit(solution)/shard_map/ppermute | solution.py:25
  (11 other events, 111.9 us)

commit v18 on v17

--- a/solution.py
+++ b/solution.py
@@ -153,6 +153,16 @@
     def usable(query):
         return range(reach * steps + query + 1)
 
+    spans = key_count * zone_rows // span
+    pairs = range(0, steps, 2)
+    every = 2 * chunks * len(pairs) // spans
+    ticks = [0]
+
+    def tick(head):
+        ticks[0] += 1
+        if ticks[0] % every == 0 and pending and pending[0][0] <= head + 1:
+            project_some(1)
+
     def attend(head, queries):
         def tile(kind, chunk, key):
             row = kind * head_size + chunk * 8
@@ -167,6 +177,7 @@
                     if key in usable(q):
                         term = q_tiles[q] * k_tile
                         sums[q, key] = term if chunk == 0 else sums[q, key] + term
+            tick(head)
         weights_of, scales = {}, {}
         for q in queries:
             scores = jnp.concatenate([row_sum(sums[q, key]) for key in usable(q)], axis=0)
@@ -194,13 +205,12 @@
             for q in queries:
                 row = head * head_size + chunk * 8
                 context[row : row + 8, q * zone_rows : (q + 1) * zone_rows] = sums[q] * scales[q]
-
-    spans = key_count * zone_rows // span
-    project_some(spans)
-    pairs = range(0, steps, 2)
+            tick(head)
+
     for head in range(HEADS):
+        while pending and pending[0][0] <= head:
+            project_some(1)
         for pair in pairs:
-            project_some(-(-spans // len(pairs)))
             attend(head, range(pair, min(pair + 2, steps)))
 
     for step in range(steps):

time: 74.1 us -> 74.1 us (level)
  no operation moved by 1% of the time
where the time goes in v18:
time: 74.1 us; the launch traced here: 73.9 us
  waiting for transfers between devices  31.8 us (43%)
  starting transfers between devices  24.4 us (33%)
  Pallas kernels  14.3 us (19%)
  local copies, waits for them, and re-layouts  2.14 us (3%)
  other arithmetic  1.04 us (1%)
    ppermute x17, waiting for transfers between devices, swapped(): lax.ppermute(value, axis, [(source, source ^ bits) for source in range(co...  20.3 us
    ppermute x17, starting transfers between devices, swapped(): lax.ppermute(value, axis, [(source, source ^ bits) for source in range(co...  15.2 us
    pallas_call x11, Pallas kernels, call(): pl.pallas_call(kernel, out_shape=out_shape, in_specs=[pl.BlockSpec(memory...  14.3 us
    ppermute x4, waiting for transfers between devices, crossed(): return lax.ppermute(value, axis, pairs)  11.5 us
    ppermute x1, starting transfers between devices, shifted(): lax.ppermute(value, axis, [(source, source + steps) for source in range(c...  4.99 us
    ppermute x4, starting transfers between devices, crossed(): return lax.ppermute(value, axis, pairs)  4.22 us
    unnamed x26, local copies, waits for them, and re-layouts  2.14 us
  transfers between devices with their start and end apart: 22, of which 11 were waited for; matrix products, arithmetic and copies ran while one was open for 1% of the time, Pallas kernels for 14%

profile of v18, /device:TPU:0, one launch (start us, length us, event | category | flops | bytes accessed | tf_op | source)
XLA Modules:
  0.0 73.9 jit_solution(9624062615873746361)
XLA Ops:
  0.0 5.0 %collective-permute-start = (bf16[4,128,512]{2,1,0:T(8,128)(2,1)}, bf16[4,128,512]{2,1,0:T(8,128)(2,1)S(1)}, u32[]{:S(2)}, u32[]{:S(2)}) collective-permute-start(bf16[4,128,512]{2,1,0:T(8,128)(2,1)} %states.3), channel_id=1, source_target_pairs={{0,8},{4,12},{8,16},{12,20},{16,24},{20,28},{1,9},{5,13},{9,17},{1... | collective-permute-start | bytes 1572872 | tf_op jit(solution)/shard_map/ppermute | solution.py:20
  6.0 3.7 %collective-permute-start.3 = (bf16[128,512]{1,0:T(8,128)(2,1)S(1)}, bf16[128,512]{1,0:T(8,128)(2,1)S(1)}, u32[]{:S(2)}, u32[]{:S(2)}) collective-permute-start(bf16[128,512]{1,0:T(8,128)(2,1)S(1)} %fusion), channel_id=1, source_target_pairs={{0,3},{1,2},{2,1},{3,0},{4,7},{5,6},{6,5},{7,4},{8,11},{9,10},{10,... | collective-permute-start | bytes 393224 | tf_op jit(solution)/shard_map/ppermute | solution.py:25
  10.5 1.0 %copy-done = bf16[512,512]{1,0:T(8,128)(2,1)S(1)} copy-done((bf16[512,512]{1,0:T(8,128)(2,1)S(1)}, bf16[512,512]{1,0:T(8,128)(2,1)}, u32[]{:S(2)}) %copy-start) | copy-done | bytes 524312
  11.6 1.0 %copy-done.5 = bf16[128,2048]{1,0:T(8,128)(2,1)S(1)} copy-done((bf16[128,2048]{1,0:T(8,128)(2,1)S(1)}, bf16[128,2048]{1,0:T(8,128)(2,1)}, u32[]{:S(2)}) %copy-start.5) | copy-done | bytes 524312
  13.5 1.3 %collective-permute-start.1 = (bf16[256,256]{1,0:T(8,128)(2,1)S(1)}, bf16[256,256]{1,0:T(8,128)(2,1)S(1)}, u32[]{:S(2)}, u32[]{:S(2)}) collective-permute-start(bf16[256,256]{1,0:T(8,128)(2,1)S(1)} %get-tuple-element.30.packed), channel_id=1, source_target_pairs={{0,1},{1,0},{2,3},{3,2},{4,5},{5,4},{6,7},{7,6},{8,9},{9,8},{10,11... | collective-permute-start | bytes 393224 | tf_op jit(solution)/shard_map/ppermute | solution.py:25
  14.8 5.8 %collective-permute-done.2.refs_0_ = bf16[128,512]{1,0:T(8,128)(2,1)S(1)} collective-permute-done((bf16[128,512]{1,0:T(8,128)(2,1)S(1)}, bf16[128,512]{1,0:T(8,128)(2,1)S(1)}, u32[]{:S(2)}, u32[]{:S(2)}) %collective-permute-start.2) | collective-permute-done | bytes 131104 | tf_op jit(solution)/shard_map/ppermute | solution.py:25
  22.2 1.5 %collective-permute-start.6 = (bf16[3,64,512]{2,1,0:T(8,128)(2,1)S(1)}, bf16[3,64,512]{2,1,0:T(8,128)(2,1)S(1)}, u32[]{:S(2)}, u32[]{:S(2)}) collective-permute-start(bf16[3,64,512]{2,1,0:T(8,128)(2,1)S(1)} %get-tuple-element.33), channel_id=1, source_target_pairs={{0,8},{4,20},{8,0},{12,28},{16,24},{20,4},{24,16},{28,12},{1,9},{5... | collective-permute-start | bytes 589832 | tf_op jit(solution)/shard_map/ppermute | solution.py:31
  24.3 1.3 %collective-permute-start.14 = (bf16[2,256,256]{2,1,0:T(8,128)(2,1)S(1)}, bf16[2,256,256]{2,1,0:T(8,128)(2,1)S(1)}, u32[]{:S(2)}, u32[]{:S(2)}) collective-permute-start(bf16[2,256,256]{2,1,0:T(8,128)(2,1)S(1)} %get-tuple-element.42.doubled), channel_id=1, source_target_pairs={{0,2},{1,3},{2,0},{3,1},{4,6},{5,7},{6,4},{7,5},{8,10},{9,11},{10,... | collective-permute-start | bytes 786440 | tf_op jit(solution)/shard_map/ppermute | solution.py:25
  25.6 2.4 %collective-permute-done.6.refs_1_ = bf16[3,64,512]{2,1,0:T(8,128)(2,1)S(1)} collective-permute-done((bf16[3,64,512]{2,1,0:T(8,128)(2,1)S(1)}, bf16[3,64,512]{2,1,0:T(8,128)(2,1)S(1)}, u32[]{:S(2)}, u32[]{:S(2)}) %collective-permute-start.6) | collective-permute-done | bytes 196640 | tf_op jit(solution)/shard_map/ppermute | solution.py:31
  27.9 2.1 %collective-permute-done.7.refs_2_ = bf16[3,64,512]{2,1,0:T(8,128)(2,1)S(1)} collective-permute-done((bf16[3,64,512]{2,1,0:T(8,128)(2,1)S(1)}, bf16[3,64,512]{2,1,0:T(8,128)(2,1)S(1)}, u32[]{:S(2)}, u32[]{:S(2)}) %collective-permute-start.7) | collective-permute-done | bytes 196640 | tf_op jit(solution)/shard_map/ppermute | solution.py:31
  31.5 4.2 %shard_map.121 = (bf16[512,512]{1,0:T(8,128)(2,1)S(1)}, bf16[512,512]{1,0:T(8,128)(2,1)S(1)}) custom-call(s32[2]{0:T(128)S(1)} %pad_add_fusion.place, s32[1,2]{1,0:T(1,128)S(1)} %copy-done.11, bf16[1536,512]{1,0:T(8,128)(2,1)S(1)} %shard_map.120.normed, bf16[128,1536]{1,0:T(8,128)(2,1)S(1)} %copy-done.3, bf16[128,512]{1,0:T(8,128)(2,1)S(1)} %copy-done.4, ...), custom_call_target="tpu_custom_call" | custom-call | tf_op jit(solution)/shard_map/pallas_call | solution.py:367
  35.7 1.1 %shard_map.122 = (f32[512,512]{1,0:T(8,128)S(1)}, bf16[512,128]{1,0:T(8,128)(2,1)S(1)}, bf16[512,128]{1,0:T(8,128)(2,1)S(1)}, bf16[512,128]{1,0:T(8,128)(2,1)S(1)}, bf16[512,128]{1,0:T(8,128)(2,1)S(1)}) custom-call(s32[2]{0:T(128)S(1)} %pad_add_fusion.place, bf16[4,128,512]{2,1,0:T(8,128)(2,1)S(1)} %copy-done.2, ...), custom_call_target="tpu_custom_call" | custom-call | tf_op jit(solution)/shard_map/pallas_call | solution.py:367
  36.8 2.7 %collective-permute-done.14.arrived = bf16[2,256,256]{2,1,0:T(8,128)(2,1)S(1)} collective-permute-done((bf16[2,256,256]{2,1,0:T(8,128)(2,1)S(1)}, bf16[2,256,256]{2,1,0:T(8,128)(2,1)S(1)}, u32[]{:S(2)}, u32[]{:S(2)}) %collective-permute-start.14) | collective-permute-done | bytes 262176 | tf_op jit(solution)/shard_map/ppermute | solution.py:25
  39.5 1.5 %collective-permute-start.15 = (bf16[3,256,256]{2,1,0:T(8,128)(2,1)S(1)}, bf16[3,256,256]{2,1,0:T(8,128)(2,1)S(1)}, u32[]{:S(2)}, u32[]{:S(2)}) collective-permute-start(bf16[3,256,256]{2,1,0:T(8,128)(2,1)S(1)} %shard_map.123.refs_4_), channel_id=1, source_target_pairs={{0,8},{4,20},{8,0},{12,28},{16,24},{20,4},{24,16},{28,12},{1,9},{5... | collective-permute-start | bytes 1179656 | tf_op jit(solution)/shard_map/ppermute | solution.py:31
  41.1 2.2 %collective-permute-start.12 = (bf16[512,128]{1,0:T(8,128)(2,1)S(1)}, bf16[512,128]{1,0:T(8,128)(2,1)S(1)}, u32[]{:S(2)}, u32[]{:S(2)}) collective-permute-start(bf16[512,128]{1,0:T(8,128)(2,1)S(1)} %get-tuple-element.40), channel_id=1, source_target_pairs={{0,3},{1,2},{2,1},{3,0},{4,7},{5,6},{6,5},{7,4},{8,11},{9,10},{10,... | collective-permute-start | bytes 393224 | tf_op jit(solution)/shard_map/ppermute | solution.py:25
  43.3 1.3 %collective-permute-start.13 = (bf16[512,128]{1,0:T(8,128)(2,1)S(1)}, bf16[512,128]{1,0:T(8,128)(2,1)S(1)}, u32[]{:S(2)}, u32[]{:S(2)}) collective-permute-start(bf16[512,128]{1,0:T(8,128)(2,1)S(1)} %get-tuple-element.41), channel_id=1, source_target_pairs={{0,1},{1,0},{2,3},{3,2},{4,5},{5,4},{6,7},{7,6},{8,9},{9,8},{10,11... | collective-permute-start | bytes 393224 | tf_op jit(solution)/shard_map/ppermute | solution.py:25
  44.6 7.9 %collective-permute-done.11.refs_1_ = bf16[512,128]{1,0:T(8,128)(2,1)S(1)} collective-permute-done((bf16[512,128]{1,0:T(8,128)(2,1)S(1)}, bf16[512,128]{1,0:T(8,128)(2,1)S(1)}, u32[]{:S(2)}, u32[]{:S(2)}) %collective-permute-start.11) | collective-permute-done | bytes 131104 | tf_op jit(solution)/shard_map/ppermute | solution.py:25
  52.5 1.2 %collective-permute-done.13.refs_3_ = bf16[512,128]{1,0:T(8,128)(2,1)S(1)} collective-permute-done((bf16[512,128]{1,0:T(8,128)(2,1)S(1)}, bf16[512,128]{1,0:T(8,128)(2,1)S(1)}, u32[]{:S(2)}, u32[]{:S(2)}) %collective-permute-start.13) | collective-permute-done | bytes 131104 | tf_op jit(solution)/shard_map/ppermute | solution.py:25
  53.7 1.1 %shard_map.124 = (bf16[512,128]{1,0:T(8,128)(2,1)S(1)}, bf16[512,128]{1,0:T(8,128)(2,1)S(1)}, bf16[512,128]{1,0:T(8,128)(2,1)S(1)}, bf16[512,128]{1,0:T(8,128)(2,1)S(1)}, bf16[2,3,256,256]{3,2,1,0:T(8,128)(2,1)S(1)}) custom-call(s32[2]{0:T(128)S(1)} %pad_add_fusion.place, s32[4,3]{1,0:T(4,128)S(1)} %copy-done.8, s32[4]{0:T(128)S(1)} %copy-done.12, ...), custom_call_target="tpu_custom_call" | custom-call | tf_op jit(solution)/shard_map/pallas_call | solution.py:367
  55.5 1.9 %collective-permute-start.18 = (bf16[512,128]{1,0:T(8,128)(2,1)S(1)}, bf16[512,128]{1,0:T(8,128)(2,1)S(1)}, u32[]{:S(2)}, u32[]{:S(2)}) collective-permute-start(bf16[512,128]{1,0:T(8,128)(2,1)S(1)} %get-tuple-element.48), channel_id=1, source_target_pairs={{0,2},{1,3},{2,0},{3,1},{4,6},{5,7},{6,4},{7,5},{8,10},{9,11},{10,... | collective-permute-start | bytes 393224 | tf_op jit(solution)/shard_map/ppermute | solution.py:25
  57.4 2.5 %collective-permute-start.19 = (bf16[512,128]{1,0:T(8,128)(2,1)S(1)}, bf16[512,128]{1,0:T(8,128)(2,1)S(1)}, u32[]{:S(2)}, u32[]{:S(2)}) collective-permute-start(bf16[512,128]{1,0:T(8,128)(2,1)S(1)} %get-tuple-element.49), channel_id=1, source_target_pairs={{0,3},{1,2},{2,1},{3,0},{4,7},{5,6},{6,5},{7,4},{8,11},{9,10},{10,... | collective-permute-start | bytes 393224 | tf_op jit(solution)/shard_map/ppermute | solution.py:25
  60.0 7.0 %collective-permute-done.16.far = bf16[2,3,256,256]{3,2,1,0:T(8,128)(2,1)S(1)} collective-permute-done((bf16[2,3,256,256]{3,2,1,0:T(8,128)(2,1)S(1)}, bf16[2,3,256,256]{3,2,1,0:T(8,128)(2,1)S(1)}, u32[]{:S(2)}, u32[]{:S(2)}) %collective-permute-start.16) | collective-permute-done | bytes 786464 | tf_op jit(solution)/shard_map/ppermute | solution.py:31
  69.0 2.6 %shard_map.126 = (f32[512,512]{1,0:T(8,128)S(1)}, bf16[512,512]{1,0:T(8,128)(2,1)S(1)}) custom-call(s32[2]{0:T(128)S(1)} %pad_add_fusion.place, f32[512,512]{1,0:T(8,128)S(1)} %get-tuple-element.37.refs_0_.after_attn, f32[1,512]{1,0:T(1,128)S(1)} %get-tuple-element.44.gain_ffn, bf16[6,512,256]{2,1,0:T(8,128)(2,1)S(1)} %get-tuple-element.45.w_in, ...), custom_call_target="tpu_custom_call" | custom-call | tf_op jit(solution)/shard_map/pallas_call | solution.py:367
  71.6 2.2 %shard_map.128 = bf16[512,512]{1,0:T(8,128)(2,1)} custom-call(s32[2]{0:T(128)S(1)} %pad_add_fusion.place, bf16[8,128,256]{2,1,0:T(8,128)(2,1)S(1)} %get-tuple-element.29.own_in, bf16[512,512]{1,0:T(8,128)(2,1)S(1)} %copy-done.1, f32[512,512]{1,0:T(8,128)S(1)} %get-tuple-element.51.total, bf16[512,512]{1,0:T(8,128)(2,1)S(1)} %get-tuple-element.52.ffn_in, ...), custom_call_target="tpu_custom_call" | custom-call | tf_op jit(solution)/shard_map/pallas_call | solution.py:367
  (59 shorter events, 9.0 us)
Async XLA Ops:
  0.0 21.4 %collective-permute-start = (bf16[4,128,512]{2,1,0:T(8,128)(2,1)}, bf16[4,128,512]{2,1,0:T(8,128)(2,1)S(1)}, u32[]{:S(2)}, u32[]{:S(2)}) collective-permute-start(bf16[4,128,512]{2,1,0:T(8,128)(2,1)} %states.3), channel_id=1, source_target_pairs={{0,8},{4,12},{8,16},{12,20},{16,24},{20,28},{1,9},{5,13},{9,17},{1... | collective-permute-start | bytes 1572872 | tf_op jit(solution)/shard_map/ppermute | solution.py:20
  6.0 8.8 %collective-permute-start.3 = (bf16[128,512]{1,0:T(8,128)(2,1)S(1)}, bf16[128,512]{1,0:T(8,128)(2,1)S(1)}, u32[]{:S(2)}, u32[]{:S(2)}) collective-permute-start(bf16[128,512]{1,0:T(8,128)(2,1)S(1)} %fusion), channel_id=1, source_target_pairs={{0,3},{1,2},{2,1},{3,0},{4,7},{5,6},{6,5},{7,4},{8,11},{9,10},{10,... | collective-permute-start | bytes 393224 | tf_op jit(solution)/shard_map/ppermute | solution.py:25
  9.7 10.9 %collective-permute-start.2 = (bf16[128,512]{1,0:T(8,128)(2,1)S(1)}, bf16[128,512]{1,0:T(8,128)(2,1)S(1)}, u32[]{:S(2)}, u32[]{:S(2)}) collective-permute-start(bf16[128,512]{1,0:T(8,128)(2,1)S(1)} %fusion), channel_id=1, source_target_pairs={{0,2},{1,3},{2,0},{3,1},{4,6},{5,7},{6,4},{7,5},{8,10},{9,11},{10,... | collective-permute-start | bytes 393224 | tf_op jit(solution)/shard_map/ppermute | solution.py:25
  9.7 10.9 %collective-permute-start.4 = (bf16[128,512]{1,0:T(8,128)(2,1)S(1)}, bf16[128,512]{1,0:T(8,128)(2,1)S(1)}, u32[]{:S(2)}, u32[]{:S(2)}) collective-permute-start(bf16[128,512]{1,0:T(8,128)(2,1)S(1)} %fusion), channel_id=1, source_target_pairs={{0,1},{1,0},{2,3},{3,2},{4,5},{5,4},{6,7},{7,6},{8,9},{9,8},{10,11... | collective-permute-start | bytes 393224 | tf_op jit(solution)/shard_map/ppermute | solution.py:25
  13.5 7.9 %collective-permute-start.1 = (bf16[256,256]{1,0:T(8,128)(2,1)S(1)}, bf16[256,256]{1,0:T(8,128)(2,1)S(1)}, u32[]{:S(2)}, u32[]{:S(2)}) collective-permute-start(bf16[256,256]{1,0:T(8,128)(2,1)S(1)} %get-tuple-element.30.packed), channel_id=1, source_target_pairs={{0,1},{1,0},{2,3},{3,2},{4,5},{5,4},{6,7},{7,6},{8,9},{9,8},{10,11... | collective-permute-start | bytes 393224 | tf_op jit(solution)/shard_map/ppermute | solution.py:25
  22.1 7.9 %collective-permute-start.5 = (bf16[4,128,512]{2,1,0:T(8,128)(2,1)S(1)}, bf16[4,128,512]{2,1,0:T(8,128)(2,1)S(1)}, u32[]{:S(2)}, u32[]{:S(2)}) collective-permute-start(bf16[4,128,512]{2,1,0:T(8,128)(2,1)S(1)} %get-tuple-element.31), channel_id=1, source_target_pairs={{0,4},{4,0},{8,12},{12,8},{16,20},{20,16},{24,28},{28,24},{1,5},{5... | collective-permute-start | bytes 1572872 | tf_op jit(solution)/shard_map/ppermute | solution.py:25
  22.2 5.7 %collective-permute-start.6 = (bf16[3,64,512]{2,1,0:T(8,128)(2,1)S(1)}, bf16[3,64,512]{2,1,0:T(8,128)(2,1)S(1)}, u32[]{:S(2)}, u32[]{:S(2)}) collective-permute-start(bf16[3,64,512]{2,1,0:T(8,128)(2,1)S(1)} %get-tuple-element.33), channel_id=1, source_target_pairs={{0,8},{4,20},{8,0},{12,28},{16,24},{20,4},{24,16},{28,12},{1,9},{5... | collective-permute-start | bytes 589832 | tf_op jit(solution)/shard_map/ppermute | solution.py:31
  23.7 6.3 %collective-permute-start.7 = (bf16[3,64,512]{2,1,0:T(8,128)(2,1)S(1)}, bf16[3,64,512]{2,1,0:T(8,128)(2,1)S(1)}, u32[]{:S(2)}, u32[]{:S(2)}) collective-permute-start(bf16[3,64,512]{2,1,0:T(8,128)(2,1)S(1)} %get-tuple-element.34), channel_id=1, source_target_pairs={{0,8},{4,20},{8,0},{12,28},{16,24},{20,4},{24,16},{28,12},{1,9},{5... | collective-permute-start | bytes 589832 | tf_op jit(solution)/shard_map/ppermute | solution.py:31
  24.3 7.2 %collective-permute-start.8 = (bf16[3,128,512]{2,1,0:T(8,128)(2,1)S(1)}, bf16[3,128,512]{2,1,0:T(8,128)(2,1)S(1)}, u32[]{:S(2)}, u32[]{:S(2)}) collective-permute-start(bf16[3,128,512]{2,1,0:T(8,128)(2,1)S(1)} %get-tuple-element.32.refs_0_), channel_id=1, source_target_pairs={{0,4},{4,0},{8,12},{12,8},{16,20},{20,16},{24,28},{28,24},{1,5},{5... | collective-permute-start | bytes 1179656 | tf_op jit(solution)/shard_map/ppermute | solution.py:25
  24.3 15.2 %collective-permute-start.14 = (bf16[2,256,256]{2,1,0:T(8,128)(2,1)S(1)}, bf16[2,256,256]{2,1,0:T(8,128)(2,1)S(1)}, u32[]{:S(2)}, u32[]{:S(2)}) collective-permute-start(bf16[2,256,256]{2,1,0:T(8,128)(2,1)S(1)} %get-tuple-element.42.doubled), channel_id=1, source_target_pairs={{0,2},{1,3},{2,0},{3,1},{4,6},{5,7},{6,4},{7,5},{8,10},{9,11},{10,... | collective-permute-start | bytes 786440 | tf_op jit(solution)/shard_map/ppermute | solution.py:25
  27.9 2.8 %collective-permute-start.9 = (bf16[3,64,512]{2,1,0:T(8,128)(2,1)S(1)}, bf16[3,64,512]{2,1,0:T(8,128)(2,1)S(1)}, u32[]{:S(2)}, u32[]{:S(2)}) collective-permute-start(bf16[3,64,512]{2,1,0:T(8,128)(2,1)S(1)} %collective-permute-done.6.refs_1_), channel_id=1, source_target_pairs={{0,4},{4,0},{8,12},{12,8},{16,20},{20,16},{24,28},{28,24},{1,5},{5... | collective-permute-start | bytes 589832 | tf_op jit(solution)/shard_map/ppermute | solution.py:25
  30.0 1.4 %collective-permute-start.10 = (bf16[3,64,512]{2,1,0:T(8,128)(2,1)S(1)}, bf16[3,64,512]{2,1,0:T(8,128)(2,1)S(1)}, u32[]{:S(2)}, u32[]{:S(2)}) collective-permute-start(bf16[3,64,512]{2,1,0:T(8,128)(2,1)S(1)} %collective-permute-done.7.refs_2_), channel_id=1, source_target_pairs={{0,4},{4,0},{8,12},{12,8},{16,20},{20,16},{24,28},{28,24},{1,5},{5... | collective-permute-start | bytes 589832 | tf_op jit(solution)/shard_map/ppermute | solution.py:25
  39.5 27.5 %copy-start.1 = (bf16[512,512]{1,0:T(8,128)(2,1)S(1)}, bf16[512,512]{1,0:T(8,128)(2,1)}, u32[]{:S(2)}) copy-start(bf16[512,512]{1,0:T(8,128)(2,1)} %own_out.3) | copy-start | bytes 1572868
  39.5 27.5 %copy-start.9 = (f32[512]{0:T(512)S(1)}, f32[512]{0:T(512)}, u32[]{:S(2)}) copy-start(f32[512]{0:T(512)} %param.21) | copy-start | bytes 6148
  39.5 14.2 %collective-permute-start.15 = (bf16[3,256,256]{2,1,0:T(8,128)(2,1)S(1)}, bf16[3,256,256]{2,1,0:T(8,128)(2,1)S(1)}, u32[]{:S(2)}, u32[]{:S(2)}) collective-permute-start(bf16[3,256,256]{2,1,0:T(8,128)(2,1)S(1)} %shard_map.123.refs_4_), channel_id=1, source_target_pairs={{0,8},{4,20},{8,0},{12,28},{16,24},{20,4},{24,16},{28,12},{1,9},{5... | collective-permute-start | bytes 1179656 | tf_op jit(solution)/shard_map/ppermute | solution.py:31
  41.1 11.4 %collective-permute-start.11 = (bf16[512,128]{1,0:T(8,128)(2,1)S(1)}, bf16[512,128]{1,0:T(8,128)(2,1)S(1)}, u32[]{:S(2)}, u32[]{:S(2)}) collective-permute-start(bf16[512,128]{1,0:T(8,128)(2,1)S(1)} %get-tuple-element.39), channel_id=1, source_target_pairs={{0,2},{1,3},{2,0},{3,1},{4,6},{5,7},{6,4},{7,5},{8,10},{9,11},{10,... | collective-permute-start | bytes 393224 | tf_op jit(solution)/shard_map/ppermute | solution.py:25
  41.1 11.4 %collective-permute-start.12 = (bf16[512,128]{1,0:T(8,128)(2,1)S(1)}, bf16[512,128]{1,0:T(8,128)(2,1)S(1)}, u32[]{:S(2)}, u32[]{:S(2)}) collective-permute-start(bf16[512,128]{1,0:T(8,128)(2,1)S(1)} %get-tuple-element.40), channel_id=1, source_target_pairs={{0,3},{1,2},{2,1},{3,0},{4,7},{5,6},{6,5},{7,4},{8,11},{9,10},{10,... | collective-permute-start | bytes 393224 | tf_op jit(solution)/shard_map/ppermute | solution.py:25
  43.3 10.5 %collective-permute-start.13 = (bf16[512,128]{1,0:T(8,128)(2,1)S(1)}, bf16[512,128]{1,0:T(8,128)(2,1)S(1)}, u32[]{:S(2)}, u32[]{:S(2)}) collective-permute-start(bf16[512,128]{1,0:T(8,128)(2,1)S(1)} %get-tuple-element.41), channel_id=1, source_target_pairs={{0,1},{1,0},{2,3},{3,2},{4,5},{5,4},{6,7},{7,6},{8,9},{9,8},{10,11... | collective-permute-start | bytes 393224 | tf_op jit(solution)/shard_map/ppermute | solution.py:25
  54.9 5.1 %collective-permute-start.17 = (bf16[2,3,256,256]{3,2,1,0:T(8,128)(2,1)S(1)}, bf16[2,3,256,256]{3,2,1,0:T(8,128)(2,1)S(1)}, u32[]{:S(2)}, u32[]{:S(2)}) collective-permute-start(bf16[2,3,256,256]{3,2,1,0:T(8,128)(2,1)S(1)} %get-tuple-element.43.pair), channel_id=1, source_target_pairs={{0,4},{4,0},{8,12},{12,8},{16,20},{20,16},{24,28},{28,24},{1,5},{5... | collective-permute-start | bytes 2359304 | tf_op jit(solution)/shard_map/ppermute | solution.py:25
  54.9 12.1 %collective-permute-start.16 = (bf16[2,3,256,256]{3,2,1,0:T(8,128)(2,1)S(1)}, bf16[2,3,256,256]{3,2,1,0:T(8,128)(2,1)S(1)}, u32[]{:S(2)}, u32[]{:S(2)}) collective-permute-start(bf16[2,3,256,256]{3,2,1,0:T(8,128)(2,1)S(1)} %get-tuple-element.43.pair), channel_id=1, source_target_pairs={{0,16},{4,12},{8,24},{12,4},{16,0},{20,28},{24,8},{28,20},{1,17},{... | collective-permute-start | bytes 2359304 | tf_op jit(solution)/shard_map/ppermute | solution.py:31
  55.5 12.9 %collective-permute-start.18 = (bf16[512,128]{1,0:T(8,128)(2,1)S(1)}, bf16[512,128]{1,0:T(8,128)(2,1)S(1)}, u32[]{:S(2)}, u32[]{:S(2)}) collective-permute-start(bf16[512,128]{1,0:T(8,128)(2,1)S(1)} %get-tuple-element.48), channel_id=1, source_target_pairs={{0,2},{1,3},{2,0},{3,1},{4,6},{5,7},{6,4},{7,5},{8,10},{9,11},{10,... | collective-permute-start | bytes 393224 | tf_op jit(solution)/shard_map/ppermute | solution.py:25
  57.4 11.0 %collective-permute-start.19 = (bf16[512,128]{1,0:T(8,128)(2,1)S(1)}, bf16[512,128]{1,0:T(8,128)(2,1)S(1)}, u32[]{:S(2)}, u32[]{:S(2)}) collective-permute-start(bf16[512,128]{1,0:T(8,128)(2,1)S(1)} %get-tuple-element.49), channel_id=1, source_target_pairs={{0,3},{1,2},{2,1},{3,0},{4,7},{5,6},{6,5},{7,4},{8,11},{9,10},{10,... | collective-permute-start | bytes 393224 | tf_op jit(solution)/shard_map/ppermute | solution.py:25
  60.0 8.9 %collective-permute-start.20 = (bf16[512,128]{1,0:T(8,128)(2,1)S(1)}, bf16[512,128]{1,0:T(8,128)(2,1)S(1)}, u32[]{:S(2)}, u32[]{:S(2)}) collective-permute-start(bf16[512,128]{1,0:T(8,128)(2,1)S(1)} %get-tuple-element.50), channel_id=1, source_target_pairs={{0,1},{1,0},{2,3},{3,2},{4,5},{5,4},{6,7},{7,6},{8,9},{9,8},{10,11... | collective-permute-start | bytes 393224 | tf_op jit(solution)/shard_map/ppermute | solution.py:25
  68.9 2.7 %collective-permute-start.21 = (bf16[2,3,256,256]{3,2,1,0:T(8,128)(2,1)S(1)}, bf16[2,3,256,256]{3,2,1,0:T(8,128)(2,1)S(1)}, u32[]{:S(2)}, u32[]{:S(2)}) collective-permute-start(bf16[2,3,256,256]{3,2,1,0:T(8,128)(2,1)S(1)} %shard_map.127), channel_id=1, source_target_pairs={{0,4},{4,0},{8,12},{12,8},{16,20},{20,16},{24,28},{28,24},{1,5},{5... | collective-permute-start | bytes 2359304 | tf_op jit(solution)/shard_map/ppermute | solution.py:25
  (11 other events, 111.9 us)

commit v19 on v17

--- a/solution.py
+++ b/solution.py
@@ -133,7 +133,7 @@
             normed[first : first + span, :],
             (((1,), (1,)), ((), ())),
             preferred_element_type=F32,
-        )
+        ).astype(BF16).astype(F32)
 
     span = 2 * zone_rows
     pending = [(head, first) for head in range(HEADS) for first in range(0, key_count * zone_rows, span)]

time: 74.1 us -> 74.1 us (level)
  no operation moved by 1% of the time
where the time goes in v19:
time: 74.1 us; the launch traced here: 73.9 us
  waiting for transfers between devices  31.6 us (43%)
  starting transfers between devices  24.4 us (33%)
  Pallas kernels  14.4 us (19%)
  local copies, waits for them, and re-layouts  2.14 us (3%)
  other arithmetic  1.04 us (1%)
    ppermute x17, waiting for transfers between devices, swapped(): lax.ppermute(value, axis, [(source, source ^ bits) for source in range(co...  20.1 us
    ppermute x17, starting transfers between devices, swapped(): lax.ppermute(value, axis, [(source, source ^ bits) for source in range(co...  15.2 us
    pallas_call x11, Pallas kernels, call(): pl.pallas_call(kernel, out_shape=out_shape, in_specs=[pl.BlockSpec(memory...  14.4 us
    ppermute x4, waiting for transfers between devices, crossed(): return lax.ppermute(value, axis, pairs)  11.5 us
    ppermute x1, starting transfers between devices, shifted(): lax.ppermute(value, axis, [(source, source + steps) for source in range(c...  4.99 us
    ppermute x4, starting transfers between devices, crossed(): return lax.ppermute(value, axis, pairs)  4.22 us
    unnamed x26, local copies, waits for them, and re-layouts  2.14 us
  transfers between devices with their start and end apart: 22, of which 11 were waited for; matrix products, arithmetic and copies ran while one was open for 1% of the time, Pallas kernels for 14%

profile of v19, /device:TPU:0, one launch (start us, length us, event | category | flops | bytes accessed | tf_op | source)
XLA Modules:
  0.0 73.9 jit_solution(16963294133508823642)
XLA Ops:
  0.0 5.0 %collective-permute-start = (bf16[4,128,512]{2,1,0:T(8,128)(2,1)}, bf16[4,128,512]{2,1,0:T(8,128)(2,1)S(1)}, u32[]{:S(2)}, u32[]{:S(2)}) collective-permute-start(bf16[4,128,512]{2,1,0:T(8,128)(2,1)} %states.3), channel_id=1, source_target_pairs={{0,8},{4,12},{8,16},{12,20},{16,24},{20,28},{1,9},{5,13},{9,17},{1... | collective-permute-start | bytes 1572872 | tf_op jit(solution)/shard_map/ppermute | solution.py:20
  6.0 3.7 %collective-permute-start.3 = (bf16[128,512]{1,0:T(8,128)(2,1)S(1)}, bf16[128,512]{1,0:T(8,128)(2,1)S(1)}, u32[]{:S(2)}, u32[]{:S(2)}) collective-permute-start(bf16[128,512]{1,0:T(8,128)(2,1)S(1)} %fusion), channel_id=1, source_target_pairs={{0,3},{1,2},{2,1},{3,0},{4,7},{5,6},{6,5},{7,4},{8,11},{9,10},{10,... | collective-permute-start | bytes 393224 | tf_op jit(solution)/shard_map/ppermute | solution.py:25
  10.5 1.0 %copy-done = bf16[512,512]{1,0:T(8,128)(2,1)S(1)} copy-done((bf16[512,512]{1,0:T(8,128)(2,1)S(1)}, bf16[512,512]{1,0:T(8,128)(2,1)}, u32[]{:S(2)}) %copy-start) | copy-done | bytes 524312
  11.6 1.0 %copy-done.5 = bf16[128,2048]{1,0:T(8,128)(2,1)S(1)} copy-done((bf16[128,2048]{1,0:T(8,128)(2,1)S(1)}, bf16[128,2048]{1,0:T(8,128)(2,1)}, u32[]{:S(2)}) %copy-start.5) | copy-done | bytes 524312
  13.5 1.3 %collective-permute-start.1 = (bf16[256,256]{1,0:T(8,128)(2,1)S(1)}, bf16[256,256]{1,0:T(8,128)(2,1)S(1)}, u32[]{:S(2)}, u32[]{:S(2)}) collective-permute-start(bf16[256,256]{1,0:T(8,128)(2,1)S(1)} %get-tuple-element.30.packed), channel_id=1, source_target_pairs={{0,1},{1,0},{2,3},{3,2},{4,5},{5,4},{6,7},{7,6},{8,9},{9,8},{10,11... | collective-permute-start | bytes 393224 | tf_op jit(solution)/shard_map/ppermute | solution.py:25
  14.8 5.8 %collective-permute-done.2.refs_0_ = bf16[128,512]{1,0:T(8,128)(2,1)S(1)} collective-permute-done((bf16[128,512]{1,0:T(8,128)(2,1)S(1)}, bf16[128,512]{1,0:T(8,128)(2,1)S(1)}, u32[]{:S(2)}, u32[]{:S(2)}) %collective-permute-start.2) | collective-permute-done | bytes 131104 | tf_op jit(solution)/shard_map/ppermute | solution.py:25
  22.2 1.5 %collective-permute-start.6 = (bf16[3,64,512]{2,1,0:T(8,128)(2,1)S(1)}, bf16[3,64,512]{2,1,0:T(8,128)(2,1)S(1)}, u32[]{:S(2)}, u32[]{:S(2)}) collective-permute-start(bf16[3,64,512]{2,1,0:T(8,128)(2,1)S(1)} %get-tuple-element.33), channel_id=1, source_target_pairs={{0,8},{4,20},{8,0},{12,28},{16,24},{20,4},{24,16},{28,12},{1,9},{5... | collective-permute-start | bytes 589832 | tf_op jit(solution)/shard_map/ppermute | solution.py:31
  24.3 1.3 %collective-permute-start.14 = (bf16[2,256,256]{2,1,0:T(8,128)(2,1)S(1)}, bf16[2,256,256]{2,1,0:T(8,128)(2,1)S(1)}, u32[]{:S(2)}, u32[]{:S(2)}) collective-permute-start(bf16[2,256,256]{2,1,0:T(8,128)(2,1)S(1)} %get-tuple-element.42.doubled), channel_id=1, source_target_pairs={{0,2},{1,3},{2,0},{3,1},{4,6},{5,7},{6,4},{7,5},{8,10},{9,11},{10,... | collective-permute-start | bytes 786440 | tf_op jit(solution)/shard_map/ppermute | solution.py:25
  25.6 2.4 %collective-permute-done.6.refs_1_ = bf16[3,64,512]{2,1,0:T(8,128)(2,1)S(1)} collective-permute-done((bf16[3,64,512]{2,1,0:T(8,128)(2,1)S(1)}, bf16[3,64,512]{2,1,0:T(8,128)(2,1)S(1)}, u32[]{:S(2)}, u32[]{:S(2)}) %collective-permute-start.6) | collective-permute-done | bytes 196640 | tf_op jit(solution)/shard_map/ppermute | solution.py:31
  27.9 2.1 %collective-permute-done.7.refs_2_ = bf16[3,64,512]{2,1,0:T(8,128)(2,1)S(1)} collective-permute-done((bf16[3,64,512]{2,1,0:T(8,128)(2,1)S(1)}, bf16[3,64,512]{2,1,0:T(8,128)(2,1)S(1)}, u32[]{:S(2)}, u32[]{:S(2)}) %collective-permute-start.7) | collective-permute-done | bytes 196640 | tf_op jit(solution)/shard_map/ppermute | solution.py:31
  31.5 4.3 %shard_map.121 = (bf16[512,512]{1,0:T(8,128)(2,1)S(1)}, bf16[512,512]{1,0:T(8,128)(2,1)S(1)}) custom-call(s32[2]{0:T(128)S(1)} %pad_add_fusion.place, s32[1,2]{1,0:T(1,128)S(1)} %copy-done.11, bf16[1536,512]{1,0:T(8,128)(2,1)S(1)} %shard_map.120.normed, bf16[128,1536]{1,0:T(8,128)(2,1)S(1)} %copy-done.3, bf16[128,512]{1,0:T(8,128)(2,1)S(1)} %copy-done.4, ...), custom_call_target="tpu_custom_call" | custom-call | tf_op jit(solution)/shard_map/pallas_call | solution.py:357
  35.8 1.1 %shard_map.122 = (f32[512,512]{1,0:T(8,128)S(1)}, bf16[512,128]{1,0:T(8,128)(2,1)S(1)}, bf16[512,128]{1,0:T(8,128)(2,1)S(1)}, bf16[512,128]{1,0:T(8,128)(2,1)S(1)}, bf16[512,128]{1,0:T(8,128)(2,1)S(1)}) custom-call(s32[2]{0:T(128)S(1)} %pad_add_fusion.place, bf16[4,128,512]{2,1,0:T(8,128)(2,1)S(1)} %copy-done.2, ...), custom_call_target="tpu_custom_call" | custom-call | tf_op jit(solution)/shard_map/pallas_call | solution.py:357
  37.0 2.5 %collective-permute-done.14.arrived = bf16[2,256,256]{2,1,0:T(8,128)(2,1)S(1)} collective-permute-done((bf16[2,256,256]{2,1,0:T(8,128)(2,1)S(1)}, bf16[2,256,256]{2,1,0:T(8,128)(2,1)S(1)}, u32[]{:S(2)}, u32[]{:S(2)}) %collective-permute-start.14) | collective-permute-done | bytes 262176 | tf_op jit(solution)/shard_map/ppermute | solution.py:25
  39.5 1.5 %collective-permute-start.15 = (bf16[3,256,256]{2,1,0:T(8,128)(2,1)S(1)}, bf16[3,256,256]{2,1,0:T(8,128)(2,1)S(1)}, u32[]{:S(2)}, u32[]{:S(2)}) collective-permute-start(bf16[3,256,256]{2,1,0:T(8,128)(2,1)S(1)} %shard_map.123.refs_4_), channel_id=1, source_target_pairs={{0,8},{4,20},{8,0},{12,28},{16,24},{20,4},{24,16},{28,12},{1,9},{5... | collective-permute-start | bytes 1179656 | tf_op jit(solution)/shard_map/ppermute | solution.py:31
  41.1 2.2 %collective-permute-start.12 = (bf16[512,128]{1,0:T(8,128)(2,1)S(1)}, bf16[512,128]{1,0:T(8,128)(2,1)S(1)}, u32[]{:S(2)}, u32[]{:S(2)}) collective-permute-start(bf16[512,128]{1,0:T(8,128)(2,1)S(1)} %get-tuple-element.40), channel_id=1, source_target_pairs={{0,3},{1,2},{2,1},{3,0},{4,7},{5,6},{6,5},{7,4},{8,11},{9,10},{10,... | collective-permute-start | bytes 393224 | tf_op jit(solution)/shard_map/ppermute | solution.py:25
  43.3 1.3 %collective-permute-start.13 = (bf16[512,128]{1,0:T(8,128)(2,1)S(1)}, bf16[512,128]{1,0:T(8,128)(2,1)S(1)}, u32[]{:S(2)}, u32[]{:S(2)}) collective-permute-start(bf16[512,128]{1,0:T(8,128)(2,1)S(1)} %get-tuple-element.41), channel_id=1, source_target_pairs={{0,1},{1,0},{2,3},{3,2},{4,5},{5,4},{6,7},{7,6},{8,9},{9,8},{10,11... | collective-permute-start | bytes 393224 | tf_op jit(solution)/shard_map/ppermute | solution.py:25
  44.6 7.9 %collective-permute-done.11.refs_1_ = bf16[512,128]{1,0:T(8,128)(2,1)S(1)} collective-permute-done((bf16[512,128]{1,0:T(8,128)(2,1)S(1)}, bf16[512,128]{1,0:T(8,128)(2,1)S(1)}, u32[]{:S(2)}, u32[]{:S(2)}) %collective-permute-start.11) | collective-permute-done | bytes 131104 | tf_op jit(solution)/shard_map/ppermute | solution.py:25
  52.5 1.2 %collective-permute-done.13.refs_3_ = bf16[512,128]{1,0:T(8,128)(2,1)S(1)} collective-permute-done((bf16[512,128]{1,0:T(8,128)(2,1)S(1)}, bf16[512,128]{1,0:T(8,128)(2,1)S(1)}, u32[]{:S(2)}, u32[]{:S(2)}) %collective-permute-start.13) | collective-permute-done | bytes 131104 | tf_op jit(solution)/shard_map/ppermute | solution.py:25
  53.7 1.1 %shard_map.124 = (bf16[512,128]{1,0:T(8,128)(2,1)S(1)}, bf16[512,128]{1,0:T(8,128)(2,1)S(1)}, bf16[512,128]{1,0:T(8,128)(2,1)S(1)}, bf16[512,128]{1,0:T(8,128)(2,1)S(1)}, bf16[2,3,256,256]{3,2,1,0:T(8,128)(2,1)S(1)}) custom-call(s32[2]{0:T(128)S(1)} %pad_add_fusion.place, s32[4,3]{1,0:T(4,128)S(1)} %copy-done.8, s32[4]{0:T(128)S(1)} %copy-done.12, ...), custom_call_target="tpu_custom_call" | custom-call | tf_op jit(solution)/shard_map/pallas_call | solution.py:357
  55.5 1.9 %collective-permute-start.18 = (bf16[512,128]{1,0:T(8,128)(2,1)S(1)}, bf16[512,128]{1,0:T(8,128)(2,1)S(1)}, u32[]{:S(2)}, u32[]{:S(2)}) collective-permute-start(bf16[512,128]{1,0:T(8,128)(2,1)S(1)} %get-tuple-element.48), channel_id=1, source_target_pairs={{0,2},{1,3},{2,0},{3,1},{4,6},{5,7},{6,4},{7,5},{8,10},{9,11},{10,... | collective-permute-start | bytes 393224 | tf_op jit(solution)/shard_map/ppermute | solution.py:25
  57.4 2.5 %collective-permute-start.19 = (bf16[512,128]{1,0:T(8,128)(2,1)S(1)}, bf16[512,128]{1,0:T(8,128)(2,1)S(1)}, u32[]{:S(2)}, u32[]{:S(2)}) collective-permute-start(bf16[512,128]{1,0:T(8,128)(2,1)S(1)} %get-tuple-element.49), channel_id=1, source_target_pairs={{0,3},{1,2},{2,1},{3,0},{4,7},{5,6},{6,5},{7,4},{8,11},{9,10},{10,... | collective-permute-start | bytes 393224 | tf_op jit(solution)/shard_map/ppermute | solution.py:25
  60.0 7.0 %collective-permute-done.16.far = bf16[2,3,256,256]{3,2,1,0:T(8,128)(2,1)S(1)} collective-permute-done((bf16[2,3,256,256]{3,2,1,0:T(8,128)(2,1)S(1)}, bf16[2,3,256,256]{3,2,1,0:T(8,128)(2,1)S(1)}, u32[]{:S(2)}, u32[]{:S(2)}) %collective-permute-start.16) | collective-permute-done | bytes 786464 | tf_op jit(solution)/shard_map/ppermute | solution.py:31
  69.0 2.6 %shard_map.126 = (f32[512,512]{1,0:T(8,128)S(1)}, bf16[512,512]{1,0:T(8,128)(2,1)S(1)}) custom-call(s32[2]{0:T(128)S(1)} %pad_add_fusion.place, f32[512,512]{1,0:T(8,128)S(1)} %get-tuple-element.37.refs_0_.after_attn, f32[1,512]{1,0:T(1,128)S(1)} %get-tuple-element.44.gain_ffn, bf16[6,512,256]{2,1,0:T(8,128)(2,1)S(1)} %get-tuple-element.45.w_in, ...), custom_call_target="tpu_custom_call" | custom-call | tf_op jit(solution)/shard_map/pallas_call | solution.py:357
  71.6 2.2 %shard_map.128 = bf16[512,512]{1,0:T(8,128)(2,1)} custom-call(s32[2]{0:T(128)S(1)} %pad_add_fusion.place, bf16[8,128,256]{2,1,0:T(8,128)(2,1)S(1)} %get-tuple-element.29.own_in, bf16[512,512]{1,0:T(8,128)(2,1)S(1)} %copy-done.1, f32[512,512]{1,0:T(8,128)S(1)} %get-tuple-element.51.total, bf16[512,512]{1,0:T(8,128)(2,1)S(1)} %get-tuple-element.52.ffn_in, ...), custom_call_target="tpu_custom_call" | custom-call | tf_op jit(solution)/shard_map/pallas_call | solution.py:357
  (59 shorter events, 9.0 us)
Async XLA Ops:
  0.0 21.4 %collective-permute-start = (bf16[4,128,512]{2,1,0:T(8,128)(2,1)}, bf16[4,128,512]{2,1,0:T(8,128)(2,1)S(1)}, u32[]{:S(2)}, u32[]{:S(2)}) collective-permute-start(bf16[4,128,512]{2,1,0:T(8,128)(2,1)} %states.3), channel_id=1, source_target_pairs={{0,8},{4,12},{8,16},{12,20},{16,24},{20,28},{1,9},{5,13},{9,17},{1... | collective-permute-start | bytes 1572872 | tf_op jit(solution)/shard_map/ppermute | solution.py:20
  6.0 8.8 %collective-permute-start.3 = (bf16[128,512]{1,0:T(8,128)(2,1)S(1)}, bf16[128,512]{1,0:T(8,128)(2,1)S(1)}, u32[]{:S(2)}, u32[]{:S(2)}) collective-permute-start(bf16[128,512]{1,0:T(8,128)(2,1)S(1)} %fusion), channel_id=1, source_target_pairs={{0,3},{1,2},{2,1},{3,0},{4,7},{5,6},{6,5},{7,4},{8,11},{9,10},{10,... | collective-permute-start | bytes 393224 | tf_op jit(solution)/shard_map/ppermute | solution.py:25
  9.7 10.9 %collective-permute-start.2 = (bf16[128,512]{1,0:T(8,128)(2,1)S(1)}, bf16[128,512]{1,0:T(8,128)(2,1)S(1)}, u32[]{:S(2)}, u32[]{:S(2)}) collective-permute-start(bf16[128,512]{1,0:T(8,128)(2,1)S(1)} %fusion), channel_id=1, source_target_pairs={{0,2},{1,3},{2,0},{3,1},{4,6},{5,7},{6,4},{7,5},{8,10},{9,11},{10,... | collective-permute-start | bytes 393224 | tf_op jit(solution)/shard_map/ppermute | solution.py:25
  9.7 10.9 %collective-permute-start.4 = (bf16[128,512]{1,0:T(8,128)(2,1)S(1)}, bf16[128,512]{1,0:T(8,128)(2,1)S(1)}, u32[]{:S(2)}, u32[]{:S(2)}) collective-permute-start(bf16[128,512]{1,0:T(8,128)(2,1)S(1)} %fusion), channel_id=1, source_target_pairs={{0,1},{1,0},{2,3},{3,2},{4,5},{5,4},{6,7},{7,6},{8,9},{9,8},{10,11... | collective-permute-start | bytes 393224 | tf_op jit(solution)/shard_map/ppermute | solution.py:25
  13.5 7.9 %collective-permute-start.1 = (bf16[256,256]{1,0:T(8,128)(2,1)S(1)}, bf16[256,256]{1,0:T(8,128)(2,1)S(1)}, u32[]{:S(2)}, u32[]{:S(2)}) collective-permute-start(bf16[256,256]{1,0:T(8,128)(2,1)S(1)} %get-tuple-element.30.packed), channel_id=1, source_target_pairs={{0,1},{1,0},{2,3},{3,2},{4,5},{5,4},{6,7},{7,6},{8,9},{9,8},{10,11... | collective-permute-start | bytes 393224 | tf_op jit(solution)/shard_map/ppermute | solution.py:25
  22.1 7.9 %collective-permute-start.5 = (bf16[4,128,512]{2,1,0:T(8,128)(2,1)S(1)}, bf16[4,128,512]{2,1,0:T(8,128)(2,1)S(1)}, u32[]{:S(2)}, u32[]{:S(2)}) collective-permute-start(bf16[4,128,512]{2,1,0:T(8,128)(2,1)S(1)} %get-tuple-element.31), channel_id=1, source_target_pairs={{0,4},{4,0},{8,12},{12,8},{16,20},{20,16},{24,28},{28,24},{1,5},{5... | collective-permute-start | bytes 1572872 | tf_op jit(solution)/shard_map/ppermute | solution.py:25
  22.2 5.7 %collective-permute-start.6 = (bf16[3,64,512]{2,1,0:T(8,128)(2,1)S(1)}, bf16[3,64,512]{2,1,0:T(8,128)(2,1)S(1)}, u32[]{:S(2)}, u32[]{:S(2)}) collective-permute-start(bf16[3,64,512]{2,1,0:T(8,128)(2,1)S(1)} %get-tuple-element.33), channel_id=1, source_target_pairs={{0,8},{4,20},{8,0},{12,28},{16,24},{20,4},{24,16},{28,12},{1,9},{5... | collective-permute-start | bytes 589832 | tf_op jit(solution)/shard_map/ppermute | solution.py:31
  23.7 6.3 %collective-permute-start.7 = (bf16[3,64,512]{2,1,0:T(8,128)(2,1)S(1)}, bf16[3,64,512]{2,1,0:T(8,128)(2,1)S(1)}, u32[]{:S(2)}, u32[]{:S(2)}) collective-permute-start(bf16[3,64,512]{2,1,0:T(8,128)(2,1)S(1)} %get-tuple-element.34), channel_id=1, source_target_pairs={{0,8},{4,20},{8,0},{12,28},{16,24},{20,4},{24,16},{28,12},{1,9},{5... | collective-permute-start | bytes 589832 | tf_op jit(solution)/shard_map/ppermute | solution.py:31
  24.3 7.2 %collective-permute-start.8 = (bf16[3,128,512]{2,1,0:T(8,128)(2,1)S(1)}, bf16[3,128,512]{2,1,0:T(8,128)(2,1)S(1)}, u32[]{:S(2)}, u32[]{:S(2)}) collective-permute-start(bf16[3,128,512]{2,1,0:T(8,128)(2,1)S(1)} %get-tuple-element.32.refs_0_), channel_id=1, source_target_pairs={{0,4},{4,0},{8,12},{12,8},{16,20},{20,16},{24,28},{28,24},{1,5},{5... | collective-permute-start | bytes 1179656 | tf_op jit(solution)/shard_map/ppermute | solution.py:25
  24.3 15.2 %collective-permute-start.14 = (bf16[2,256,256]{2,1,0:T(8,128)(2,1)S(1)}, bf16[2,256,256]{2,1,0:T(8,128)(2,1)S(1)}, u32[]{:S(2)}, u32[]{:S(2)}) collective-permute-start(bf16[2,256,256]{2,1,0:T(8,128)(2,1)S(1)} %get-tuple-element.42.doubled), channel_id=1, source_target_pairs={{0,2},{1,3},{2,0},{3,1},{4,6},{5,7},{6,4},{7,5},{8,10},{9,11},{10,... | collective-permute-start | bytes 786440 | tf_op jit(solution)/shard_map/ppermute | solution.py:25
  27.9 2.8 %collective-permute-start.9 = (bf16[3,64,512]{2,1,0:T(8,128)(2,1)S(1)}, bf16[3,64,512]{2,1,0:T(8,128)(2,1)S(1)}, u32[]{:S(2)}, u32[]{:S(2)}) collective-permute-start(bf16[3,64,512]{2,1,0:T(8,128)(2,1)S(1)} %collective-permute-done.6.refs_1_), channel_id=1, source_target_pairs={{0,4},{4,0},{8,12},{12,8},{16,20},{20,16},{24,28},{28,24},{1,5},{5... | collective-permute-start | bytes 589832 | tf_op jit(solution)/shard_map/ppermute | solution.py:25
  30.0 1.4 %collective-permute-start.10 = (bf16[3,64,512]{2,1,0:T(8,128)(2,1)S(1)}, bf16[3,64,512]{2,1,0:T(8,128)(2,1)S(1)}, u32[]{:S(2)}, u32[]{:S(2)}) collective-permute-start(bf16[3,64,512]{2,1,0:T(8,128)(2,1)S(1)} %collective-permute-done.7.refs_2_), channel_id=1, source_target_pairs={{0,4},{4,0},{8,12},{12,8},{16,20},{20,16},{24,28},{28,24},{1,5},{5... | collective-permute-start | bytes 589832 | tf_op jit(solution)/shard_map/ppermute | solution.py:25
  39.5 27.5 %copy-start.1 = (bf16[512,512]{1,0:T(8,128)(2,1)S(1)}, bf16[512,512]{1,0:T(8,128)(2,1)}, u32[]{:S(2)}) copy-start(bf16[512,512]{1,0:T(8,128)(2,1)} %own_out.3) | copy-start | bytes 1572868
  39.5 27.5 %copy-start.9 = (f32[512]{0:T(512)S(1)}, f32[512]{0:T(512)}, u32[]{:S(2)}) copy-start(f32[512]{0:T(512)} %param.21) | copy-start | bytes 6148
  39.5 14.2 %collective-permute-start.15 = (bf16[3,256,256]{2,1,0:T(8,128)(2,1)S(1)}, bf16[3,256,256]{2,1,0:T(8,128)(2,1)S(1)}, u32[]{:S(2)}, u32[]{:S(2)}) collective-permute-start(bf16[3,256,256]{2,1,0:T(8,128)(2,1)S(1)} %shard_map.123.refs_4_), channel_id=1, source_target_pairs={{0,8},{4,20},{8,0},{12,28},{16,24},{20,4},{24,16},{28,12},{1,9},{5... | collective-permute-start | bytes 1179656 | tf_op jit(solution)/shard_map/ppermute | solution.py:31
  41.1 11.4 %collective-permute-start.11 = (bf16[512,128]{1,0:T(8,128)(2,1)S(1)}, bf16[512,128]{1,0:T(8,128)(2,1)S(1)}, u32[]{:S(2)}, u32[]{:S(2)}) collective-permute-start(bf16[512,128]{1,0:T(8,128)(2,1)S(1)} %get-tuple-element.39), channel_id=1, source_target_pairs={{0,2},{1,3},{2,0},{3,1},{4,6},{5,7},{6,4},{7,5},{8,10},{9,11},{10,... | collective-permute-start | bytes 393224 | tf_op jit(solution)/shard_map/ppermute | solution.py:25
  41.1 11.4 %collective-permute-start.12 = (bf16[512,128]{1,0:T(8,128)(2,1)S(1)}, bf16[512,128]{1,0:T(8,128)(2,1)S(1)}, u32[]{:S(2)}, u32[]{:S(2)}) collective-permute-start(bf16[512,128]{1,0:T(8,128)(2,1)S(1)} %get-tuple-element.40), channel_id=1, source_target_pairs={{0,3},{1,2},{2,1},{3,0},{4,7},{5,6},{6,5},{7,4},{8,11},{9,10},{10,... | collective-permute-start | bytes 393224 | tf_op jit(solution)/shard_map/ppermute | solution.py:25
  43.3 10.5 %collective-permute-start.13 = (bf16[512,128]{1,0:T(8,128)(2,1)S(1)}, bf16[512,128]{1,0:T(8,128)(2,1)S(1)}, u32[]{:S(2)}, u32[]{:S(2)}) collective-permute-start(bf16[512,128]{1,0:T(8,128)(2,1)S(1)} %get-tuple-element.41), channel_id=1, source_target_pairs={{0,1},{1,0},{2,3},{3,2},{4,5},{5,4},{6,7},{7,6},{8,9},{9,8},{10,11... | collective-permute-start | bytes 393224 | tf_op jit(solution)/shard_map/ppermute | solution.py:25
  54.9 5.1 %collective-permute-start.17 = (bf16[2,3,256,256]{3,2,1,0:T(8,128)(2,1)S(1)}, bf16[2,3,256,256]{3,2,1,0:T(8,128)(2,1)S(1)}, u32[]{:S(2)}, u32[]{:S(2)}) collective-permute-start(bf16[2,3,256,256]{3,2,1,0:T(8,128)(2,1)S(1)} %get-tuple-element.43.pair), channel_id=1, source_target_pairs={{0,4},{4,0},{8,12},{12,8},{16,20},{20,16},{24,28},{28,24},{1,5},{5... | collective-permute-start | bytes 2359304 | tf_op jit(solution)/shard_map/ppermute | solution.py:25
  54.9 12.1 %collective-permute-start.16 = (bf16[2,3,256,256]{3,2,1,0:T(8,128)(2,1)S(1)}, bf16[2,3,256,256]{3,2,1,0:T(8,128)(2,1)S(1)}, u32[]{:S(2)}, u32[]{:S(2)}) collective-permute-start(bf16[2,3,256,256]{3,2,1,0:T(8,128)(2,1)S(1)} %get-tuple-element.43.pair), channel_id=1, source_target_pairs={{0,16},{4,12},{8,24},{12,4},{16,0},{20,28},{24,8},{28,20},{1,17},{... | collective-permute-start | bytes 2359304 | tf_op jit(solution)/shard_map/ppermute | solution.py:31
  55.5 12.9 %collective-permute-start.18 = (bf16[512,128]{1,0:T(8,128)(2,1)S(1)}, bf16[512,128]{1,0:T(8,128)(2,1)S(1)}, u32[]{:S(2)}, u32[]{:S(2)}) collective-permute-start(bf16[512,128]{1,0:T(8,128)(2,1)S(1)} %get-tuple-element.48), channel_id=1, source_target_pairs={{0,2},{1,3},{2,0},{3,1},{4,6},{5,7},{6,4},{7,5},{8,10},{9,11},{10,... | collective-permute-start | bytes 393224 | tf_op jit(solution)/shard_map/ppermute | solution.py:25
  57.4 11.0 %collective-permute-start.19 = (bf16[512,128]{1,0:T(8,128)(2,1)S(1)}, bf16[512,128]{1,0:T(8,128)(2,1)S(1)}, u32[]{:S(2)}, u32[]{:S(2)}) collective-permute-start(bf16[512,128]{1,0:T(8,128)(2,1)S(1)} %get-tuple-element.49), channel_id=1, source_target_pairs={{0,3},{1,2},{2,1},{3,0},{4,7},{5,6},{6,5},{7,4},{8,11},{9,10},{10,... | collective-permute-start | bytes 393224 | tf_op jit(solution)/shard_map/ppermute | solution.py:25
  60.0 8.9 %collective-permute-start.20 = (bf16[512,128]{1,0:T(8,128)(2,1)S(1)}, bf16[512,128]{1,0:T(8,128)(2,1)S(1)}, u32[]{:S(2)}, u32[]{:S(2)}) collective-permute-start(bf16[512,128]{1,0:T(8,128)(2,1)S(1)} %get-tuple-element.50), channel_id=1, source_target_pairs={{0,1},{1,0},{2,3},{3,2},{4,5},{5,4},{6,7},{7,6},{8,9},{9,8},{10,11... | collective-permute-start | bytes 393224 | tf_op jit(solution)/shard_map/ppermute | solution.py:25
  68.9 2.7 %collective-permute-start.21 = (bf16[2,3,256,256]{3,2,1,0:T(8,128)(2,1)S(1)}, bf16[2,3,256,256]{3,2,1,0:T(8,128)(2,1)S(1)}, u32[]{:S(2)}, u32[]{:S(2)}) collective-permute-start(bf16[2,3,256,256]{3,2,1,0:T(8,128)(2,1)S(1)} %shard_map.127), channel_id=1, source_target_pairs={{0,4},{4,0},{8,12},{12,8},{16,20},{20,16},{24,28},{28,24},{1,5},{5... | collective-permute-start | bytes 2359304 | tf_op jit(solution)/shard_map/ppermute | solution.py:25
  (11 other events, 111.6 us)

commit v20 on v19

--- a/solution.py
+++ b/solution.py
@@ -94,7 +94,8 @@
     out = refs[-1]
     near = doubled.shape[0]
     out[: near - 1] = doubled[1:]
-    out[near - 1 :] = arrived[...]
+    for index in range(near):
+        out[2 * near - 2 - index] = arrived[index]
 
 
 def attention_kernel(zones, reach, steps, place, pattern, normed, own_qkv, own_attn, *refs):
@@ -481,7 +482,7 @@
         (),
         (),
         4,
-        [doubled, swapped(doubled, "zone", bits), after_attn],
+        [doubled, swapped(doubled, "zone", 2 * bits - 1), after_attn],
     )
     nearest = crossed(across, "tm", 2, 4)
 

time: 74.1 us -> 73.3 us (0.989)
  waiting for transfers between devices: 31.6 us -> 26.9 us
  starting transfers between devices: 24.4 us -> 28.2 us
    ppermute x17, starting transfers between devices: 15.2 us -> 19.1 us  [swapped(): lax.ppermute(value, axis, [(source, source ^ bits) for source in range(co...]
    ppermute x17, waiting for transfers between devices: 20.1 us -> 17.1 us  [swapped(): lax.ppermute(value, axis, [(source, source ^ bits) for source in range(co...]
    ppermute x4, waiting for transfers between devices: 11.5 us -> 9.8 us  [crossed(): return lax.ppermute(value, axis, pairs)]
where the time goes in v20:
time: 73.3 us; the launch traced here: 73 us
  starting transfers between devices  28.2 us (38%)
  waiting for transfers between devices  26.9 us (37%)
  Pallas kernels  14.4 us (20%)
  local copies, waits for them, and re-layouts  2.15 us (3%)
  other arithmetic  1.04 us (1%)
    ppermute x17, starting transfers between devices, swapped(): lax.ppermute(value, axis, [(source, source ^ bits) for source in range(co...  19.1 us
    ppermute x17, waiting for transfers between devices, swapped(): lax.ppermute(value, axis, [(source, source ^ bits) for source in range(co...  17.1 us
    pallas_call x11, Pallas kernels, call(): pl.pallas_call(kernel, out_shape=out_shape, in_specs=[pl.BlockSpec(memory...  14.4 us
    ppermute x4, waiting for transfers between devices, crossed(): return lax.ppermute(value, axis, pairs)  9.8 us
    ppermute x1, starting transfers between devices, shifted(): lax.ppermute(value, axis, [(source, source + steps) for source in range(c...  4.99 us
    ppermute x4, starting transfers between devices, crossed(): return lax.ppermute(value, axis, pairs)  4.16 us
    unnamed x26, local copies, waits for them, and re-layouts  2.15 us
  transfers between devices with their start and end apart: 22, of which 11 were waited for; matrix products, arithmetic and copies ran while one was open for 1% of the time, Pallas kernels for 14%

profile of v20, /device:TPU:0, one launch (start us, length us, event | category | flops | bytes accessed | tf_op | source)
XLA Modules:
  0.0 73.0 jit_solution(10813721116494088948)
XLA Ops:
  0.0 5.0 %collective-permute-start = (bf16[4,128,512]{2,1,0:T(8,128)(2,1)}, bf16[4,128,512]{2,1,0:T(8,128)(2,1)S(1)}, u32[]{:S(2)}, u32[]{:S(2)}) collective-permute-start(bf16[4,128,512]{2,1,0:T(8,128)(2,1)} %states.3), channel_id=1, source_target_pairs={{0,8},{4,12},{8,16},{12,20},{16,24},{20,28},{1,9},{5,13},{9,17},{1... | collective-permute-start | bytes 1572872 | tf_op jit(solution)/shard_map/ppermute | solution.py:20
  5.0 1.0 %fusion = bf16[128,512]{1,0:T(8,128)(2,1)S(1)} fusion(s32[]{:T(128)S(6)} %select_n.3, bf16[128,1536]{1,0:T(8,128)(2,1)} %own_qkv.1, bf16[128,512]{1,0:T(8,128)(2,1)} %own_attn.1), kind=kLoop, calls=%fused_computation.2 | loop fusion | flops 262144 | bytes 655364 | tf_op jit(solution)/shard_map/concatenate | solution.py:400
  6.0 3.7 %collective-permute-start.3 = (bf16[128,512]{1,0:T(8,128)(2,1)S(1)}, bf16[128,512]{1,0:T(8,128)(2,1)S(1)}, u32[]{:S(2)}, u32[]{:S(2)}) collective-permute-start(bf16[128,512]{1,0:T(8,128)(2,1)S(1)} %fusion), channel_id=1, source_target_pairs={{0,3},{1,2},{2,1},{3,0},{4,7},{5,6},{6,5},{7,4},{8,11},{9,10},{10,... | collective-permute-start | bytes 393224 | tf_op jit(solution)/shard_map/ppermute | solution.py:25
  10.5 1.0 %copy-done = bf16[512,512]{1,0:T(8,128)(2,1)S(1)} copy-done((bf16[512,512]{1,0:T(8,128)(2,1)S(1)}, bf16[512,512]{1,0:T(8,128)(2,1)}, u32[]{:S(2)}) %copy-start) | copy-done | bytes 524312
  11.6 1.0 %copy-done.5 = bf16[128,2048]{1,0:T(8,128)(2,1)S(1)} copy-done((bf16[128,2048]{1,0:T(8,128)(2,1)S(1)}, bf16[128,2048]{1,0:T(8,128)(2,1)}, u32[]{:S(2)}) %copy-start.5) | copy-done | bytes 524312
  12.6 0.9 %shard_map.118 = (bf16[8,128,256]{2,1,0:T(8,128)(2,1)S(1)}, bf16[256,256]{1,0:T(8,128)(2,1)S(1)}) custom-call(s32[2]{0:T(128)S(1)} %pad_add_fusion.place, bf16[128,2048]{1,0:T(8,128)(2,1)S(1)} %copy-done.5, bf16[512,512]{1,0:T(8,128)(2,1)S(1)} %copy-done), custom_call_target="tpu_custom_call" | custom-call | tf_op jit(solution)/shard_map/pallas_call | solution.py:358
  13.5 1.3 %collective-permute-start.1 = (bf16[256,256]{1,0:T(8,128)(2,1)S(1)}, bf16[256,256]{1,0:T(8,128)(2,1)S(1)}, u32[]{:S(2)}, u32[]{:S(2)}) collective-permute-start(bf16[256,256]{1,0:T(8,128)(2,1)S(1)} %get-tuple-element.30.packed), channel_id=1, source_target_pairs={{0,1},{1,0},{2,3},{3,2},{4,5},{5,4},{6,7},{7,6},{8,9},{9,8},{10,11... | collective-permute-start | bytes 393224 | tf_op jit(solution)/shard_map/ppermute | solution.py:25
  14.8 5.8 %collective-permute-done.2.refs_0_ = bf16[128,512]{1,0:T(8,128)(2,1)S(1)} collective-permute-done((bf16[128,512]{1,0:T(8,128)(2,1)S(1)}, bf16[128,512]{1,0:T(8,128)(2,1)S(1)}, u32[]{:S(2)}, u32[]{:S(2)}) %collective-permute-start.2) | collective-permute-done | bytes 131104 | tf_op jit(solution)/shard_map/ppermute | solution.py:25
  22.2 1.5 %collective-permute-start.6 = (bf16[3,64,512]{2,1,0:T(8,128)(2,1)S(1)}, bf16[3,64,512]{2,1,0:T(8,128)(2,1)S(1)}, u32[]{:S(2)}, u32[]{:S(2)}) collective-permute-start(bf16[3,64,512]{2,1,0:T(8,128)(2,1)S(1)} %get-tuple-element.33), channel_id=1, source_target_pairs={{0,8},{4,20},{8,0},{12,28},{16,24},{20,4},{24,16},{28,12},{1,9},{5... | collective-permute-start | bytes 589832 | tf_op jit(solution)/shard_map/ppermute | solution.py:31
  24.3 3.2 %collective-permute-start.14 = (bf16[2,256,256]{2,1,0:T(8,128)(2,1)S(1)}, bf16[2,256,256]{2,1,0:T(8,128)(2,1)S(1)}, u32[]{:S(2)}, u32[]{:S(2)}) collective-permute-start(bf16[2,256,256]{2,1,0:T(8,128)(2,1)S(1)} %get-tuple-element.42.doubled), channel_id=1, source_target_pairs={{0,3},{1,2},{2,1},{3,0},{4,7},{5,6},{6,5},{7,4},{8,11},{9,10},{10,... | collective-permute-start | bytes 786440 | tf_op jit(solution)/shard_map/ppermute | solution.py:25
  27.9 2.1 %collective-permute-done.7.refs_2_ = bf16[3,64,512]{2,1,0:T(8,128)(2,1)S(1)} collective-permute-done((bf16[3,64,512]{2,1,0:T(8,128)(2,1)S(1)}, bf16[3,64,512]{2,1,0:T(8,128)(2,1)S(1)}, u32[]{:S(2)}, u32[]{:S(2)}) %collective-permute-start.7) | collective-permute-done | bytes 196640 | tf_op jit(solution)/shard_map/ppermute | solution.py:31
  31.5 4.3 %shard_map.121 = (bf16[512,512]{1,0:T(8,128)(2,1)S(1)}, bf16[512,512]{1,0:T(8,128)(2,1)S(1)}) custom-call(s32[2]{0:T(128)S(1)} %pad_add_fusion.place, s32[1,2]{1,0:T(1,128)S(1)} %copy-done.11, bf16[1536,512]{1,0:T(8,128)(2,1)S(1)} %shard_map.120.normed, bf16[128,1536]{1,0:T(8,128)(2,1)S(1)} %copy-done.3, bf16[128,512]{1,0:T(8,128)(2,1)S(1)} %copy-done.4, ...), custom_call_target="tpu_custom_call" | custom-call | tf_op jit(solution)/shard_map/pallas_call | solution.py:358
  35.8 1.1 %shard_map.122 = (f32[512,512]{1,0:T(8,128)S(1)}, bf16[512,128]{1,0:T(8,128)(2,1)S(1)}, bf16[512,128]{1,0:T(8,128)(2,1)S(1)}, bf16[512,128]{1,0:T(8,128)(2,1)S(1)}, bf16[512,128]{1,0:T(8,128)(2,1)S(1)}) custom-call(s32[2]{0:T(128)S(1)} %pad_add_fusion.place, bf16[4,128,512]{2,1,0:T(8,128)(2,1)S(1)} %copy-done.2, ...), custom_call_target="tpu_custom_call" | custom-call | tf_op jit(solution)/shard_map/pallas_call | solution.py:358
  37.1 1.5 %collective-permute-start.15 = (bf16[3,256,256]{2,1,0:T(8,128)(2,1)S(1)}, bf16[3,256,256]{2,1,0:T(8,128)(2,1)S(1)}, u32[]{:S(2)}, u32[]{:S(2)}) collective-permute-start(bf16[3,256,256]{2,1,0:T(8,128)(2,1)S(1)} %shard_map.123.refs_4_), channel_id=1, source_target_pairs={{0,8},{4,20},{8,0},{12,28},{16,24},{20,4},{24,16},{28,12},{1,9},{5... | collective-permute-start | bytes 1179656 | tf_op jit(solution)/shard_map/ppermute | solution.py:31
  38.6 3.0 %collective-permute-start.11 = (bf16[512,128]{1,0:T(8,128)(2,1)S(1)}, bf16[512,128]{1,0:T(8,128)(2,1)S(1)}, u32[]{:S(2)}, u32[]{:S(2)}) collective-permute-start(bf16[512,128]{1,0:T(8,128)(2,1)S(1)} %get-tuple-element.39), channel_id=1, source_target_pairs={{0,2},{1,3},{2,0},{3,1},{4,6},{5,7},{6,4},{7,5},{8,10},{9,11},{10,... | collective-permute-start | bytes 393224 | tf_op jit(solution)/shard_map/ppermute | solution.py:25
  41.6 2.6 %collective-permute-start.12 = (bf16[512,128]{1,0:T(8,128)(2,1)S(1)}, bf16[512,128]{1,0:T(8,128)(2,1)S(1)}, u32[]{:S(2)}, u32[]{:S(2)}) collective-permute-start(bf16[512,128]{1,0:T(8,128)(2,1)S(1)} %get-tuple-element.40), channel_id=1, source_target_pairs={{0,3},{1,2},{2,1},{3,0},{4,7},{5,6},{6,5},{7,4},{8,11},{9,10},{10,... | collective-permute-start | bytes 393224 | tf_op jit(solution)/shard_map/ppermute | solution.py:25
  44.2 6.7 %collective-permute-done.11.refs_1_ = bf16[512,128]{1,0:T(8,128)(2,1)S(1)} collective-permute-done((bf16[512,128]{1,0:T(8,128)(2,1)S(1)}, bf16[512,128]{1,0:T(8,128)(2,1)S(1)}, u32[]{:S(2)}, u32[]{:S(2)}) %collective-permute-start.11) | collective-permute-done | bytes 131104 | tf_op jit(solution)/shard_map/ppermute | solution.py:25
  52.0 1.1 %shard_map.124 = (bf16[512,128]{1,0:T(8,128)(2,1)S(1)}, bf16[512,128]{1,0:T(8,128)(2,1)S(1)}, bf16[512,128]{1,0:T(8,128)(2,1)S(1)}, bf16[512,128]{1,0:T(8,128)(2,1)S(1)}, bf16[2,3,256,256]{3,2,1,0:T(8,128)(2,1)S(1)}) custom-call(s32[2]{0:T(128)S(1)} %pad_add_fusion.place, s32[4,3]{1,0:T(4,128)S(1)} %copy-done.8, s32[4]{0:T(128)S(1)} %copy-done.12, ...), custom_call_target="tpu_custom_call" | custom-call | tf_op jit(solution)/shard_map/pallas_call | solution.py:358
  53.7 3.7 %collective-permute-start.18 = (bf16[512,128]{1,0:T(8,128)(2,1)S(1)}, bf16[512,128]{1,0:T(8,128)(2,1)S(1)}, u32[]{:S(2)}, u32[]{:S(2)}) collective-permute-start(bf16[512,128]{1,0:T(8,128)(2,1)S(1)} %get-tuple-element.48), channel_id=1, source_target_pairs={{0,2},{1,3},{2,0},{3,1},{4,6},{5,7},{6,4},{7,5},{8,10},{9,11},{10,... | collective-permute-start | bytes 393224 | tf_op jit(solution)/shard_map/ppermute | solution.py:25
  58.0 7.3 %collective-permute-done.16.far = bf16[2,3,256,256]{3,2,1,0:T(8,128)(2,1)S(1)} collective-permute-done((bf16[2,3,256,256]{3,2,1,0:T(8,128)(2,1)S(1)}, bf16[2,3,256,256]{3,2,1,0:T(8,128)(2,1)S(1)}, u32[]{:S(2)}, u32[]{:S(2)}) %collective-permute-start.16) | collective-permute-done | bytes 786464 | tf_op jit(solution)/shard_map/ppermute | solution.py:31
  66.0 1.0 %collective-permute-done.18.refs_1_.refs_0_ = bf16[512,128]{1,0:T(8,128)(2,1)S(1)} collective-permute-done((bf16[512,128]{1,0:T(8,128)(2,1)S(1)}, bf16[512,128]{1,0:T(8,128)(2,1)S(1)}, u32[]{:S(2)}, u32[]{:S(2)}) %collective-permute-start.18) | collective-permute-done | bytes 131104 | tf_op jit(solution)/shard_map/ppermute | solution.py:25
  67.0 1.0 %collective-permute-done.20.refs_3_.refs_2_ = bf16[512,128]{1,0:T(8,128)(2,1)S(1)} collective-permute-done((bf16[512,128]{1,0:T(8,128)(2,1)S(1)}, bf16[512,128]{1,0:T(8,128)(2,1)S(1)}, u32[]{:S(2)}, u32[]{:S(2)}) %collective-permute-start.20) | collective-permute-done | bytes 131104 | tf_op jit(solution)/shard_map/ppermute | solution.py:25
  68.1 2.6 %shard_map.126 = (f32[512,512]{1,0:T(8,128)S(1)}, bf16[512,512]{1,0:T(8,128)(2,1)S(1)}) custom-call(s32[2]{0:T(128)S(1)} %pad_add_fusion.place, f32[512,512]{1,0:T(8,128)S(1)} %get-tuple-element.37.refs_0_.after_attn, f32[1,512]{1,0:T(1,128)S(1)} %get-tuple-element.44.gain_ffn, bf16[6,512,256]{2,1,0:T(8,128)(2,1)S(1)} %get-tuple-element.45.w_in, ...), custom_call_target="tpu_custom_call" | custom-call | tf_op jit(solution)/shard_map/pallas_call | solution.py:358
  70.7 2.2 %shard_map.128 = bf16[512,512]{1,0:T(8,128)(2,1)} custom-call(s32[2]{0:T(128)S(1)} %pad_add_fusion.place, bf16[8,128,256]{2,1,0:T(8,128)(2,1)S(1)} %get-tuple-element.29.own_in, bf16[512,512]{1,0:T(8,128)(2,1)S(1)} %copy-done.1, f32[512,512]{1,0:T(8,128)S(1)} %get-tuple-element.51.total, bf16[512,512]{1,0:T(8,128)(2,1)S(1)} %get-tuple-element.52.ffn_in, ...), custom_call_target="tpu_custom_call" | custom-call | tf_op jit(solution)/shard_map/pallas_call | solution.py:358
  (59 shorter events, 8.0 us)
Async XLA Ops:
  0.0 21.4 %collective-permute-start = (bf16[4,128,512]{2,1,0:T(8,128)(2,1)}, bf16[4,128,512]{2,1,0:T(8,128)(2,1)S(1)}, u32[]{:S(2)}, u32[]{:S(2)}) collective-permute-start(bf16[4,128,512]{2,1,0:T(8,128)(2,1)} %states.3), channel_id=1, source_target_pairs={{0,8},{4,12},{8,16},{12,20},{16,24},{20,28},{1,9},{5,13},{9,17},{1... | collective-permute-start | bytes 1572872 | tf_op jit(solution)/shard_map/ppermute | solution.py:20
  6.0 8.8 %collective-permute-start.3 = (bf16[128,512]{1,0:T(8,128)(2,1)S(1)}, bf16[128,512]{1,0:T(8,128)(2,1)S(1)}, u32[]{:S(2)}, u32[]{:S(2)}) collective-permute-start(bf16[128,512]{1,0:T(8,128)(2,1)S(1)} %fusion), channel_id=1, source_target_pairs={{0,3},{1,2},{2,1},{3,0},{4,7},{5,6},{6,5},{7,4},{8,11},{9,10},{10,... | collective-permute-start | bytes 393224 | tf_op jit(solution)/shard_map/ppermute | solution.py:25
  9.7 10.9 %collective-permute-start.2 = (bf16[128,512]{1,0:T(8,128)(2,1)S(1)}, bf16[128,512]{1,0:T(8,128)(2,1)S(1)}, u32[]{:S(2)}, u32[]{:S(2)}) collective-permute-start(bf16[128,512]{1,0:T(8,128)(2,1)S(1)} %fusion), channel_id=1, source_target_pairs={{0,2},{1,3},{2,0},{3,1},{4,6},{5,7},{6,4},{7,5},{8,10},{9,11},{10,... | collective-permute-start | bytes 393224 | tf_op jit(solution)/shard_map/ppermute | solution.py:25
  9.7 10.9 %collective-permute-start.4 = (bf16[128,512]{1,0:T(8,128)(2,1)S(1)}, bf16[128,512]{1,0:T(8,128)(2,1)S(1)}, u32[]{:S(2)}, u32[]{:S(2)}) collective-permute-start(bf16[128,512]{1,0:T(8,128)(2,1)S(1)} %fusion), channel_id=1, source_target_pairs={{0,1},{1,0},{2,3},{3,2},{4,5},{5,4},{6,7},{7,6},{8,9},{9,8},{10,11... | collective-permute-start | bytes 393224 | tf_op jit(solution)/shard_map/ppermute | solution.py:25
  13.5 7.9 %collective-permute-start.1 = (bf16[256,256]{1,0:T(8,128)(2,1)S(1)}, bf16[256,256]{1,0:T(8,128)(2,1)S(1)}, u32[]{:S(2)}, u32[]{:S(2)}) collective-permute-start(bf16[256,256]{1,0:T(8,128)(2,1)S(1)} %get-tuple-element.30.packed), channel_id=1, source_target_pairs={{0,1},{1,0},{2,3},{3,2},{4,5},{5,4},{6,7},{7,6},{8,9},{9,8},{10,11... | collective-permute-start | bytes 393224 | tf_op jit(solution)/shard_map/ppermute | solution.py:25
  22.1 7.9 %collective-permute-start.5 = (bf16[4,128,512]{2,1,0:T(8,128)(2,1)S(1)}, bf16[4,128,512]{2,1,0:T(8,128)(2,1)S(1)}, u32[]{:S(2)}, u32[]{:S(2)}) collective-permute-start(bf16[4,128,512]{2,1,0:T(8,128)(2,1)S(1)} %get-tuple-element.31), channel_id=1, source_target_pairs={{0,4},{4,0},{8,12},{12,8},{16,20},{20,16},{24,28},{28,24},{1,5},{5... | collective-permute-start | bytes 1572872 | tf_op jit(solution)/shard_map/ppermute | solution.py:25
  22.2 5.7 %collective-permute-start.6 = (bf16[3,64,512]{2,1,0:T(8,128)(2,1)S(1)}, bf16[3,64,512]{2,1,0:T(8,128)(2,1)S(1)}, u32[]{:S(2)}, u32[]{:S(2)}) collective-permute-start(bf16[3,64,512]{2,1,0:T(8,128)(2,1)S(1)} %get-tuple-element.33), channel_id=1, source_target_pairs={{0,8},{4,20},{8,0},{12,28},{16,24},{20,4},{24,16},{28,12},{1,9},{5... | collective-permute-start | bytes 589832 | tf_op jit(solution)/shard_map/ppermute | solution.py:31
  23.7 6.3 %collective-permute-start.7 = (bf16[3,64,512]{2,1,0:T(8,128)(2,1)S(1)}, bf16[3,64,512]{2,1,0:T(8,128)(2,1)S(1)}, u32[]{:S(2)}, u32[]{:S(2)}) collective-permute-start(bf16[3,64,512]{2,1,0:T(8,128)(2,1)S(1)} %get-tuple-element.34), channel_id=1, source_target_pairs={{0,8},{4,20},{8,0},{12,28},{16,24},{20,4},{24,16},{28,12},{1,9},{5... | collective-permute-start | bytes 589832 | tf_op jit(solution)/shard_map/ppermute | solution.py:31
  24.3 7.2 %collective-permute-start.8 = (bf16[3,128,512]{2,1,0:T(8,128)(2,1)S(1)}, bf16[3,128,512]{2,1,0:T(8,128)(2,1)S(1)}, u32[]{:S(2)}, u32[]{:S(2)}) collective-permute-start(bf16[3,128,512]{2,1,0:T(8,128)(2,1)S(1)} %get-tuple-element.32.refs_0_), channel_id=1, source_target_pairs={{0,4},{4,0},{8,12},{12,8},{16,20},{20,16},{24,28},{28,24},{1,5},{5... | collective-permute-start | bytes 1179656 | tf_op jit(solution)/shard_map/ppermute | solution.py:25
  24.3 12.7 %collective-permute-start.14 = (bf16[2,256,256]{2,1,0:T(8,128)(2,1)S(1)}, bf16[2,256,256]{2,1,0:T(8,128)(2,1)S(1)}, u32[]{:S(2)}, u32[]{:S(2)}) collective-permute-start(bf16[2,256,256]{2,1,0:T(8,128)(2,1)S(1)} %get-tuple-element.42.doubled), channel_id=1, source_target_pairs={{0,3},{1,2},{2,1},{3,0},{4,7},{5,6},{6,5},{7,4},{8,11},{9,10},{10,... | collective-permute-start | bytes 786440 | tf_op jit(solution)/shard_map/ppermute | solution.py:25
  27.9 2.8 %collective-permute-start.9 = (bf16[3,64,512]{2,1,0:T(8,128)(2,1)S(1)}, bf16[3,64,512]{2,1,0:T(8,128)(2,1)S(1)}, u32[]{:S(2)}, u32[]{:S(2)}) collective-permute-start(bf16[3,64,512]{2,1,0:T(8,128)(2,1)S(1)} %collective-permute-done.6.refs_1_), channel_id=1, source_target_pairs={{0,4},{4,0},{8,12},{12,8},{16,20},{20,16},{24,28},{28,24},{1,5},{5... | collective-permute-start | bytes 589832 | tf_op jit(solution)/shard_map/ppermute | solution.py:25
  30.0 1.4 %collective-permute-start.10 = (bf16[3,64,512]{2,1,0:T(8,128)(2,1)S(1)}, bf16[3,64,512]{2,1,0:T(8,128)(2,1)S(1)}, u32[]{:S(2)}, u32[]{:S(2)}) collective-permute-start(bf16[3,64,512]{2,1,0:T(8,128)(2,1)S(1)} %collective-permute-done.7.refs_2_), channel_id=1, source_target_pairs={{0,4},{4,0},{8,12},{12,8},{16,20},{20,16},{24,28},{28,24},{1,5},{5... | collective-permute-start | bytes 589832 | tf_op jit(solution)/shard_map/ppermute | solution.py:25
  37.0 28.2 %copy-start.1 = (bf16[512,512]{1,0:T(8,128)(2,1)S(1)}, bf16[512,512]{1,0:T(8,128)(2,1)}, u32[]{:S(2)}) copy-start(bf16[512,512]{1,0:T(8,128)(2,1)} %own_out.3) | copy-start | bytes 1572868
  37.0 28.2 %copy-start.9 = (f32[512]{0:T(512)S(1)}, f32[512]{0:T(512)}, u32[]{:S(2)}) copy-start(f32[512]{0:T(512)} %param.21) | copy-start | bytes 6148
  37.1 14.9 %collective-permute-start.15 = (bf16[3,256,256]{2,1,0:T(8,128)(2,1)S(1)}, bf16[3,256,256]{2,1,0:T(8,128)(2,1)S(1)}, u32[]{:S(2)}, u32[]{:S(2)}) collective-permute-start(bf16[3,256,256]{2,1,0:T(8,128)(2,1)S(1)} %shard_map.123.refs_4_), channel_id=1, source_target_pairs={{0,8},{4,20},{8,0},{12,28},{16,24},{20,4},{24,16},{28,12},{1,9},{5... | collective-permute-start | bytes 1179656 | tf_op jit(solution)/shard_map/ppermute | solution.py:31
  38.6 12.3 %collective-permute-start.11 = (bf16[512,128]{1,0:T(8,128)(2,1)S(1)}, bf16[512,128]{1,0:T(8,128)(2,1)S(1)}, u32[]{:S(2)}, u32[]{:S(2)}) collective-permute-start(bf16[512,128]{1,0:T(8,128)(2,1)S(1)} %get-tuple-element.39), channel_id=1, source_target_pairs={{0,2},{1,3},{2,0},{3,1},{4,6},{5,7},{6,4},{7,5},{8,10},{9,11},{10,... | collective-permute-start | bytes 393224 | tf_op jit(solution)/shard_map/ppermute | solution.py:25
  41.6 9.8 %collective-permute-start.12 = (bf16[512,128]{1,0:T(8,128)(2,1)S(1)}, bf16[512,128]{1,0:T(8,128)(2,1)S(1)}, u32[]{:S(2)}, u32[]{:S(2)}) collective-permute-start(bf16[512,128]{1,0:T(8,128)(2,1)S(1)} %get-tuple-element.40), channel_id=1, source_target_pairs={{0,3},{1,2},{2,1},{3,0},{4,7},{5,6},{6,5},{7,4},{8,11},{9,10},{10,... | collective-permute-start | bytes 393224 | tf_op jit(solution)/shard_map/ppermute | solution.py:25
  44.2 7.7 %collective-permute-start.13 = (bf16[512,128]{1,0:T(8,128)(2,1)S(1)}, bf16[512,128]{1,0:T(8,128)(2,1)S(1)}, u32[]{:S(2)}, u32[]{:S(2)}) collective-permute-start(bf16[512,128]{1,0:T(8,128)(2,1)S(1)} %get-tuple-element.41), channel_id=1, source_target_pairs={{0,1},{1,0},{2,3},{3,2},{4,5},{5,4},{6,7},{7,6},{8,9},{9,8},{10,11... | collective-permute-start | bytes 393224 | tf_op jit(solution)/shard_map/ppermute | solution.py:25
  53.1 4.9 %collective-permute-start.17 = (bf16[2,3,256,256]{3,2,1,0:T(8,128)(2,1)S(1)}, bf16[2,3,256,256]{3,2,1,0:T(8,128)(2,1)S(1)}, u32[]{:S(2)}, u32[]{:S(2)}) collective-permute-start(bf16[2,3,256,256]{3,2,1,0:T(8,128)(2,1)S(1)} %get-tuple-element.43.pair), channel_id=1, source_target_pairs={{0,4},{4,0},{8,12},{12,8},{16,20},{20,16},{24,28},{28,24},{1,5},{5... | collective-permute-start | bytes 2359304 | tf_op jit(solution)/shard_map/ppermute | solution.py:25
  53.2 12.1 %collective-permute-start.16 = (bf16[2,3,256,256]{3,2,1,0:T(8,128)(2,1)S(1)}, bf16[2,3,256,256]{3,2,1,0:T(8,128)(2,1)S(1)}, u32[]{:S(2)}, u32[]{:S(2)}) collective-permute-start(bf16[2,3,256,256]{3,2,1,0:T(8,128)(2,1)S(1)} %get-tuple-element.43.pair), channel_id=1, source_target_pairs={{0,16},{4,12},{8,24},{12,4},{16,0},{20,28},{24,8},{28,20},{1,17},{... | collective-permute-start | bytes 2359304 | tf_op jit(solution)/shard_map/ppermute | solution.py:31
  53.7 13.3 %collective-permute-start.18 = (bf16[512,128]{1,0:T(8,128)(2,1)S(1)}, bf16[512,128]{1,0:T(8,128)(2,1)S(1)}, u32[]{:S(2)}, u32[]{:S(2)}) collective-permute-start(bf16[512,128]{1,0:T(8,128)(2,1)S(1)} %get-tuple-element.48), channel_id=1, source_target_pairs={{0,2},{1,3},{2,0},{3,1},{4,6},{5,7},{6,4},{7,5},{8,10},{9,11},{10,... | collective-permute-start | bytes 393224 | tf_op jit(solution)/shard_map/ppermute | solution.py:25
  57.4 9.6 %collective-permute-start.19 = (bf16[512,128]{1,0:T(8,128)(2,1)S(1)}, bf16[512,128]{1,0:T(8,128)(2,1)S(1)}, u32[]{:S(2)}, u32[]{:S(2)}) collective-permute-start(bf16[512,128]{1,0:T(8,128)(2,1)S(1)} %get-tuple-element.49), channel_id=1, source_target_pairs={{0,3},{1,2},{2,1},{3,0},{4,7},{5,6},{6,5},{7,4},{8,11},{9,10},{10,... | collective-permute-start | bytes 393224 | tf_op jit(solution)/shard_map/ppermute | solution.py:25
  58.0 10.0 %collective-permute-start.20 = (bf16[512,128]{1,0:T(8,128)(2,1)S(1)}, bf16[512,128]{1,0:T(8,128)(2,1)S(1)}, u32[]{:S(2)}, u32[]{:S(2)}) collective-permute-start(bf16[512,128]{1,0:T(8,128)(2,1)S(1)} %get-tuple-element.50), channel_id=1, source_target_pairs={{0,1},{1,0},{2,3},{3,2},{4,5},{5,4},{6,7},{7,6},{8,9},{9,8},{10,11... | collective-permute-start | bytes 393224 | tf_op jit(solution)/shard_map/ppermute | solution.py:25
  68.0 2.7 %collective-permute-start.21 = (bf16[2,3,256,256]{3,2,1,0:T(8,128)(2,1)S(1)}, bf16[2,3,256,256]{3,2,1,0:T(8,128)(2,1)S(1)}, u32[]{:S(2)}, u32[]{:S(2)}) collective-permute-start(bf16[2,3,256,256]{3,2,1,0:T(8,128)(2,1)S(1)} %shard_map.127), channel_id=1, source_target_pairs={{0,4},{4,0},{8,12},{12,8},{16,20},{20,16},{24,28},{28,24},{1,5},{5... | collective-permute-start | bytes 2359304 | tf_op jit(solution)/shard_map/ppermute | solution.py:25
  (11 other events, 106.3 us)

commit v21 on v20

--- a/solution.py
+++ b/solution.py
@@ -33,7 +33,7 @@
 
 def steps_over(count):
     half = count // 2
-    return tuple(range(half, count)) + tuple(range(1, half))
+    return tuple(range(count - 1, 0, -1))
 
 
 def rms_scale(values, gain):

time: 73.3 us -> 73.8 us (level)
  waiting for transfers between devices: 26.9 us -> 27.8 us
    ppermute x17, waiting for transfers between devices: 17.1 us -> 18.5 us  [swapped(): lax.ppermute(value, axis, [(source, source ^ bits) for source in range(co...]
  transfers between devices with their start and end apart: 22 -> 22, of which waited for: 11 -> 10; matrix products, arithmetic and copies ran while one was open for 1% -> 1% of each run, Pallas kernels for 14% -> 14%
where the time goes in v21:
time: 73.8 us; the launch traced here: 73.5 us
  starting transfers between devices  27.9 us (38%)
  waiting for transfers between devices  27.8 us (38%)
  Pallas kernels  14.4 us (20%)
  local copies, waits for them, and re-layouts  2.15 us (3%)
  other arithmetic  1.04 us (1%)
    ppermute x17, starting transfers between devices, swapped(): lax.ppermute(value, axis, [(source, source ^ bits) for source in range(co...  18.6 us
    ppermute x17, waiting for transfers between devices, swapped(): lax.ppermute(value, axis, [(source, source ^ bits) for source in range(co...  18.5 us
    pallas_call x11, Pallas kernels, call(): pl.pallas_call(kernel, out_shape=out_shape, in_specs=[pl.BlockSpec(memory...  14.4 us
    ppermute x4, waiting for transfers between devices, crossed(): return lax.ppermute(value, axis, pairs)  9.29 us
    ppermute x1, starting transfers between devices, shifted(): lax.ppermute(value, axis, [(source, source + steps) for source in range(c...  4.99 us
    ppermute x4, starting transfers between devices, crossed(): return lax.ppermute(value, axis, pairs)  4.22 us
    unnamed x26, local copies, waits for them, and re-layouts  2.15 us
  transfers between devices with their start and end apart: 22, of which 10 were waited for; matrix products, arithmetic and copies ran while one was open for 1% of the time, Pallas kernels for 14%

profile of v21, /device:TPU:0, one launch (start us, length us, event | category | flops | bytes accessed | tf_op | source)
XLA Modules:
  0.0 73.5 jit_solution(9884520761661503010)
XLA Ops:
  0.0 5.0 %collective-permute-start = (bf16[4,128,512]{2,1,0:T(8,128)(2,1)}, bf16[4,128,512]{2,1,0:T(8,128)(2,1)S(1)}, u32[]{:S(2)}, u32[]{:S(2)}) collective-permute-start(bf16[4,128,512]{2,1,0:T(8,128)(2,1)} %states.3), channel_id=1, source_target_pairs={{0,8},{4,12},{8,16},{12,20},{16,24},{20,28},{1,9},{5,13},{9,17},{1... | collective-permute-start | bytes 1572872 | tf_op jit(solution)/shard_map/ppermute | solution.py:20
  6.0 2.7 %collective-permute-start.3 = (bf16[128,512]{1,0:T(8,128)(2,1)S(1)}, bf16[128,512]{1,0:T(8,128)(2,1)S(1)}, u32[]{:S(2)}, u32[]{:S(2)}) collective-permute-start(bf16[128,512]{1,0:T(8,128)(2,1)S(1)} %fusion), channel_id=1, source_target_pairs={{0,2},{1,3},{2,0},{3,1},{4,6},{5,7},{6,4},{7,5},{8,10},{9,11},{10,... | collective-permute-start | bytes 393224 | tf_op jit(solution)/shard_map/ppermute | solution.py:25
  8.7 1.3 %collective-permute-start.2 = (bf16[128,512]{1,0:T(8,128)(2,1)S(1)}, bf16[128,512]{1,0:T(8,128)(2,1)S(1)}, u32[]{:S(2)}, u32[]{:S(2)}) collective-permute-start(bf16[128,512]{1,0:T(8,128)(2,1)S(1)} %fusion), channel_id=1, source_target_pairs={{0,3},{1,2},{2,1},{3,0},{4,7},{5,6},{6,5},{7,4},{8,11},{9,10},{10,... | collective-permute-start | bytes 393224 | tf_op jit(solution)/shard_map/ppermute | solution.py:25
  10.3 1.0 %copy-done = bf16[512,512]{1,0:T(8,128)(2,1)S(1)} copy-done((bf16[512,512]{1,0:T(8,128)(2,1)S(1)}, bf16[512,512]{1,0:T(8,128)(2,1)}, u32[]{:S(2)}) %copy-start) | copy-done | bytes 524312
  11.4 1.0 %copy-done.5 = bf16[128,2048]{1,0:T(8,128)(2,1)S(1)} copy-done((bf16[128,2048]{1,0:T(8,128)(2,1)S(1)}, bf16[128,2048]{1,0:T(8,128)(2,1)}, u32[]{:S(2)}) %copy-start.5) | copy-done | bytes 524312
  13.3 1.9 %collective-permute-start.1 = (bf16[256,256]{1,0:T(8,128)(2,1)S(1)}, bf16[256,256]{1,0:T(8,128)(2,1)S(1)}, u32[]{:S(2)}, u32[]{:S(2)}) collective-permute-start(bf16[256,256]{1,0:T(8,128)(2,1)S(1)} %get-tuple-element.30.packed), channel_id=1, source_target_pairs={{0,1},{1,0},{2,3},{3,2},{4,5},{5,4},{6,7},{7,6},{8,9},{9,8},{10,11... | collective-permute-start | bytes 393224 | tf_op jit(solution)/shard_map/ppermute | solution.py:25
  15.2 3.6 %collective-permute-done.3.refs_1_ = bf16[128,512]{1,0:T(8,128)(2,1)S(1)} collective-permute-done((bf16[128,512]{1,0:T(8,128)(2,1)S(1)}, bf16[128,512]{1,0:T(8,128)(2,1)S(1)}, u32[]{:S(2)}, u32[]{:S(2)}) %collective-permute-start.3) | collective-permute-done | bytes 131104 | tf_op jit(solution)/shard_map/ppermute | solution.py:25
  18.7 1.6 %collective-permute-done.4.refs_2_ = bf16[128,512]{1,0:T(8,128)(2,1)S(1)} collective-permute-done((bf16[128,512]{1,0:T(8,128)(2,1)S(1)}, bf16[128,512]{1,0:T(8,128)(2,1)S(1)}, u32[]{:S(2)}, u32[]{:S(2)}) %collective-permute-start.4) | collective-permute-done | bytes 131104 | tf_op jit(solution)/shard_map/ppermute | solution.py:25
  20.3 1.5 %collective-permute-done.1.beside = bf16[256,256]{1,0:T(8,128)(2,1)S(1)} collective-permute-done((bf16[256,256]{1,0:T(8,128)(2,1)S(1)}, bf16[256,256]{1,0:T(8,128)(2,1)S(1)}, u32[]{:S(2)}, u32[]{:S(2)}) %collective-permute-start.1) | collective-permute-done | bytes 131104 | tf_op jit(solution)/shard_map/ppermute | solution.py:25
  22.5 1.5 %collective-permute-start.6 = (bf16[3,64,512]{2,1,0:T(8,128)(2,1)S(1)}, bf16[3,64,512]{2,1,0:T(8,128)(2,1)S(1)}, u32[]{:S(2)}, u32[]{:S(2)}) collective-permute-start(bf16[3,64,512]{2,1,0:T(8,128)(2,1)S(1)} %get-tuple-element.33), channel_id=1, source_target_pairs={{0,8},{4,20},{8,0},{12,28},{16,24},{20,4},{24,16},{28,12},{1,9},{5... | collective-permute-start | bytes 589832 | tf_op jit(solution)/shard_map/ppermute | solution.py:31
  24.6 3.5 %collective-permute-start.14 = (bf16[2,256,256]{2,1,0:T(8,128)(2,1)S(1)}, bf16[2,256,256]{2,1,0:T(8,128)(2,1)S(1)}, u32[]{:S(2)}, u32[]{:S(2)}) collective-permute-start(bf16[2,256,256]{2,1,0:T(8,128)(2,1)S(1)} %get-tuple-element.42.doubled), channel_id=1, source_target_pairs={{0,3},{1,2},{2,1},{3,0},{4,7},{5,6},{6,5},{7,4},{8,11},{9,10},{10,... | collective-permute-start | bytes 786440 | tf_op jit(solution)/shard_map/ppermute | solution.py:25
  28.3 2.0 %collective-permute-done.7.refs_2_ = bf16[3,64,512]{2,1,0:T(8,128)(2,1)S(1)} collective-permute-done((bf16[3,64,512]{2,1,0:T(8,128)(2,1)S(1)}, bf16[3,64,512]{2,1,0:T(8,128)(2,1)S(1)}, u32[]{:S(2)}, u32[]{:S(2)}) %collective-permute-start.7) | collective-permute-done | bytes 196640 | tf_op jit(solution)/shard_map/ppermute | solution.py:31
  31.8 4.3 %shard_map.121 = (bf16[512,512]{1,0:T(8,128)(2,1)S(1)}, bf16[512,512]{1,0:T(8,128)(2,1)S(1)}) custom-call(s32[2]{0:T(128)S(1)} %pad_add_fusion.place, s32[1,2]{1,0:T(1,128)S(1)} %copy-done.11, bf16[1536,512]{1,0:T(8,128)(2,1)S(1)} %shard_map.120.normed, bf16[128,1536]{1,0:T(8,128)(2,1)S(1)} %copy-done.3, bf16[128,512]{1,0:T(8,128)(2,1)S(1)} %copy-done.4, ...), custom_call_target="tpu_custom_call" | custom-call | tf_op jit(solution)/shard_map/pallas_call | solution.py:358
  36.2 1.1 %shard_map.122 = (f32[512,512]{1,0:T(8,128)S(1)}, bf16[512,128]{1,0:T(8,128)(2,1)S(1)}, bf16[512,128]{1,0:T(8,128)(2,1)S(1)}, bf16[512,128]{1,0:T(8,128)(2,1)S(1)}, bf16[512,128]{1,0:T(8,128)(2,1)S(1)}) custom-call(s32[2]{0:T(128)S(1)} %pad_add_fusion.place, bf16[4,128,512]{2,1,0:T(8,128)(2,1)S(1)} %copy-done.2, ...), custom_call_target="tpu_custom_call" | custom-call | tf_op jit(solution)/shard_map/pallas_call | solution.py:358
  37.4 1.5 %collective-permute-start.15 = (bf16[3,256,256]{2,1,0:T(8,128)(2,1)S(1)}, bf16[3,256,256]{2,1,0:T(8,128)(2,1)S(1)}, u32[]{:S(2)}, u32[]{:S(2)}) collective-permute-start(bf16[3,256,256]{2,1,0:T(8,128)(2,1)S(1)} %shard_map.123.refs_4_), channel_id=1, source_target_pairs={{0,8},{4,20},{8,0},{12,28},{16,24},{20,4},{24,16},{28,12},{1,9},{5... | collective-permute-start | bytes 1179656 | tf_op jit(solution)/shard_map/ppermute | solution.py:31
  38.9 3.5 %collective-permute-start.11 = (bf16[512,128]{1,0:T(8,128)(2,1)S(1)}, bf16[512,128]{1,0:T(8,128)(2,1)S(1)}, u32[]{:S(2)}, u32[]{:S(2)}) collective-permute-start(bf16[512,128]{1,0:T(8,128)(2,1)S(1)} %get-tuple-element.39), channel_id=1, source_target_pairs={{0,3},{1,2},{2,1},{3,0},{4,7},{5,6},{6,5},{7,4},{8,11},{9,10},{10,... | collective-permute-start | bytes 393224 | tf_op jit(solution)/shard_map/ppermute | solution.py:25
  43.3 3.8 %collective-permute-done.11.refs_1_ = bf16[512,128]{1,0:T(8,128)(2,1)S(1)} collective-permute-done((bf16[512,128]{1,0:T(8,128)(2,1)S(1)}, bf16[512,128]{1,0:T(8,128)(2,1)S(1)}, u32[]{:S(2)}, u32[]{:S(2)}) %collective-permute-start.11) | collective-permute-done | bytes 131104 | tf_op jit(solution)/shard_map/ppermute | solution.py:25
  47.1 6.5 %collective-permute-done.12.refs_2_ = bf16[512,128]{1,0:T(8,128)(2,1)S(1)} collective-permute-done((bf16[512,128]{1,0:T(8,128)(2,1)S(1)}, bf16[512,128]{1,0:T(8,128)(2,1)S(1)}, u32[]{:S(2)}, u32[]{:S(2)}) %collective-permute-start.12) | collective-permute-done | bytes 131104 | tf_op jit(solution)/shard_map/ppermute | solution.py:25
  53.7 1.1 %shard_map.124 = (bf16[512,128]{1,0:T(8,128)(2,1)S(1)}, bf16[512,128]{1,0:T(8,128)(2,1)S(1)}, bf16[512,128]{1,0:T(8,128)(2,1)S(1)}, bf16[512,128]{1,0:T(8,128)(2,1)S(1)}, bf16[2,3,256,256]{3,2,1,0:T(8,128)(2,1)S(1)}) custom-call(s32[2]{0:T(128)S(1)} %pad_add_fusion.place, s32[4,3]{1,0:T(4,128)S(1)} %copy-done.8, s32[4]{0:T(128)S(1)} %copy-done.12, ...), custom_call_target="tpu_custom_call" | custom-call | tf_op jit(solution)/shard_map/pallas_call | solution.py:358
  55.5 2.6 %collective-permute-start.18 = (bf16[512,128]{1,0:T(8,128)(2,1)S(1)}, bf16[512,128]{1,0:T(8,128)(2,1)S(1)}, u32[]{:S(2)}, u32[]{:S(2)}) collective-permute-start(bf16[512,128]{1,0:T(8,128)(2,1)S(1)} %get-tuple-element.48), channel_id=1, source_target_pairs={{0,3},{1,2},{2,1},{3,0},{4,7},{5,6},{6,5},{7,4},{8,11},{9,10},{10,... | collective-permute-start | bytes 393224 | tf_op jit(solution)/shard_map/ppermute | solution.py:25
  58.1 1.7 %collective-permute-start.20 = (bf16[512,128]{1,0:T(8,128)(2,1)S(1)}, bf16[512,128]{1,0:T(8,128)(2,1)S(1)}, u32[]{:S(2)}, u32[]{:S(2)}) collective-permute-start(bf16[512,128]{1,0:T(8,128)(2,1)S(1)} %get-tuple-element.50), channel_id=1, source_target_pairs={{0,1},{1,0},{2,3},{3,2},{4,5},{5,4},{6,7},{7,6},{8,9},{9,8},{10,11... | collective-permute-start | bytes 393224 | tf_op jit(solution)/shard_map/ppermute | solution.py:25
  59.9 7.1 %collective-permute-done.16.far = bf16[2,3,256,256]{3,2,1,0:T(8,128)(2,1)S(1)} collective-permute-done((bf16[2,3,256,256]{3,2,1,0:T(8,128)(2,1)S(1)}, bf16[2,3,256,256]{3,2,1,0:T(8,128)(2,1)S(1)}, u32[]{:S(2)}, u32[]{:S(2)}) %collective-permute-start.16) | collective-permute-done | bytes 786464 | tf_op jit(solution)/shard_map/ppermute | solution.py:31
  68.6 2.6 %shard_map.126 = (f32[512,512]{1,0:T(8,128)S(1)}, bf16[512,512]{1,0:T(8,128)(2,1)S(1)}) custom-call(s32[2]{0:T(128)S(1)} %pad_add_fusion.place, f32[512,512]{1,0:T(8,128)S(1)} %get-tuple-element.37.refs_0_.after_attn, f32[1,512]{1,0:T(1,128)S(1)} %get-tuple-element.44.gain_ffn, bf16[6,512,256]{2,1,0:T(8,128)(2,1)S(1)} %get-tuple-element.45.w_in, ...), custom_call_target="tpu_custom_call" | custom-call | tf_op jit(solution)/shard_map/pallas_call | solution.py:358
  71.3 2.2 %shard_map.128 = bf16[512,512]{1,0:T(8,128)(2,1)} custom-call(s32[2]{0:T(128)S(1)} %pad_add_fusion.place, bf16[8,128,256]{2,1,0:T(8,128)(2,1)S(1)} %get-tuple-element.29.own_in, bf16[512,512]{1,0:T(8,128)(2,1)S(1)} %copy-done.1, f32[512,512]{1,0:T(8,128)S(1)} %get-tuple-element.51.total, bf16[512,512]{1,0:T(8,128)(2,1)S(1)} %get-tuple-element.52.ffn_in, ...), custom_call_target="tpu_custom_call" | custom-call | tf_op jit(solution)/shard_map/pallas_call | solution.py:358
  (59 shorter events, 8.4 us)
Async XLA Ops:
  0.0 21.8 %collective-permute-start = (bf16[4,128,512]{2,1,0:T(8,128)(2,1)}, bf16[4,128,512]{2,1,0:T(8,128)(2,1)S(1)}, u32[]{:S(2)}, u32[]{:S(2)}) collective-permute-start(bf16[4,128,512]{2,1,0:T(8,128)(2,1)} %states.3), channel_id=1, source_target_pairs={{0,8},{4,12},{8,16},{12,20},{16,24},{20,28},{1,9},{5,13},{9,17},{1... | collective-permute-start | bytes 1572872 | tf_op jit(solution)/shard_map/ppermute | solution.py:20
  6.0 12.7 %collective-permute-start.3 = (bf16[128,512]{1,0:T(8,128)(2,1)S(1)}, bf16[128,512]{1,0:T(8,128)(2,1)S(1)}, u32[]{:S(2)}, u32[]{:S(2)}) collective-permute-start(bf16[128,512]{1,0:T(8,128)(2,1)S(1)} %fusion), channel_id=1, source_target_pairs={{0,2},{1,3},{2,0},{3,1},{4,6},{5,7},{6,4},{7,5},{8,10},{9,11},{10,... | collective-permute-start | bytes 393224 | tf_op jit(solution)/shard_map/ppermute | solution.py:25
  8.7 10.1 %collective-permute-start.2 = (bf16[128,512]{1,0:T(8,128)(2,1)S(1)}, bf16[128,512]{1,0:T(8,128)(2,1)S(1)}, u32[]{:S(2)}, u32[]{:S(2)}) collective-permute-start(bf16[128,512]{1,0:T(8,128)(2,1)S(1)} %fusion), channel_id=1, source_target_pairs={{0,3},{1,2},{2,1},{3,0},{4,7},{5,6},{6,5},{7,4},{8,11},{9,10},{10,... | collective-permute-start | bytes 393224 | tf_op jit(solution)/shard_map/ppermute | solution.py:25
  10.0 10.3 %collective-permute-start.4 = (bf16[128,512]{1,0:T(8,128)(2,1)S(1)}, bf16[128,512]{1,0:T(8,128)(2,1)S(1)}, u32[]{:S(2)}, u32[]{:S(2)}) collective-permute-start(bf16[128,512]{1,0:T(8,128)(2,1)S(1)} %fusion), channel_id=1, source_target_pairs={{0,1},{1,0},{2,3},{3,2},{4,5},{5,4},{6,7},{7,6},{8,9},{9,8},{10,11... | collective-permute-start | bytes 393224 | tf_op jit(solution)/shard_map/ppermute | solution.py:25
  13.3 8.5 %collective-permute-start.1 = (bf16[256,256]{1,0:T(8,128)(2,1)S(1)}, bf16[256,256]{1,0:T(8,128)(2,1)S(1)}, u32[]{:S(2)}, u32[]{:S(2)}) collective-permute-start(bf16[256,256]{1,0:T(8,128)(2,1)S(1)} %get-tuple-element.30.packed), channel_id=1, source_target_pairs={{0,1},{1,0},{2,3},{3,2},{4,5},{5,4},{6,7},{7,6},{8,9},{9,8},{10,11... | collective-permute-start | bytes 393224 | tf_op jit(solution)/shard_map/ppermute | solution.py:25
  22.4 7.9 %collective-permute-start.5 = (bf16[4,128,512]{2,1,0:T(8,128)(2,1)S(1)}, bf16[4,128,512]{2,1,0:T(8,128)(2,1)S(1)}, u32[]{:S(2)}, u32[]{:S(2)}) collective-permute-start(bf16[4,128,512]{2,1,0:T(8,128)(2,1)S(1)} %get-tuple-element.31), channel_id=1, source_target_pairs={{0,4},{4,0},{8,12},{12,8},{16,20},{20,16},{24,28},{28,24},{1,5},{5... | collective-permute-start | bytes 1572872 | tf_op jit(solution)/shard_map/ppermute | solution.py:25
  22.5 5.7 %collective-permute-start.6 = (bf16[3,64,512]{2,1,0:T(8,128)(2,1)S(1)}, bf16[3,64,512]{2,1,0:T(8,128)(2,1)S(1)}, u32[]{:S(2)}, u32[]{:S(2)}) collective-permute-start(bf16[3,64,512]{2,1,0:T(8,128)(2,1)S(1)} %get-tuple-element.33), channel_id=1, source_target_pairs={{0,8},{4,20},{8,0},{12,28},{16,24},{20,4},{24,16},{28,12},{1,9},{5... | collective-permute-start | bytes 589832 | tf_op jit(solution)/shard_map/ppermute | solution.py:31
  24.0 6.3 %collective-permute-start.7 = (bf16[3,64,512]{2,1,0:T(8,128)(2,1)S(1)}, bf16[3,64,512]{2,1,0:T(8,128)(2,1)S(1)}, u32[]{:S(2)}, u32[]{:S(2)}) collective-permute-start(bf16[3,64,512]{2,1,0:T(8,128)(2,1)S(1)} %get-tuple-element.34), channel_id=1, source_target_pairs={{0,8},{4,20},{8,0},{12,28},{16,24},{20,4},{24,16},{28,12},{1,9},{5... | collective-permute-start | bytes 589832 | tf_op jit(solution)/shard_map/ppermute | solution.py:31
  24.6 7.2 %collective-permute-start.8 = (bf16[3,128,512]{2,1,0:T(8,128)(2,1)S(1)}, bf16[3,128,512]{2,1,0:T(8,128)(2,1)S(1)}, u32[]{:S(2)}, u32[]{:S(2)}) collective-permute-start(bf16[3,128,512]{2,1,0:T(8,128)(2,1)S(1)} %get-tuple-element.32.refs_0_), channel_id=1, source_target_pairs={{0,4},{4,0},{8,12},{12,8},{16,20},{20,16},{24,28},{28,24},{1,5},{5... | collective-permute-start | bytes 1179656 | tf_op jit(solution)/shard_map/ppermute | solution.py:25
  24.6 12.7 %collective-permute-start.14 = (bf16[2,256,256]{2,1,0:T(8,128)(2,1)S(1)}, bf16[2,256,256]{2,1,0:T(8,128)(2,1)S(1)}, u32[]{:S(2)}, u32[]{:S(2)}) collective-permute-start(bf16[2,256,256]{2,1,0:T(8,128)(2,1)S(1)} %get-tuple-element.42.doubled), channel_id=1, source_target_pairs={{0,3},{1,2},{2,1},{3,0},{4,7},{5,6},{6,5},{7,4},{8,11},{9,10},{10,... | collective-permute-start | bytes 786440 | tf_op jit(solution)/shard_map/ppermute | solution.py:25
  28.2 2.8 %collective-permute-start.9 = (bf16[3,64,512]{2,1,0:T(8,128)(2,1)S(1)}, bf16[3,64,512]{2,1,0:T(8,128)(2,1)S(1)}, u32[]{:S(2)}, u32[]{:S(2)}) collective-permute-start(bf16[3,64,512]{2,1,0:T(8,128)(2,1)S(1)} %collective-permute-done.6.refs_1_), channel_id=1, source_target_pairs={{0,4},{4,0},{8,12},{12,8},{16,20},{20,16},{24,28},{28,24},{1,5},{5... | collective-permute-start | bytes 589832 | tf_op jit(solution)/shard_map/ppermute | solution.py:25
  30.3 1.4 %collective-permute-start.10 = (bf16[3,64,512]{2,1,0:T(8,128)(2,1)S(1)}, bf16[3,64,512]{2,1,0:T(8,128)(2,1)S(1)}, u32[]{:S(2)}, u32[]{:S(2)}) collective-permute-start(bf16[3,64,512]{2,1,0:T(8,128)(2,1)S(1)} %collective-permute-done.7.refs_2_), channel_id=1, source_target_pairs={{0,4},{4,0},{8,12},{12,8},{16,20},{20,16},{24,28},{28,24},{1,5},{5... | collective-permute-start | bytes 589832 | tf_op jit(solution)/shard_map/ppermute | solution.py:25
  37.3 29.6 %copy-start.1 = (bf16[512,512]{1,0:T(8,128)(2,1)S(1)}, bf16[512,512]{1,0:T(8,128)(2,1)}, u32[]{:S(2)}) copy-start(bf16[512,512]{1,0:T(8,128)(2,1)} %own_out.3) | copy-start | bytes 1572868
  37.3 29.6 %copy-start.9 = (f32[512]{0:T(512)S(1)}, f32[512]{0:T(512)}, u32[]{:S(2)}) copy-start(f32[512]{0:T(512)} %param.21) | copy-start | bytes 6148
  37.4 16.3 %collective-permute-start.15 = (bf16[3,256,256]{2,1,0:T(8,128)(2,1)S(1)}, bf16[3,256,256]{2,1,0:T(8,128)(2,1)S(1)}, u32[]{:S(2)}, u32[]{:S(2)}) collective-permute-start(bf16[3,256,256]{2,1,0:T(8,128)(2,1)S(1)} %shard_map.123.refs_4_), channel_id=1, source_target_pairs={{0,8},{4,20},{8,0},{12,28},{16,24},{20,4},{24,16},{28,12},{1,9},{5... | collective-permute-start | bytes 1179656 | tf_op jit(solution)/shard_map/ppermute | solution.py:31
  38.9 8.2 %collective-permute-start.11 = (bf16[512,128]{1,0:T(8,128)(2,1)S(1)}, bf16[512,128]{1,0:T(8,128)(2,1)S(1)}, u32[]{:S(2)}, u32[]{:S(2)}) collective-permute-start(bf16[512,128]{1,0:T(8,128)(2,1)S(1)} %get-tuple-element.39), channel_id=1, source_target_pairs={{0,3},{1,2},{2,1},{3,0},{4,7},{5,6},{6,5},{7,4},{8,11},{9,10},{10,... | collective-permute-start | bytes 393224 | tf_op jit(solution)/shard_map/ppermute | solution.py:25
  42.4 11.2 %collective-permute-start.12 = (bf16[512,128]{1,0:T(8,128)(2,1)S(1)}, bf16[512,128]{1,0:T(8,128)(2,1)S(1)}, u32[]{:S(2)}, u32[]{:S(2)}) collective-permute-start(bf16[512,128]{1,0:T(8,128)(2,1)S(1)} %get-tuple-element.40), channel_id=1, source_target_pairs={{0,2},{1,3},{2,0},{3,1},{4,6},{5,7},{6,4},{7,5},{8,10},{9,11},{10,... | collective-permute-start | bytes 393224 | tf_op jit(solution)/shard_map/ppermute | solution.py:25
  42.4 11.2 %collective-permute-start.13 = (bf16[512,128]{1,0:T(8,128)(2,1)S(1)}, bf16[512,128]{1,0:T(8,128)(2,1)S(1)}, u32[]{:S(2)}, u32[]{:S(2)}) collective-permute-start(bf16[512,128]{1,0:T(8,128)(2,1)S(1)} %get-tuple-element.41), channel_id=1, source_target_pairs={{0,1},{1,0},{2,3},{3,2},{4,5},{5,4},{6,7},{7,6},{8,9},{9,8},{10,11... | collective-permute-start | bytes 393224 | tf_op jit(solution)/shard_map/ppermute | solution.py:25
  54.8 5.1 %collective-permute-start.17 = (bf16[2,3,256,256]{3,2,1,0:T(8,128)(2,1)S(1)}, bf16[2,3,256,256]{3,2,1,0:T(8,128)(2,1)S(1)}, u32[]{:S(2)}, u32[]{:S(2)}) collective-permute-start(bf16[2,3,256,256]{3,2,1,0:T(8,128)(2,1)S(1)} %get-tuple-element.43.pair), channel_id=1, source_target_pairs={{0,4},{4,0},{8,12},{12,8},{16,20},{20,16},{24,28},{28,24},{1,5},{5... | collective-permute-start | bytes 2359304 | tf_op jit(solution)/shard_map/ppermute | solution.py:25
  54.9 12.1 %collective-permute-start.16 = (bf16[2,3,256,256]{3,2,1,0:T(8,128)(2,1)S(1)}, bf16[2,3,256,256]{3,2,1,0:T(8,128)(2,1)S(1)}, u32[]{:S(2)}, u32[]{:S(2)}) collective-permute-start(bf16[2,3,256,256]{3,2,1,0:T(8,128)(2,1)S(1)} %get-tuple-element.43.pair), channel_id=1, source_target_pairs={{0,16},{4,12},{8,24},{12,4},{16,0},{20,28},{24,8},{28,20},{1,17},{... | collective-permute-start | bytes 2359304 | tf_op jit(solution)/shard_map/ppermute | solution.py:31
  55.5 12.2 %collective-permute-start.18 = (bf16[512,128]{1,0:T(8,128)(2,1)S(1)}, bf16[512,128]{1,0:T(8,128)(2,1)S(1)}, u32[]{:S(2)}, u32[]{:S(2)}) collective-permute-start(bf16[512,128]{1,0:T(8,128)(2,1)S(1)} %get-tuple-element.48), channel_id=1, source_target_pairs={{0,3},{1,2},{2,1},{3,0},{4,7},{5,6},{6,5},{7,4},{8,11},{9,10},{10,... | collective-permute-start | bytes 393224 | tf_op jit(solution)/shard_map/ppermute | solution.py:25
  58.1 10.4 %collective-permute-start.19 = (bf16[512,128]{1,0:T(8,128)(2,1)S(1)}, bf16[512,128]{1,0:T(8,128)(2,1)S(1)}, u32[]{:S(2)}, u32[]{:S(2)}) collective-permute-start(bf16[512,128]{1,0:T(8,128)(2,1)S(1)} %get-tuple-element.49), channel_id=1, source_target_pairs={{0,2},{1,3},{2,0},{3,1},{4,6},{5,7},{6,4},{7,5},{8,10},{9,11},{10,... | collective-permute-start | bytes 393224 | tf_op jit(solution)/shard_map/ppermute | solution.py:25
  58.1 10.4 %collective-permute-start.20 = (bf16[512,128]{1,0:T(8,128)(2,1)S(1)}, bf16[512,128]{1,0:T(8,128)(2,1)S(1)}, u32[]{:S(2)}, u32[]{:S(2)}) collective-permute-start(bf16[512,128]{1,0:T(8,128)(2,1)S(1)} %get-tuple-element.50), channel_id=1, source_target_pairs={{0,1},{1,0},{2,3},{3,2},{4,5},{5,4},{6,7},{7,6},{8,9},{9,8},{10,11... | collective-permute-start | bytes 393224 | tf_op jit(solution)/shard_map/ppermute | solution.py:25
  68.5 2.7 %collective-permute-start.21 = (bf16[2,3,256,256]{3,2,1,0:T(8,128)(2,1)S(1)}, bf16[2,3,256,256]{3,2,1,0:T(8,128)(2,1)S(1)}, u32[]{:S(2)}, u32[]{:S(2)}) collective-permute-start(bf16[2,3,256,256]{3,2,1,0:T(8,128)(2,1)S(1)} %shard_map.127), channel_id=1, source_target_pairs={{0,4},{4,0},{8,12},{12,8},{16,20},{20,16},{24,28},{28,24},{1,5},{5... | collective-permute-start | bytes 2359304 | tf_op jit(solution)/shard_map/ppermute | solution.py:25
  (11 other events, 111.1 us)
